TPU v7x, 32 devices: a whole 2x2x4 slice. The times are simulated.
32 devices in a mesh: fsdp: 16 (over z, y, core), tp: 2 (over x).
Axes of the slice: x: 2, y: 2, z: 4, core: 2. Of those that a mesh axis runs over, the one named last changes fastest.
Arguments:
- momentum: float32 [1536, 27648], P('fsdp', 'tp'), may hold values from -1800 to 1800
- gradient: bfloat16 [1536, 27648], P('fsdp', 'tp'), may hold values from -1800 to 1800
- basis: bfloat16 [27648, 256], P('tp'), may hold values from -0.0390625 to 0.0390625
Outputs:
- new_momentum: float32 [1536, 27648], P('fsdp', 'tp')
- new_basis: bfloat16 [27648, 256], P('tp')
- update: bfloat16 [1536, 27648], P('fsdp', 'tp')
All inputs are finite; a program needn't handle non-finite values.
Results may differ from a plain program's by a relative error of at most 0.0083.
Values may be sent and summed in bfloat16 or wider, within the bound.
No kernel may reach another device: no remote copies, remote signals or barrier semaphores. Data moves between devices by JAX's collectives and lax.ppermute only.
A program may use at most 128 MiB of HBM per device.

v0:
```python
import math

import jax
import jax.numpy as jnp
from jax import lax
from jax.sharding import PartitionSpec as P


def orthonormal(sketch, gram):
    lower = jnp.linalg.cholesky(gram)
    return lax.linalg.triangular_solve(
        lower, sketch, left_side=False, lower=True, transpose_a=True
    ).astype(jnp.bfloat16)


def local(momentum, gradient, basis):
    rows_here, cols_here = momentum.shape
    rank_cols = basis.shape[1]
    fsdp_count = lax.axis_size("fsdp")
    tp_count = lax.axis_size("tp")
    base = momentum + gradient.astype(jnp.float32)
    base_b = base.astype(jnp.bfloat16)
    sketch = lax.psum(jnp.dot(base_b, basis, preferred_element_type=jnp.float32), "tp")
    gram = lax.psum(jnp.dot(sketch.T, sketch, precision=lax.Precision.HIGHEST), "fsdp")
    ortho = orthonormal(sketch, gram)
    back_share = lax.psum_scatter(
        lax.dot_general(
            base_b, ortho, (((0,), (0,)), ((), ())), preferred_element_type=jnp.float32
        ),
        "fsdp",
        scatter_dimension=0,
        tiled=True,
    ).astype(jnp.bfloat16)
    back = lax.all_gather(back_share, "fsdp", axis=0, tiled=True)
    back_f = back.astype(jnp.float32)
    colsq = lax.psum(jnp.sum(back_f * back_f, axis=0), "tp")
    new_basis = (back_f * lax.rsqrt(colsq + 1e-06)).astype(jnp.bfloat16)
    new_momentum = base - 0.05 * jnp.dot(ortho, back.T, preferred_element_type=jnp.float32)
    total_rows = rows_here * fsdp_count
    total_cols = cols_here * tp_count
    factor = math.sqrt(total_rows * total_cols / rank_cols)
    update = (factor * jnp.dot(ortho, new_basis.T, preferred_element_type=jnp.float32)).astype(
        jnp.bfloat16
    )
    return (new_momentum, new_basis, update)


def solution(mesh):
    return jax.shard_map(
        local,
        mesh=mesh,
        in_specs=(P("fsdp", "tp"), P("fsdp", "tp"), P("tp", None)),
        out_specs=(P("fsdp", "tp"), P("tp", None), P("fsdp", "tp")),
        check_vma=False,
    )
```

profile of v0, /device:TPU:1, one launch (start us, length us, event | category | flops | bytes accessed | tf_op | source)
XLA Modules:
  0.0 452.8 jit_solution(11829093512577204785)
XLA Ops:
  7.2 7.1 %fusion.17 = f32[96,256]{1,0:T(8,128)} fusion(bf16[13824,256]{1,0:T(8,128)(2,1)} %param.5, f32[96,13824]{1,0:T(8,128)} %param.3, bf16[96,13824]{1,0:T(8,128)(2,1)} %param.4), kind=kOutput, calls=%fused_computation.43 | convolution fusion | flops 683458560 | bytes 15138816 | tf_op jit(solution)/shard_map/dot_general | solution.py:23
  14.4 22.8 %all-reduce.4.cloned.1.call-done = f32[96,256]{1,0:T(8,128)} async-done(((f32[96,256]{1,0:T(8,128)}), f32[96,256]{1,0:T(8,128)}) %all-reduce.4.cloned.1.call-update) | async-done | bytes 98320 | tf_op jit(solution)/shard_map/psum | solution.py:23
  37.2 2.1 fusion.21
  39.4 91.7 %all-reduce.6.cloned.1.call-done = f32[256,256]{0,1:T(8,128)} async-done(((f32[256,256]{0,1:T(8,128)}), f32[256,256]{0,1:T(8,128)}) %all-reduce.6.cloned.1.call-update) | async-done | bytes 262160 | tf_op jit(solution)/shard_map/psum | solution.py:24
  131.1 1.1 copy.7
  132.1 1.0 fusion.5
  133.1 11.7 %cholesky.50 = f32[128,128]{1,0:T(8,128)S(1)} custom-call(f32[128,128]{1,0:T(8,128)S(1)} %cholesky.118), custom_call_target="Cholesky" | custom-call | tf_op jit(solution)/shard_map/jit(cholesky)/cholesky | solution.py:10
  144.9 9.8 %custom-call.14 = f32[1,128,128]{1,2,0:T(8,128)S(1)} custom-call(f32[1,128,128]{2,1,0:T(8,128)S(1)} %get-tuple-element.24), custom_call_target="InvertDiagBlocksLowerTriangular" | custom-call | tf_op jit(solution)/shard_map/jit(cholesky)/cholesky | solution.py:10
  155.2 11.7 %cholesky.105 = f32[128,128]{1,0:T(8,128)S(1)} custom-call(f32[128,128]{1,0:T(8,128)S(1)} %convolution_subtract_fusion), custom_call_target="Cholesky" | custom-call | tf_op jit(solution)/shard_map/jit(cholesky)/cholesky | solution.py:10
  169.1 5.5 %while.1 = (s32[]{:T(128)}, f32[256,256]{1,0:T(8,128)S(1)}, s32[2,2]{1,0:T(2,128)S(1)}, f32[2,128,128]{2,1,0:T(8,128)}, s32[]{:T(128)}) while((s32[]{:T(128)}, f32[256,256]{1,0:T(8,128)S(1)}, s32[2,2]{1,0:T(2,128)S(1)}, f32[2,128,128]{2,1,0:T(8,128)}, s32[]{:T(128)}) %tuple.28), condition=%wide.while_cond, body=%wide.while_body.sunk | while | flops 2 | bytes 132205 | solution.py:11
  169.9 2.1 bitcast_dynamic-update-slice_fusion.2
  172.6 2.1 bitcast_dynamic-update-slice_fusion.2
  174.6 20.5 %custom-call.15 = f32[2,128,128]{1,2,0:T(8,128)S(1)} custom-call(f32[2,128,128]{2,1,0:T(8,128)} %get-tuple-element.10), custom_call_target="InvertDiagBlocksLowerTriangular" | custom-call | tf_op jit(solution)/shard_map/triangular_solve | solution.py:11
  195.1 1.0 fusion.20
  196.1 1.0 convolution_subtract_fusion.1
  197.4 9.6 %fusion.12 = f32[13824,256]{1,0:T(8,128)} fusion(bf16[96,128]{1,0:T(8,128)(2,1)S(1)} %convolution_convert_fusion, bf16[96,128]{1,0:T(8,128)(2,1)S(1)} %get-tuple-element.27, f32[96,13824]{1,0:T(8,128)} %param.3, bf16[96,13824]{1,0:T(8,128)(2,1)S(1)} %copy-done), kind=kOutput, calls=%fused_computation.33 | convolution fusion | flops 683556864 | bytes 22167552 | tf_op jit(solution)/shard_map/dot_general | solution.py:27
  207.1 144.6 %reduce-scatter.2.cloned.1.call-done = f32[864,256]{1,0:T(8,128)} async-done(((f32[13824,256]{1,0:T(8,128)}), f32[864,256]{1,0:T(8,128)}) %reduce-scatter.2.cloned.1.call-update) | async-done | bytes 884752 | tf_op jit(solution)/shard_map/reduce_scatter | solution.py:26
  351.7 2.0 convert_element_type.21
  353.7 67.8 %all-gather.2.cloned.1.call-done = bf16[13824,256]{1,0:T(8,128)(2,1)} async-done(((bf16[864,256]{1,0:T(8,128)(2,1)}), bf16[13824,256]{1,0:T(8,128)(2,1)}) %all-gather.2.cloned.1.call-update) | async-done | bytes 7077904 | tf_op jit(solution)/shard_map/all_gather | solution.py:34
  421.4 4.8 %fusion.2 = f32[256]{0:T(256)S(1)} fusion(bf16[13824,256]{1,0:T(8,128)(2,1)} %all-gather.2.cloned.1.call-done), kind=kLoop, calls=%fused_computation.8 | loop fusion | flops 10616576 | bytes 7078912 | tf_op jit(solution)/shard_map/reduce_sum | solution.py:36
  426.2 3.8 psum.23
  430.0 4.8 %fusion.3 = bf16[13824,256]{1,0:T(8,128)(2,1)S(1)} fusion(bf16[13824,256]{1,0:T(8,128)(2,1)} %all-gather.2.cloned.1.call-done, f32[256]{0:T(256)S(1)} %add_rsqrt_fusion), kind=kLoop, calls=%fused_computation.9 | loop fusion | flops 10616832 | bytes 14156800 | tf_op jit(solution)/shard_map/convert_element_type | solution.py:37
  434.9 3.8 fusion.1
  438.7 7.6 %fusion = f32[96,13824]{1,0:T(8,128)} fusion(bf16[13824,256]{1,0:T(8,128)(2,1)S(1)} %bitcast.39, f32[96,13824]{1,0:T(8,128)} %param.3, bf16[96,13824]{1,0:T(8,128)(2,1)S(1)} %copy-done.1, bf16[96,128]{1,0:T(8,128)(2,1)S(1)} %convolution_convert_fusion, bf16[96,128]{1,0:T(8,128)(2,1)S(1)} %get-tuple-element.27), kind=kOutput, calls=%fused_computation.6 | convolution fusion | flops 684883968 | bytes 20398080 | tf_op jit(solution)/shard_map/dot_general | solution.py:38
  (36 shorter events, 3.1 us)
Async XLA Ops:
  7.2 30.0 %all-reduce.4.cloned.1.call-start = ((), (), s32[]{:S(2)}) async-start(), calls=%async_computation.1 | async-start | bytes 196608 | tf_op jit(solution)/shard_map/psum | solution.py:23
  14.4 183.0 %copy-start = (bf16[96,13824]{1,0:T(8,128)(2,1)S(1)}, bf16[96,13824]{1,0:T(8,128)(2,1)}, u32[]{:S(2)}) copy-start(bf16[96,13824]{1,0:T(8,128)(2,1)} %param.4) | copy-start | bytes 7962628
  14.4 116.7 %all-reduce.6.cloned.1.call-start = ((), (), s32[]{:S(2)}) async-start(), calls=%async_computation.2 | async-start | bytes 524288 | tf_op jit(solution)/shard_map/psum | solution.py:24
  39.3 312.4 %reduce-scatter.2.cloned.1.call-start = ((), (), s32[]{:S(2)}) async-start(), calls=%async_computation.3 | async-start | bytes 15040512 | tf_op jit(solution)/shard_map/reduce_scatter | solution.py:26
  207.0 214.4 %all-gather.2.cloned.1.call-start = ((), (), s32[]{:S(2)}) async-start(), calls=%async_computation.4 | async-start | bytes 7520256 | tf_op jit(solution)/shard_map/all_gather | solution.py:34
  421.4 17.2 %slice-start = ((s8[7077888]{0:T(1024)(128)(4,1)}), s8[2883584]{0:T(1024)(128)(4,1)S(1)}, s32[]{:S(2)}) async-start(s8[7077888]{0:T(1024)(128)(4,1)} %bitcast.38), calls=%async_computation.5 | async-start | bytes 5767168
  430.0 8.6 %slice-start.1 = ((s8[7077888]{0:T(1024)(128)(4,1)}), s8[4194304]{0:T(1024)(128)(4,1)S(1)}, s32[]{:S(2)}) async-start(s8[7077888]{0:T(1024)(128)(4,1)} %bitcast.38), calls=%async_computation.6 | async-start | bytes 8388608
  434.9 11.4 %copy-start.2 = (bf16[13824,256]{1,0:T(8,128)(2,1)}, bf16[13824,256]{1,0:T(8,128)(2,1)S(1)}, u32[]{:S(2)}) copy-start(bf16[13824,256]{1,0:T(8,128)(2,1)S(1)} %fusion.3) | copy-start | bytes 21233668
  434.9 3.8 copy-start.1
Sparse Core Ops, SparseCore 0:
  14.5 22.6 all-reduce.3
  41.2 89.8 all-reduce.5
  207.1 144.5 reduce-scatter.1
  354.4 67.0 all-gather.1
where the time goes:
time: 455 us; the launch traced here: 453 us
  waiting for transfers between devices  327 us (72%)
  other arithmetic  67.1 us (15%)
  matrix products  32.9 us (7%)
  between operations  15.2 us (3%)
  local copies, waits for them, and re-layouts  6.52 us (1%)
    reduce_scatter x1, waiting for transfers between devices, local(): lax.psum_scatter(lax.dot_general(base_b, ortho, (((0,), (0,)), ((), ())),...  145 us
    psum x1, waiting for transfers between devices, local(): lax.psum(jnp.dot(sketch.T, sketch, precision=lax.Precision.HIGHEST), 'fsdp')  91.7 us
    all_gather x1, waiting for transfers between devices, local(): back = lax.all_gather(back_share, 'fsdp', axis=0, tiled=True)  67.8 us
    another operation x6, other arithmetic, orthonormal(): lower = jnp.linalg.cholesky(gram)  34 us
    psum x1, waiting for transfers between devices, local(): lax.psum(jnp.dot(base_b, basis, preferred_element_type=jnp.float32), 'tp')  22.8 us
    another operation x3, other arithmetic, orthonormal(): lax.linalg.triangular_solve(lower, sketch, left_side=False, lower=True, t...  20.5 us
    dot_general x1, matrix products, local(): lax.dot_general(base_b, ortho, (((0,), (0,)), ((), ())), preferred_elemen...  9.6 us
  transfers between devices with their start and end apart: 4, of which 4 were waited for; matrix products, arithmetic and copies ran while one was open for 0% of the time, Pallas kernels for 0%

commit v1 on v0

v1 whole, which is shorter than its diff:
```python
import math

import jax
import jax.numpy as jnp
from jax import lax
from jax.sharding import PartitionSpec as P

LANES = 128


def orthonormal(sketch, gram):
    lower = jnp.linalg.cholesky(gram)
    return lax.linalg.triangular_solve(
        lower, sketch, left_side=False, lower=True, transpose_a=True
    ).astype(jnp.bfloat16)


def local(momentum, gradient, basis):
    rows_here, cols_here = momentum.shape
    rank_cols = basis.shape[1]
    fsdp_count = lax.axis_size("fsdp")
    tp_count = lax.axis_size("tp")
    share = -(-cols_here // (fsdp_count * LANES)) * LANES
    base = momentum + gradient.astype(jnp.float32)
    base_b = base.astype(jnp.bfloat16)

    padded = jnp.pad(base_b, ((0, 0), (0, share * fsdp_count - cols_here)))
    outgoing = jnp.swapaxes(padded.reshape(rows_here, fsdp_count, share), 0, 1)
    columns = lax.all_to_all(outgoing, "fsdp", 0, 0, tiled=True)
    columns = columns.reshape(rows_here * fsdp_count, share)

    sketch = jnp.dot(base_b, basis, preferred_element_type=jnp.float32)
    if tp_count == 2:
        sketch = sketch + lax.ppermute(sketch, "tp", [(0, 1), (1, 0)])
    else:
        sketch = lax.psum(sketch, "tp")
    whole = lax.all_gather(sketch, "fsdp", axis=0, tiled=True)
    gram = jnp.dot(whole.T, whole, precision=lax.Precision.HIGHEST)
    ortho = orthonormal(whole, gram)
    ortho_here = lax.dynamic_slice_in_dim(
        ortho, lax.axis_index("fsdp") * rows_here, rows_here, axis=0
    )
    back_share = lax.dot_general(
        columns, ortho, (((0,), (0,)), ((), ())), preferred_element_type=jnp.float32
    ).astype(jnp.bfloat16)
    share_f = back_share.astype(jnp.float32)
    colsq = lax.psum(jnp.sum(share_f * share_f, axis=0), ("fsdp", "tp"))
    back = lax.all_gather(back_share, "fsdp", axis=0, tiled=True)[:cols_here]
    back_f = back.astype(jnp.float32)
    new_basis = (back_f * lax.rsqrt(colsq + 1e-06)).astype(jnp.bfloat16)
    new_momentum = base - 0.05 * jnp.dot(ortho_here, back.T, preferred_element_type=jnp.float32)
    total_rows = rows_here * fsdp_count
    total_cols = cols_here * tp_count
    factor = math.sqrt(total_rows * total_cols / rank_cols)
    update = (factor * jnp.dot(ortho_here, new_basis.T, preferred_element_type=jnp.float32)).astype(
        jnp.bfloat16
    )
    return (new_momentum, new_basis, update)


def solution(mesh):
    return jax.shard_map(
        local,
        mesh=mesh,
        in_specs=(P("fsdp", "tp"), P("fsdp", "tp"), P("tp", None)),
        out_specs=(P("fsdp", "tp"), P("tp", None), P("fsdp", "tp")),
        check_vma=False,
    )
```

time: 455 us -> 256 us (0.56)
  waiting for transfers between devices: 327 us -> 91.9 us
  blocking collectives: 3.79 us -> 41 us
  matrix products: 32.9 us -> 23.2 us
  starting transfers between devices: 0.16 us -> 9.76 us
    reduce_scatter x1 -> x0, waiting for transfers between devices: 145 us -> none  [local(): lax.psum_scatter(lax.dot_general(base_b, ortho, (((0,), (0,)), ((), ())),...]
    psum x2 -> x0, waiting for transfers between devices: 114 us -> none  [the longest x1 91.7 us: local(): lax.psum(jnp.dot(sketch.T, sketch, precision=lax.Precision.HIGHEST), 'fsdp')]
    psum x1, blocking collectives: 3.79 us -> 41 us  [local(): colsq = lax.psum(jnp.sum(share_f * share_f, axis=0), ('fsdp', 'tp'))]
    all_gather x1 -> x2, waiting for transfers between devices: 67.8 us -> 89.4 us  [the longest x1 61.3 us: local(): whole = lax.all_gather(sketch, 'fsdp', axis=0, tiled=True)]
    dot_general x5, matrix products: 30.2 us -> 19.6 us  [the longest x1 6.24 us: local(): jnp.dot(ortho_here, back.T, preferred_element_type=jnp.float32)]
    all_to_all x0 -> x1, starting transfers between devices: none -> 7.4 us  [local(): columns = lax.all_to_all(outgoing, 'fsdp', 0, 0, tiled=True)]
    reduce_sum x1 -> x0, other arithmetic: 4.77 us -> none  [local(): colsq = lax.psum(jnp.sum(back_f * back_f, axis=0), 'tp')]
    unnamed x10, local copies, waits for them, and re-layouts: 0.02 us -> 4.66 us
  transfers between devices with their start and end apart: 4 -> 4, of which waited for: 4 -> 3; matrix products, arithmetic and copies ran while one was open for 0% -> 27% of each run, Pallas kernels for 0% -> 0%
where the time goes in v1:
time: 256 us; the launch traced here: 255 us
  waiting for transfers between devices  91.9 us (36%)
  other arithmetic  62.8 us (25%)
  blocking collectives  41 us (16%)
  matrix products  23.2 us (9%)
  between operations  15.6 us (6%)
  local copies, waits for them, and re-layouts  10.9 us (4%)
  starting transfers between devices  9.76 us (4%)
    all_gather x1, waiting for transfers between devices, local(): whole = lax.all_gather(sketch, 'fsdp', axis=0, tiled=True)  61.3 us
    psum x1, blocking collectives, local(): colsq = lax.psum(jnp.sum(share_f * share_f, axis=0), ('fsdp', 'tp'))  41 us
    another operation x6, other arithmetic, orthonormal(): lower = jnp.linalg.cholesky(gram)  34.2 us
    all_gather x1, waiting for transfers between devices, local(): back = lax.all_gather(back_share, 'fsdp', axis=0, tiled=True)[:cols_here]  28 us
    another operation x3, other arithmetic, orthonormal(): lax.linalg.triangular_solve(lower, sketch, left_side=False, lower=True, t...  19.7 us
    all_to_all x1, starting transfers between devices, local(): columns = lax.all_to_all(outgoing, 'fsdp', 0, 0, tiled=True)  7.4 us
    dot_general x1, matrix products, local(): jnp.dot(ortho_here, back.T, preferred_element_type=jnp.float32)  6.24 us
  transfers between devices with their start and end apart: 4, of which 3 were waited for; matrix products, arithmetic and copies ran while one was open for 27% of the time, Pallas kernels for 0%

profile of v1, /device:TPU:1, one launch (start us, length us, event | category | flops | bytes accessed | tf_op | source)
XLA Modules:
  0.0 255.3 jit_solution(4251374564084797537)
XLA Ops:
  7.2 3.9 %fusion.3 = bf16[96,13824]{1,0:T(8,128)(2,1)S(1)} fusion(f32[96,13824]{1,0:T(8,128)} %param.3, bf16[96,13824]{1,0:T(8,128)(2,1)} %param.4), kind=kLoop, calls=%fused_computation.9 | loop fusion | flops 3981312 | bytes 10616832 | tf_op jit(solution)/shard_map/convert_element_type | solution.py:25
  11.1 1.4 copy-done.2
  12.5 1.2 fusion.18
  13.8 2.1 collective-permute-start
  15.9 2.5 collective-permute-done
  19.3 1.8 copy.11
  21.1 7.4 %all-to-all-start = ((bf16[16,96,896]{2,1,0:T(8,128)(2,1)}), bf16[16,96,896]{2,1,0:T(8,128)(2,1)}, u32[]{:S(2)}, u32[]{:S(2)}) async-start(bf16[16,96,896]{2,1,0:T(8,128)(2,1)} %bitcast.39), calls=%async_computation | async-start | bytes 5505024 | tf_op jit(solution)/shard_map/all_to_all | solution.py:29
  28.8 61.3 %all-gather.3.cloned.1.call-done = f32[1536,256]{1,0:T(8,128)} async-done(((f32[96,256]{1,0:T(8,128)}), f32[1536,256]{1,0:T(8,128)}) %all-gather.3.cloned.1.call-update) | async-done | bytes 1572880 | tf_op jit(solution)/shard_map/all_gather | solution.py:37
  90.1 4.6 %fusion.19 = f32[256,256]{1,0:T(8,128)S(1)} fusion(f32[1536,256]{1,0:T(8,128)} %all-gather.3.cloned.1.call-done), kind=kOutput, calls=%fused_computation.48 | convolution fusion | flops 1207959552 | bytes 1835008 | tf_op jit(solution)/shard_map/dot_general | solution.py:38
  94.9 11.7 %cholesky.50 = f32[128,128]{1,0:T(8,128)S(1)} custom-call(f32[128,128]{1,0:T(8,128)S(1)} %cholesky.118), custom_call_target="Cholesky" | custom-call | tf_op jit(solution)/shard_map/jit(cholesky)/cholesky | solution.py:12
  106.7 9.8 %custom-call.14 = f32[1,128,128]{1,2,0:T(8,128)S(1)} custom-call(f32[1,128,128]{2,1,0:T(8,128)S(1)} %get-tuple-element.24), custom_call_target="InvertDiagBlocksLowerTriangular" | custom-call | tf_op jit(solution)/shard_map/jit(cholesky)/cholesky | solution.py:12
  117.0 11.9 %cholesky.105 = f32[128,128]{1,0:T(8,128)S(1)} custom-call(f32[128,128]{1,0:T(8,128)S(1)} %convolution_subtract_fusion), custom_call_target="Cholesky" | custom-call | tf_op jit(solution)/shard_map/jit(cholesky)/cholesky | solution.py:12
  131.1 4.1 %while.1 = (s32[]{:T(128)}, f32[256,256]{1,0:T(8,128)S(1)}, s32[2,2]{1,0:T(2,128)S(1)}, f32[2,128,128]{2,1,0:T(8,128)S(1)}, s32[]{:T(128)}) while((s32[]{:T(128)}, f32[256,256]{1,0:T(8,128)S(1)}, s32[2,2]{1,0:T(2,128)S(1)}, f32[2,128,128]{2,1,0:T(8,128)S(1)}, s32[]{:T(128)}) %tuple.29), condition=%wide.while_cond, body=%wide.while_body.sunk | while | flops 2 | bytes 131189 | solution.py:13
  131.7 1.4 bitcast_dynamic-update-slice_fusion.2
  133.8 1.4 bitcast_dynamic-update-slice_fusion.2
  135.2 19.7 %custom-call.15 = f32[2,128,128]{1,2,0:T(8,128)S(1)} custom-call(f32[2,128,128]{2,1,0:T(8,128)S(1)} %get-tuple-element.10), custom_call_target="InvertDiagBlocksLowerTriangular" | custom-call | tf_op jit(solution)/shard_map/triangular_solve | solution.py:13
  155.8 1.4 fusion.8
  158.1 3.5 %multiply_reduce_fusion = (f32[256]{0:T(256)S(1)}, bf16[896,256]{1,0:T(8,128)(2,1)}) fusion(bf16[1536,896]{1,0:T(8,128)(2,1)} %bitcast.6, bf16[1536,128]{0,1:T(8,128)(2,1)S(1)} %convolution_convert_fusion, bf16[1536,128]{0,1:T(8,128)(2,1)S(1)} %get-tuple-element.27), kind=kOutput, calls=%fused_computation.14 | convolution fusion | flops 707133184 | bytes 3998720 | tf_op jit(solution)/shard_map/dot_general | solution.py:43
  161.6 41.0 %psum.7 = f32[256]{0:T(256)S(1)} all-reduce(f32[256]{0:T(256)S(1)} %get-tuple-element.29), channel_id=1, replica_groups=mesh['fsdp'=16,'tp'=2] {'fsdp','tp'}, use_global_device_ids=true, to_apply=%region_5.6 | all-reduce | flops 256 | bytes 2048 | tf_op jit(solution)/shard_map/psum | solution.py:47
  202.6 28.0 %all-gather.5.cloned.1.call-done = bf16[14336,256]{1,0:T(8,128)(2,1)} async-done(((bf16[896,256]{1,0:T(8,128)(2,1)}), bf16[14336,256]{1,0:T(8,128)(2,1)}) %all-gather.5.cloned.1.call-update) | async-done | bytes 7340048 | tf_op jit(solution)/shard_map/all_gather | solution.py:48
  230.6 4.3 %multiply_convert_fusion = bf16[13824,256]{1,0:T(8,128)(2,1)S(1)} fusion(f32[256]{0:T(256)S(1)} %add_rsqrt_fusion, bf16[14336,256]{1,0:T(8,128)(2,1)} %all-gather.5.cloned.1.call-done), kind=kLoop, calls=%fused_computation.6 | loop fusion | flops 10616832 | bytes 14156800 | tf_op jit(solution)/shard_map/convert_element_type | solution.py:50
  235.0 4.0 %fusion.1 = bf16[96,13824]{1,0:T(8,128)(2,1)} fusion(bf16[13824,256]{1,0:T(8,128)(2,1)S(1)} %multiply_convert_fusion, s32[]{:T(128)S(6)} %select_n.8, bf16[1536,128]{0,1:T(8,128)(2,1)S(1)} %get-tuple-element.27, bf16[1536,128]{0,1:T(8,128)(2,1)S(1)} %convolution_convert_fusion), kind=kOutput, calls=%fused_computation.5 | convolution fusion | flops 682229760 | bytes 10518532 | tf_op jit(solution)/shard_map/dot_general | solution.py:55
  239.0 2.5 copy-done.1
  242.2 6.2 %fusion = f32[96,13824]{1,0:T(8,128)} fusion(bf16[14336,256]{1,0:T(8,128)(2,1)S(1)} %copy-done.1, f32[96,13824]{1,0:T(8,128)} %param.3, bf16[96,13824]{1,0:T(8,128)(2,1)S(1)} %copy-done.4, s32[]{:T(128)S(6)} %select_n.8, bf16[1536,128]{0,1:T(8,128)(2,1)S(1)} %get-tuple-element.27, bf16[1536,128]{0,1:T(8,128)(2,1)S(1)} %convolution_convert_fusion), kind=kOutput, calls=%fused_computation.4 | convolution fusion | flops 684883968 | bytes 21135364 | tf_op jit(solution)/shard_map/dot_general | solution.py:51
  (35 shorter events, 6.5 us)
Async XLA Ops:
  7.2 82.9 %all-gather.3.cloned.1.call-start = ((), (), s32[]{:S(2)}) async-start(), calls=%async_computation.1 | async-start | bytes 1671168 | tf_op jit(solution)/shard_map/all_gather | solution.py:37
  7.2 5.3 %copy-start.2 = (bf16[13824,256]{1,0:T(8,128)(2,1)S(1)}, bf16[13824,256]{1,0:T(8,128)(2,1)}, u32[]{:S(2)}) copy-start(bf16[13824,256]{1,0:T(8,128)(2,1)} %param.5) | copy-start | bytes 21233668
  13.8 4.6 %collective-permute-start = (f32[96,256]{1,0:T(8,128)S(1)}, f32[96,256]{1,0:T(8,128)S(1)}, u32[]{:S(2)}, u32[]{:S(2)}) collective-permute-start(f32[96,256]{1,0:T(8,128)S(1)} %fusion.18), channel_id=1, source_target_pairs={{0,1},{1,0},{2,3},{3,2},{4,5},{5,4},{6,7},{7,6},{8,9},{9,8},{10,11... | collective-permute-start | bytes 294920 | tf_op jit(solution)/shard_map/ppermute | solution.py:34
  21.1 137.0 %all-to-all-start = ((bf16[16,96,896]{2,1,0:T(8,128)(2,1)}), bf16[16,96,896]{2,1,0:T(8,128)(2,1)}, u32[]{:S(2)}, u32[]{:S(2)}) async-start(bf16[16,96,896]{2,1,0:T(8,128)(2,1)} %bitcast.39), calls=%async_computation | async-start | bytes 5505024 | tf_op jit(solution)/shard_map/all_to_all | solution.py:29
  28.5 202.1 %all-gather.5.cloned.1.call-start = ((), (), s32[]{:S(2)}) async-start(), calls=%async_computation.2 | async-start | bytes 7798784 | tf_op jit(solution)/shard_map/all_gather | solution.py:48
  90.1 64.8 %copy-start.3 = (f32[1536,256]{1,0:T(8,128)S(1)}, f32[1536,256]{1,0:T(8,128)}, u32[]{:S(2)}) copy-start(f32[1536,256]{1,0:T(8,128)} %all-gather.3.cloned.1.call-done) | copy-start | bytes 4718596
  234.9 13.5 %copy-start = (bf16[13824,256]{1,0:T(8,128)(2,1)}, bf16[13824,256]{1,0:T(8,128)(2,1)S(1)}, u32[]{:S(2)}) copy-start(bf16[13824,256]{1,0:T(8,128)(2,1)S(1)} %multiply_convert_fusion) | copy-start | bytes 21233668
  235.0 6.5 %copy-start.1 = (bf16[14336,256]{1,0:T(8,128)(2,1)S(1)}, bf16[14336,256]{1,0:T(8,128)(2,1)}, u32[]{:S(2)}) copy-start(bf16[14336,256]{1,0:T(8,128)(2,1)} %all-gather.5.cloned.1.call-done) | copy-start | bytes 22020100
  235.0 7.3 %copy-start.4 = (bf16[96,13824]{1,0:T(8,128)(2,1)S(1)}, bf16[96,13824]{1,0:T(8,128)(2,1)}, u32[]{:S(2)}) copy-start(bf16[96,13824]{1,0:T(8,128)(2,1)} %param.4) | copy-start | bytes 7962628
Sparse Core Ops, SparseCore 0:
  19.2 70.8 all-gather.2
  161.7 68.8 all-gather.4

commit v2 on v1

v2 whole, which is shorter than its diff:
```python
import functools
import math

import jax
import jax.numpy as jnp
from jax import lax
from jax.experimental import pallas as pl
from jax.experimental.pallas import tpu as pltpu
from jax.sharding import PartitionSpec as P

LANES = 128
SUBLANES = 8
PANEL = 64
LONGEST_RING = 32
VMEM_LIMIT = 48 * 1024 * 1024
FULL = lax.Precision.HIGHEST
F32 = jnp.float32
BF16 = jnp.bfloat16


def cost(flops, nbytes):
    return pl.CostEstimate(flops=flops, bytes_accessed=nbytes, transcendentals=0)


def params():
    return pltpu.CompilerParams(vmem_limit_bytes=VMEM_LIMIT)


def sketch_kernel(cols, m_ref, g_ref, b_ref, out_ref, sketch_ref):
    step = pl.program_id(0)
    share = m_ref.shape[1]
    left = cols - step * share
    base_b = (m_ref[...] + g_ref[...].astype(F32)).astype(BF16)
    basis = b_ref[...]
    if cols % share:
        lane = lax.broadcasted_iota(jnp.int32, base_b.shape, 1)
        base_b = jnp.where(lane < left, base_b, jnp.zeros_like(base_b))
        row = lax.broadcasted_iota(jnp.int32, basis.shape, 0)
        basis = jnp.where(row < left, basis, jnp.zeros_like(basis))
    out_ref[0] = base_b
    term = jnp.dot(base_b, basis, preferred_element_type=F32)

    @pl.when(step == 0)
    def _():
        sketch_ref[...] = term

    @pl.when(step > 0)
    def _():
        sketch_ref[...] += term


def sketch_call(momentum, gradient, basis, share, count):
    rows, cols = momentum.shape
    rank = basis.shape[1]
    last = pl.cdiv(cols, share) - 1
    return pl.pallas_call(
        functools.partial(sketch_kernel, cols),
        grid=(count,),
        in_specs=[
            pl.BlockSpec((rows, share), lambda i: (0, jnp.minimum(i, last))),
            pl.BlockSpec((rows, share), lambda i: (0, jnp.minimum(i, last))),
            pl.BlockSpec((share, rank), lambda i: (jnp.minimum(i, last), 0)),
        ],
        out_specs=[
            pl.BlockSpec((1, rows, share), lambda i: (i, 0, 0)),
            pl.BlockSpec((rows, rank), lambda i: (0, 0)),
        ],
        out_shape=[
            jax.ShapeDtypeStruct((count, rows, share), BF16),
            jax.ShapeDtypeStruct((rows, rank), F32),
        ],
        compiler_params=params(),
        cost_estimate=cost(2 * rows * cols * rank, rows * cols * 8 + cols * rank * 2),
        name="sketch",
    )(momentum, gradient, basis)


def spread(x, lane):
    return jnp.broadcast_to(x[:, lane : lane + 1], (x.shape[0], LANES))


def row_of(x, row):
    return jnp.broadcast_to(x[row : row + 1, :], (SUBLANES, LANES))


def eliminate(block):
    sub = lax.broadcasted_iota(jnp.int32, (SUBLANES, LANES), 0)
    groups = PANEL // SUBLANES
    top = [block[SUBLANES * g : SUBLANES * (g + 1)] for g in range(groups)]
    for g in range(groups):
        first = PANEL + SUBLANES * g
        t = top[g]
        cols = [spread(t, first + j) for j in range(SUBLANES)]
        below = [[spread(top[i], first + j) for j in range(SUBLANES)] for i in range(g + 1, groups)]
        pivots = jnp.zeros((SUBLANES, LANES), F32)
        inverse, corner = [], {}
        for j in range(SUBLANES):
            pivot = row_of(cols[j], j)
            pivots = jnp.where(sub == j, pivot, pivots)
            inverse.append(1.0 / pivot)
            factor = jnp.where(sub > j, cols[j] * inverse[j], 0.0)
            t = t - factor * row_of(t, j)
            for k in range(j + 1, SUBLANES):
                corner[j, k] = row_of(cols[k], j)
                cols[k] = cols[k] - factor * corner[j, k]
        lines = [row_of(t, j) for j in range(SUBLANES)]
        for i in range(g + 1, groups):
            entries = below[i - g - 1]
            acc = top[i]
            for j in range(SUBLANES):
                factor = entries[j] * inverse[j]
                acc = acc - factor * lines[j]
                for k in range(j + 1, SUBLANES):
                    entries[k] = entries[k] - factor * corner[j, k]
            top[i] = acc
        top[g] = t * lax.rsqrt(pivots)
    return jnp.concatenate(top, axis=0)[:, :PANEL]


def dot(a, b, dims):
    return lax.dot_general(a, b, (dims, ((), ())), precision=FULL, preferred_element_type=F32)


def factor_kernel(count, ids_ref, *refs):
    pieces, (ortho_t_ref, here_ref, whole_ref, work_ref) = refs[:count], refs[count:]
    rows, rank = pieces[0].shape
    for n, piece in enumerate(pieces):
        whole_ref[pl.ds(pl.multiple_of(ids_ref[n] * rows, SUBLANES), rows), :] = piece[...]
    total = count * rows

    work_ref[:, :rank] = jnp.zeros((rank, rank), F32)
    chunk = 4 * rows

    @pl.loop(0, total // chunk)
    def _(n):
        part = whole_ref[pl.ds(pl.multiple_of(n * chunk, SUBLANES), chunk), :]
        work_ref[:, :rank] += dot(part, part, ((0,), (0,)))

    line = lax.broadcasted_iota(jnp.int32, (rank, rank), 0)
    column = lax.broadcasted_iota(jnp.int32, (rank, rank), 1)
    work_ref[:, rank:] = jnp.where(line == column, 1.0, 0.0).astype(F32)
    eye = jnp.where(line == column, 1.0, 0.0).astype(F32)[:PANEL, :PANEL]
    for start in range(0, rank, PANEL):
        stop = start + PANEL
        diagonal = work_ref[start:stop, start:stop]
        small = eliminate(jnp.concatenate([eye, diagonal], axis=1))
        panel = dot(small, work_ref[start:stop, :], ((1,), (0,)))
        work_ref[start:stop, :] = panel
        if stop < rank:
            work_ref[stop:, :] -= dot(panel[:, stop:rank], panel, ((0,), (0,)))
    inverse = work_ref[:, rank:]
    here_ref[...] = dot(pieces[0][...], inverse, ((1,), (1,))).astype(BF16)
    for n in range(0, total, chunk):
        ortho_t_ref[:, n : n + chunk] = dot(
            inverse, whole_ref[n : n + chunk, :], ((1,), (1,))
        ).astype(BF16)


def factor_call(ids, pieces):
    count = len(pieces)
    rows, rank = pieces[0].shape
    total = count * rows
    vmem = pl.BlockSpec(memory_space=pltpu.VMEM)
    return pl.pallas_call(
        functools.partial(factor_kernel, count),
        in_specs=[pl.BlockSpec(memory_space=pltpu.SMEM)] + [vmem] * count,
        out_specs=[vmem, vmem],
        out_shape=[
            jax.ShapeDtypeStruct((rank, total), BF16),
            jax.ShapeDtypeStruct((rows, rank), BF16),
        ],
        scratch_shapes=[pltpu.VMEM((total, rank), F32), pltpu.VMEM((rank, 2 * rank), F32)],
        compiler_params=params(),
        cost_estimate=cost(40 * total * rank * rank, total * rank * 6),
        name="factor",
    )(ids, *pieces)


def back_kernel(ortho_t_ref, columns_ref, back_ref, colsq_ref):
    back_t = jnp.dot(ortho_t_ref[...], columns_ref[...], preferred_element_type=F32)
    back = back_t.T.astype(BF16)
    back_ref[...] = back
    wide = back.astype(F32)
    colsq_ref[...] = jnp.sum(wide * wide, axis=0, keepdims=True)


def back_call(ortho_t, columns):
    rank, total = ortho_t.shape
    share = columns.shape[1]
    return pl.pallas_call(
        back_kernel,
        in_specs=[pl.BlockSpec(memory_space=pltpu.VMEM)] * 2,
        out_specs=[pl.BlockSpec(memory_space=pltpu.VMEM)] * 2,
        out_shape=[
            jax.ShapeDtypeStruct((share, rank), BF16),
            jax.ShapeDtypeStruct((1, rank), F32),
        ],
        compiler_params=params(),
        cost_estimate=cost(2 * rank * total * share, total * share * 2),
        name="back",
    )(ortho_t, columns)


def output_kernel(count, factor, carried, ids_ref, m_ref, g_ref, ortho_ref, colsq_ref, *refs):
    pieces, (nm_ref, nb_ref, up_ref) = refs[:count], refs[count + carried :]
    step = pl.program_id(0)
    scale = lax.rsqrt(colsq_ref[...] + 1e-06)
    ortho = ortho_ref[...]
    over = (((1,), (1,)), ((), ()))
    for n, piece in enumerate(pieces):

        @pl.when(step == n)
        def _():
            back = piece[...]
            unit = (back.astype(F32) * scale).astype(BF16)
            nb_ref[...] = unit
            base = m_ref[...] + g_ref[...].astype(F32)
            nm_ref[...] = base - 0.05 * lax.dot_general(
                ortho, back, over, preferred_element_type=F32
            )
            up_ref[...] = (
                factor * lax.dot_general(ortho, unit, over, preferred_element_type=F32)
            ).astype(BF16)


def output_call(ids, momentum, gradient, ortho, colsq, pieces, factor, previous):
    rows, cols = momentum.shape
    share, rank = pieces[0].shape
    count = len(pieces)
    wide = pl.BlockSpec((rows, share), lambda i, ids: (0, ids[i]))
    tall = pl.BlockSpec((share, rank), lambda i, ids: (ids[i], 0))
    carried = 3 if previous else 0
    aliases = {5 + count + n: n for n in range(carried)}
    return pl.pallas_call(
        functools.partial(output_kernel, count, factor, carried),
        grid_spec=pltpu.PrefetchScalarGridSpec(
            num_scalar_prefetch=1,
            grid=(count,),
            in_specs=[
                wide,
                wide,
                pl.BlockSpec((rows, rank), lambda i, ids: (0, 0)),
                pl.BlockSpec((1, rank), lambda i, ids: (0, 0)),
            ]
            + [pl.BlockSpec((share, rank), lambda i, ids: (0, 0))] * count
            + [pl.BlockSpec(memory_space=pl.ANY)] * carried,
            out_specs=[wide, tall, wide],
        ),
        out_shape=[
            jax.ShapeDtypeStruct((rows, cols), F32),
            jax.ShapeDtypeStruct((cols, rank), BF16),
            jax.ShapeDtypeStruct((rows, cols), BF16),
        ],
        input_output_aliases=aliases,
        compiler_params=params(),
        cost_estimate=cost(
            4 * rows * share * rank * count, count * share * (rows * 12 + rank * 4)
        ),
        name="outputs",
    )(ids, momentum, gradient, ortho, colsq, *pieces, *(previous or ()))


def chip_at(position, chips):
    half = chips // 2
    return jnp.where(position < half, 2 * position, 2 * (chips - 1 - position) + 1)


def position_of(chip, chips):
    return jnp.where(chip % 2 == 0, chip // 2, chips - 1 - chip // 2)


def ring_order(chips):
    half = chips // 2
    return [2 * q for q in range(half)] + [2 * (chips - 1 - q) + 1 for q in range(half, chips)]


def ring_steps(count, by_core):
    order = ring_order(count // 2)
    after = dict(zip(order, order[1:] + order[:1]))
    before = {b: a for a, b in after.items()}
    up = [(2 * c + k, 2 * after[c] + k) for c in order for k in (0, 1)]
    down = [(2 * c + k, 2 * before[c] + k) for c in order for k in (0, 1)]
    if not by_core:
        return up, down
    return [p for p in up if p[0] % 2 == 0] + [p for p in down if p[0] % 2 == 1]


def swap_pairs(count):
    return [(n, n ^ 1) for n in range(count)]


def gather_small(x, count):
    chips = count // 2
    me = lax.axis_index("fsdp")
    place, core = position_of(me // 2, chips), me % 2
    up, down = ring_steps(count, False)
    offsets, held = [0], [x]
    ahead = behind = x
    for step in range(1, chips // 2 + 1):
        ahead = lax.ppermute(ahead, "fsdp", up)
        held.append(ahead)
        offsets.append(-step)
        if 2 * step < chips:
            behind = lax.ppermute(behind, "fsdp", down)
            held.append(behind)
            offsets.append(step)
    other = [lax.ppermute(h, "fsdp", swap_pairs(count)) for h in held]
    chip = chip_at((place + jnp.array(offsets, jnp.int32)) % chips, chips)
    ids = jnp.concatenate([2 * chip + core, 2 * chip + 1 - core])
    return held + other, ids.astype(jnp.int32)


def total_of(x, fsdp_count, tp_count):
    if tp_count != 2 or fsdp_count & (fsdp_count - 1):
        return lax.psum(x, ("fsdp", "tp"))
    x = x + lax.ppermute(x, "tp", [(0, 1), (1, 0)])
    bit = 1
    while bit < fsdp_count:
        x = x + lax.ppermute(x, "fsdp", [(n, n ^ bit) for n in range(fsdp_count)])
        bit *= 2
    return x


def local(momentum, gradient, basis):
    rows, cols = momentum.shape
    rank = basis.shape[1]
    count = lax.axis_size("fsdp")
    tp_count = lax.axis_size("tp")
    chips = count // 2
    share = -(-cols // (count * LANES)) * LANES
    factor = math.sqrt(rows * count * cols * tp_count / rank)
    me = lax.axis_index("fsdp")
    ring = count % 4 == 0 and count <= LONGEST_RING and (count - 1) * share < cols

    outgoing, sketch = sketch_call(momentum, gradient, basis, share, count)
    columns = lax.all_to_all(outgoing, "fsdp", 0, 0, tiled=True)
    columns = columns.reshape(rows * count, share)
    if tp_count == 2:
        sketch = sketch + lax.ppermute(sketch, "tp", [(0, 1), (1, 0)])
    else:
        sketch = lax.psum(sketch, "tp")

    if ring:
        pieces, ids = gather_small(sketch, count)
    else:
        whole = lax.all_gather(sketch, "fsdp", axis=0)
        pieces = [lax.dynamic_index_in_dim(whole, (me + n) % count, 0, False) for n in range(count)]
        ids = ((me + jnp.arange(count)) % count).astype(jnp.int32)
    ortho_t, ortho_here = factor_call(ids, pieces)
    back, part = back_call(ortho_t, columns)
    colsq = total_of(part, count, tp_count)

    outputs = functools.partial(output_call, factor=factor)
    if not ring:
        whole = lax.all_gather(back, "fsdp", axis=0)
        valid = -(-cols // share)
        return tuple(
            outputs(
                jnp.arange(valid, dtype=jnp.int32), momentum, gradient, ortho_here, colsq,
                [whole[n] for n in range(valid)], previous=None,
            )
        )

    place, core = position_of(me // 2, chips), me % 2
    turn = ring_steps(count, True)
    swap = swap_pairs(count)
    steps = jnp.arange(chips, dtype=jnp.int32)
    way = 1 - 2 * core
    mine = 2 * chip_at((place - way * steps) % chips, chips) + core
    theirs = 2 * chip_at((place + way * steps) % chips, chips) + 1 - core
    ids = jnp.stack([mine, theirs], axis=1).astype(jnp.int32)
    result, block = None, back
    for step in range(chips):
        if step:
            block = lax.ppermute(block, "fsdp", turn)
        other = lax.ppermute(block, "fsdp", swap)
        result = outputs(
            ids[step], momentum, gradient, ortho_here, colsq, [block, other], previous=result
        )
    return tuple(result)


def solution(mesh):
    return jax.shard_map(
        local,
        mesh=mesh,
        in_specs=(P("fsdp", "tp"), P("fsdp", "tp"), P("tp", None)),
        out_specs=(P("fsdp", "tp"), P("tp", None), P("fsdp", "tp")),
        check_vma=False,
    )
```

time: 256 us -> 224 us (0.88)
  other arithmetic: 62.8 us -> 0.15 us
  starting transfers between devices: 9.76 us -> 70.1 us
  Pallas kernels: 0 us -> 59.5 us
  blocking collectives: 41 us -> 0 us
  matrix products: 23.2 us -> 0 us
  between operations: 15.6 us -> 0.78 us
  waiting for transfers between devices: 91.9 us -> 83.7 us
    all_gather x2 -> x0, waiting for transfers between devices: 89.4 us -> none  [the longest x1 61.3 us: local(): whole = lax.all_gather(sketch, 'fsdp', axis=0, tiled=True)]
    ppermute x0 -> x35, waiting for transfers between devices: none -> 80.6 us  [the longest x4 42.9 us: gather_small(): ahead = lax.ppermute(ahead, 'fsdp', up)]
    ppermute x0 -> x35, starting transfers between devices: none -> 61.4 us  [the longest x4 20.3 us: gather_small(): ahead = lax.ppermute(ahead, 'fsdp', up)]
    pallas_call x0 -> x11, Pallas kernels: none -> 59.5 us  [the longest x8 28.8 us: output_call(): pl.pallas_call(functools.partial(output_kernel, count, factor, carried),...]
    another operation x9 -> x1, other arithmetic: 53.9 us -> 0.01 us  [local(): ids = jnp.stack([mine, theirs], axis=1).astype(jnp.int32)]
    psum x1 -> x0, blocking collectives: 41 us -> none  [local(): colsq = lax.psum(jnp.sum(share_f * share_f, axis=0), ('fsdp', 'tp'))]
    dot_general x5 -> x0, matrix products: 19.6 us -> none  [the longest x1 6.24 us: local(): jnp.dot(ortho_here, back.T, preferred_element_type=jnp.float32)]
    convert_element_type x2 -> x0, other arithmetic: 8.25 us -> none  [the longest x1 4.34 us: local(): new_basis = (back_f * lax.rsqrt(colsq + 1e-06)).astype(jnp.bfloat16)]
  transfers between devices with their start and end apart: 4 -> 37, of which waited for: 3 -> 15; matrix products, arithmetic and copies ran while one was open for 27% -> 0% of each run, Pallas kernels for 0% -> 18%
where the time goes in v2:
time: 224 us; the launch traced here: 223 us
  waiting for transfers between devices  83.7 us (37%)
  starting transfers between devices  70.1 us (31%)
  Pallas kernels  59.5 us (27%)
  local copies, waits for them, and re-layouts  8.79 us (4%)
    ppermute x4, waiting for transfers between devices, gather_small(): ahead = lax.ppermute(ahead, 'fsdp', up)  42.9 us
    ppermute x7, waiting for transfers between devices, local(): block = lax.ppermute(block, 'fsdp', turn)  30.1 us
    pallas_call x8, Pallas kernels, output_call(): pl.pallas_call(functools.partial(output_kernel, count, factor, carried),...  28.8 us
    ppermute x4, starting transfers between devices, gather_small(): ahead = lax.ppermute(ahead, 'fsdp', up)  20.3 us
    pallas_call x1, Pallas kernels, factor_call(): pl.pallas_call(functools.partial(factor_kernel, count), in_specs=[pl.Bloc...  14.7 us
    pallas_call x1, Pallas kernels, sketch_call(): pl.pallas_call(functools.partial(sketch_kernel, cols), grid=(count,), in_...  13 us
    ppermute x7, starting transfers between devices, local(): block = lax.ppermute(block, 'fsdp', turn)  11.7 us
    ppermute x4, starting transfers between devices, total_of(): x = x + lax.ppermute(x, 'fsdp', [(n, n ^ bit) for n in range(fsdp_count)])  10.5 us
  transfers between devices with their start and end apart: 37, of which 15 were waited for; matrix products, arithmetic and copies ran while one was open for 0% of the time, Pallas kernels for 18%

profile of v2, /device:TPU:1, one launch (start us, length us, event | category | flops | bytes accessed | tf_op | source)
XLA Modules:
  0.0 223.0 jit_solution(277155062008647124)
XLA Ops:
  2.4 13.0 %sketch.1 = (bf16[16,96,896]{2,1,0:T(8,128)(2,1)}, f32[96,256]{1,0:T(8,128)S(1)}) custom-call(f32[96,13824]{1,0:T(8,128)} %m_ref.17, bf16[96,13824]{1,0:T(8,128)(2,1)S(1)} %copy-done, bf16[13824,256]{1,0:T(8,128)(2,1)} %b_ref.1), custom_call_target="tpu_custom_call" | custom-call | flops 679477248 | bytes 17694720 | tf_op jit(solution)/shard_map/sketch/pallas_call | solution.py:56
  15.4 7.5 %all-to-all-start = ((bf16[16,96,896]{2,1,0:T(8,128)(2,1)}), bf16[16,96,896]{2,1,0:T(8,128)(2,1)}, u32[]{:S(2)}, u32[]{:S(2)}) async-start(bf16[16,96,896]{2,1,0:T(8,128)(2,1)} %get-tuple-element.33), calls=%async_computation | async-start | bytes 5505024 | tf_op jit(solution)/shard_map/all_to_all | solution.py:336
  24.1 3.1 %collective-permute-done = f32[96,256]{1,0:T(8,128)S(1)} collective-permute-done((f32[96,256]{1,0:T(8,128)S(1)}, f32[96,256]{1,0:T(8,128)S(1)}, u32[]{:S(2)}, u32[]{:S(2)}) %collective-permute-start) | collective-permute-done | bytes 98336 | tf_op jit(solution)/shard_map/ppermute | solution.py:339
  28.7 41.2 %collective-permute-done.1.refs_1_ = f32[96,256]{1,0:T(8,128)S(1)} collective-permute-done((f32[96,256]{1,0:T(8,128)S(1)}, f32[96,256]{1,0:T(8,128)S(1)}, u32[]{:S(2)}, u32[]{:S(2)}) %collective-permute-start.1) | collective-permute-done | bytes 98336 | tf_op jit(solution)/shard_map/ppermute | solution.py:300
  69.9 15.8 %collective-permute-start.3 = (f32[96,256]{1,0:T(8,128)S(1)}, f32[96,256]{1,0:T(8,128)S(1)}, u32[]{:S(2)}, u32[]{:S(2)}) collective-permute-start(f32[96,256]{1,0:T(8,128)S(1)} %collective-permute-done.1.refs_1_), channel_id=1, source_target_pairs={{0,8},{2,10},{8,16},{10,18},{16,24},{18,26},{24,28},{26,30},{28,20... | collective-permute-start | bytes 294920 | tf_op jit(solution)/shard_map/ppermute | solution.py:300
  101.1 14.7 %factor.1 = (bf16[256,1536]{1,0:T(8,128)(2,1)S(1)}, bf16[96,256]{1,0:T(8,128)(2,1)S(1)}) custom-call(s32[16]{0:T(128)S(1)} %pad_add_fusion.1.ids_ref, f32[96,256]{1,0:T(8,128)S(1)} %add.143.refs_0_, f32[96,256]{1,0:T(8,128)S(1)} %collective-permute-done.1.refs_1_, f32[96,256]{1,0:T(8,128)S(1)} %collective-permute-done.2.refs_2_, ...), custom_call_target="tpu_custom_call" | custom-call | flops 4026531840 | bytes 2359296 | tf_op jit(solution)/shard_map/factor/pallas_call | solution.py:164
  115.8 3.0 %back.1 = (bf16[896,256]{1,0:T(8,128)(2,1)S(1)}, f32[1,256]{1,0:T(1,128)S(1)}) custom-call(bf16[256,1536]{1,0:T(8,128)(2,1)S(1)} %get-tuple-element.32.ortho_t_ref, bf16[1536,896]{1,0:T(8,128)(2,1)} %bitcast.columns_ref), custom_call_target="tpu_custom_call" | custom-call | flops 704643072 | bytes 2752512 | tf_op jit(solution)/shard_map/back/pallas_call | solution.py:190
  120.6 5.9 %collective-permute-done.21.refs_0_ = bf16[896,256]{1,0:T(8,128)(2,1)S(1)} collective-permute-done((bf16[896,256]{1,0:T(8,128)(2,1)S(1)}, bf16[896,256]{1,0:T(8,128)(2,1)S(1)}, u32[]{:S(2)}, u32[]{:S(2)}) %collective-permute-start.21) | collective-permute-done | bytes 458784 | tf_op jit(solution)/shard_map/ppermute | solution.py:375
  128.2 5.9 %collective-permute-done.22.refs_0_ = bf16[896,256]{1,0:T(8,128)(2,1)S(1)} collective-permute-done((bf16[896,256]{1,0:T(8,128)(2,1)S(1)}, bf16[896,256]{1,0:T(8,128)(2,1)S(1)}, u32[]{:S(2)}, u32[]{:S(2)}) %collective-permute-start.22) | collective-permute-done | bytes 458784 | tf_op jit(solution)/shard_map/ppermute | solution.py:375
  135.9 6.0 %collective-permute-done.23.refs_0_ = bf16[896,256]{1,0:T(8,128)(2,1)} collective-permute-done((bf16[896,256]{1,0:T(8,128)(2,1)S(1)}, bf16[896,256]{1,0:T(8,128)(2,1)}, u32[]{:S(2)}, u32[]{:S(2)}) %collective-permute-start.23) | collective-permute-done | bytes 458784 | tf_op jit(solution)/shard_map/ppermute | solution.py:375
  143.6 6.2 %collective-permute-done.24.refs_0_ = bf16[896,256]{1,0:T(8,128)(2,1)} collective-permute-done((bf16[896,256]{1,0:T(8,128)(2,1)}, bf16[896,256]{1,0:T(8,128)(2,1)}, u32[]{:S(2)}, u32[]{:S(2)}) %collective-permute-start.24) | collective-permute-done | bytes 458784 | tf_op jit(solution)/shard_map/ppermute | solution.py:375
  151.5 6.2 %collective-permute-done.25.refs_0_ = bf16[896,256]{1,0:T(8,128)(2,1)} collective-permute-done((bf16[896,256]{1,0:T(8,128)(2,1)}, bf16[896,256]{1,0:T(8,128)(2,1)}, u32[]{:S(2)}, u32[]{:S(2)}) %collective-permute-start.25) | collective-permute-done | bytes 458784 | tf_op jit(solution)/shard_map/ppermute | solution.py:375
  159.5 3.5 %collective-permute-start.35 = (bf16[896,256]{1,0:T(8,128)(2,1)S(1)}, bf16[896,256]{1,0:T(8,128)(2,1)S(1)}, u32[]{:S(2)}, u32[]{:S(2)}) collective-permute-start(bf16[896,256]{1,0:T(8,128)(2,1)S(1)} %get-tuple-element.35.refs_0_), channel_id=1, source_target_pairs={{0,2},{2,0},{4,6},{6,4},{8,10},{10,8},{12,14},{14,12},{16,18},{18,... | collective-permute-start | bytes 1376264 | tf_op jit(solution)/shard_map/ppermute | solution.py:376
  169.7 5.6 %collective-permute-start.17 = (f32[1,256]{1,0:T(1,128)S(1)}, f32[1,256]{1,0:T(1,128)S(1)}, u32[]{:S(2)}, u32[]{:S(2)}) collective-permute-start(f32[1,256]{1,0:T(1,128)S(1)} %add.144), channel_id=1, source_target_pairs={{0,2},{2,0},{4,6},{6,4},{8,10},{10,8},{12,14},{14,12},{16,18},{18,... | collective-permute-start | bytes 3080 | tf_op jit(solution)/shard_map/ppermute | solution.py:319
  181.6 2.3 %collective-permute-start.20 = (f32[1,256]{1,0:T(1,128)S(1)}, f32[1,256]{1,0:T(1,128)S(1)}, u32[]{:S(2)}, u32[]{:S(2)}) collective-permute-start(f32[1,256]{1,0:T(1,128)S(1)} %add.147), channel_id=1, source_target_pairs={{0,16},{2,18},{4,20},{6,22},{8,24},{10,26},{12,28},{14,30},{16,0},... | collective-permute-start | bytes 3080 | tf_op jit(solution)/shard_map/ppermute | solution.py:319
  184.9 3.5 %collective-permute-start.32 = (bf16[896,256]{1,0:T(8,128)(2,1)}, bf16[896,256]{1,0:T(8,128)(2,1)}, u32[]{:S(2)}, u32[]{:S(2)}) collective-permute-start(bf16[896,256]{1,0:T(8,128)(2,1)} %collective-permute-done.23.refs_0_), channel_id=1, source_target_pairs={{0,2},{2,0},{4,6},{6,4},{8,10},{10,8},{12,14},{14,12},{16,18},{18,... | collective-permute-start | bytes 1376264 | tf_op jit(solution)/shard_map/ppermute | solution.py:376
  194.2 3.4 %outputs.8 = (f32[96,13824]{1,0:T(8,128)}, bf16[13824,256]{1,0:T(8,128)(2,1)}, bf16[96,13824]{1,0:T(8,128)(2,1)}) custom-call(s32[2]{0:T(128)S(1)} %get-tuple-element.57.ids_ref, f32[96,13824]{1,0:T(8,128)} %m_ref.17, bf16[96,13824]{1,0:T(8,128)(2,1)S(1)} %copy-done.1, bf16[96,256]{1,0:T(8,128)(2,1)S(1)} %get-tuple-element.31.ortho_ref, ...), custom_call_target="tpu_custom_call" | custom-call | flops 176160768 | bytes 3899392 | tf_op jit(solution)/shard_map/outputs/pallas_call | solution.py:234
  197.6 3.4 %outputs.9 = (f32[96,13824]{1,0:T(8,128)}, bf16[13824,256]{1,0:T(8,128)(2,1)}, bf16[96,13824]{1,0:T(8,128)(2,1)}) custom-call(s32[2]{0:T(128)S(1)} %get-tuple-element.58.ids_ref, f32[96,13824]{1,0:T(8,128)} %m_ref.17, bf16[96,13824]{1,0:T(8,128)(2,1)S(1)} %copy-done.1, ...), custom_call_target="tpu_custom_call", output_to_operand_aliasing={{0}: (7, {}), {1}: (8, {}), {2}: (9, {})} | custom-call | flops 176160768 | bytes 3899392 | tf_op jit(solution)/shard_map/outputs/pallas_call | solution.py:234
  201.0 3.4 %outputs.10 = (f32[96,13824]{1,0:T(8,128)}, bf16[13824,256]{1,0:T(8,128)(2,1)}, bf16[96,13824]{1,0:T(8,128)(2,1)}) custom-call(s32[2]{0:T(128)S(1)} %get-tuple-element.59.ids_ref, f32[96,13824]{1,0:T(8,128)} %m_ref.17, bf16[96,13824]{1,0:T(8,128)(2,1)S(1)} %copy-done.1, ...), custom_call_target="tpu_custom_call", output_to_operand_aliasing={{0}: (7, {}), {1}: (8, {}), {2}: (9, {})} | custom-call | flops 176160768 | bytes 3899392 | tf_op jit(solution)/shard_map/outputs/pallas_call | solution.py:234
  204.4 3.7 %outputs.11 = (f32[96,13824]{1,0:T(8,128)}, bf16[13824,256]{1,0:T(8,128)(2,1)}, bf16[96,13824]{1,0:T(8,128)(2,1)}) custom-call(s32[2]{0:T(128)S(1)} %get-tuple-element.60.ids_ref, f32[96,13824]{1,0:T(8,128)} %m_ref.17, bf16[96,13824]{1,0:T(8,128)(2,1)S(1)} %copy-done.1, ...), custom_call_target="tpu_custom_call", output_to_operand_aliasing={{0}: (7, {}), {1}: (8, {}), {2}: (9, {})} | custom-call | flops 176160768 | bytes 3899392 | tf_op jit(solution)/shard_map/outputs/pallas_call | solution.py:234
  208.2 3.7 %outputs.12 = (f32[96,13824]{1,0:T(8,128)}, bf16[13824,256]{1,0:T(8,128)(2,1)}, bf16[96,13824]{1,0:T(8,128)(2,1)}) custom-call(s32[2]{0:T(128)S(1)} %get-tuple-element.61.ids_ref, f32[96,13824]{1,0:T(8,128)} %m_ref.17, bf16[96,13824]{1,0:T(8,128)(2,1)S(1)} %copy-done.1, ...), custom_call_target="tpu_custom_call", output_to_operand_aliasing={{0}: (7, {}), {1}: (8, {}), {2}: (9, {})} | custom-call | flops 176160768 | bytes 3899392 | tf_op jit(solution)/shard_map/outputs/pallas_call | solution.py:234
  211.9 3.7 %outputs.13 = (f32[96,13824]{1,0:T(8,128)}, bf16[13824,256]{1,0:T(8,128)(2,1)}, bf16[96,13824]{1,0:T(8,128)(2,1)}) custom-call(s32[2]{0:T(128)S(1)} %get-tuple-element.62.ids_ref, f32[96,13824]{1,0:T(8,128)} %m_ref.17, bf16[96,13824]{1,0:T(8,128)(2,1)S(1)} %copy-done.1, ...), custom_call_target="tpu_custom_call", output_to_operand_aliasing={{0}: (7, {}), {1}: (8, {}), {2}: (9, {})} | custom-call | flops 176160768 | bytes 3899392 | tf_op jit(solution)/shard_map/outputs/pallas_call | solution.py:234
  215.6 3.6 %outputs.14 = (f32[96,13824]{1,0:T(8,128)}, bf16[13824,256]{1,0:T(8,128)(2,1)}, bf16[96,13824]{1,0:T(8,128)(2,1)}) custom-call(s32[2]{0:T(128)S(1)} %get-tuple-element.63.ids_ref, f32[96,13824]{1,0:T(8,128)} %m_ref.17, bf16[96,13824]{1,0:T(8,128)(2,1)S(1)} %copy-done.1, ...), custom_call_target="tpu_custom_call", output_to_operand_aliasing={{0}: (7, {}), {1}: (8, {}), {2}: (9, {})} | custom-call | flops 176160768 | bytes 3899392 | tf_op jit(solution)/shard_map/outputs/pallas_call | solution.py:234
  219.2 3.7 %outputs.15 = (f32[96,13824]{1,0:T(8,128)}, bf16[13824,256]{1,0:T(8,128)(2,1)}, bf16[96,13824]{1,0:T(8,128)(2,1)}) custom-call(s32[2]{0:T(128)S(1)} %get-tuple-element.64.ids_ref, f32[96,13824]{1,0:T(8,128)} %m_ref.17, bf16[96,13824]{1,0:T(8,128)(2,1)S(1)} %copy-done.1, ...), custom_call_target="tpu_custom_call", output_to_operand_aliasing={{0}: (7, {}), {1}: (8, {}), {2}: (9, {})} | custom-call | flops 176160768 | bytes 3899392 | tf_op jit(solution)/shard_map/outputs/pallas_call | solution.py:234
  (103 shorter events, 50.3 us)
Async XLA Ops:
  15.4 100.4 %all-to-all-start = ((bf16[16,96,896]{2,1,0:T(8,128)(2,1)}), bf16[16,96,896]{2,1,0:T(8,128)(2,1)}, u32[]{:S(2)}, u32[]{:S(2)}) async-start(bf16[16,96,896]{2,1,0:T(8,128)(2,1)} %get-tuple-element.33), calls=%async_computation | async-start | bytes 5505024 | tf_op jit(solution)/shard_map/all_to_all | solution.py:336
  27.2 42.7 %collective-permute-start.1 = (f32[96,256]{1,0:T(8,128)S(1)}, f32[96,256]{1,0:T(8,128)S(1)}, u32[]{:S(2)}, u32[]{:S(2)}) collective-permute-start(f32[96,256]{1,0:T(8,128)S(1)} %add.143.refs_0_), channel_id=1, source_target_pairs={{0,8},{2,10},{8,16},{10,18},{16,24},{18,26},{24,28},{26,30},{28,20... | collective-permute-start | bytes 294920 | tf_op jit(solution)/shard_map/ppermute | solution.py:300
  28.5 57.2 %collective-permute-start.2 = (f32[96,256]{1,0:T(8,128)S(1)}, f32[96,256]{1,0:T(8,128)S(1)}, u32[]{:S(2)}, u32[]{:S(2)}) collective-permute-start(f32[96,256]{1,0:T(8,128)S(1)} %add.143.refs_0_), channel_id=1, source_target_pairs={{0,4},{2,6},{8,0},{10,2},{16,8},{18,10},{24,16},{26,18},{28,24},{3... | collective-permute-start | bytes 294920 | tf_op jit(solution)/shard_map/ppermute | solution.py:304
  69.9 17.4 %collective-permute-start.3 = (f32[96,256]{1,0:T(8,128)S(1)}, f32[96,256]{1,0:T(8,128)S(1)}, u32[]{:S(2)}, u32[]{:S(2)}) collective-permute-start(f32[96,256]{1,0:T(8,128)S(1)} %collective-permute-done.1.refs_1_), channel_id=1, source_target_pairs={{0,8},{2,10},{8,16},{10,18},{16,24},{18,26},{24,28},{26,30},{28,20... | collective-permute-start | bytes 294920 | tf_op jit(solution)/shard_map/ppermute | solution.py:300
  85.7 6.4 %collective-permute-start.4 = (f32[96,256]{1,0:T(8,128)S(1)}, f32[96,256]{1,0:T(8,128)S(1)}, u32[]{:S(2)}, u32[]{:S(2)}) collective-permute-start(f32[96,256]{1,0:T(8,128)S(1)} %collective-permute-done.2.refs_2_), channel_id=1, source_target_pairs={{0,4},{2,6},{8,0},{10,2},{16,8},{18,10},{24,16},{26,18},{28,24},{3... | collective-permute-start | bytes 294920 | tf_op jit(solution)/shard_map/ppermute | solution.py:304
  87.3 5.9 %collective-permute-start.5 = (f32[96,256]{1,0:T(8,128)S(1)}, f32[96,256]{1,0:T(8,128)S(1)}, u32[]{:S(2)}, u32[]{:S(2)}) collective-permute-start(f32[96,256]{1,0:T(8,128)S(1)} %collective-permute-done.3.refs_3_), channel_id=1, source_target_pairs={{0,8},{2,10},{8,16},{10,18},{16,24},{18,26},{24,28},{26,30},{28,20... | collective-permute-start | bytes 294920 | tf_op jit(solution)/shard_map/ppermute | solution.py:300
  92.1 5.2 %collective-permute-start.6 = (f32[96,256]{1,0:T(8,128)S(1)}, f32[96,256]{1,0:T(8,128)S(1)}, u32[]{:S(2)}, u32[]{:S(2)}) collective-permute-start(f32[96,256]{1,0:T(8,128)S(1)} %collective-permute-done.4.refs_4_), channel_id=1, source_target_pairs={{0,4},{2,6},{8,0},{10,2},{16,8},{18,10},{24,16},{26,18},{28,24},{3... | collective-permute-start | bytes 294920 | tf_op jit(solution)/shard_map/ppermute | solution.py:304
  94.3 5.9 %collective-permute-start.11 = (f32[96,256]{1,0:T(8,128)S(1)}, f32[96,256]{1,0:T(8,128)S(1)}, u32[]{:S(2)}, u32[]{:S(2)}) collective-permute-start(f32[96,256]{1,0:T(8,128)S(1)} %collective-permute-done.3.refs_3_), channel_id=1, source_target_pairs={{0,2},{2,0},{4,6},{6,4},{8,10},{10,8},{12,14},{14,12},{16,18},{18,... | collective-permute-start | bytes 294920 | tf_op jit(solution)/shard_map/ppermute | solution.py:307
  118.8 7.7 %collective-permute-start.21 = (bf16[896,256]{1,0:T(8,128)(2,1)S(1)}, bf16[896,256]{1,0:T(8,128)(2,1)S(1)}, u32[]{:S(2)}, u32[]{:S(2)}) collective-permute-start(bf16[896,256]{1,0:T(8,128)(2,1)S(1)} %get-tuple-element.35.refs_0_), channel_id=1, source_target_pairs={{0,8},{8,16},{16,24},{24,28},{28,20},{20,12},{12,4},{4,0},{2,6},{1... | collective-permute-start | bytes 1376264 | tf_op jit(solution)/shard_map/ppermute | solution.py:375
  126.5 7.6 %collective-permute-start.22 = (bf16[896,256]{1,0:T(8,128)(2,1)S(1)}, bf16[896,256]{1,0:T(8,128)(2,1)S(1)}, u32[]{:S(2)}, u32[]{:S(2)}) collective-permute-start(bf16[896,256]{1,0:T(8,128)(2,1)S(1)} %collective-permute-done.21.refs_0_), channel_id=1, source_target_pairs={{0,8},{8,16},{16,24},{24,28},{28,20},{20,12},{12,4},{4,0},{2,6},{1... | collective-permute-start | bytes 1376264 | tf_op jit(solution)/shard_map/ppermute | solution.py:375
  134.1 7.7 %collective-permute-start.23 = (bf16[896,256]{1,0:T(8,128)(2,1)S(1)}, bf16[896,256]{1,0:T(8,128)(2,1)}, u32[]{:S(2)}, u32[]{:S(2)}) collective-permute-start(bf16[896,256]{1,0:T(8,128)(2,1)S(1)} %collective-permute-done.22.refs_0_), channel_id=1, source_target_pairs={{0,8},{8,16},{16,24},{24,28},{28,20},{20,12},{12,4},{4,0},{2,6},{1... | collective-permute-start | bytes 1376264 | tf_op jit(solution)/shard_map/ppermute | solution.py:375
  141.8 7.9 %collective-permute-start.24 = (bf16[896,256]{1,0:T(8,128)(2,1)}, bf16[896,256]{1,0:T(8,128)(2,1)}, u32[]{:S(2)}, u32[]{:S(2)}) collective-permute-start(bf16[896,256]{1,0:T(8,128)(2,1)} %collective-permute-done.23.refs_0_), channel_id=1, source_target_pairs={{0,8},{8,16},{16,24},{24,28},{28,20},{20,12},{12,4},{4,0},{2,6},{1... | collective-permute-start | bytes 1376264 | tf_op jit(solution)/shard_map/ppermute | solution.py:375
  149.8 7.9 %collective-permute-start.25 = (bf16[896,256]{1,0:T(8,128)(2,1)}, bf16[896,256]{1,0:T(8,128)(2,1)}, u32[]{:S(2)}, u32[]{:S(2)}) collective-permute-start(bf16[896,256]{1,0:T(8,128)(2,1)} %collective-permute-done.24.refs_0_), channel_id=1, source_target_pairs={{0,8},{8,16},{16,24},{24,28},{28,20},{20,12},{12,4},{4,0},{2,6},{1... | collective-permute-start | bytes 1376264 | tf_op jit(solution)/shard_map/ppermute | solution.py:375
  157.7 8.2 %collective-permute-start.26 = (bf16[896,256]{1,0:T(8,128)(2,1)}, bf16[896,256]{1,0:T(8,128)(2,1)S(1)}, u32[]{:S(2)}, u32[]{:S(2)}) collective-permute-start(bf16[896,256]{1,0:T(8,128)(2,1)} %collective-permute-done.25.refs_0_), channel_id=1, source_target_pairs={{0,8},{8,16},{16,24},{24,28},{28,20},{20,12},{12,4},{4,0},{2,6},{1... | collective-permute-start | bytes 1376264 | tf_op jit(solution)/shard_map/ppermute | solution.py:375
  159.5 28.9 %collective-permute-start.35 = (bf16[896,256]{1,0:T(8,128)(2,1)S(1)}, bf16[896,256]{1,0:T(8,128)(2,1)S(1)}, u32[]{:S(2)}, u32[]{:S(2)}) collective-permute-start(bf16[896,256]{1,0:T(8,128)(2,1)S(1)} %get-tuple-element.35.refs_0_), channel_id=1, source_target_pairs={{0,2},{2,0},{4,6},{6,4},{8,10},{10,8},{12,14},{14,12},{16,18},{18,... | collective-permute-start | bytes 1376264 | tf_op jit(solution)/shard_map/ppermute | solution.py:376
  163.8 25.4 %collective-permute-start.34 = (bf16[896,256]{1,0:T(8,128)(2,1)S(1)}, bf16[896,256]{1,0:T(8,128)(2,1)S(1)}, u32[]{:S(2)}, u32[]{:S(2)}) collective-permute-start(bf16[896,256]{1,0:T(8,128)(2,1)S(1)} %collective-permute-done.21.refs_0_), channel_id=1, source_target_pairs={{0,2},{2,0},{4,6},{6,4},{8,10},{10,8},{12,14},{14,12},{16,18},{18,... | collective-permute-start | bytes 1376264 | tf_op jit(solution)/shard_map/ppermute | solution.py:376
  164.6 25.9 %collective-permute-start.33 = (bf16[896,256]{1,0:T(8,128)(2,1)S(1)}, bf16[896,256]{1,0:T(8,128)(2,1)S(1)}, u32[]{:S(2)}, u32[]{:S(2)}) collective-permute-start(bf16[896,256]{1,0:T(8,128)(2,1)S(1)} %collective-permute-done.22.refs_0_), channel_id=1, source_target_pairs={{0,2},{2,0},{4,6},{6,4},{8,10},{10,8},{12,14},{14,12},{16,18},{18,... | collective-permute-start | bytes 1376264 | tf_op jit(solution)/shard_map/ppermute | solution.py:376
  165.9 25.4 %collective-permute-start.27 = (bf16[896,256]{1,0:T(8,128)(2,1)S(1)}, bf16[896,256]{1,0:T(8,128)(2,1)}, u32[]{:S(2)}, u32[]{:S(2)}) collective-permute-start(bf16[896,256]{1,0:T(8,128)(2,1)S(1)} %collective-permute-done.26.refs_0_), channel_id=1, source_target_pairs={{0,8},{8,16},{16,24},{24,28},{28,20},{20,12},{12,4},{4,0},{2,6},{1... | collective-permute-start | bytes 1376264 | tf_op jit(solution)/shard_map/ppermute | solution.py:375
  169.7 6.4 %collective-permute-start.17 = (f32[1,256]{1,0:T(1,128)S(1)}, f32[1,256]{1,0:T(1,128)S(1)}, u32[]{:S(2)}, u32[]{:S(2)}) collective-permute-start(f32[1,256]{1,0:T(1,128)S(1)} %add.144), channel_id=1, source_target_pairs={{0,2},{2,0},{4,6},{6,4},{8,10},{10,8},{12,14},{14,12},{16,18},{18,... | collective-permute-start | bytes 3080 | tf_op jit(solution)/shard_map/ppermute | solution.py:319
  184.9 19.5 %collective-permute-start.32 = (bf16[896,256]{1,0:T(8,128)(2,1)}, bf16[896,256]{1,0:T(8,128)(2,1)}, u32[]{:S(2)}, u32[]{:S(2)}) collective-permute-start(bf16[896,256]{1,0:T(8,128)(2,1)} %collective-permute-done.23.refs_0_), channel_id=1, source_target_pairs={{0,2},{2,0},{4,6},{6,4},{8,10},{10,8},{12,14},{14,12},{16,18},{18,... | collective-permute-start | bytes 1376264 | tf_op jit(solution)/shard_map/ppermute | solution.py:376
  189.2 19.0 %collective-permute-start.31 = (bf16[896,256]{1,0:T(8,128)(2,1)}, bf16[896,256]{1,0:T(8,128)(2,1)}, u32[]{:S(2)}, u32[]{:S(2)}) collective-permute-start(bf16[896,256]{1,0:T(8,128)(2,1)} %collective-permute-done.24.refs_0_), channel_id=1, source_target_pairs={{0,2},{2,0},{4,6},{6,4},{8,10},{10,8},{12,14},{14,12},{16,18},{18,... | collective-permute-start | bytes 1376264 | tf_op jit(solution)/shard_map/ppermute | solution.py:376
  190.0 21.9 %collective-permute-start.30 = (bf16[896,256]{1,0:T(8,128)(2,1)}, bf16[896,256]{1,0:T(8,128)(2,1)}, u32[]{:S(2)}, u32[]{:S(2)}) collective-permute-start(bf16[896,256]{1,0:T(8,128)(2,1)} %collective-permute-done.25.refs_0_), channel_id=1, source_target_pairs={{0,2},{2,0},{4,6},{6,4},{8,10},{10,8},{12,14},{14,12},{16,18},{18,... | collective-permute-start | bytes 1376264 | tf_op jit(solution)/shard_map/ppermute | solution.py:376
  191.3 24.4 %collective-permute-start.29 = (bf16[896,256]{1,0:T(8,128)(2,1)S(1)}, bf16[896,256]{1,0:T(8,128)(2,1)}, u32[]{:S(2)}, u32[]{:S(2)}) collective-permute-start(bf16[896,256]{1,0:T(8,128)(2,1)S(1)} %collective-permute-done.26.refs_0_), channel_id=1, source_target_pairs={{0,2},{2,0},{4,6},{6,4},{8,10},{10,8},{12,14},{14,12},{16,18},{18,... | collective-permute-start | bytes 1376264 | tf_op jit(solution)/shard_map/ppermute | solution.py:376
  191.3 28.0 %collective-permute-start.28 = (bf16[896,256]{1,0:T(8,128)(2,1)}, bf16[896,256]{1,0:T(8,128)(2,1)}, u32[]{:S(2)}, u32[]{:S(2)}) collective-permute-start(bf16[896,256]{1,0:T(8,128)(2,1)} %collective-permute-done.27.refs_0_), channel_id=1, source_target_pairs={{0,2},{2,0},{4,6},{6,4},{8,10},{10,8},{12,14},{14,12},{16,18},{18,... | collective-permute-start | bytes 1376264 | tf_op jit(solution)/shard_map/ppermute | solution.py:376
  (28 other events, 223.5 us)

commit v3 on v2

--- a/solution.py
+++ b/solution.py
@@ -11,8 +11,7 @@
 LANES = 128
 SUBLANES = 8
 PANEL = 64
-LONGEST_RING = 32
-VMEM_LIMIT = 48 * 1024 * 1024
+MIB = 1024 * 1024
 FULL = lax.Precision.HIGHEST
 F32 = jnp.float32
 BF16 = jnp.bfloat16
@@ -22,57 +21,78 @@
     return pl.CostEstimate(flops=flops, bytes_accessed=nbytes, transcendentals=0)
 
 
-def params():
-    return pltpu.CompilerParams(vmem_limit_bytes=VMEM_LIMIT)
-
-
-def sketch_kernel(cols, m_ref, g_ref, b_ref, out_ref, sketch_ref):
+def params(mib):
+    return pltpu.CompilerParams(vmem_limit_bytes=mib * MIB)
+
+
+def tile_of(cols, most):
+    tiles = cols // LANES
+    return LANES * max(d for d in range(1, most // LANES + 1) if tiles % d == 0)
+
+
+def sketch_kernel(m_ref, g_ref, b_ref, sketch_ref):
+    base_b = (m_ref[...] + g_ref[...].astype(F32)).astype(BF16)
+    term = jnp.dot(base_b, b_ref[...], preferred_element_type=F32)
+
+    @pl.when(pl.program_id(0) == 0)
+    def _():
+        sketch_ref[...] = term
+
+    @pl.when(pl.program_id(0) > 0)
+    def _():
+        sketch_ref[...] += term
+
+
+def sketch_call(momentum, gradient, basis):
+    rows, cols = momentum.shape
+    rank = basis.shape[1]
+    tile = tile_of(cols, 1536)
+    return pl.pallas_call(
+        sketch_kernel,
+        grid=(cols // tile,),
+        in_specs=[
+            pl.BlockSpec((rows, tile), lambda i: (0, i)),
+            pl.BlockSpec((rows, tile), lambda i: (0, i)),
+            pl.BlockSpec((tile, rank), lambda i: (i, 0)),
+        ],
+        out_specs=pl.BlockSpec((rows, rank), lambda i: (0, 0)),
+        out_shape=jax.ShapeDtypeStruct((rows, rank), F32),
+        compiler_params=params(60),
+        cost_estimate=cost(2 * rows * cols * rank, rows * cols * 6 + cols * rank * 2),
+        name="sketch",
+    )(momentum, gradient, basis)
+
+
+def pack_kernel(cols, m_ref, g_ref, after_ref, out_ref):
     step = pl.program_id(0)
     share = m_ref.shape[1]
     left = cols - step * share
-    base_b = (m_ref[...] + g_ref[...].astype(F32)).astype(BF16)
-    basis = b_ref[...]
-    if cols % share:
-        lane = lax.broadcasted_iota(jnp.int32, base_b.shape, 1)
-        base_b = jnp.where(lane < left, base_b, jnp.zeros_like(base_b))
-        row = lax.broadcasted_iota(jnp.int32, basis.shape, 0)
-        basis = jnp.where(row < left, basis, jnp.zeros_like(basis))
-    out_ref[0] = base_b
-    term = jnp.dot(base_b, basis, preferred_element_type=F32)
-
-    @pl.when(step == 0)
+
+    @pl.when(left >= share)
     def _():
-        sketch_ref[...] = term
-
-    @pl.when(step > 0)
+        out_ref[0] = (m_ref[...] + g_ref[...].astype(F32)).astype(BF16)
+
+    @pl.when(left < share)
     def _():
-        sketch_ref[...] += term
-
-
-def sketch_call(momentum, gradient, basis, share, count):
+        lane = lax.broadcasted_iota(jnp.int32, m_ref.shape, 1)
+        base = m_ref[...] + g_ref[...].astype(F32)
+        out_ref[0] = jnp.where(lane < left, base, 0.0).astype(BF16)
+
+
+def pack_call(momentum, gradient, share, count, after):
     rows, cols = momentum.shape
-    rank = basis.shape[1]
     last = pl.cdiv(cols, share) - 1
+    block = pl.BlockSpec((rows, share), lambda i: (0, jnp.minimum(i, last)))
     return pl.pallas_call(
-        functools.partial(sketch_kernel, cols),
+        functools.partial(pack_kernel, cols),
         grid=(count,),
-        in_specs=[
-            pl.BlockSpec((rows, share), lambda i: (0, jnp.minimum(i, last))),
-            pl.BlockSpec((rows, share), lambda i: (0, jnp.minimum(i, last))),
-            pl.BlockSpec((share, rank), lambda i: (jnp.minimum(i, last), 0)),
-        ],
-        out_specs=[
-            pl.BlockSpec((1, rows, share), lambda i: (i, 0, 0)),
-            pl.BlockSpec((rows, rank), lambda i: (0, 0)),
-        ],
-        out_shape=[
-            jax.ShapeDtypeStruct((count, rows, share), BF16),
-            jax.ShapeDtypeStruct((rows, rank), F32),
-        ],
-        compiler_params=params(),
-        cost_estimate=cost(2 * rows * cols * rank, rows * cols * 8 + cols * rank * 2),
-        name="sketch",
-    )(momentum, gradient, basis)
+        in_specs=[block, block, pl.BlockSpec(memory_space=pl.ANY)],
+        out_specs=pl.BlockSpec((1, rows, share), lambda i: (i, 0, 0)),
+        out_shape=jax.ShapeDtypeStruct((count, rows, share), BF16),
+        compiler_params=params(48),
+        cost_estimate=cost(rows * cols, rows * cols * 8),
+        name="pack",
+    )(momentum, gradient, after)
 
 
 def spread(x, lane):
@@ -170,7 +190,7 @@
             jax.ShapeDtypeStruct((rows, rank), BF16),
         ],
         scratch_shapes=[pltpu.VMEM((total, rank), F32), pltpu.VMEM((rank, 2 * rank), F32)],
-        compiler_params=params(),
+        compiler_params=params(24),
         cost_estimate=cost(40 * total * rank * rank, total * rank * 6),
         name="factor",
     )(ids, *pieces)
@@ -195,7 +215,7 @@
             jax.ShapeDtypeStruct((share, rank), BF16),
             jax.ShapeDtypeStruct((1, rank), F32),
         ],
-        compiler_params=params(),
+        compiler_params=params(24),
         cost_estimate=cost(2 * rank * total * share, total * share * 2),
         name="back",
     )(ortho_t, columns)
@@ -252,7 +272,7 @@
             jax.ShapeDtypeStruct((rows, cols), BF16),
         ],
         input_output_aliases=aliases,
-        compiler_params=params(),
+        compiler_params=params(32),
         cost_estimate=cost(
             4 * rows * share * rank * count, count * share * (rows * 12 + rank * 4)
         ),
@@ -310,15 +330,17 @@
     return held + other, ids.astype(jnp.int32)
 
 
-def total_of(x, fsdp_count, tp_count):
-    if tp_count != 2 or fsdp_count & (fsdp_count - 1):
-        return lax.psum(x, ("fsdp", "tp"))
-    x = x + lax.ppermute(x, "tp", [(0, 1), (1, 0)])
+def tie(x, *work):
+    return lax.optimization_barrier((x, *work))[0] if work else x
+
+
+def sum_rounds(count, tp_count):
+    rounds = [("tp", [(0, 1), (1, 0)])]
     bit = 1
-    while bit < fsdp_count:
-        x = x + lax.ppermute(x, "fsdp", [(n, n ^ bit) for n in range(fsdp_count)])
+    while bit < count:
+        rounds.append(("fsdp", [(n, n ^ bit) for n in range(count)]))
         bit *= 2
-    return x
+    return rounds
 
 
 def local(momentum, gradient, basis):
@@ -330,11 +352,9 @@
     share = -(-cols // (count * LANES)) * LANES
     factor = math.sqrt(rows * count * cols * tp_count / rank)
     me = lax.axis_index("fsdp")
-    ring = count % 4 == 0 and count <= LONGEST_RING and (count - 1) * share < cols
-
-    outgoing, sketch = sketch_call(momentum, gradient, basis, share, count)
-    columns = lax.all_to_all(outgoing, "fsdp", 0, 0, tiled=True)
-    columns = columns.reshape(rows * count, share)
+    ring = tp_count == 2 and count in (4, 8, 16, 32) and (count - 1) * share < cols
+
+    sketch = sketch_call(momentum, gradient, basis)
     if tp_count == 2:
         sketch = sketch + lax.ppermute(sketch, "tp", [(0, 1), (1, 0)])
     else:
@@ -346,12 +366,15 @@
         whole = lax.all_gather(sketch, "fsdp", axis=0)
         pieces = [lax.dynamic_index_in_dim(whole, (me + n) % count, 0, False) for n in range(count)]
         ids = ((me + jnp.arange(count)) % count).astype(jnp.int32)
+    outgoing = pack_call(momentum, gradient, share, count, pieces[min(4, count - 1)])
+    columns = lax.all_to_all(outgoing, "fsdp", 0, 0, tiled=True)
+    columns = columns.reshape(rows * count, share)
     ortho_t, ortho_here = factor_call(ids, pieces)
     back, part = back_call(ortho_t, columns)
-    colsq = total_of(part, count, tp_count)
 
     outputs = functools.partial(output_call, factor=factor)
     if not ring:
+        colsq = lax.psum(part, ("fsdp", "tp"))
         whole = lax.all_gather(back, "fsdp", axis=0)
         valid = -(-cols // share)
         return tuple(
@@ -369,13 +392,30 @@
     mine = 2 * chip_at((place - way * steps) % chips, chips) + core
     theirs = 2 * chip_at((place + way * steps) % chips, chips) + 1 - core
     ids = jnp.stack([mine, theirs], axis=1).astype(jnp.int32)
-    result, block = None, back
+    rounds = sum_rounds(count, tp_count)
+    colsq, result = part, None
+    blocks, others = [back], []
+    written = 0
+    waiting = ()
     for step in range(chips):
-        if step:
-            block = lax.ppermute(block, "fsdp", turn)
-        other = lax.ppermute(block, "fsdp", swap)
+        if step + 1 < chips:
+            blocks.append(lax.ppermute(tie(blocks[step], *waiting), "fsdp", turn))
+        others.append(lax.ppermute(blocks[step], "fsdp", swap))
+        for axis, pairs in rounds[:2]:
+            colsq = colsq + lax.ppermute(colsq, axis, pairs)
+        done, rounds = not rounds, rounds[2:]
+        waiting = (colsq,)
+        if done and step > written + 1:
+            ready = slice(written, min(written + 2, step))
+            written = ready.stop
+            result = outputs(
+                ids[ready].reshape(-1), momentum, gradient, ortho_here, colsq,
+                [x for pair in zip(blocks[ready], others[ready]) for x in pair], previous=result,
+            )
+            waiting = tuple(result)
+    for n in range(written, chips):
         result = outputs(
-            ids[step], momentum, gradient, ortho_here, colsq, [block, other], previous=result
+            ids[n], momentum, gradient, ortho_here, colsq, [blocks[n], others[n]], previous=result
         )
     return tuple(result)
 

time: 224 us -> 228 us (1.018)
  local copies, waits for them, and re-layouts: 8.79 us -> 16 us
  starting transfers between devices: 70.1 us -> 63.1 us
    ppermute x20, starting transfers between devices: 32 us -> 20 us  [the longest x7 9.51 us: local(): blocks.append(lax.ppermute(tie(blocks[step], *waiting), 'fsdp', turn))]
    unnamed x30 -> x36, local copies, waits for them, and re-layouts: 8.5 us -> 15.2 us
    ppermute x20, waiting for transfers between devices: 36.2 us -> 29.7 us  [the longest x7 17.2 us: local(): blocks.append(lax.ppermute(tie(blocks[step], *waiting), 'fsdp', turn))]
    pallas_call x1 -> x2, Pallas kernels: 13 us -> 18 us  [the longest x1 9.52 us: sketch_call(): pl.pallas_call(sketch_kernel, grid=(cols // tile,), in_specs=[pl.BlockSpe...]
    pallas_call x8 -> x5, Pallas kernels: 28.8 us -> 23.8 us  [output_call(): pl.pallas_call(functools.partial(output_kernel, count, factor, carried),...]
    ppermute x4, waiting for transfers between devices: 42.9 us -> 47.3 us  [gather_small(): ahead = lax.ppermute(ahead, 'fsdp', up)]
    ppermute x3, waiting for transfers between devices: 0.67 us -> 4.98 us  [gather_small(): behind = lax.ppermute(behind, 'fsdp', down)]
    all_to_all x1, starting transfers between devices: 7.49 us -> 9.84 us  [local(): columns = lax.all_to_all(outgoing, 'fsdp', 0, 0, tiled=True)]
  transfers between devices with their start and end apart: 37 -> 37, of which waited for: 15 -> 15; matrix products, arithmetic and copies ran while one was open for 0% -> 0% of each run, Pallas kernels for 18% -> 15%
where the time goes in v3:
time: 228 us; the launch traced here: 227 us
  waiting for transfers between devices  85.6 us (38%)
  starting transfers between devices  63.1 us (28%)
  Pallas kernels  60.1 us (26%)
  local copies, waits for them, and re-layouts  16 us (7%)
    ppermute x4, waiting for transfers between devices, gather_small(): ahead = lax.ppermute(ahead, 'fsdp', up)  47.3 us
    pallas_call x5, Pallas kernels, output_call(): pl.pallas_call(functools.partial(output_kernel, count, factor, carried),...  23.8 us
    ppermute x4, starting transfers between devices, gather_small(): ahead = lax.ppermute(ahead, 'fsdp', up)  20.3 us
    ppermute x7, waiting for transfers between devices, local(): blocks.append(lax.ppermute(tie(blocks[step], *waiting), 'fsdp', turn))  17.2 us
    unnamed x36, local copies, waits for them, and re-layouts  15.2 us
    pallas_call x1, Pallas kernels, factor_call(): pl.pallas_call(functools.partial(factor_kernel, count), in_specs=[pl.Bloc...  14.7 us
    ppermute x5, waiting for transfers between devices, local(): colsq = colsq + lax.ppermute(colsq, axis, pairs)  12.5 us
    all_to_all x1, starting transfers between devices, local(): columns = lax.all_to_all(outgoing, 'fsdp', 0, 0, tiled=True)  9.84 us
  transfers between devices with their start and end apart: 37, of which 15 were waited for; matrix products, arithmetic and copies ran while one was open for 0% of the time, Pallas kernels for 15%

profile of v3, /device:TPU:1, one launch (start us, length us, event | category | flops | bytes accessed | tf_op | source)
XLA Modules:
  0.0 226.6 jit_solution(4201473692402082626)
XLA Ops:
  0.6 9.5 %sketch.1 = f32[96,256]{1,0:T(8,128)} custom-call(f32[96,13824]{1,0:T(8,128)} %m_ref.13, bf16[96,13824]{1,0:T(8,128)(2,1)} %g_ref.13, bf16[13824,256]{1,0:T(8,128)(2,1)} %b_ref.1), custom_call_target="tpu_custom_call" | custom-call | flops 679477248 | bytes 15040512 | tf_op jit(solution)/shard_map/sketch/pallas_call | solution.py:50
  12.2 2.7 %collective-permute-done = f32[96,256]{1,0:T(8,128)S(1)} collective-permute-done((f32[96,256]{1,0:T(8,128)}, f32[96,256]{1,0:T(8,128)S(1)}, u32[]{:S(2)}, u32[]{:S(2)}) %collective-permute-start) | collective-permute-done | bytes 98336 | tf_op jit(solution)/shard_map/ppermute | solution.py:359
  16.9 2.5 %collective-permute-done.2.refs_2_ = f32[96,256]{1,0:T(8,128)S(1)} collective-permute-done((f32[96,256]{1,0:T(8,128)S(1)}, f32[96,256]{1,0:T(8,128)S(1)}, u32[]{:S(2)}, u32[]{:S(2)}) %collective-permute-start.2) | collective-permute-done | bytes 98336 | tf_op jit(solution)/shard_map/ppermute | solution.py:324
  20.3 2.5 %collective-permute-done.4.refs_4_.after_ref = f32[96,256]{1,0:T(8,128)S(1)} collective-permute-done((f32[96,256]{1,0:T(8,128)S(1)}, f32[96,256]{1,0:T(8,128)S(1)}, u32[]{:S(2)}, u32[]{:S(2)}) %collective-permute-start.4) | collective-permute-done | bytes 98336 | tf_op jit(solution)/shard_map/ppermute | solution.py:324
  22.8 8.5 %pack.1 = bf16[16,96,896]{2,1,0:T(8,128)(2,1)S(1)} custom-call(f32[96,13824]{1,0:T(8,128)} %m_ref.13, bf16[96,13824]{1,0:T(8,128)(2,1)S(1)} %copy-done.3, f32[96,256]{1,0:T(8,128)S(1)} %collective-permute-done.4.refs_4_.after_ref), custom_call_target="tpu_custom_call" | custom-call | flops 1327104 | bytes 10616832 | tf_op jit(solution)/shard_map/pack/pallas_call | solution.py:86
  32.9 9.8 %all-to-all-start = ((bf16[16,96,896]{2,1,0:T(8,128)(2,1)}), bf16[16,96,896]{2,1,0:T(8,128)(2,1)}, u32[]{:S(2)}, u32[]{:S(2)}) async-start(bf16[16,96,896]{2,1,0:T(8,128)(2,1)} %copy-done.4), calls=%async_computation | async-start | bytes 5505024 | tf_op jit(solution)/shard_map/all_to_all | solution.py:370
  44.1 45.7 %collective-permute-done.1.refs_1_ = f32[96,256]{1,0:T(8,128)S(1)} collective-permute-done((f32[96,256]{1,0:T(8,128)S(1)}, f32[96,256]{1,0:T(8,128)S(1)}, u32[]{:S(2)}, u32[]{:S(2)}) %collective-permute-start.1) | collective-permute-done | bytes 98336 | tf_op jit(solution)/shard_map/ppermute | solution.py:320
  89.8 15.8 %collective-permute-start.3 = (f32[96,256]{1,0:T(8,128)S(1)}, f32[96,256]{1,0:T(8,128)S(1)}, u32[]{:S(2)}, u32[]{:S(2)}) collective-permute-start(f32[96,256]{1,0:T(8,128)S(1)} %collective-permute-done.1.refs_1_), channel_id=1, source_target_pairs={{0,8},{2,10},{8,16},{10,18},{16,24},{18,26},{24,28},{26,30},{28,20... | collective-permute-start | bytes 294920 | tf_op jit(solution)/shard_map/ppermute | solution.py:320
  125.4 14.7 %factor.1 = (bf16[256,1536]{1,0:T(8,128)(2,1)S(1)}, bf16[96,256]{1,0:T(8,128)(2,1)S(1)}) custom-call(s32[16]{0:T(128)S(1)} %pad_add_fusion.1.ids_ref, f32[96,256]{1,0:T(8,128)S(1)} %copy-done.10, f32[96,256]{1,0:T(8,128)S(1)} %copy-done.14, f32[96,256]{1,0:T(8,128)S(1)} %copy-done.12, f32[96,256]{1,0:T(8,128)S(1)} %copy-done.16, f32[96,256]{1,0:T(8,128)S(1)} %copy-done.8, ...), custom_call_target="tpu_custom_call" | custom-call | flops 4026531840 | bytes 2359296 | tf_op jit(solution)/shard_map/factor/pallas_call | solution.py:184
  140.1 3.6 %back.1 = (bf16[896,256]{1,0:T(8,128)(2,1)}, f32[1,256]{1,0:T(1,128)S(1)}) custom-call(bf16[256,1536]{1,0:T(8,128)(2,1)S(1)} %get-tuple-element.26.ortho_t_ref, bf16[1536,896]{1,0:T(8,128)(2,1)} %bitcast.columns_ref), custom_call_target="tpu_custom_call" | custom-call | flops 704643072 | bytes 2752512 | tf_op jit(solution)/shard_map/back/pallas_call | solution.py:210
  155.1 4.0 %collective-permute-done.18 = f32[1,256]{1,0:T(1,128)S(1)} collective-permute-done((f32[1,256]{1,0:T(1,128)S(1)}, f32[1,256]{1,0:T(1,128)S(1)}, u32[]{:S(2)}, u32[]{:S(2)}) %collective-permute-start.18) | collective-permute-done | bytes 1056 | tf_op jit(solution)/shard_map/ppermute | solution.py:405
  159.1 2.4 %collective-permute-done.19 = f32[1,256]{1,0:T(1,128)S(1)} collective-permute-done((f32[1,256]{1,0:T(1,128)S(1)}, f32[1,256]{1,0:T(1,128)S(1)}, u32[]{:S(2)}, u32[]{:S(2)}) %collective-permute-start.19) | collective-permute-done | bytes 1056 | tf_op jit(solution)/shard_map/ppermute | solution.py:405
  165.4 3.3 %collective-permute-done.20 = f32[1,256]{1,0:T(1,128)S(1)} collective-permute-done((f32[1,256]{1,0:T(1,128)S(1)}, f32[1,256]{1,0:T(1,128)S(1)}, u32[]{:S(2)}, u32[]{:S(2)}) %collective-permute-start.20) | collective-permute-done | bytes 1056 | tf_op jit(solution)/shard_map/ppermute | solution.py:405
  171.7 2.4 %collective-permute-start.28 = (bf16[896,256]{1,0:T(8,128)(2,1)}, bf16[896,256]{1,0:T(8,128)(2,1)}, u32[]{:S(2)}, u32[]{:S(2)}) collective-permute-start(bf16[896,256]{1,0:T(8,128)(2,1)} %copy-done.5), channel_id=1, source_target_pairs={{0,2},{2,0},{4,6},{6,4},{8,10},{10,8},{12,14},{14,12},{16,18},{18,... | collective-permute-start | bytes 1376264 | tf_op jit(solution)/shard_map/ppermute | solution.py:403
  174.2 2.5 %copy-done = f32[96,13824]{1,0:T(8,128)S(1)} copy-done((f32[96,13824]{1,0:T(8,128)S(1)}, f32[96,13824]{1,0:T(8,128)}, u32[]{:S(2)}) %copy-start) | copy-done | bytes 5308440
  176.7 5.5 %outputs.5 = (f32[96,13824]{1,0:T(8,128)}, bf16[13824,256]{1,0:T(8,128)(2,1)}, bf16[96,13824]{1,0:T(8,128)(2,1)}) custom-call(s32[4]{0:T(128)S(1)} %reshape.150.ids_ref, f32[96,13824]{1,0:T(8,128)S(1)} %copy-done, bf16[96,13824]{1,0:T(8,128)(2,1)S(1)} %copy-done.3, bf16[96,256]{1,0:T(8,128)(2,1)S(1)} %get-tuple-element.25.ortho_ref, ...), custom_call_target="tpu_custom_call" | custom-call | flops 352321536 | bytes 7798784 | tf_op jit(solution)/shard_map/outputs/pallas_call | solution.py:254
  184.2 2.5 %copy-done.1 = f32[96,13824]{1,0:T(8,128)S(1)} copy-done((f32[96,13824]{1,0:T(8,128)S(1)}, f32[96,13824]{1,0:T(8,128)}, u32[]{:S(2)}) %copy-start.1) | copy-done | bytes 5308440
  187.7 5.4 %outputs.6 = (f32[96,13824]{1,0:T(8,128)}, bf16[13824,256]{1,0:T(8,128)(2,1)}, bf16[96,13824]{1,0:T(8,128)(2,1)}) custom-call(s32[4]{0:T(128)S(1)} %reshape.151.ids_ref, f32[96,13824]{1,0:T(8,128)S(1)} %copy-done.1, bf16[96,13824]{1,0:T(8,128)(2,1)S(1)} %copy-done.3, ...), custom_call_target="tpu_custom_call", output_to_operand_aliasing={{0}: (9, {}), {1}: (10, {}), {2}: (11, {})} | custom-call | flops 352321536 | bytes 7798784 | tf_op jit(solution)/shard_map/outputs/pallas_call | solution.py:254
  193.1 7.9 %collective-permute-done.30.refs_0_ = bf16[896,256]{1,0:T(8,128)(2,1)} collective-permute-done((bf16[896,256]{1,0:T(8,128)(2,1)}, bf16[896,256]{1,0:T(8,128)(2,1)}, u32[]{:S(2)}, u32[]{:S(2)}) %collective-permute-start.30) | collective-permute-done | bytes 458784 | tf_op jit(solution)/shard_map/ppermute | solution.py:402
  202.5 6.4 %collective-permute-done.31.refs_0_ = bf16[896,256]{1,0:T(8,128)(2,1)} collective-permute-done((bf16[896,256]{1,0:T(8,128)(2,1)}, bf16[896,256]{1,0:T(8,128)(2,1)}, u32[]{:S(2)}, u32[]{:S(2)}) %collective-permute-start.31) | collective-permute-done | bytes 458784 | tf_op jit(solution)/shard_map/ppermute | solution.py:402
  211.2 2.5 %copy-done.2 = f32[96,13824]{1,0:T(8,128)S(1)} copy-done((f32[96,13824]{1,0:T(8,128)S(1)}, f32[96,13824]{1,0:T(8,128)}, u32[]{:S(2)}) %copy-start.2) | copy-done | bytes 5308440
  213.7 5.4 %outputs.7 = (f32[96,13824]{1,0:T(8,128)}, bf16[13824,256]{1,0:T(8,128)(2,1)}, bf16[96,13824]{1,0:T(8,128)(2,1)}) custom-call(s32[4]{0:T(128)S(1)} %reshape.152.ids_ref, f32[96,13824]{1,0:T(8,128)S(1)} %copy-done.2, bf16[96,13824]{1,0:T(8,128)(2,1)S(1)} %copy-done.3, ...), custom_call_target="tpu_custom_call", output_to_operand_aliasing={{0}: (9, {}), {1}: (10, {}), {2}: (11, {})} | custom-call | flops 352321536 | bytes 7798784 | tf_op jit(solution)/shard_map/outputs/pallas_call | solution.py:254
  219.1 3.8 %outputs.8 = (f32[96,13824]{1,0:T(8,128)}, bf16[13824,256]{1,0:T(8,128)(2,1)}, bf16[96,13824]{1,0:T(8,128)(2,1)}) custom-call(s32[2]{0:T(128)S(1)} %get-tuple-element.47.ids_ref, f32[96,13824]{1,0:T(8,128)S(1)} %copy-done.2, bf16[96,13824]{1,0:T(8,128)(2,1)S(1)} %copy-done.3, ...), custom_call_target="tpu_custom_call", output_to_operand_aliasing={{0}: (7, {}), {1}: (8, {}), {2}: (9, {})} | custom-call | flops 176160768 | bytes 3899392 | tf_op jit(solution)/shard_map/outputs/pallas_call | solution.py:254
  222.9 3.8 %outputs.9 = (f32[96,13824]{1,0:T(8,128)}, bf16[13824,256]{1,0:T(8,128)(2,1)}, bf16[96,13824]{1,0:T(8,128)(2,1)}) custom-call(s32[2]{0:T(128)S(1)} %get-tuple-element.48.ids_ref, f32[96,13824]{1,0:T(8,128)S(1)} %copy-done.2, bf16[96,13824]{1,0:T(8,128)(2,1)S(1)} %copy-done.3, ...), custom_call_target="tpu_custom_call", output_to_operand_aliasing={{0}: (7, {}), {1}: (8, {}), {2}: (9, {})} | custom-call | flops 176160768 | bytes 3899392 | tf_op jit(solution)/shard_map/outputs/pallas_call | solution.py:254
  (114 shorter events, 52.8 us)
Async XLA Ops:
  10.2 4.8 %collective-permute-start = (f32[96,256]{1,0:T(8,128)}, f32[96,256]{1,0:T(8,128)S(1)}, u32[]{:S(2)}, u32[]{:S(2)}) collective-permute-start(f32[96,256]{1,0:T(8,128)} %sketch.1), channel_id=1, source_target_pairs={{0,1},{1,0},{2,3},{3,2},{4,5},{5,4},{6,7},{7,6},{8,9},{9,8},{10,11... | collective-permute-start | bytes 294920 | tf_op jit(solution)/shard_map/ppermute | solution.py:359
  32.9 107.2 %all-to-all-start = ((bf16[16,96,896]{2,1,0:T(8,128)(2,1)}), bf16[16,96,896]{2,1,0:T(8,128)(2,1)}, u32[]{:S(2)}, u32[]{:S(2)}) async-start(bf16[16,96,896]{2,1,0:T(8,128)(2,1)} %copy-done.4), calls=%async_computation | async-start | bytes 5505024 | tf_op jit(solution)/shard_map/all_to_all | solution.py:370
  42.7 47.0 %collective-permute-start.1 = (f32[96,256]{1,0:T(8,128)S(1)}, f32[96,256]{1,0:T(8,128)S(1)}, u32[]{:S(2)}, u32[]{:S(2)}) collective-permute-start(f32[96,256]{1,0:T(8,128)S(1)} %add.143.refs_0_), channel_id=1, source_target_pairs={{0,8},{2,10},{8,16},{10,18},{16,24},{18,26},{24,28},{26,30},{28,20... | collective-permute-start | bytes 294920 | tf_op jit(solution)/shard_map/ppermute | solution.py:320
  89.8 17.4 %collective-permute-start.3 = (f32[96,256]{1,0:T(8,128)S(1)}, f32[96,256]{1,0:T(8,128)S(1)}, u32[]{:S(2)}, u32[]{:S(2)}) collective-permute-start(f32[96,256]{1,0:T(8,128)S(1)} %collective-permute-done.1.refs_1_), channel_id=1, source_target_pairs={{0,8},{2,10},{8,16},{10,18},{16,24},{18,26},{24,28},{26,30},{28,20... | collective-permute-start | bytes 294920 | tf_op jit(solution)/shard_map/ppermute | solution.py:320
  107.2 5.9 %collective-permute-start.5 = (f32[96,256]{1,0:T(8,128)S(1)}, f32[96,256]{1,0:T(8,128)S(1)}, u32[]{:S(2)}, u32[]{:S(2)}) collective-permute-start(f32[96,256]{1,0:T(8,128)S(1)} %collective-permute-done.3.refs_3_), channel_id=1, source_target_pairs={{0,8},{2,10},{8,16},{10,18},{16,24},{18,26},{24,28},{26,30},{28,20... | collective-permute-start | bytes 294920 | tf_op jit(solution)/shard_map/ppermute | solution.py:320
  111.6 5.2 %collective-permute-start.9 = (f32[96,256]{1,0:T(8,128)S(1)}, f32[96,256]{1,0:T(8,128)S(1)}, u32[]{:S(2)}, u32[]{:S(2)}) collective-permute-start(f32[96,256]{1,0:T(8,128)S(1)} %collective-permute-done.1.refs_1_), channel_id=1, source_target_pairs={{0,2},{2,0},{4,6},{6,4},{8,10},{10,8},{12,14},{14,12},{16,18},{18,... | collective-permute-start | bytes 294920 | tf_op jit(solution)/shard_map/ppermute | solution.py:327
  112.0 5.2 %collective-permute-start.6 = (f32[96,256]{1,0:T(8,128)S(1)}, f32[96,256]{1,0:T(8,128)S(1)}, u32[]{:S(2)}, u32[]{:S(2)}) collective-permute-start(f32[96,256]{1,0:T(8,128)S(1)} %collective-permute-done.4.refs_4_.after_ref), channel_id=1, source_target_pairs={{0,4},{2,6},{8,0},{10,2},{16,8},{18,10},{24,16},{26,18},{28,24},{3... | collective-permute-start | bytes 294920 | tf_op jit(solution)/shard_map/ppermute | solution.py:324
  114.1 5.9 %collective-permute-start.12 = (f32[96,256]{1,0:T(8,128)S(1)}, f32[96,256]{1,0:T(8,128)S(1)}, u32[]{:S(2)}, u32[]{:S(2)}) collective-permute-start(f32[96,256]{1,0:T(8,128)S(1)} %collective-permute-done.4.refs_4_.after_ref), channel_id=1, source_target_pairs={{0,2},{2,0},{4,6},{6,4},{8,10},{10,8},{12,14},{14,12},{16,18},{18,... | collective-permute-start | bytes 294920 | tf_op jit(solution)/shard_map/ppermute | solution.py:327
  143.7 7.9 %collective-permute-start.21 = (bf16[896,256]{1,0:T(8,128)(2,1)}, bf16[896,256]{1,0:T(8,128)(2,1)}, u32[]{:S(2)}, u32[]{:S(2)}) collective-permute-start(bf16[896,256]{1,0:T(8,128)(2,1)} %get-tuple-element.28.refs_0_), channel_id=1, source_target_pairs={{0,8},{8,16},{16,24},{24,28},{28,20},{20,12},{12,4},{4,0},{2,6},{1... | collective-permute-start | bytes 1376264 | tf_op jit(solution)/shard_map/ppermute | solution.py:402
  151.6 9.9 %collective-permute-start.22 = (bf16[896,256]{1,0:T(8,128)(2,1)}, bf16[896,256]{1,0:T(8,128)(2,1)S(1)}, u32[]{:S(2)}, u32[]{:S(2)}) collective-permute-start(bf16[896,256]{1,0:T(8,128)(2,1)} %collective-permute-done.21.refs_2_), channel_id=1, source_target_pairs={{0,8},{8,16},{16,24},{24,28},{28,20},{20,12},{12,4},{4,0},{2,6},{1... | collective-permute-start | bytes 1376264 | tf_op jit(solution)/shard_map/ppermute | solution.py:402
  153.4 5.8 %collective-permute-start.18 = (f32[1,256]{1,0:T(1,128)S(1)}, f32[1,256]{1,0:T(1,128)S(1)}, u32[]{:S(2)}, u32[]{:S(2)}) collective-permute-start(f32[1,256]{1,0:T(1,128)S(1)} %add.145), channel_id=1, source_target_pairs={{0,4},{2,6},{4,0},{6,2},{8,12},{10,14},{12,8},{14,10},{16,20},{18,... | collective-permute-start | bytes 3080 | tf_op jit(solution)/shard_map/ppermute | solution.py:405
  161.6 7.8 %collective-permute-start.23 = (bf16[896,256]{1,0:T(8,128)(2,1)S(1)}, bf16[896,256]{1,0:T(8,128)(2,1)}, u32[]{:S(2)}, u32[]{:S(2)}) collective-permute-start(bf16[896,256]{1,0:T(8,128)(2,1)S(1)} %collective-permute-done.22.refs_0_), channel_id=1, source_target_pairs={{0,8},{8,16},{16,24},{24,28},{28,20},{20,12},{12,4},{4,0},{2,6},{1... | collective-permute-start | bytes 1376264 | tf_op jit(solution)/shard_map/ppermute | solution.py:402
  163.7 10.4 %collective-permute-start.25 = (bf16[896,256]{1,0:T(8,128)(2,1)}, bf16[896,256]{1,0:T(8,128)(2,1)}, u32[]{:S(2)}, u32[]{:S(2)}) collective-permute-start(bf16[896,256]{1,0:T(8,128)(2,1)} %get-tuple-element.28.refs_0_), channel_id=1, source_target_pairs={{0,2},{2,0},{4,6},{6,4},{8,10},{10,8},{12,14},{14,12},{16,18},{18,... | collective-permute-start | bytes 1376264 | tf_op jit(solution)/shard_map/ppermute | solution.py:403
  165.3 8.8 %collective-permute-start.26 = (bf16[896,256]{1,0:T(8,128)(2,1)}, bf16[896,256]{1,0:T(8,128)(2,1)}, u32[]{:S(2)}, u32[]{:S(2)}) collective-permute-start(bf16[896,256]{1,0:T(8,128)(2,1)} %collective-permute-done.21.refs_2_), channel_id=1, source_target_pairs={{0,2},{2,0},{4,6},{6,4},{8,10},{10,8},{12,14},{14,12},{16,18},{18,... | collective-permute-start | bytes 1376264 | tf_op jit(solution)/shard_map/ppermute | solution.py:403
  169.4 12.8 %collective-permute-start.24 = (bf16[896,256]{1,0:T(8,128)(2,1)}, bf16[896,256]{1,0:T(8,128)(2,1)S(1)}, u32[]{:S(2)}, u32[]{:S(2)}) collective-permute-start(bf16[896,256]{1,0:T(8,128)(2,1)} %collective-permute-done.23.refs_2_), channel_id=1, source_target_pairs={{0,8},{8,16},{16,24},{24,28},{28,20},{20,12},{12,4},{4,0},{2,6},{1... | collective-permute-start | bytes 1376264 | tf_op jit(solution)/shard_map/ppermute | solution.py:402
  171.7 12.4 %collective-permute-start.28 = (bf16[896,256]{1,0:T(8,128)(2,1)}, bf16[896,256]{1,0:T(8,128)(2,1)}, u32[]{:S(2)}, u32[]{:S(2)}) collective-permute-start(bf16[896,256]{1,0:T(8,128)(2,1)} %copy-done.5), channel_id=1, source_target_pairs={{0,2},{2,0},{4,6},{6,4},{8,10},{10,8},{12,14},{14,12},{16,18},{18,... | collective-permute-start | bytes 1376264 | tf_op jit(solution)/shard_map/ppermute | solution.py:403
  174.1 10.0 %collective-permute-start.29 = (bf16[896,256]{1,0:T(8,128)(2,1)}, bf16[896,256]{1,0:T(8,128)(2,1)}, u32[]{:S(2)}, u32[]{:S(2)}) collective-permute-start(bf16[896,256]{1,0:T(8,128)(2,1)} %collective-permute-done.23.refs_2_), channel_id=1, source_target_pairs={{0,2},{2,0},{4,6},{6,4},{8,10},{10,8},{12,14},{14,12},{16,18},{18,... | collective-permute-start | bytes 1376264 | tf_op jit(solution)/shard_map/ppermute | solution.py:403
  182.2 10.8 %collective-permute-start.27 = (bf16[896,256]{1,0:T(8,128)(2,1)S(1)}, bf16[896,256]{1,0:T(8,128)(2,1)}, u32[]{:S(2)}, u32[]{:S(2)}) collective-permute-start(bf16[896,256]{1,0:T(8,128)(2,1)S(1)} %collective-permute-done.24.refs_0_), channel_id=1, source_target_pairs={{0,8},{8,16},{16,24},{24,28},{28,20},{20,12},{12,4},{4,0},{2,6},{1... | collective-permute-start | bytes 1376264 | tf_op jit(solution)/shard_map/ppermute | solution.py:402
  193.1 7.9 %collective-permute-start.30 = (bf16[896,256]{1,0:T(8,128)(2,1)}, bf16[896,256]{1,0:T(8,128)(2,1)}, u32[]{:S(2)}, u32[]{:S(2)}) collective-permute-start(bf16[896,256]{1,0:T(8,128)(2,1)} %collective-permute-done.27.refs_2_), channel_id=1, source_target_pairs={{0,8},{8,16},{16,24},{24,28},{28,20},{20,12},{12,4},{4,0},{2,6},{1... | collective-permute-start | bytes 1376264 | tf_op jit(solution)/shard_map/ppermute | solution.py:402
  201.0 7.9 %collective-permute-start.31 = (bf16[896,256]{1,0:T(8,128)(2,1)}, bf16[896,256]{1,0:T(8,128)(2,1)}, u32[]{:S(2)}, u32[]{:S(2)}) collective-permute-start(bf16[896,256]{1,0:T(8,128)(2,1)} %collective-permute-done.30.refs_0_), channel_id=1, source_target_pairs={{0,8},{8,16},{16,24},{24,28},{28,20},{20,12},{12,4},{4,0},{2,6},{1... | collective-permute-start | bytes 1376264 | tf_op jit(solution)/shard_map/ppermute | solution.py:402
  201.0 10.2 %collective-permute-start.34 = (bf16[896,256]{1,0:T(8,128)(2,1)S(1)}, bf16[896,256]{1,0:T(8,128)(2,1)}, u32[]{:S(2)}, u32[]{:S(2)}) collective-permute-start(bf16[896,256]{1,0:T(8,128)(2,1)S(1)} %collective-permute-done.24.refs_0_), channel_id=1, source_target_pairs={{0,2},{2,0},{4,6},{6,4},{8,10},{10,8},{12,14},{14,12},{16,18},{18,... | collective-permute-start | bytes 1376264 | tf_op jit(solution)/shard_map/ppermute | solution.py:403
  202.0 9.2 %collective-permute-start.35 = (bf16[896,256]{1,0:T(8,128)(2,1)}, bf16[896,256]{1,0:T(8,128)(2,1)}, u32[]{:S(2)}, u32[]{:S(2)}) collective-permute-start(bf16[896,256]{1,0:T(8,128)(2,1)} %collective-permute-done.27.refs_2_), channel_id=1, source_target_pairs={{0,2},{2,0},{4,6},{6,4},{8,10},{10,8},{12,14},{14,12},{16,18},{18,... | collective-permute-start | bytes 1376264 | tf_op jit(solution)/shard_map/ppermute | solution.py:403
  202.0 17.1 %collective-permute-start.33 = (bf16[896,256]{1,0:T(8,128)(2,1)}, bf16[896,256]{1,0:T(8,128)(2,1)}, u32[]{:S(2)}, u32[]{:S(2)}) collective-permute-start(bf16[896,256]{1,0:T(8,128)(2,1)} %collective-permute-done.30.refs_0_), channel_id=1, source_target_pairs={{0,2},{2,0},{4,6},{6,4},{8,10},{10,8},{12,14},{14,12},{16,18},{18,... | collective-permute-start | bytes 1376264 | tf_op jit(solution)/shard_map/ppermute | solution.py:403
  209.0 13.9 %collective-permute-start.32 = (bf16[896,256]{1,0:T(8,128)(2,1)}, bf16[896,256]{1,0:T(8,128)(2,1)}, u32[]{:S(2)}, u32[]{:S(2)}) collective-permute-start(bf16[896,256]{1,0:T(8,128)(2,1)} %collective-permute-done.31.refs_0_), channel_id=1, source_target_pairs={{0,2},{2,0},{4,6},{6,4},{8,10},{10,8},{12,14},{14,12},{16,18},{18,... | collective-permute-start | bytes 1376264 | tf_op jit(solution)/shard_map/ppermute | solution.py:403
  (31 other events, 472.2 us)

commit v4 on v3

--- a/solution.py
+++ b/solution.py
@@ -23,76 +23,6 @@
 
 def params(mib):
     return pltpu.CompilerParams(vmem_limit_bytes=mib * MIB)
-
-
-def tile_of(cols, most):
-    tiles = cols // LANES
-    return LANES * max(d for d in range(1, most // LANES + 1) if tiles % d == 0)
-
-
-def sketch_kernel(m_ref, g_ref, b_ref, sketch_ref):
-    base_b = (m_ref[...] + g_ref[...].astype(F32)).astype(BF16)
-    term = jnp.dot(base_b, b_ref[...], preferred_element_type=F32)
-
-    @pl.when(pl.program_id(0) == 0)
-    def _():
-        sketch_ref[...] = term
-
-    @pl.when(pl.program_id(0) > 0)
-    def _():
-        sketch_ref[...] += term
-
-
-def sketch_call(momentum, gradient, basis):
-    rows, cols = momentum.shape
-    rank = basis.shape[1]
-    tile = tile_of(cols, 1536)
-    return pl.pallas_call(
-        sketch_kernel,
-        grid=(cols // tile,),
-        in_specs=[
-            pl.BlockSpec((rows, tile), lambda i: (0, i)),
-            pl.BlockSpec((rows, tile), lambda i: (0, i)),
-            pl.BlockSpec((tile, rank), lambda i: (i, 0)),
-        ],
-        out_specs=pl.BlockSpec((rows, rank), lambda i: (0, 0)),
-        out_shape=jax.ShapeDtypeStruct((rows, rank), F32),
-        compiler_params=params(60),
-        cost_estimate=cost(2 * rows * cols * rank, rows * cols * 6 + cols * rank * 2),
-        name="sketch",
-    )(momentum, gradient, basis)
-
-
-def pack_kernel(cols, m_ref, g_ref, after_ref, out_ref):
-    step = pl.program_id(0)
-    share = m_ref.shape[1]
-    left = cols - step * share
-
-    @pl.when(left >= share)
-    def _():
-        out_ref[0] = (m_ref[...] + g_ref[...].astype(F32)).astype(BF16)
-
-    @pl.when(left < share)
-    def _():
-        lane = lax.broadcasted_iota(jnp.int32, m_ref.shape, 1)
-        base = m_ref[...] + g_ref[...].astype(F32)
-        out_ref[0] = jnp.where(lane < left, base, 0.0).astype(BF16)
-
-
-def pack_call(momentum, gradient, share, count, after):
-    rows, cols = momentum.shape
-    last = pl.cdiv(cols, share) - 1
-    block = pl.BlockSpec((rows, share), lambda i: (0, jnp.minimum(i, last)))
-    return pl.pallas_call(
-        functools.partial(pack_kernel, cols),
-        grid=(count,),
-        in_specs=[block, block, pl.BlockSpec(memory_space=pl.ANY)],
-        out_specs=pl.BlockSpec((1, rows, share), lambda i: (i, 0, 0)),
-        out_shape=jax.ShapeDtypeStruct((count, rows, share), BF16),
-        compiler_params=params(48),
-        cost_estimate=cost(rows * cols, rows * cols * 8),
-        name="pack",
-    )(momentum, gradient, after)
 
 
 def spread(x, lane):
@@ -196,63 +126,77 @@
     )(ids, *pieces)
 
 
-def back_kernel(ortho_t_ref, columns_ref, back_ref, colsq_ref):
+def back_kernel(ortho_t_ref, columns_ref, colsq_ref, *part_refs):
     back_t = jnp.dot(ortho_t_ref[...], columns_ref[...], preferred_element_type=F32)
     back = back_t.T.astype(BF16)
-    back_ref[...] = back
+    start = 0
+    for part_ref in part_refs:
+        stop = start + part_ref.shape[0]
+        part_ref[...] = back[start:stop]
+        start = stop
     wide = back.astype(F32)
     colsq_ref[...] = jnp.sum(wide * wide, axis=0, keepdims=True)
 
 
-def back_call(ortho_t, columns):
+def back_call(ortho_t, columns, parts):
     rank, total = ortho_t.shape
     share = columns.shape[1]
+    vmem = pl.BlockSpec(memory_space=pltpu.VMEM)
     return pl.pallas_call(
         back_kernel,
-        in_specs=[pl.BlockSpec(memory_space=pltpu.VMEM)] * 2,
-        out_specs=[pl.BlockSpec(memory_space=pltpu.VMEM)] * 2,
-        out_shape=[
-            jax.ShapeDtypeStruct((share, rank), BF16),
-            jax.ShapeDtypeStruct((1, rank), F32),
-        ],
+        in_specs=[vmem] * 2,
+        out_specs=[vmem] * (1 + len(parts)),
+        out_shape=[jax.ShapeDtypeStruct((1, rank), F32)]
+        + [jax.ShapeDtypeStruct((part, rank), BF16) for part in parts],
         compiler_params=params(24),
         cost_estimate=cost(2 * rank * total * share, total * share * 2),
         name="back",
     )(ortho_t, columns)
 
 
-def output_kernel(count, factor, carried, ids_ref, m_ref, g_ref, ortho_ref, colsq_ref, *refs):
+def output_kernel(parts, factor, carried, ids_ref, m_ref, g_ref, ortho_ref, colsq_ref, *refs):
+    count = len(refs) - carried - 3
     pieces, (nm_ref, nb_ref, up_ref) = refs[:count], refs[count + carried :]
     step = pl.program_id(0)
     scale = lax.rsqrt(colsq_ref[...] + 1e-06)
     ortho = ortho_ref[...]
     over = (((1,), (1,)), ((), ()))
-    for n, piece in enumerate(pieces):
+
+    def write(piece, here):
+        back = piece[...]
+        unit = (back.astype(F32) * scale).astype(BF16)
+        nb_ref[here, :] = unit
+        base = m_ref[:, here] + g_ref[:, here].astype(F32)
+        nm_ref[:, here] = base - 0.05 * lax.dot_general(
+            ortho, back, over, preferred_element_type=F32
+        )
+        up_ref[:, here] = (
+            factor * lax.dot_general(ortho, unit, over, preferred_element_type=F32)
+        ).astype(BF16)
+
+    for n in range(count // parts):
 
         @pl.when(step == n)
         def _():
-            back = piece[...]
-            unit = (back.astype(F32) * scale).astype(BF16)
-            nb_ref[...] = unit
-            base = m_ref[...] + g_ref[...].astype(F32)
-            nm_ref[...] = base - 0.05 * lax.dot_general(
-                ortho, back, over, preferred_element_type=F32
-            )
-            up_ref[...] = (
-                factor * lax.dot_general(ortho, unit, over, preferred_element_type=F32)
-            ).astype(BF16)
-
-
-def output_call(ids, momentum, gradient, ortho, colsq, pieces, factor, previous):
+            start = 0
+            for piece in pieces[n * parts : (n + 1) * parts]:
+                stop = start + piece.shape[0]
+                write(piece, slice(start, stop))
+                start = stop
+
+
+def output_call(ids, momentum, gradient, ortho, colsq, blocks, factor, previous):
     rows, cols = momentum.shape
-    share, rank = pieces[0].shape
-    count = len(pieces)
+    rank = ortho.shape[1]
+    count, parts = len(blocks), len(blocks[0])
+    pieces = [part for block in blocks for part in block]
+    share = sum(part.shape[0] for part in blocks[0])
     wide = pl.BlockSpec((rows, share), lambda i, ids: (0, ids[i]))
     tall = pl.BlockSpec((share, rank), lambda i, ids: (ids[i], 0))
     carried = 3 if previous else 0
-    aliases = {5 + count + n: n for n in range(carried)}
+    aliases = {5 + len(pieces) + n: n for n in range(carried)}
     return pl.pallas_call(
-        functools.partial(output_kernel, count, factor, carried),
+        functools.partial(output_kernel, parts, factor, carried),
         grid_spec=pltpu.PrefetchScalarGridSpec(
             num_scalar_prefetch=1,
             grid=(count,),
@@ -262,7 +206,7 @@
                 pl.BlockSpec((rows, rank), lambda i, ids: (0, 0)),
                 pl.BlockSpec((1, rank), lambda i, ids: (0, 0)),
             ]
-            + [pl.BlockSpec((share, rank), lambda i, ids: (0, 0))] * count
+            + [pl.BlockSpec(part.shape, lambda i, ids: (0, 0)) for part in pieces]
             + [pl.BlockSpec(memory_space=pl.ANY)] * carried,
             out_specs=[wide, tall, wide],
         ),
@@ -272,7 +216,7 @@
             jax.ShapeDtypeStruct((rows, cols), BF16),
         ],
         input_output_aliases=aliases,
-        compiler_params=params(32),
+        compiler_params=params(24),
         cost_estimate=cost(
             4 * rows * share * rank * count, count * share * (rows * 12 + rank * 4)
         ),
@@ -317,6 +261,7 @@
     offsets, held = [0], [x]
     ahead = behind = x
     for step in range(1, chips // 2 + 1):
+        ahead, behind = lax.optimization_barrier((ahead, behind))
         ahead = lax.ppermute(ahead, "fsdp", up)
         held.append(ahead)
         offsets.append(-step)
@@ -327,7 +272,7 @@
     other = [lax.ppermute(h, "fsdp", swap_pairs(count)) for h in held]
     chip = chip_at((place + jnp.array(offsets, jnp.int32)) % chips, chips)
     ids = jnp.concatenate([2 * chip + core, 2 * chip + 1 - core])
-    return held + other, ids.astype(jnp.int32)
+    return held + other, ids.astype(jnp.int32), held
 
 
 def tie(x, *work):
@@ -354,33 +299,41 @@
     me = lax.axis_index("fsdp")
     ring = tp_count == 2 and count in (4, 8, 16, 32) and (count - 1) * share < cols
 
-    sketch = sketch_call(momentum, gradient, basis)
+    base_b = (momentum + gradient.astype(F32)).astype(BF16)
+    sketch = jnp.dot(base_b, basis, preferred_element_type=F32)
+    outgoing = jnp.pad(base_b, ((0, 0), (0, share * count - cols)))
+    outgoing = jnp.swapaxes(outgoing.reshape(rows, count, share), 0, 1)
     if tp_count == 2:
         sketch = sketch + lax.ppermute(sketch, "tp", [(0, 1), (1, 0)])
     else:
         sketch = lax.psum(sketch, "tp")
 
     if ring:
-        pieces, ids = gather_small(sketch, count)
+        pieces, ids, travelled = gather_small(sketch, count)
+        outgoing = tie(outgoing, *travelled)
     else:
         whole = lax.all_gather(sketch, "fsdp", axis=0)
         pieces = [lax.dynamic_index_in_dim(whole, (me + n) % count, 0, False) for n in range(count)]
         ids = ((me + jnp.arange(count)) % count).astype(jnp.int32)
-    outgoing = pack_call(momentum, gradient, share, count, pieces[min(4, count - 1)])
     columns = lax.all_to_all(outgoing, "fsdp", 0, 0, tiled=True)
     columns = columns.reshape(rows * count, share)
     ortho_t, ortho_here = factor_call(ids, pieces)
-    back, part = back_call(ortho_t, columns)
+    momentum = pltpu.with_memory_space_constraint(momentum, pltpu.HBM)
+    tiles = share // LANES
+    cuts = [share]
+    if ring and tiles > 1:
+        cuts = [share - tiles // 2 * LANES, tiles // 2 * LANES]
+    part, *back = back_call(ortho_t, columns, cuts)
 
     outputs = functools.partial(output_call, factor=factor)
     if not ring:
         colsq = lax.psum(part, ("fsdp", "tp"))
-        whole = lax.all_gather(back, "fsdp", axis=0)
+        whole = lax.all_gather(back[0], "fsdp", axis=0)
         valid = -(-cols // share)
         return tuple(
             outputs(
                 jnp.arange(valid, dtype=jnp.int32), momentum, gradient, ortho_here, colsq,
-                [whole[n] for n in range(valid)], previous=None,
+                [[whole[n]] for n in range(valid)], previous=None,
             )
         )
 
@@ -394,28 +347,30 @@
     ids = jnp.stack([mine, theirs], axis=1).astype(jnp.int32)
     rounds = sum_rounds(count, tp_count)
     colsq, result = part, None
-    blocks, others = [back], []
-    written = 0
-    waiting = ()
+    mine, theirs = [list(back)], []
+    written, waiting = 0, ()
     for step in range(chips):
-        if step + 1 < chips:
-            blocks.append(lax.ppermute(tie(blocks[step], *waiting), "fsdp", turn))
-        others.append(lax.ppermute(blocks[step], "fsdp", swap))
-        for axis, pairs in rounds[:2]:
-            colsq = colsq + lax.ppermute(colsq, axis, pairs)
-        done, rounds = not rounds, rounds[2:]
-        waiting = (colsq,)
-        if done and step > written + 1:
-            ready = slice(written, min(written + 2, step))
-            written = ready.stop
-            result = outputs(
-                ids[ready].reshape(-1), momentum, gradient, ortho_here, colsq,
-                [x for pair in zip(blocks[ready], others[ready]) for x in pair], previous=result,
-            )
-            waiting = tuple(result)
+        mine.append([])
+        theirs.append([])
+        for n in range(len(cuts)):
+            block = mine[step][n]
+            if step + 1 < chips:
+                mine[step + 1].append(lax.ppermute(tie(block, *waiting), "fsdp", turn))
+            theirs[step].append(lax.ppermute(block, "fsdp", swap))
+            if rounds:
+                axis, pairs = rounds.pop(0)
+                colsq = colsq + lax.ppermute(tie(colsq, block), axis, pairs)
+                waiting = ()
+            elif written + 1 < step:
+                result = outputs(
+                    ids[written], momentum, gradient, ortho_here, colsq,
+                    [mine[written], theirs[written]], previous=result,
+                )
+                written += 1
+                waiting = tuple(result)
     for n in range(written, chips):
         result = outputs(
-            ids[n], momentum, gradient, ortho_here, colsq, [blocks[n], others[n]], previous=result
+            ids[n], momentum, gradient, ortho_here, colsq, [mine[n], theirs[n]], previous=result
         )
     return tuple(result)
 

time: 228 us -> 181 us (0.79)
  waiting for transfers between devices: 85.6 us -> 69 us
  Pallas kernels: 60.1 us -> 45.7 us
  local copies, waits for them, and re-layouts: 16 us -> 4.68 us
  starting transfers between devices: 63.1 us -> 54.9 us
  other arithmetic: 1.05 us -> 4.06 us
    ppermute x4, waiting for transfers between devices: 47.3 us -> 7.71 us  [gather_small(): ahead = lax.ppermute(ahead, 'fsdp', up)]
    all_to_all x1, waiting for transfers between devices: 0.01 us -> 34.9 us  [local(): columns = lax.all_to_all(outgoing, 'fsdp', 0, 0, tiled=True)]
    ppermute x4, starting transfers between devices: 20.3 us -> 4.96 us  [gather_small(): ahead = lax.ppermute(ahead, 'fsdp', up)]
    ppermute x20 -> x35, starting transfers between devices: 20 us -> 34.4 us  [the longest x14 20.1 us: local(): mine[step + 1].append(lax.ppermute(tie(block, *waiting), 'fsdp', turn))]
    pallas_call x8 -> x9, Pallas kernels: 45.5 us -> 31 us  [the longest x8 27.5 us: output_call(): pl.pallas_call(functools.partial(output_kernel, parts, factor, carried),...]
    unnamed x36 -> x10, local copies, waits for them, and re-layouts: 15.2 us -> 2.38 us
    ppermute x20 -> x35, waiting for transfers between devices: 29.7 us -> 19.3 us  [the longest x14 12.1 us: local(): mine[step + 1].append(lax.ppermute(tie(block, *waiting), 'fsdp', turn))]
    ppermute x8, starting transfers between devices: 7.78 us -> 2.38 us  [gather_small(): other = [lax.ppermute(h, 'fsdp', swap_pairs(count)) for h in held]]
  transfers between devices with their start and end apart: 37 -> 52, of which waited for: 15 -> 24; matrix products, arithmetic and copies ran while one was open for 0% -> 1% of each run, Pallas kernels for 15% -> 21%
where the time goes in v4:
time: 181 us; the launch traced here: 180 us
  waiting for transfers between devices  69 us (38%)
  starting transfers between devices  54.9 us (30%)
  Pallas kernels  45.7 us (25%)
  local copies, waits for them, and re-layouts  4.68 us (3%)
  other arithmetic  4.06 us (2%)
    all_to_all x1, waiting for transfers between devices, local(): columns = lax.all_to_all(outgoing, 'fsdp', 0, 0, tiled=True)  34.9 us
    pallas_call x8, Pallas kernels, output_call(): pl.pallas_call(functools.partial(output_kernel, parts, factor, carried),...  27.5 us
    ppermute x14, starting transfers between devices, local(): mine[step + 1].append(lax.ppermute(tie(block, *waiting), 'fsdp', turn))  20.1 us
    pallas_call x1, Pallas kernels, factor_call(): pl.pallas_call(functools.partial(factor_kernel, count), in_specs=[pl.Bloc...  14.7 us
    ppermute x14, waiting for transfers between devices, local(): mine[step + 1].append(lax.ppermute(tie(block, *waiting), 'fsdp', turn))  12.1 us
    all_to_all x1, starting transfers between devices, local(): columns = lax.all_to_all(outgoing, 'fsdp', 0, 0, tiled=True)  10.2 us
    ppermute x16, starting transfers between devices, local(): theirs[step].append(lax.ppermute(block, 'fsdp', swap))  9.48 us
    ppermute x4, waiting for transfers between devices, gather_small(): ahead = lax.ppermute(ahead, 'fsdp', up)  7.71 us
  transfers between devices with their start and end apart: 52, of which 24 were waited for; matrix products, arithmetic and copies ran while one was open for 1% of the time, Pallas kernels for 21%

profile of v4, /device:TPU:1, one launch (start us, length us, event | category | flops | bytes accessed | tf_op | source)
XLA Modules:
  0.0 180.4 jit_solution(10063209831499867439)
XLA Ops:
  0.6 3.9 %add_convert_fusion = bf16[96,13824]{1,0:T(8,128)(2,1)S(1)} fusion(f32[96,13824]{1,0:T(8,128)} %m_ref.15, bf16[96,13824]{1,0:T(8,128)(2,1)} %g_ref.15), kind=kLoop, calls=%fused_computation | loop fusion | flops 3981312 | bytes 10616832 | tf_op jit(solution)/shard_map/convert_element_type | solution.py:302
  7.2 2.1 %collective-permute-start = (f32[96,256]{1,0:T(8,128)S(1)}, f32[96,256]{1,0:T(8,128)S(1)}, u32[]{:S(2)}, u32[]{:S(2)}) collective-permute-start(f32[96,256]{1,0:T(8,128)S(1)} %fusion.8), channel_id=1, source_target_pairs={{0,1},{1,0},{2,3},{3,2},{4,5},{5,4},{6,7},{7,6},{8,9},{9,8},{10,11... | collective-permute-start | bytes 294920 | tf_op jit(solution)/shard_map/ppermute | solution.py:307
  9.3 2.5 %collective-permute-done = f32[96,256]{1,0:T(8,128)S(1)} collective-permute-done((f32[96,256]{1,0:T(8,128)S(1)}, f32[96,256]{1,0:T(8,128)S(1)}, u32[]{:S(2)}, u32[]{:S(2)}) %collective-permute-start) | collective-permute-done | bytes 98336 | tf_op jit(solution)/shard_map/ppermute | solution.py:307
  22.9 2.3 %collective-permute-done.5.refs_5_ = f32[96,256]{1,0:T(8,128)S(1)} collective-permute-done((f32[96,256]{1,0:T(8,128)S(1)}, f32[96,256]{1,0:T(8,128)S(1)}, u32[]{:S(2)}, u32[]{:S(2)}) %collective-permute-start.5) | collective-permute-done | bytes 98336 | tf_op jit(solution)/shard_map/ppermute | solution.py:265
  31.0 10.2 %all-to-all-start = ((bf16[16,96,896]{2,1,0:T(8,128)(2,1)}), bf16[16,96,896]{2,1,0:T(8,128)(2,1)}, u32[]{:S(2)}, u32[]{:S(2)}) async-start(bf16[16,96,896]{2,1,0:T(8,128)(2,1)} %bitcast.10), calls=%async_computation | async-start | bytes 5505024 | tf_op jit(solution)/shard_map/all_to_all | solution.py:318
  44.6 14.7 %factor.1 = (bf16[256,1536]{1,0:T(8,128)(2,1)S(1)}, bf16[96,256]{1,0:T(8,128)(2,1)S(1)}) custom-call(s32[16]{0:T(128)S(1)} %pad_add_fusion.1.ids_ref, f32[96,256]{1,0:T(8,128)S(1)} %add.149.refs_0_, f32[96,256]{1,0:T(8,128)S(1)} %collective-permute-done.1.refs_1_, f32[96,256]{1,0:T(8,128)S(1)} %collective-permute-done.2.refs_2_, ...), custom_call_target="tpu_custom_call" | custom-call | flops 4026531840 | bytes 2359296 | tf_op jit(solution)/shard_map/factor/pallas_call | solution.py:114
  59.3 34.9 %all-to-all-done = bf16[16,96,896]{2,1,0:T(8,128)(2,1)} async-done(((bf16[16,96,896]{2,1,0:T(8,128)(2,1)}), bf16[16,96,896]{2,1,0:T(8,128)(2,1)}, u32[]{:S(2)}, u32[]{:S(2)}) %all-to-all-start) | async-done | bytes 2752544 | tf_op jit(solution)/shard_map/all_to_all | solution.py:318
  94.2 3.5 %back.1 = (f32[1,256]{1,0:T(1,128)S(1)}, bf16[512,256]{1,0:T(8,128)(2,1)S(1)}, bf16[384,256]{1,0:T(8,128)(2,1)}) custom-call(bf16[256,1536]{1,0:T(8,128)(2,1)S(1)} %get-tuple-element.58.ortho_t_ref, bf16[1536,896]{1,0:T(8,128)(2,1)} %bitcast.1.columns_ref), custom_call_target="tpu_custom_call" | custom-call | flops 704643072 | bytes 2752512 | tf_op jit(solution)/shard_map/back/pallas_call | solution.py:145
  97.8 4.0 %collective-permute-start.18 = (bf16[512,256]{1,0:T(8,128)(2,1)S(1)}, bf16[512,256]{1,0:T(8,128)(2,1)S(1)}, u32[]{:S(2)}, u32[]{:S(2)}) collective-permute-start(bf16[512,256]{1,0:T(8,128)(2,1)S(1)} %get-tuple-element.61.refs_0_), channel_id=1, source_target_pairs={{0,8},{8,16},{16,24},{24,28},{28,20},{20,12},{12,4},{4,0},{2,6},{1... | collective-permute-start | bytes 786440 | tf_op jit(solution)/shard_map/ppermute | solution.py:358
  101.7 7.4 %collective-permute-done.18.refs_0_ = bf16[512,256]{1,0:T(8,128)(2,1)S(1)} collective-permute-done((bf16[512,256]{1,0:T(8,128)(2,1)S(1)}, bf16[512,256]{1,0:T(8,128)(2,1)S(1)}, u32[]{:S(2)}, u32[]{:S(2)}) %collective-permute-start.18) | collective-permute-done | bytes 262176 | tf_op jit(solution)/shard_map/ppermute | solution.py:358
  109.2 3.1 %collective-permute-start.22 = (bf16[512,256]{1,0:T(8,128)(2,1)S(1)}, bf16[512,256]{1,0:T(8,128)(2,1)S(1)}, u32[]{:S(2)}, u32[]{:S(2)}) collective-permute-start(bf16[512,256]{1,0:T(8,128)(2,1)S(1)} %collective-permute-done.18.refs_0_), channel_id=1, source_target_pairs={{0,8},{8,16},{16,24},{24,28},{28,20},{20,12},{12,4},{4,0},{2,6},{1... | collective-permute-start | bytes 786440 | tf_op jit(solution)/shard_map/ppermute | solution.py:358
  112.2 2.2 %collective-permute-start.20 = (bf16[384,256]{1,0:T(8,128)(2,1)}, bf16[384,256]{1,0:T(8,128)(2,1)S(1)}, u32[]{:S(2)}, u32[]{:S(2)}) collective-permute-start(bf16[384,256]{1,0:T(8,128)(2,1)} %get-tuple-element.63.refs_1_), channel_id=1, source_target_pairs={{0,8},{8,16},{16,24},{24,28},{28,20},{20,12},{12,4},{4,0},{2,6},{1... | collective-permute-start | bytes 589832 | tf_op jit(solution)/shard_map/ppermute | solution.py:358
  117.1 2.8 %collective-permute-start.17 = (f32[1,256]{1,0:T(1,128)S(1)}, f32[1,256]{1,0:T(1,128)S(1)}, u32[]{:S(2)}, u32[]{:S(2)}) collective-permute-start(f32[1,256]{1,0:T(1,128)S(1)} %add.150), channel_id=1, source_target_pairs={{0,2},{2,0},{4,6},{6,4},{8,10},{10,8},{12,14},{14,12},{16,18},{18,... | collective-permute-start | bytes 3080 | tf_op jit(solution)/shard_map/ppermute | solution.py:362
  127.5 2.3 %collective-permute-done.23 = f32[1,256]{1,0:T(1,128)S(1)} collective-permute-done((f32[1,256]{1,0:T(1,128)S(1)}, f32[1,256]{1,0:T(1,128)S(1)}, u32[]{:S(2)}, u32[]{:S(2)}) %collective-permute-start.23) | collective-permute-done | bytes 1056 | tf_op jit(solution)/shard_map/ppermute | solution.py:362
  129.7 3.1 %collective-permute-start.28 = (bf16[512,256]{1,0:T(8,128)(2,1)S(1)}, bf16[512,256]{1,0:T(8,128)(2,1)S(1)}, u32[]{:S(2)}, u32[]{:S(2)}) collective-permute-start(bf16[512,256]{1,0:T(8,128)(2,1)S(1)} %collective-permute-done.18.refs_0_), channel_id=1, source_target_pairs={{0,2},{2,0},{4,6},{6,4},{8,10},{10,8},{12,14},{14,12},{16,18},{18,... | collective-permute-start | bytes 786440 | tf_op jit(solution)/shard_map/ppermute | solution.py:359
  133.8 3.5 %outputs.8 = (f32[96,13824]{1,0:T(8,128)}, bf16[13824,256]{1,0:T(8,128)(2,1)}, bf16[96,13824]{1,0:T(8,128)(2,1)}) custom-call(s32[2]{0:T(128)S(1)} %get-tuple-element.103.ids_ref, f32[96,13824]{1,0:T(8,128)} %m_ref.15, bf16[96,13824]{1,0:T(8,128)(2,1)S(1)} %copy-done, bf16[96,256]{1,0:T(8,128)(2,1)S(1)} %get-tuple-element.57.ortho_ref, ...), custom_call_target="tpu_custom_call" | custom-call | flops 176160768 | bytes 3899392 | tf_op jit(solution)/shard_map/outputs/pallas_call | solution.py:198
  139.7 3.4 %outputs.9 = (f32[96,13824]{1,0:T(8,128)}, bf16[13824,256]{1,0:T(8,128)(2,1)}, bf16[96,13824]{1,0:T(8,128)(2,1)}) custom-call(s32[2]{0:T(128)S(1)} %get-tuple-element.102.ids_ref, f32[96,13824]{1,0:T(8,128)} %m_ref.15, bf16[96,13824]{1,0:T(8,128)(2,1)S(1)} %copy-done, ...), custom_call_target="tpu_custom_call", output_to_operand_aliasing={{0}: (9, {}), {1}: (10, {}), {2}: (11, {})} | custom-call | flops 176160768 | bytes 3899392 | tf_op jit(solution)/shard_map/outputs/pallas_call | solution.py:198
  146.4 3.4 %outputs.10 = (f32[96,13824]{1,0:T(8,128)}, bf16[13824,256]{1,0:T(8,128)(2,1)}, bf16[96,13824]{1,0:T(8,128)(2,1)}) custom-call(s32[2]{0:T(128)S(1)} %get-tuple-element.101.ids_ref, f32[96,13824]{1,0:T(8,128)} %m_ref.15, bf16[96,13824]{1,0:T(8,128)(2,1)S(1)} %copy-done, ...), custom_call_target="tpu_custom_call", output_to_operand_aliasing={{0}: (9, {}), {1}: (10, {}), {2}: (11, {})} | custom-call | flops 176160768 | bytes 3899392 | tf_op jit(solution)/shard_map/outputs/pallas_call | solution.py:198
  153.6 3.4 %outputs.11 = (f32[96,13824]{1,0:T(8,128)}, bf16[13824,256]{1,0:T(8,128)(2,1)}, bf16[96,13824]{1,0:T(8,128)(2,1)}) custom-call(s32[2]{0:T(128)S(1)} %get-tuple-element.100.ids_ref, f32[96,13824]{1,0:T(8,128)} %m_ref.15, bf16[96,13824]{1,0:T(8,128)(2,1)S(1)} %copy-done, ...), custom_call_target="tpu_custom_call", output_to_operand_aliasing={{0}: (9, {}), {1}: (10, {}), {2}: (11, {})} | custom-call | flops 176160768 | bytes 3899392 | tf_op jit(solution)/shard_map/outputs/pallas_call | solution.py:198
  161.1 3.4 %outputs.12 = (f32[96,13824]{1,0:T(8,128)}, bf16[13824,256]{1,0:T(8,128)(2,1)}, bf16[96,13824]{1,0:T(8,128)(2,1)}) custom-call(s32[2]{0:T(128)S(1)} %get-tuple-element.99.ids_ref, f32[96,13824]{1,0:T(8,128)} %m_ref.15, bf16[96,13824]{1,0:T(8,128)(2,1)S(1)} %copy-done, ...), custom_call_target="tpu_custom_call", output_to_operand_aliasing={{0}: (9, {}), {1}: (10, {}), {2}: (11, {})} | custom-call | flops 176160768 | bytes 3899392 | tf_op jit(solution)/shard_map/outputs/pallas_call | solution.py:198
  167.1 2.2 %collective-permute-done.44.refs_1_ = bf16[384,256]{1,0:T(8,128)(2,1)S(1)} collective-permute-done((bf16[384,256]{1,0:T(8,128)(2,1)S(1)}, bf16[384,256]{1,0:T(8,128)(2,1)S(1)}, u32[]{:S(2)}, u32[]{:S(2)}) %collective-permute-start.44) | collective-permute-done | bytes 196640 | tf_op jit(solution)/shard_map/ppermute | solution.py:358
  170.0 3.4 %outputs.13 = (f32[96,13824]{1,0:T(8,128)}, bf16[13824,256]{1,0:T(8,128)(2,1)}, bf16[96,13824]{1,0:T(8,128)(2,1)}) custom-call(s32[2]{0:T(128)S(1)} %get-tuple-element.97.ids_ref, f32[96,13824]{1,0:T(8,128)} %m_ref.15, bf16[96,13824]{1,0:T(8,128)(2,1)S(1)} %copy-done, ...), custom_call_target="tpu_custom_call", output_to_operand_aliasing={{0}: (9, {}), {1}: (10, {}), {2}: (11, {})} | custom-call | flops 176160768 | bytes 3899392 | tf_op jit(solution)/shard_map/outputs/pallas_call | solution.py:198
  173.4 3.4 %outputs.14 = (f32[96,13824]{1,0:T(8,128)}, bf16[13824,256]{1,0:T(8,128)(2,1)}, bf16[96,13824]{1,0:T(8,128)(2,1)}) custom-call(s32[2]{0:T(128)S(1)} %get-tuple-element.98.ids_ref, f32[96,13824]{1,0:T(8,128)} %m_ref.15, bf16[96,13824]{1,0:T(8,128)(2,1)S(1)} %copy-done, ...), custom_call_target="tpu_custom_call", output_to_operand_aliasing={{0}: (9, {}), {1}: (10, {}), {2}: (11, {})} | custom-call | flops 176160768 | bytes 3899392 | tf_op jit(solution)/shard_map/outputs/pallas_call | solution.py:198
  176.9 3.4 %outputs.15 = (f32[96,13824]{1,0:T(8,128)}, bf16[13824,256]{1,0:T(8,128)(2,1)}, bf16[96,13824]{1,0:T(8,128)(2,1)}) custom-call(s32[2]{0:T(128)S(1)} %get-tuple-element.104.ids_ref, f32[96,13824]{1,0:T(8,128)} %m_ref.15, bf16[96,13824]{1,0:T(8,128)(2,1)S(1)} %copy-done, ...), custom_call_target="tpu_custom_call", output_to_operand_aliasing={{0}: (9, {}), {1}: (10, {}), {2}: (11, {})} | custom-call | flops 176160768 | bytes 3899392 | tf_op jit(solution)/shard_map/outputs/pallas_call | solution.py:198
  (116 shorter events, 50.8 us)
Async XLA Ops:
  31.0 63.3 %all-to-all-start = ((bf16[16,96,896]{2,1,0:T(8,128)(2,1)}), bf16[16,96,896]{2,1,0:T(8,128)(2,1)}, u32[]{:S(2)}, u32[]{:S(2)}) async-start(bf16[16,96,896]{2,1,0:T(8,128)(2,1)} %bitcast.10), calls=%async_computation | async-start | bytes 5505024 | tf_op jit(solution)/shard_map/all_to_all | solution.py:318
  97.8 11.4 %collective-permute-start.18 = (bf16[512,256]{1,0:T(8,128)(2,1)S(1)}, bf16[512,256]{1,0:T(8,128)(2,1)S(1)}, u32[]{:S(2)}, u32[]{:S(2)}) collective-permute-start(bf16[512,256]{1,0:T(8,128)(2,1)S(1)} %get-tuple-element.61.refs_0_), channel_id=1, source_target_pairs={{0,8},{8,16},{16,24},{24,28},{28,20},{20,12},{12,4},{4,0},{2,6},{1... | collective-permute-start | bytes 786440 | tf_op jit(solution)/shard_map/ppermute | solution.py:358
  109.2 11.7 %collective-permute-start.22 = (bf16[512,256]{1,0:T(8,128)(2,1)S(1)}, bf16[512,256]{1,0:T(8,128)(2,1)S(1)}, u32[]{:S(2)}, u32[]{:S(2)}) collective-permute-start(bf16[512,256]{1,0:T(8,128)(2,1)S(1)} %collective-permute-done.18.refs_0_), channel_id=1, source_target_pairs={{0,8},{8,16},{16,24},{24,28},{28,20},{20,12},{12,4},{4,0},{2,6},{1... | collective-permute-start | bytes 786440 | tf_op jit(solution)/shard_map/ppermute | solution.py:358
  112.2 11.0 %collective-permute-start.20 = (bf16[384,256]{1,0:T(8,128)(2,1)}, bf16[384,256]{1,0:T(8,128)(2,1)S(1)}, u32[]{:S(2)}, u32[]{:S(2)}) collective-permute-start(bf16[384,256]{1,0:T(8,128)(2,1)} %get-tuple-element.63.refs_1_), channel_id=1, source_target_pairs={{0,8},{8,16},{16,24},{24,28},{28,20},{20,12},{12,4},{4,0},{2,6},{1... | collective-permute-start | bytes 589832 | tf_op jit(solution)/shard_map/ppermute | solution.py:358
  120.0 12.8 %collective-permute-start.25 = (bf16[512,256]{1,0:T(8,128)(2,1)}, bf16[512,256]{1,0:T(8,128)(2,1)S(1)}, u32[]{:S(2)}, u32[]{:S(2)}) collective-permute-start(bf16[512,256]{1,0:T(8,128)(2,1)} %copy-done.1), channel_id=1, source_target_pairs={{0,2},{2,0},{4,6},{6,4},{8,10},{10,8},{12,14},{14,12},{16,18},{18,... | collective-permute-start | bytes 786440 | tf_op jit(solution)/shard_map/ppermute | solution.py:359
  120.8 16.5 %collective-permute-start.24 = (bf16[512,256]{1,0:T(8,128)(2,1)S(1)}, bf16[512,256]{1,0:T(8,128)(2,1)S(1)}, u32[]{:S(2)}, u32[]{:S(2)}) collective-permute-start(bf16[512,256]{1,0:T(8,128)(2,1)S(1)} %collective-permute-done.22.refs_0_), channel_id=1, source_target_pairs={{0,8},{8,16},{16,24},{24,28},{28,20},{20,12},{12,4},{4,0},{2,6},{1... | collective-permute-start | bytes 786440 | tf_op jit(solution)/shard_map/ppermute | solution.py:358
  122.3 10.5 %collective-permute-start.26 = (bf16[384,256]{1,0:T(8,128)(2,1)}, bf16[384,256]{1,0:T(8,128)(2,1)S(1)}, u32[]{:S(2)}, u32[]{:S(2)}) collective-permute-start(bf16[384,256]{1,0:T(8,128)(2,1)} %get-tuple-element.63.refs_1_), channel_id=1, source_target_pairs={{0,2},{2,0},{4,6},{6,4},{8,10},{10,8},{12,14},{14,12},{16,18},{18,... | collective-permute-start | bytes 589832 | tf_op jit(solution)/shard_map/ppermute | solution.py:359
  123.3 15.0 %collective-permute-start.31 = (bf16[384,256]{1,0:T(8,128)(2,1)S(1)}, bf16[384,256]{1,0:T(8,128)(2,1)S(1)}, u32[]{:S(2)}, u32[]{:S(2)}) collective-permute-start(bf16[384,256]{1,0:T(8,128)(2,1)S(1)} %collective-permute-done.20.refs_1_), channel_id=1, source_target_pairs={{0,8},{8,16},{16,24},{24,28},{28,20},{20,12},{12,4},{4,0},{2,6},{1... | collective-permute-start | bytes 589832 | tf_op jit(solution)/shard_map/ppermute | solution.py:358
  129.7 10.0 %collective-permute-start.28 = (bf16[512,256]{1,0:T(8,128)(2,1)S(1)}, bf16[512,256]{1,0:T(8,128)(2,1)S(1)}, u32[]{:S(2)}, u32[]{:S(2)}) collective-permute-start(bf16[512,256]{1,0:T(8,128)(2,1)S(1)} %collective-permute-done.18.refs_0_), channel_id=1, source_target_pairs={{0,2},{2,0},{4,6},{6,4},{8,10},{10,8},{12,14},{14,12},{16,18},{18,... | collective-permute-start | bytes 786440 | tf_op jit(solution)/shard_map/ppermute | solution.py:359
  138.3 6.7 %collective-permute-start.35 = (bf16[384,256]{1,0:T(8,128)(2,1)S(1)}, bf16[384,256]{1,0:T(8,128)(2,1)S(1)}, u32[]{:S(2)}, u32[]{:S(2)}) collective-permute-start(bf16[384,256]{1,0:T(8,128)(2,1)S(1)} %collective-permute-done.31.refs_1_), channel_id=1, source_target_pairs={{0,8},{8,16},{16,24},{24,28},{28,20},{20,12},{12,4},{4,0},{2,6},{1... | collective-permute-start | bytes 589832 | tf_op jit(solution)/shard_map/ppermute | solution.py:358
  139.1 7.3 %collective-permute-start.32 = (bf16[512,256]{1,0:T(8,128)(2,1)S(1)}, bf16[512,256]{1,0:T(8,128)(2,1)S(1)}, u32[]{:S(2)}, u32[]{:S(2)}) collective-permute-start(bf16[512,256]{1,0:T(8,128)(2,1)S(1)} %collective-permute-done.22.refs_0_), channel_id=1, source_target_pairs={{0,2},{2,0},{4,6},{6,4},{8,10},{10,8},{12,14},{14,12},{16,18},{18,... | collective-permute-start | bytes 786440 | tf_op jit(solution)/shard_map/ppermute | solution.py:359
  143.2 8.5 %collective-permute-start.30 = (bf16[512,256]{1,0:T(8,128)(2,1)S(1)}, bf16[512,256]{1,0:T(8,128)(2,1)S(1)}, u32[]{:S(2)}, u32[]{:S(2)}) collective-permute-start(bf16[512,256]{1,0:T(8,128)(2,1)S(1)} %collective-permute-done.27.refs_0_), channel_id=1, source_target_pairs={{0,8},{8,16},{16,24},{24,28},{28,20},{20,12},{12,4},{4,0},{2,6},{1... | collective-permute-start | bytes 786440 | tf_op jit(solution)/shard_map/ppermute | solution.py:358
  145.9 7.7 %collective-permute-start.36 = (bf16[512,256]{1,0:T(8,128)(2,1)S(1)}, bf16[512,256]{1,0:T(8,128)(2,1)S(1)}, u32[]{:S(2)}, u32[]{:S(2)}) collective-permute-start(bf16[512,256]{1,0:T(8,128)(2,1)S(1)} %collective-permute-done.24.refs_0_), channel_id=1, source_target_pairs={{0,2},{2,0},{4,6},{6,4},{8,10},{10,8},{12,14},{14,12},{16,18},{18,... | collective-permute-start | bytes 786440 | tf_op jit(solution)/shard_map/ppermute | solution.py:359
  145.9 7.7 %collective-permute-start.37 = (bf16[384,256]{1,0:T(8,128)(2,1)S(1)}, bf16[384,256]{1,0:T(8,128)(2,1)S(1)}, u32[]{:S(2)}, u32[]{:S(2)}) collective-permute-start(bf16[384,256]{1,0:T(8,128)(2,1)S(1)} %collective-permute-done.35.refs_1_), channel_id=1, source_target_pairs={{0,2},{2,0},{4,6},{6,4},{8,10},{10,8},{12,14},{14,12},{16,18},{18,... | collective-permute-start | bytes 589832 | tf_op jit(solution)/shard_map/ppermute | solution.py:359
  151.6 6.8 %collective-permute-start.34 = (bf16[512,256]{1,0:T(8,128)(2,1)S(1)}, bf16[512,256]{1,0:T(8,128)(2,1)S(1)}, u32[]{:S(2)}, u32[]{:S(2)}) collective-permute-start(bf16[512,256]{1,0:T(8,128)(2,1)S(1)} %collective-permute-done.30.refs_0_), channel_id=1, source_target_pairs={{0,8},{8,16},{16,24},{24,28},{28,20},{20,12},{12,4},{4,0},{2,6},{1... | collective-permute-start | bytes 786440 | tf_op jit(solution)/shard_map/ppermute | solution.py:358
  152.2 8.9 %collective-permute-start.42 = (bf16[512,256]{1,0:T(8,128)(2,1)S(1)}, bf16[512,256]{1,0:T(8,128)(2,1)S(1)}, u32[]{:S(2)}, u32[]{:S(2)}) collective-permute-start(bf16[512,256]{1,0:T(8,128)(2,1)S(1)} %collective-permute-done.27.refs_0_), channel_id=1, source_target_pairs={{0,2},{2,0},{4,6},{6,4},{8,10},{10,8},{12,14},{14,12},{16,18},{18,... | collective-permute-start | bytes 786440 | tf_op jit(solution)/shard_map/ppermute | solution.py:359
  153.6 7.5 %collective-permute-start.43 = (bf16[384,256]{1,0:T(8,128)(2,1)S(1)}, bf16[384,256]{1,0:T(8,128)(2,1)S(1)}, u32[]{:S(2)}, u32[]{:S(2)}) collective-permute-start(bf16[384,256]{1,0:T(8,128)(2,1)S(1)} %collective-permute-done.39.refs_1_), channel_id=1, source_target_pairs={{0,2},{2,0},{4,6},{6,4},{8,10},{10,8},{12,14},{14,12},{16,18},{18,... | collective-permute-start | bytes 589832 | tf_op jit(solution)/shard_map/ppermute | solution.py:359
  157.1 7.4 %collective-permute-start.41 = (bf16[384,256]{1,0:T(8,128)(2,1)S(1)}, bf16[384,256]{1,0:T(8,128)(2,1)S(1)}, u32[]{:S(2)}, u32[]{:S(2)}) collective-permute-start(bf16[384,256]{1,0:T(8,128)(2,1)S(1)} %collective-permute-done.40.refs_1_), channel_id=1, source_target_pairs={{0,8},{8,16},{16,24},{24,28},{28,20},{20,12},{12,4},{4,0},{2,6},{1... | collective-permute-start | bytes 589832 | tf_op jit(solution)/shard_map/ppermute | solution.py:358
  158.4 8.0 %collective-permute-start.38 = (bf16[512,256]{1,0:T(8,128)(2,1)S(1)}, bf16[512,256]{1,0:T(8,128)(2,1)S(1)}, u32[]{:S(2)}, u32[]{:S(2)}) collective-permute-start(bf16[512,256]{1,0:T(8,128)(2,1)S(1)} %collective-permute-done.34.refs_0_), channel_id=1, source_target_pairs={{0,8},{8,16},{16,24},{24,28},{28,20},{20,12},{12,4},{4,0},{2,6},{1... | collective-permute-start | bytes 786440 | tf_op jit(solution)/shard_map/ppermute | solution.py:358
  159.2 7.8 %collective-permute-start.50 = (bf16[384,256]{1,0:T(8,128)(2,1)S(1)}, bf16[384,256]{1,0:T(8,128)(2,1)S(1)}, u32[]{:S(2)}, u32[]{:S(2)}) collective-permute-start(bf16[384,256]{1,0:T(8,128)(2,1)S(1)} %collective-permute-done.40.refs_1_), channel_id=1, source_target_pairs={{0,2},{2,0},{4,6},{6,4},{8,10},{10,8},{12,14},{14,12},{16,18},{18,... | collective-permute-start | bytes 589832 | tf_op jit(solution)/shard_map/ppermute | solution.py:359
  165.9 7.6 %collective-permute-start.47 = (bf16[512,256]{1,0:T(8,128)(2,1)S(1)}, bf16[512,256]{1,0:T(8,128)(2,1)S(1)}, u32[]{:S(2)}, u32[]{:S(2)}) collective-permute-start(bf16[512,256]{1,0:T(8,128)(2,1)S(1)} %collective-permute-done.34.refs_0_), channel_id=1, source_target_pairs={{0,2},{2,0},{4,6},{6,4},{8,10},{10,8},{12,14},{14,12},{16,18},{18,... | collective-permute-start | bytes 786440 | tf_op jit(solution)/shard_map/ppermute | solution.py:359
  166.4 10.5 %collective-permute-start.45 = (bf16[512,256]{1,0:T(8,128)(2,1)S(1)}, bf16[512,256]{1,0:T(8,128)(2,1)S(1)}, u32[]{:S(2)}, u32[]{:S(2)}) collective-permute-start(bf16[512,256]{1,0:T(8,128)(2,1)S(1)} %collective-permute-done.38.refs_0_), channel_id=1, source_target_pairs={{0,2},{2,0},{4,6},{6,4},{8,10},{10,8},{12,14},{14,12},{16,18},{18,... | collective-permute-start | bytes 786440 | tf_op jit(solution)/shard_map/ppermute | solution.py:359
  167.0 6.4 %collective-permute-start.48 = (bf16[384,256]{1,0:T(8,128)(2,1)S(1)}, bf16[384,256]{1,0:T(8,128)(2,1)S(1)}, u32[]{:S(2)}, u32[]{:S(2)}) collective-permute-start(bf16[384,256]{1,0:T(8,128)(2,1)S(1)} %collective-permute-done.41.refs_1_), channel_id=1, source_target_pairs={{0,2},{2,0},{4,6},{6,4},{8,10},{10,8},{12,14},{14,12},{16,18},{18,... | collective-permute-start | bytes 589832 | tf_op jit(solution)/shard_map/ppermute | solution.py:359
  169.2 7.6 %collective-permute-start.46 = (bf16[384,256]{1,0:T(8,128)(2,1)S(1)}, bf16[384,256]{1,0:T(8,128)(2,1)S(1)}, u32[]{:S(2)}, u32[]{:S(2)}) collective-permute-start(bf16[384,256]{1,0:T(8,128)(2,1)S(1)} %collective-permute-done.44.refs_1_), channel_id=1, source_target_pairs={{0,2},{2,0},{4,6},{6,4},{8,10},{10,8},{12,14},{14,12},{16,18},{18,... | collective-permute-start | bytes 589832 | tf_op jit(solution)/shard_map/ppermute | solution.py:359
  (33 other events, 192.0 us)

commit v5 on v4

--- a/solution.py
+++ b/solution.py
@@ -23,6 +23,28 @@
 
 def params(mib):
     return pltpu.CompilerParams(vmem_limit_bytes=mib * MIB)
+
+
+def pack_kernel(ids_ref, base_ref, *out_refs):
+    for n, out_ref in enumerate(out_refs):
+        share = out_ref.shape[1]
+        start = pl.multiple_of(ids_ref[n] * share, LANES)
+        out_ref[...] = base_ref[:, pl.ds(start, share)]
+
+
+def pack_call(ids, base_b, share):
+    rows = base_b.shape[0]
+    count = base_b.shape[1] // share
+    vmem = pl.BlockSpec(memory_space=pltpu.VMEM)
+    return pl.pallas_call(
+        pack_kernel,
+        in_specs=[pl.BlockSpec(memory_space=pltpu.SMEM), vmem],
+        out_specs=[vmem] * count,
+        out_shape=[jax.ShapeDtypeStruct((rows, share), BF16)] * count,
+        compiler_params=params(16),
+        cost_estimate=cost(0, 4 * rows * share * count),
+        name="pack",
+    )(ids, base_b)
 
 
 def spread(x, lane):
@@ -126,8 +148,12 @@
     )(ids, *pieces)
 
 
-def back_kernel(ortho_t_ref, columns_ref, colsq_ref, *part_refs):
-    back_t = jnp.dot(ortho_t_ref[...], columns_ref[...], preferred_element_type=F32)
+def back_kernel(pieces, ids_ref, ortho_t_ref, *refs):
+    columns, (colsq_ref, *part_refs), whole_ref = refs[:pieces], refs[pieces:-1], refs[-1]
+    rows = columns[0].shape[0]
+    for n, piece in enumerate(columns):
+        whole_ref[pl.ds(pl.multiple_of(ids_ref[n] * rows, 16), rows), :] = piece[...]
+    back_t = jnp.dot(ortho_t_ref[...], whole_ref[...], preferred_element_type=F32)
     back = back_t.T.astype(BF16)
     start = 0
     for part_ref in part_refs:
@@ -138,20 +164,21 @@
     colsq_ref[...] = jnp.sum(wide * wide, axis=0, keepdims=True)
 
 
-def back_call(ortho_t, columns, parts):
+def back_call(ids, ortho_t, columns, parts):
     rank, total = ortho_t.shape
-    share = columns.shape[1]
+    share = columns[0].shape[1]
     vmem = pl.BlockSpec(memory_space=pltpu.VMEM)
     return pl.pallas_call(
-        back_kernel,
-        in_specs=[vmem] * 2,
+        functools.partial(back_kernel, len(columns)),
+        in_specs=[pl.BlockSpec(memory_space=pltpu.SMEM), vmem] + [vmem] * len(columns),
         out_specs=[vmem] * (1 + len(parts)),
         out_shape=[jax.ShapeDtypeStruct((1, rank), F32)]
         + [jax.ShapeDtypeStruct((part, rank), BF16) for part in parts],
+        scratch_shapes=[pltpu.VMEM((total, share), BF16)],
         compiler_params=params(24),
         cost_estimate=cost(2 * rank * total * share, total * share * 2),
         name="back",
-    )(ortho_t, columns)
+    )(ids, ortho_t, *columns)
 
 
 def output_kernel(parts, factor, carried, ids_ref, m_ref, g_ref, ortho_ref, colsq_ref, *refs):
@@ -253,15 +280,31 @@
     return [(n, n ^ 1) for n in range(count)]
 
 
-def gather_small(x, count):
+def tie(x, *work):
+    return lax.optimization_barrier((x, *work))[0] if work else x
+
+
+def gather_and_exchange(sketch, outgoing, count):
     chips = count // 2
     me = lax.axis_index("fsdp")
     place, core = position_of(me // 2, chips), me % 2
     up, down = ring_steps(count, False)
-    offsets, held = [0], [x]
-    ahead = behind = x
+    columns = {0: outgoing[0]}
+
+    def exchange(window, *after):
+        for k in window:
+            pairs = [(n, n ^ k) for n in range(count)]
+            columns[k] = lax.ppermute(tie(outgoing[k], *after), "fsdp", pairs)
+
+    far = [[k + chips] + [k] * (k > 0) for k in range(chips)]
+    exchange(far[0], sketch)
+    sketch = sketch + lax.ppermute(sketch, "tp", [(0, 1), (1, 0)])
+    offsets, held = [0], [sketch]
+    ahead = behind = sketch
     for step in range(1, chips // 2 + 1):
-        ahead, behind = lax.optimization_barrier((ahead, behind))
+        sent = [columns[k] for k in far[step - 2]] if step > 1 else []
+        ahead, behind = lax.optimization_barrier((ahead, behind, *sent))[:2]
+        exchange(far[step], ahead, behind)
         ahead = lax.ppermute(ahead, "fsdp", up)
         held.append(ahead)
         offsets.append(-step)
@@ -269,14 +312,12 @@
             behind = lax.ppermute(behind, "fsdp", down)
             held.append(behind)
             offsets.append(step)
+    for window in far[chips // 2 + 1 :]:
+        exchange(window, ahead, behind)
     other = [lax.ppermute(h, "fsdp", swap_pairs(count)) for h in held]
     chip = chip_at((place + jnp.array(offsets, jnp.int32)) % chips, chips)
     ids = jnp.concatenate([2 * chip + core, 2 * chip + 1 - core])
-    return held + other, ids.astype(jnp.int32), held
-
-
-def tie(x, *work):
-    return lax.optimization_barrier((x, *work))[0] if work else x
+    return held + other, ids.astype(jnp.int32), [columns[k] for k in range(count)]
 
 
 def sum_rounds(count, tp_count):
@@ -301,29 +342,26 @@
 
     base_b = (momentum + gradient.astype(F32)).astype(BF16)
     sketch = jnp.dot(base_b, basis, preferred_element_type=F32)
-    outgoing = jnp.pad(base_b, ((0, 0), (0, share * count - cols)))
-    outgoing = jnp.swapaxes(outgoing.reshape(rows, count, share), 0, 1)
-    if tp_count == 2:
-        sketch = sketch + lax.ppermute(sketch, "tp", [(0, 1), (1, 0)])
+    padded = jnp.pad(base_b, ((0, 0), (0, share * count - cols)))
+    if ring:
+        partners = me ^ jnp.arange(count, dtype=jnp.int32)
+        outgoing = pack_call(partners, padded, share)
+        pieces, ids, columns = gather_and_exchange(sketch, outgoing, count)
     else:
-        sketch = lax.psum(sketch, "tp")
-
-    if ring:
-        pieces, ids, travelled = gather_small(sketch, count)
-        outgoing = tie(outgoing, *travelled)
-    else:
-        whole = lax.all_gather(sketch, "fsdp", axis=0)
+        outgoing = jnp.swapaxes(padded.reshape(rows, count, share), 0, 1)
+        columns = lax.all_to_all(outgoing, "fsdp", 0, 0, tiled=True)
+        columns = [columns.reshape(rows * count, share)]
+        partners = jnp.zeros((1,), jnp.int32)
+        whole = lax.all_gather(lax.psum(sketch, "tp"), "fsdp", axis=0)
         pieces = [lax.dynamic_index_in_dim(whole, (me + n) % count, 0, False) for n in range(count)]
         ids = ((me + jnp.arange(count)) % count).astype(jnp.int32)
-    columns = lax.all_to_all(outgoing, "fsdp", 0, 0, tiled=True)
-    columns = columns.reshape(rows * count, share)
     ortho_t, ortho_here = factor_call(ids, pieces)
     momentum = pltpu.with_memory_space_constraint(momentum, pltpu.HBM)
     tiles = share // LANES
     cuts = [share]
     if ring and tiles > 1:
         cuts = [share - tiles // 2 * LANES, tiles // 2 * LANES]
-    part, *back = back_call(ortho_t, columns, cuts)
+    part, *back = back_call(partners, ortho_t, columns, cuts)
 
     outputs = functools.partial(output_call, factor=factor)
     if not ring:

time: 181 us -> 172 us (0.950)
  waiting for transfers between devices: 69 us -> 25.8 us
  starting transfers between devices: 54.9 us -> 89.5 us
    ppermute x16 -> x31, starting transfers between devices: 10.2 us -> 56.7 us  [the longest x15 31.5 us: exchange(): columns[k] = lax.ppermute(tie(outgoing[k], *after), 'fsdp', pairs)]
    all_to_all x1 -> x0, waiting for transfers between devices: 34.9 us -> none  [local(): columns = lax.all_to_all(outgoing, 'fsdp', 0, 0, tiled=True)]
    all_to_all x1 -> x0, starting transfers between devices: 10.2 us -> none  [local(): columns = lax.all_to_all(outgoing, 'fsdp', 0, 0, tiled=True)]
    ppermute x14, starting transfers between devices: 20.1 us -> 12.7 us  [local(): mine[step + 1].append(lax.ppermute(tie(block, *waiting), 'fsdp', turn))]
    ppermute x14, waiting for transfers between devices: 12.1 us -> 6.84 us  [local(): mine[step + 1].append(lax.ppermute(tie(block, *waiting), 'fsdp', turn))]
    ppermute x16, starting transfers between devices: 9.48 us -> 13.1 us  [local(): theirs[step].append(lax.ppermute(block, 'fsdp', swap))]
    ppermute x5, starting transfers between devices: 4.83 us -> 7.02 us  [local(): colsq = colsq + lax.ppermute(tie(colsq, block), axis, pairs)]
    ppermute x16 -> x31, waiting for transfers between devices: 14.8 us -> 13.2 us  [the longest x15 11.6 us: exchange(): columns[k] = lax.ppermute(tie(outgoing[k], *after), 'fsdp', pairs)]
  transfers between devices with their start and end apart: 52 -> 66, of which waited for: 24 -> 12; matrix products, arithmetic and copies ran while one was open for 1% -> 0% of each run, Pallas kernels for 21% -> 24%
where the time goes in v5:
time: 172 us
  starting transfers between devices  89.5 us (52%)
  Pallas kernels  46.4 us (27%)
  waiting for transfers between devices  25.8 us (15%)
  other arithmetic  4.06 us (2%)
  local copies, waits for them, and re-layouts  3.99 us (2%)
    ppermute x15, starting transfers between devices, exchange(): columns[k] = lax.ppermute(tie(outgoing[k], *after), 'fsdp', pairs)  31.5 us
    pallas_call x8, Pallas kernels, output_call(): pl.pallas_call(functools.partial(output_kernel, parts, factor, carried),...  27.6 us
    pallas_call x1, Pallas kernels, factor_call(): pl.pallas_call(functools.partial(factor_kernel, count), in_specs=[pl.Bloc...  14.7 us
    ppermute x16, starting transfers between devices, local(): theirs[step].append(lax.ppermute(block, 'fsdp', swap))  13.1 us
    ppermute x14, starting transfers between devices, local(): mine[step + 1].append(lax.ppermute(tie(block, *waiting), 'fsdp', turn))  12.7 us
    ppermute x15, waiting for transfers between devices, exchange(): columns[k] = lax.ppermute(tie(outgoing[k], *after), 'fsdp', pairs)  11.6 us
    ppermute x8, starting transfers between devices, gather_and_exchange(): other = [lax.ppermute(h, 'fsdp', swap_pairs(count)) for h in held]  11.5 us
    ppermute x4, starting transfers between devices, gather_and_exchange(): ahead = lax.ppermute(ahead, 'fsdp', up)  10 us
  transfers between devices with their start and end apart: 66, of which 12 were waited for; matrix products, arithmetic and copies ran while one was open for 0% of the time, Pallas kernels for 24%

profile of v5, /device:TPU:1, one launch (start us, length us, event | category | flops | bytes accessed | tf_op | source)
XLA Modules:
  0.0 171.9 jit_solution(8047182899482608828)
XLA Ops:
  0.6 3.9 %add_convert_fusion = bf16[96,13824]{1,0:T(8,128)(2,1)S(1)} fusion(f32[96,13824]{1,0:T(8,128)} %m_ref.15, bf16[96,13824]{1,0:T(8,128)(2,1)} %g_ref.15), kind=kLoop, calls=%fused_computation | loop fusion | flops 3981312 | bytes 10616832 | tf_op jit(solution)/shard_map/convert_element_type | solution.py:343
  17.8 3.2 %collective-permute-done.3.refs_8_ = bf16[96,896]{1,0:T(8,128)(2,1)S(1)} collective-permute-done((bf16[96,896]{1,0:T(8,128)(2,1)S(1)}, bf16[96,896]{1,0:T(8,128)(2,1)S(1)}, u32[]{:S(2)}, u32[]{:S(2)}) %collective-permute-start.3) | collective-permute-done | bytes 172064 | tf_op jit(solution)/shard_map/ppermute | solution.py:297
  21.8 6.4 %collective-permute-start.4 = (f32[96,256]{1,0:T(8,128)S(1)}, f32[96,256]{1,0:T(8,128)S(1)}, u32[]{:S(2)}, u32[]{:S(2)}) collective-permute-start(f32[96,256]{1,0:T(8,128)S(1)} %collective-permute-done.1.refs_1_), channel_id=1, source_target_pairs={{0,8},{2,10},{8,16},{10,18},{16,24},{18,26},{24,28},{26,30},{28,20... | collective-permute-start | bytes 294920 | tf_op jit(solution)/shard_map/ppermute | solution.py:308
  29.4 3.3 %collective-permute-start.10 = (bf16[96,896]{1,0:T(8,128)(2,1)S(1)}, bf16[96,896]{1,0:T(8,128)(2,1)S(1)}, u32[]{:S(2)}, u32[]{:S(2)}) collective-permute-start(bf16[96,896]{1,0:T(8,128)(2,1)S(1)} %get-tuple-element.94), channel_id=1, source_target_pairs={{0,20},{2,22},{4,16},{6,18},{8,28},{10,30},{12,24},{14,26},{16,4},... | collective-permute-start | bytes 516104 | tf_op jit(solution)/shard_map/ppermute | solution.py:297
  35.5 5.4 %collective-permute-start.13 = (f32[96,256]{1,0:T(8,128)S(1)}, f32[96,256]{1,0:T(8,128)S(1)}, u32[]{:S(2)}, u32[]{:S(2)}) collective-permute-start(f32[96,256]{1,0:T(8,128)S(1)} %add.149.refs_0_), channel_id=1, source_target_pairs={{0,2},{2,0},{4,6},{6,4},{8,10},{10,8},{12,14},{14,12},{16,18},{18,... | collective-permute-start | bytes 294920 | tf_op jit(solution)/shard_map/ppermute | solution.py:317
  47.2 2.9 %collective-permute-start.17 = (f32[96,256]{1,0:T(8,128)S(1)}, f32[96,256]{1,0:T(8,128)S(1)}, u32[]{:S(2)}, u32[]{:S(2)}) collective-permute-start(f32[96,256]{1,0:T(8,128)S(1)} %collective-permute-done.5.refs_4_), channel_id=1, source_target_pairs={{0,2},{2,0},{4,6},{6,4},{8,10},{10,8},{12,14},{14,12},{16,18},{18,... | collective-permute-start | bytes 294920 | tf_op jit(solution)/shard_map/ppermute | solution.py:317
  53.1 8.4 %collective-permute-done.26.refs_11_ = bf16[96,896]{1,0:T(8,128)(2,1)S(1)} collective-permute-done((bf16[96,896]{1,0:T(8,128)(2,1)S(1)}, bf16[96,896]{1,0:T(8,128)(2,1)S(1)}, u32[]{:S(2)}, u32[]{:S(2)}) %collective-permute-start.26) | collective-permute-done | bytes 172064 | tf_op jit(solution)/shard_map/ppermute | solution.py:297
  61.5 2.7 %collective-permute-start.30 = (bf16[96,896]{1,0:T(8,128)(2,1)S(1)}, bf16[96,896]{1,0:T(8,128)(2,1)S(1)}, u32[]{:S(2)}, u32[]{:S(2)}) collective-permute-start(bf16[96,896]{1,0:T(8,128)(2,1)S(1)} %get-tuple-element.121), channel_id=1, source_target_pairs={{0,30},{2,28},{4,26},{6,24},{8,22},{10,20},{12,18},{14,16},{16,14}... | collective-permute-start | bytes 516104 | tf_op jit(solution)/shard_map/ppermute | solution.py:297
  72.0 9.1 %collective-permute-start.23 = (bf16[96,896]{1,0:T(8,128)(2,1)S(1)}, bf16[96,896]{1,0:T(8,128)(2,1)S(1)}, u32[]{:S(2)}, u32[]{:S(2)}) collective-permute-start(bf16[96,896]{1,0:T(8,128)(2,1)S(1)} %get-tuple-element.107), channel_id=1, source_target_pairs={{0,10},{2,8},{4,14},{6,12},{8,2},{10,0},{12,6},{14,4},{16,26},{18,... | collective-permute-start | bytes 516104 | tf_op jit(solution)/shard_map/ppermute | solution.py:297
  81.1 14.7 %factor.1 = (bf16[256,1536]{1,0:T(8,128)(2,1)S(1)}, bf16[96,256]{1,0:T(8,128)(2,1)S(1)}) custom-call(s32[16]{0:T(128)S(1)} %pad_add_fusion.1.ids_ref, f32[96,256]{1,0:T(8,128)S(1)} %add.149.refs_0_, f32[96,256]{1,0:T(8,128)S(1)} %collective-permute-done.1.refs_1_, f32[96,256]{1,0:T(8,128)S(1)} %collective-permute-done.2.refs_2_, ...), custom_call_target="tpu_custom_call" | custom-call | flops 4026531840 | bytes 2359296 | tf_op jit(solution)/shard_map/factor/pallas_call | solution.py:136
  95.9 2.5 %back.1 = (f32[1,256]{1,0:T(1,128)S(1)}, bf16[512,256]{1,0:T(8,128)(2,1)S(1)}, bf16[384,256]{1,0:T(8,128)(2,1)}) custom-call(s32[16]{0:T(128)S(1)} %iota_xor_fusion.ids_ref, bf16[256,1536]{1,0:T(8,128)(2,1)S(1)} %get-tuple-element.99.ortho_t_ref, bf16[96,896]{1,0:T(8,128)(2,1)S(1)} %get-tuple-element.100.refs_0_, ...), custom_call_target="tpu_custom_call" | custom-call | flops 704643072 | bytes 2752512 | tf_op jit(solution)/shard_map/back/pallas_call | solution.py:171
  98.4 2.5 %collective-permute-start.33 = (bf16[512,256]{1,0:T(8,128)(2,1)S(1)}, bf16[512,256]{1,0:T(8,128)(2,1)S(1)}, u32[]{:S(2)}, u32[]{:S(2)}) collective-permute-start(bf16[512,256]{1,0:T(8,128)(2,1)S(1)} %get-tuple-element.123.refs_0_), channel_id=1, source_target_pairs={{0,8},{8,16},{16,24},{24,28},{28,20},{20,12},{12,4},{4,0},{2,6},{1... | collective-permute-start | bytes 786440 | tf_op jit(solution)/shard_map/ppermute | solution.py:396
  100.9 3.3 %collective-permute-done.33.refs_0_ = bf16[512,256]{1,0:T(8,128)(2,1)S(1)} collective-permute-done((bf16[512,256]{1,0:T(8,128)(2,1)S(1)}, bf16[512,256]{1,0:T(8,128)(2,1)S(1)}, u32[]{:S(2)}, u32[]{:S(2)}) %collective-permute-start.33) | collective-permute-done | bytes 262176 | tf_op jit(solution)/shard_map/ppermute | solution.py:396
  118.0 2.9 %collective-permute-start.38 = (f32[1,256]{1,0:T(1,128)S(1)}, f32[1,256]{1,0:T(1,128)S(1)}, u32[]{:S(2)}, u32[]{:S(2)}) collective-permute-start(f32[1,256]{1,0:T(1,128)S(1)} %add.153), channel_id=1, source_target_pairs={{0,16},{2,18},{4,20},{6,22},{8,24},{10,26},{12,28},{14,30},{16,0},... | collective-permute-start | bytes 3080 | tf_op jit(solution)/shard_map/ppermute | solution.py:400
  123.6 3.5 %outputs.8 = (f32[96,13824]{1,0:T(8,128)}, bf16[13824,256]{1,0:T(8,128)(2,1)}, bf16[96,13824]{1,0:T(8,128)(2,1)}) custom-call(s32[2]{0:T(128)S(1)} %get-tuple-element.165.ids_ref, f32[96,13824]{1,0:T(8,128)} %m_ref.15, bf16[96,13824]{1,0:T(8,128)(2,1)S(1)} %copy-done, bf16[96,256]{1,0:T(8,128)(2,1)S(1)} %get-tuple-element.98.ortho_ref, ...), custom_call_target="tpu_custom_call" | custom-call | flops 176160768 | bytes 3899392 | tf_op jit(solution)/shard_map/outputs/pallas_call | solution.py:225
  130.5 3.5 %outputs.9 = (f32[96,13824]{1,0:T(8,128)}, bf16[13824,256]{1,0:T(8,128)(2,1)}, bf16[96,13824]{1,0:T(8,128)(2,1)}) custom-call(s32[2]{0:T(128)S(1)} %get-tuple-element.164.ids_ref, f32[96,13824]{1,0:T(8,128)} %m_ref.15, bf16[96,13824]{1,0:T(8,128)(2,1)S(1)} %copy-done, ...), custom_call_target="tpu_custom_call", output_to_operand_aliasing={{0}: (9, {}), {1}: (10, {}), {2}: (11, {})} | custom-call | flops 176160768 | bytes 3899392 | tf_op jit(solution)/shard_map/outputs/pallas_call | solution.py:225
  137.7 3.4 %outputs.10 = (f32[96,13824]{1,0:T(8,128)}, bf16[13824,256]{1,0:T(8,128)(2,1)}, bf16[96,13824]{1,0:T(8,128)(2,1)}) custom-call(s32[2]{0:T(128)S(1)} %get-tuple-element.163.ids_ref, f32[96,13824]{1,0:T(8,128)} %m_ref.15, bf16[96,13824]{1,0:T(8,128)(2,1)S(1)} %copy-done, ...), custom_call_target="tpu_custom_call", output_to_operand_aliasing={{0}: (9, {}), {1}: (10, {}), {2}: (11, {})} | custom-call | flops 176160768 | bytes 3899392 | tf_op jit(solution)/shard_map/outputs/pallas_call | solution.py:225
  144.9 3.4 %outputs.11 = (f32[96,13824]{1,0:T(8,128)}, bf16[13824,256]{1,0:T(8,128)(2,1)}, bf16[96,13824]{1,0:T(8,128)(2,1)}) custom-call(s32[2]{0:T(128)S(1)} %get-tuple-element.162.ids_ref, f32[96,13824]{1,0:T(8,128)} %m_ref.15, bf16[96,13824]{1,0:T(8,128)(2,1)S(1)} %copy-done, ...), custom_call_target="tpu_custom_call", output_to_operand_aliasing={{0}: (9, {}), {1}: (10, {}), {2}: (11, {})} | custom-call | flops 176160768 | bytes 3899392 | tf_op jit(solution)/shard_map/outputs/pallas_call | solution.py:225
  149.9 2.7 %collective-permute-start.65 = (bf16[384,256]{1,0:T(8,128)(2,1)S(1)}, bf16[384,256]{1,0:T(8,128)(2,1)S(1)}, u32[]{:S(2)}, u32[]{:S(2)}) collective-permute-start(bf16[384,256]{1,0:T(8,128)(2,1)S(1)} %collective-permute-done.55.refs_1_), channel_id=1, source_target_pairs={{0,2},{2,0},{4,6},{6,4},{8,10},{10,8},{12,14},{14,12},{16,18},{18,... | collective-permute-start | bytes 589832 | tf_op jit(solution)/shard_map/ppermute | solution.py:397
  152.6 3.4 %outputs.12 = (f32[96,13824]{1,0:T(8,128)}, bf16[13824,256]{1,0:T(8,128)(2,1)}, bf16[96,13824]{1,0:T(8,128)(2,1)}) custom-call(s32[2]{0:T(128)S(1)} %get-tuple-element.161.ids_ref, f32[96,13824]{1,0:T(8,128)} %m_ref.15, bf16[96,13824]{1,0:T(8,128)(2,1)S(1)} %copy-done, ...), custom_call_target="tpu_custom_call", output_to_operand_aliasing={{0}: (9, {}), {1}: (10, {}), {2}: (11, {})} | custom-call | flops 176160768 | bytes 3899392 | tf_op jit(solution)/shard_map/outputs/pallas_call | solution.py:225
  157.8 3.0 %collective-permute-done.59.refs_1_ = bf16[384,256]{1,0:T(8,128)(2,1)S(1)} collective-permute-done((bf16[384,256]{1,0:T(8,128)(2,1)S(1)}, bf16[384,256]{1,0:T(8,128)(2,1)S(1)}, u32[]{:S(2)}, u32[]{:S(2)}) %collective-permute-start.59) | collective-permute-done | bytes 196640 | tf_op jit(solution)/shard_map/ppermute | solution.py:396
  161.5 3.4 %outputs.13 = (f32[96,13824]{1,0:T(8,128)}, bf16[13824,256]{1,0:T(8,128)(2,1)}, bf16[96,13824]{1,0:T(8,128)(2,1)}) custom-call(s32[2]{0:T(128)S(1)} %get-tuple-element.159.ids_ref, f32[96,13824]{1,0:T(8,128)} %m_ref.15, bf16[96,13824]{1,0:T(8,128)(2,1)S(1)} %copy-done, ...), custom_call_target="tpu_custom_call", output_to_operand_aliasing={{0}: (9, {}), {1}: (10, {}), {2}: (11, {})} | custom-call | flops 176160768 | bytes 3899392 | tf_op jit(solution)/shard_map/outputs/pallas_call | solution.py:225
  165.0 3.4 %outputs.14 = (f32[96,13824]{1,0:T(8,128)}, bf16[13824,256]{1,0:T(8,128)(2,1)}, bf16[96,13824]{1,0:T(8,128)(2,1)}) custom-call(s32[2]{0:T(128)S(1)} %get-tuple-element.160.ids_ref, f32[96,13824]{1,0:T(8,128)} %m_ref.15, bf16[96,13824]{1,0:T(8,128)(2,1)S(1)} %copy-done, ...), custom_call_target="tpu_custom_call", output_to_operand_aliasing={{0}: (9, {}), {1}: (10, {}), {2}: (11, {})} | custom-call | flops 176160768 | bytes 3899392 | tf_op jit(solution)/shard_map/outputs/pallas_call | solution.py:225
  168.4 3.4 %outputs.15 = (f32[96,13824]{1,0:T(8,128)}, bf16[13824,256]{1,0:T(8,128)(2,1)}, bf16[96,13824]{1,0:T(8,128)(2,1)}) custom-call(s32[2]{0:T(128)S(1)} %get-tuple-element.166.ids_ref, f32[96,13824]{1,0:T(8,128)} %m_ref.15, bf16[96,13824]{1,0:T(8,128)(2,1)S(1)} %copy-done, ...), custom_call_target="tpu_custom_call", output_to_operand_aliasing={{0}: (9, {}), {1}: (10, {}), {2}: (11, {})} | custom-call | flops 176160768 | bytes 3899392 | tf_op jit(solution)/shard_map/outputs/pallas_call | solution.py:225
  (153 shorter events, 66.5 us)
Async XLA Ops:
  11.1 9.9 %collective-permute-start.3 = (bf16[96,896]{1,0:T(8,128)(2,1)S(1)}, bf16[96,896]{1,0:T(8,128)(2,1)S(1)}, u32[]{:S(2)}, u32[]{:S(2)}) collective-permute-start(bf16[96,896]{1,0:T(8,128)(2,1)S(1)} %get-tuple-element.84), channel_id=1, source_target_pairs={{0,16},{2,18},{4,20},{6,22},{8,24},{10,26},{12,28},{14,30},{16,0},... | collective-permute-start | bytes 516104 | tf_op jit(solution)/shard_map/ppermute | solution.py:297
  13.5 16.0 %collective-permute-start.7 = (bf16[96,896]{1,0:T(8,128)(2,1)S(1)}, bf16[96,896]{1,0:T(8,128)(2,1)S(1)}, u32[]{:S(2)}, u32[]{:S(2)}) collective-permute-start(bf16[96,896]{1,0:T(8,128)(2,1)S(1)} %get-tuple-element.90), channel_id=1, source_target_pairs={{0,2},{2,0},{4,6},{6,4},{8,10},{10,8},{12,14},{14,12},{16,18},{18,... | collective-permute-start | bytes 516104 | tf_op jit(solution)/shard_map/ppermute | solution.py:297
  16.2 16.5 %collective-permute-start.6 = (bf16[96,896]{1,0:T(8,128)(2,1)S(1)}, bf16[96,896]{1,0:T(8,128)(2,1)S(1)}, u32[]{:S(2)}, u32[]{:S(2)}) collective-permute-start(bf16[96,896]{1,0:T(8,128)(2,1)S(1)} %get-tuple-element.88), channel_id=1, source_target_pairs={{0,18},{2,16},{4,22},{6,20},{8,26},{10,24},{12,30},{14,28},{16,2},... | collective-permute-start | bytes 516104 | tf_op jit(solution)/shard_map/ppermute | solution.py:297
  21.8 11.7 %collective-permute-start.4 = (f32[96,256]{1,0:T(8,128)S(1)}, f32[96,256]{1,0:T(8,128)S(1)}, u32[]{:S(2)}, u32[]{:S(2)}) collective-permute-start(f32[96,256]{1,0:T(8,128)S(1)} %collective-permute-done.1.refs_1_), channel_id=1, source_target_pairs={{0,8},{2,10},{8,16},{10,18},{16,24},{18,26},{24,28},{26,30},{28,20... | collective-permute-start | bytes 294920 | tf_op jit(solution)/shard_map/ppermute | solution.py:308
  28.2 12.7 %collective-permute-start.11 = (bf16[96,896]{1,0:T(8,128)(2,1)S(1)}, bf16[96,896]{1,0:T(8,128)(2,1)S(1)}, u32[]{:S(2)}, u32[]{:S(2)}) collective-permute-start(bf16[96,896]{1,0:T(8,128)(2,1)S(1)} %get-tuple-element.96), channel_id=1, source_target_pairs={{0,4},{2,6},{4,0},{6,2},{8,12},{10,14},{12,8},{14,10},{16,20},{18,... | collective-permute-start | bytes 516104 | tf_op jit(solution)/shard_map/ppermute | solution.py:297
  29.4 12.1 %collective-permute-start.10 = (bf16[96,896]{1,0:T(8,128)(2,1)S(1)}, bf16[96,896]{1,0:T(8,128)(2,1)S(1)}, u32[]{:S(2)}, u32[]{:S(2)}) collective-permute-start(bf16[96,896]{1,0:T(8,128)(2,1)S(1)} %get-tuple-element.94), channel_id=1, source_target_pairs={{0,20},{2,22},{4,16},{6,18},{8,28},{10,30},{12,24},{14,26},{16,4},... | collective-permute-start | bytes 516104 | tf_op jit(solution)/shard_map/ppermute | solution.py:297
  33.5 8.8 %collective-permute-start.8 = (f32[96,256]{1,0:T(8,128)S(1)}, f32[96,256]{1,0:T(8,128)S(1)}, u32[]{:S(2)}, u32[]{:S(2)}) collective-permute-start(f32[96,256]{1,0:T(8,128)S(1)} %collective-permute-done.4.refs_3_), channel_id=1, source_target_pairs={{0,8},{2,10},{8,16},{10,18},{16,24},{18,26},{24,28},{26,30},{28,20... | collective-permute-start | bytes 294920 | tf_op jit(solution)/shard_map/ppermute | solution.py:308
  35.5 11.8 %collective-permute-start.13 = (f32[96,256]{1,0:T(8,128)S(1)}, f32[96,256]{1,0:T(8,128)S(1)}, u32[]{:S(2)}, u32[]{:S(2)}) collective-permute-start(f32[96,256]{1,0:T(8,128)S(1)} %add.149.refs_0_), channel_id=1, source_target_pairs={{0,2},{2,0},{4,6},{6,4},{8,10},{10,8},{12,14},{14,12},{16,18},{18,... | collective-permute-start | bytes 294920 | tf_op jit(solution)/shard_map/ppermute | solution.py:317
  45.6 15.9 %collective-permute-start.26 = (bf16[96,896]{1,0:T(8,128)(2,1)S(1)}, bf16[96,896]{1,0:T(8,128)(2,1)S(1)}, u32[]{:S(2)}, u32[]{:S(2)}) collective-permute-start(bf16[96,896]{1,0:T(8,128)(2,1)S(1)} %get-tuple-element.113), channel_id=1, source_target_pairs={{0,22},{2,20},{4,18},{6,16},{8,30},{10,28},{12,26},{14,24},{16,6},... | collective-permute-start | bytes 516104 | tf_op jit(solution)/shard_map/ppermute | solution.py:297
  50.2 14.0 %collective-permute-start.21 = (bf16[96,896]{1,0:T(8,128)(2,1)S(1)}, bf16[96,896]{1,0:T(8,128)(2,1)S(1)}, u32[]{:S(2)}, u32[]{:S(2)}) collective-permute-start(bf16[96,896]{1,0:T(8,128)(2,1)S(1)} %get-tuple-element.102), channel_id=1, source_target_pairs={{0,6},{2,4},{4,2},{6,0},{8,14},{10,12},{12,10},{14,8},{16,22},{18,... | collective-permute-start | bytes 516104 | tf_op jit(solution)/shard_map/ppermute | solution.py:297
  50.5 16.7 %collective-permute-start.27 = (bf16[96,896]{1,0:T(8,128)(2,1)S(1)}, bf16[96,896]{1,0:T(8,128)(2,1)S(1)}, u32[]{:S(2)}, u32[]{:S(2)}) collective-permute-start(bf16[96,896]{1,0:T(8,128)(2,1)S(1)} %get-tuple-element.115), channel_id=1, source_target_pairs={{0,24},{2,26},{4,28},{6,30},{8,16},{10,18},{12,20},{14,22},{16,8},... | collective-permute-start | bytes 516104 | tf_op jit(solution)/shard_map/ppermute | solution.py:297
  52.0 17.6 %collective-permute-start.22 = (bf16[96,896]{1,0:T(8,128)(2,1)S(1)}, bf16[96,896]{1,0:T(8,128)(2,1)S(1)}, u32[]{:S(2)}, u32[]{:S(2)}) collective-permute-start(bf16[96,896]{1,0:T(8,128)(2,1)S(1)} %get-tuple-element.105), channel_id=1, source_target_pairs={{0,8},{2,10},{4,12},{6,14},{8,0},{10,2},{12,4},{14,6},{16,24},{18,... | collective-permute-start | bytes 516104 | tf_op jit(solution)/shard_map/ppermute | solution.py:297
  52.0 12.2 %collective-permute-start.18 = (f32[96,256]{1,0:T(8,128)S(1)}, f32[96,256]{1,0:T(8,128)S(1)}, u32[]{:S(2)}, u32[]{:S(2)}) collective-permute-start(f32[96,256]{1,0:T(8,128)S(1)} %collective-permute-done.8.refs_5_), channel_id=1, source_target_pairs={{0,2},{2,0},{4,6},{6,4},{8,10},{10,8},{12,14},{14,12},{16,18},{18,... | collective-permute-start | bytes 294920 | tf_op jit(solution)/shard_map/ppermute | solution.py:317
  61.5 10.5 %collective-permute-start.30 = (bf16[96,896]{1,0:T(8,128)(2,1)S(1)}, bf16[96,896]{1,0:T(8,128)(2,1)S(1)}, u32[]{:S(2)}, u32[]{:S(2)}) collective-permute-start(bf16[96,896]{1,0:T(8,128)(2,1)S(1)} %get-tuple-element.121), channel_id=1, source_target_pairs={{0,30},{2,28},{4,26},{6,24},{8,22},{10,20},{12,18},{14,16},{16,14}... | collective-permute-start | bytes 516104 | tf_op jit(solution)/shard_map/ppermute | solution.py:297
  65.4 30.4 %collective-permute-start.29 = (bf16[96,896]{1,0:T(8,128)(2,1)}, bf16[96,896]{1,0:T(8,128)(2,1)S(1)}, u32[]{:S(2)}, u32[]{:S(2)}) collective-permute-start(bf16[96,896]{1,0:T(8,128)(2,1)} %get-tuple-element.119), channel_id=1, source_target_pairs={{0,28},{2,30},{4,24},{6,26},{8,20},{10,22},{12,16},{14,18},{16,12}... | collective-permute-start | bytes 516104 | tf_op jit(solution)/shard_map/ppermute | solution.py:297
  67.2 28.6 %collective-permute-start.28 = (bf16[96,896]{1,0:T(8,128)(2,1)}, bf16[96,896]{1,0:T(8,128)(2,1)S(1)}, u32[]{:S(2)}, u32[]{:S(2)}) collective-permute-start(bf16[96,896]{1,0:T(8,128)(2,1)} %get-tuple-element.117), channel_id=1, source_target_pairs={{0,26},{2,24},{4,30},{6,28},{8,18},{10,16},{12,22},{14,20},{16,10}... | collective-permute-start | bytes 516104 | tf_op jit(solution)/shard_map/ppermute | solution.py:297
  69.6 26.2 %collective-permute-start.25 = (bf16[96,896]{1,0:T(8,128)(2,1)}, bf16[96,896]{1,0:T(8,128)(2,1)S(1)}, u32[]{:S(2)}, u32[]{:S(2)}) collective-permute-start(bf16[96,896]{1,0:T(8,128)(2,1)} %get-tuple-element.111), channel_id=1, source_target_pairs={{0,14},{2,12},{4,10},{6,8},{8,6},{10,4},{12,2},{14,0},{16,30},{18,... | collective-permute-start | bytes 516104 | tf_op jit(solution)/shard_map/ppermute | solution.py:297
  69.6 26.2 %collective-permute-start.24 = (bf16[96,896]{1,0:T(8,128)(2,1)}, bf16[96,896]{1,0:T(8,128)(2,1)S(1)}, u32[]{:S(2)}, u32[]{:S(2)}) collective-permute-start(bf16[96,896]{1,0:T(8,128)(2,1)} %get-tuple-element.109), channel_id=1, source_target_pairs={{0,12},{2,14},{4,8},{6,10},{8,4},{10,6},{12,0},{14,2},{16,28},{18,... | collective-permute-start | bytes 516104 | tf_op jit(solution)/shard_map/ppermute | solution.py:297
  72.0 23.9 %collective-permute-start.23 = (bf16[96,896]{1,0:T(8,128)(2,1)S(1)}, bf16[96,896]{1,0:T(8,128)(2,1)S(1)}, u32[]{:S(2)}, u32[]{:S(2)}) collective-permute-start(bf16[96,896]{1,0:T(8,128)(2,1)S(1)} %get-tuple-element.107), channel_id=1, source_target_pairs={{0,10},{2,8},{4,14},{6,12},{8,2},{10,0},{12,6},{14,4},{16,26},{18,... | collective-permute-start | bytes 516104 | tf_op jit(solution)/shard_map/ppermute | solution.py:297
  110.4 13.1 %collective-permute-start.40 = (bf16[512,256]{1,0:T(8,128)(2,1)S(1)}, bf16[512,256]{1,0:T(8,128)(2,1)S(1)}, u32[]{:S(2)}, u32[]{:S(2)}) collective-permute-start(bf16[512,256]{1,0:T(8,128)(2,1)S(1)} %get-tuple-element.123.refs_0_), channel_id=1, source_target_pairs={{0,2},{2,0},{4,6},{6,4},{8,10},{10,8},{12,14},{14,12},{16,18},{18,... | collective-permute-start | bytes 786440 | tf_op jit(solution)/shard_map/ppermute | solution.py:397
  112.2 14.9 %collective-permute-start.39 = (bf16[512,256]{1,0:T(8,128)(2,1)S(1)}, bf16[512,256]{1,0:T(8,128)(2,1)S(1)}, u32[]{:S(2)}, u32[]{:S(2)}) collective-permute-start(bf16[512,256]{1,0:T(8,128)(2,1)S(1)} %collective-permute-done.37.refs_0_), channel_id=1, source_target_pairs={{0,8},{8,16},{16,24},{24,28},{28,20},{20,12},{12,4},{4,0},{2,6},{1... | collective-permute-start | bytes 786440 | tf_op jit(solution)/shard_map/ppermute | solution.py:396
  112.8 10.8 %collective-permute-start.41 = (bf16[384,256]{1,0:T(8,128)(2,1)}, bf16[384,256]{1,0:T(8,128)(2,1)S(1)}, u32[]{:S(2)}, u32[]{:S(2)}) collective-permute-start(bf16[384,256]{1,0:T(8,128)(2,1)} %get-tuple-element.125.refs_1_), channel_id=1, source_target_pairs={{0,2},{2,0},{4,6},{6,4},{8,10},{10,8},{12,14},{14,12},{16,18},{18,... | collective-permute-start | bytes 589832 | tf_op jit(solution)/shard_map/ppermute | solution.py:397
  116.7 12.6 %collective-permute-start.46 = (bf16[384,256]{1,0:T(8,128)(2,1)}, bf16[384,256]{1,0:T(8,128)(2,1)S(1)}, u32[]{:S(2)}, u32[]{:S(2)}) collective-permute-start(bf16[384,256]{1,0:T(8,128)(2,1)} %collective-permute-done.35.refs_1_), channel_id=1, source_target_pairs={{0,8},{8,16},{16,24},{24,28},{28,20},{20,12},{12,4},{4,0},{2,6},{1... | collective-permute-start | bytes 589832 | tf_op jit(solution)/shard_map/ppermute | solution.py:396
  157.1 11.3 %collective-permute-start.60 = (bf16[512,256]{1,0:T(8,128)(2,1)S(1)}, bf16[512,256]{1,0:T(8,128)(2,1)S(1)}, u32[]{:S(2)}, u32[]{:S(2)}) collective-permute-start(bf16[512,256]{1,0:T(8,128)(2,1)S(1)} %collective-permute-done.53.refs_0_), channel_id=1, source_target_pairs={{0,2},{2,0},{4,6},{6,4},{8,10},{10,8},{12,14},{14,12},{16,18},{18,... | collective-permute-start | bytes 786440 | tf_op jit(solution)/shard_map/ppermute | solution.py:397
  (51 other events, 424.6 us)

commit v6 on v5

--- a/solution.py
+++ b/solution.py
@@ -25,16 +25,41 @@
     return pltpu.CompilerParams(vmem_limit_bytes=mib * MIB)
 
 
+def by_width(block, cols, share, start, stop, act):
+    last = (cols - 1) // share
+    width, short = stop - start, max(0, min(cols - last * share, stop) - start)
+    if short == width:
+        act(width)
+        return
+
+    @pl.when(block < last)
+    def _():
+        act(width)
+
+    if short:
+
+        @pl.when(block == last)
+        def _():
+            act(short)
+
+
 def pack_kernel(ids_ref, base_ref, *out_refs):
+    cols = base_ref.shape[1]
     for n, out_ref in enumerate(out_refs):
         share = out_ref.shape[1]
         start = pl.multiple_of(ids_ref[n] * share, LANES)
-        out_ref[...] = base_ref[:, pl.ds(start, share)]
-
-
-def pack_call(ids, base_b, share):
-    rows = base_b.shape[0]
-    count = base_b.shape[1] // share
+
+        def fill(width):
+            out_ref[:, :width] = base_ref[:, pl.ds(start, width)].astype(BF16)
+            if width < share:
+                out_ref[:, width:] = jnp.zeros((out_ref.shape[0], share - width), BF16)
+
+        by_width(ids_ref[n], cols, share, 0, share, fill)
+
+
+def pack_call(ids, base, share):
+    rows = base.shape[0]
+    count = ids.shape[0]
     vmem = pl.BlockSpec(memory_space=pltpu.VMEM)
     return pl.pallas_call(
         pack_kernel,
@@ -42,9 +67,9 @@
         out_specs=[vmem] * count,
         out_shape=[jax.ShapeDtypeStruct((rows, share), BF16)] * count,
         compiler_params=params(16),
-        cost_estimate=cost(0, 4 * rows * share * count),
+        cost_estimate=cost(0, 6 * rows * share * count),
         name="pack",
-    )(ids, base_b)
+    )(ids, base)
 
 
 def spread(x, lane):
@@ -181,74 +206,88 @@
     )(ids, ortho_t, *columns)
 
 
-def output_kernel(parts, factor, carried, ids_ref, m_ref, g_ref, ortho_ref, colsq_ref, *refs):
-    count = len(refs) - carried - 3
-    pieces, (nm_ref, nb_ref, up_ref) = refs[:count], refs[count + carried :]
-    step = pl.program_id(0)
+def output_kernel(parts, factor, ids_ref, base_ref, ortho_ref, colsq_ref, *refs):
+    *pieces, nm_ref, nb_ref, up_ref, nm_tile, nb_tile, up_tile, sems = refs
+    share, cols = nm_tile.shape[2], nm_ref.shape[1]
     scale = lax.rsqrt(colsq_ref[...] + 1e-06)
     ortho = ortho_ref[...]
     over = (((1,), (1,)), ((), ()))
 
-    def write(piece, here):
-        back = piece[...]
-        unit = (back.astype(F32) * scale).astype(BF16)
-        nb_ref[here, :] = unit
-        base = m_ref[:, here] + g_ref[:, here].astype(F32)
-        nm_ref[:, here] = base - 0.05 * lax.dot_general(
-            ortho, back, over, preferred_element_type=F32
+    def copies(n, part, start, width):
+        there = pl.ds(pl.multiple_of(ids_ref[n] * share + start, LANES), width)
+        here = slice(start, start + width)
+        return (
+            pltpu.make_async_copy(nm_tile.at[n, :, here], nm_ref.at[:, there], sems.at[n, part, 0]),
+            pltpu.make_async_copy(nb_tile.at[n, here, :], nb_ref.at[there, :], sems.at[n, part, 1]),
+            pltpu.make_async_copy(up_tile.at[n, :, here], up_ref.at[:, there], sems.at[n, part, 2]),
         )
-        up_ref[:, here] = (
-            factor * lax.dot_general(ortho, unit, over, preferred_element_type=F32)
-        ).astype(BF16)
-
-    for n in range(count // parts):
-
-        @pl.when(step == n)
-        def _():
-            start = 0
-            for piece in pieces[n * parts : (n + 1) * parts]:
-                stop = start + piece.shape[0]
-                write(piece, slice(start, stop))
-                start = stop
-
-
-def output_call(ids, momentum, gradient, ortho, colsq, blocks, factor, previous):
-    rows, cols = momentum.shape
-    rank = ortho.shape[1]
+
+    ranges = []
+    for n in range(nm_tile.shape[0]):
+        start = 0
+        for part in range(parts):
+            piece = pieces[n * parts + part]
+            stop = start + piece.shape[0]
+
+            def compute(width):
+                here = slice(start, start + width)
+                there = pl.ds(pl.multiple_of(ids_ref[n] * share + start, LANES), width)
+                back = piece[:width, :]
+                unit = (back.astype(F32) * scale).astype(BF16)
+                nb_tile[n, here, :] = unit
+                nm_tile[n, :, here] = base_ref[:, there] - 0.05 * lax.dot_general(
+                    ortho, back, over, preferred_element_type=F32
+                )
+                up_tile[n, :, here] = (
+                    factor * lax.dot_general(ortho, unit, over, preferred_element_type=F32)
+                ).astype(BF16)
+                for copy in copies(n, part, start, width):
+                    copy.start()
+
+            by_width(ids_ref[n], cols, share, start, stop, compute)
+            ranges.append((n, part, start, stop))
+            start = stop
+
+    for n, part, start, stop in ranges:
+
+        def wait(width):
+            for copy in copies(n, part, start, width):
+                copy.wait()
+
+        by_width(ids_ref[n], cols, share, start, stop, wait)
+
+
+def output_call(ids, base, cols, ortho, colsq, blocks, factor, previous):
+    rows, rank = ortho.shape
     count, parts = len(blocks), len(blocks[0])
     pieces = [part for block in blocks for part in block]
     share = sum(part.shape[0] for part in blocks[0])
-    wide = pl.BlockSpec((rows, share), lambda i, ids: (0, ids[i]))
-    tall = pl.BlockSpec((share, rank), lambda i, ids: (ids[i], 0))
-    carried = 3 if previous else 0
-    aliases = {5 + len(pieces) + n: n for n in range(carried)}
+    previous = previous or ()
+    vmem, hbm = pl.BlockSpec(memory_space=pltpu.VMEM), pl.BlockSpec(memory_space=pltpu.HBM)
     return pl.pallas_call(
-        functools.partial(output_kernel, parts, factor, carried),
-        grid_spec=pltpu.PrefetchScalarGridSpec(
-            num_scalar_prefetch=1,
-            grid=(count,),
-            in_specs=[
-                wide,
-                wide,
-                pl.BlockSpec((rows, rank), lambda i, ids: (0, 0)),
-                pl.BlockSpec((1, rank), lambda i, ids: (0, 0)),
-            ]
-            + [pl.BlockSpec(part.shape, lambda i, ids: (0, 0)) for part in pieces]
-            + [pl.BlockSpec(memory_space=pl.ANY)] * carried,
-            out_specs=[wide, tall, wide],
-        ),
+        functools.partial(output_kernel, parts, factor),
+        in_specs=[pl.BlockSpec(memory_space=pltpu.SMEM)]
+        + [vmem] * (3 + len(pieces))
+        + [hbm] * len(previous),
+        out_specs=[hbm] * 3,
         out_shape=[
             jax.ShapeDtypeStruct((rows, cols), F32),
             jax.ShapeDtypeStruct((cols, rank), BF16),
             jax.ShapeDtypeStruct((rows, cols), BF16),
         ],
-        input_output_aliases=aliases,
-        compiler_params=params(24),
+        scratch_shapes=[
+            pltpu.VMEM((count, rows, share), F32),
+            pltpu.VMEM((count, share, rank), BF16),
+            pltpu.VMEM((count, rows, share), BF16),
+            pltpu.SemaphoreType.DMA((count, parts, 3)),
+        ],
+        input_output_aliases={4 + len(pieces) + n: n for n in range(len(previous))},
+        compiler_params=params(16),
         cost_estimate=cost(
-            4 * rows * share * rank * count, count * share * (rows * 12 + rank * 4)
+            4 * rows * share * rank * count, count * share * (rows * 10 + rank * 4)
         ),
         name="outputs",
-    )(ids, momentum, gradient, ortho, colsq, *pieces, *(previous or ()))
+    )(ids, base, ortho, colsq, *pieces, *previous)
 
 
 def chip_at(position, chips):
@@ -284,6 +323,14 @@
     return lax.optimization_barrier((x, *work))[0] if work else x
 
 
+def exchange_windows(count):
+    if count != 16:
+        far = [[k + count // 2] + [k] * (k > 0) for k in range(count // 2)]
+        steps = count // 4 + 1
+        return far[:steps] + [sum(far[steps:], [])]
+    return [[8, 4], [9, 5], [10, 6], [11, 7], [12, 1, 2, 3], [13, 14, 15]]
+
+
 def gather_and_exchange(sketch, outgoing, count):
     chips = count // 2
     me = lax.axis_index("fsdp")
@@ -296,37 +343,51 @@
             pairs = [(n, n ^ k) for n in range(count)]
             columns[k] = lax.ppermute(tie(outgoing[k], *after), "fsdp", pairs)
 
-    far = [[k + chips] + [k] * (k > 0) for k in range(chips)]
-    exchange(far[0], sketch)
+    windows = exchange_windows(count)
+    swap = swap_pairs(count)
+    exchange(windows[0], sketch)
     sketch = sketch + lax.ppermute(sketch, "tp", [(0, 1), (1, 0)])
-    offsets, held = [0], [sketch]
+    offsets, held, other = [0], [sketch], []
     ahead = behind = sketch
+    arrived, earlier = [sketch], []
     for step in range(1, chips // 2 + 1):
-        sent = [columns[k] for k in far[step - 2]] if step > 1 else []
-        ahead, behind = lax.optimization_barrier((ahead, behind, *sent))[:2]
-        exchange(far[step], ahead, behind)
+        work = [columns[k] for k in windows[step - 2]] if step > 1 else []
+        ahead, behind, *_ = lax.optimization_barrier((ahead, behind, *work, *earlier))
+        exchange(windows[step], ahead, behind)
+        earlier = [lax.ppermute(x, "fsdp", swap) for x in arrived]
+        other += earlier
         ahead = lax.ppermute(ahead, "fsdp", up)
-        held.append(ahead)
+        arrived = [ahead]
         offsets.append(-step)
         if 2 * step < chips:
             behind = lax.ppermute(behind, "fsdp", down)
-            held.append(behind)
+            arrived.append(behind)
             offsets.append(step)
-    for window in far[chips // 2 + 1 :]:
+        held += arrived
+    for window in windows[chips // 2 + 1 :]:
         exchange(window, ahead, behind)
-    other = [lax.ppermute(h, "fsdp", swap_pairs(count)) for h in held]
+    other += [lax.ppermute(x, "fsdp", swap) for x in arrived]
     chip = chip_at((place + jnp.array(offsets, jnp.int32)) % chips, chips)
     ids = jnp.concatenate([2 * chip + core, 2 * chip + 1 - core])
     return held + other, ids.astype(jnp.int32), [columns[k] for k in range(count)]
 
 
-def sum_rounds(count, tp_count):
-    rounds = [("tp", [(0, 1), (1, 0)])]
-    bit = 1
+def sum_rounds(count):
+    rounds, bit = [("tp", [1])], 1
     while bit < count:
-        rounds.append(("fsdp", [(n, n ^ bit) for n in range(count)]))
-        bit *= 2
+        rounds.append(("fsdp", [bit, 2 * bit, 3 * bit] if 2 * bit < count else [bit]))
+        bit *= 4
     return rounds
+
+
+def sum_round(x, axis, distances):
+    size = lax.axis_size(axis)
+    terms = [x]
+    for d in distances:
+        terms.append(lax.ppermute(x, axis, [(n, n ^ d) for n in range(size)]))
+    if len(terms) == 2:
+        return terms[0] + terms[1]
+    return (terms[0] + terms[1]) + (terms[2] + terms[3])
 
 
 def local(momentum, gradient, basis):
@@ -340,14 +401,16 @@
     me = lax.axis_index("fsdp")
     ring = tp_count == 2 and count in (4, 8, 16, 32) and (count - 1) * share < cols
 
-    base_b = (momentum + gradient.astype(F32)).astype(BF16)
+    base = momentum + gradient.astype(F32)
+    base_b = base.astype(BF16)
     sketch = jnp.dot(base_b, basis, preferred_element_type=F32)
-    padded = jnp.pad(base_b, ((0, 0), (0, share * count - cols)))
+    base = pltpu.with_memory_space_constraint(base, pltpu.VMEM)
     if ring:
         partners = me ^ jnp.arange(count, dtype=jnp.int32)
-        outgoing = pack_call(partners, padded, share)
+        outgoing = pack_call(partners, base, share)
         pieces, ids, columns = gather_and_exchange(sketch, outgoing, count)
     else:
+        padded = jnp.pad(base_b, ((0, 0), (0, share * count - cols)))
         outgoing = jnp.swapaxes(padded.reshape(rows, count, share), 0, 1)
         columns = lax.all_to_all(outgoing, "fsdp", 0, 0, tiled=True)
         columns = [columns.reshape(rows * count, share)]
@@ -356,7 +419,6 @@
         pieces = [lax.dynamic_index_in_dim(whole, (me + n) % count, 0, False) for n in range(count)]
         ids = ((me + jnp.arange(count)) % count).astype(jnp.int32)
     ortho_t, ortho_here = factor_call(ids, pieces)
-    momentum = pltpu.with_memory_space_constraint(momentum, pltpu.HBM)
     tiles = share // LANES
     cuts = [share]
     if ring and tiles > 1:
@@ -370,7 +432,7 @@
         valid = -(-cols // share)
         return tuple(
             outputs(
-                jnp.arange(valid, dtype=jnp.int32), momentum, gradient, ortho_here, colsq,
+                jnp.arange(valid, dtype=jnp.int32), base, cols, ortho_here, colsq,
                 [[whole[n]] for n in range(valid)], previous=None,
             )
         )
@@ -383,32 +445,33 @@
     mine = 2 * chip_at((place - way * steps) % chips, chips) + core
     theirs = 2 * chip_at((place + way * steps) % chips, chips) + 1 - core
     ids = jnp.stack([mine, theirs], axis=1).astype(jnp.int32)
-    rounds = sum_rounds(count, tp_count)
+    rounds = sum_rounds(count)
     colsq, result = part, None
     mine, theirs = [list(back)], []
     written, waiting = 0, ()
     for step in range(chips):
         mine.append([])
         theirs.append([])
+        if step == 1:
+            waiting += tuple(mine[1])
         for n in range(len(cuts)):
             block = mine[step][n]
             if step + 1 < chips:
                 mine[step + 1].append(lax.ppermute(tie(block, *waiting), "fsdp", turn))
             theirs[step].append(lax.ppermute(block, "fsdp", swap))
+            waiting = ()
             if rounds:
-                axis, pairs = rounds.pop(0)
-                colsq = colsq + lax.ppermute(tie(colsq, block), axis, pairs)
-                waiting = ()
+                colsq = sum_round(tie(colsq, block), *rounds.pop(0))
             elif written + 1 < step:
                 result = outputs(
-                    ids[written], momentum, gradient, ortho_here, colsq,
+                    ids[written], base, cols, ortho_here, colsq,
                     [mine[written], theirs[written]], previous=result,
                 )
                 written += 1
                 waiting = tuple(result)
     for n in range(written, chips):
         result = outputs(
-            ids[n], momentum, gradient, ortho_here, colsq, [mine[n], theirs[n]], previous=result
+            ids[n], base, cols, ortho_here, colsq, [mine[n], theirs[n]], previous=result
         )
     return tuple(result)
 

time: 172 us -> 161 us (0.936)
  starting transfers between devices: 89.5 us -> 77.9 us
  waiting for transfers between devices: 25.8 us -> 34.6 us
  Pallas kernels: 46.4 us -> 37.8 us
    ppermute x4, starting transfers between devices: 10 us -> 0.84 us  [gather_and_exchange(): ahead = lax.ppermute(ahead, 'fsdp', up)]
    pallas_call x8, Pallas kernels: 27.6 us -> 19.7 us  [output_call(): pl.pallas_call(functools.partial(output_kernel, parts, factor), in_specs=...]
    ppermute x4, waiting for transfers between devices: 0.01 us -> 4.44 us  [gather_and_exchange(): ahead = lax.ppermute(ahead, 'fsdp', up)]
    add x5 -> x4, other arithmetic: 0.02 us -> 3.97 us  [the longest x1 3.95 us: local(): base = momentum + gradient.astype(F32)]
    convert_element_type x1 -> x0, other arithmetic: 3.9 us -> none  [local(): base_b = (momentum + gradient.astype(F32)).astype(BF16)]
    ppermute x14, waiting for transfers between devices: 6.84 us -> 10 us  [local(): mine[step + 1].append(lax.ppermute(tie(block, *waiting), 'fsdp', turn))]
    ppermute x13 -> x15, waiting for transfers between devices: 5.97 us -> 2.87 us  [the longest x7 2.85 us: sum_round(): terms.append(lax.ppermute(x, axis, [(n, n ^ d) for n in range(size)]))]
    ppermute x15, waiting for transfers between devices: 11.6 us -> 14.7 us  [exchange(): columns[k] = lax.ppermute(tie(outgoing[k], *after), 'fsdp', pairs)]
  transfers between devices with their start and end apart: 66 -> 68, of which waited for: 12 -> 17; matrix products, arithmetic and copies ran while one was open for 0% -> 0% of each run, Pallas kernels for 24% -> 20%
where the time goes in v6:
time: 161 us
  starting transfers between devices  77.9 us (48%)
  Pallas kernels  37.8 us (23%)
  waiting for transfers between devices  34.6 us (21%)
  other arithmetic  4.11 us (3%)
  local copies, waits for them, and re-layouts  3.97 us (2%)
    ppermute x15, starting transfers between devices, exchange(): columns[k] = lax.ppermute(tie(outgoing[k], *after), 'fsdp', pairs)  29.7 us
    pallas_call x8, Pallas kernels, output_call(): pl.pallas_call(functools.partial(output_kernel, parts, factor), in_specs=...  19.7 us
    pallas_call x1, Pallas kernels, factor_call(): pl.pallas_call(functools.partial(factor_kernel, count), in_specs=[pl.Bloc...  15.2 us
    ppermute x15, waiting for transfers between devices, exchange(): columns[k] = lax.ppermute(tie(outgoing[k], *after), 'fsdp', pairs)  14.7 us
    ppermute x16, starting transfers between devices, local(): theirs[step].append(lax.ppermute(block, 'fsdp', swap))  14.6 us
    ppermute x14, starting transfers between devices, local(): mine[step + 1].append(lax.ppermute(tie(block, *waiting), 'fsdp', turn))  11 us
    ppermute x7, starting transfers between devices, sum_round(): terms.append(lax.ppermute(x, axis, [(n, n ^ d) for n in range(size)]))  10.7 us
    ppermute x14, waiting for transfers between devices, local(): mine[step + 1].append(lax.ppermute(tie(block, *waiting), 'fsdp', turn))  10 us
  transfers between devices with their start and end apart: 68, of which 17 were waited for; matrix products, arithmetic and copies ran while one was open for 0% of the time, Pallas kernels for 20%

profile of v6, /device:TPU:1, one launch (start us, length us, event | category | flops | bytes accessed | tf_op | source)
XLA Modules:
  0.0 160.9 jit_solution(1366246731368167475)
XLA Ops:
  0.7 4.0 %convert_add_fusion.base_ref = f32[96,13824]{1,0:T(8,128)S(1)} fusion(f32[96,13824]{1,0:T(8,128)} %param.4, bf16[96,13824]{1,0:T(8,128)(2,1)} %param.5), kind=kLoop, calls=%fused_computation | loop fusion | flops 2654208 | bytes 13271040 | tf_op jit(solution)/shard_map/add | solution.py:404
  13.8 2.6 %collective-permute-done = f32[96,256]{1,0:T(8,128)S(1)} collective-permute-done((f32[96,256]{1,0:T(8,128)S(1)}, f32[96,256]{1,0:T(8,128)S(1)}, u32[]{:S(2)}, u32[]{:S(2)}) %collective-permute-start) | collective-permute-done | bytes 98336 | tf_op jit(solution)/shard_map/ppermute | solution.py:349
  26.7 2.9 %collective-permute-done.9.refs_5_ = bf16[96,896]{1,0:T(8,128)(2,1)S(1)} collective-permute-done((bf16[96,896]{1,0:T(8,128)(2,1)S(1)}, bf16[96,896]{1,0:T(8,128)(2,1)S(1)}, u32[]{:S(2)}, u32[]{:S(2)}) %collective-permute-start.9) | collective-permute-done | bytes 172064 | tf_op jit(solution)/shard_map/ppermute | solution.py:344
  29.6 2.3 %collective-permute-done.8.refs_9_ = bf16[96,896]{1,0:T(8,128)(2,1)S(1)} collective-permute-done((bf16[96,896]{1,0:T(8,128)(2,1)S(1)}, bf16[96,896]{1,0:T(8,128)(2,1)S(1)}, u32[]{:S(2)}, u32[]{:S(2)}) %collective-permute-start.8) | collective-permute-done | bytes 172064 | tf_op jit(solution)/shard_map/ppermute | solution.py:344
  34.5 3.0 %collective-permute-start.14 = (bf16[96,896]{1,0:T(8,128)(2,1)S(1)}, bf16[96,896]{1,0:T(8,128)(2,1)S(1)}, u32[]{:S(2)}, u32[]{:S(2)}) collective-permute-start(bf16[96,896]{1,0:T(8,128)(2,1)S(1)} %get-tuple-element.92), channel_id=1, source_target_pairs={{0,20},{2,22},{4,16},{6,18},{8,28},{10,30},{12,24},{14,26},{16,4},... | collective-permute-start | bytes 516104 | tf_op jit(solution)/shard_map/ppermute | solution.py:344
  40.5 4.8 %collective-permute-done.14.refs_10_ = bf16[96,896]{1,0:T(8,128)(2,1)S(1)} collective-permute-done((bf16[96,896]{1,0:T(8,128)(2,1)S(1)}, bf16[96,896]{1,0:T(8,128)(2,1)S(1)}, u32[]{:S(2)}, u32[]{:S(2)}) %collective-permute-start.14) | collective-permute-done | bytes 172064 | tf_op jit(solution)/shard_map/ppermute | solution.py:344
  47.1 3.6 %collective-permute-start.25 = (bf16[96,896]{1,0:T(8,128)(2,1)S(1)}, bf16[96,896]{1,0:T(8,128)(2,1)S(1)}, u32[]{:S(2)}, u32[]{:S(2)}) collective-permute-start(bf16[96,896]{1,0:T(8,128)(2,1)S(1)} %get-tuple-element.107), channel_id=1, source_target_pairs={{0,14},{2,12},{4,10},{6,8},{8,6},{10,4},{12,2},{14,0},{16,30},{18,... | collective-permute-start | bytes 516104 | tf_op jit(solution)/shard_map/ppermute | solution.py:344
  51.0 2.5 %collective-permute-start.27 = (bf16[96,896]{1,0:T(8,128)(2,1)S(1)}, bf16[96,896]{1,0:T(8,128)(2,1)S(1)}, u32[]{:S(2)}, u32[]{:S(2)}) collective-permute-start(bf16[96,896]{1,0:T(8,128)(2,1)S(1)} %get-tuple-element.111), channel_id=1, source_target_pairs={{0,24},{2,26},{4,28},{6,30},{8,16},{10,18},{12,20},{14,22},{16,8},... | collective-permute-start | bytes 516104 | tf_op jit(solution)/shard_map/ppermute | solution.py:344
  54.3 3.4 %collective-permute-done.26.refs_11_ = bf16[96,896]{1,0:T(8,128)(2,1)S(1)} collective-permute-done((bf16[96,896]{1,0:T(8,128)(2,1)S(1)}, bf16[96,896]{1,0:T(8,128)(2,1)S(1)}, u32[]{:S(2)}, u32[]{:S(2)}) %collective-permute-start.26) | collective-permute-done | bytes 172064 | tf_op jit(solution)/shard_map/ppermute | solution.py:344
  62.0 3.9 %collective-permute-start.23 = (bf16[96,896]{1,0:T(8,128)(2,1)S(1)}, bf16[96,896]{1,0:T(8,128)(2,1)S(1)}, u32[]{:S(2)}, u32[]{:S(2)}) collective-permute-start(bf16[96,896]{1,0:T(8,128)(2,1)S(1)} %get-tuple-element.103), channel_id=1, source_target_pairs={{0,4},{2,6},{4,0},{6,2},{8,12},{10,14},{12,8},{14,10},{16,20},{18,... | collective-permute-start | bytes 516104 | tf_op jit(solution)/shard_map/ppermute | solution.py:344
  71.6 15.2 %factor.1 = (bf16[256,1536]{1,0:T(8,128)(2,1)S(1)}, bf16[96,256]{1,0:T(8,128)(2,1)S(1)}) custom-call(s32[16]{0:T(128)S(1)} %pad_add_fusion.1.ids_ref, f32[96,256]{1,0:T(8,128)S(1)} %add.153.refs_0_, f32[96,256]{1,0:T(8,128)S(1)} %collective-permute-done.1.refs_1_, f32[96,256]{1,0:T(8,128)} %collective-permute-done.2.refs_2_, ...), custom_call_target="tpu_custom_call" | custom-call | flops 4026531840 | bytes 2359296 | tf_op jit(solution)/shard_map/factor/pallas_call | solution.py:161
  90.4 3.1 %collective-permute-start.39 = (bf16[384,256]{1,0:T(8,128)(2,1)S(1)}, bf16[384,256]{1,0:T(8,128)(2,1)S(1)}, u32[]{:S(2)}, u32[]{:S(2)}) collective-permute-start(bf16[384,256]{1,0:T(8,128)(2,1)S(1)} %get-tuple-element.121.refs_1_), channel_id=1, source_target_pairs={{0,8},{8,16},{16,24},{24,28},{28,20},{20,12},{12,4},{4,0},{2,6},{1... | collective-permute-start | bytes 589832 | tf_op jit(solution)/shard_map/ppermute | solution.py:460
  93.5 6.6 %collective-permute-done.39.refs_1_ = bf16[384,256]{1,0:T(8,128)(2,1)S(1)} collective-permute-done((bf16[384,256]{1,0:T(8,128)(2,1)S(1)}, bf16[384,256]{1,0:T(8,128)(2,1)S(1)}, u32[]{:S(2)}, u32[]{:S(2)}) %collective-permute-start.39) | collective-permute-done | bytes 196640 | tf_op jit(solution)/shard_map/ppermute | solution.py:460
  102.6 4.3 %collective-permute-start.32 = (f32[1,256]{1,0:T(1,128)S(1)}, f32[1,256]{1,0:T(1,128)S(1)}, u32[]{:S(2)}, u32[]{:S(2)}) collective-permute-start(f32[1,256]{1,0:T(1,128)S(1)} %add.154), channel_id=1, source_target_pairs={{0,2},{2,0},{4,6},{6,4},{8,10},{10,8},{12,14},{14,12},{16,18},{18,... | collective-permute-start | bytes 3080 | tf_op jit(solution)/shard_map/ppermute | solution.py:387
  118.3 2.5 %copy-done.1 = f32[96,13824]{1,0:T(8,128)S(1)} copy-done((f32[96,13824]{1,0:T(8,128)S(1)}, f32[96,13824]{1,0:T(8,128)}, u32[]{:S(2)}) %copy-start.1) | copy-done | bytes 5308440
  120.8 2.7 %outputs.8 = (f32[96,13824]{1,0:T(8,128)}, bf16[13824,256]{1,0:T(8,128)(2,1)}, bf16[96,13824]{1,0:T(8,128)(2,1)}) custom-call(s32[2]{0:T(128)S(1)} %get-tuple-element.157.ids_ref, f32[96,13824]{1,0:T(8,128)S(1)} %copy-done.1, bf16[96,256]{1,0:T(8,128)(2,1)S(1)} %get-tuple-element.96.ortho_ref, f32[1,256]{1,0:T(1,128)S(1)} %add_add_fusion.colsq_ref, ...), custom_call_target="tpu_custom_call" | custom-call | flops 176160768 | bytes 3555328 | tf_op jit(solution)/shard_map/outputs/pallas_call | solution.py:267
  126.8 2.5 %outputs.9 = (f32[96,13824]{1,0:T(8,128)}, bf16[13824,256]{1,0:T(8,128)(2,1)}, bf16[96,13824]{1,0:T(8,128)(2,1)}) custom-call(s32[2]{0:T(128)S(1)} %get-tuple-element.156.ids_ref, f32[96,13824]{1,0:T(8,128)S(1)} %copy-done.1, bf16[96,256]{1,0:T(8,128)(2,1)S(1)} %get-tuple-element.96.ortho_ref, ...), custom_call_target="tpu_custom_call", output_to_operand_aliasing={{0}: (8, {}), {1}: (9, {}), {2}: (10, {})} | custom-call | flops 176160768 | bytes 3555328 | tf_op jit(solution)/shard_map/outputs/pallas_call | solution.py:267
  131.1 2.5 %outputs.10 = (f32[96,13824]{1,0:T(8,128)}, bf16[13824,256]{1,0:T(8,128)(2,1)}, bf16[96,13824]{1,0:T(8,128)(2,1)}) custom-call(s32[2]{0:T(128)S(1)} %get-tuple-element.155.ids_ref, f32[96,13824]{1,0:T(8,128)S(1)} %copy-done.1, bf16[96,256]{1,0:T(8,128)(2,1)S(1)} %get-tuple-element.96.ortho_ref, ...), custom_call_target="tpu_custom_call", output_to_operand_aliasing={{0}: (8, {}), {1}: (9, {}), {2}: (10, {})} | custom-call | flops 176160768 | bytes 3555328 | tf_op jit(solution)/shard_map/outputs/pallas_call | solution.py:267
  135.0 3.1 %collective-permute-start.59 = (bf16[512,256]{1,0:T(8,128)(2,1)S(1)}, bf16[512,256]{1,0:T(8,128)(2,1)S(1)}, u32[]{:S(2)}, u32[]{:S(2)}) collective-permute-start(bf16[512,256]{1,0:T(8,128)(2,1)S(1)} %collective-permute-done.42.refs_0_), channel_id=1, source_target_pairs={{0,2},{2,0},{4,6},{6,4},{8,10},{10,8},{12,14},{14,12},{16,18},{18,... | collective-permute-start | bytes 786440 | tf_op jit(solution)/shard_map/ppermute | solution.py:461
  138.2 2.5 %outputs.11 = (f32[96,13824]{1,0:T(8,128)}, bf16[13824,256]{1,0:T(8,128)(2,1)}, bf16[96,13824]{1,0:T(8,128)(2,1)}) custom-call(s32[2]{0:T(128)S(1)} %get-tuple-element.154.ids_ref, f32[96,13824]{1,0:T(8,128)S(1)} %copy-done.1, bf16[96,256]{1,0:T(8,128)(2,1)S(1)} %get-tuple-element.96.ortho_ref, ...), custom_call_target="tpu_custom_call", output_to_operand_aliasing={{0}: (8, {}), {1}: (9, {}), {2}: (10, {})} | custom-call | flops 176160768 | bytes 3555328 | tf_op jit(solution)/shard_map/outputs/pallas_call | solution.py:267
  142.3 3.0 %collective-permute-start.67 = (bf16[384,256]{1,0:T(8,128)(2,1)S(1)}, bf16[384,256]{1,0:T(8,128)(2,1)S(1)}, u32[]{:S(2)}, u32[]{:S(2)}) collective-permute-start(bf16[384,256]{1,0:T(8,128)(2,1)S(1)} %collective-permute-done.55.refs_1_), channel_id=1, source_target_pairs={{0,2},{2,0},{4,6},{6,4},{8,10},{10,8},{12,14},{14,12},{16,18},{18,... | collective-permute-start | bytes 589832 | tf_op jit(solution)/shard_map/ppermute | solution.py:461
  153.2 2.5 %outputs.13 = (f32[96,13824]{1,0:T(8,128)}, bf16[13824,256]{1,0:T(8,128)(2,1)}, bf16[96,13824]{1,0:T(8,128)(2,1)}) custom-call(s32[2]{0:T(128)S(1)} %get-tuple-element.151.ids_ref, f32[96,13824]{1,0:T(8,128)S(1)} %copy-done.1, bf16[96,256]{1,0:T(8,128)(2,1)S(1)} %get-tuple-element.96.ortho_ref, ...), custom_call_target="tpu_custom_call", output_to_operand_aliasing={{0}: (8, {}), {1}: (9, {}), {2}: (10, {})} | custom-call | flops 176160768 | bytes 3555328 | tf_op jit(solution)/shard_map/outputs/pallas_call | solution.py:267
  155.7 2.5 %outputs.14 = (f32[96,13824]{1,0:T(8,128)}, bf16[13824,256]{1,0:T(8,128)(2,1)}, bf16[96,13824]{1,0:T(8,128)(2,1)}) custom-call(s32[2]{0:T(128)S(1)} %get-tuple-element.152.ids_ref, f32[96,13824]{1,0:T(8,128)S(1)} %copy-done.1, bf16[96,256]{1,0:T(8,128)(2,1)S(1)} %get-tuple-element.96.ortho_ref, ...), custom_call_target="tpu_custom_call", output_to_operand_aliasing={{0}: (8, {}), {1}: (9, {}), {2}: (10, {})} | custom-call | flops 176160768 | bytes 3555328 | tf_op jit(solution)/shard_map/outputs/pallas_call | solution.py:267
  158.2 2.5 %outputs.15 = (f32[96,13824]{1,0:T(8,128)}, bf16[13824,256]{1,0:T(8,128)(2,1)}, bf16[96,13824]{1,0:T(8,128)(2,1)}) custom-call(s32[2]{0:T(128)S(1)} %get-tuple-element.158.ids_ref, f32[96,13824]{1,0:T(8,128)S(1)} %copy-done.1, bf16[96,256]{1,0:T(8,128)(2,1)S(1)} %get-tuple-element.96.ortho_ref, ...), custom_call_target="tpu_custom_call", output_to_operand_aliasing={{0}: (8, {}), {1}: (9, {}), {2}: (10, {})} | custom-call | flops 176160768 | bytes 3555328 | tf_op jit(solution)/shard_map/outputs/pallas_call | solution.py:267
  (144 shorter events, 71.2 us)
Async XLA Ops:
  8.1 11.9 %collective-permute-start.4 = (bf16[96,896]{1,0:T(8,128)(2,1)S(1)}, bf16[96,896]{1,0:T(8,128)(2,1)S(1)}, u32[]{:S(2)}, u32[]{:S(2)}) collective-permute-start(bf16[96,896]{1,0:T(8,128)(2,1)S(1)} %get-tuple-element.82), channel_id=1, source_target_pairs={{0,8},{2,10},{4,12},{6,14},{8,0},{10,2},{12,4},{14,6},{16,24},{18,... | collective-permute-start | bytes 516104 | tf_op jit(solution)/shard_map/ppermute | solution.py:344
  10.3 10.4 %collective-permute-start.3 = (bf16[96,896]{1,0:T(8,128)(2,1)S(1)}, bf16[96,896]{1,0:T(8,128)(2,1)S(1)}, u32[]{:S(2)}, u32[]{:S(2)}) collective-permute-start(bf16[96,896]{1,0:T(8,128)(2,1)S(1)} %get-tuple-element.80), channel_id=1, source_target_pairs={{0,16},{2,18},{4,20},{6,22},{8,24},{10,26},{12,28},{14,30},{16,0},... | collective-permute-start | bytes 516104 | tf_op jit(solution)/shard_map/ppermute | solution.py:344
  20.7 11.3 %collective-permute-start.8 = (bf16[96,896]{1,0:T(8,128)(2,1)S(1)}, bf16[96,896]{1,0:T(8,128)(2,1)S(1)}, u32[]{:S(2)}, u32[]{:S(2)}) collective-permute-start(bf16[96,896]{1,0:T(8,128)(2,1)S(1)} %get-tuple-element.86), channel_id=1, source_target_pairs={{0,18},{2,16},{4,22},{6,20},{8,26},{10,24},{12,30},{14,28},{16,2},... | collective-permute-start | bytes 516104 | tf_op jit(solution)/shard_map/ppermute | solution.py:344
  23.0 17.5 %collective-permute-start.15 = (bf16[96,896]{1,0:T(8,128)(2,1)S(1)}, bf16[96,896]{1,0:T(8,128)(2,1)S(1)}, u32[]{:S(2)}, u32[]{:S(2)}) collective-permute-start(bf16[96,896]{1,0:T(8,128)(2,1)S(1)} %get-tuple-element.94), channel_id=1, source_target_pairs={{0,12},{2,14},{4,8},{6,10},{8,4},{10,6},{12,0},{14,2},{16,28},{18,... | collective-permute-start | bytes 516104 | tf_op jit(solution)/shard_map/ppermute | solution.py:344
  25.6 11.9 %collective-permute-start.7 = (f32[96,256]{1,0:T(8,128)}, f32[96,256]{1,0:T(8,128)}, u32[]{:S(2)}, u32[]{:S(2)}) collective-permute-start(f32[96,256]{1,0:T(8,128)} %collective-permute-done.2.refs_2_), channel_id=1, source_target_pairs={{0,4},{2,6},{8,0},{10,2},{16,8},{18,10},{24,16},{26,18},{28,24},{3... | collective-permute-start | bytes 294920 | tf_op jit(solution)/shard_map/ppermute | solution.py:363
  34.5 10.8 %collective-permute-start.14 = (bf16[96,896]{1,0:T(8,128)(2,1)S(1)}, bf16[96,896]{1,0:T(8,128)(2,1)S(1)}, u32[]{:S(2)}, u32[]{:S(2)}) collective-permute-start(bf16[96,896]{1,0:T(8,128)(2,1)S(1)} %get-tuple-element.92), channel_id=1, source_target_pairs={{0,20},{2,22},{4,16},{6,18},{8,28},{10,30},{12,24},{14,26},{16,4},... | collective-permute-start | bytes 516104 | tf_op jit(solution)/shard_map/ppermute | solution.py:344
  37.6 13.1 %collective-permute-start.13 = (f32[96,256]{1,0:T(8,128)}, f32[96,256]{1,0:T(8,128)S(1)}, u32[]{:S(2)}, u32[]{:S(2)}) collective-permute-start(f32[96,256]{1,0:T(8,128)} %collective-permute-done.7.refs_4_), channel_id=1, source_target_pairs={{0,4},{2,6},{8,0},{10,2},{16,8},{18,10},{24,16},{26,18},{28,24},{3... | collective-permute-start | bytes 294920 | tf_op jit(solution)/shard_map/ppermute | solution.py:363
  39.1 11.6 %collective-permute-start.16 = (f32[96,256]{1,0:T(8,128)S(1)}, f32[96,256]{1,0:T(8,128)S(1)}, u32[]{:S(2)}, u32[]{:S(2)}) collective-permute-start(f32[96,256]{1,0:T(8,128)S(1)} %collective-permute-done.6.refs_3_), channel_id=1, source_target_pairs={{0,2},{2,0},{4,6},{6,4},{8,10},{10,8},{12,14},{14,12},{16,18},{18,... | collective-permute-start | bytes 294920 | tf_op jit(solution)/shard_map/ppermute | solution.py:357
  40.5 10.2 %collective-permute-start.17 = (f32[96,256]{1,0:T(8,128)}, f32[96,256]{1,0:T(8,128)S(1)}, u32[]{:S(2)}, u32[]{:S(2)}) collective-permute-start(f32[96,256]{1,0:T(8,128)} %collective-permute-done.7.refs_4_), channel_id=1, source_target_pairs={{0,2},{2,0},{4,6},{6,4},{8,10},{10,8},{12,14},{14,12},{16,18},{18,... | collective-permute-start | bytes 294920 | tf_op jit(solution)/shard_map/ppermute | solution.py:357
  45.3 12.4 %collective-permute-start.26 = (bf16[96,896]{1,0:T(8,128)(2,1)S(1)}, bf16[96,896]{1,0:T(8,128)(2,1)S(1)}, u32[]{:S(2)}, u32[]{:S(2)}) collective-permute-start(bf16[96,896]{1,0:T(8,128)(2,1)S(1)} %get-tuple-element.109), channel_id=1, source_target_pairs={{0,22},{2,20},{4,18},{6,16},{8,30},{10,28},{12,26},{14,24},{16,6},... | collective-permute-start | bytes 516104 | tf_op jit(solution)/shard_map/ppermute | solution.py:344
  47.1 12.5 %collective-permute-start.25 = (bf16[96,896]{1,0:T(8,128)(2,1)S(1)}, bf16[96,896]{1,0:T(8,128)(2,1)S(1)}, u32[]{:S(2)}, u32[]{:S(2)}) collective-permute-start(bf16[96,896]{1,0:T(8,128)(2,1)S(1)} %get-tuple-element.107), channel_id=1, source_target_pairs={{0,14},{2,12},{4,10},{6,8},{8,6},{10,4},{12,2},{14,0},{16,30},{18,... | collective-permute-start | bytes 516104 | tf_op jit(solution)/shard_map/ppermute | solution.py:344
  50.7 10.7 %collective-permute-start.18 = (f32[96,256]{1,0:T(8,128)S(1)}, f32[96,256]{1,0:T(8,128)S(1)}, u32[]{:S(2)}, u32[]{:S(2)}) collective-permute-start(f32[96,256]{1,0:T(8,128)S(1)} %collective-permute-done.12.refs_5_), channel_id=1, source_target_pairs={{0,8},{2,10},{8,16},{10,18},{16,24},{18,26},{24,28},{26,30},{28,20... | collective-permute-start | bytes 294920 | tf_op jit(solution)/shard_map/ppermute | solution.py:359
  51.0 15.3 %collective-permute-start.27 = (bf16[96,896]{1,0:T(8,128)(2,1)S(1)}, bf16[96,896]{1,0:T(8,128)(2,1)S(1)}, u32[]{:S(2)}, u32[]{:S(2)}) collective-permute-start(bf16[96,896]{1,0:T(8,128)(2,1)S(1)} %get-tuple-element.111), channel_id=1, source_target_pairs={{0,24},{2,26},{4,28},{6,30},{8,16},{10,18},{12,20},{14,22},{16,8},... | collective-permute-start | bytes 516104 | tf_op jit(solution)/shard_map/ppermute | solution.py:344
  53.5 14.8 %collective-permute-start.24 = (bf16[96,896]{1,0:T(8,128)(2,1)S(1)}, bf16[96,896]{1,0:T(8,128)(2,1)S(1)}, u32[]{:S(2)}, u32[]{:S(2)}) collective-permute-start(bf16[96,896]{1,0:T(8,128)(2,1)S(1)} %get-tuple-element.105), channel_id=1, source_target_pairs={{0,6},{2,4},{4,2},{6,0},{8,14},{10,12},{12,10},{14,8},{16,22},{18,... | collective-permute-start | bytes 516104 | tf_op jit(solution)/shard_map/ppermute | solution.py:344
  62.0 24.7 %collective-permute-start.23 = (bf16[96,896]{1,0:T(8,128)(2,1)S(1)}, bf16[96,896]{1,0:T(8,128)(2,1)S(1)}, u32[]{:S(2)}, u32[]{:S(2)}) collective-permute-start(bf16[96,896]{1,0:T(8,128)(2,1)S(1)} %get-tuple-element.103), channel_id=1, source_target_pairs={{0,4},{2,6},{4,0},{6,2},{8,12},{10,14},{12,8},{14,10},{16,20},{18,... | collective-permute-start | bytes 516104 | tf_op jit(solution)/shard_map/ppermute | solution.py:344
  66.0 20.8 %collective-permute-start.22 = (bf16[96,896]{1,0:T(8,128)(2,1)S(1)}, bf16[96,896]{1,0:T(8,128)(2,1)S(1)}, u32[]{:S(2)}, u32[]{:S(2)}) collective-permute-start(bf16[96,896]{1,0:T(8,128)(2,1)S(1)} %get-tuple-element.101), channel_id=1, source_target_pairs={{0,2},{2,0},{4,6},{6,4},{8,10},{10,8},{12,14},{14,12},{16,18},{18,... | collective-permute-start | bytes 516104 | tf_op jit(solution)/shard_map/ppermute | solution.py:344
  66.3 20.5 %collective-permute-start.30 = (bf16[96,896]{1,0:T(8,128)(2,1)S(1)}, bf16[96,896]{1,0:T(8,128)(2,1)S(1)}, u32[]{:S(2)}, u32[]{:S(2)}) collective-permute-start(bf16[96,896]{1,0:T(8,128)(2,1)S(1)} %get-tuple-element.117), channel_id=1, source_target_pairs={{0,30},{2,28},{4,26},{6,24},{8,22},{10,20},{12,18},{14,16},{16,14}... | collective-permute-start | bytes 516104 | tf_op jit(solution)/shard_map/ppermute | solution.py:344
  68.3 18.5 %collective-permute-start.29 = (bf16[96,896]{1,0:T(8,128)(2,1)S(1)}, bf16[96,896]{1,0:T(8,128)(2,1)S(1)}, u32[]{:S(2)}, u32[]{:S(2)}) collective-permute-start(bf16[96,896]{1,0:T(8,128)(2,1)S(1)} %get-tuple-element.115), channel_id=1, source_target_pairs={{0,28},{2,30},{4,24},{6,26},{8,20},{10,22},{12,16},{14,18},{16,12}... | collective-permute-start | bytes 516104 | tf_op jit(solution)/shard_map/ppermute | solution.py:344
  70.5 16.3 %collective-permute-start.28 = (bf16[96,896]{1,0:T(8,128)(2,1)S(1)}, bf16[96,896]{1,0:T(8,128)(2,1)S(1)}, u32[]{:S(2)}, u32[]{:S(2)}) collective-permute-start(bf16[96,896]{1,0:T(8,128)(2,1)S(1)} %get-tuple-element.113), channel_id=1, source_target_pairs={{0,26},{2,24},{4,30},{6,28},{8,18},{10,16},{12,22},{14,20},{16,10}... | collective-permute-start | bytes 516104 | tf_op jit(solution)/shard_map/ppermute | solution.py:344
  88.7 11.4 %collective-permute-start.35 = (bf16[512,256]{1,0:T(8,128)(2,1)S(1)}, bf16[512,256]{1,0:T(8,128)(2,1)S(1)}, u32[]{:S(2)}, u32[]{:S(2)}) collective-permute-start(bf16[512,256]{1,0:T(8,128)(2,1)S(1)} %get-tuple-element.119.refs_0_), channel_id=1, source_target_pairs={{0,8},{8,16},{16,24},{24,28},{28,20},{20,12},{12,4},{4,0},{2,6},{1... | collective-permute-start | bytes 786440 | tf_op jit(solution)/shard_map/ppermute | solution.py:460
  90.4 9.8 %collective-permute-start.39 = (bf16[384,256]{1,0:T(8,128)(2,1)S(1)}, bf16[384,256]{1,0:T(8,128)(2,1)S(1)}, u32[]{:S(2)}, u32[]{:S(2)}) collective-permute-start(bf16[384,256]{1,0:T(8,128)(2,1)S(1)} %get-tuple-element.121.refs_1_), channel_id=1, source_target_pairs={{0,8},{8,16},{16,24},{24,28},{28,20},{20,12},{12,4},{4,0},{2,6},{1... | collective-permute-start | bytes 589832 | tf_op jit(solution)/shard_map/ppermute | solution.py:460
  108.6 9.7 %collective-permute-start.47 = (bf16[512,256]{1,0:T(8,128)(2,1)S(1)}, bf16[512,256]{1,0:T(8,128)(2,1)S(1)}, u32[]{:S(2)}, u32[]{:S(2)}) collective-permute-start(bf16[512,256]{1,0:T(8,128)(2,1)S(1)} %get-tuple-element.119.refs_0_), channel_id=1, source_target_pairs={{0,2},{2,0},{4,6},{6,4},{8,10},{10,8},{12,14},{14,12},{16,18},{18,... | collective-permute-start | bytes 786440 | tf_op jit(solution)/shard_map/ppermute | solution.py:461
  116.4 10.4 %collective-permute-start.50 = (bf16[512,256]{1,0:T(8,128)(2,1)S(1)}, bf16[512,256]{1,0:T(8,128)(2,1)S(1)}, u32[]{:S(2)}, u32[]{:S(2)}) collective-permute-start(bf16[512,256]{1,0:T(8,128)(2,1)S(1)} %collective-permute-done.35.refs_0_), channel_id=1, source_target_pairs={{0,2},{2,0},{4,6},{6,4},{8,10},{10,8},{12,14},{14,12},{16,18},{18,... | collective-permute-start | bytes 786440 | tf_op jit(solution)/shard_map/ppermute | solution.py:461
  135.0 10.2 %collective-permute-start.59 = (bf16[512,256]{1,0:T(8,128)(2,1)S(1)}, bf16[512,256]{1,0:T(8,128)(2,1)S(1)}, u32[]{:S(2)}, u32[]{:S(2)}) collective-permute-start(bf16[512,256]{1,0:T(8,128)(2,1)S(1)} %collective-permute-done.42.refs_0_), channel_id=1, source_target_pairs={{0,2},{2,0},{4,6},{6,4},{8,10},{10,8},{12,14},{14,12},{16,18},{18,... | collective-permute-start | bytes 786440 | tf_op jit(solution)/shard_map/ppermute | solution.py:461
  (48 other events, 326.4 us)

commit v7 on v6

--- a/solution.py
+++ b/solution.py
@@ -173,7 +173,7 @@
     )(ids, *pieces)
 
 
-def back_kernel(pieces, ids_ref, ortho_t_ref, *refs):
+def back_kernel(pieces, ids_ref, base_ref, ortho_t_ref, *refs):
     columns, (colsq_ref, *part_refs), whole_ref = refs[:pieces], refs[pieces:-1], refs[-1]
     rows = columns[0].shape[0]
     for n, piece in enumerate(columns):
@@ -189,13 +189,13 @@
     colsq_ref[...] = jnp.sum(wide * wide, axis=0, keepdims=True)
 
 
-def back_call(ids, ortho_t, columns, parts):
+def back_call(ids, base, ortho_t, columns, parts):
     rank, total = ortho_t.shape
     share = columns[0].shape[1]
     vmem = pl.BlockSpec(memory_space=pltpu.VMEM)
     return pl.pallas_call(
         functools.partial(back_kernel, len(columns)),
-        in_specs=[pl.BlockSpec(memory_space=pltpu.SMEM), vmem] + [vmem] * len(columns),
+        in_specs=[pl.BlockSpec(memory_space=pltpu.SMEM)] + [vmem] * (2 + len(columns)),
         out_specs=[vmem] * (1 + len(parts)),
         out_shape=[jax.ShapeDtypeStruct((1, rank), F32)]
         + [jax.ShapeDtypeStruct((part, rank), BF16) for part in parts],
@@ -203,7 +203,7 @@
         compiler_params=params(24),
         cost_estimate=cost(2 * rank * total * share, total * share * 2),
         name="back",
-    )(ids, ortho_t, *columns)
+    )(ids, base, ortho_t, *columns)
 
 
 def output_kernel(parts, factor, ids_ref, base_ref, ortho_ref, colsq_ref, *refs):
@@ -423,7 +423,7 @@
     cuts = [share]
     if ring and tiles > 1:
         cuts = [share - tiles // 2 * LANES, tiles // 2 * LANES]
-    part, *back = back_call(partners, ortho_t, columns, cuts)
+    part, *back = back_call(partners, base, ortho_t, columns, cuts)
 
     outputs = functools.partial(output_call, factor=factor)
     if not ring:
@@ -445,34 +445,39 @@
     mine = 2 * chip_at((place - way * steps) % chips, chips) + core
     theirs = 2 * chip_at((place + way * steps) % chips, chips) + 1 - core
     ids = jnp.stack([mine, theirs], axis=1).astype(jnp.int32)
+    colsq, result = part, None
     rounds = sum_rounds(count)
-    colsq, result = part, None
+
+    def write(ids, blocks):
+        return outputs(ids, base, cols, ortho_here, colsq, blocks, previous=result)
+
     mine, theirs = [list(back)], []
     written, waiting = 0, ()
     for step in range(chips):
         mine.append([])
         theirs.append([])
         if step == 1:
-            waiting += tuple(mine[1])
+            waiting += (*mine[1], colsq)
+        elif step == 2:
+            waiting += (colsq,)
         for n in range(len(cuts)):
-            block = mine[step][n]
+            block = tie(mine[step][n], *waiting)
+            waiting = ()
             if step + 1 < chips:
-                mine[step + 1].append(lax.ppermute(tie(block, *waiting), "fsdp", turn))
+                mine[step + 1].append(lax.ppermute(block, "fsdp", turn))
             theirs[step].append(lax.ppermute(block, "fsdp", swap))
-            waiting = ()
-            if rounds:
-                colsq = sum_round(tie(colsq, block), *rounds.pop(0))
-            elif written + 1 < step:
-                result = outputs(
-                    ids[written], base, cols, ortho_here, colsq,
-                    [mine[written], theirs[written]], previous=result,
-                )
+            for _ in range(2 if step == 0 else 1):
+                if rounds and n == 0:
+                    colsq = sum_round(tie(colsq, block), *rounds.pop(0))
+            ready = step if step + 1 == chips else step + n - 1
+            if step > 1 and written < ready:
+                result = write(ids[written], [mine[written], theirs[written]])
                 written += 1
                 waiting = tuple(result)
-    for n in range(written, chips):
-        result = outputs(
-            ids[n], base, cols, ortho_here, colsq, [mine[n], theirs[n]], previous=result
-        )
+    for n in range(written, chips - 1):
+        result = write(ids[n], [mine[n], theirs[n]])
+    result = write(ids[-1, :1], [mine[chips - 1]])
+    result = write(ids[-1, 1:], [theirs[chips - 1]])
     return tuple(result)
 
 

time: 161 us -> 164 us (1.019)
    pallas_call x8 -> x9, Pallas kernels: 19.7 us -> 21.1 us  [output_call(): pl.pallas_call(functools.partial(output_kernel, parts, factor), in_specs=...]
    unnamed x8 -> x12, local copies, waits for them, and re-layouts: 3.68 us -> 3.69 us
  transfers between devices with their start and end apart: 68 -> 68, of which waited for: 17 -> 17; matrix products, arithmetic and copies ran while one was open for 0% -> 1% of each run, Pallas kernels for 20% -> 21%
where the time goes in v7:
time: 164 us
  starting transfers between devices  78.5 us (48%)
  Pallas kernels  39.2 us (24%)
  waiting for transfers between devices  34.4 us (21%)
  local copies, waits for them, and re-layouts  5.23 us (3%)
  other arithmetic  4.14 us (3%)
    ppermute x15, starting transfers between devices, exchange(): columns[k] = lax.ppermute(tie(outgoing[k], *after), 'fsdp', pairs)  29.7 us
    pallas_call x9, Pallas kernels, output_call(): pl.pallas_call(functools.partial(output_kernel, parts, factor), in_specs=...  21.1 us
    pallas_call x1, Pallas kernels, factor_call(): pl.pallas_call(functools.partial(factor_kernel, count), in_specs=[pl.Bloc...  15.2 us
    ppermute x16, starting transfers between devices, local(): theirs[step].append(lax.ppermute(block, 'fsdp', swap))  14.8 us
    ppermute x15, waiting for transfers between devices, exchange(): columns[k] = lax.ppermute(tie(outgoing[k], *after), 'fsdp', pairs)  14.7 us
    ppermute x7, starting transfers between devices, sum_round(): terms.append(lax.ppermute(x, axis, [(n, n ^ d) for n in range(size)]))  11.7 us
    ppermute x14, starting transfers between devices, local(): mine[step + 1].append(lax.ppermute(block, 'fsdp', turn))  10.3 us
    ppermute x14, waiting for transfers between devices, local(): mine[step + 1].append(lax.ppermute(block, 'fsdp', turn))  9.57 us
  transfers between devices with their start and end apart: 68, of which 17 were waited for; matrix products, arithmetic and copies ran while one was open for 1% of the time, Pallas kernels for 21%

profile of v7, /device:TPU:1, one launch (start us, length us, event | category | flops | bytes accessed | tf_op | source)
XLA Modules:
  0.0 163.8 jit_solution(18105737467571954035)
XLA Ops:
  0.7 4.0 %convert_add_fusion.base_ref = f32[96,13824]{1,0:T(8,128)S(1)} fusion(f32[96,13824]{1,0:T(8,128)} %param.4, bf16[96,13824]{1,0:T(8,128)(2,1)} %param.5), kind=kLoop, calls=%fused_computation | loop fusion | flops 2654208 | bytes 13271040 | tf_op jit(solution)/shard_map/add | solution.py:404
  10.3 2.3 %collective-permute-start.3 = (bf16[96,896]{1,0:T(8,128)(2,1)S(1)}, bf16[96,896]{1,0:T(8,128)(2,1)S(1)}, u32[]{:S(2)}, u32[]{:S(2)}) collective-permute-start(bf16[96,896]{1,0:T(8,128)(2,1)S(1)} %get-tuple-element.86), channel_id=1, source_target_pairs={{0,16},{2,18},{4,20},{6,22},{8,24},{10,26},{12,28},{14,30},{16,0},... | collective-permute-start | bytes 516104 | tf_op jit(solution)/shard_map/ppermute | solution.py:344
  13.8 2.6 %collective-permute-done = f32[96,256]{1,0:T(8,128)S(1)} collective-permute-done((f32[96,256]{1,0:T(8,128)S(1)}, f32[96,256]{1,0:T(8,128)S(1)}, u32[]{:S(2)}, u32[]{:S(2)}) %collective-permute-start) | collective-permute-done | bytes 98336 | tf_op jit(solution)/shard_map/ppermute | solution.py:349
  26.7 2.9 %collective-permute-done.9.refs_5_ = bf16[96,896]{1,0:T(8,128)(2,1)S(1)} collective-permute-done((bf16[96,896]{1,0:T(8,128)(2,1)S(1)}, bf16[96,896]{1,0:T(8,128)(2,1)S(1)}, u32[]{:S(2)}, u32[]{:S(2)}) %collective-permute-start.9) | collective-permute-done | bytes 172064 | tf_op jit(solution)/shard_map/ppermute | solution.py:344
  29.6 2.3 %collective-permute-done.8.refs_9_ = bf16[96,896]{1,0:T(8,128)(2,1)S(1)} collective-permute-done((bf16[96,896]{1,0:T(8,128)(2,1)S(1)}, bf16[96,896]{1,0:T(8,128)(2,1)S(1)}, u32[]{:S(2)}, u32[]{:S(2)}) %collective-permute-start.8) | collective-permute-done | bytes 172064 | tf_op jit(solution)/shard_map/ppermute | solution.py:344
  34.5 3.0 %collective-permute-start.14 = (bf16[96,896]{1,0:T(8,128)(2,1)S(1)}, bf16[96,896]{1,0:T(8,128)(2,1)S(1)}, u32[]{:S(2)}, u32[]{:S(2)}) collective-permute-start(bf16[96,896]{1,0:T(8,128)(2,1)S(1)} %get-tuple-element.98), channel_id=1, source_target_pairs={{0,20},{2,22},{4,16},{6,18},{8,28},{10,30},{12,24},{14,26},{16,4},... | collective-permute-start | bytes 516104 | tf_op jit(solution)/shard_map/ppermute | solution.py:344
  40.5 4.8 %collective-permute-done.14.refs_10_ = bf16[96,896]{1,0:T(8,128)(2,1)S(1)} collective-permute-done((bf16[96,896]{1,0:T(8,128)(2,1)S(1)}, bf16[96,896]{1,0:T(8,128)(2,1)S(1)}, u32[]{:S(2)}, u32[]{:S(2)}) %collective-permute-start.14) | collective-permute-done | bytes 172064 | tf_op jit(solution)/shard_map/ppermute | solution.py:344
  47.1 3.6 %collective-permute-start.25 = (bf16[96,896]{1,0:T(8,128)(2,1)S(1)}, bf16[96,896]{1,0:T(8,128)(2,1)S(1)}, u32[]{:S(2)}, u32[]{:S(2)}) collective-permute-start(bf16[96,896]{1,0:T(8,128)(2,1)S(1)} %get-tuple-element.113), channel_id=1, source_target_pairs={{0,14},{2,12},{4,10},{6,8},{8,6},{10,4},{12,2},{14,0},{16,30},{18,... | collective-permute-start | bytes 516104 | tf_op jit(solution)/shard_map/ppermute | solution.py:344
  51.0 2.5 %collective-permute-start.27 = (bf16[96,896]{1,0:T(8,128)(2,1)S(1)}, bf16[96,896]{1,0:T(8,128)(2,1)S(1)}, u32[]{:S(2)}, u32[]{:S(2)}) collective-permute-start(bf16[96,896]{1,0:T(8,128)(2,1)S(1)} %get-tuple-element.117), channel_id=1, source_target_pairs={{0,24},{2,26},{4,28},{6,30},{8,16},{10,18},{12,20},{14,22},{16,8},... | collective-permute-start | bytes 516104 | tf_op jit(solution)/shard_map/ppermute | solution.py:344
  54.3 3.4 %collective-permute-done.26.refs_11_ = bf16[96,896]{1,0:T(8,128)(2,1)S(1)} collective-permute-done((bf16[96,896]{1,0:T(8,128)(2,1)S(1)}, bf16[96,896]{1,0:T(8,128)(2,1)S(1)}, u32[]{:S(2)}, u32[]{:S(2)}) %collective-permute-start.26) | collective-permute-done | bytes 172064 | tf_op jit(solution)/shard_map/ppermute | solution.py:344
  62.1 4.0 %collective-permute-start.23 = (bf16[96,896]{1,0:T(8,128)(2,1)S(1)}, bf16[96,896]{1,0:T(8,128)(2,1)S(1)}, u32[]{:S(2)}, u32[]{:S(2)}) collective-permute-start(bf16[96,896]{1,0:T(8,128)(2,1)S(1)} %get-tuple-element.109), channel_id=1, source_target_pairs={{0,4},{2,6},{4,0},{6,2},{8,12},{10,14},{12,8},{14,10},{16,20},{18,... | collective-permute-start | bytes 516104 | tf_op jit(solution)/shard_map/ppermute | solution.py:344
  68.3 2.3 %collective-permute-start.29 = (bf16[96,896]{1,0:T(8,128)(2,1)S(1)}, bf16[96,896]{1,0:T(8,128)(2,1)S(1)}, u32[]{:S(2)}, u32[]{:S(2)}) collective-permute-start(bf16[96,896]{1,0:T(8,128)(2,1)S(1)} %get-tuple-element.121), channel_id=1, source_target_pairs={{0,28},{2,30},{4,24},{6,26},{8,20},{10,22},{12,16},{14,18},{16,12}... | collective-permute-start | bytes 516104 | tf_op jit(solution)/shard_map/ppermute | solution.py:344
  71.7 15.2 %factor.1 = (bf16[256,1536]{1,0:T(8,128)(2,1)S(1)}, bf16[96,256]{1,0:T(8,128)(2,1)S(1)}) custom-call(s32[16]{0:T(128)S(1)} %pad_add_fusion.1.ids_ref, f32[96,256]{1,0:T(8,128)S(1)} %add.163.refs_0_, f32[96,256]{1,0:T(8,128)S(1)} %collective-permute-done.1.refs_1_, f32[96,256]{1,0:T(8,128)} %collective-permute-done.2.refs_2_, ...), custom_call_target="tpu_custom_call" | custom-call | flops 4026531840 | bytes 2359296 | tf_op jit(solution)/shard_map/factor/pallas_call | solution.py:161
  93.2 5.3 %collective-permute-start.32 = (f32[1,256]{1,0:T(1,128)S(1)}, f32[1,256]{1,0:T(1,128)S(1)}, u32[]{:S(2)}, u32[]{:S(2)}) collective-permute-start(f32[1,256]{1,0:T(1,128)S(1)} %add.164), channel_id=1, source_target_pairs={{0,2},{2,0},{4,6},{6,4},{8,10},{10,8},{12,14},{14,12},{16,18},{18,... | collective-permute-start | bytes 3080 | tf_op jit(solution)/shard_map/ppermute | solution.py:387
  101.6 3.3 %collective-permute-done.36.refs_1_ = bf16[384,256]{1,0:T(8,128)(2,1)S(1)} collective-permute-done((bf16[384,256]{1,0:T(8,128)(2,1)S(1)}, bf16[384,256]{1,0:T(8,128)(2,1)S(1)}, u32[]{:S(2)}, u32[]{:S(2)}) %collective-permute-start.36) | collective-permute-done | bytes 196640 | tf_op jit(solution)/shard_map/ppermute | solution.py:467
  114.5 2.5 %copy-done.1 = f32[96,13824]{1,0:T(8,128)S(1)} copy-done((f32[96,13824]{1,0:T(8,128)S(1)}, f32[96,13824]{1,0:T(8,128)}, u32[]{:S(2)}) %copy-start.1) | copy-done | bytes 5308440
  117.0 2.7 %outputs.9 = (f32[96,13824]{1,0:T(8,128)}, bf16[13824,256]{1,0:T(8,128)(2,1)}, bf16[96,13824]{1,0:T(8,128)(2,1)}) custom-call(s32[2]{0:T(128)S(1)} %get-tuple-element.168.ids_ref, f32[96,13824]{1,0:T(8,128)S(1)} %copy-done.1, bf16[96,256]{1,0:T(8,128)(2,1)S(1)} %get-tuple-element.102.ortho_ref, f32[1,256]{1,0:T(1,128)S(1)} %add_add_fusion.colsq_ref, ...), custom_call_target="tpu_custom_call" | custom-call | flops 176160768 | bytes 3555328 | tf_op jit(solution)/shard_map/outputs/pallas_call | solution.py:267
  119.7 2.8 %collective-permute-start.48 = (bf16[512,256]{1,0:T(8,128)(2,1)S(1)}, bf16[512,256]{1,0:T(8,128)(2,1)S(1)}, u32[]{:S(2)}, u32[]{:S(2)}) collective-permute-start(bf16[512,256]{1,0:T(8,128)(2,1)S(1)} %collective-permute-done.40.refs_0_), channel_id=1, source_target_pairs={{0,2},{2,0},{4,6},{6,4},{8,10},{10,8},{12,14},{14,12},{16,18},{18,... | collective-permute-start | bytes 786440 | tf_op jit(solution)/shard_map/ppermute | solution.py:468
  122.5 2.5 %outputs.10 = (f32[96,13824]{1,0:T(8,128)}, bf16[13824,256]{1,0:T(8,128)(2,1)}, bf16[96,13824]{1,0:T(8,128)(2,1)}) custom-call(s32[2]{0:T(128)S(1)} %get-tuple-element.169.ids_ref, f32[96,13824]{1,0:T(8,128)S(1)} %copy-done.1, bf16[96,256]{1,0:T(8,128)(2,1)S(1)} %get-tuple-element.102.ortho_ref, ...), custom_call_target="tpu_custom_call", output_to_operand_aliasing={{0}: (8, {}), {1}: (9, {}), {2}: (10, {})} | custom-call | flops 176160768 | bytes 3555328 | tf_op jit(solution)/shard_map/outputs/pallas_call | solution.py:267
  127.7 2.5 %outputs.11 = (f32[96,13824]{1,0:T(8,128)}, bf16[13824,256]{1,0:T(8,128)(2,1)}, bf16[96,13824]{1,0:T(8,128)(2,1)}) custom-call(s32[2]{0:T(128)S(1)} %get-tuple-element.167.ids_ref, f32[96,13824]{1,0:T(8,128)S(1)} %copy-done.1, bf16[96,256]{1,0:T(8,128)(2,1)S(1)} %get-tuple-element.102.ortho_ref, ...), custom_call_target="tpu_custom_call", output_to_operand_aliasing={{0}: (8, {}), {1}: (9, {}), {2}: (10, {})} | custom-call | flops 176160768 | bytes 3555328 | tf_op jit(solution)/shard_map/outputs/pallas_call | solution.py:267
  134.2 3.9 %collective-permute-done.55.refs_1_ = bf16[384,256]{1,0:T(8,128)(2,1)S(1)} collective-permute-done((bf16[384,256]{1,0:T(8,128)(2,1)S(1)}, bf16[384,256]{1,0:T(8,128)(2,1)S(1)}, u32[]{:S(2)}, u32[]{:S(2)}) %collective-permute-start.55) | collective-permute-done | bytes 196640 | tf_op jit(solution)/shard_map/ppermute | solution.py:467
  140.6 2.5 %outputs.12 = (f32[96,13824]{1,0:T(8,128)}, bf16[13824,256]{1,0:T(8,128)(2,1)}, bf16[96,13824]{1,0:T(8,128)(2,1)}) custom-call(s32[2]{0:T(128)S(1)} %get-tuple-element.166.ids_ref, f32[96,13824]{1,0:T(8,128)S(1)} %copy-done.1, bf16[96,256]{1,0:T(8,128)(2,1)S(1)} %get-tuple-element.102.ortho_ref, ...), custom_call_target="tpu_custom_call", output_to_operand_aliasing={{0}: (8, {}), {1}: (9, {}), {2}: (10, {})} | custom-call | flops 176160768 | bytes 3555328 | tf_op jit(solution)/shard_map/outputs/pallas_call | solution.py:267
  152.6 2.5 %outputs.14 = (f32[96,13824]{1,0:T(8,128)}, bf16[13824,256]{1,0:T(8,128)(2,1)}, bf16[96,13824]{1,0:T(8,128)(2,1)}) custom-call(s32[2]{0:T(128)S(1)} %get-tuple-element.164.ids_ref, f32[96,13824]{1,0:T(8,128)S(1)} %copy-done.1, bf16[96,256]{1,0:T(8,128)(2,1)S(1)} %get-tuple-element.102.ortho_ref, ...), custom_call_target="tpu_custom_call", output_to_operand_aliasing={{0}: (8, {}), {1}: (9, {}), {2}: (10, {})} | custom-call | flops 176160768 | bytes 3555328 | tf_op jit(solution)/shard_map/outputs/pallas_call | solution.py:267
  155.9 2.5 %outputs.15 = (f32[96,13824]{1,0:T(8,128)}, bf16[13824,256]{1,0:T(8,128)(2,1)}, bf16[96,13824]{1,0:T(8,128)(2,1)}) custom-call(s32[2]{0:T(128)S(1)} %get-tuple-element.163.ids_ref, f32[96,13824]{1,0:T(8,128)S(1)} %copy-done.1, bf16[96,256]{1,0:T(8,128)(2,1)S(1)} %get-tuple-element.102.ortho_ref, ...), custom_call_target="tpu_custom_call", output_to_operand_aliasing={{0}: (8, {}), {1}: (9, {}), {2}: (10, {})} | custom-call | flops 176160768 | bytes 3555328 | tf_op jit(solution)/shard_map/outputs/pallas_call | solution.py:267
  (154 shorter events, 77.0 us)
Async XLA Ops:
  8.1 11.9 %collective-permute-start.4 = (bf16[96,896]{1,0:T(8,128)(2,1)S(1)}, bf16[96,896]{1,0:T(8,128)(2,1)S(1)}, u32[]{:S(2)}, u32[]{:S(2)}) collective-permute-start(bf16[96,896]{1,0:T(8,128)(2,1)S(1)} %get-tuple-element.88), channel_id=1, source_target_pairs={{0,8},{2,10},{4,12},{6,14},{8,0},{10,2},{12,4},{14,6},{16,24},{18,... | collective-permute-start | bytes 516104 | tf_op jit(solution)/shard_map/ppermute | solution.py:344
  10.3 10.4 %collective-permute-start.3 = (bf16[96,896]{1,0:T(8,128)(2,1)S(1)}, bf16[96,896]{1,0:T(8,128)(2,1)S(1)}, u32[]{:S(2)}, u32[]{:S(2)}) collective-permute-start(bf16[96,896]{1,0:T(8,128)(2,1)S(1)} %get-tuple-element.86), channel_id=1, source_target_pairs={{0,16},{2,18},{4,20},{6,22},{8,24},{10,26},{12,28},{14,30},{16,0},... | collective-permute-start | bytes 516104 | tf_op jit(solution)/shard_map/ppermute | solution.py:344
  20.7 11.3 %collective-permute-start.8 = (bf16[96,896]{1,0:T(8,128)(2,1)S(1)}, bf16[96,896]{1,0:T(8,128)(2,1)S(1)}, u32[]{:S(2)}, u32[]{:S(2)}) collective-permute-start(bf16[96,896]{1,0:T(8,128)(2,1)S(1)} %get-tuple-element.92), channel_id=1, source_target_pairs={{0,18},{2,16},{4,22},{6,20},{8,26},{10,24},{12,30},{14,28},{16,2},... | collective-permute-start | bytes 516104 | tf_op jit(solution)/shard_map/ppermute | solution.py:344
  23.0 17.5 %collective-permute-start.15 = (bf16[96,896]{1,0:T(8,128)(2,1)S(1)}, bf16[96,896]{1,0:T(8,128)(2,1)S(1)}, u32[]{:S(2)}, u32[]{:S(2)}) collective-permute-start(bf16[96,896]{1,0:T(8,128)(2,1)S(1)} %get-tuple-element.100), channel_id=1, source_target_pairs={{0,12},{2,14},{4,8},{6,10},{8,4},{10,6},{12,0},{14,2},{16,28},{18,... | collective-permute-start | bytes 516104 | tf_op jit(solution)/shard_map/ppermute | solution.py:344
  25.6 11.9 %collective-permute-start.7 = (f32[96,256]{1,0:T(8,128)}, f32[96,256]{1,0:T(8,128)}, u32[]{:S(2)}, u32[]{:S(2)}) collective-permute-start(f32[96,256]{1,0:T(8,128)} %collective-permute-done.2.refs_2_), channel_id=1, source_target_pairs={{0,4},{2,6},{8,0},{10,2},{16,8},{18,10},{24,16},{26,18},{28,24},{3... | collective-permute-start | bytes 294920 | tf_op jit(solution)/shard_map/ppermute | solution.py:363
  34.5 10.8 %collective-permute-start.14 = (bf16[96,896]{1,0:T(8,128)(2,1)S(1)}, bf16[96,896]{1,0:T(8,128)(2,1)S(1)}, u32[]{:S(2)}, u32[]{:S(2)}) collective-permute-start(bf16[96,896]{1,0:T(8,128)(2,1)S(1)} %get-tuple-element.98), channel_id=1, source_target_pairs={{0,20},{2,22},{4,16},{6,18},{8,28},{10,30},{12,24},{14,26},{16,4},... | collective-permute-start | bytes 516104 | tf_op jit(solution)/shard_map/ppermute | solution.py:344
  37.6 13.1 %collective-permute-start.13 = (f32[96,256]{1,0:T(8,128)}, f32[96,256]{1,0:T(8,128)S(1)}, u32[]{:S(2)}, u32[]{:S(2)}) collective-permute-start(f32[96,256]{1,0:T(8,128)} %collective-permute-done.7.refs_4_), channel_id=1, source_target_pairs={{0,4},{2,6},{8,0},{10,2},{16,8},{18,10},{24,16},{26,18},{28,24},{3... | collective-permute-start | bytes 294920 | tf_op jit(solution)/shard_map/ppermute | solution.py:363
  39.1 11.6 %collective-permute-start.16 = (f32[96,256]{1,0:T(8,128)S(1)}, f32[96,256]{1,0:T(8,128)S(1)}, u32[]{:S(2)}, u32[]{:S(2)}) collective-permute-start(f32[96,256]{1,0:T(8,128)S(1)} %collective-permute-done.6.refs_3_), channel_id=1, source_target_pairs={{0,2},{2,0},{4,6},{6,4},{8,10},{10,8},{12,14},{14,12},{16,18},{18,... | collective-permute-start | bytes 294920 | tf_op jit(solution)/shard_map/ppermute | solution.py:357
  40.5 10.2 %collective-permute-start.17 = (f32[96,256]{1,0:T(8,128)}, f32[96,256]{1,0:T(8,128)S(1)}, u32[]{:S(2)}, u32[]{:S(2)}) collective-permute-start(f32[96,256]{1,0:T(8,128)} %collective-permute-done.7.refs_4_), channel_id=1, source_target_pairs={{0,2},{2,0},{4,6},{6,4},{8,10},{10,8},{12,14},{14,12},{16,18},{18,... | collective-permute-start | bytes 294920 | tf_op jit(solution)/shard_map/ppermute | solution.py:357
  45.3 12.4 %collective-permute-start.26 = (bf16[96,896]{1,0:T(8,128)(2,1)S(1)}, bf16[96,896]{1,0:T(8,128)(2,1)S(1)}, u32[]{:S(2)}, u32[]{:S(2)}) collective-permute-start(bf16[96,896]{1,0:T(8,128)(2,1)S(1)} %get-tuple-element.115), channel_id=1, source_target_pairs={{0,22},{2,20},{4,18},{6,16},{8,30},{10,28},{12,26},{14,24},{16,6},... | collective-permute-start | bytes 516104 | tf_op jit(solution)/shard_map/ppermute | solution.py:344
  47.1 12.5 %collective-permute-start.25 = (bf16[96,896]{1,0:T(8,128)(2,1)S(1)}, bf16[96,896]{1,0:T(8,128)(2,1)S(1)}, u32[]{:S(2)}, u32[]{:S(2)}) collective-permute-start(bf16[96,896]{1,0:T(8,128)(2,1)S(1)} %get-tuple-element.113), channel_id=1, source_target_pairs={{0,14},{2,12},{4,10},{6,8},{8,6},{10,4},{12,2},{14,0},{16,30},{18,... | collective-permute-start | bytes 516104 | tf_op jit(solution)/shard_map/ppermute | solution.py:344
  50.7 10.7 %collective-permute-start.18 = (f32[96,256]{1,0:T(8,128)S(1)}, f32[96,256]{1,0:T(8,128)S(1)}, u32[]{:S(2)}, u32[]{:S(2)}) collective-permute-start(f32[96,256]{1,0:T(8,128)S(1)} %collective-permute-done.12.refs_5_), channel_id=1, source_target_pairs={{0,8},{2,10},{8,16},{10,18},{16,24},{18,26},{24,28},{26,30},{28,20... | collective-permute-start | bytes 294920 | tf_op jit(solution)/shard_map/ppermute | solution.py:359
  51.0 15.4 %collective-permute-start.27 = (bf16[96,896]{1,0:T(8,128)(2,1)S(1)}, bf16[96,896]{1,0:T(8,128)(2,1)S(1)}, u32[]{:S(2)}, u32[]{:S(2)}) collective-permute-start(bf16[96,896]{1,0:T(8,128)(2,1)S(1)} %get-tuple-element.117), channel_id=1, source_target_pairs={{0,24},{2,26},{4,28},{6,30},{8,16},{10,18},{12,20},{14,22},{16,8},... | collective-permute-start | bytes 516104 | tf_op jit(solution)/shard_map/ppermute | solution.py:344
  53.5 14.8 %collective-permute-start.24 = (bf16[96,896]{1,0:T(8,128)(2,1)S(1)}, bf16[96,896]{1,0:T(8,128)(2,1)S(1)}, u32[]{:S(2)}, u32[]{:S(2)}) collective-permute-start(bf16[96,896]{1,0:T(8,128)(2,1)S(1)} %get-tuple-element.111), channel_id=1, source_target_pairs={{0,6},{2,4},{4,2},{6,0},{8,14},{10,12},{12,10},{14,8},{16,22},{18,... | collective-permute-start | bytes 516104 | tf_op jit(solution)/shard_map/ppermute | solution.py:344
  62.1 24.8 %collective-permute-start.23 = (bf16[96,896]{1,0:T(8,128)(2,1)S(1)}, bf16[96,896]{1,0:T(8,128)(2,1)S(1)}, u32[]{:S(2)}, u32[]{:S(2)}) collective-permute-start(bf16[96,896]{1,0:T(8,128)(2,1)S(1)} %get-tuple-element.109), channel_id=1, source_target_pairs={{0,4},{2,6},{4,0},{6,2},{8,12},{10,14},{12,8},{14,10},{16,20},{18,... | collective-permute-start | bytes 516104 | tf_op jit(solution)/shard_map/ppermute | solution.py:344
  66.0 20.8 %collective-permute-start.22 = (bf16[96,896]{1,0:T(8,128)(2,1)S(1)}, bf16[96,896]{1,0:T(8,128)(2,1)S(1)}, u32[]{:S(2)}, u32[]{:S(2)}) collective-permute-start(bf16[96,896]{1,0:T(8,128)(2,1)S(1)} %get-tuple-element.107), channel_id=1, source_target_pairs={{0,2},{2,0},{4,6},{6,4},{8,10},{10,8},{12,14},{14,12},{16,18},{18,... | collective-permute-start | bytes 516104 | tf_op jit(solution)/shard_map/ppermute | solution.py:344
  66.3 20.6 %collective-permute-start.30 = (bf16[96,896]{1,0:T(8,128)(2,1)S(1)}, bf16[96,896]{1,0:T(8,128)(2,1)S(1)}, u32[]{:S(2)}, u32[]{:S(2)}) collective-permute-start(bf16[96,896]{1,0:T(8,128)(2,1)S(1)} %get-tuple-element.123), channel_id=1, source_target_pairs={{0,30},{2,28},{4,26},{6,24},{8,22},{10,20},{12,18},{14,16},{16,14}... | collective-permute-start | bytes 516104 | tf_op jit(solution)/shard_map/ppermute | solution.py:344
  68.3 18.5 %collective-permute-start.29 = (bf16[96,896]{1,0:T(8,128)(2,1)S(1)}, bf16[96,896]{1,0:T(8,128)(2,1)S(1)}, u32[]{:S(2)}, u32[]{:S(2)}) collective-permute-start(bf16[96,896]{1,0:T(8,128)(2,1)S(1)} %get-tuple-element.121), channel_id=1, source_target_pairs={{0,28},{2,30},{4,24},{6,26},{8,20},{10,22},{12,16},{14,18},{16,12}... | collective-permute-start | bytes 516104 | tf_op jit(solution)/shard_map/ppermute | solution.py:344
  70.6 16.3 %collective-permute-start.28 = (bf16[96,896]{1,0:T(8,128)(2,1)S(1)}, bf16[96,896]{1,0:T(8,128)(2,1)S(1)}, u32[]{:S(2)}, u32[]{:S(2)}) collective-permute-start(bf16[96,896]{1,0:T(8,128)(2,1)S(1)} %get-tuple-element.119), channel_id=1, source_target_pairs={{0,26},{2,24},{4,30},{6,28},{8,18},{10,16},{12,22},{14,20},{16,10}... | collective-permute-start | bytes 516104 | tf_op jit(solution)/shard_map/ppermute | solution.py:344
  88.8 16.1 %collective-permute-start.35 = (bf16[512,256]{1,0:T(8,128)(2,1)S(1)}, bf16[512,256]{1,0:T(8,128)(2,1)S(1)}, u32[]{:S(2)}, u32[]{:S(2)}) collective-permute-start(bf16[512,256]{1,0:T(8,128)(2,1)S(1)} %get-tuple-element.125.refs_0_), channel_id=1, source_target_pairs={{0,8},{8,16},{16,24},{24,28},{28,20},{20,12},{12,4},{4,0},{2,6},{1... | collective-permute-start | bytes 786440 | tf_op jit(solution)/shard_map/ppermute | solution.py:467
  110.5 12.0 %collective-permute-start.42 = (bf16[512,256]{1,0:T(8,128)(2,1)S(1)}, bf16[512,256]{1,0:T(8,128)(2,1)S(1)}, u32[]{:S(2)}, u32[]{:S(2)}) collective-permute-start(bf16[512,256]{1,0:T(8,128)(2,1)S(1)} %collective-permute-done.35.refs_0_), channel_id=1, source_target_pairs={{0,2},{2,0},{4,6},{6,4},{8,10},{10,8},{12,14},{14,12},{16,18},{18,... | collective-permute-start | bytes 786440 | tf_op jit(solution)/shard_map/ppermute | solution.py:468
  111.0 13.9 %collective-permute-start.41 = (bf16[512,256]{1,0:T(8,128)(2,1)S(1)}, bf16[512,256]{1,0:T(8,128)(2,1)S(1)}, u32[]{:S(2)}, u32[]{:S(2)}) collective-permute-start(bf16[512,256]{1,0:T(8,128)(2,1)S(1)} %collective-permute-done.40.refs_0_), channel_id=1, source_target_pairs={{0,8},{8,16},{16,24},{24,28},{28,20},{20,12},{12,4},{4,0},{2,6},{1... | collective-permute-start | bytes 786440 | tf_op jit(solution)/shard_map/ppermute | solution.py:467
  126.7 13.8 %collective-permute-start.52 = (bf16[512,256]{1,0:T(8,128)(2,1)S(1)}, bf16[512,256]{1,0:T(8,128)(2,1)S(1)}, u32[]{:S(2)}, u32[]{:S(2)}) collective-permute-start(bf16[512,256]{1,0:T(8,128)(2,1)S(1)} %collective-permute-done.41.refs_0_), channel_id=1, source_target_pairs={{0,2},{2,0},{4,6},{6,4},{8,10},{10,8},{12,14},{14,12},{16,18},{18,... | collective-permute-start | bytes 786440 | tf_op jit(solution)/shard_map/ppermute | solution.py:468
  130.5 12.6 %collective-permute-start.50 = (bf16[512,256]{1,0:T(8,128)(2,1)S(1)}, bf16[512,256]{1,0:T(8,128)(2,1)S(1)}, u32[]{:S(2)}, u32[]{:S(2)}) collective-permute-start(bf16[512,256]{1,0:T(8,128)(2,1)S(1)} %collective-permute-done.46.refs_0_), channel_id=1, source_target_pairs={{0,8},{8,16},{16,24},{24,28},{28,20},{20,12},{12,4},{4,0},{2,6},{1... | collective-permute-start | bytes 786440 | tf_op jit(solution)/shard_map/ppermute | solution.py:467
  (50 other events, 353.5 us)

commit v8 on v7

--- a/solution.py
+++ b/solution.py
@@ -206,69 +206,63 @@
     )(ids, base, ortho_t, *columns)
 
 
-def output_kernel(parts, factor, ids_ref, base_ref, ortho_ref, colsq_ref, *refs):
-    *pieces, nm_ref, nb_ref, up_ref, nm_tile, nb_tile, up_tile, sems = refs
-    share, cols = nm_tile.shape[2], nm_ref.shape[1]
+def output_kernel(share, first, factor, ids_ref, base_ref, ortho_ref, colsq_ref, *refs):
+    piece_ref, *_, nm_ref, nb_ref, up_ref, nm_tile, nb_tile, up_tile, sems = refs
+    count, full = nm_tile.shape[0], nm_tile.shape[2]
+    cols = nm_ref.shape[1]
     scale = lax.rsqrt(colsq_ref[...] + 1e-06)
     ortho = ortho_ref[...]
     over = (((1,), (1,)), ((), ()))
 
-    def copies(n, part, start, width):
-        there = pl.ds(pl.multiple_of(ids_ref[n] * share + start, LANES), width)
-        here = slice(start, start + width)
-        return (
-            pltpu.make_async_copy(nm_tile.at[n, :, here], nm_ref.at[:, there], sems.at[n, part, 0]),
-            pltpu.make_async_copy(nb_tile.at[n, here, :], nb_ref.at[there, :], sems.at[n, part, 1]),
-            pltpu.make_async_copy(up_tile.at[n, :, here], up_ref.at[:, there], sems.at[n, part, 2]),
+    def copies(n, width):
+        there = pl.ds(pl.multiple_of(ids_ref[n] * share + first, LANES), width)
+        sides = (
+            (nm_tile.at[n, :, :width], nm_ref.at[:, there]),
+            (nb_tile.at[n, :width, :], nb_ref.at[there, :]),
+            (up_tile.at[n, :, :width], up_ref.at[:, there]),
         )
-
-    ranges = []
-    for n in range(nm_tile.shape[0]):
-        start = 0
-        for part in range(parts):
-            piece = pieces[n * parts + part]
-            stop = start + piece.shape[0]
-
-            def compute(width):
-                here = slice(start, start + width)
-                there = pl.ds(pl.multiple_of(ids_ref[n] * share + start, LANES), width)
-                back = piece[:width, :]
-                unit = (back.astype(F32) * scale).astype(BF16)
-                nb_tile[n, here, :] = unit
-                nm_tile[n, :, here] = base_ref[:, there] - 0.05 * lax.dot_general(
-                    ortho, back, over, preferred_element_type=F32
-                )
-                up_tile[n, :, here] = (
-                    factor * lax.dot_general(ortho, unit, over, preferred_element_type=F32)
-                ).astype(BF16)
-                for copy in copies(n, part, start, width):
-                    copy.start()
-
-            by_width(ids_ref[n], cols, share, start, stop, compute)
-            ranges.append((n, part, start, stop))
-            start = stop
-
-    for n, part, start, stop in ranges:
+        return [
+            pltpu.make_async_copy(source, target, sems.at[n, which])
+            for which, (source, target) in enumerate(sides)
+        ]
+
+    for n in range(count):
+
+        def compute(width):
+            there = pl.ds(pl.multiple_of(ids_ref[n] * share + first, LANES), width)
+            back = piece_ref[n * full : n * full + width, :]
+            unit = (back.astype(F32) * scale).astype(BF16)
+            nb_tile[n, :width, :] = unit
+            nm_tile[n, :, :width] = base_ref[:, there] - 0.05 * lax.dot_general(
+                ortho, back, over, preferred_element_type=F32
+            )
+            up_tile[n, :, :width] = (
+                factor * lax.dot_general(ortho, unit, over, preferred_element_type=F32)
+            ).astype(BF16)
+            for copy in copies(n, width):
+                copy.start()
+
+        by_width(ids_ref[n], cols, share, first, first + full, compute)
+
+    for n in range(count):
 
         def wait(width):
-            for copy in copies(n, part, start, width):
+            for copy in copies(n, width):
                 copy.wait()
 
-        by_width(ids_ref[n], cols, share, start, stop, wait)
-
-
-def output_call(ids, base, cols, ortho, colsq, blocks, factor, previous):
-    rows, rank = ortho.shape
-    count, parts = len(blocks), len(blocks[0])
-    pieces = [part for block in blocks for part in block]
-    share = sum(part.shape[0] for part in blocks[0])
+        by_width(ids_ref[n], cols, share, first, first + full, wait)
+
+
+def output_call(ids, base, ortho, colsq, share, first, blocks, factor, previous):
+    rows, cols = base.shape
+    rank = ortho.shape[1]
+    count = ids.shape[0]
+    width = blocks.shape[0] // count
     previous = previous or ()
     vmem, hbm = pl.BlockSpec(memory_space=pltpu.VMEM), pl.BlockSpec(memory_space=pltpu.HBM)
     return pl.pallas_call(
-        functools.partial(output_kernel, parts, factor),
-        in_specs=[pl.BlockSpec(memory_space=pltpu.SMEM)]
-        + [vmem] * (3 + len(pieces))
-        + [hbm] * len(previous),
+        functools.partial(output_kernel, share, first, factor),
+        in_specs=[pl.BlockSpec(memory_space=pltpu.SMEM)] + [vmem] * 4 + [hbm] * len(previous),
         out_specs=[hbm] * 3,
         out_shape=[
             jax.ShapeDtypeStruct((rows, cols), F32),
@@ -276,18 +270,18 @@
             jax.ShapeDtypeStruct((rows, cols), BF16),
         ],
         scratch_shapes=[
-            pltpu.VMEM((count, rows, share), F32),
-            pltpu.VMEM((count, share, rank), BF16),
-            pltpu.VMEM((count, rows, share), BF16),
-            pltpu.SemaphoreType.DMA((count, parts, 3)),
+            pltpu.VMEM((count, rows, width), F32),
+            pltpu.VMEM((count, width, rank), BF16),
+            pltpu.VMEM((count, rows, width), BF16),
+            pltpu.SemaphoreType.DMA((count, 3)),
         ],
-        input_output_aliases={4 + len(pieces) + n: n for n in range(len(previous))},
-        compiler_params=params(16),
+        input_output_aliases={5 + n: n for n in range(len(previous))},
+        compiler_params=params(24),
         cost_estimate=cost(
-            4 * rows * share * rank * count, count * share * (rows * 10 + rank * 4)
+            4 * rows * width * rank * count, count * width * (rows * 10 + rank * 4)
         ),
         name="outputs",
-    )(ids, base, ortho, colsq, *pieces, *previous)
+    )(ids, base, ortho, colsq, blocks, *previous)
 
 
 def chip_at(position, chips):
@@ -304,15 +298,11 @@
     return [2 * q for q in range(half)] + [2 * (chips - 1 - q) + 1 for q in range(half, chips)]
 
 
-def ring_steps(count, by_core):
+def ring_steps(count):
     order = ring_order(count // 2)
     after = dict(zip(order, order[1:] + order[:1]))
-    before = {b: a for a, b in after.items()}
     up = [(2 * c + k, 2 * after[c] + k) for c in order for k in (0, 1)]
-    down = [(2 * c + k, 2 * before[c] + k) for c in order for k in (0, 1)]
-    if not by_core:
-        return up, down
-    return [p for p in up if p[0] % 2 == 0] + [p for p in down if p[0] % 2 == 1]
+    return up, [(b, a) for a, b in up]
 
 
 def swap_pairs(count):
@@ -335,7 +325,7 @@
     chips = count // 2
     me = lax.axis_index("fsdp")
     place, core = position_of(me // 2, chips), me % 2
-    up, down = ring_steps(count, False)
+    up, down = ring_steps(count)
     columns = {0: outgoing[0]}
 
     def exchange(window, *after):
@@ -425,59 +415,29 @@
         cuts = [share - tiles // 2 * LANES, tiles // 2 * LANES]
     part, *back = back_call(partners, base, ortho_t, columns, cuts)
 
-    outputs = functools.partial(output_call, factor=factor)
-    if not ring:
+    if ring:
+        groups = [list(range(core, count, 2)) for core in (0, 1)]
+        colsq = part
+        for axis, distances in sum_rounds(count):
+            colsq = sum_round(colsq, axis, distances)
+        chip = 2 * jnp.arange(chips, dtype=jnp.int32)
+        owners = [chip + me % 2, chip + 1 - me % 2]
+    else:
         colsq = lax.psum(part, ("fsdp", "tp"))
-        whole = lax.all_gather(back[0], "fsdp", axis=0)
-        valid = -(-cols // share)
-        return tuple(
-            outputs(
-                jnp.arange(valid, dtype=jnp.int32), base, cols, ortho_here, colsq,
-                [[whole[n]] for n in range(valid)], previous=None,
+        owners = [jnp.arange(-(-cols // share), dtype=jnp.int32)]
+    result, first = None, 0
+    for piece in back:
+        if ring:
+            mine = lax.all_gather(piece, "fsdp", axis=0, tiled=True, axis_index_groups=groups)
+            mine = tie(mine, *(result or (colsq,)))
+            gathered = [mine, lax.ppermute(mine, "fsdp", swap_pairs(count))]
+        else:
+            gathered = [lax.all_gather(piece, "fsdp", axis=0, tiled=True)[: owners[0].size * share]]
+        for ids, blocks in zip(owners, gathered):
+            result = output_call(
+                ids, base, ortho_here, colsq, share, first, blocks, factor, result
             )
-        )
-
-    place, core = position_of(me // 2, chips), me % 2
-    turn = ring_steps(count, True)
-    swap = swap_pairs(count)
-    steps = jnp.arange(chips, dtype=jnp.int32)
-    way = 1 - 2 * core
-    mine = 2 * chip_at((place - way * steps) % chips, chips) + core
-    theirs = 2 * chip_at((place + way * steps) % chips, chips) + 1 - core
-    ids = jnp.stack([mine, theirs], axis=1).astype(jnp.int32)
-    colsq, result = part, None
-    rounds = sum_rounds(count)
-
-    def write(ids, blocks):
-        return outputs(ids, base, cols, ortho_here, colsq, blocks, previous=result)
-
-    mine, theirs = [list(back)], []
-    written, waiting = 0, ()
-    for step in range(chips):
-        mine.append([])
-        theirs.append([])
-        if step == 1:
-            waiting += (*mine[1], colsq)
-        elif step == 2:
-            waiting += (colsq,)
-        for n in range(len(cuts)):
-            block = tie(mine[step][n], *waiting)
-            waiting = ()
-            if step + 1 < chips:
-                mine[step + 1].append(lax.ppermute(block, "fsdp", turn))
-            theirs[step].append(lax.ppermute(block, "fsdp", swap))
-            for _ in range(2 if step == 0 else 1):
-                if rounds and n == 0:
-                    colsq = sum_round(tie(colsq, block), *rounds.pop(0))
-            ready = step if step + 1 == chips else step + n - 1
-            if step > 1 and written < ready:
-                result = write(ids[written], [mine[written], theirs[written]])
-                written += 1
-                waiting = tuple(result)
-    for n in range(written, chips - 1):
-        result = write(ids[n], [mine[n], theirs[n]])
-    result = write(ids[-1, :1], [mine[chips - 1]])
-    result = write(ids[-1, 1:], [theirs[chips - 1]])
+        first += piece.shape[0]
     return tuple(result)
 
 

time: 164 us -> 211 us (1.29)
  waiting for transfers between devices: 34.4 us -> 92.4 us
  starting transfers between devices: 78.5 us -> 55.7 us
  between operations: 1.18 us -> 14.3 us
  Pallas kernels: 39.2 us -> 33.4 us
  local copies, waits for them, and re-layouts: 5.23 us -> 9.19 us
    all_gather x0 -> x2, waiting for transfers between devices: none -> 64 us  [local(): lax.all_gather(piece, 'fsdp', axis=0, tiled=True, axis_index_groups=groups)]
    ppermute x30 -> x2, starting transfers between devices: 25.1 us -> 3.08 us  [local(): gathered = [mine, lax.ppermute(mine, 'fsdp', swap_pairs(count))]]
    ppermute x30 -> x2, waiting for transfers between devices: 9.61 us -> 0.01 us  [local(): gathered = [mine, lax.ppermute(mine, 'fsdp', swap_pairs(count))]]
    pallas_call x9 -> x4, Pallas kernels: 21.1 us -> 14.7 us  [output_call(): pl.pallas_call(functools.partial(output_kernel, share, first, factor), in...]
    unnamed x12 -> x18, local copies, waits for them, and re-layouts: 3.69 us -> 9.19 us
    ppermute x7, waiting for transfers between devices: 3.05 us -> 6.14 us  [sum_round(): terms.append(lax.ppermute(x, axis, [(n, n ^ d) for n in range(size)]))]
  transfers between devices with their start and end apart: 68 -> 42, of which waited for: 17 -> 16; matrix products, arithmetic and copies ran while one was open for 1% -> 0% of each run, Pallas kernels for 21% -> 13%
where the time goes in v8:
time: 211 us; the launch traced here: 210 us
  waiting for transfers between devices  92.4 us (44%)
  starting transfers between devices  55.7 us (26%)
  Pallas kernels  33.4 us (16%)
  between operations  14.3 us (7%)
  local copies, waits for them, and re-layouts  9.19 us (4%)
  other arithmetic  4.09 us (2%)
    all_gather x2, waiting for transfers between devices, local(): lax.all_gather(piece, 'fsdp', axis=0, tiled=True, axis_index_groups=groups)  64 us
    ppermute x15, starting transfers between devices, exchange(): columns[k] = lax.ppermute(tie(outgoing[k], *after), 'fsdp', pairs)  29.8 us
    pallas_call x1, Pallas kernels, factor_call(): pl.pallas_call(functools.partial(factor_kernel, count), in_specs=[pl.Bloc...  15.2 us
    ppermute x15, waiting for transfers between devices, exchange(): columns[k] = lax.ppermute(tie(outgoing[k], *after), 'fsdp', pairs)  14.7 us
    pallas_call x4, Pallas kernels, output_call(): pl.pallas_call(functools.partial(output_kernel, share, first, factor), in...  14.7 us
    ppermute x7, starting transfers between devices, sum_round(): terms.append(lax.ppermute(x, axis, [(n, n ^ d) for n in range(size)]))  10.8 us
    unnamed x18, local copies, waits for them, and re-layouts  9.19 us
    ppermute x7, waiting for transfers between devices, sum_round(): terms.append(lax.ppermute(x, axis, [(n, n ^ d) for n in range(size)]))  6.14 us
  transfers between devices with their start and end apart: 42, of which 16 were waited for; matrix products, arithmetic and copies ran while one was open for 0% of the time, Pallas kernels for 13%

profile of v8, /device:TPU:1, one launch (start us, length us, event | category | flops | bytes accessed | tf_op | source)
XLA Modules:
  0.0 210.4 jit_solution(5859672186467957058)
XLA Ops:
  7.2 4.0 %convert_add_fusion.base_ref = f32[96,13824]{1,0:T(8,128)S(1)} fusion(f32[96,13824]{1,0:T(8,128)} %param.4, bf16[96,13824]{1,0:T(8,128)(2,1)} %param.5), kind=kLoop, calls=%fused_computation | loop fusion | flops 2654208 | bytes 13271040 | tf_op jit(solution)/shard_map/add | solution.py:394
  16.9 2.3 %collective-permute-start.3 = (bf16[96,896]{1,0:T(8,128)(2,1)S(1)}, bf16[96,896]{1,0:T(8,128)(2,1)S(1)}, u32[]{:S(2)}, u32[]{:S(2)}) collective-permute-start(bf16[96,896]{1,0:T(8,128)(2,1)S(1)} %get-tuple-element.61), channel_id=1, source_target_pairs={{0,16},{2,18},{4,20},{6,22},{8,24},{10,26},{12,28},{14,30},{16,0},... | collective-permute-start | bytes 516104 | tf_op jit(solution)/shard_map/ppermute | solution.py:334
  20.4 2.5 %collective-permute-done = f32[96,256]{1,0:T(8,128)S(1)} collective-permute-done((f32[96,256]{1,0:T(8,128)S(1)}, f32[96,256]{1,0:T(8,128)S(1)}, u32[]{:S(2)}, u32[]{:S(2)}) %collective-permute-start) | collective-permute-done | bytes 98336 | tf_op jit(solution)/shard_map/ppermute | solution.py:339
  29.5 2.3 %collective-permute-start.15 = (bf16[96,896]{1,0:T(8,128)(2,1)S(1)}, bf16[96,896]{1,0:T(8,128)(2,1)S(1)}, u32[]{:S(2)}, u32[]{:S(2)}) collective-permute-start(bf16[96,896]{1,0:T(8,128)(2,1)S(1)} %get-tuple-element.75), channel_id=1, source_target_pairs={{0,12},{2,14},{4,8},{6,10},{8,4},{10,6},{12,0},{14,2},{16,28},{18,... | collective-permute-start | bytes 516104 | tf_op jit(solution)/shard_map/ppermute | solution.py:334
  33.3 2.9 %collective-permute-done.9.refs_5_ = bf16[96,896]{1,0:T(8,128)(2,1)S(1)} collective-permute-done((bf16[96,896]{1,0:T(8,128)(2,1)S(1)}, bf16[96,896]{1,0:T(8,128)(2,1)S(1)}, u32[]{:S(2)}, u32[]{:S(2)}) %collective-permute-start.9) | collective-permute-done | bytes 172064 | tf_op jit(solution)/shard_map/ppermute | solution.py:334
  36.2 2.4 %collective-permute-done.8.refs_9_ = bf16[96,896]{1,0:T(8,128)(2,1)S(1)} collective-permute-done((bf16[96,896]{1,0:T(8,128)(2,1)S(1)}, bf16[96,896]{1,0:T(8,128)(2,1)S(1)}, u32[]{:S(2)}, u32[]{:S(2)}) %collective-permute-start.8) | collective-permute-done | bytes 172064 | tf_op jit(solution)/shard_map/ppermute | solution.py:334
  41.1 3.0 %collective-permute-start.14 = (bf16[96,896]{1,0:T(8,128)(2,1)S(1)}, bf16[96,896]{1,0:T(8,128)(2,1)S(1)}, u32[]{:S(2)}, u32[]{:S(2)}) collective-permute-start(bf16[96,896]{1,0:T(8,128)(2,1)S(1)} %get-tuple-element.73), channel_id=1, source_target_pairs={{0,20},{2,22},{4,16},{6,18},{8,28},{10,30},{12,24},{14,26},{16,4},... | collective-permute-start | bytes 516104 | tf_op jit(solution)/shard_map/ppermute | solution.py:334
  47.1 4.8 %collective-permute-done.14.refs_10_ = bf16[96,896]{1,0:T(8,128)(2,1)S(1)} collective-permute-done((bf16[96,896]{1,0:T(8,128)(2,1)S(1)}, bf16[96,896]{1,0:T(8,128)(2,1)S(1)}, u32[]{:S(2)}, u32[]{:S(2)}) %collective-permute-start.14) | collective-permute-done | bytes 172064 | tf_op jit(solution)/shard_map/ppermute | solution.py:334
  53.6 3.6 %collective-permute-start.25 = (bf16[96,896]{1,0:T(8,128)(2,1)S(1)}, bf16[96,896]{1,0:T(8,128)(2,1)S(1)}, u32[]{:S(2)}, u32[]{:S(2)}) collective-permute-start(bf16[96,896]{1,0:T(8,128)(2,1)S(1)} %get-tuple-element.88), channel_id=1, source_target_pairs={{0,14},{2,12},{4,10},{6,8},{8,6},{10,4},{12,2},{14,0},{16,30},{18,... | collective-permute-start | bytes 516104 | tf_op jit(solution)/shard_map/ppermute | solution.py:334
  57.5 2.5 %collective-permute-start.27 = (bf16[96,896]{1,0:T(8,128)(2,1)S(1)}, bf16[96,896]{1,0:T(8,128)(2,1)S(1)}, u32[]{:S(2)}, u32[]{:S(2)}) collective-permute-start(bf16[96,896]{1,0:T(8,128)(2,1)S(1)} %get-tuple-element.92), channel_id=1, source_target_pairs={{0,24},{2,26},{4,28},{6,30},{8,16},{10,18},{12,20},{14,22},{16,8},... | collective-permute-start | bytes 516104 | tf_op jit(solution)/shard_map/ppermute | solution.py:334
  60.9 3.4 %collective-permute-done.26.refs_11_ = bf16[96,896]{1,0:T(8,128)(2,1)S(1)} collective-permute-done((bf16[96,896]{1,0:T(8,128)(2,1)S(1)}, bf16[96,896]{1,0:T(8,128)(2,1)S(1)}, u32[]{:S(2)}, u32[]{:S(2)}) %collective-permute-start.26) | collective-permute-done | bytes 172064 | tf_op jit(solution)/shard_map/ppermute | solution.py:334
  68.6 4.0 %collective-permute-start.23 = (bf16[96,896]{1,0:T(8,128)(2,1)S(1)}, bf16[96,896]{1,0:T(8,128)(2,1)S(1)}, u32[]{:S(2)}, u32[]{:S(2)}) collective-permute-start(bf16[96,896]{1,0:T(8,128)(2,1)S(1)} %get-tuple-element.84), channel_id=1, source_target_pairs={{0,4},{2,6},{4,0},{6,2},{8,12},{10,14},{12,8},{14,10},{16,20},{18,... | collective-permute-start | bytes 516104 | tf_op jit(solution)/shard_map/ppermute | solution.py:334
  74.9 2.3 %collective-permute-start.29 = (bf16[96,896]{1,0:T(8,128)(2,1)S(1)}, bf16[96,896]{1,0:T(8,128)(2,1)S(1)}, u32[]{:S(2)}, u32[]{:S(2)}) collective-permute-start(bf16[96,896]{1,0:T(8,128)(2,1)S(1)} %get-tuple-element.96), channel_id=1, source_target_pairs={{0,28},{2,30},{4,24},{6,26},{8,20},{10,22},{12,16},{14,18},{16,12}... | collective-permute-start | bytes 516104 | tf_op jit(solution)/shard_map/ppermute | solution.py:334
  78.2 15.2 %factor.1 = (bf16[256,1536]{1,0:T(8,128)(2,1)S(1)}, bf16[96,256]{1,0:T(8,128)(2,1)S(1)}) custom-call(s32[16]{0:T(128)S(1)} %pad_add_fusion.ids_ref, f32[96,256]{1,0:T(8,128)S(1)} %add.77.refs_0_, f32[96,256]{1,0:T(8,128)S(1)} %collective-permute-done.1.refs_1_, f32[96,256]{1,0:T(8,128)S(1)} %collective-permute-done.2.refs_2_, ...), custom_call_target="tpu_custom_call" | custom-call | flops 4026531840 | bytes 2359296 | tf_op jit(solution)/shard_map/factor/pallas_call | solution.py:161
  93.5 2.5 %back.1 = (f32[1,256]{1,0:T(1,128)S(1)}, bf16[512,256]{1,0:T(8,128)(2,1)}, bf16[384,256]{1,0:T(8,128)(2,1)}) custom-call(s32[16]{0:T(128)S(1)} %iota_xor_fusion.ids_ref, f32[96,13824]{1,0:T(8,128)S(1)} %bitcast.2, bf16[256,1536]{1,0:T(8,128)(2,1)S(1)} %get-tuple-element.78.ortho_t_ref, bf16[96,896]{1,0:T(8,128)(2,1)S(1)} %get-tuple-element.79.refs_0_, ...), custom_call_target="tpu_custom_call" | custom-call | flops 704643072 | bytes 2752512 | tf_op jit(solution)/shard_map/back/pallas_call | solution.py:196
  104.9 4.4 %collective-permute-start.35 = (f32[1,256]{1,0:T(1,128)S(1)}, f32[1,256]{1,0:T(1,128)S(1)}, u32[]{:S(2)}, u32[]{:S(2)}) collective-permute-start(f32[1,256]{1,0:T(1,128)S(1)} %add_add_fusion.1), channel_id=1, source_target_pairs={{0,8},{2,10},{4,12},{6,14},{8,0},{10,2},{12,4},{14,6},{16,24},{18,... | collective-permute-start | bytes 3080 | tf_op jit(solution)/shard_map/ppermute | solution.py:377
  113.7 32.7 %all-gather.5.cloned.1.call-done.refs_0_ = bf16[4096,256]{1,0:T(8,128)(2,1)} async-done(((bf16[512,256]{1,0:T(8,128)(2,1)}), bf16[4096,256]{1,0:T(8,128)(2,1)}) %all-gather.5.cloned.1.call-update) | async-done | bytes 2097168 | tf_op jit(solution)/shard_map/all_gather | solution.py:431
  148.2 2.5 %copy-done.1 = f32[96,13824]{1,0:T(8,128)S(1)} copy-done((f32[96,13824]{1,0:T(8,128)S(1)}, f32[96,13824]{1,0:T(8,128)}, u32[]{:S(2)}) %copy-start.1) | copy-done | bytes 5308440
  152.3 4.1 %outputs.4 = (f32[96,13824]{1,0:T(8,128)}, bf16[13824,256]{1,0:T(8,128)(2,1)}, bf16[96,13824]{1,0:T(8,128)(2,1)}) custom-call(s32[8]{0:T(128)S(1)} %fusion.4.ids_ref, f32[96,13824]{1,0:T(8,128)S(1)} %copy-done.1, bf16[96,256]{1,0:T(8,128)(2,1)S(1)} %get-tuple-element.77.ortho_ref, f32[1,256]{1,0:T(1,128)S(1)} %add_add_fusion.colsq_ref, ...), custom_call_target="tpu_custom_call" | custom-call | flops 402653184 | bytes 8126464 | tf_op jit(solution)/shard_map/outputs/pallas_call | solution.py:263
  156.4 3.9 %outputs.5 = (f32[96,13824]{1,0:T(8,128)}, bf16[13824,256]{1,0:T(8,128)(2,1)}, bf16[96,13824]{1,0:T(8,128)(2,1)}) custom-call(s32[8]{0:T(128)S(1)} %add_subtract_fusion.1.ids_ref, f32[96,13824]{1,0:T(8,128)S(1)} %copy-done.1, bf16[96,256]{1,0:T(8,128)(2,1)S(1)} %get-tuple-element.77.ortho_ref, ...), custom_call_target="tpu_custom_call", output_to_operand_aliasing={{0}: (5, {}), {1}: (6, {}), {2}: (7, {})} | custom-call | flops 402653184 | bytes 8126464 | tf_op jit(solution)/shard_map/outputs/pallas_call | solution.py:263
  160.3 31.3 %all-gather.3.cloned.1.call-done.refs_0_ = bf16[3072,256]{1,0:T(8,128)(2,1)} async-done(((bf16[384,256]{1,0:T(8,128)(2,1)}), bf16[3072,256]{1,0:T(8,128)(2,1)}) %all-gather.3.cloned.1.call-update) | async-done | bytes 1572880 | tf_op jit(solution)/shard_map/all_gather | solution.py:431
  192.9 2.5 %copy-done.2 = f32[96,13824]{1,0:T(8,128)S(1)} copy-done((f32[96,13824]{1,0:T(8,128)S(1)}, f32[96,13824]{1,0:T(8,128)}, u32[]{:S(2)}) %copy-start.2) | copy-done | bytes 5308440
  196.8 3.2 %outputs.6 = (f32[96,13824]{1,0:T(8,128)}, bf16[13824,256]{1,0:T(8,128)(2,1)}, bf16[96,13824]{1,0:T(8,128)(2,1)}) custom-call(s32[8]{0:T(128)S(1)} %fusion.4.ids_ref, f32[96,13824]{1,0:T(8,128)S(1)} %copy-done.2, bf16[96,256]{1,0:T(8,128)(2,1)S(1)} %get-tuple-element.77.ortho_ref, ...), custom_call_target="tpu_custom_call", output_to_operand_aliasing={{0}: (5, {}), {1}: (6, {}), {2}: (7, {})} | custom-call | flops 301989888 | bytes 6094848 | tf_op jit(solution)/shard_map/outputs/pallas_call | solution.py:263
  200.1 3.5 %outputs.7 = (f32[96,13824]{1,0:T(8,128)}, bf16[13824,256]{1,0:T(8,128)(2,1)}, bf16[96,13824]{1,0:T(8,128)(2,1)}) custom-call(s32[8]{0:T(128)S(1)} %add_subtract_fusion.1.ids_ref, f32[96,13824]{1,0:T(8,128)S(1)} %copy-done.2, bf16[96,256]{1,0:T(8,128)(2,1)S(1)} %get-tuple-element.77.ortho_ref, ...), custom_call_target="tpu_custom_call", output_to_operand_aliasing={{0}: (5, {}), {1}: (6, {}), {2}: (7, {})} | custom-call | flops 301989888 | bytes 6094848 | tf_op jit(solution)/shard_map/outputs/pallas_call | solution.py:263
  (100 shorter events, 50.3 us)
Async XLA Ops:
  7.2 139.3 %all-gather.5.cloned.1.call-start = ((), (), s32[]{:S(2)}) async-start(), calls=%async_computation.1 | async-start | bytes 2359296 | tf_op jit(solution)/shard_map/all_gather | solution.py:431
  14.7 11.9 %collective-permute-start.4 = (bf16[96,896]{1,0:T(8,128)(2,1)S(1)}, bf16[96,896]{1,0:T(8,128)(2,1)S(1)}, u32[]{:S(2)}, u32[]{:S(2)}) collective-permute-start(bf16[96,896]{1,0:T(8,128)(2,1)S(1)} %get-tuple-element.63), channel_id=1, source_target_pairs={{0,8},{2,10},{4,12},{6,14},{8,0},{10,2},{12,4},{14,6},{16,24},{18,... | collective-permute-start | bytes 516104 | tf_op jit(solution)/shard_map/ppermute | solution.py:334
  16.9 10.4 %collective-permute-start.3 = (bf16[96,896]{1,0:T(8,128)(2,1)S(1)}, bf16[96,896]{1,0:T(8,128)(2,1)S(1)}, u32[]{:S(2)}, u32[]{:S(2)}) collective-permute-start(bf16[96,896]{1,0:T(8,128)(2,1)S(1)} %get-tuple-element.61), channel_id=1, source_target_pairs={{0,16},{2,18},{4,20},{6,22},{8,24},{10,26},{12,28},{14,30},{16,0},... | collective-permute-start | bytes 516104 | tf_op jit(solution)/shard_map/ppermute | solution.py:334
  26.6 9.6 %collective-permute-start.9 = (bf16[96,896]{1,0:T(8,128)(2,1)S(1)}, bf16[96,896]{1,0:T(8,128)(2,1)S(1)}, u32[]{:S(2)}, u32[]{:S(2)}) collective-permute-start(bf16[96,896]{1,0:T(8,128)(2,1)S(1)} %get-tuple-element.69), channel_id=1, source_target_pairs={{0,10},{2,8},{4,14},{6,12},{8,2},{10,0},{12,6},{14,4},{16,26},{18,... | collective-permute-start | bytes 516104 | tf_op jit(solution)/shard_map/ppermute | solution.py:334
  27.3 11.3 %collective-permute-start.8 = (bf16[96,896]{1,0:T(8,128)(2,1)S(1)}, bf16[96,896]{1,0:T(8,128)(2,1)S(1)}, u32[]{:S(2)}, u32[]{:S(2)}) collective-permute-start(bf16[96,896]{1,0:T(8,128)(2,1)S(1)} %get-tuple-element.67), channel_id=1, source_target_pairs={{0,18},{2,16},{4,22},{6,20},{8,26},{10,24},{12,30},{14,28},{16,2},... | collective-permute-start | bytes 516104 | tf_op jit(solution)/shard_map/ppermute | solution.py:334
  29.5 17.6 %collective-permute-start.15 = (bf16[96,896]{1,0:T(8,128)(2,1)S(1)}, bf16[96,896]{1,0:T(8,128)(2,1)S(1)}, u32[]{:S(2)}, u32[]{:S(2)}) collective-permute-start(bf16[96,896]{1,0:T(8,128)(2,1)S(1)} %get-tuple-element.75), channel_id=1, source_target_pairs={{0,12},{2,14},{4,8},{6,10},{8,4},{10,6},{12,0},{14,2},{16,28},{18,... | collective-permute-start | bytes 516104 | tf_op jit(solution)/shard_map/ppermute | solution.py:334
  32.1 12.0 %collective-permute-start.7 = (f32[96,256]{1,0:T(8,128)S(1)}, f32[96,256]{1,0:T(8,128)}, u32[]{:S(2)}, u32[]{:S(2)}) collective-permute-start(f32[96,256]{1,0:T(8,128)S(1)} %collective-permute-done.2.refs_2_), channel_id=1, source_target_pairs={{8,0},{10,2},{16,8},{18,10},{24,16},{26,18},{28,24},{30,26},{20,28... | collective-permute-start | bytes 294920 | tf_op jit(solution)/shard_map/ppermute | solution.py:353
  41.1 10.8 %collective-permute-start.14 = (bf16[96,896]{1,0:T(8,128)(2,1)S(1)}, bf16[96,896]{1,0:T(8,128)(2,1)S(1)}, u32[]{:S(2)}, u32[]{:S(2)}) collective-permute-start(bf16[96,896]{1,0:T(8,128)(2,1)S(1)} %get-tuple-element.73), channel_id=1, source_target_pairs={{0,20},{2,22},{4,16},{6,18},{8,28},{10,30},{12,24},{14,26},{16,4},... | collective-permute-start | bytes 516104 | tf_op jit(solution)/shard_map/ppermute | solution.py:334
  44.1 9.5 %collective-permute-start.12 = (f32[96,256]{1,0:T(8,128)S(1)}, f32[96,256]{1,0:T(8,128)S(1)}, u32[]{:S(2)}, u32[]{:S(2)}) collective-permute-start(f32[96,256]{1,0:T(8,128)S(1)} %collective-permute-done.6.refs_3_), channel_id=1, source_target_pairs={{0,8},{2,10},{8,16},{10,18},{16,24},{18,26},{24,28},{26,30},{28,20... | collective-permute-start | bytes 294920 | tf_op jit(solution)/shard_map/ppermute | solution.py:349
  44.2 13.1 %collective-permute-start.13 = (f32[96,256]{1,0:T(8,128)}, f32[96,256]{1,0:T(8,128)S(1)}, u32[]{:S(2)}, u32[]{:S(2)}) collective-permute-start(f32[96,256]{1,0:T(8,128)} %collective-permute-done.7.refs_4_), channel_id=1, source_target_pairs={{8,0},{10,2},{16,8},{18,10},{24,16},{26,18},{28,24},{30,26},{20,28... | collective-permute-start | bytes 294920 | tf_op jit(solution)/shard_map/ppermute | solution.py:353
  45.6 11.6 %collective-permute-start.16 = (f32[96,256]{1,0:T(8,128)S(1)}, f32[96,256]{1,0:T(8,128)S(1)}, u32[]{:S(2)}, u32[]{:S(2)}) collective-permute-start(f32[96,256]{1,0:T(8,128)S(1)} %collective-permute-done.6.refs_3_), channel_id=1, source_target_pairs={{0,2},{2,0},{4,6},{6,4},{8,10},{10,8},{12,14},{14,12},{16,18},{18,... | collective-permute-start | bytes 294920 | tf_op jit(solution)/shard_map/ppermute | solution.py:347
  47.1 10.2 %collective-permute-start.17 = (f32[96,256]{1,0:T(8,128)}, f32[96,256]{1,0:T(8,128)S(1)}, u32[]{:S(2)}, u32[]{:S(2)}) collective-permute-start(f32[96,256]{1,0:T(8,128)} %collective-permute-done.7.refs_4_), channel_id=1, source_target_pairs={{0,2},{2,0},{4,6},{6,4},{8,10},{10,8},{12,14},{14,12},{16,18},{18,... | collective-permute-start | bytes 294920 | tf_op jit(solution)/shard_map/ppermute | solution.py:347
  51.9 12.4 %collective-permute-start.26 = (bf16[96,896]{1,0:T(8,128)(2,1)S(1)}, bf16[96,896]{1,0:T(8,128)(2,1)S(1)}, u32[]{:S(2)}, u32[]{:S(2)}) collective-permute-start(bf16[96,896]{1,0:T(8,128)(2,1)S(1)} %get-tuple-element.90), channel_id=1, source_target_pairs={{0,22},{2,20},{4,18},{6,16},{8,30},{10,28},{12,26},{14,24},{16,6},... | collective-permute-start | bytes 516104 | tf_op jit(solution)/shard_map/ppermute | solution.py:334
  53.6 12.5 %collective-permute-start.25 = (bf16[96,896]{1,0:T(8,128)(2,1)S(1)}, bf16[96,896]{1,0:T(8,128)(2,1)S(1)}, u32[]{:S(2)}, u32[]{:S(2)}) collective-permute-start(bf16[96,896]{1,0:T(8,128)(2,1)S(1)} %get-tuple-element.88), channel_id=1, source_target_pairs={{0,14},{2,12},{4,10},{6,8},{8,6},{10,4},{12,2},{14,0},{16,30},{18,... | collective-permute-start | bytes 516104 | tf_op jit(solution)/shard_map/ppermute | solution.py:334
  57.3 10.7 %collective-permute-start.18 = (f32[96,256]{1,0:T(8,128)S(1)}, f32[96,256]{1,0:T(8,128)S(1)}, u32[]{:S(2)}, u32[]{:S(2)}) collective-permute-start(f32[96,256]{1,0:T(8,128)S(1)} %collective-permute-done.12.refs_5_), channel_id=1, source_target_pairs={{0,8},{2,10},{8,16},{10,18},{16,24},{18,26},{24,28},{26,30},{28,20... | collective-permute-start | bytes 294920 | tf_op jit(solution)/shard_map/ppermute | solution.py:349
  57.5 15.4 %collective-permute-start.27 = (bf16[96,896]{1,0:T(8,128)(2,1)S(1)}, bf16[96,896]{1,0:T(8,128)(2,1)S(1)}, u32[]{:S(2)}, u32[]{:S(2)}) collective-permute-start(bf16[96,896]{1,0:T(8,128)(2,1)S(1)} %get-tuple-element.92), channel_id=1, source_target_pairs={{0,24},{2,26},{4,28},{6,30},{8,16},{10,18},{12,20},{14,22},{16,8},... | collective-permute-start | bytes 516104 | tf_op jit(solution)/shard_map/ppermute | solution.py:334
  60.1 14.8 %collective-permute-start.24 = (bf16[96,896]{1,0:T(8,128)(2,1)S(1)}, bf16[96,896]{1,0:T(8,128)(2,1)S(1)}, u32[]{:S(2)}, u32[]{:S(2)}) collective-permute-start(bf16[96,896]{1,0:T(8,128)(2,1)S(1)} %get-tuple-element.86), channel_id=1, source_target_pairs={{0,6},{2,4},{4,2},{6,0},{8,14},{10,12},{12,10},{14,8},{16,22},{18,... | collective-permute-start | bytes 516104 | tf_op jit(solution)/shard_map/ppermute | solution.py:334
  68.6 24.8 %collective-permute-start.23 = (bf16[96,896]{1,0:T(8,128)(2,1)S(1)}, bf16[96,896]{1,0:T(8,128)(2,1)S(1)}, u32[]{:S(2)}, u32[]{:S(2)}) collective-permute-start(bf16[96,896]{1,0:T(8,128)(2,1)S(1)} %get-tuple-element.84), channel_id=1, source_target_pairs={{0,4},{2,6},{4,0},{6,2},{8,12},{10,14},{12,8},{14,10},{16,20},{18,... | collective-permute-start | bytes 516104 | tf_op jit(solution)/shard_map/ppermute | solution.py:334
  72.6 20.8 %collective-permute-start.22 = (bf16[96,896]{1,0:T(8,128)(2,1)S(1)}, bf16[96,896]{1,0:T(8,128)(2,1)S(1)}, u32[]{:S(2)}, u32[]{:S(2)}) collective-permute-start(bf16[96,896]{1,0:T(8,128)(2,1)S(1)} %get-tuple-element.82), channel_id=1, source_target_pairs={{0,2},{2,0},{4,6},{6,4},{8,10},{10,8},{12,14},{14,12},{16,18},{18,... | collective-permute-start | bytes 516104 | tf_op jit(solution)/shard_map/ppermute | solution.py:334
  72.9 20.5 %collective-permute-start.30 = (bf16[96,896]{1,0:T(8,128)(2,1)S(1)}, bf16[96,896]{1,0:T(8,128)(2,1)S(1)}, u32[]{:S(2)}, u32[]{:S(2)}) collective-permute-start(bf16[96,896]{1,0:T(8,128)(2,1)S(1)} %get-tuple-element.98), channel_id=1, source_target_pairs={{0,30},{2,28},{4,26},{6,24},{8,22},{10,20},{12,18},{14,16},{16,14}... | collective-permute-start | bytes 516104 | tf_op jit(solution)/shard_map/ppermute | solution.py:334
  74.9 18.5 %collective-permute-start.29 = (bf16[96,896]{1,0:T(8,128)(2,1)S(1)}, bf16[96,896]{1,0:T(8,128)(2,1)S(1)}, u32[]{:S(2)}, u32[]{:S(2)}) collective-permute-start(bf16[96,896]{1,0:T(8,128)(2,1)S(1)} %get-tuple-element.96), channel_id=1, source_target_pairs={{0,28},{2,30},{4,24},{6,26},{8,20},{10,22},{12,16},{14,18},{16,12}... | collective-permute-start | bytes 516104 | tf_op jit(solution)/shard_map/ppermute | solution.py:334
  77.2 16.3 %collective-permute-start.28 = (bf16[96,896]{1,0:T(8,128)(2,1)S(1)}, bf16[96,896]{1,0:T(8,128)(2,1)S(1)}, u32[]{:S(2)}, u32[]{:S(2)}) collective-permute-start(bf16[96,896]{1,0:T(8,128)(2,1)S(1)} %get-tuple-element.94), channel_id=1, source_target_pairs={{0,26},{2,24},{4,30},{6,28},{8,18},{10,16},{12,22},{14,20},{16,10}... | collective-permute-start | bytes 516104 | tf_op jit(solution)/shard_map/ppermute | solution.py:334
  96.0 95.6 %all-gather.3.cloned.1.call-start = ((), (), s32[]{:S(2)}) async-start(), calls=%async_computation | async-start | bytes 1769472 | tf_op jit(solution)/shard_map/all_gather | solution.py:431
  146.4 10.0 %collective-permute-start.38 = (bf16[4096,256]{1,0:T(8,128)(2,1)}, bf16[4096,256]{1,0:T(8,128)(2,1)S(1)}, u32[]{:S(2)}, u32[]{:S(2)}) collective-permute-start(bf16[4096,256]{1,0:T(8,128)(2,1)} %all-gather.5.cloned.1.call-done.refs_0_), channel_id=1, source_target_pairs={{0,2},{2,0},{4,6},{6,4},{8,10},{10,8},{12,14},{14,12},{16,18},{18,... | collective-permute-start | bytes 6291464 | tf_op jit(solution)/shard_map/ppermute | solution.py:433
  (27 other events, 196.0 us)
Sparse Core Ops, SparseCore 0:
  96.1 50.2 all-gather.4
  148.6 42.9 all-gather.2

commit v9 on v8

--- a/solution.py
+++ b/solution.py
@@ -118,8 +118,9 @@
     return lax.dot_general(a, b, (dims, ((), ())), precision=FULL, preferred_element_type=F32)
 
 
-def factor_kernel(count, ids_ref, *refs):
-    pieces, (ortho_t_ref, here_ref, whole_ref, work_ref) = refs[:count], refs[count:]
+def factor_kernel(count, ids_ref, base_ref, *refs):
+    pieces, (ortho_t_ref, here_ref, whole_ref, work_ref, corner_ref) = refs[:count], refs[count:]
+    corner_ref[...] = base_ref[:SUBLANES, :LANES]
     rows, rank = pieces[0].shape
     for n, piece in enumerate(pieces):
         whole_ref[pl.ds(pl.multiple_of(ids_ref[n] * rows, SUBLANES), rows), :] = piece[...]
@@ -153,69 +154,71 @@
         ).astype(BF16)
 
 
-def factor_call(ids, pieces):
+def factor_call(ids, base, pieces):
     count = len(pieces)
     rows, rank = pieces[0].shape
     total = count * rows
     vmem = pl.BlockSpec(memory_space=pltpu.VMEM)
     return pl.pallas_call(
         functools.partial(factor_kernel, count),
-        in_specs=[pl.BlockSpec(memory_space=pltpu.SMEM)] + [vmem] * count,
+        in_specs=[pl.BlockSpec(memory_space=pltpu.SMEM)] + [vmem] * (1 + count),
         out_specs=[vmem, vmem],
         out_shape=[
             jax.ShapeDtypeStruct((rank, total), BF16),
             jax.ShapeDtypeStruct((rows, rank), BF16),
         ],
-        scratch_shapes=[pltpu.VMEM((total, rank), F32), pltpu.VMEM((rank, 2 * rank), F32)],
+        scratch_shapes=[
+            pltpu.VMEM((total, rank), F32),
+            pltpu.VMEM((rank, 2 * rank), F32),
+            pltpu.VMEM((SUBLANES, LANES), F32),
+        ],
         compiler_params=params(24),
         cost_estimate=cost(40 * total * rank * rank, total * rank * 6),
         name="factor",
-    )(ids, *pieces)
+    )(ids, base, *pieces)
 
 
 def back_kernel(pieces, ids_ref, base_ref, ortho_t_ref, *refs):
-    columns, (colsq_ref, *part_refs), whole_ref = refs[:pieces], refs[pieces:-1], refs[-1]
+    columns, (colsq_ref, back_ref, whole_ref, corner_ref) = refs[:pieces], refs[pieces:]
+    corner_ref[...] = base_ref[:SUBLANES, :LANES]
     rows = columns[0].shape[0]
     for n, piece in enumerate(columns):
         whole_ref[pl.ds(pl.multiple_of(ids_ref[n] * rows, 16), rows), :] = piece[...]
     back_t = jnp.dot(ortho_t_ref[...], whole_ref[...], preferred_element_type=F32)
     back = back_t.T.astype(BF16)
-    start = 0
-    for part_ref in part_refs:
-        stop = start + part_ref.shape[0]
-        part_ref[...] = back[start:stop]
-        start = stop
+    back_ref[...] = back
     wide = back.astype(F32)
     colsq_ref[...] = jnp.sum(wide * wide, axis=0, keepdims=True)
 
 
-def back_call(ids, base, ortho_t, columns, parts):
+def back_call(ids, base, ortho_t, columns):
     rank, total = ortho_t.shape
     share = columns[0].shape[1]
     vmem = pl.BlockSpec(memory_space=pltpu.VMEM)
     return pl.pallas_call(
         functools.partial(back_kernel, len(columns)),
         in_specs=[pl.BlockSpec(memory_space=pltpu.SMEM)] + [vmem] * (2 + len(columns)),
-        out_specs=[vmem] * (1 + len(parts)),
-        out_shape=[jax.ShapeDtypeStruct((1, rank), F32)]
-        + [jax.ShapeDtypeStruct((part, rank), BF16) for part in parts],
-        scratch_shapes=[pltpu.VMEM((total, share), BF16)],
+        out_specs=[vmem] * 2,
+        out_shape=[
+            jax.ShapeDtypeStruct((1, rank), F32),
+            jax.ShapeDtypeStruct((share, rank), BF16),
+        ],
+        scratch_shapes=[pltpu.VMEM((total, share), BF16), pltpu.VMEM((SUBLANES, LANES), F32)],
         compiler_params=params(24),
         cost_estimate=cost(2 * rank * total * share, total * share * 2),
         name="back",
     )(ids, base, ortho_t, *columns)
 
 
-def output_kernel(share, first, factor, ids_ref, base_ref, ortho_ref, colsq_ref, *refs):
-    piece_ref, *_, nm_ref, nb_ref, up_ref, nm_tile, nb_tile, up_tile, sems = refs
-    count, full = nm_tile.shape[0], nm_tile.shape[2]
-    cols = nm_ref.shape[1]
+def output_kernel(places, factor, ids_ref, base_ref, ortho_ref, colsq_ref, *refs):
+    *pieces, nm_ref, nb_ref, up_ref, nm_tile, nb_tile, up_tile, sems = refs
+    count, share, cols = nm_tile.shape[0], nm_tile.shape[2], nm_ref.shape[1]
     scale = lax.rsqrt(colsq_ref[...] + 1e-06)
     ortho = ortho_ref[...]
     over = (((1,), (1,)), ((), ()))
 
     def copies(n, width):
-        there = pl.ds(pl.multiple_of(ids_ref[n] * share + first, LANES), width)
+        there = pl.ds(pl.multiple_of(ids_ref[places[n]] * share, LANES), width)
         sides = (
             (nm_tile.at[n, :, :width], nm_ref.at[:, there]),
             (nb_tile.at[n, :width, :], nb_ref.at[there, :]),
@@ -229,8 +232,8 @@
     for n in range(count):
 
         def compute(width):
-            there = pl.ds(pl.multiple_of(ids_ref[n] * share + first, LANES), width)
-            back = piece_ref[n * full : n * full + width, :]
+            there = pl.ds(pl.multiple_of(ids_ref[places[n]] * share, LANES), width)
+            back = pieces[n][:width, :]
             unit = (back.astype(F32) * scale).astype(BF16)
             nb_tile[n, :width, :] = unit
             nm_tile[n, :, :width] = base_ref[:, there] - 0.05 * lax.dot_general(
@@ -242,7 +245,7 @@
             for copy in copies(n, width):
                 copy.start()
 
-        by_width(ids_ref[n], cols, share, first, first + full, compute)
+        by_width(ids_ref[places[n]], cols, share, 0, share, compute)
 
     for n in range(count):
 
@@ -250,19 +253,20 @@
             for copy in copies(n, width):
                 copy.wait()
 
-        by_width(ids_ref[n], cols, share, first, first + full, wait)
-
-
-def output_call(ids, base, ortho, colsq, share, first, blocks, factor, previous):
+        by_width(ids_ref[places[n]], cols, share, 0, share, wait)
+
+
+def output_call(ids, places, blocks, colsq, previous, base, ortho, factor):
     rows, cols = base.shape
-    rank = ortho.shape[1]
-    count = ids.shape[0]
-    width = blocks.shape[0] // count
+    share, rank = blocks[0].shape
+    count = len(blocks)
     previous = previous or ()
     vmem, hbm = pl.BlockSpec(memory_space=pltpu.VMEM), pl.BlockSpec(memory_space=pltpu.HBM)
     return pl.pallas_call(
-        functools.partial(output_kernel, share, first, factor),
-        in_specs=[pl.BlockSpec(memory_space=pltpu.SMEM)] + [vmem] * 4 + [hbm] * len(previous),
+        functools.partial(output_kernel, tuple(places), factor),
+        in_specs=[pl.BlockSpec(memory_space=pltpu.SMEM)]
+        + [vmem] * (3 + count)
+        + [hbm] * len(previous),
         out_specs=[hbm] * 3,
         out_shape=[
             jax.ShapeDtypeStruct((rows, cols), F32),
@@ -270,18 +274,18 @@
             jax.ShapeDtypeStruct((rows, cols), BF16),
         ],
         scratch_shapes=[
-            pltpu.VMEM((count, rows, width), F32),
-            pltpu.VMEM((count, width, rank), BF16),
-            pltpu.VMEM((count, rows, width), BF16),
+            pltpu.VMEM((count, rows, share), F32),
+            pltpu.VMEM((count, share, rank), BF16),
+            pltpu.VMEM((count, rows, share), BF16),
             pltpu.SemaphoreType.DMA((count, 3)),
         ],
-        input_output_aliases={5 + n: n for n in range(len(previous))},
-        compiler_params=params(24),
+        input_output_aliases={4 + count + n: n for n in range(len(previous))},
+        compiler_params=params(16),
         cost_estimate=cost(
-            4 * rows * width * rank * count, count * width * (rows * 10 + rank * 4)
+            4 * rows * share * rank * count, count * share * (rows * 10 + rank * 4)
         ),
         name="outputs",
-    )(ids, base, ortho, colsq, blocks, *previous)
+    )(ids, base, ortho, colsq, *blocks, *previous)
 
 
 def chip_at(position, chips):
@@ -302,7 +306,20 @@
     order = ring_order(count // 2)
     after = dict(zip(order, order[1:] + order[:1]))
     up = [(2 * c + k, 2 * after[c] + k) for c in order for k in (0, 1)]
-    return up, [(b, a) for a, b in up]
+    down = [(b, a) for a, b in up]
+    first = [p for p in up if p[0] % 2 == 0] + [p for p in down if p[0] % 2 == 1]
+    second = [p for p in down if p[0] % 2 == 0] + [p for p in up if p[0] % 2 == 1]
+    return first, second
+
+
+def owners(hops, count):
+    me = lax.axis_index("fsdp")
+    chips, core = count // 2, me % 2
+    hops = hops * (2 * core - 1)
+    place = position_of(me // 2, chips)
+    mine = 2 * chip_at((place + hops) % chips, chips) + core
+    theirs = 2 * chip_at((place - hops) % chips, chips) + 1 - core
+    return jnp.stack([mine, theirs], axis=1).astype(jnp.int32)
 
 
 def swap_pairs(count):
@@ -324,8 +341,7 @@
 def gather_and_exchange(sketch, outgoing, count):
     chips = count // 2
     me = lax.axis_index("fsdp")
-    place, core = position_of(me // 2, chips), me % 2
-    up, down = ring_steps(count)
+    first, second = ring_steps(count)
     columns = {0: outgoing[0]}
 
     def exchange(window, *after):
@@ -346,19 +362,19 @@
         exchange(windows[step], ahead, behind)
         earlier = [lax.ppermute(x, "fsdp", swap) for x in arrived]
         other += earlier
-        ahead = lax.ppermute(ahead, "fsdp", up)
+        ahead = lax.ppermute(ahead, "fsdp", first)
         arrived = [ahead]
-        offsets.append(-step)
+        offsets.append(step)
         if 2 * step < chips:
-            behind = lax.ppermute(behind, "fsdp", down)
+            behind = lax.ppermute(behind, "fsdp", second)
             arrived.append(behind)
-            offsets.append(step)
+            offsets.append(-step)
         held += arrived
     for window in windows[chips // 2 + 1 :]:
         exchange(window, ahead, behind)
     other += [lax.ppermute(x, "fsdp", swap) for x in arrived]
-    chip = chip_at((place + jnp.array(offsets, jnp.int32)) % chips, chips)
-    ids = jnp.concatenate([2 * chip + core, 2 * chip + 1 - core])
+    ids = owners(jnp.array(offsets, jnp.int32), count)
+    ids = jnp.concatenate([ids[:, 0], ids[:, 1]])
     return held + other, ids.astype(jnp.int32), [columns[k] for k in range(count)]
 
 
@@ -408,37 +424,40 @@
         whole = lax.all_gather(lax.psum(sketch, "tp"), "fsdp", axis=0)
         pieces = [lax.dynamic_index_in_dim(whole, (me + n) % count, 0, False) for n in range(count)]
         ids = ((me + jnp.arange(count)) % count).astype(jnp.int32)
-    ortho_t, ortho_here = factor_call(ids, pieces)
-    tiles = share // LANES
-    cuts = [share]
-    if ring and tiles > 1:
-        cuts = [share - tiles // 2 * LANES, tiles // 2 * LANES]
-    part, *back = back_call(partners, base, ortho_t, columns, cuts)
-
-    if ring:
-        groups = [list(range(core, count, 2)) for core in (0, 1)]
-        colsq = part
-        for axis, distances in sum_rounds(count):
-            colsq = sum_round(colsq, axis, distances)
-        chip = 2 * jnp.arange(chips, dtype=jnp.int32)
-        owners = [chip + me % 2, chip + 1 - me % 2]
-    else:
-        colsq = lax.psum(part, ("fsdp", "tp"))
-        owners = [jnp.arange(-(-cols // share), dtype=jnp.int32)]
-    result, first = None, 0
-    for piece in back:
-        if ring:
-            mine = lax.all_gather(piece, "fsdp", axis=0, tiled=True, axis_index_groups=groups)
-            mine = tie(mine, *(result or (colsq,)))
-            gathered = [mine, lax.ppermute(mine, "fsdp", swap_pairs(count))]
-        else:
-            gathered = [lax.all_gather(piece, "fsdp", axis=0, tiled=True)[: owners[0].size * share]]
-        for ids, blocks in zip(owners, gathered):
-            result = output_call(
-                ids, base, ortho_here, colsq, share, first, blocks, factor, result
-            )
-        first += piece.shape[0]
-    return tuple(result)
+    ortho_t, ortho_here = factor_call(ids, base, pieces)
+    part, back = back_call(partners, base, ortho_t, columns)
+    write = functools.partial(output_call, base=base, ortho=ortho_here, factor=factor)
+    if not ring:
+        whole = lax.all_gather(back, "fsdp", axis=0)
+        valid = -(-cols // share)
+        colsq, blocks = lax.psum(part, ("fsdp", "tp")), [whole[n] for n in range(valid)]
+        return tuple(
+            write(jnp.arange(valid, dtype=jnp.int32), range(valid), blocks, colsq, None)
+        )
+
+    turns, swap = ring_steps(count), swap_pairs(count)
+    hops = [0] + [h * sign for h in range(1, chips // 2 + 1) for sign in (1, -1)][: chips - 1]
+    ids = owners(jnp.array(hops, jnp.int32), count)
+    write = functools.partial(write, ids.reshape(-1))
+    rounds = sum_rounds(count)
+    colsq, result, waiting = part, None, ()
+    arrived, blocks, written = {0: back}, [], 0
+    for n in range(chips):
+        block = tie(arrived[n], *waiting)
+        waiting = ()
+        for later in (1, 2) if n == 0 else (n + 2,):
+            if later < chips:
+                arrived[later] = lax.ppermute(block, "fsdp", turns[(later + 1) % 2])
+        blocks += [block, lax.ppermute(block, "fsdp", swap)]
+        for _ in range(2 if n == 0 else 1):
+            if rounds:
+                colsq = sum_round(tie(colsq, block), *rounds.pop(0))
+                waiting = (colsq,)
+        ready = 2 * n if n + 1 < chips else 2 * n + 1
+        if n >= 2 and ready >= written + 3:
+            result = write(range(written, ready), blocks[written:ready], colsq, result)
+            written, waiting = ready, tuple(result)
+    return tuple(write(range(written, 2 * chips), blocks[written:], colsq, result))
 
 
 def solution(mesh):

time: 211 us -> 154 us (0.73)
  waiting for transfers between devices: 92.4 us -> 49.7 us
  between operations: 14.3 us -> 1.07 us
    all_gather x2 -> x0, waiting for transfers between devices: 64 us -> none  [local(): lax.all_gather(piece, 'fsdp', axis=0, tiled=True, axis_index_groups=groups)]
    ppermute x7, waiting for transfers between devices: 6.14 us -> 19.2 us  [sum_round(): terms.append(lax.ppermute(x, axis, [(n, n ^ d) for n in range(size)]))]
    ppermute x9 -> x22, waiting for transfers between devices: 4.3 us -> 15.7 us  [the longest x7 10.1 us: local(): arrived[later] = lax.ppermute(block, 'fsdp', turns[(later + 1) % 2])]
    ppermute x9 -> x22, starting transfers between devices: 7.76 us -> 16.6 us  [the longest x8 7.05 us: local(): blocks += [block, lax.ppermute(block, 'fsdp', swap)]]
    ppermute x7, starting transfers between devices: 10.8 us -> 4.4 us  [sum_round(): terms.append(lax.ppermute(x, axis, [(n, n ^ d) for n in range(size)]))]
    ppermute x15, starting transfers between devices: 29.8 us -> 25.9 us  [exchange(): columns[k] = lax.ppermute(tie(outgoing[k], *after), 'fsdp', pairs)]
    ppermute x15, waiting for transfers between devices: 14.7 us -> 12.3 us  [exchange(): columns[k] = lax.ppermute(tie(outgoing[k], *after), 'fsdp', pairs)]
    ppermute x7, starting transfers between devices: 5.49 us -> 7.74 us  [gather_and_exchange(): earlier = [lax.ppermute(x, 'fsdp', swap) for x in arrived]]
  transfers between devices with their start and end apart: 42 -> 53, of which waited for: 16 -> 17; matrix products, arithmetic and copies ran while one was open for 0% -> 0% of each run, Pallas kernels for 13% -> 18%
where the time goes in v9:
time: 154 us; the launch traced here: 153 us
  starting transfers between devices  55.9 us (36%)
  waiting for transfers between devices  49.7 us (32%)
  Pallas kernels  32 us (21%)
  local copies, waits for them, and re-layouts  9.42 us (6%)
  other arithmetic  4.08 us (3%)
    ppermute x15, starting transfers between devices, exchange(): columns[k] = lax.ppermute(tie(outgoing[k], *after), 'fsdp', pairs)  25.9 us
    ppermute x7, waiting for transfers between devices, sum_round(): terms.append(lax.ppermute(x, axis, [(n, n ^ d) for n in range(size)]))  19.2 us
    pallas_call x1, Pallas kernels, factor_call(): pl.pallas_call(functools.partial(factor_kernel, count), in_specs=[pl.Bloc...  15.4 us
    pallas_call x5, Pallas kernels, output_call(): pl.pallas_call(functools.partial(output_kernel, tuple(places), factor), i...  13.7 us
    ppermute x15, waiting for transfers between devices, exchange(): columns[k] = lax.ppermute(tie(outgoing[k], *after), 'fsdp', pairs)  12.3 us
    ppermute x7, waiting for transfers between devices, local(): arrived[later] = lax.ppermute(block, 'fsdp', turns[(later + 1) % 2])  10.1 us
    unnamed x20, local copies, waits for them, and re-layouts  9.25 us
    ppermute x7, starting transfers between devices, gather_and_exchange(): earlier = [lax.ppermute(x, 'fsdp', swap) for x in arrived]  7.74 us
  transfers between devices with their start and end apart: 53, of which 17 were waited for; matrix products, arithmetic and copies ran while one was open for 0% of the time, Pallas kernels for 18%

profile of v9, /device:TPU:1, one launch (start us, length us, event | category | flops | bytes accessed | tf_op | source)
XLA Modules:
  0.0 153.4 jit_solution(7733707055328821247)
XLA Ops:
  0.7 4.0 %convert_add_fusion.base_ref = f32[96,13824]{1,0:T(8,128)S(1)} fusion(f32[96,13824]{1,0:T(8,128)} %param.5, bf16[96,13824]{1,0:T(8,128)(2,1)} %param.6), kind=kLoop, calls=%fused_computation | loop fusion | flops 2654208 | bytes 13271040 | tf_op jit(solution)/shard_map/add | solution.py:410
  10.3 2.3 %collective-permute-start.3 = (bf16[96,896]{1,0:T(8,128)(2,1)S(1)}, bf16[96,896]{1,0:T(8,128)(2,1)S(1)}, u32[]{:S(2)}, u32[]{:S(2)}) collective-permute-start(bf16[96,896]{1,0:T(8,128)(2,1)S(1)} %get-tuple-element.69), channel_id=1, source_target_pairs={{0,16},{2,18},{4,20},{6,22},{8,24},{10,26},{12,28},{14,30},{16,0},... | collective-permute-start | bytes 516104 | tf_op jit(solution)/shard_map/ppermute | solution.py:350
  13.8 2.6 %collective-permute-done = f32[96,256]{1,0:T(8,128)S(1)} collective-permute-done((f32[96,256]{1,0:T(8,128)S(1)}, f32[96,256]{1,0:T(8,128)S(1)}, u32[]{:S(2)}, u32[]{:S(2)}) %collective-permute-start) | collective-permute-done | bytes 98336 | tf_op jit(solution)/shard_map/ppermute | solution.py:355
  29.5 2.6 %collective-permute-done.8.refs_9_ = bf16[96,896]{1,0:T(8,128)(2,1)S(1)} collective-permute-done((bf16[96,896]{1,0:T(8,128)(2,1)S(1)}, bf16[96,896]{1,0:T(8,128)(2,1)S(1)}, u32[]{:S(2)}, u32[]{:S(2)}) %collective-permute-start.8) | collective-permute-done | bytes 172064 | tf_op jit(solution)/shard_map/ppermute | solution.py:350
  33.1 3.2 %collective-permute-start.14 = (bf16[96,896]{1,0:T(8,128)(2,1)S(1)}, bf16[96,896]{1,0:T(8,128)(2,1)S(1)}, u32[]{:S(2)}, u32[]{:S(2)}) collective-permute-start(bf16[96,896]{1,0:T(8,128)(2,1)S(1)} %get-tuple-element.81), channel_id=1, source_target_pairs={{0,20},{2,22},{4,16},{6,18},{8,28},{10,30},{12,24},{14,26},{16,4},... | collective-permute-start | bytes 516104 | tf_op jit(solution)/shard_map/ppermute | solution.py:350
  40.4 4.1 %collective-permute-done.14.refs_10_ = bf16[96,896]{1,0:T(8,128)(2,1)S(1)} collective-permute-done((bf16[96,896]{1,0:T(8,128)(2,1)S(1)}, bf16[96,896]{1,0:T(8,128)(2,1)S(1)}, u32[]{:S(2)}, u32[]{:S(2)}) %collective-permute-start.14) | collective-permute-done | bytes 172064 | tf_op jit(solution)/shard_map/ppermute | solution.py:350
  44.9 2.8 %collective-permute-start.25 = (bf16[96,896]{1,0:T(8,128)(2,1)S(1)}, bf16[96,896]{1,0:T(8,128)(2,1)S(1)}, u32[]{:S(2)}, u32[]{:S(2)}) collective-permute-start(bf16[96,896]{1,0:T(8,128)(2,1)S(1)} %get-tuple-element.96), channel_id=1, source_target_pairs={{0,14},{2,12},{4,10},{6,8},{8,6},{10,4},{12,2},{14,0},{16,30},{18,... | collective-permute-start | bytes 516104 | tf_op jit(solution)/shard_map/ppermute | solution.py:350
  52.0 3.8 %collective-permute-done.26.refs_11_ = bf16[96,896]{1,0:T(8,128)(2,1)S(1)} collective-permute-done((bf16[96,896]{1,0:T(8,128)(2,1)S(1)}, bf16[96,896]{1,0:T(8,128)(2,1)S(1)}, u32[]{:S(2)}, u32[]{:S(2)}) %collective-permute-start.26) | collective-permute-done | bytes 172064 | tf_op jit(solution)/shard_map/ppermute | solution.py:350
  56.4 2.6 %collective-permute-start.20 = (f32[96,256]{1,0:T(8,128)}, f32[96,256]{1,0:T(8,128)S(1)}, u32[]{:S(2)}, u32[]{:S(2)}) collective-permute-start(f32[96,256]{1,0:T(8,128)} %collective-permute-done.13.refs_6_), channel_id=1, source_target_pairs={{0,2},{2,0},{4,6},{6,4},{8,10},{10,8},{12,14},{14,12},{16,18},{18,... | collective-permute-start | bytes 294920 | tf_op jit(solution)/shard_map/ppermute | solution.py:363
  61.7 3.7 %collective-permute-start.30 = (bf16[96,896]{1,0:T(8,128)(2,1)S(1)}, bf16[96,896]{1,0:T(8,128)(2,1)S(1)}, u32[]{:S(2)}, u32[]{:S(2)}) collective-permute-start(bf16[96,896]{1,0:T(8,128)(2,1)S(1)} %get-tuple-element.106), channel_id=1, source_target_pairs={{0,30},{2,28},{4,26},{6,24},{8,22},{10,20},{12,18},{14,16},{16,14}... | collective-permute-start | bytes 516104 | tf_op jit(solution)/shard_map/ppermute | solution.py:350
  65.8 3.7 %collective-permute-start.28 = (bf16[96,896]{1,0:T(8,128)(2,1)S(1)}, bf16[96,896]{1,0:T(8,128)(2,1)S(1)}, u32[]{:S(2)}, u32[]{:S(2)}) collective-permute-start(bf16[96,896]{1,0:T(8,128)(2,1)S(1)} %get-tuple-element.102), channel_id=1, source_target_pairs={{0,26},{2,24},{4,30},{6,28},{8,18},{10,16},{12,22},{14,20},{16,10}... | collective-permute-start | bytes 516104 | tf_op jit(solution)/shard_map/ppermute | solution.py:350
  69.5 2.5 %copy-done.1 = f32[96,13824]{1,0:T(8,128)S(1)} copy-done((f32[96,13824]{1,0:T(8,128)S(1)}, f32[96,13824]{1,0:T(8,128)}, u32[]{:S(2)}) %copy-start.1) | copy-done | bytes 5308440
  73.8 15.4 %factor.1 = (bf16[256,1536]{1,0:T(8,128)(2,1)S(1)}, bf16[96,256]{1,0:T(8,128)(2,1)S(1)}) custom-call(s32[16]{0:T(128)S(1)} %pad_add_fusion.1.ids_ref, f32[96,13824]{1,0:T(8,128)S(1)} %copy-done.1, f32[96,256]{1,0:T(8,128)S(1)} %add.114.refs_0_, f32[96,256]{1,0:T(8,128)S(1)} %collective-permute-done.1.refs_1_, f32[96,256]{1,0:T(8,128)S(1)} %collective-permute-done.2.refs_2_, ...), custom_call_target="tpu_custom_call" | custom-call | flops 4026531840 | bytes 2359296 | tf_op jit(solution)/shard_map/factor/pallas_call | solution.py:162
  101.1 9.0 %collective-permute-done.36 = f32[1,256]{1,0:T(1,128)S(1)} collective-permute-done((f32[1,256]{1,0:T(1,128)S(1)}, f32[1,256]{1,0:T(1,128)S(1)}, u32[]{:S(2)}, u32[]{:S(2)}) %collective-permute-start.36) | collective-permute-done | bytes 1056 | tf_op jit(solution)/shard_map/ppermute | solution.py:393
  110.4 3.0 %collective-permute-done.37 = f32[1,256]{1,0:T(1,128)S(1)} collective-permute-done((f32[1,256]{1,0:T(1,128)S(1)}, f32[1,256]{1,0:T(1,128)S(1)}, u32[]{:S(2)}, u32[]{:S(2)}) %collective-permute-start.37) | collective-permute-done | bytes 1056 | tf_op jit(solution)/shard_map/ppermute | solution.py:393
  113.6 4.0 %collective-permute-done.38 = f32[1,256]{1,0:T(1,128)S(1)} collective-permute-done((f32[1,256]{1,0:T(1,128)S(1)}, f32[1,256]{1,0:T(1,128)S(1)}, u32[]{:S(2)}, u32[]{:S(2)}) %collective-permute-start.38) | collective-permute-done | bytes 1056 | tf_op jit(solution)/shard_map/ppermute | solution.py:393
  118.8 2.5 %copy-done.3 = f32[96,13824]{1,0:T(8,128)S(1)} copy-done((f32[96,13824]{1,0:T(8,128)S(1)}, f32[96,13824]{1,0:T(8,128)}, u32[]{:S(2)}) %copy-start.3) | copy-done | bytes 5308440
  121.3 3.3 %outputs.5 = (f32[96,13824]{1,0:T(8,128)}, bf16[13824,256]{1,0:T(8,128)(2,1)}, bf16[96,13824]{1,0:T(8,128)(2,1)}) custom-call(s32[16]{0:T(128)S(1)} %reshape.9.ids_ref, f32[96,13824]{1,0:T(8,128)S(1)} %copy-done.3, bf16[96,256]{1,0:T(8,128)(2,1)S(1)} %get-tuple-element.85.ortho_ref, f32[1,256]{1,0:T(1,128)S(1)} %add_add_fusion.colsq_ref, ...), custom_call_target="tpu_custom_call" | custom-call | flops 352321536 | bytes 7110656 | tf_op jit(solution)/shard_map/outputs/pallas_call | solution.py:265
  124.6 2.7 %collective-permute-start.45 = (bf16[896,256]{1,0:T(8,128)(2,1)S(1)}, bf16[896,256]{1,0:T(8,128)(2,1)S(1)}, u32[]{:S(2)}, u32[]{:S(2)}) collective-permute-start(bf16[896,256]{1,0:T(8,128)(2,1)S(1)} %collective-permute-done.39.refs_2_), channel_id=1, source_target_pairs={{0,2},{2,0},{4,6},{6,4},{8,10},{10,8},{12,14},{14,12},{16,18},{18,... | collective-permute-start | bytes 1376264 | tf_op jit(solution)/shard_map/ppermute | solution.py:451
  128.8 3.1 %outputs.6 = (f32[96,13824]{1,0:T(8,128)}, bf16[13824,256]{1,0:T(8,128)(2,1)}, bf16[96,13824]{1,0:T(8,128)(2,1)}) custom-call(s32[16]{0:T(128)S(1)} %reshape.9.ids_ref, f32[96,13824]{1,0:T(8,128)S(1)} %copy-done.3, bf16[96,256]{1,0:T(8,128)(2,1)S(1)} %get-tuple-element.85.ortho_ref, ...), custom_call_target="tpu_custom_call", output_to_operand_aliasing={{0}: (8, {}), {1}: (9, {}), {2}: (10, {})} | custom-call | flops 352321536 | bytes 7110656 | tf_op jit(solution)/shard_map/outputs/pallas_call | solution.py:265
  131.9 7.0 %collective-permute-done.42.refs_2_ = bf16[896,256]{1,0:T(8,128)(2,1)S(1)} collective-permute-done((bf16[896,256]{1,0:T(8,128)(2,1)S(1)}, bf16[896,256]{1,0:T(8,128)(2,1)S(1)}, u32[]{:S(2)}, u32[]{:S(2)}) %collective-permute-start.42) | collective-permute-done | bytes 458784 | tf_op jit(solution)/shard_map/ppermute | solution.py:450
  141.9 3.1 %outputs.7 = (f32[96,13824]{1,0:T(8,128)}, bf16[13824,256]{1,0:T(8,128)(2,1)}, bf16[96,13824]{1,0:T(8,128)(2,1)}) custom-call(s32[16]{0:T(128)S(1)} %reshape.9.ids_ref, f32[96,13824]{1,0:T(8,128)S(1)} %copy-done.3, bf16[96,256]{1,0:T(8,128)(2,1)S(1)} %get-tuple-element.85.ortho_ref, ...), custom_call_target="tpu_custom_call", output_to_operand_aliasing={{0}: (8, {}), {1}: (9, {}), {2}: (10, {})} | custom-call | flops 352321536 | bytes 7110656 | tf_op jit(solution)/shard_map/outputs/pallas_call | solution.py:265
  145.0 3.1 %collective-permute-done.46.refs_2_ = bf16[896,256]{1,0:T(8,128)(2,1)S(1)} collective-permute-done((bf16[896,256]{1,0:T(8,128)(2,1)S(1)}, bf16[896,256]{1,0:T(8,128)(2,1)S(1)}, u32[]{:S(2)}, u32[]{:S(2)}) %collective-permute-start.46) | collective-permute-done | bytes 458784 | tf_op jit(solution)/shard_map/ppermute | solution.py:450
  149.0 2.4 %outputs.8 = (f32[96,13824]{1,0:T(8,128)}, bf16[13824,256]{1,0:T(8,128)(2,1)}, bf16[96,13824]{1,0:T(8,128)(2,1)}) custom-call(s32[16]{0:T(128)S(1)} %reshape.9.ids_ref, f32[96,13824]{1,0:T(8,128)S(1)} %copy-done.3, bf16[96,256]{1,0:T(8,128)(2,1)S(1)} %get-tuple-element.85.ortho_ref, ...), custom_call_target="tpu_custom_call", output_to_operand_aliasing={{0}: (7, {}), {1}: (8, {}), {2}: (9, {})} | custom-call | flops 264241152 | bytes 5332992 | tf_op jit(solution)/shard_map/outputs/pallas_call | solution.py:265
  (122 shorter events, 55.7 us)
Async XLA Ops:
  8.1 11.9 %collective-permute-start.4 = (bf16[96,896]{1,0:T(8,128)(2,1)S(1)}, bf16[96,896]{1,0:T(8,128)(2,1)S(1)}, u32[]{:S(2)}, u32[]{:S(2)}) collective-permute-start(bf16[96,896]{1,0:T(8,128)(2,1)S(1)} %get-tuple-element.71), channel_id=1, source_target_pairs={{0,8},{2,10},{4,12},{6,14},{8,0},{10,2},{12,4},{14,6},{16,24},{18,... | collective-permute-start | bytes 516104 | tf_op jit(solution)/shard_map/ppermute | solution.py:350
  10.3 10.4 %collective-permute-start.3 = (bf16[96,896]{1,0:T(8,128)(2,1)S(1)}, bf16[96,896]{1,0:T(8,128)(2,1)S(1)}, u32[]{:S(2)}, u32[]{:S(2)}) collective-permute-start(bf16[96,896]{1,0:T(8,128)(2,1)S(1)} %get-tuple-element.69), channel_id=1, source_target_pairs={{0,16},{2,18},{4,20},{6,22},{8,24},{10,26},{12,28},{14,30},{16,0},... | collective-permute-start | bytes 516104 | tf_op jit(solution)/shard_map/ppermute | solution.py:350
  20.7 11.3 %collective-permute-start.8 = (bf16[96,896]{1,0:T(8,128)(2,1)S(1)}, bf16[96,896]{1,0:T(8,128)(2,1)S(1)}, u32[]{:S(2)}, u32[]{:S(2)}) collective-permute-start(bf16[96,896]{1,0:T(8,128)(2,1)S(1)} %get-tuple-element.75), channel_id=1, source_target_pairs={{0,18},{2,16},{4,22},{6,20},{8,26},{10,24},{12,30},{14,28},{16,2},... | collective-permute-start | bytes 516104 | tf_op jit(solution)/shard_map/ppermute | solution.py:350
  24.5 15.9 %collective-permute-start.15 = (bf16[96,896]{1,0:T(8,128)(2,1)S(1)}, bf16[96,896]{1,0:T(8,128)(2,1)S(1)}, u32[]{:S(2)}, u32[]{:S(2)}) collective-permute-start(bf16[96,896]{1,0:T(8,128)(2,1)S(1)} %get-tuple-element.83), channel_id=1, source_target_pairs={{0,12},{2,14},{4,8},{6,10},{8,4},{10,6},{12,0},{14,2},{16,28},{18,... | collective-permute-start | bytes 516104 | tf_op jit(solution)/shard_map/ppermute | solution.py:350
  26.4 9.9 %collective-permute-start.7 = (f32[96,256]{1,0:T(8,128)S(1)}, f32[96,256]{1,0:T(8,128)}, u32[]{:S(2)}, u32[]{:S(2)}) collective-permute-start(f32[96,256]{1,0:T(8,128)S(1)} %collective-permute-done.2.refs_2_), channel_id=1, source_target_pairs={{8,0},{16,8},{24,16},{28,24},{20,28},{12,20},{4,12},{0,4},{2,10},{... | collective-permute-start | bytes 294920 | tf_op jit(solution)/shard_map/ppermute | solution.py:369
  33.1 11.5 %collective-permute-start.14 = (bf16[96,896]{1,0:T(8,128)(2,1)S(1)}, bf16[96,896]{1,0:T(8,128)(2,1)S(1)}, u32[]{:S(2)}, u32[]{:S(2)}) collective-permute-start(bf16[96,896]{1,0:T(8,128)(2,1)S(1)} %get-tuple-element.81), channel_id=1, source_target_pairs={{0,20},{2,22},{4,16},{6,18},{8,28},{10,30},{12,24},{14,26},{16,4},... | collective-permute-start | bytes 516104 | tf_op jit(solution)/shard_map/ppermute | solution.py:350
  44.6 11.2 %collective-permute-start.26 = (bf16[96,896]{1,0:T(8,128)(2,1)S(1)}, bf16[96,896]{1,0:T(8,128)(2,1)S(1)}, u32[]{:S(2)}, u32[]{:S(2)}) collective-permute-start(bf16[96,896]{1,0:T(8,128)(2,1)S(1)} %get-tuple-element.98), channel_id=1, source_target_pairs={{0,22},{2,20},{4,18},{6,16},{8,30},{10,28},{12,26},{14,24},{16,6},... | collective-permute-start | bytes 516104 | tf_op jit(solution)/shard_map/ppermute | solution.py:350
  44.9 11.5 %collective-permute-start.25 = (bf16[96,896]{1,0:T(8,128)(2,1)S(1)}, bf16[96,896]{1,0:T(8,128)(2,1)S(1)}, u32[]{:S(2)}, u32[]{:S(2)}) collective-permute-start(bf16[96,896]{1,0:T(8,128)(2,1)S(1)} %get-tuple-element.96), channel_id=1, source_target_pairs={{0,14},{2,12},{4,10},{6,8},{8,6},{10,4},{12,2},{14,0},{16,30},{18,... | collective-permute-start | bytes 516104 | tf_op jit(solution)/shard_map/ppermute | solution.py:350
  47.8 13.2 %collective-permute-start.18 = (f32[96,256]{1,0:T(8,128)}, f32[96,256]{1,0:T(8,128)S(1)}, u32[]{:S(2)}, u32[]{:S(2)}) collective-permute-start(f32[96,256]{1,0:T(8,128)} %collective-permute-done.12.refs_5_), channel_id=1, source_target_pairs={{0,8},{8,16},{16,24},{24,28},{28,20},{20,12},{12,4},{4,0},{10,2},{... | collective-permute-start | bytes 294920 | tf_op jit(solution)/shard_map/ppermute | solution.py:365
  48.8 12.8 %collective-permute-start.27 = (bf16[96,896]{1,0:T(8,128)(2,1)S(1)}, bf16[96,896]{1,0:T(8,128)(2,1)S(1)}, u32[]{:S(2)}, u32[]{:S(2)}) collective-permute-start(bf16[96,896]{1,0:T(8,128)(2,1)S(1)} %get-tuple-element.100), channel_id=1, source_target_pairs={{0,24},{2,26},{4,28},{6,30},{8,16},{10,18},{12,20},{14,22},{16,8},... | collective-permute-start | bytes 516104 | tf_op jit(solution)/shard_map/ppermute | solution.py:350
  50.2 15.2 %collective-permute-start.24 = (bf16[96,896]{1,0:T(8,128)(2,1)S(1)}, bf16[96,896]{1,0:T(8,128)(2,1)S(1)}, u32[]{:S(2)}, u32[]{:S(2)}) collective-permute-start(bf16[96,896]{1,0:T(8,128)(2,1)S(1)} %get-tuple-element.94), channel_id=1, source_target_pairs={{0,6},{2,4},{4,2},{6,0},{8,14},{10,12},{12,10},{14,8},{16,22},{18,... | collective-permute-start | bytes 516104 | tf_op jit(solution)/shard_map/ppermute | solution.py:350
  61.1 28.1 %collective-permute-start.23 = (bf16[96,896]{1,0:T(8,128)(2,1)S(1)}, bf16[96,896]{1,0:T(8,128)(2,1)S(1)}, u32[]{:S(2)}, u32[]{:S(2)}) collective-permute-start(bf16[96,896]{1,0:T(8,128)(2,1)S(1)} %get-tuple-element.92), channel_id=1, source_target_pairs={{0,4},{2,6},{4,0},{6,2},{8,12},{10,14},{12,8},{14,10},{16,20},{18,... | collective-permute-start | bytes 516104 | tf_op jit(solution)/shard_map/ppermute | solution.py:350
  61.1 28.1 %collective-permute-start.22 = (bf16[96,896]{1,0:T(8,128)(2,1)S(1)}, bf16[96,896]{1,0:T(8,128)(2,1)S(1)}, u32[]{:S(2)}, u32[]{:S(2)}) collective-permute-start(bf16[96,896]{1,0:T(8,128)(2,1)S(1)} %get-tuple-element.90), channel_id=1, source_target_pairs={{0,2},{2,0},{4,6},{6,4},{8,10},{10,8},{12,14},{14,12},{16,18},{18,... | collective-permute-start | bytes 516104 | tf_op jit(solution)/shard_map/ppermute | solution.py:350
  61.7 27.6 %collective-permute-start.30 = (bf16[96,896]{1,0:T(8,128)(2,1)S(1)}, bf16[96,896]{1,0:T(8,128)(2,1)S(1)}, u32[]{:S(2)}, u32[]{:S(2)}) collective-permute-start(bf16[96,896]{1,0:T(8,128)(2,1)S(1)} %get-tuple-element.106), channel_id=1, source_target_pairs={{0,30},{2,28},{4,26},{6,24},{8,22},{10,20},{12,18},{14,16},{16,14}... | collective-permute-start | bytes 516104 | tf_op jit(solution)/shard_map/ppermute | solution.py:350
  65.4 23.9 %collective-permute-start.29 = (bf16[96,896]{1,0:T(8,128)(2,1)S(1)}, bf16[96,896]{1,0:T(8,128)(2,1)S(1)}, u32[]{:S(2)}, u32[]{:S(2)}) collective-permute-start(bf16[96,896]{1,0:T(8,128)(2,1)S(1)} %get-tuple-element.104), channel_id=1, source_target_pairs={{0,28},{2,30},{4,24},{6,26},{8,20},{10,22},{12,16},{14,18},{16,12}... | collective-permute-start | bytes 516104 | tf_op jit(solution)/shard_map/ppermute | solution.py:350
  65.8 23.4 %collective-permute-start.28 = (bf16[96,896]{1,0:T(8,128)(2,1)S(1)}, bf16[96,896]{1,0:T(8,128)(2,1)S(1)}, u32[]{:S(2)}, u32[]{:S(2)}) collective-permute-start(bf16[96,896]{1,0:T(8,128)(2,1)S(1)} %get-tuple-element.102), channel_id=1, source_target_pairs={{0,26},{2,24},{4,30},{6,28},{8,18},{10,16},{12,22},{14,20},{16,10}... | collective-permute-start | bytes 516104 | tf_op jit(solution)/shard_map/ppermute | solution.py:350
  96.8 22.0 %collective-permute-start.40 = (bf16[896,256]{1,0:T(8,128)(2,1)S(1)}, bf16[896,256]{1,0:T(8,128)(2,1)S(1)}, u32[]{:S(2)}, u32[]{:S(2)}) collective-permute-start(bf16[896,256]{1,0:T(8,128)(2,1)S(1)} %get-tuple-element.108.refs_0_), channel_id=1, source_target_pairs={{0,2},{2,0},{4,6},{6,4},{8,10},{10,8},{12,14},{14,12},{16,18},{18,... | collective-permute-start | bytes 1376264 | tf_op jit(solution)/shard_map/ppermute | solution.py:451
  97.0 20.6 %collective-permute-start.43 = (bf16[896,256]{1,0:T(8,128)(2,1)S(1)}, bf16[896,256]{1,0:T(8,128)(2,1)S(1)}, u32[]{:S(2)}, u32[]{:S(2)}) collective-permute-start(bf16[896,256]{1,0:T(8,128)(2,1)S(1)} %get-tuple-element.108.refs_0_), channel_id=1, source_target_pairs={{8,0},{16,8},{24,16},{28,24},{20,28},{12,20},{4,12},{0,4},{2,10},{... | collective-permute-start | bytes 1376264 | tf_op jit(solution)/shard_map/ppermute | solution.py:450
  99.3 19.5 %collective-permute-start.41 = (bf16[896,256]{1,0:T(8,128)(2,1)S(1)}, bf16[896,256]{1,0:T(8,128)(2,1)S(1)}, u32[]{:S(2)}, u32[]{:S(2)}) collective-permute-start(bf16[896,256]{1,0:T(8,128)(2,1)S(1)} %collective-permute-done.35.refs_2_), channel_id=1, source_target_pairs={{0,2},{2,0},{4,6},{6,4},{8,10},{10,8},{12,14},{14,12},{16,18},{18,... | collective-permute-start | bytes 1376264 | tf_op jit(solution)/shard_map/ppermute | solution.py:451
  99.6 25.0 %collective-permute-start.39 = (bf16[896,256]{1,0:T(8,128)(2,1)S(1)}, bf16[896,256]{1,0:T(8,128)(2,1)S(1)}, u32[]{:S(2)}, u32[]{:S(2)}) collective-permute-start(bf16[896,256]{1,0:T(8,128)(2,1)S(1)} %collective-permute-done.35.refs_2_), channel_id=1, source_target_pairs={{0,8},{8,16},{16,24},{24,28},{28,20},{20,12},{12,4},{4,0},{10,2},{... | collective-permute-start | bytes 1376264 | tf_op jit(solution)/shard_map/ppermute | solution.py:450
  117.6 11.2 %collective-permute-start.44 = (bf16[896,256]{1,0:T(8,128)(2,1)S(1)}, bf16[896,256]{1,0:T(8,128)(2,1)S(1)}, u32[]{:S(2)}, u32[]{:S(2)}) collective-permute-start(bf16[896,256]{1,0:T(8,128)(2,1)S(1)} %collective-permute-done.43.refs_0_), channel_id=1, source_target_pairs={{0,2},{2,0},{4,6},{6,4},{8,10},{10,8},{12,14},{14,12},{16,18},{18,... | collective-permute-start | bytes 1376264 | tf_op jit(solution)/shard_map/ppermute | solution.py:451
  127.3 11.6 %collective-permute-start.42 = (bf16[896,256]{1,0:T(8,128)(2,1)S(1)}, bf16[896,256]{1,0:T(8,128)(2,1)S(1)}, u32[]{:S(2)}, u32[]{:S(2)}) collective-permute-start(bf16[896,256]{1,0:T(8,128)(2,1)S(1)} %collective-permute-done.39.refs_2_), channel_id=1, source_target_pairs={{0,8},{8,16},{16,24},{24,28},{28,20},{20,12},{12,4},{4,0},{10,2},{... | collective-permute-start | bytes 1376264 | tf_op jit(solution)/shard_map/ppermute | solution.py:450
  127.3 13.2 %collective-permute-start.48 = (bf16[896,256]{1,0:T(8,128)(2,1)S(1)}, bf16[896,256]{1,0:T(8,128)(2,1)S(1)}, u32[]{:S(2)}, u32[]{:S(2)}) collective-permute-start(bf16[896,256]{1,0:T(8,128)(2,1)S(1)} %collective-permute-done.47.refs_0_), channel_id=1, source_target_pairs={{0,2},{2,0},{4,6},{6,4},{8,10},{10,8},{12,14},{14,12},{16,18},{18,... | collective-permute-start | bytes 1376264 | tf_op jit(solution)/shard_map/ppermute | solution.py:451
  127.5 13.0 %collective-permute-start.51 = (bf16[896,256]{1,0:T(8,128)(2,1)S(1)}, bf16[896,256]{1,0:T(8,128)(2,1)S(1)}, u32[]{:S(2)}, u32[]{:S(2)}) collective-permute-start(bf16[896,256]{1,0:T(8,128)(2,1)S(1)} %collective-permute-done.47.refs_0_), channel_id=1, source_target_pairs={{8,0},{16,8},{24,16},{28,24},{20,28},{12,20},{4,12},{0,4},{2,10},{... | collective-permute-start | bytes 1376264 | tf_op jit(solution)/shard_map/ppermute | solution.py:450
  (39 other events, 246.6 us)

commit v10 on v9

v10 whole, which is shorter than its diff:
```python
import functools
import math

import jax
import jax.numpy as jnp
from jax import lax
from jax.experimental import pallas as pl
from jax.experimental.pallas import tpu as pltpu
from jax.sharding import PartitionSpec as P

LANES = 128
SUBLANES = 8
PANEL = 64
MIB = 1024 * 1024
FULL = lax.Precision.HIGHEST
F32 = jnp.float32
BF16 = jnp.bfloat16


def cost(flops, nbytes):
    return pl.CostEstimate(flops=flops, bytes_accessed=nbytes, transcendentals=0)


def params(mib):
    return pltpu.CompilerParams(vmem_limit_bytes=mib * MIB)


def by_width(block, cols, share, start, stop, act):
    last = (cols - 1) // share
    width, short = stop - start, max(0, min(cols - last * share, stop) - start)
    if short == width:
        act(width)
        return

    @pl.when(block < last)
    def _():
        act(width)

    if short:

        @pl.when(block == last)
        def _():
            act(short)


def pack_kernel(me_ref, base_ref, near_ref, *far_refs):
    cols = base_ref.shape[1]
    group = near_ref.shape[0]
    share = near_ref.shape[2]
    me = me_ref[0]
    first = me & ~(group - 1)
    near = [(first + n, near_ref.at[n]) for n in range(group)]
    far = [(me ^ (group + n), ref) for n, ref in enumerate(far_refs)]
    for owner, out_ref in near + far:

        def fill(width):
            start = pl.multiple_of(owner * share, LANES)
            out_ref[:, :width] = base_ref[:, pl.ds(start, width)].astype(BF16)
            if width < share:
                out_ref[:, width:] = jnp.zeros((out_ref.shape[0], share - width), BF16)

        by_width(owner, cols, share, 0, share, fill)


def pack_call(me, base, share, count):
    rows, half = base.shape[0], count // 2
    vmem = pl.BlockSpec(memory_space=pltpu.VMEM)
    return pl.pallas_call(
        pack_kernel,
        in_specs=[pl.BlockSpec(memory_space=pltpu.SMEM), vmem],
        out_specs=[vmem] * (1 + half),
        out_shape=[jax.ShapeDtypeStruct((half, rows, share), BF16)]
        + [jax.ShapeDtypeStruct((rows, share), BF16)] * half,
        compiler_params=params(16),
        cost_estimate=cost(0, 6 * rows * share * count),
        name="pack",
    )(me, base)


def spread(x, lane):
    return jnp.broadcast_to(x[:, lane : lane + 1], (x.shape[0], LANES))


def row_of(x, row):
    return jnp.broadcast_to(x[row : row + 1, :], (SUBLANES, LANES))


def eliminate(block):
    sub = lax.broadcasted_iota(jnp.int32, (SUBLANES, LANES), 0)
    groups = PANEL // SUBLANES
    top = [block[SUBLANES * g : SUBLANES * (g + 1)] for g in range(groups)]
    for g in range(groups):
        first = PANEL + SUBLANES * g
        t = top[g]
        cols = [spread(t, first + j) for j in range(SUBLANES)]
        below = [[spread(top[i], first + j) for j in range(SUBLANES)] for i in range(g + 1, groups)]
        pivots = jnp.zeros((SUBLANES, LANES), F32)
        inverse, corner = [], {}
        for j in range(SUBLANES):
            pivot = row_of(cols[j], j)
            pivots = jnp.where(sub == j, pivot, pivots)
            inverse.append(1.0 / pivot)
            factor = jnp.where(sub > j, cols[j] * inverse[j], 0.0)
            t = t - factor * row_of(t, j)
            for k in range(j + 1, SUBLANES):
                corner[j, k] = row_of(cols[k], j)
                cols[k] = cols[k] - factor * corner[j, k]
        lines = [row_of(t, j) for j in range(SUBLANES)]
        for i in range(g + 1, groups):
            entries = below[i - g - 1]
            acc = top[i]
            for j in range(SUBLANES):
                factor = entries[j] * inverse[j]
                acc = acc - factor * lines[j]
                for k in range(j + 1, SUBLANES):
                    entries[k] = entries[k] - factor * corner[j, k]
            top[i] = acc
        top[g] = t * lax.rsqrt(pivots)
    return jnp.concatenate(top, axis=0)[:, :PANEL]


def dot(a, b, dims):
    return lax.dot_general(a, b, (dims, ((), ())), precision=FULL, preferred_element_type=F32)


def factor_kernel(stacks, owner, me_ref, base_ref, *refs):
    stacked, (ortho_t_ref, here_ref, whole_ref, work_ref, corner_ref) = refs[:stacks], refs[stacks:]
    corner_ref[...] = base_ref[:SUBLANES, :LANES]
    rows, rank = here_ref.shape
    total = whole_ref.shape[0]
    pieces = [stack.at[n] for stack in stacked for n in range(stack.shape[0])]
    for n, piece in enumerate(pieces):
        start = pl.multiple_of(owner(me_ref[0], n) * rows, SUBLANES)
        whole_ref[pl.ds(start, rows), :] = piece[...]

    work_ref[:, :rank] = jnp.zeros((rank, rank), F32)
    chunk = 4 * rows

    @pl.loop(0, total // chunk)
    def _(n):
        part = whole_ref[pl.ds(pl.multiple_of(n * chunk, SUBLANES), chunk), :]
        work_ref[:, :rank] += dot(part, part, ((0,), (0,)))

    line = lax.broadcasted_iota(jnp.int32, (rank, rank), 0)
    column = lax.broadcasted_iota(jnp.int32, (rank, rank), 1)
    work_ref[:, rank:] = jnp.where(line == column, 1.0, 0.0).astype(F32)
    eye = jnp.where(line == column, 1.0, 0.0).astype(F32)[:PANEL, :PANEL]
    for start in range(0, rank, PANEL):
        stop = start + PANEL
        diagonal = work_ref[start:stop, start:stop]
        small = eliminate(jnp.concatenate([eye, diagonal], axis=1))
        panel = dot(small, work_ref[start:stop, :], ((1,), (0,)))
        work_ref[start:stop, :] = panel
        if stop < rank:
            work_ref[stop:, :] -= dot(panel[:, stop:rank], panel, ((0,), (0,)))
    inverse = work_ref[:, rank:]
    start = pl.multiple_of(me_ref[0] * rows, SUBLANES)
    here_ref[...] = dot(whole_ref[pl.ds(start, rows), :], inverse, ((1,), (1,))).astype(BF16)
    for n in range(0, total, chunk):
        ortho_t_ref[:, n : n + chunk] = dot(
            inverse, whole_ref[n : n + chunk, :], ((1,), (1,))
        ).astype(BF16)


def factor_call(me, owner, base, stacked):
    _, rows, rank = stacked[0].shape
    total = rows * sum(stack.shape[0] for stack in stacked)
    vmem = pl.BlockSpec(memory_space=pltpu.VMEM)
    return pl.pallas_call(
        functools.partial(factor_kernel, len(stacked), owner),
        in_specs=[pl.BlockSpec(memory_space=pltpu.SMEM)] + [vmem] * (1 + len(stacked)),
        out_specs=[vmem, vmem],
        out_shape=[
            jax.ShapeDtypeStruct((rank, total), BF16),
            jax.ShapeDtypeStruct((rows, rank), BF16),
        ],
        scratch_shapes=[
            pltpu.VMEM((total, rank), F32),
            pltpu.VMEM((rank, 2 * rank), F32),
            pltpu.VMEM((SUBLANES, LANES), F32),
        ],
        compiler_params=params(24),
        cost_estimate=cost(40 * total * rank * rank, total * rank * 6),
        name="factor",
    )(me, base, *stacked)


def back_kernel(me_ref, base_ref, ortho_t_ref, near_ref, *refs):
    *far, colsq_ref, back_ref, whole_ref, corner_ref = refs
    corner_ref[...] = base_ref[:SUBLANES, :LANES]
    group, rows, _ = near_ref.shape
    me = me_ref[0]
    first = me & ~(group - 1) if far else 0
    pieces = [(first + n, near_ref.at[n]) for n in range(group)]
    pieces += [(me ^ (group + n), ref) for n, ref in enumerate(far)]
    for owner, piece in pieces:
        whole_ref[pl.ds(pl.multiple_of(owner * rows, 16), rows), :] = piece[...]
    back_t = jnp.dot(ortho_t_ref[...], whole_ref[...], preferred_element_type=F32)
    back = back_t.T.astype(BF16)
    back_ref[...] = back
    wide = back.astype(F32)
    colsq_ref[...] = jnp.sum(wide * wide, axis=0, keepdims=True)


def back_call(me, base, ortho_t, near, far):
    rank, total = ortho_t.shape
    share = near.shape[2]
    vmem = pl.BlockSpec(memory_space=pltpu.VMEM)
    return pl.pallas_call(
        back_kernel,
        in_specs=[pl.BlockSpec(memory_space=pltpu.SMEM)] + [vmem] * (3 + len(far)),
        out_specs=[vmem] * 2,
        out_shape=[
            jax.ShapeDtypeStruct((1, rank), F32),
            jax.ShapeDtypeStruct((share, rank), BF16),
        ],
        scratch_shapes=[pltpu.VMEM((total, share), BF16), pltpu.VMEM((SUBLANES, LANES), F32)],
        compiler_params=params(24),
        cost_estimate=cost(2 * rank * total * share, total * share * 2),
        name="back",
    )(me, base, ortho_t, near, *far)


def output_kernel(owner, factor, me_ref, base_ref, ortho_ref, colsq_ref, *refs):
    *pieces, nm_ref, nb_ref, up_ref, nm_tile, nb_tile, up_tile, sems = refs
    count, share, cols = nm_tile.shape[0], nm_tile.shape[2], nm_ref.shape[1]
    scale = lax.rsqrt(colsq_ref[...] + 1e-06)
    ortho = ortho_ref[...]
    over = (((1,), (1,)), ((), ()))

    def copies(n, width):
        there = pl.ds(pl.multiple_of(owner(me_ref[0], n) * share, LANES), width)
        sides = (
            (nm_tile.at[n, :, :width], nm_ref.at[:, there]),
            (nb_tile.at[n, :width, :], nb_ref.at[there, :]),
            (up_tile.at[n, :, :width], up_ref.at[:, there]),
        )
        return [
            pltpu.make_async_copy(source, target, sems.at[n, which])
            for which, (source, target) in enumerate(sides)
        ]

    for n in range(count):

        def compute(width):
            there = pl.ds(pl.multiple_of(owner(me_ref[0], n) * share, LANES), width)
            back = pieces[n][:width, :]
            unit = (back.astype(F32) * scale).astype(BF16)
            nb_tile[n, :width, :] = unit
            nm_tile[n, :, :width] = base_ref[:, there] - 0.05 * lax.dot_general(
                ortho, back, over, preferred_element_type=F32
            )
            up_tile[n, :, :width] = (
                factor * lax.dot_general(ortho, unit, over, preferred_element_type=F32)
            ).astype(BF16)
            for copy in copies(n, width):
                copy.start()

        by_width(owner(me_ref[0], n), cols, share, 0, share, compute)

    for n in range(count):

        def wait(width):
            for copy in copies(n, width):
                copy.wait()

        by_width(owner(me_ref[0], n), cols, share, 0, share, wait)


def output_call(owner, blocks, colsq, previous, me, base, ortho, factor):
    rows, cols = base.shape
    share, rank = blocks[0].shape
    count = len(blocks)
    previous = previous or ()
    vmem, hbm = pl.BlockSpec(memory_space=pltpu.VMEM), pl.BlockSpec(memory_space=pltpu.HBM)
    return pl.pallas_call(
        functools.partial(output_kernel, owner, factor),
        in_specs=[pl.BlockSpec(memory_space=pltpu.SMEM)]
        + [vmem] * (3 + count)
        + [hbm] * len(previous),
        out_specs=[hbm] * 3,
        out_shape=[
            jax.ShapeDtypeStruct((rows, cols), F32),
            jax.ShapeDtypeStruct((cols, rank), BF16),
            jax.ShapeDtypeStruct((rows, cols), BF16),
        ],
        scratch_shapes=[
            pltpu.VMEM((count, rows, share), F32),
            pltpu.VMEM((count, share, rank), BF16),
            pltpu.VMEM((count, rows, share), BF16),
            pltpu.SemaphoreType.DMA((count, 3)),
        ],
        input_output_aliases={4 + count + n: n for n in range(len(previous))},
        compiler_params=params(16),
        cost_estimate=cost(
            4 * rows * share * rank * count, count * share * (rows * 10 + rank * 4)
        ),
        name="outputs",
    )(me, base, ortho, colsq, *blocks, *previous)


def ring_order(chips):
    half = chips // 2
    return [2 * q for q in range(half)] + [2 * (chips - 1 - q) + 1 for q in range(half, chips)]


def ring_steps(count):
    order = ring_order(count // 2)
    after = dict(zip(order, order[1:] + order[:1]))
    up = [(2 * c + k, 2 * after[c] + k) for c in order for k in (0, 1)]
    down = [(b, a) for a, b in up]
    first = [p for p in up if p[0] % 2 == 0] + [p for p in down if p[0] % 2 == 1]
    second = [p for p in down if p[0] % 2 == 0] + [p for p in up if p[0] % 2 == 1]
    return first, second


def ring_owner(count, hops, other, me):
    chips = count // 2
    half = chips // 2
    core, chip = me & 1, me >> 1
    place = jnp.where((chip & 1) == 0, chip >> 1, chips - 1 - (chip >> 1))
    forward = hops * (2 * core - 1)
    place = lax.rem(place + chips + (-forward if other else forward), chips)
    chip = jnp.where(place < half, 2 * place, 2 * (chips - 1 - place) + 1)
    return 2 * chip + (1 - core if other else core)


def owner_of(ways):
    return lambda me, n: ways[n](me)


def swap_pairs(count):
    return [(n, n ^ 1) for n in range(count)]


def tie(x, *work):
    return lax.optimization_barrier((x, *work))[0] if work else x


def gather_and_exchange(sketch, near, far, count):
    chips = count // 2
    first, second = ring_steps(count)
    columns = []

    def exchange(*after):
        k = len(columns)
        pairs = [(n, n ^ (chips + k)) for n in range(count)]
        columns.append(lax.ppermute(tie(far[k], *after), "fsdp", pairs))

    exchange(sketch)
    sketch = sketch + lax.ppermute(sketch, "tp", [(0, 1), (1, 0)])
    hops, held = [0], [sketch]
    ahead = behind = sketch
    for step in range(1, chips // 2 + 1):
        work = columns[step - 2 : step - 1] if step > 1 else []
        ahead, behind, *_ = lax.optimization_barrier((ahead, behind, *work))
        exchange(ahead, behind)
        ahead = lax.ppermute(ahead, "fsdp", first)
        held.append(ahead)
        hops.append(step)
        if 2 * step < chips:
            behind = lax.ppermute(behind, "fsdp", second)
            held.append(behind)
            hops.append(-step)
    while len(columns) < chips:
        exchange(ahead, behind)
    groups = [list(range(chips)), list(range(chips, count))]
    near = lax.all_to_all(
        tie(near, ahead, behind), "fsdp", 0, 0, tiled=True, axis_index_groups=groups
    )
    held = jnp.stack(held)
    other = lax.ppermute(held, "fsdp", swap_pairs(count))
    ways = [(h, far) for far in (False, True) for h in hops]
    return [held, other], ways, near, columns


def total_of(x):
    x = x + lax.ppermute(x, "tp", [(0, 1), (1, 0)])
    copies = jnp.broadcast_to(x[None], (lax.axis_size("fsdp"), *x.shape))
    return jnp.sum(lax.all_to_all(copies, "fsdp", 0, 0, tiled=True), axis=0)


def local(momentum, gradient, basis):
    rows, cols = momentum.shape
    rank = basis.shape[1]
    count = lax.axis_size("fsdp")
    tp_count = lax.axis_size("tp")
    chips = count // 2
    share = -(-cols // (count * LANES)) * LANES
    factor = math.sqrt(rows * count * cols * tp_count / rank)
    me = lax.axis_index("fsdp")
    ring = tp_count == 2 and count in (16, 32) and (count - 1) * share < cols

    base = momentum + gradient.astype(F32)
    base_b = base.astype(BF16)
    sketch = jnp.dot(base_b, basis, preferred_element_type=F32)
    base = pltpu.with_memory_space_constraint(base, pltpu.VMEM)
    here = me.reshape(1)
    if ring:
        near, *far = pack_call(here, base, share, count)
        pieces, ways, near, far = gather_and_exchange(sketch, near, far, count)
        owner = owner_of([functools.partial(ring_owner, count, *way) for way in ways])
    else:
        padded = jnp.pad(base_b, ((0, 0), (0, share * count - cols)))
        near = jnp.swapaxes(padded.reshape(rows, count, share), 0, 1)
        near, far = lax.all_to_all(near, "fsdp", 0, 0, tiled=True), []
        whole = lax.all_gather(lax.psum(sketch, "tp"), "fsdp", axis=0)
        pieces, owner = [whole], lambda me, n: n
    ortho_t, ortho_here = factor_call(here, owner, base, pieces)
    part, back = back_call(here, base, ortho_t, near, far)
    write = functools.partial(output_call, me=here, base=base, ortho=ortho_here, factor=factor)
    if not ring:
        whole = lax.all_gather(back, "fsdp", axis=0)
        blocks = [whole[n] for n in range(-(-cols // share))]
        colsq = lax.psum(part, ("fsdp", "tp"))
        return tuple(write(lambda me, n: n, blocks, colsq, None))

    turns, swap = ring_steps(count), swap_pairs(count)
    colsq, result, waiting = part, None, {}
    arrived, blocks, owners, written = {0: back}, [], [], 0
    ready = {chips - 3: 2 * chips - 8, chips - 2: 2 * chips - 4, chips - 1: 2 * chips - 1}
    for n in range(chips):
        block = tie(arrived[n], *waiting.get(n, ()))
        for later in (1, 2) if n == 0 else (n + 2,):
            if later < chips:
                arrived[later] = lax.ppermute(block, "fsdp", turns[(later + 1) % 2])
        blocks += [block, lax.ppermute(block, "fsdp", swap)]
        hops = (n + 1) // 2 if n % 2 else -(n // 2)
        owners += [functools.partial(ring_owner, count, hops, far) for far in (False, True)]
        waiting[n + 2] = (blocks[-1],)
        if n == 0:
            colsq = total_of(part)
        if n == 2:
            waiting[n + 2] += (colsq,)
        if n in ready:
            upto = ready[n]
            result = write(owner_of(owners[written:upto]), blocks[written:upto], colsq, result)
            written, waiting[n + 1] = upto, tuple(result) + waiting.get(n + 1, ())
    return tuple(write(owner_of(owners[written:]), blocks[written:], colsq, result))


def solution(mesh):
    return jax.shard_map(
        local,
        mesh=mesh,
        in_specs=(P("fsdp", "tp"), P("fsdp", "tp"), P("tp", None)),
        out_specs=(P("fsdp", "tp"), P("tp", None), P("fsdp", "tp")),
        check_vma=False,
    )
```

time: 154 us -> 170 us (1.10)
  waiting for transfers between devices: 49.7 us -> 36.4 us
  local copies, waits for them, and re-layouts: 9.42 us -> 21.2 us
  blocking collectives: 0 us -> 10.4 us
  starting transfers between devices: 55.9 us -> 65 us
  Pallas kernels: 32 us -> 29.4 us
    ppermute x30 -> x10, starting transfers between devices: 38.1 us -> 19.5 us  [the longest x8 18.9 us: exchange(): columns.append(lax.ppermute(tie(far[k], *after), 'fsdp', pairs))]
    unnamed x20 -> x42, local copies, waits for them, and re-layouts: 9.25 us -> 21.1 us
    ppermute x30 -> x10, waiting for transfers between devices: 31.5 us -> 19.9 us  [the longest x8 17.3 us: exchange(): columns.append(lax.ppermute(tie(far[k], *after), 'fsdp', pairs))]
    all_to_all x0 -> x1, blocking collectives: none -> 10.4 us  [total_of(): return jnp.sum(lax.all_to_all(copies, 'fsdp', 0, 0, tiled=True), axis=0)]
    ppermute x7, starting transfers between devices: 3.51 us -> 12.9 us  [local(): arrived[later] = lax.ppermute(block, 'fsdp', turns[(later + 1) % 2])]
    ppermute x8, starting transfers between devices: 7.05 us -> 13.8 us  [local(): blocks += [block, lax.ppermute(block, 'fsdp', swap)]]
    all_to_all x0 -> x1, starting transfers between devices: none -> 5.23 us  [gather_and_exchange(): lax.all_to_all(tie(near, ahead, behind), 'fsdp', 0, 0, tiled=True, axis_i...]
    ppermute x3, starting transfers between devices: 1.86 us -> 6.24 us  [gather_and_exchange(): behind = lax.ppermute(behind, 'fsdp', second)]
  transfers between devices with their start and end apart: 53 -> 34, of which waited for: 17 -> 11; matrix products, arithmetic and copies ran while one was open for 0% -> 0% of each run, Pallas kernels for 18% -> 16%
where the time goes in v10:
time: 170 us; the launch traced here: 169 us
  starting transfers between devices  65 us (38%)
  waiting for transfers between devices  36.4 us (21%)
  Pallas kernels  29.4 us (17%)
  local copies, waits for them, and re-layouts  21.2 us (12%)
  blocking collectives  10.4 us (6%)
  other arithmetic  4 us (2%)
    unnamed x42, local copies, waits for them, and re-layouts  21.1 us
    ppermute x8, starting transfers between devices, exchange(): columns.append(lax.ppermute(tie(far[k], *after), 'fsdp', pairs))  18.9 us
    ppermute x8, waiting for transfers between devices, exchange(): columns.append(lax.ppermute(tie(far[k], *after), 'fsdp', pairs))  17.3 us
    pallas_call x1, Pallas kernels, factor_call(): pl.pallas_call(functools.partial(factor_kernel, len(stacked), owner), in_...  14.2 us
    ppermute x8, starting transfers between devices, local(): blocks += [block, lax.ppermute(block, 'fsdp', swap)]  13.8 us
    ppermute x7, starting transfers between devices, local(): arrived[later] = lax.ppermute(block, 'fsdp', turns[(later + 1) % 2])  12.9 us
    pallas_call x4, Pallas kernels, output_call(): pl.pallas_call(functools.partial(output_kernel, owner, factor), in_specs=...  12.2 us
    ppermute x7, waiting for transfers between devices, local(): arrived[later] = lax.ppermute(block, 'fsdp', turns[(later + 1) % 2])  11.5 us
  transfers between devices with their start and end apart: 34, of which 11 were waited for; matrix products, arithmetic and copies ran while one was open for 0% of the time, Pallas kernels for 16%

profile of v10, /device:TPU:1, one launch (start us, length us, event | category | flops | bytes accessed | tf_op | source)
XLA Modules:
  0.0 168.7 jit_solution(3299848718281015088)
XLA Ops:
  0.6 4.0 %convert_add_fusion.base_ref = f32[96,13824]{1,0:T(8,128)S(1)} fusion(f32[96,13824]{1,0:T(8,128)} %param.3, bf16[96,13824]{1,0:T(8,128)(2,1)} %param.4), kind=kLoop, calls=%fused_computation | loop fusion | flops 2654208 | bytes 13271040 | tf_op jit(solution)/shard_map/add | solution.py:394
  10.4 2.5 %copy-done.1 = f32[96,13824]{1,0:T(8,128)S(1)} copy-done((f32[96,13824]{1,0:T(8,128)S(1)}, f32[96,13824]{1,0:T(8,128)}, u32[]{:S(2)}) %copy-start.1) | copy-done | bytes 5308440
  18.4 2.5 %collective-permute-start.6 = (bf16[96,896]{1,0:T(8,128)(2,1)S(1)}, bf16[96,896]{1,0:T(8,128)(2,1)S(1)}, u32[]{:S(2)}, u32[]{:S(2)}) collective-permute-start(bf16[96,896]{1,0:T(8,128)(2,1)S(1)} %get-tuple-element.55), channel_id=1, source_target_pairs={{0,18},{2,16},{4,22},{6,20},{8,26},{10,24},{12,30},{14,28},{16,2},... | collective-permute-start | bytes 516104 | tf_op jit(solution)/shard_map/ppermute | solution.py:348
  20.9 3.5 %collective-permute-done.3.refs_0_ = bf16[96,896]{1,0:T(8,128)(2,1)S(1)} collective-permute-done((bf16[96,896]{1,0:T(8,128)(2,1)S(1)}, bf16[96,896]{1,0:T(8,128)(2,1)S(1)}, u32[]{:S(2)}, u32[]{:S(2)}) %collective-permute-start.3) | collective-permute-done | bytes 172064 | tf_op jit(solution)/shard_map/ppermute | solution.py:348
  25.6 6.0 %collective-permute-start.5 = (f32[96,256]{1,0:T(8,128)S(1)}, f32[96,256]{1,0:T(8,128)S(1)}, u32[]{:S(2)}, u32[]{:S(2)}) collective-permute-start(f32[96,256]{1,0:T(8,128)S(1)} %collective-permute-done.2), channel_id=1, source_target_pairs={{8,0},{16,8},{24,16},{28,24},{20,28},{12,20},{4,12},{0,4},{2,10},{... | collective-permute-start | bytes 294920 | tf_op jit(solution)/shard_map/ppermute | solution.py:362
  31.6 4.3 %collective-permute-start.9 = (bf16[96,896]{1,0:T(8,128)(2,1)S(1)}, bf16[96,896]{1,0:T(8,128)(2,1)S(1)}, u32[]{:S(2)}, u32[]{:S(2)}) collective-permute-start(bf16[96,896]{1,0:T(8,128)(2,1)S(1)} %get-tuple-element.59), channel_id=1, source_target_pairs={{0,20},{2,22},{4,16},{6,18},{8,28},{10,30},{12,24},{14,26},{16,4},... | collective-permute-start | bytes 516104 | tf_op jit(solution)/shard_map/ppermute | solution.py:348
  38.3 8.1 %collective-permute-done.9.refs_2_ = bf16[96,896]{1,0:T(8,128)(2,1)S(1)} collective-permute-done((bf16[96,896]{1,0:T(8,128)(2,1)S(1)}, bf16[96,896]{1,0:T(8,128)(2,1)S(1)}, u32[]{:S(2)}, u32[]{:S(2)}) %collective-permute-start.9) | collective-permute-done | bytes 172064 | tf_op jit(solution)/shard_map/ppermute | solution.py:348
  48.9 3.0 %collective-permute-done.10 = f32[96,256]{1,0:T(8,128)S(1)} collective-permute-done((f32[96,256]{1,0:T(8,128)S(1)}, f32[96,256]{1,0:T(8,128)S(1)}, u32[]{:S(2)}, u32[]{:S(2)}) %collective-permute-start.10) | collective-permute-done | bytes 98336 | tf_op jit(solution)/shard_map/ppermute | solution.py:358
  51.9 5.2 %all-to-all-start = ((bf16[8,96,896]{2,1,0:T(8,128)(2,1)}), bf16[8,96,896]{2,1,0:T(8,128)(2,1)S(1)}, u32[]{:S(2)}, u32[]{:S(2)}) async-start(bf16[8,96,896]{2,1,0:T(8,128)(2,1)} %get-tuple-element.65), calls=%async_computation | async-start | bytes 2752512 | tf_op jit(solution)/shard_map/all_to_all | solution.py:368
  60.2 2.7 %collective-permute-start.13 = (bf16[96,896]{1,0:T(8,128)(2,1)}, bf16[96,896]{1,0:T(8,128)(2,1)S(1)}, u32[]{:S(2)}, u32[]{:S(2)}) collective-permute-start(bf16[96,896]{1,0:T(8,128)(2,1)} %get-tuple-element.69), channel_id=1, source_target_pairs={{0,24},{2,26},{4,28},{6,30},{8,16},{10,18},{12,20},{14,22},{16,8},... | collective-permute-start | bytes 516104 | tf_op jit(solution)/shard_map/ppermute | solution.py:348
  63.5 4.1 %collective-permute-start.15 = (bf16[96,896]{1,0:T(8,128)(2,1)}, bf16[96,896]{1,0:T(8,128)(2,1)S(1)}, u32[]{:S(2)}, u32[]{:S(2)}) collective-permute-start(bf16[96,896]{1,0:T(8,128)(2,1)} %copy-done.16), channel_id=1, source_target_pairs={{0,28},{2,30},{4,24},{6,26},{8,20},{10,22},{12,16},{14,18},{16,12}... | collective-permute-start | bytes 516104 | tf_op jit(solution)/shard_map/ppermute | solution.py:348
  68.2 2.5 %copy-done.2 = f32[96,13824]{1,0:T(8,128)S(1)} copy-done((f32[96,13824]{1,0:T(8,128)S(1)}, f32[96,13824]{1,0:T(8,128)}, u32[]{:S(2)}) %copy-start.2) | copy-done | bytes 5308440
  71.8 14.2 %factor.1 = (bf16[256,1536]{1,0:T(8,128)(2,1)S(1)}, bf16[96,256]{1,0:T(8,128)(2,1)S(1)}) custom-call(s32[1]{0:T(128)} %bitcast.me_ref, f32[96,13824]{1,0:T(8,128)S(1)} %copy-done.2, f32[8,96,256]{2,1,0:T(8,128)S(1)} %copy-done.14, f32[8,96,256]{2,1,0:T(8,128)S(1)} %collective-permute-done.11.refs_1_), custom_call_target="tpu_custom_call" | custom-call | flops 4026531840 | bytes 2359296 | tf_op jit(solution)/shard_map/factor/pallas_call | solution.py:169
  93.9 2.5 %copy-done.3 = f32[96,13824]{1,0:T(8,128)S(1)} copy-done((f32[96,13824]{1,0:T(8,128)S(1)}, f32[96,13824]{1,0:T(8,128)}, u32[]{:S(2)}) %copy-start.3) | copy-done | bytes 5308440
  101.7 6.1 %collective-permute-start.24 = (bf16[896,256]{1,0:T(8,128)(2,1)S(1)}, bf16[896,256]{1,0:T(8,128)(2,1)S(1)}, u32[]{:S(2)}, u32[]{:S(2)}) collective-permute-start(bf16[896,256]{1,0:T(8,128)(2,1)S(1)} %get-tuple-element.77.refs_0_), channel_id=1, source_target_pairs={{8,0},{16,8},{24,16},{28,24},{20,28},{12,20},{4,12},{0,4},{2,10},{... | collective-permute-start | bytes 1376264 | tf_op jit(solution)/shard_map/ppermute | solution.py:426
  108.2 8.1 %collective-permute-done.18.refs_2_ = bf16[896,256]{1,0:T(8,128)(2,1)S(1)} collective-permute-done((bf16[896,256]{1,0:T(8,128)(2,1)S(1)}, bf16[896,256]{1,0:T(8,128)(2,1)S(1)}, u32[]{:S(2)}, u32[]{:S(2)}) %collective-permute-start.18) | collective-permute-done | bytes 458784 | tf_op jit(solution)/shard_map/ppermute | solution.py:426
  117.4 3.5 %collective-permute-start.20 = (bf16[896,256]{1,0:T(8,128)(2,1)S(1)}, bf16[896,256]{1,0:T(8,128)(2,1)S(1)}, u32[]{:S(2)}, u32[]{:S(2)}) collective-permute-start(bf16[896,256]{1,0:T(8,128)(2,1)S(1)} %collective-permute-done.18.refs_2_), channel_id=1, source_target_pairs={{0,2},{2,0},{4,6},{6,4},{8,10},{10,8},{12,14},{14,12},{16,18},{18,... | collective-permute-start | bytes 1376264 | tf_op jit(solution)/shard_map/ppermute | solution.py:427
  122.0 2.8 %collective-permute-done.19.refs_6_ = bf16[896,256]{1,0:T(8,128)(2,1)S(1)} collective-permute-done((bf16[896,256]{1,0:T(8,128)(2,1)S(1)}, bf16[896,256]{1,0:T(8,128)(2,1)S(1)}, u32[]{:S(2)}, u32[]{:S(2)}) %collective-permute-start.19) | collective-permute-done | bytes 458784 | tf_op jit(solution)/shard_map/ppermute | solution.py:426
  127.9 6.4 %collective-permute-start.22 = (bf16[896,256]{1,0:T(8,128)(2,1)S(1)}, bf16[896,256]{1,0:T(8,128)(2,1)}, u32[]{:S(2)}, u32[]{:S(2)}) collective-permute-start(bf16[896,256]{1,0:T(8,128)(2,1)S(1)} %collective-permute-done.19.refs_6_), channel_id=1, source_target_pairs={{0,2},{2,0},{4,6},{6,4},{8,10},{10,8},{12,14},{14,12},{16,18},{18,... | collective-permute-start | bytes 1376264 | tf_op jit(solution)/shard_map/ppermute | solution.py:427
  134.5 2.6 %collective-permute-done.17 = f32[1,256]{1,0:T(1,128)S(1)} collective-permute-done((f32[1,256]{1,0:T(1,128)S(1)}, f32[1,256]{1,0:T(1,128)S(1)}, u32[]{:S(2)}, u32[]{:S(2)}) %collective-permute-start.17) | collective-permute-done | bytes 1056 | tf_op jit(solution)/shard_map/ppermute | solution.py:378
  137.1 10.4 %all_to_all.10 = f32[16,1,256]{2,1,0:T(1,128)S(1)} all-to-all(f32[16,1,256]{2,1,0:T(1,128)S(1)} %broadcast_in_dim.9), channel_id=1, replica_groups=mesh['fsdp'=16,'tp'=2] {'fsdp'}, dimensions={0} | all-to-all | bytes 32768 | tf_op jit(solution)/shard_map/all_to_all | solution.py:380
  149.9 2.5 %copy-done.4 = f32[96,13824]{1,0:T(8,128)S(1)} copy-done((f32[96,13824]{1,0:T(8,128)S(1)}, f32[96,13824]{1,0:T(8,128)}, u32[]{:S(2)}) %copy-start.4) | copy-done | bytes 5308440
  153.4 5.4 %outputs.4 = (f32[96,13824]{1,0:T(8,128)}, bf16[13824,256]{1,0:T(8,128)(2,1)}, bf16[96,13824]{1,0:T(8,128)(2,1)}) custom-call(s32[1]{0:T(128)} %bitcast.me_ref, f32[96,13824]{1,0:T(8,128)S(1)} %copy-done.4, bf16[96,256]{1,0:T(8,128)(2,1)S(1)} %get-tuple-element.61.ortho_ref, f32[1,256]{1,0:T(1,128)S(1)} %bitcast.20, ...), custom_call_target="tpu_custom_call" | custom-call | flops 704643072 | bytes 14221312 | tf_op jit(solution)/shard_map/outputs/pallas_call | solution.py:276
  161.6 3.6 %outputs.5 = (f32[96,13824]{1,0:T(8,128)}, bf16[13824,256]{1,0:T(8,128)(2,1)}, bf16[96,13824]{1,0:T(8,128)(2,1)}) custom-call(s32[1]{0:T(128)} %bitcast.me_ref, f32[96,13824]{1,0:T(8,128)S(1)} %copy-done.4, bf16[96,256]{1,0:T(8,128)(2,1)S(1)} %get-tuple-element.61.ortho_ref, ...), custom_call_target="tpu_custom_call", output_to_operand_aliasing={{0}: (8, {}), {1}: (9, {}), {2}: (10, {})} | custom-call | flops 352321536 | bytes 7110656 | tf_op jit(solution)/shard_map/outputs/pallas_call | solution.py:276
  (101 shorter events, 51.1 us)
Async XLA Ops:
  18.4 17.6 %collective-permute-start.6 = (bf16[96,896]{1,0:T(8,128)(2,1)S(1)}, bf16[96,896]{1,0:T(8,128)(2,1)S(1)}, u32[]{:S(2)}, u32[]{:S(2)}) collective-permute-start(bf16[96,896]{1,0:T(8,128)(2,1)S(1)} %get-tuple-element.55), channel_id=1, source_target_pairs={{0,18},{2,16},{4,22},{6,20},{8,26},{10,24},{12,30},{14,28},{16,2},... | collective-permute-start | bytes 516104 | tf_op jit(solution)/shard_map/ppermute | solution.py:348
  24.4 11.6 %collective-permute-start.4 = (f32[96,256]{1,0:T(8,128)S(1)}, f32[96,256]{1,0:T(8,128)S(1)}, u32[]{:S(2)}, u32[]{:S(2)}) collective-permute-start(f32[96,256]{1,0:T(8,128)S(1)} %collective-permute-done.1), channel_id=1, source_target_pairs={{0,8},{8,16},{16,24},{24,28},{28,20},{20,12},{12,4},{4,0},{10,2},{... | collective-permute-start | bytes 294920 | tf_op jit(solution)/shard_map/ppermute | solution.py:358
  25.6 10.4 %collective-permute-start.5 = (f32[96,256]{1,0:T(8,128)S(1)}, f32[96,256]{1,0:T(8,128)S(1)}, u32[]{:S(2)}, u32[]{:S(2)}) collective-permute-start(f32[96,256]{1,0:T(8,128)S(1)} %collective-permute-done.2), channel_id=1, source_target_pairs={{8,0},{16,8},{24,16},{28,24},{20,28},{12,20},{4,12},{0,4},{2,10},{... | collective-permute-start | bytes 294920 | tf_op jit(solution)/shard_map/ppermute | solution.py:362
  31.6 14.8 %collective-permute-start.9 = (bf16[96,896]{1,0:T(8,128)(2,1)S(1)}, bf16[96,896]{1,0:T(8,128)(2,1)S(1)}, u32[]{:S(2)}, u32[]{:S(2)}) collective-permute-start(bf16[96,896]{1,0:T(8,128)(2,1)S(1)} %get-tuple-element.59), channel_id=1, source_target_pairs={{0,20},{2,22},{4,16},{6,18},{8,28},{10,30},{12,24},{14,26},{16,4},... | collective-permute-start | bytes 516104 | tf_op jit(solution)/shard_map/ppermute | solution.py:348
  36.0 10.4 %collective-permute-start.7 = (f32[96,256]{1,0:T(8,128)S(1)}, f32[96,256]{1,0:T(8,128)S(1)}, u32[]{:S(2)}, u32[]{:S(2)}) collective-permute-start(f32[96,256]{1,0:T(8,128)S(1)} %collective-permute-done.4), channel_id=1, source_target_pairs={{0,8},{8,16},{16,24},{24,28},{28,20},{20,12},{12,4},{4,0},{10,2},{... | collective-permute-start | bytes 294920 | tf_op jit(solution)/shard_map/ppermute | solution.py:358
  38.3 10.1 %collective-permute-start.8 = (f32[96,256]{1,0:T(8,128)S(1)}, f32[96,256]{1,0:T(8,128)S(1)}, u32[]{:S(2)}, u32[]{:S(2)}) collective-permute-start(f32[96,256]{1,0:T(8,128)S(1)} %collective-permute-done.5), channel_id=1, source_target_pairs={{8,0},{16,8},{24,16},{28,24},{20,28},{12,20},{4,12},{0,4},{2,10},{... | collective-permute-start | bytes 294920 | tf_op jit(solution)/shard_map/ppermute | solution.py:362
  51.9 42.0 %all-to-all-start = ((bf16[8,96,896]{2,1,0:T(8,128)(2,1)}), bf16[8,96,896]{2,1,0:T(8,128)(2,1)S(1)}, u32[]{:S(2)}, u32[]{:S(2)}) async-start(bf16[8,96,896]{2,1,0:T(8,128)(2,1)} %get-tuple-element.65), calls=%async_computation | async-start | bytes 2752512 | tf_op jit(solution)/shard_map/all_to_all | solution.py:368
  57.2 10.4 %collective-permute-start.11 = (f32[8,96,256]{2,1,0:T(8,128)S(1)}, f32[8,96,256]{2,1,0:T(8,128)S(1)}, u32[]{:S(2)}, u32[]{:S(2)}) collective-permute-start(f32[8,96,256]{2,1,0:T(8,128)S(1)} %bitcast_dynamic-update-slice_fusion.refs_0_), channel_id=1, source_target_pairs={{0,2},{2,0},{4,6},{6,4},{8,10},{10,8},{12,14},{14,12},{16,18},{18,... | collective-permute-start | bytes 2359304 | tf_op jit(solution)/shard_map/ppermute | solution.py:372
  58.4 27.7 %collective-permute-start.12 = (bf16[96,896]{1,0:T(8,128)(2,1)}, bf16[96,896]{1,0:T(8,128)(2,1)S(1)}, u32[]{:S(2)}, u32[]{:S(2)}) collective-permute-start(bf16[96,896]{1,0:T(8,128)(2,1)} %get-tuple-element.67), channel_id=1, source_target_pairs={{0,22},{2,20},{4,18},{6,16},{8,30},{10,28},{12,26},{14,24},{16,6},... | collective-permute-start | bytes 516104 | tf_op jit(solution)/shard_map/ppermute | solution.py:348
  60.2 25.9 %collective-permute-start.13 = (bf16[96,896]{1,0:T(8,128)(2,1)}, bf16[96,896]{1,0:T(8,128)(2,1)S(1)}, u32[]{:S(2)}, u32[]{:S(2)}) collective-permute-start(bf16[96,896]{1,0:T(8,128)(2,1)} %get-tuple-element.69), channel_id=1, source_target_pairs={{0,24},{2,26},{4,28},{6,30},{8,16},{10,18},{12,20},{14,22},{16,8},... | collective-permute-start | bytes 516104 | tf_op jit(solution)/shard_map/ppermute | solution.py:348
  62.9 24.3 %collective-permute-start.16 = (bf16[96,896]{1,0:T(8,128)(2,1)}, bf16[96,896]{1,0:T(8,128)(2,1)S(1)}, u32[]{:S(2)}, u32[]{:S(2)}) collective-permute-start(bf16[96,896]{1,0:T(8,128)(2,1)} %get-tuple-element.75), channel_id=1, source_target_pairs={{0,30},{2,28},{4,26},{6,24},{8,22},{10,20},{12,18},{14,16},{16,14}... | collective-permute-start | bytes 516104 | tf_op jit(solution)/shard_map/ppermute | solution.py:348
  63.5 26.7 %collective-permute-start.15 = (bf16[96,896]{1,0:T(8,128)(2,1)}, bf16[96,896]{1,0:T(8,128)(2,1)S(1)}, u32[]{:S(2)}, u32[]{:S(2)}) collective-permute-start(bf16[96,896]{1,0:T(8,128)(2,1)} %copy-done.16), channel_id=1, source_target_pairs={{0,28},{2,30},{4,24},{6,26},{8,20},{10,22},{12,16},{14,18},{16,12}... | collective-permute-start | bytes 516104 | tf_op jit(solution)/shard_map/ppermute | solution.py:348
  67.6 25.6 %collective-permute-start.14 = (bf16[96,896]{1,0:T(8,128)(2,1)}, bf16[96,896]{1,0:T(8,128)(2,1)S(1)}, u32[]{:S(2)}, u32[]{:S(2)}) collective-permute-start(bf16[96,896]{1,0:T(8,128)(2,1)} %copy-done.15), channel_id=1, source_target_pairs={{0,26},{2,24},{4,30},{6,28},{8,18},{10,16},{12,22},{14,20},{16,10}... | collective-permute-start | bytes 516104 | tf_op jit(solution)/shard_map/ppermute | solution.py:348
  100.4 15.8 %collective-permute-start.18 = (bf16[896,256]{1,0:T(8,128)(2,1)S(1)}, bf16[896,256]{1,0:T(8,128)(2,1)S(1)}, u32[]{:S(2)}, u32[]{:S(2)}) collective-permute-start(bf16[896,256]{1,0:T(8,128)(2,1)S(1)} %get-tuple-element.77.refs_0_), channel_id=1, source_target_pairs={{0,8},{8,16},{16,24},{24,28},{28,20},{20,12},{12,4},{4,0},{10,2},{... | collective-permute-start | bytes 1376264 | tf_op jit(solution)/shard_map/ppermute | solution.py:426
  101.7 19.3 %collective-permute-start.24 = (bf16[896,256]{1,0:T(8,128)(2,1)S(1)}, bf16[896,256]{1,0:T(8,128)(2,1)S(1)}, u32[]{:S(2)}, u32[]{:S(2)}) collective-permute-start(bf16[896,256]{1,0:T(8,128)(2,1)S(1)} %get-tuple-element.77.refs_0_), channel_id=1, source_target_pairs={{8,0},{16,8},{24,16},{28,24},{20,28},{12,20},{4,12},{0,4},{2,10},{... | collective-permute-start | bytes 1376264 | tf_op jit(solution)/shard_map/ppermute | solution.py:426
  107.7 13.2 %collective-permute-start.25 = (bf16[896,256]{1,0:T(8,128)(2,1)S(1)}, bf16[896,256]{1,0:T(8,128)(2,1)S(1)}, u32[]{:S(2)}, u32[]{:S(2)}) collective-permute-start(bf16[896,256]{1,0:T(8,128)(2,1)S(1)} %get-tuple-element.77.refs_0_), channel_id=1, source_target_pairs={{0,2},{2,0},{4,6},{6,4},{8,10},{10,8},{12,14},{14,12},{16,18},{18,... | collective-permute-start | bytes 1376264 | tf_op jit(solution)/shard_map/ppermute | solution.py:427
  121.0 26.6 %collective-permute-start.27 = (bf16[896,256]{1,0:T(8,128)(2,1)S(1)}, bf16[896,256]{1,0:T(8,128)(2,1)}, u32[]{:S(2)}, u32[]{:S(2)}) collective-permute-start(bf16[896,256]{1,0:T(8,128)(2,1)S(1)} %collective-permute-done.24.refs_4_), channel_id=1, source_target_pairs={{0,2},{2,0},{4,6},{6,4},{8,10},{10,8},{12,14},{14,12},{16,18},{18,... | collective-permute-start | bytes 1376264 | tf_op jit(solution)/shard_map/ppermute | solution.py:427
  121.0 26.5 %collective-permute-start.26 = (bf16[896,256]{1,0:T(8,128)(2,1)S(1)}, bf16[896,256]{1,0:T(8,128)(2,1)S(1)}, u32[]{:S(2)}, u32[]{:S(2)}) collective-permute-start(bf16[896,256]{1,0:T(8,128)(2,1)S(1)} %collective-permute-done.24.refs_4_), channel_id=1, source_target_pairs={{8,0},{16,8},{24,16},{28,24},{20,28},{12,20},{4,12},{0,4},{2,10},{... | collective-permute-start | bytes 1376264 | tf_op jit(solution)/shard_map/ppermute | solution.py:426
  125.6 23.0 %collective-permute-start.21 = (bf16[896,256]{1,0:T(8,128)(2,1)S(1)}, bf16[896,256]{1,0:T(8,128)(2,1)}, u32[]{:S(2)}, u32[]{:S(2)}) collective-permute-start(bf16[896,256]{1,0:T(8,128)(2,1)S(1)} %collective-permute-done.19.refs_6_), channel_id=1, source_target_pairs={{0,8},{8,16},{16,24},{24,28},{28,20},{20,12},{12,4},{4,0},{10,2},{... | collective-permute-start | bytes 1376264 | tf_op jit(solution)/shard_map/ppermute | solution.py:426
  127.9 20.7 %collective-permute-start.22 = (bf16[896,256]{1,0:T(8,128)(2,1)S(1)}, bf16[896,256]{1,0:T(8,128)(2,1)}, u32[]{:S(2)}, u32[]{:S(2)}) collective-permute-start(bf16[896,256]{1,0:T(8,128)(2,1)S(1)} %collective-permute-done.19.refs_6_), channel_id=1, source_target_pairs={{0,2},{2,0},{4,6},{6,4},{8,10},{10,8},{12,14},{14,12},{16,18},{18,... | collective-permute-start | bytes 1376264 | tf_op jit(solution)/shard_map/ppermute | solution.py:427
  147.6 11.3 %collective-permute-start.28 = (bf16[896,256]{1,0:T(8,128)(2,1)S(1)}, bf16[896,256]{1,0:T(8,128)(2,1)S(1)}, u32[]{:S(2)}, u32[]{:S(2)}) collective-permute-start(bf16[896,256]{1,0:T(8,128)(2,1)S(1)} %collective-permute-done.26.refs_0_), channel_id=1, source_target_pairs={{0,2},{2,0},{4,6},{6,4},{8,10},{10,8},{12,14},{14,12},{16,18},{18,... | collective-permute-start | bytes 1376264 | tf_op jit(solution)/shard_map/ppermute | solution.py:427
  148.4 11.1 %collective-permute-start.31 = (bf16[896,256]{1,0:T(8,128)(2,1)S(1)}, bf16[896,256]{1,0:T(8,128)(2,1)S(1)}, u32[]{:S(2)}, u32[]{:S(2)}) collective-permute-start(bf16[896,256]{1,0:T(8,128)(2,1)S(1)} %collective-permute-done.26.refs_0_), channel_id=1, source_target_pairs={{8,0},{16,8},{24,16},{28,24},{20,28},{12,20},{4,12},{0,4},{2,10},{... | collective-permute-start | bytes 1376264 | tf_op jit(solution)/shard_map/ppermute | solution.py:426
  148.6 13.0 %collective-permute-start.29 = (bf16[896,256]{1,0:T(8,128)(2,1)}, bf16[896,256]{1,0:T(8,128)(2,1)S(1)}, u32[]{:S(2)}, u32[]{:S(2)}) collective-permute-start(bf16[896,256]{1,0:T(8,128)(2,1)} %collective-permute-done.21.refs_2_), channel_id=1, source_target_pairs={{0,2},{2,0},{4,6},{6,4},{8,10},{10,8},{12,14},{14,12},{16,18},{18,... | collective-permute-start | bytes 1376264 | tf_op jit(solution)/shard_map/ppermute | solution.py:427
  149.0 16.2 %collective-permute-start.23 = (bf16[896,256]{1,0:T(8,128)(2,1)}, bf16[896,256]{1,0:T(8,128)(2,1)S(1)}, u32[]{:S(2)}, u32[]{:S(2)}) collective-permute-start(bf16[896,256]{1,0:T(8,128)(2,1)} %collective-permute-done.21.refs_2_), channel_id=1, source_target_pairs={{0,8},{8,16},{16,24},{24,28},{28,20},{20,12},{12,4},{4,0},{10,2},{... | collective-permute-start | bytes 1376264 | tf_op jit(solution)/shard_map/ppermute | solution.py:426
  (28 other events, 159.9 us)

commit v11 on v10

--- a/solution.py
+++ b/solution.py
@@ -43,15 +43,12 @@
             act(short)
 
 
-def pack_kernel(me_ref, base_ref, near_ref, *far_refs):
+def pack_kernel(base_ref, *out_refs):
     cols = base_ref.shape[1]
-    group = near_ref.shape[0]
-    share = near_ref.shape[2]
-    me = me_ref[0]
-    first = me & ~(group - 1)
-    near = [(first + n, near_ref.at[n]) for n in range(group)]
-    far = [(me ^ (group + n), ref) for n, ref in enumerate(far_refs)]
-    for owner, out_ref in near + far:
+    share = out_refs[0].shape[1]
+    me = lax.axis_index("fsdp")
+    for n, out_ref in enumerate(out_refs):
+        owner = me ^ n
 
         def fill(width):
             start = pl.multiple_of(owner * share, LANES)
@@ -62,19 +59,18 @@
         by_width(owner, cols, share, 0, share, fill)
 
 
-def pack_call(me, base, share, count):
-    rows, half = base.shape[0], count // 2
+def pack_call(base, share, count):
+    rows = base.shape[0]
     vmem = pl.BlockSpec(memory_space=pltpu.VMEM)
     return pl.pallas_call(
         pack_kernel,
-        in_specs=[pl.BlockSpec(memory_space=pltpu.SMEM), vmem],
-        out_specs=[vmem] * (1 + half),
-        out_shape=[jax.ShapeDtypeStruct((half, rows, share), BF16)]
-        + [jax.ShapeDtypeStruct((rows, share), BF16)] * half,
+        in_specs=[vmem],
+        out_specs=[vmem] * count,
+        out_shape=[jax.ShapeDtypeStruct((rows, share), BF16)] * count,
         compiler_params=params(16),
         cost_estimate=cost(0, 6 * rows * share * count),
         name="pack",
-    )(me, base)
+    )(base)
 
 
 def spread(x, lane):
@@ -123,14 +119,15 @@
     return lax.dot_general(a, b, (dims, ((), ())), precision=FULL, preferred_element_type=F32)
 
 
-def factor_kernel(stacks, owner, me_ref, base_ref, *refs):
+def factor_kernel(stacks, owner, base_ref, *refs):
+    me = lax.axis_index("fsdp")
     stacked, (ortho_t_ref, here_ref, whole_ref, work_ref, corner_ref) = refs[:stacks], refs[stacks:]
     corner_ref[...] = base_ref[:SUBLANES, :LANES]
     rows, rank = here_ref.shape
     total = whole_ref.shape[0]
     pieces = [stack.at[n] for stack in stacked for n in range(stack.shape[0])]
     for n, piece in enumerate(pieces):
-        start = pl.multiple_of(owner(me_ref[0], n) * rows, SUBLANES)
+        start = pl.multiple_of(owner(me, n) * rows, SUBLANES)
         whole_ref[pl.ds(start, rows), :] = piece[...]
 
     work_ref[:, :rank] = jnp.zeros((rank, rank), F32)
@@ -154,7 +151,7 @@
         if stop < rank:
             work_ref[stop:, :] -= dot(panel[:, stop:rank], panel, ((0,), (0,)))
     inverse = work_ref[:, rank:]
-    start = pl.multiple_of(me_ref[0] * rows, SUBLANES)
+    start = pl.multiple_of(me * rows, SUBLANES)
     here_ref[...] = dot(whole_ref[pl.ds(start, rows), :], inverse, ((1,), (1,))).astype(BF16)
     for n in range(0, total, chunk):
         ortho_t_ref[:, n : n + chunk] = dot(
@@ -162,13 +159,13 @@
         ).astype(BF16)
 
 
-def factor_call(me, owner, base, stacked):
+def factor_call(owner, base, stacked):
     _, rows, rank = stacked[0].shape
     total = rows * sum(stack.shape[0] for stack in stacked)
     vmem = pl.BlockSpec(memory_space=pltpu.VMEM)
     return pl.pallas_call(
         functools.partial(factor_kernel, len(stacked), owner),
-        in_specs=[pl.BlockSpec(memory_space=pltpu.SMEM)] + [vmem] * (1 + len(stacked)),
+        in_specs=[vmem] * (1 + len(stacked)),
         out_specs=[vmem, vmem],
         out_shape=[
             jax.ShapeDtypeStruct((rank, total), BF16),
@@ -182,19 +179,16 @@
         compiler_params=params(24),
         cost_estimate=cost(40 * total * rank * rank, total * rank * 6),
         name="factor",
-    )(me, base, *stacked)
-
-
-def back_kernel(me_ref, base_ref, ortho_t_ref, near_ref, *refs):
-    *far, colsq_ref, back_ref, whole_ref, corner_ref = refs
+    )(base, *stacked)
+
+
+def back_kernel(base_ref, ortho_t_ref, *refs):
+    *columns, colsq_ref, back_ref, whole_ref, corner_ref = refs
     corner_ref[...] = base_ref[:SUBLANES, :LANES]
-    group, rows, _ = near_ref.shape
-    me = me_ref[0]
-    first = me & ~(group - 1) if far else 0
-    pieces = [(first + n, near_ref.at[n]) for n in range(group)]
-    pieces += [(me ^ (group + n), ref) for n, ref in enumerate(far)]
-    for owner, piece in pieces:
-        whole_ref[pl.ds(pl.multiple_of(owner * rows, 16), rows), :] = piece[...]
+    me = lax.axis_index("fsdp") if len(columns) > 1 else 0
+    rows = columns[0].shape[0]
+    for n, piece in enumerate(columns):
+        whole_ref[pl.ds(pl.multiple_of((me ^ n) * rows, 16), rows), :] = piece[...]
     back_t = jnp.dot(ortho_t_ref[...], whole_ref[...], preferred_element_type=F32)
     back = back_t.T.astype(BF16)
     back_ref[...] = back
@@ -202,13 +196,13 @@
     colsq_ref[...] = jnp.sum(wide * wide, axis=0, keepdims=True)
 
 
-def back_call(me, base, ortho_t, near, far):
+def back_call(base, ortho_t, columns):
     rank, total = ortho_t.shape
-    share = near.shape[2]
+    share = columns[0].shape[1]
     vmem = pl.BlockSpec(memory_space=pltpu.VMEM)
     return pl.pallas_call(
         back_kernel,
-        in_specs=[pl.BlockSpec(memory_space=pltpu.SMEM)] + [vmem] * (3 + len(far)),
+        in_specs=[vmem] * (2 + len(columns)),
         out_specs=[vmem] * 2,
         out_shape=[
             jax.ShapeDtypeStruct((1, rank), F32),
@@ -218,10 +212,11 @@
         compiler_params=params(24),
         cost_estimate=cost(2 * rank * total * share, total * share * 2),
         name="back",
-    )(me, base, ortho_t, near, *far)
-
-
-def output_kernel(owner, factor, me_ref, base_ref, ortho_ref, colsq_ref, *refs):
+    )(base, ortho_t, *columns)
+
+
+def output_kernel(owner, factor, base_ref, ortho_ref, colsq_ref, *refs):
+    me = lax.axis_index("fsdp")
     *pieces, nm_ref, nb_ref, up_ref, nm_tile, nb_tile, up_tile, sems = refs
     count, share, cols = nm_tile.shape[0], nm_tile.shape[2], nm_ref.shape[1]
     scale = lax.rsqrt(colsq_ref[...] + 1e-06)
@@ -229,7 +224,7 @@
     over = (((1,), (1,)), ((), ()))
 
     def copies(n, width):
-        there = pl.ds(pl.multiple_of(owner(me_ref[0], n) * share, LANES), width)
+        there = pl.ds(pl.multiple_of(owner(me, n) * share, LANES), width)
         sides = (
             (nm_tile.at[n, :, :width], nm_ref.at[:, there]),
             (nb_tile.at[n, :width, :], nb_ref.at[there, :]),
@@ -243,7 +238,7 @@
     for n in range(count):
 
         def compute(width):
-            there = pl.ds(pl.multiple_of(owner(me_ref[0], n) * share, LANES), width)
+            there = pl.ds(pl.multiple_of(owner(me, n) * share, LANES), width)
             back = pieces[n][:width, :]
             unit = (back.astype(F32) * scale).astype(BF16)
             nb_tile[n, :width, :] = unit
@@ -256,7 +251,7 @@
             for copy in copies(n, width):
                 copy.start()
 
-        by_width(owner(me_ref[0], n), cols, share, 0, share, compute)
+        by_width(owner(me, n), cols, share, 0, share, compute)
 
     for n in range(count):
 
@@ -264,10 +259,10 @@
             for copy in copies(n, width):
                 copy.wait()
 
-        by_width(owner(me_ref[0], n), cols, share, 0, share, wait)
-
-
-def output_call(owner, blocks, colsq, previous, me, base, ortho, factor):
+        by_width(owner(me, n), cols, share, 0, share, wait)
+
+
+def output_call(owner, blocks, colsq, previous, base, ortho, factor):
     rows, cols = base.shape
     share, rank = blocks[0].shape
     count = len(blocks)
@@ -275,9 +270,7 @@
     vmem, hbm = pl.BlockSpec(memory_space=pltpu.VMEM), pl.BlockSpec(memory_space=pltpu.HBM)
     return pl.pallas_call(
         functools.partial(output_kernel, owner, factor),
-        in_specs=[pl.BlockSpec(memory_space=pltpu.SMEM)]
-        + [vmem] * (3 + count)
-        + [hbm] * len(previous),
+        in_specs=[vmem] * (3 + count) + [hbm] * len(previous),
         out_specs=[hbm] * 3,
         out_shape=[
             jax.ShapeDtypeStruct((rows, cols), F32),
@@ -290,13 +283,13 @@
             pltpu.VMEM((count, rows, share), BF16),
             pltpu.SemaphoreType.DMA((count, 3)),
         ],
-        input_output_aliases={4 + count + n: n for n in range(len(previous))},
+        input_output_aliases={3 + count + n: n for n in range(len(previous))},
         compiler_params=params(16),
         cost_estimate=cost(
             4 * rows * share * rank * count, count * share * (rows * 10 + rank * 4)
         ),
         name="outputs",
-    )(me, base, ortho, colsq, *blocks, *previous)
+    )(base, ortho, colsq, *blocks, *previous)
 
 
 def ring_order(chips):
@@ -337,24 +330,33 @@
     return lax.optimization_barrier((x, *work))[0] if work else x
 
 
-def gather_and_exchange(sketch, near, far, count):
+def exchange_windows(count):
+    chips, steps = count // 2, count // 4
+    far, near = list(range(chips, count)), list(range(1, chips))
+    each = -(-len(near) // (steps + 1))
+    windows = [far[w : w + 1] + near[w * each : (w + 1) * each] for w in range(steps + 1)]
+    return windows + [far[steps + 1 :]]
+
+
+def gather_and_exchange(sketch, outgoing, count):
     chips = count // 2
     first, second = ring_steps(count)
-    columns = []
-
-    def exchange(*after):
-        k = len(columns)
-        pairs = [(n, n ^ (chips + k)) for n in range(count)]
-        columns.append(lax.ppermute(tie(far[k], *after), "fsdp", pairs))
-
-    exchange(sketch)
+    windows = exchange_windows(count)
+    columns = {0: outgoing[0]}
+
+    def exchange(window, *after):
+        for k in window:
+            pairs = [(n, n ^ k) for n in range(count)]
+            columns[k] = lax.ppermute(tie(outgoing[k], *after), "fsdp", pairs)
+
+    exchange(windows[0], sketch)
     sketch = sketch + lax.ppermute(sketch, "tp", [(0, 1), (1, 0)])
     hops, held = [0], [sketch]
     ahead = behind = sketch
     for step in range(1, chips // 2 + 1):
-        work = columns[step - 2 : step - 1] if step > 1 else []
+        work = [columns[k] for k in windows[step - 2]] if step > 1 else []
         ahead, behind, *_ = lax.optimization_barrier((ahead, behind, *work))
-        exchange(ahead, behind)
+        exchange(windows[step], ahead, behind)
         ahead = lax.ppermute(ahead, "fsdp", first)
         held.append(ahead)
         hops.append(step)
@@ -362,22 +364,29 @@
             behind = lax.ppermute(behind, "fsdp", second)
             held.append(behind)
             hops.append(-step)
-    while len(columns) < chips:
-        exchange(ahead, behind)
-    groups = [list(range(chips)), list(range(chips, count))]
-    near = lax.all_to_all(
-        tie(near, ahead, behind), "fsdp", 0, 0, tiled=True, axis_index_groups=groups
-    )
-    held = jnp.stack(held)
+    exchange(windows[-1], ahead, behind)
+    held = tie(jnp.stack(held), *[columns[k] for k in windows[-3]])
     other = lax.ppermute(held, "fsdp", swap_pairs(count))
     ways = [(h, far) for far in (False, True) for h in hops]
-    return [held, other], ways, near, columns
-
-
-def total_of(x):
-    x = x + lax.ppermute(x, "tp", [(0, 1), (1, 0)])
-    copies = jnp.broadcast_to(x[None], (lax.axis_size("fsdp"), *x.shape))
-    return jnp.sum(lax.all_to_all(copies, "fsdp", 0, 0, tiled=True), axis=0)
+    return [held, other], ways, [columns[k] for k in range(count)]
+
+
+def sum_rounds(count):
+    rounds, bit = [("tp", [1])], 1
+    while bit < count:
+        rounds.append(("fsdp", [bit, 2 * bit, 3 * bit] if 2 * bit < count else [bit]))
+        bit *= 4
+    return rounds
+
+
+def sum_round(x, axis, distances):
+    size = lax.axis_size(axis)
+    terms = [x]
+    for d in distances:
+        terms.append(lax.ppermute(x, axis, [(n, n ^ d) for n in range(size)]))
+    if len(terms) == 2:
+        return terms[0] + terms[1]
+    return (terms[0] + terms[1]) + (terms[2] + terms[3])
 
 
 def local(momentum, gradient, basis):
@@ -388,27 +397,26 @@
     chips = count // 2
     share = -(-cols // (count * LANES)) * LANES
     factor = math.sqrt(rows * count * cols * tp_count / rank)
-    me = lax.axis_index("fsdp")
     ring = tp_count == 2 and count in (16, 32) and (count - 1) * share < cols
 
     base = momentum + gradient.astype(F32)
     base_b = base.astype(BF16)
     sketch = jnp.dot(base_b, basis, preferred_element_type=F32)
     base = pltpu.with_memory_space_constraint(base, pltpu.VMEM)
-    here = me.reshape(1)
     if ring:
-        near, *far = pack_call(here, base, share, count)
-        pieces, ways, near, far = gather_and_exchange(sketch, near, far, count)
+        outgoing = pack_call(base, share, count)
+        pieces, ways, columns = gather_and_exchange(sketch, outgoing, count)
         owner = owner_of([functools.partial(ring_owner, count, *way) for way in ways])
     else:
         padded = jnp.pad(base_b, ((0, 0), (0, share * count - cols)))
-        near = jnp.swapaxes(padded.reshape(rows, count, share), 0, 1)
-        near, far = lax.all_to_all(near, "fsdp", 0, 0, tiled=True), []
-        whole = lax.all_gather(lax.psum(sketch, "tp"), "fsdp", axis=0)
-        pieces, owner = [whole], lambda me, n: n
-    ortho_t, ortho_here = factor_call(here, owner, base, pieces)
-    part, back = back_call(here, base, ortho_t, near, far)
-    write = functools.partial(output_call, me=here, base=base, ortho=ortho_here, factor=factor)
+        columns = jnp.swapaxes(padded.reshape(rows, count, share), 0, 1)
+        columns = lax.all_to_all(columns, "fsdp", 0, 0, tiled=True)
+        columns = [columns.reshape(count * rows, share)]
+        pieces = [lax.all_gather(lax.psum(sketch, "tp"), "fsdp", axis=0)]
+        owner = lambda me, n: n
+    ortho_t, ortho_here = factor_call(owner, base, pieces)
+    part, back = back_call(base, ortho_t, columns)
+    write = functools.partial(output_call, base=base, ortho=ortho_here, factor=factor)
     if not ring:
         whole = lax.all_gather(back, "fsdp", axis=0)
         blocks = [whole[n] for n in range(-(-cols // share))]
@@ -416,10 +424,16 @@
         return tuple(write(lambda me, n: n, blocks, colsq, None))
 
     turns, swap = ring_steps(count), swap_pairs(count)
+    rounds = sum_rounds(count)
     colsq, result, waiting = part, None, {}
     arrived, blocks, owners, written = {0: back}, [], [], 0
     ready = {chips - 3: 2 * chips - 8, chips - 2: 2 * chips - 4, chips - 1: 2 * chips - 1}
     for n in range(chips):
+        if n < 2:
+            for _ in range(2 - n):
+                colsq = sum_round(tie(colsq, arrived[n]), *rounds.pop(0))
+        if n == 1:
+            waiting[1] = (colsq,)
         block = tie(arrived[n], *waiting.get(n, ()))
         for later in (1, 2) if n == 0 else (n + 2,):
             if later < chips:
@@ -427,11 +441,6 @@
         blocks += [block, lax.ppermute(block, "fsdp", swap)]
         hops = (n + 1) // 2 if n % 2 else -(n // 2)
         owners += [functools.partial(ring_owner, count, hops, far) for far in (False, True)]
-        waiting[n + 2] = (blocks[-1],)
-        if n == 0:
-            colsq = total_of(part)
-        if n == 2:
-            waiting[n + 2] += (colsq,)
         if n in ready:
             upto = ready[n]
             result = write(owner_of(owners[written:upto]), blocks[written:upto], colsq, result)

time: 170 us -> 147 us (0.86)
  the two profiles are of different devices: /device:TPU:1 before, /device:TPU:25 now
where the time goes in v11:
time: 147 us
  starting transfers between devices  73.4 us (50%)
  waiting for transfers between devices  39.3 us (27%)
  Pallas kernels  26.4 us (18%)
  other arithmetic  3.98 us (3%)
    ppermute x8, starting transfers between devices, local(): blocks += [block, lax.ppermute(block, 'fsdp', swap)]  30.6 us
    ppermute x15, starting transfers between devices, exchange(): columns[k] = lax.ppermute(tie(outgoing[k], *after), 'fsdp', pairs)  19.8 us
    ppermute x15, waiting for transfers between devices, exchange(): columns[k] = lax.ppermute(tie(outgoing[k], *after), 'fsdp', pairs)  15.4 us
    pallas_call x1, Pallas kernels, factor_call(): pl.pallas_call(functools.partial(factor_kernel, len(stacked), owner), in_...  14.2 us
    pallas_call x4, Pallas kernels, output_call(): pl.pallas_call(functools.partial(output_kernel, owner, factor), in_specs=...  10.4 us
    ppermute x7, starting transfers between devices, local(): arrived[later] = lax.ppermute(block, 'fsdp', turns[(later + 1) % 2])  9.85 us
    ppermute x4, waiting for transfers between devices, gather_and_exchange(): ahead = lax.ppermute(ahead, 'fsdp', first)  6.63 us
    ppermute x7, waiting for transfers between devices, sum_round(): terms.append(lax.ppermute(x, axis, [(n, n ^ d) for n in range(size)]))  6.61 us
  transfers between devices with their start and end apart: 46, of which 16 were waited for; matrix products, arithmetic and copies ran while one was open for 0% of the time, Pallas kernels for 16%

profile of v11, /device:TPU:25, one launch (start us, length us, event | category | flops | bytes accessed | tf_op | source)
XLA Modules:
  0.0 146.7 jit_solution(7392040596105017854)
XLA Ops:
  0.6 4.0 %convert_add_fusion.base_ref = f32[96,13824]{1,0:T(8,128)S(1)} fusion(f32[96,13824]{1,0:T(8,128)} %param.3, bf16[96,13824]{1,0:T(8,128)(2,1)} %param.4), kind=kLoop, calls=%fused_computation | loop fusion | flops 2654208 | bytes 13271040 | tf_op jit(solution)/shard_map/add | solution.py:402
  14.2 3.5 %collective-permute-start.9 = (bf16[96,896]{1,0:T(8,128)(2,1)S(1)}, bf16[96,896]{1,0:T(8,128)(2,1)S(1)}, u32[]{:S(2)}, u32[]{:S(2)}) collective-permute-start(bf16[96,896]{1,0:T(8,128)(2,1)S(1)} %get-tuple-element.75), channel_id=1, source_target_pairs={{0,6},{2,4},{4,2},{6,0},{8,14},{10,12},{12,10},{14,8},{16,22},{18,... | collective-permute-start | bytes 516104 | tf_op jit(solution)/shard_map/ppermute | solution.py:350
  17.7 4.6 %collective-permute-done.3.refs_8_ = bf16[96,896]{1,0:T(8,128)(2,1)S(1)} collective-permute-done((bf16[96,896]{1,0:T(8,128)(2,1)S(1)}, bf16[96,896]{1,0:T(8,128)(2,1)S(1)}, u32[]{:S(2)}, u32[]{:S(2)}) %collective-permute-start.3) | collective-permute-done | bytes 172064 | tf_op jit(solution)/shard_map/ppermute | solution.py:350
  22.4 2.7 %collective-permute-start.6 = (f32[96,256]{1,0:T(8,128)S(1)}, f32[96,256]{1,0:T(8,128)S(1)}, u32[]{:S(2)}, u32[]{:S(2)}) collective-permute-start(f32[96,256]{1,0:T(8,128)S(1)} %collective-permute-done.1), channel_id=1, source_target_pairs={{0,8},{8,16},{16,24},{24,28},{28,20},{20,12},{12,4},{4,0},{10,2},{... | collective-permute-start | bytes 294920 | tf_op jit(solution)/shard_map/ppermute | solution.py:360
  27.7 4.2 %collective-permute-done.8.refs_9_ = bf16[96,896]{1,0:T(8,128)(2,1)S(1)} collective-permute-done((bf16[96,896]{1,0:T(8,128)(2,1)S(1)}, bf16[96,896]{1,0:T(8,128)(2,1)S(1)}, u32[]{:S(2)}, u32[]{:S(2)}) %collective-permute-start.8) | collective-permute-done | bytes 172064 | tf_op jit(solution)/shard_map/ppermute | solution.py:350
  35.5 2.8 %collective-permute-start.18 = (bf16[96,896]{1,0:T(8,128)(2,1)S(1)}, bf16[96,896]{1,0:T(8,128)(2,1)S(1)}, u32[]{:S(2)}, u32[]{:S(2)}) collective-permute-start(bf16[96,896]{1,0:T(8,128)(2,1)S(1)} %get-tuple-element.90), channel_id=1, source_target_pairs={{0,14},{2,12},{4,10},{6,8},{8,6},{10,4},{12,2},{14,0},{16,30},{18,... | collective-permute-start | bytes 516104 | tf_op jit(solution)/shard_map/ppermute | solution.py:350
  38.3 4.0 %collective-permute-done.14.refs_5_ = bf16[96,896]{1,0:T(8,128)(2,1)S(1)} collective-permute-done((bf16[96,896]{1,0:T(8,128)(2,1)S(1)}, bf16[96,896]{1,0:T(8,128)(2,1)S(1)}, u32[]{:S(2)}, u32[]{:S(2)}) %collective-permute-start.14) | collective-permute-done | bytes 172064 | tf_op jit(solution)/shard_map/ppermute | solution.py:350
  43.2 5.3 %collective-permute-done.12 = f32[96,256]{1,0:T(8,128)S(1)} collective-permute-done((f32[96,256]{1,0:T(8,128)S(1)}, f32[96,256]{1,0:T(8,128)S(1)}, u32[]{:S(2)}, u32[]{:S(2)}) %collective-permute-start.12) | collective-permute-done | bytes 98336 | tf_op jit(solution)/shard_map/ppermute | solution.py:364
  48.5 6.6 %collective-permute-done.16 = f32[96,256]{1,0:T(8,128)S(1)} collective-permute-done((f32[96,256]{1,0:T(8,128)S(1)}, f32[96,256]{1,0:T(8,128)S(1)}, u32[]{:S(2)}, u32[]{:S(2)}) %collective-permute-start.16) | collective-permute-done | bytes 98336 | tf_op jit(solution)/shard_map/ppermute | solution.py:360
  56.1 3.2 %collective-permute-start.23 = (bf16[96,896]{1,0:T(8,128)(2,1)S(1)}, bf16[96,896]{1,0:T(8,128)(2,1)S(1)}, u32[]{:S(2)}, u32[]{:S(2)}) collective-permute-start(bf16[96,896]{1,0:T(8,128)(2,1)S(1)} %get-tuple-element.103), channel_id=1, source_target_pairs={{0,30},{2,28},{4,26},{6,24},{8,22},{10,20},{12,18},{14,16},{16,14}... | collective-permute-start | bytes 516104 | tf_op jit(solution)/shard_map/ppermute | solution.py:350
  60.5 2.8 %collective-permute-start.21 = (bf16[96,896]{1,0:T(8,128)(2,1)S(1)}, bf16[96,896]{1,0:T(8,128)(2,1)S(1)}, u32[]{:S(2)}, u32[]{:S(2)}) collective-permute-start(bf16[96,896]{1,0:T(8,128)(2,1)S(1)} %get-tuple-element.99), channel_id=1, source_target_pairs={{0,26},{2,24},{4,30},{6,28},{8,18},{10,16},{12,22},{14,20},{16,10}... | collective-permute-start | bytes 516104 | tf_op jit(solution)/shard_map/ppermute | solution.py:350
  63.3 14.2 %factor.1 = (bf16[256,1536]{1,0:T(8,128)(2,1)S(1)}, bf16[96,256]{1,0:T(8,128)(2,1)S(1)}) custom-call(f32[96,13824]{1,0:T(8,128)S(1)} %convert_add_fusion.base_ref, f32[8,96,256]{2,1,0:T(8,128)S(1)} %bitcast_dynamic-update-slice_fusion.refs_0_, f32[8,96,256]{2,1,0:T(8,128)S(1)} %collective-permute-done.19.refs_1_), custom_call_target="tpu_custom_call" | custom-call | flops 4026531840 | bytes 2359296 | tf_op jit(solution)/shard_map/factor/pallas_call | solution.py:166
  78.9 9.2 %collective-permute-start.28 = (bf16[896,256]{1,0:T(8,128)(2,1)S(1)}, bf16[896,256]{1,0:T(8,128)(2,1)S(1)}, u32[]{:S(2)}, u32[]{:S(2)}) collective-permute-start(bf16[896,256]{1,0:T(8,128)(2,1)S(1)} %get-tuple-element.105.refs_0_), channel_id=1, source_target_pairs={{0,8},{8,16},{16,24},{24,28},{28,20},{20,12},{12,4},{4,0},{10,2},{... | collective-permute-start | bytes 1376264 | tf_op jit(solution)/shard_map/ppermute | solution.py:440
  88.4 2.5 %collective-permute-done.24 = f32[1,256]{1,0:T(1,128)S(1)} collective-permute-done((f32[1,256]{1,0:T(1,128)S(1)}, f32[1,256]{1,0:T(1,128)S(1)}, u32[]{:S(2)}, u32[]{:S(2)}) %collective-permute-start.24) | collective-permute-done | bytes 1056 | tf_op jit(solution)/shard_map/ppermute | solution.py:386
  90.8 1.9 %collective-permute-start.26 = (f32[1,256]{1,0:T(1,128)S(1)}, f32[1,256]{1,0:T(1,128)S(1)}, u32[]{:S(2)}, u32[]{:S(2)}) collective-permute-start(f32[1,256]{1,0:T(1,128)S(1)} %add.29), channel_id=1, source_target_pairs={{0,4},{2,6},{4,0},{6,2},{8,12},{10,14},{12,8},{14,10},{16,20},{18,... | collective-permute-start | bytes 3080 | tf_op jit(solution)/shard_map/ppermute | solution.py:386
  96.7 2.7 %collective-permute-start.31 = (f32[1,256]{1,0:T(1,128)S(1)}, f32[1,256]{1,0:T(1,128)S(1)}, u32[]{:S(2)}, u32[]{:S(2)}) collective-permute-start(f32[1,256]{1,0:T(1,128)S(1)} %add_add_fusion.1), channel_id=1, source_target_pairs={{0,24},{2,26},{4,28},{6,30},{8,16},{10,18},{12,20},{14,22},{16,8},... | collective-permute-start | bytes 3080 | tf_op jit(solution)/shard_map/ppermute | solution.py:386
  100.9 3.3 %collective-permute-start.39 = (bf16[896,256]{1,0:T(8,128)(2,1)S(1)}, bf16[896,256]{1,0:T(8,128)(2,1)S(1)}, u32[]{:S(2)}, u32[]{:S(2)}) collective-permute-start(bf16[896,256]{1,0:T(8,128)(2,1)S(1)} %get-tuple-element.105.refs_0_), channel_id=1, source_target_pairs={{0,2},{2,0},{4,6},{6,4},{8,10},{10,8},{12,14},{14,12},{16,18},{18,... | collective-permute-start | bytes 1376264 | tf_op jit(solution)/shard_map/ppermute | solution.py:441
  104.2 3.4 %collective-permute-done.35.refs_4_ = bf16[896,256]{1,0:T(8,128)(2,1)S(1)} collective-permute-done((bf16[896,256]{1,0:T(8,128)(2,1)S(1)}, bf16[896,256]{1,0:T(8,128)(2,1)S(1)}, u32[]{:S(2)}, u32[]{:S(2)}) %collective-permute-start.35) | collective-permute-done | bytes 458784 | tf_op jit(solution)/shard_map/ppermute | solution.py:440
  107.6 6.5 %collective-permute-start.41 = (bf16[896,256]{1,0:T(8,128)(2,1)S(1)}, bf16[896,256]{1,0:T(8,128)(2,1)S(1)}, u32[]{:S(2)}, u32[]{:S(2)}) collective-permute-start(bf16[896,256]{1,0:T(8,128)(2,1)S(1)} %collective-permute-done.35.refs_4_), channel_id=1, source_target_pairs={{0,2},{2,0},{4,6},{6,4},{8,10},{10,8},{12,14},{14,12},{16,18},{18,... | collective-permute-start | bytes 1376264 | tf_op jit(solution)/shard_map/ppermute | solution.py:441
  117.0 10.3 %collective-permute-start.37 = (bf16[896,256]{1,0:T(8,128)(2,1)S(1)}, bf16[896,256]{1,0:T(8,128)(2,1)S(1)}, u32[]{:S(2)}, u32[]{:S(2)}) collective-permute-start(bf16[896,256]{1,0:T(8,128)(2,1)S(1)} %collective-permute-done.36.refs_0_), channel_id=1, source_target_pairs={{0,2},{2,0},{4,6},{6,4},{8,10},{10,8},{12,14},{14,12},{16,18},{18,... | collective-permute-start | bytes 1376264 | tf_op jit(solution)/shard_map/ppermute | solution.py:441
  127.4 4.4 %outputs.4 = (f32[96,13824]{1,0:T(8,128)}, bf16[13824,256]{1,0:T(8,128)(2,1)}, bf16[96,13824]{1,0:T(8,128)(2,1)}) custom-call(f32[96,13824]{1,0:T(8,128)S(1)} %convert_add_fusion.base_ref, bf16[96,256]{1,0:T(8,128)(2,1)S(1)} %get-tuple-element.92.ortho_ref, f32[1,256]{1,0:T(1,128)S(1)} %add_add_fusion.colsq_ref, ...), custom_call_target="tpu_custom_call" | custom-call | flops 704643072 | bytes 14221312 | tf_op jit(solution)/shard_map/outputs/pallas_call | solution.py:271
  131.8 8.6 %collective-permute-start.45 = (bf16[896,256]{1,0:T(8,128)(2,1)S(1)}, bf16[896,256]{1,0:T(8,128)(2,1)S(1)}, u32[]{:S(2)}, u32[]{:S(2)}) collective-permute-start(bf16[896,256]{1,0:T(8,128)(2,1)S(1)} %collective-permute-done.44.refs_0_), channel_id=1, source_target_pairs={{0,2},{2,0},{4,6},{6,4},{8,10},{10,8},{12,14},{14,12},{16,18},{18,... | collective-permute-start | bytes 1376264 | tf_op jit(solution)/shard_map/ppermute | solution.py:441
  140.4 2.6 %outputs.5 = (f32[96,13824]{1,0:T(8,128)}, bf16[13824,256]{1,0:T(8,128)(2,1)}, bf16[96,13824]{1,0:T(8,128)(2,1)}) custom-call(f32[96,13824]{1,0:T(8,128)S(1)} %convert_add_fusion.base_ref, bf16[96,256]{1,0:T(8,128)(2,1)S(1)} %get-tuple-element.92.ortho_ref, ...), custom_call_target="tpu_custom_call", output_to_operand_aliasing={{0}: (7, {}), {1}: (8, {}), {2}: (9, {})} | custom-call | flops 352321536 | bytes 7110656 | tf_op jit(solution)/shard_map/outputs/pallas_call | solution.py:271
  143.1 2.2 %outputs.6 = (f32[96,13824]{1,0:T(8,128)}, bf16[13824,256]{1,0:T(8,128)(2,1)}, bf16[96,13824]{1,0:T(8,128)(2,1)}) custom-call(f32[96,13824]{1,0:T(8,128)S(1)} %convert_add_fusion.base_ref, bf16[96,256]{1,0:T(8,128)(2,1)S(1)} %get-tuple-element.92.ortho_ref, ...), custom_call_target="tpu_custom_call", output_to_operand_aliasing={{0}: (6, {}), {1}: (7, {}), {2}: (8, {})} | custom-call | flops 264241152 | bytes 5332992 | tf_op jit(solution)/shard_map/outputs/pallas_call | solution.py:271
  (90 shorter events, 30.2 us)
Async XLA Ops:
  11.5 10.9 %collective-permute-start.3 = (bf16[96,896]{1,0:T(8,128)(2,1)S(1)}, bf16[96,896]{1,0:T(8,128)(2,1)S(1)}, u32[]{:S(2)}, u32[]{:S(2)}) collective-permute-start(bf16[96,896]{1,0:T(8,128)(2,1)S(1)} %get-tuple-element.65), channel_id=1, source_target_pairs={{0,16},{2,18},{4,20},{6,22},{8,24},{10,26},{12,28},{14,30},{16,0},... | collective-permute-start | bytes 516104 | tf_op jit(solution)/shard_map/ppermute | solution.py:350
  11.6 10.8 %collective-permute-start.1 = (f32[96,256]{1,0:T(8,128)S(1)}, f32[96,256]{1,0:T(8,128)S(1)}, u32[]{:S(2)}, u32[]{:S(2)}) collective-permute-start(f32[96,256]{1,0:T(8,128)S(1)} %get-tuple-element.63), channel_id=1, source_target_pairs={{0,8},{8,16},{16,24},{24,28},{28,20},{20,12},{12,4},{4,0},{10,2},{... | collective-permute-start | bytes 294920 | tf_op jit(solution)/shard_map/ppermute | solution.py:360
  13.9 11.2 %collective-permute-start.10 = (bf16[96,896]{1,0:T(8,128)(2,1)S(1)}, bf16[96,896]{1,0:T(8,128)(2,1)S(1)}, u32[]{:S(2)}, u32[]{:S(2)}) collective-permute-start(bf16[96,896]{1,0:T(8,128)(2,1)S(1)} %get-tuple-element.77), channel_id=1, source_target_pairs={{0,8},{2,10},{4,12},{6,14},{8,0},{10,2},{12,4},{14,6},{16,24},{18,... | collective-permute-start | bytes 516104 | tf_op jit(solution)/shard_map/ppermute | solution.py:350
  14.2 12.4 %collective-permute-start.9 = (bf16[96,896]{1,0:T(8,128)(2,1)S(1)}, bf16[96,896]{1,0:T(8,128)(2,1)S(1)}, u32[]{:S(2)}, u32[]{:S(2)}) collective-permute-start(bf16[96,896]{1,0:T(8,128)(2,1)S(1)} %get-tuple-element.75), channel_id=1, source_target_pairs={{0,6},{2,4},{4,2},{6,0},{8,14},{10,12},{12,10},{14,8},{16,22},{18,... | collective-permute-start | bytes 516104 | tf_op jit(solution)/shard_map/ppermute | solution.py:350
  26.6 15.8 %collective-permute-start.14 = (bf16[96,896]{1,0:T(8,128)(2,1)S(1)}, bf16[96,896]{1,0:T(8,128)(2,1)S(1)}, u32[]{:S(2)}, u32[]{:S(2)}) collective-permute-start(bf16[96,896]{1,0:T(8,128)(2,1)S(1)} %get-tuple-element.83), channel_id=1, source_target_pairs={{0,10},{2,8},{4,14},{6,12},{8,2},{10,0},{12,6},{14,4},{16,26},{18,... | collective-permute-start | bytes 516104 | tf_op jit(solution)/shard_map/ppermute | solution.py:350
  31.9 11.3 %collective-permute-start.13 = (bf16[96,896]{1,0:T(8,128)(2,1)S(1)}, bf16[96,896]{1,0:T(8,128)(2,1)S(1)}, u32[]{:S(2)}, u32[]{:S(2)}) collective-permute-start(bf16[96,896]{1,0:T(8,128)(2,1)S(1)} %get-tuple-element.81), channel_id=1, source_target_pairs={{0,20},{2,22},{4,16},{6,18},{8,28},{10,30},{12,24},{14,26},{16,4},... | collective-permute-start | bytes 516104 | tf_op jit(solution)/shard_map/ppermute | solution.py:350
  34.3 14.2 %collective-permute-start.12 = (f32[96,256]{1,0:T(8,128)S(1)}, f32[96,256]{1,0:T(8,128)S(1)}, u32[]{:S(2)}, u32[]{:S(2)}) collective-permute-start(f32[96,256]{1,0:T(8,128)S(1)} %collective-permute-done.7), channel_id=1, source_target_pairs={{8,0},{16,8},{24,16},{28,24},{20,28},{12,20},{4,12},{0,4},{2,10},{... | collective-permute-start | bytes 294920 | tf_op jit(solution)/shard_map/ppermute | solution.py:364
  35.5 19.6 %collective-permute-start.18 = (bf16[96,896]{1,0:T(8,128)(2,1)S(1)}, bf16[96,896]{1,0:T(8,128)(2,1)S(1)}, u32[]{:S(2)}, u32[]{:S(2)}) collective-permute-start(bf16[96,896]{1,0:T(8,128)(2,1)S(1)} %get-tuple-element.90), channel_id=1, source_target_pairs={{0,14},{2,12},{4,10},{6,8},{8,6},{10,4},{12,2},{14,0},{16,30},{18,... | collective-permute-start | bytes 516104 | tf_op jit(solution)/shard_map/ppermute | solution.py:350
  42.4 12.8 %collective-permute-start.17 = (bf16[96,896]{1,0:T(8,128)(2,1)S(1)}, bf16[96,896]{1,0:T(8,128)(2,1)S(1)}, u32[]{:S(2)}, u32[]{:S(2)}) collective-permute-start(bf16[96,896]{1,0:T(8,128)(2,1)S(1)} %get-tuple-element.88), channel_id=1, source_target_pairs={{0,22},{2,20},{4,18},{6,16},{8,30},{10,28},{12,26},{14,24},{16,6},... | collective-permute-start | bytes 516104 | tf_op jit(solution)/shard_map/ppermute | solution.py:350
  55.2 22.3 %collective-permute-start.20 = (bf16[96,896]{1,0:T(8,128)(2,1)S(1)}, bf16[96,896]{1,0:T(8,128)(2,1)S(1)}, u32[]{:S(2)}, u32[]{:S(2)}) collective-permute-start(bf16[96,896]{1,0:T(8,128)(2,1)S(1)} %get-tuple-element.97), channel_id=1, source_target_pairs={{0,24},{2,26},{4,28},{6,30},{8,16},{10,18},{12,20},{14,22},{16,8},... | collective-permute-start | bytes 516104 | tf_op jit(solution)/shard_map/ppermute | solution.py:350
  56.1 21.5 %collective-permute-start.23 = (bf16[96,896]{1,0:T(8,128)(2,1)S(1)}, bf16[96,896]{1,0:T(8,128)(2,1)S(1)}, u32[]{:S(2)}, u32[]{:S(2)}) collective-permute-start(bf16[96,896]{1,0:T(8,128)(2,1)S(1)} %get-tuple-element.103), channel_id=1, source_target_pairs={{0,30},{2,28},{4,26},{6,24},{8,22},{10,20},{12,18},{14,16},{16,14}... | collective-permute-start | bytes 516104 | tf_op jit(solution)/shard_map/ppermute | solution.py:350
  59.2 18.3 %collective-permute-start.22 = (bf16[96,896]{1,0:T(8,128)(2,1)S(1)}, bf16[96,896]{1,0:T(8,128)(2,1)S(1)}, u32[]{:S(2)}, u32[]{:S(2)}) collective-permute-start(bf16[96,896]{1,0:T(8,128)(2,1)S(1)} %get-tuple-element.101), channel_id=1, source_target_pairs={{0,28},{2,30},{4,24},{6,26},{8,20},{10,22},{12,16},{14,18},{16,12}... | collective-permute-start | bytes 516104 | tf_op jit(solution)/shard_map/ppermute | solution.py:350
  60.5 17.1 %collective-permute-start.21 = (bf16[96,896]{1,0:T(8,128)(2,1)S(1)}, bf16[96,896]{1,0:T(8,128)(2,1)S(1)}, u32[]{:S(2)}, u32[]{:S(2)}) collective-permute-start(bf16[96,896]{1,0:T(8,128)(2,1)S(1)} %get-tuple-element.99), channel_id=1, source_target_pairs={{0,26},{2,24},{4,30},{6,28},{8,18},{10,16},{12,22},{14,20},{16,10}... | collective-permute-start | bytes 516104 | tf_op jit(solution)/shard_map/ppermute | solution.py:350
  78.9 16.9 %collective-permute-start.28 = (bf16[896,256]{1,0:T(8,128)(2,1)S(1)}, bf16[896,256]{1,0:T(8,128)(2,1)S(1)}, u32[]{:S(2)}, u32[]{:S(2)}) collective-permute-start(bf16[896,256]{1,0:T(8,128)(2,1)S(1)} %get-tuple-element.105.refs_0_), channel_id=1, source_target_pairs={{0,8},{8,16},{16,24},{24,28},{28,20},{20,12},{12,4},{4,0},{10,2},{... | collective-permute-start | bytes 1376264 | tf_op jit(solution)/shard_map/ppermute | solution.py:440
  100.9 13.2 %collective-permute-start.32 = (bf16[896,256]{1,0:T(8,128)(2,1)S(1)}, bf16[896,256]{1,0:T(8,128)(2,1)S(1)}, u32[]{:S(2)}, u32[]{:S(2)}) collective-permute-start(bf16[896,256]{1,0:T(8,128)(2,1)S(1)} %collective-permute-done.28.refs_2_), channel_id=1, source_target_pairs={{0,8},{8,16},{16,24},{24,28},{28,20},{20,12},{12,4},{4,0},{10,2},{... | collective-permute-start | bytes 1376264 | tf_op jit(solution)/shard_map/ppermute | solution.py:440
  100.9 15.0 %collective-permute-start.39 = (bf16[896,256]{1,0:T(8,128)(2,1)S(1)}, bf16[896,256]{1,0:T(8,128)(2,1)S(1)}, u32[]{:S(2)}, u32[]{:S(2)}) collective-permute-start(bf16[896,256]{1,0:T(8,128)(2,1)S(1)} %get-tuple-element.105.refs_0_), channel_id=1, source_target_pairs={{0,2},{2,0},{4,6},{6,4},{8,10},{10,8},{12,14},{14,12},{16,18},{18,... | collective-permute-start | bytes 1376264 | tf_op jit(solution)/shard_map/ppermute | solution.py:441
  114.1 13.2 %collective-permute-start.33 = (bf16[896,256]{1,0:T(8,128)(2,1)S(1)}, bf16[896,256]{1,0:T(8,128)(2,1)S(1)}, u32[]{:S(2)}, u32[]{:S(2)}) collective-permute-start(bf16[896,256]{1,0:T(8,128)(2,1)S(1)} %collective-permute-done.32.refs_6_), channel_id=1, source_target_pairs={{0,8},{8,16},{16,24},{24,28},{28,20},{20,12},{12,4},{4,0},{10,2},{... | collective-permute-start | bytes 1376264 | tf_op jit(solution)/shard_map/ppermute | solution.py:440
  114.1 13.3 %collective-permute-start.40 = (bf16[896,256]{1,0:T(8,128)(2,1)S(1)}, bf16[896,256]{1,0:T(8,128)(2,1)S(1)}, u32[]{:S(2)}, u32[]{:S(2)}) collective-permute-start(bf16[896,256]{1,0:T(8,128)(2,1)S(1)} %collective-permute-done.28.refs_2_), channel_id=1, source_target_pairs={{0,2},{2,0},{4,6},{6,4},{8,10},{10,8},{12,14},{14,12},{16,18},{18,... | collective-permute-start | bytes 1376264 | tf_op jit(solution)/shard_map/ppermute | solution.py:441
  115.9 11.5 %collective-permute-start.42 = (bf16[896,256]{1,0:T(8,128)(2,1)S(1)}, bf16[896,256]{1,0:T(8,128)(2,1)S(1)}, u32[]{:S(2)}, u32[]{:S(2)}) collective-permute-start(bf16[896,256]{1,0:T(8,128)(2,1)S(1)} %collective-permute-done.32.refs_6_), channel_id=1, source_target_pairs={{0,2},{2,0},{4,6},{6,4},{8,10},{10,8},{12,14},{14,12},{16,18},{18,... | collective-permute-start | bytes 1376264 | tf_op jit(solution)/shard_map/ppermute | solution.py:441
  116.6 15.2 %collective-permute-start.44 = (bf16[896,256]{1,0:T(8,128)(2,1)S(1)}, bf16[896,256]{1,0:T(8,128)(2,1)S(1)}, u32[]{:S(2)}, u32[]{:S(2)}) collective-permute-start(bf16[896,256]{1,0:T(8,128)(2,1)S(1)} %collective-permute-done.36.refs_0_), channel_id=1, source_target_pairs={{8,0},{16,8},{24,16},{28,24},{20,28},{12,20},{4,12},{0,4},{2,10},{... | collective-permute-start | bytes 1376264 | tf_op jit(solution)/shard_map/ppermute | solution.py:440
  117.0 23.4 %collective-permute-start.37 = (bf16[896,256]{1,0:T(8,128)(2,1)S(1)}, bf16[896,256]{1,0:T(8,128)(2,1)S(1)}, u32[]{:S(2)}, u32[]{:S(2)}) collective-permute-start(bf16[896,256]{1,0:T(8,128)(2,1)S(1)} %collective-permute-done.36.refs_0_), channel_id=1, source_target_pairs={{0,2},{2,0},{4,6},{6,4},{8,10},{10,8},{12,14},{14,12},{16,18},{18,... | collective-permute-start | bytes 1376264 | tf_op jit(solution)/shard_map/ppermute | solution.py:441
  127.3 13.1 %collective-permute-start.38 = (bf16[896,256]{1,0:T(8,128)(2,1)S(1)}, bf16[896,256]{1,0:T(8,128)(2,1)S(1)}, u32[]{:S(2)}, u32[]{:S(2)}) collective-permute-start(bf16[896,256]{1,0:T(8,128)(2,1)S(1)} %collective-permute-done.33.refs_2_), channel_id=1, source_target_pairs={{0,2},{2,0},{4,6},{6,4},{8,10},{10,8},{12,14},{14,12},{16,18},{18,... | collective-permute-start | bytes 1376264 | tf_op jit(solution)/shard_map/ppermute | solution.py:441
  127.4 15.6 %collective-permute-start.34 = (bf16[896,256]{1,0:T(8,128)(2,1)S(1)}, bf16[896,256]{1,0:T(8,128)(2,1)S(1)}, u32[]{:S(2)}, u32[]{:S(2)}) collective-permute-start(bf16[896,256]{1,0:T(8,128)(2,1)S(1)} %collective-permute-done.33.refs_2_), channel_id=1, source_target_pairs={{0,8},{8,16},{16,24},{24,28},{28,20},{20,12},{12,4},{4,0},{10,2},{... | collective-permute-start | bytes 1376264 | tf_op jit(solution)/shard_map/ppermute | solution.py:440
  131.8 11.3 %collective-permute-start.45 = (bf16[896,256]{1,0:T(8,128)(2,1)S(1)}, bf16[896,256]{1,0:T(8,128)(2,1)S(1)}, u32[]{:S(2)}, u32[]{:S(2)}) collective-permute-start(bf16[896,256]{1,0:T(8,128)(2,1)S(1)} %collective-permute-done.44.refs_0_), channel_id=1, source_target_pairs={{0,2},{2,0},{4,6},{6,4},{8,10},{10,8},{12,14},{14,12},{16,18},{18,... | collective-permute-start | bytes 1376264 | tf_op jit(solution)/shard_map/ppermute | solution.py:441
  (23 other events, 142.8 us)

commit v12 on v11

--- a/solution.py
+++ b/solution.py
@@ -424,27 +424,29 @@
         return tuple(write(lambda me, n: n, blocks, colsq, None))
 
     turns, swap = ring_steps(count), swap_pairs(count)
-    rounds = sum_rounds(count)
-    colsq, result, waiting = part, None, {}
+    colsq, result = part, None
+    for axis, distances in sum_rounds(count):
+        colsq = sum_round(colsq, axis, distances)
     arrived, blocks, owners, written = {0: back}, [], [], 0
-    ready = {chips - 3: 2 * chips - 8, chips - 2: 2 * chips - 4, chips - 1: 2 * chips - 1}
+    waiting = ()
     for n in range(chips):
-        if n < 2:
-            for _ in range(2 - n):
-                colsq = sum_round(tie(colsq, arrived[n]), *rounds.pop(0))
-        if n == 1:
-            waiting[1] = (colsq,)
-        block = tie(arrived[n], *waiting.get(n, ()))
+        block = tie(arrived[n], *waiting)
         for later in (1, 2) if n == 0 else (n + 2,):
             if later < chips:
                 arrived[later] = lax.ppermute(block, "fsdp", turns[(later + 1) % 2])
         blocks += [block, lax.ppermute(block, "fsdp", swap)]
         hops = (n + 1) // 2 if n % 2 else -(n // 2)
         owners += [functools.partial(ring_owner, count, hops, far) for far in (False, True)]
-        if n in ready:
-            upto = ready[n]
-            result = write(owner_of(owners[written:upto]), blocks[written:upto], colsq, result)
-            written, waiting[n + 1] = upto, tuple(result) + waiting.get(n + 1, ())
+        if n == 0:
+            waiting = (arrived[2], colsq)
+            continue
+        if n == 2:
+            waiting = ()
+            continue
+        upto = 2 * n + (2 if n == 1 else 1 if n + 1 == chips else 0)
+        upto = min(upto, written + 4) if n + 1 < chips else upto
+        result = write(owner_of(owners[written:upto]), blocks[written:upto], colsq, result)
+        written, waiting = upto, tuple(result)
     return tuple(write(owner_of(owners[written:]), blocks[written:], colsq, result))
 
 

time: 147 us -> 138 us (0.939)
  the two profiles are of different devices: /device:TPU:25 before, /device:TPU:1 now
where the time goes in v12:
time: 138 us
  starting transfers between devices  61.3 us (44%)
  waiting for transfers between devices  40.4 us (29%)
  Pallas kernels  28.8 us (21%)
  other arithmetic  3.98 us (3%)
  local copies, waits for them, and re-layouts  1.43 us (1%)
    ppermute x15, starting transfers between devices, exchange(): columns[k] = lax.ppermute(tie(outgoing[k], *after), 'fsdp', pairs)  23 us
    ppermute x15, waiting for transfers between devices, exchange(): columns[k] = lax.ppermute(tie(outgoing[k], *after), 'fsdp', pairs)  14.3 us
    pallas_call x1, Pallas kernels, factor_call(): pl.pallas_call(functools.partial(factor_kernel, len(stacked), owner), in_...  14.2 us
    pallas_call x7, Pallas kernels, output_call(): pl.pallas_call(functools.partial(output_kernel, owner, factor), in_specs=...  12.7 us
    ppermute x7, starting transfers between devices, local(): arrived[later] = lax.ppermute(block, 'fsdp', turns[(later + 1) % 2])  12.4 us
    ppermute x7, waiting for transfers between devices, local(): arrived[later] = lax.ppermute(block, 'fsdp', turns[(later + 1) % 2])  10.2 us
    ppermute x4, waiting for transfers between devices, gather_and_exchange(): ahead = lax.ppermute(ahead, 'fsdp', first)  7.97 us
    ppermute x7, waiting for transfers between devices, sum_round(): terms.append(lax.ppermute(x, axis, [(n, n ^ d) for n in range(size)]))  7.38 us
  transfers between devices with their start and end apart: 46, of which 17 were waited for; matrix products, arithmetic and copies ran while one was open for 0% of the time, Pallas kernels for 19%

profile of v12, /device:TPU:1, one launch (start us, length us, event | category | flops | bytes accessed | tf_op | source)
XLA Modules:
  0.0 138.1 jit_solution(11387855181524497379)
XLA Ops:
  0.6 4.0 %convert_add_fusion.base_ref = f32[96,13824]{1,0:T(8,128)S(1)} fusion(f32[96,13824]{1,0:T(8,128)} %param.3, bf16[96,13824]{1,0:T(8,128)(2,1)} %param.4), kind=kLoop, calls=%fused_computation | loop fusion | flops 2654208 | bytes 13271040 | tf_op jit(solution)/shard_map/add | solution.py:402
  7.2 2.1 %collective-permute-start = (f32[96,256]{1,0:T(8,128)S(1)}, f32[96,256]{1,0:T(8,128)S(1)}, u32[]{:S(2)}, u32[]{:S(2)}) collective-permute-start(f32[96,256]{1,0:T(8,128)S(1)} %fusion), channel_id=1, source_target_pairs={{0,1},{1,0},{2,3},{3,2},{4,5},{5,4},{6,7},{7,6},{8,9},{9,8},{10,11... | collective-permute-start | bytes 294920 | tf_op jit(solution)/shard_map/ppermute | solution.py:353
  12.3 2.3 %collective-permute-start.3 = (bf16[96,896]{1,0:T(8,128)(2,1)S(1)}, bf16[96,896]{1,0:T(8,128)(2,1)S(1)}, u32[]{:S(2)}, u32[]{:S(2)}) collective-permute-start(bf16[96,896]{1,0:T(8,128)(2,1)S(1)} %get-tuple-element.74), channel_id=1, source_target_pairs={{0,16},{2,18},{4,20},{6,22},{8,24},{10,26},{12,28},{14,30},{16,0},... | collective-permute-start | bytes 516104 | tf_op jit(solution)/shard_map/ppermute | solution.py:350
  17.5 1.9 %collective-permute-start.9 = (bf16[96,896]{1,0:T(8,128)(2,1)S(1)}, bf16[96,896]{1,0:T(8,128)(2,1)S(1)}, u32[]{:S(2)}, u32[]{:S(2)}) collective-permute-start(bf16[96,896]{1,0:T(8,128)(2,1)S(1)} %get-tuple-element.84), channel_id=1, source_target_pairs={{0,6},{2,4},{4,2},{6,0},{8,14},{10,12},{12,10},{14,8},{16,22},{18,... | collective-permute-start | bytes 516104 | tf_op jit(solution)/shard_map/ppermute | solution.py:350
  19.3 3.6 %collective-permute-done.3.refs_8_ = bf16[96,896]{1,0:T(8,128)(2,1)S(1)} collective-permute-done((bf16[96,896]{1,0:T(8,128)(2,1)S(1)}, bf16[96,896]{1,0:T(8,128)(2,1)S(1)}, u32[]{:S(2)}, u32[]{:S(2)}) %collective-permute-start.3) | collective-permute-done | bytes 172064 | tf_op jit(solution)/shard_map/ppermute | solution.py:350
  23.5 3.7 %collective-permute-start.7 = (f32[96,256]{1,0:T(8,128)S(1)}, f32[96,256]{1,0:T(8,128)S(1)}, u32[]{:S(2)}, u32[]{:S(2)}) collective-permute-start(f32[96,256]{1,0:T(8,128)S(1)} %collective-permute-done.2), channel_id=1, source_target_pairs={{8,0},{16,8},{24,16},{28,24},{20,28},{12,20},{4,12},{0,4},{2,10},{... | collective-permute-start | bytes 294920 | tf_op jit(solution)/shard_map/ppermute | solution.py:364
  29.3 4.8 %collective-permute-done.8.refs_9_ = bf16[96,896]{1,0:T(8,128)(2,1)S(1)} collective-permute-done((bf16[96,896]{1,0:T(8,128)(2,1)S(1)}, bf16[96,896]{1,0:T(8,128)(2,1)S(1)}, u32[]{:S(2)}, u32[]{:S(2)}) %collective-permute-start.8) | collective-permute-done | bytes 172064 | tf_op jit(solution)/shard_map/ppermute | solution.py:350
  37.3 2.8 %collective-permute-start.18 = (bf16[96,896]{1,0:T(8,128)(2,1)S(1)}, bf16[96,896]{1,0:T(8,128)(2,1)S(1)}, u32[]{:S(2)}, u32[]{:S(2)}) collective-permute-start(bf16[96,896]{1,0:T(8,128)(2,1)S(1)} %get-tuple-element.99), channel_id=1, source_target_pairs={{0,14},{2,12},{4,10},{6,8},{8,6},{10,4},{12,2},{14,0},{16,30},{18,... | collective-permute-start | bytes 516104 | tf_op jit(solution)/shard_map/ppermute | solution.py:350
  40.0 5.5 %collective-permute-done.14.refs_5_ = bf16[96,896]{1,0:T(8,128)(2,1)S(1)} collective-permute-done((bf16[96,896]{1,0:T(8,128)(2,1)S(1)}, bf16[96,896]{1,0:T(8,128)(2,1)S(1)}, u32[]{:S(2)}, u32[]{:S(2)}) %collective-permute-start.14) | collective-permute-done | bytes 172064 | tf_op jit(solution)/shard_map/ppermute | solution.py:350
  45.5 1.9 %collective-permute-start.17 = (bf16[96,896]{1,0:T(8,128)(2,1)S(1)}, bf16[96,896]{1,0:T(8,128)(2,1)S(1)}, u32[]{:S(2)}, u32[]{:S(2)}) collective-permute-start(bf16[96,896]{1,0:T(8,128)(2,1)S(1)} %get-tuple-element.97), channel_id=1, source_target_pairs={{0,22},{2,20},{4,18},{6,16},{8,30},{10,28},{12,26},{14,24},{16,6},... | collective-permute-start | bytes 516104 | tf_op jit(solution)/shard_map/ppermute | solution.py:350
  47.7 8.0 %collective-permute-done.16 = f32[96,256]{1,0:T(8,128)S(1)} collective-permute-done((f32[96,256]{1,0:T(8,128)S(1)}, f32[96,256]{1,0:T(8,128)S(1)}, u32[]{:S(2)}, u32[]{:S(2)}) %collective-permute-start.16) | collective-permute-done | bytes 98336 | tf_op jit(solution)/shard_map/ppermute | solution.py:360
  56.9 2.5 %collective-permute-start.20 = (bf16[96,896]{1,0:T(8,128)(2,1)S(1)}, bf16[96,896]{1,0:T(8,128)(2,1)S(1)}, u32[]{:S(2)}, u32[]{:S(2)}) collective-permute-start(bf16[96,896]{1,0:T(8,128)(2,1)S(1)} %get-tuple-element.106), channel_id=1, source_target_pairs={{0,24},{2,26},{4,28},{6,30},{8,16},{10,18},{12,20},{14,22},{16,8},... | collective-permute-start | bytes 516104 | tf_op jit(solution)/shard_map/ppermute | solution.py:350
  60.2 4.0 %collective-permute-start.22 = (bf16[96,896]{1,0:T(8,128)(2,1)S(1)}, bf16[96,896]{1,0:T(8,128)(2,1)S(1)}, u32[]{:S(2)}, u32[]{:S(2)}) collective-permute-start(bf16[96,896]{1,0:T(8,128)(2,1)S(1)} %get-tuple-element.110), channel_id=1, source_target_pairs={{0,28},{2,30},{4,24},{6,26},{8,20},{10,22},{12,16},{14,18},{16,12}... | collective-permute-start | bytes 516104 | tf_op jit(solution)/shard_map/ppermute | solution.py:350
  64.9 14.2 %factor.1 = (bf16[256,1536]{1,0:T(8,128)(2,1)S(1)}, bf16[96,256]{1,0:T(8,128)(2,1)S(1)}) custom-call(f32[96,13824]{1,0:T(8,128)S(1)} %convert_add_fusion.base_ref, f32[8,96,256]{2,1,0:T(8,128)S(1)} %bitcast_dynamic-update-slice_fusion.refs_0_, f32[8,96,256]{2,1,0:T(8,128)S(1)} %collective-permute-done.19.refs_1_), custom_call_target="tpu_custom_call" | custom-call | flops 4026531840 | bytes 2359296 | tf_op jit(solution)/shard_map/factor/pallas_call | solution.py:166
  80.6 9.3 %collective-permute-start.32 = (bf16[896,256]{1,0:T(8,128)(2,1)S(1)}, bf16[896,256]{1,0:T(8,128)(2,1)S(1)}, u32[]{:S(2)}, u32[]{:S(2)}) collective-permute-start(bf16[896,256]{1,0:T(8,128)(2,1)S(1)} %get-tuple-element.114.refs_0_), channel_id=1, source_target_pairs={{8,0},{16,8},{24,16},{28,24},{20,28},{12,20},{4,12},{0,4},{2,10},{... | collective-permute-start | bytes 1376264 | tf_op jit(solution)/shard_map/ppermute | solution.py:436
  90.2 2.2 %collective-permute-done.24 = f32[1,256]{1,0:T(1,128)S(1)} collective-permute-done((f32[1,256]{1,0:T(1,128)S(1)}, f32[1,256]{1,0:T(1,128)S(1)}, u32[]{:S(2)}, u32[]{:S(2)}) %collective-permute-start.24) | collective-permute-done | bytes 1056 | tf_op jit(solution)/shard_map/ppermute | solution.py:386
  93.7 1.8 %collective-permute-start.26 = (f32[1,256]{1,0:T(1,128)S(1)}, f32[1,256]{1,0:T(1,128)S(1)}, u32[]{:S(2)}, u32[]{:S(2)}) collective-permute-start(f32[1,256]{1,0:T(1,128)S(1)} %add.29), channel_id=1, source_target_pairs={{0,4},{2,6},{4,0},{6,2},{8,12},{10,14},{12,8},{14,10},{16,20},{18,... | collective-permute-start | bytes 3080 | tf_op jit(solution)/shard_map/ppermute | solution.py:386
  95.5 2.0 %collective-permute-done.26 = f32[1,256]{1,0:T(1,128)S(1)} collective-permute-done((f32[1,256]{1,0:T(1,128)S(1)}, f32[1,256]{1,0:T(1,128)S(1)}, u32[]{:S(2)}, u32[]{:S(2)}) %collective-permute-start.26) | collective-permute-done | bytes 1056 | tf_op jit(solution)/shard_map/ppermute | solution.py:386
  108.0 2.8 %outputs.7 = (f32[96,13824]{1,0:T(8,128)}, bf16[13824,256]{1,0:T(8,128)(2,1)}, bf16[96,13824]{1,0:T(8,128)(2,1)}) custom-call(f32[96,13824]{1,0:T(8,128)S(1)} %convert_add_fusion.base_ref, bf16[96,256]{1,0:T(8,128)(2,1)S(1)} %get-tuple-element.101.ortho_ref, f32[1,256]{1,0:T(1,128)S(1)} %add_add_fusion.colsq_ref, ...), custom_call_target="tpu_custom_call" | custom-call | flops 352321536 | bytes 7110656 | tf_op jit(solution)/shard_map/outputs/pallas_call | solution.py:271
  111.3 3.0 %collective-permute-done.33.refs_0_ = bf16[896,256]{1,0:T(8,128)(2,1)S(1)} collective-permute-done((bf16[896,256]{1,0:T(8,128)(2,1)S(1)}, bf16[896,256]{1,0:T(8,128)(2,1)S(1)}, u32[]{:S(2)}, u32[]{:S(2)}) %collective-permute-start.33) | collective-permute-done | bytes 458784 | tf_op jit(solution)/shard_map/ppermute | solution.py:436
  118.4 1.8 %collective-permute-done.41.refs_0_ = bf16[896,256]{1,0:T(8,128)(2,1)S(1)} collective-permute-done((bf16[896,256]{1,0:T(8,128)(2,1)S(1)}, bf16[896,256]{1,0:T(8,128)(2,1)S(1)}, u32[]{:S(2)}, u32[]{:S(2)}) %collective-permute-start.41) | collective-permute-done | bytes 458784 | tf_op jit(solution)/shard_map/ppermute | solution.py:436
  122.8 2.0 %collective-permute-done.34.refs_0_ = bf16[896,256]{1,0:T(8,128)(2,1)S(1)} collective-permute-done((bf16[896,256]{1,0:T(8,128)(2,1)S(1)}, bf16[896,256]{1,0:T(8,128)(2,1)S(1)}, u32[]{:S(2)}, u32[]{:S(2)}) %collective-permute-start.34) | collective-permute-done | bytes 458784 | tf_op jit(solution)/shard_map/ppermute | solution.py:436
  131.9 2.3 %collective-permute-done.39.refs_2_ = bf16[896,256]{1,0:T(8,128)(2,1)S(1)} collective-permute-done((bf16[896,256]{1,0:T(8,128)(2,1)S(1)}, bf16[896,256]{1,0:T(8,128)(2,1)S(1)}, u32[]{:S(2)}, u32[]{:S(2)}) %collective-permute-start.39) | collective-permute-done | bytes 458784 | tf_op jit(solution)/shard_map/ppermute | solution.py:436
  134.8 1.9 %outputs.12 = (f32[96,13824]{1,0:T(8,128)}, bf16[13824,256]{1,0:T(8,128)(2,1)}, bf16[96,13824]{1,0:T(8,128)(2,1)}) custom-call(f32[96,13824]{1,0:T(8,128)S(1)} %convert_add_fusion.base_ref, bf16[96,256]{1,0:T(8,128)(2,1)S(1)} %get-tuple-element.101.ortho_ref, ...), custom_call_target="tpu_custom_call", output_to_operand_aliasing={{0}: (6, {}), {1}: (7, {}), {2}: (8, {})} | custom-call | flops 264241152 | bytes 5332992 | tf_op jit(solution)/shard_map/outputs/pallas_call | solution.py:271
  (93 shorter events, 46.8 us)
Async XLA Ops:
  12.3 10.6 %collective-permute-start.3 = (bf16[96,896]{1,0:T(8,128)(2,1)S(1)}, bf16[96,896]{1,0:T(8,128)(2,1)S(1)}, u32[]{:S(2)}, u32[]{:S(2)}) collective-permute-start(bf16[96,896]{1,0:T(8,128)(2,1)S(1)} %get-tuple-element.74), channel_id=1, source_target_pairs={{0,16},{2,18},{4,20},{6,22},{8,24},{10,26},{12,28},{14,30},{16,0},... | collective-permute-start | bytes 516104 | tf_op jit(solution)/shard_map/ppermute | solution.py:350
  14.7 8.6 %collective-permute-start.1 = (f32[96,256]{1,0:T(8,128)S(1)}, f32[96,256]{1,0:T(8,128)S(1)}, u32[]{:S(2)}, u32[]{:S(2)}) collective-permute-start(f32[96,256]{1,0:T(8,128)S(1)} %get-tuple-element.72), channel_id=1, source_target_pairs={{0,8},{8,16},{16,24},{24,28},{28,20},{20,12},{12,4},{4,0},{10,2},{... | collective-permute-start | bytes 294920 | tf_op jit(solution)/shard_map/ppermute | solution.py:360
  16.2 11.1 %collective-permute-start.10 = (bf16[96,896]{1,0:T(8,128)(2,1)S(1)}, bf16[96,896]{1,0:T(8,128)(2,1)S(1)}, u32[]{:S(2)}, u32[]{:S(2)}) collective-permute-start(bf16[96,896]{1,0:T(8,128)(2,1)S(1)} %get-tuple-element.86), channel_id=1, source_target_pairs={{0,8},{2,10},{4,12},{6,14},{8,0},{10,2},{12,4},{14,6},{16,24},{18,... | collective-permute-start | bytes 516104 | tf_op jit(solution)/shard_map/ppermute | solution.py:350
  17.5 11.2 %collective-permute-start.9 = (bf16[96,896]{1,0:T(8,128)(2,1)S(1)}, bf16[96,896]{1,0:T(8,128)(2,1)S(1)}, u32[]{:S(2)}, u32[]{:S(2)}) collective-permute-start(bf16[96,896]{1,0:T(8,128)(2,1)S(1)} %get-tuple-element.84), channel_id=1, source_target_pairs={{0,6},{2,4},{4,2},{6,0},{8,14},{10,12},{12,10},{14,8},{16,22},{18,... | collective-permute-start | bytes 516104 | tf_op jit(solution)/shard_map/ppermute | solution.py:350
  23.0 11.2 %collective-permute-start.8 = (bf16[96,896]{1,0:T(8,128)(2,1)S(1)}, bf16[96,896]{1,0:T(8,128)(2,1)S(1)}, u32[]{:S(2)}, u32[]{:S(2)}) collective-permute-start(bf16[96,896]{1,0:T(8,128)(2,1)S(1)} %get-tuple-element.82), channel_id=1, source_target_pairs={{0,18},{2,16},{4,22},{6,20},{8,26},{10,24},{12,30},{14,28},{16,2},... | collective-permute-start | bytes 516104 | tf_op jit(solution)/shard_map/ppermute | solution.py:350
  23.3 10.9 %collective-permute-start.6 = (f32[96,256]{1,0:T(8,128)S(1)}, f32[96,256]{1,0:T(8,128)S(1)}, u32[]{:S(2)}, u32[]{:S(2)}) collective-permute-start(f32[96,256]{1,0:T(8,128)S(1)} %collective-permute-done.1), channel_id=1, source_target_pairs={{0,8},{8,16},{16,24},{24,28},{28,20},{20,12},{12,4},{4,0},{10,2},{... | collective-permute-start | bytes 294920 | tf_op jit(solution)/shard_map/ppermute | solution.py:360
  23.5 10.7 %collective-permute-start.7 = (f32[96,256]{1,0:T(8,128)S(1)}, f32[96,256]{1,0:T(8,128)S(1)}, u32[]{:S(2)}, u32[]{:S(2)}) collective-permute-start(f32[96,256]{1,0:T(8,128)S(1)} %collective-permute-done.2), channel_id=1, source_target_pairs={{8,0},{16,8},{24,16},{28,24},{20,28},{12,20},{4,12},{0,4},{2,10},{... | collective-permute-start | bytes 294920 | tf_op jit(solution)/shard_map/ppermute | solution.py:364
  27.3 10.0 %collective-permute-start.15 = (bf16[96,896]{1,0:T(8,128)(2,1)S(1)}, bf16[96,896]{1,0:T(8,128)(2,1)S(1)}, u32[]{:S(2)}, u32[]{:S(2)}) collective-permute-start(bf16[96,896]{1,0:T(8,128)(2,1)S(1)} %get-tuple-element.94), channel_id=1, source_target_pairs={{0,12},{2,14},{4,8},{6,10},{8,4},{10,6},{12,0},{14,2},{16,28},{18,... | collective-permute-start | bytes 516104 | tf_op jit(solution)/shard_map/ppermute | solution.py:350
  28.7 16.8 %collective-permute-start.14 = (bf16[96,896]{1,0:T(8,128)(2,1)S(1)}, bf16[96,896]{1,0:T(8,128)(2,1)S(1)}, u32[]{:S(2)}, u32[]{:S(2)}) collective-permute-start(bf16[96,896]{1,0:T(8,128)(2,1)S(1)} %get-tuple-element.92), channel_id=1, source_target_pairs={{0,10},{2,8},{4,14},{6,12},{8,2},{10,0},{12,6},{14,4},{16,26},{18,... | collective-permute-start | bytes 516104 | tf_op jit(solution)/shard_map/ppermute | solution.py:350
  34.2 13.2 %collective-permute-start.13 = (bf16[96,896]{1,0:T(8,128)(2,1)S(1)}, bf16[96,896]{1,0:T(8,128)(2,1)S(1)}, u32[]{:S(2)}, u32[]{:S(2)}) collective-permute-start(bf16[96,896]{1,0:T(8,128)(2,1)S(1)} %get-tuple-element.90), channel_id=1, source_target_pairs={{0,20},{2,22},{4,16},{6,18},{8,28},{10,30},{12,24},{14,26},{16,4},... | collective-permute-start | bytes 516104 | tf_op jit(solution)/shard_map/ppermute | solution.py:350
  34.2 13.2 %collective-permute-start.11 = (f32[96,256]{1,0:T(8,128)S(1)}, f32[96,256]{1,0:T(8,128)S(1)}, u32[]{:S(2)}, u32[]{:S(2)}) collective-permute-start(f32[96,256]{1,0:T(8,128)S(1)} %collective-permute-done.6), channel_id=1, source_target_pairs={{0,8},{8,16},{16,24},{24,28},{28,20},{20,12},{12,4},{4,0},{10,2},{... | collective-permute-start | bytes 294920 | tf_op jit(solution)/shard_map/ppermute | solution.py:360
  35.4 12.0 %collective-permute-start.12 = (f32[96,256]{1,0:T(8,128)S(1)}, f32[96,256]{1,0:T(8,128)S(1)}, u32[]{:S(2)}, u32[]{:S(2)}) collective-permute-start(f32[96,256]{1,0:T(8,128)S(1)} %collective-permute-done.7), channel_id=1, source_target_pairs={{8,0},{16,8},{24,16},{28,24},{20,28},{12,20},{4,12},{0,4},{2,10},{... | collective-permute-start | bytes 294920 | tf_op jit(solution)/shard_map/ppermute | solution.py:364
  37.3 18.4 %collective-permute-start.18 = (bf16[96,896]{1,0:T(8,128)(2,1)S(1)}, bf16[96,896]{1,0:T(8,128)(2,1)S(1)}, u32[]{:S(2)}, u32[]{:S(2)}) collective-permute-start(bf16[96,896]{1,0:T(8,128)(2,1)S(1)} %get-tuple-element.99), channel_id=1, source_target_pairs={{0,14},{2,12},{4,10},{6,8},{8,6},{10,4},{12,2},{14,0},{16,30},{18,... | collective-permute-start | bytes 516104 | tf_op jit(solution)/shard_map/ppermute | solution.py:350
  45.5 10.2 %collective-permute-start.17 = (bf16[96,896]{1,0:T(8,128)(2,1)S(1)}, bf16[96,896]{1,0:T(8,128)(2,1)S(1)}, u32[]{:S(2)}, u32[]{:S(2)}) collective-permute-start(bf16[96,896]{1,0:T(8,128)(2,1)S(1)} %get-tuple-element.97), channel_id=1, source_target_pairs={{0,22},{2,20},{4,18},{6,16},{8,30},{10,28},{12,26},{14,24},{16,6},... | collective-permute-start | bytes 516104 | tf_op jit(solution)/shard_map/ppermute | solution.py:350
  55.7 9.2 %collective-permute-start.19 = (f32[8,96,256]{2,1,0:T(8,128)S(1)}, f32[8,96,256]{2,1,0:T(8,128)S(1)}, u32[]{:S(2)}, u32[]{:S(2)}) collective-permute-start(f32[8,96,256]{2,1,0:T(8,128)S(1)} %bitcast_dynamic-update-slice_fusion.refs_0_), channel_id=1, source_target_pairs={{0,2},{2,0},{4,6},{6,4},{8,10},{10,8},{12,14},{14,12},{16,18},{18,... | collective-permute-start | bytes 2359304 | tf_op jit(solution)/shard_map/ppermute | solution.py:369
  56.9 22.2 %collective-permute-start.20 = (bf16[96,896]{1,0:T(8,128)(2,1)S(1)}, bf16[96,896]{1,0:T(8,128)(2,1)S(1)}, u32[]{:S(2)}, u32[]{:S(2)}) collective-permute-start(bf16[96,896]{1,0:T(8,128)(2,1)S(1)} %get-tuple-element.106), channel_id=1, source_target_pairs={{0,24},{2,26},{4,28},{6,30},{8,16},{10,18},{12,20},{14,22},{16,8},... | collective-permute-start | bytes 516104 | tf_op jit(solution)/shard_map/ppermute | solution.py:350
  59.5 19.7 %collective-permute-start.23 = (bf16[96,896]{1,0:T(8,128)(2,1)S(1)}, bf16[96,896]{1,0:T(8,128)(2,1)S(1)}, u32[]{:S(2)}, u32[]{:S(2)}) collective-permute-start(bf16[96,896]{1,0:T(8,128)(2,1)S(1)} %get-tuple-element.112), channel_id=1, source_target_pairs={{0,30},{2,28},{4,26},{6,24},{8,22},{10,20},{12,18},{14,16},{16,14}... | collective-permute-start | bytes 516104 | tf_op jit(solution)/shard_map/ppermute | solution.py:350
  60.2 19.0 %collective-permute-start.22 = (bf16[96,896]{1,0:T(8,128)(2,1)S(1)}, bf16[96,896]{1,0:T(8,128)(2,1)S(1)}, u32[]{:S(2)}, u32[]{:S(2)}) collective-permute-start(bf16[96,896]{1,0:T(8,128)(2,1)S(1)} %get-tuple-element.110), channel_id=1, source_target_pairs={{0,28},{2,30},{4,24},{6,26},{8,20},{10,22},{12,16},{14,18},{16,12}... | collective-permute-start | bytes 516104 | tf_op jit(solution)/shard_map/ppermute | solution.py:350
  64.2 15.0 %collective-permute-start.21 = (bf16[96,896]{1,0:T(8,128)(2,1)S(1)}, bf16[96,896]{1,0:T(8,128)(2,1)S(1)}, u32[]{:S(2)}, u32[]{:S(2)}) collective-permute-start(bf16[96,896]{1,0:T(8,128)(2,1)S(1)} %get-tuple-element.108), channel_id=1, source_target_pairs={{0,26},{2,24},{4,30},{6,28},{8,18},{10,16},{12,22},{14,20},{16,10}... | collective-permute-start | bytes 516104 | tf_op jit(solution)/shard_map/ppermute | solution.py:350
  80.6 24.5 %collective-permute-start.31 = (bf16[896,256]{1,0:T(8,128)(2,1)S(1)}, bf16[896,256]{1,0:T(8,128)(2,1)S(1)}, u32[]{:S(2)}, u32[]{:S(2)}) collective-permute-start(bf16[896,256]{1,0:T(8,128)(2,1)S(1)} %get-tuple-element.114.refs_0_), channel_id=1, source_target_pairs={{0,8},{8,16},{16,24},{24,28},{28,20},{20,12},{12,4},{4,0},{10,2},{... | collective-permute-start | bytes 1376264 | tf_op jit(solution)/shard_map/ppermute | solution.py:436
  80.6 24.5 %collective-permute-start.32 = (bf16[896,256]{1,0:T(8,128)(2,1)S(1)}, bf16[896,256]{1,0:T(8,128)(2,1)S(1)}, u32[]{:S(2)}, u32[]{:S(2)}) collective-permute-start(bf16[896,256]{1,0:T(8,128)(2,1)S(1)} %get-tuple-element.114.refs_0_), channel_id=1, source_target_pairs={{8,0},{16,8},{24,16},{28,24},{20,28},{12,20},{4,12},{0,4},{2,10},{... | collective-permute-start | bytes 1376264 | tf_op jit(solution)/shard_map/ppermute | solution.py:436
  111.2 9.0 %collective-permute-start.41 = (bf16[896,256]{1,0:T(8,128)(2,1)S(1)}, bf16[896,256]{1,0:T(8,128)(2,1)S(1)}, u32[]{:S(2)}, u32[]{:S(2)}) collective-permute-start(bf16[896,256]{1,0:T(8,128)(2,1)S(1)} %collective-permute-done.32.refs_0_), channel_id=1, source_target_pairs={{8,0},{16,8},{24,16},{28,24},{20,28},{12,20},{4,12},{0,4},{2,10},{... | collective-permute-start | bytes 1376264 | tf_op jit(solution)/shard_map/ppermute | solution.py:436
  115.8 9.0 %collective-permute-start.34 = (bf16[896,256]{1,0:T(8,128)(2,1)S(1)}, bf16[896,256]{1,0:T(8,128)(2,1)S(1)}, u32[]{:S(2)}, u32[]{:S(2)}) collective-permute-start(bf16[896,256]{1,0:T(8,128)(2,1)S(1)} %collective-permute-done.33.refs_0_), channel_id=1, source_target_pairs={{0,8},{8,16},{16,24},{24,28},{28,20},{20,12},{12,4},{4,0},{10,2},{... | collective-permute-start | bytes 1376264 | tf_op jit(solution)/shard_map/ppermute | solution.py:436
  120.7 9.0 %collective-permute-start.44 = (bf16[896,256]{1,0:T(8,128)(2,1)S(1)}, bf16[896,256]{1,0:T(8,128)(2,1)S(1)}, u32[]{:S(2)}, u32[]{:S(2)}) collective-permute-start(bf16[896,256]{1,0:T(8,128)(2,1)S(1)} %collective-permute-done.41.refs_0_), channel_id=1, source_target_pairs={{8,0},{16,8},{24,16},{28,24},{20,28},{12,20},{4,12},{0,4},{2,10},{... | collective-permute-start | bytes 1376264 | tf_op jit(solution)/shard_map/ppermute | solution.py:436
  (23 other events, 122.1 us)

commit v13 on v12

--- a/solution.py
+++ b/solution.py
@@ -11,6 +11,7 @@
 LANES = 128
 SUBLANES = 8
 PANEL = 64
+SPLIT = 3 * LANES
 MIB = 1024 * 1024
 FULL = lax.Precision.HIGHEST
 F32 = jnp.float32
@@ -43,30 +44,47 @@
             act(short)
 
 
-def pack_kernel(base_ref, *out_refs):
+def pack_kernel(share, base_ref, *out_refs):
     cols = base_ref.shape[1]
-    share = out_refs[0].shape[1]
+    half, whole = len(out_refs) // 2, share - SPLIT
+    last = (cols - 1) // share
     me = lax.axis_index("fsdp")
+
+    def fill(out_ref, offset, owner, start, stop):
+        short = max(0, min(cols - last * share, stop) - start)
+
+        def put(width):
+            if width:
+                there = pl.ds(pl.multiple_of(owner * share + start, LANES), width)
+                out_ref[:, offset : offset + width] = base_ref[:, there].astype(BF16)
+            if width < stop - start:
+                empty = jnp.zeros((out_ref.shape[0], stop - start - width), BF16)
+                out_ref[:, offset + width : offset + stop - start] = empty
+
+        if short == stop - start:
+            put(short)
+        else:
+            pl.when(owner < last)(lambda: put(stop - start))
+            pl.when(owner == last)(lambda: put(short))
+
     for n, out_ref in enumerate(out_refs):
         owner = me ^ n
-
-        def fill(width):
-            start = pl.multiple_of(owner * share, LANES)
-            out_ref[:, :width] = base_ref[:, pl.ds(start, width)].astype(BF16)
-            if width < share:
-                out_ref[:, width:] = jnp.zeros((out_ref.shape[0], share - width), BF16)
-
-        by_width(owner, cols, share, 0, share, fill)
+        if n < half:
+            fill(out_ref, 0, owner, 0, share)
+            fill(out_ref, share, owner ^ half, whole, share)
+        else:
+            fill(out_ref, 0, owner, 0, whole)
 
 
 def pack_call(base, share, count):
-    rows = base.shape[0]
+    rows, half = base.shape[0], count // 2
+    widths = [share + SPLIT] * half + [share - SPLIT] * half
     vmem = pl.BlockSpec(memory_space=pltpu.VMEM)
     return pl.pallas_call(
-        pack_kernel,
+        functools.partial(pack_kernel, share),
         in_specs=[vmem],
         out_specs=[vmem] * count,
-        out_shape=[jax.ShapeDtypeStruct((rows, share), BF16)] * count,
+        out_shape=[jax.ShapeDtypeStruct((rows, width), BF16) for width in widths],
         compiler_params=params(16),
         cost_estimate=cost(0, 6 * rows * share * count),
         name="pack",
@@ -182,37 +200,73 @@
     )(base, *stacked)
 
 
-def back_kernel(base_ref, ortho_t_ref, *refs):
-    *columns, colsq_ref, back_ref, whole_ref, corner_ref = refs
-    corner_ref[...] = base_ref[:SUBLANES, :LANES]
-    me = lax.axis_index("fsdp") if len(columns) > 1 else 0
-    rows = columns[0].shape[0]
-    for n, piece in enumerate(columns):
-        whole_ref[pl.ds(pl.multiple_of((me ^ n) * rows, 16), rows), :] = piece[...]
-    back_t = jnp.dot(ortho_t_ref[...], whole_ref[...], preferred_element_type=F32)
-    back = back_t.T.astype(BF16)
-    back_ref[...] = back
-    wide = back.astype(F32)
-    colsq_ref[...] = jnp.sum(wide * wide, axis=0, keepdims=True)
-
-
-def back_call(base, ortho_t, columns):
-    rank, total = ortho_t.shape
-    share = columns[0].shape[1]
+def half_kernel(share, ortho_t_ref, *refs):
+    *near, mine_ref, theirs_ref, rows_ref = refs
+    me = lax.axis_index("fsdp")
+    rows, half = near[0].shape[0], len(near)
+    for n, piece in enumerate(near):
+        at = pl.ds(pl.multiple_of(((me ^ n) & (half - 1)) * rows, 16), rows)
+        rows_ref[at, :] = piece[:, share - SPLIT :]
+    first = pl.multiple_of((me & half) * rows, LANES)
+    ortho_t = ortho_t_ref[:, pl.ds(first, half * rows)]
+    back = jnp.dot(ortho_t, rows_ref[...], preferred_element_type=F32).T
+    mine_ref[...] = back[:SPLIT]
+    theirs_ref[...] = back[SPLIT:].astype(BF16)
+
+
+def half_call(ortho_t, near, share):
+    rank = ortho_t.shape[0]
+    rows = near[0].shape[0] * len(near)
     vmem = pl.BlockSpec(memory_space=pltpu.VMEM)
     return pl.pallas_call(
-        back_kernel,
-        in_specs=[vmem] * (2 + len(columns)),
+        functools.partial(half_kernel, share),
+        in_specs=[vmem] * (1 + len(near)),
+        out_specs=[vmem] * 2,
+        out_shape=[
+            jax.ShapeDtypeStruct((SPLIT, rank), F32),
+            jax.ShapeDtypeStruct((SPLIT, rank), BF16),
+        ],
+        scratch_shapes=[pltpu.VMEM((rows, 2 * SPLIT), BF16)],
+        compiler_params=params(16),
+        cost_estimate=cost(4 * rank * rows * SPLIT, rows * SPLIT * 4),
+        name="half_back",
+    )(ortho_t, *near)
+
+
+def back_kernel(pieces, base_ref, ortho_t_ref, *refs):
+    columns, (*sums, colsq_ref, back_ref, whole_ref, corner_ref) = refs[:pieces], refs[pieces:]
+    corner_ref[...] = base_ref[:SUBLANES, :LANES]
+    me = lax.axis_index("fsdp") if pieces > 1 else 0
+    rows, width = columns[0].shape[0], whole_ref.shape[1]
+    for n, piece in enumerate(columns):
+        at = pl.ds(pl.multiple_of((me ^ n) * rows, 16), rows)
+        whole_ref[at, :] = piece[:, :width]
+    back_t = jnp.dot(ortho_t_ref[...], whole_ref[...], preferred_element_type=F32)
+    back_ref[:width, :] = back_t.T.astype(BF16)
+    if sums:
+        mine_ref, other_ref = sums
+        back_ref[width:, :] = (mine_ref[...] + other_ref[...].astype(F32)).astype(BF16)
+    wide = back_ref[...].astype(F32)
+    colsq_ref[...] = jnp.sum(wide * wide, axis=0, keepdims=True)
+
+
+def back_call(base, ortho_t, columns, share, sums=()):
+    rank, total = ortho_t.shape
+    width = share - (SPLIT if sums else 0)
+    vmem = pl.BlockSpec(memory_space=pltpu.VMEM)
+    return pl.pallas_call(
+        functools.partial(back_kernel, len(columns)),
+        in_specs=[vmem] * (2 + len(columns) + len(sums)),
         out_specs=[vmem] * 2,
         out_shape=[
             jax.ShapeDtypeStruct((1, rank), F32),
             jax.ShapeDtypeStruct((share, rank), BF16),
         ],
-        scratch_shapes=[pltpu.VMEM((total, share), BF16), pltpu.VMEM((SUBLANES, LANES), F32)],
+        scratch_shapes=[pltpu.VMEM((total, width), BF16), pltpu.VMEM((SUBLANES, LANES), F32)],
         compiler_params=params(24),
-        cost_estimate=cost(2 * rank * total * share, total * share * 2),
+        cost_estimate=cost(2 * rank * total * width, total * width * 2),
         name="back",
-    )(base, ortho_t, *columns)
+    )(base, ortho_t, *columns, *sums)
 
 
 def output_kernel(owner, factor, base_ref, ortho_ref, colsq_ref, *refs):
@@ -397,7 +451,7 @@
     chips = count // 2
     share = -(-cols // (count * LANES)) * LANES
     factor = math.sqrt(rows * count * cols * tp_count / rank)
-    ring = tp_count == 2 and count in (16, 32) and (count - 1) * share < cols
+    ring = tp_count == 2 and count in (16, 32) and share > SPLIT and (count - 1) * share < cols
 
     base = momentum + gradient.astype(F32)
     base_b = base.astype(BF16)
@@ -415,7 +469,12 @@
         pieces = [lax.all_gather(lax.psum(sketch, "tp"), "fsdp", axis=0)]
         owner = lambda me, n: n
     ortho_t, ortho_here = factor_call(owner, base, pieces)
-    part, back = back_call(base, ortho_t, columns)
+    sums = ()
+    if ring:
+        mine, theirs = half_call(ortho_t, columns[:chips], share)
+        theirs = tie(theirs, *columns[chips:])
+        sums = (mine, lax.ppermute(theirs, "fsdp", [(n, n ^ chips) for n in range(count)]))
+    part, back = back_call(base, ortho_t, columns, share, sums)
     write = functools.partial(output_call, base=base, ortho=ortho_here, factor=factor)
     if not ring:
         whole = lax.all_gather(back, "fsdp", axis=0)
@@ -424,9 +483,11 @@
         return tuple(write(lambda me, n: n, blocks, colsq, None))
 
     turns, swap = ring_steps(count), swap_pairs(count)
-    colsq, result = part, None
+    result = None
+    partial = [part]
     for axis, distances in sum_rounds(count):
-        colsq = sum_round(colsq, axis, distances)
+        partial.append(sum_round(partial[-1], axis, distances))
+    colsq = partial[-1]
     arrived, blocks, owners, written = {0: back}, [], [], 0
     waiting = ()
     for n in range(chips):
@@ -438,7 +499,7 @@
         hops = (n + 1) // 2 if n % 2 else -(n // 2)
         owners += [functools.partial(ring_owner, count, hops, far) for far in (False, True)]
         if n == 0:
-            waiting = (arrived[2], colsq)
+            waiting = (arrived[2], partial[-2])
             continue
         if n == 2:
             waiting = ()

time: 138 us -> 153 us (1.11)
  waiting for transfers between devices: 40.4 us -> 60.7 us
  starting transfers between devices: 61.3 us -> 54.8 us
    ppermute x0 -> x1, waiting for transfers between devices: none -> 11.7 us  [local(): lax.ppermute(theirs, 'fsdp', [(n, n ^ chips) for n in range(count)])]
    ppermute x7, starting transfers between devices: 12.4 us -> 1.59 us  [local(): arrived[later] = lax.ppermute(block, 'fsdp', turns[(later + 1) % 2])]
    ppermute x7, waiting for transfers between devices: 7.38 us -> 17.3 us  [sum_round(): terms.append(lax.ppermute(x, axis, [(n, n ^ d) for n in range(size)]))]
    ppermute x15, waiting for transfers between devices: 14.3 us -> 4.84 us  [exchange(): columns[k] = lax.ppermute(tie(outgoing[k], *after), 'fsdp', pairs)]
    ppermute x4, waiting for transfers between devices: 7.97 us -> 14.1 us  [gather_and_exchange(): ahead = lax.ppermute(ahead, 'fsdp', first)]
    ppermute x8, starting transfers between devices: 6.88 us -> 10.9 us  [local(): blocks += [block, lax.ppermute(block, 'fsdp', swap)]]
    ppermute x15, starting transfers between devices: 23 us -> 25.9 us  [exchange(): columns[k] = lax.ppermute(tie(outgoing[k], *after), 'fsdp', pairs)]
    ppermute x3, waiting for transfers between devices: 0.01 us -> 2.83 us  [gather_and_exchange(): behind = lax.ppermute(behind, 'fsdp', second)]
  transfers between devices with their start and end apart: 46 -> 47, of which waited for: 17 -> 12; matrix products, arithmetic and copies ran while one was open for 0% -> 0% of each run, Pallas kernels for 19% -> 18%
where the time goes in v13:
time: 153 us; the launch traced here: 152 us
  waiting for transfers between devices  60.7 us (40%)
  starting transfers between devices  54.8 us (36%)
  Pallas kernels  29 us (19%)
  other arithmetic  3.98 us (3%)
    ppermute x15, starting transfers between devices, exchange(): columns[k] = lax.ppermute(tie(outgoing[k], *after), 'fsdp', pairs)  25.9 us
    ppermute x7, waiting for transfers between devices, sum_round(): terms.append(lax.ppermute(x, axis, [(n, n ^ d) for n in range(size)]))  17.3 us
    pallas_call x1, Pallas kernels, factor_call(): pl.pallas_call(functools.partial(factor_kernel, len(stacked), owner), in_...  14.2 us
    ppermute x4, waiting for transfers between devices, gather_and_exchange(): ahead = lax.ppermute(ahead, 'fsdp', first)  14.1 us
    pallas_call x7, Pallas kernels, output_call(): pl.pallas_call(functools.partial(output_kernel, owner, factor), in_specs=...  12.7 us
    ppermute x1, waiting for transfers between devices, local(): lax.ppermute(theirs, 'fsdp', [(n, n ^ chips) for n in range(count)])  11.7 us
    ppermute x8, starting transfers between devices, local(): blocks += [block, lax.ppermute(block, 'fsdp', swap)]  10.9 us
    ppermute x7, waiting for transfers between devices, local(): arrived[later] = lax.ppermute(block, 'fsdp', turns[(later + 1) % 2])  9.84 us
  transfers between devices with their start and end apart: 47, of which 12 were waited for; matrix products, arithmetic and copies ran while one was open for 0% of the time, Pallas kernels for 18%

profile of v13, /device:TPU:1, one launch (start us, length us, event | category | flops | bytes accessed | tf_op | source)
XLA Modules:
  0.0 152.3 jit_solution(4475897977868687450)
XLA Ops:
  0.6 4.0 %convert_add_fusion.base_ref = f32[96,13824]{1,0:T(8,128)S(1)} fusion(f32[96,13824]{1,0:T(8,128)} %param.3, bf16[96,13824]{1,0:T(8,128)(2,1)} %param.4), kind=kLoop, calls=%fused_computation | loop fusion | flops 2654208 | bytes 13271040 | tf_op jit(solution)/shard_map/add | solution.py:456
  9.9 2.4 %collective-permute-start.3 = (bf16[96,512]{1,0:T(8,128)(2,1)S(1)}, bf16[96,512]{1,0:T(8,128)(2,1)S(1)}, u32[]{:S(2)}, u32[]{:S(2)}) collective-permute-start(bf16[96,512]{1,0:T(8,128)(2,1)S(1)} %get-tuple-element.77), channel_id=1, source_target_pairs={{0,16},{2,18},{4,20},{6,22},{8,24},{10,26},{12,28},{14,30},{16,0},... | collective-permute-start | bytes 294920 | tf_op jit(solution)/shard_map/ppermute | solution.py:404
  18.1 2.3 %collective-permute-start.9 = (bf16[96,1280]{1,0:T(8,128)(2,1)S(1)}, bf16[96,1280]{1,0:T(8,128)(2,1)S(1)}, u32[]{:S(2)}, u32[]{:S(2)}) collective-permute-start(bf16[96,1280]{1,0:T(8,128)(2,1)S(1)} %get-tuple-element.87), channel_id=1, source_target_pairs={{0,6},{2,4},{4,2},{6,0},{8,14},{10,12},{12,10},{14,8},{16,22},{18,... | collective-permute-start | bytes 737288 | tf_op jit(solution)/shard_map/ppermute | solution.py:404
  20.4 2.8 %collective-permute-done.2 = f32[96,256]{1,0:T(8,128)S(1)} collective-permute-done((f32[96,256]{1,0:T(8,128)S(1)}, f32[96,256]{1,0:T(8,128)S(1)}, u32[]{:S(2)}, u32[]{:S(2)}) %collective-permute-start.2) | collective-permute-done | bytes 98336 | tf_op jit(solution)/shard_map/ppermute | solution.py:418
  25.8 4.8 %collective-permute-done.8.refs_9_ = bf16[96,512]{1,0:T(8,128)(2,1)S(1)} collective-permute-done((bf16[96,512]{1,0:T(8,128)(2,1)S(1)}, bf16[96,512]{1,0:T(8,128)(2,1)S(1)}, u32[]{:S(2)}, u32[]{:S(2)}) %collective-permute-start.8) | collective-permute-done | bytes 98336 | tf_op jit(solution)/shard_map/ppermute | solution.py:404
  30.6 3.1 %collective-permute-start.14 = (bf16[96,1280]{1,0:T(8,128)(2,1)S(1)}, bf16[96,1280]{1,0:T(8,128)(2,1)S(1)}, u32[]{:S(2)}, u32[]{:S(2)}) collective-permute-start(bf16[96,1280]{1,0:T(8,128)(2,1)S(1)} %get-tuple-element.95), channel_id=1, source_target_pairs={{0,10},{2,8},{4,14},{6,12},{8,2},{10,0},{12,6},{14,4},{16,26},{18,... | collective-permute-start | bytes 737288 | tf_op jit(solution)/shard_map/ppermute | solution.py:404
  35.7 6.8 %collective-permute-done.11 = f32[96,256]{1,0:T(8,128)S(1)} collective-permute-done((f32[96,256]{1,0:T(8,128)S(1)}, f32[96,256]{1,0:T(8,128)S(1)}, u32[]{:S(2)}, u32[]{:S(2)}) %collective-permute-start.11) | collective-permute-done | bytes 98336 | tf_op jit(solution)/shard_map/ppermute | solution.py:414
  42.5 4.7 %collective-permute-start.18 = (bf16[96,1280]{1,0:T(8,128)(2,1)S(1)}, bf16[96,1280]{1,0:T(8,128)(2,1)S(1)}, u32[]{:S(2)}, u32[]{:S(2)}) collective-permute-start(bf16[96,1280]{1,0:T(8,128)(2,1)S(1)} %get-tuple-element.102), channel_id=1, source_target_pairs={{0,14},{2,12},{4,10},{6,8},{8,6},{10,4},{12,2},{14,0},{16,30},{18,... | collective-permute-start | bytes 737288 | tf_op jit(solution)/shard_map/ppermute | solution.py:404
  50.2 7.3 %collective-permute-done.16 = f32[96,256]{1,0:T(8,128)S(1)} collective-permute-done((f32[96,256]{1,0:T(8,128)S(1)}, f32[96,256]{1,0:T(8,128)S(1)}, u32[]{:S(2)}, u32[]{:S(2)}) %collective-permute-start.16) | collective-permute-done | bytes 98336 | tf_op jit(solution)/shard_map/ppermute | solution.py:414
  57.7 2.2 %collective-permute-start.20 = (bf16[96,512]{1,0:T(8,128)(2,1)S(1)}, bf16[96,512]{1,0:T(8,128)(2,1)S(1)}, u32[]{:S(2)}, u32[]{:S(2)}) collective-permute-start(bf16[96,512]{1,0:T(8,128)(2,1)S(1)} %get-tuple-element.109), channel_id=1, source_target_pairs={{0,24},{2,26},{4,28},{6,30},{8,16},{10,18},{12,20},{14,22},{16,8},... | collective-permute-start | bytes 294920 | tf_op jit(solution)/shard_map/ppermute | solution.py:404
  59.9 2.5 %collective-permute-start.23 = (bf16[96,512]{1,0:T(8,128)(2,1)S(1)}, bf16[96,512]{1,0:T(8,128)(2,1)S(1)}, u32[]{:S(2)}, u32[]{:S(2)}) collective-permute-start(bf16[96,512]{1,0:T(8,128)(2,1)S(1)} %get-tuple-element.115), channel_id=1, source_target_pairs={{0,30},{2,28},{4,26},{6,24},{8,22},{10,20},{12,18},{14,16},{16,14}... | collective-permute-start | bytes 294920 | tf_op jit(solution)/shard_map/ppermute | solution.py:404
  62.4 2.3 %collective-permute-start.22 = (bf16[96,512]{1,0:T(8,128)(2,1)S(1)}, bf16[96,512]{1,0:T(8,128)(2,1)S(1)}, u32[]{:S(2)}, u32[]{:S(2)}) collective-permute-start(bf16[96,512]{1,0:T(8,128)(2,1)S(1)} %get-tuple-element.113), channel_id=1, source_target_pairs={{0,28},{2,30},{4,24},{6,26},{8,20},{10,22},{12,16},{14,18},{16,12}... | collective-permute-start | bytes 294920 | tf_op jit(solution)/shard_map/ppermute | solution.py:404
  65.7 14.2 %factor.1 = (bf16[256,1536]{1,0:T(8,128)(2,1)S(1)}, bf16[96,256]{1,0:T(8,128)(2,1)S(1)}) custom-call(f32[96,13824]{1,0:T(8,128)S(1)} %convert_add_fusion.base_ref, f32[8,96,256]{2,1,0:T(8,128)S(1)} %bitcast_dynamic-update-slice_fusion.refs_0_, f32[8,96,256]{2,1,0:T(8,128)S(1)} %collective-permute-done.19.refs_1_), custom_call_target="tpu_custom_call" | custom-call | flops 4026531840 | bytes 2359296 | tf_op jit(solution)/shard_map/factor/pallas_call | solution.py:184
  80.8 11.7 %collective-permute-done.24.refs_17_ = bf16[384,256]{1,0:T(8,128)(2,1)S(1)} collective-permute-done((bf16[384,256]{1,0:T(8,128)(2,1)S(1)}, bf16[384,256]{1,0:T(8,128)(2,1)S(1)}, u32[]{:S(2)}, u32[]{:S(2)}) %collective-permute-start.24) | collective-permute-done | bytes 196640 | tf_op jit(solution)/shard_map/ppermute | solution.py:476
  101.3 5.4 %collective-permute-done.27 = f32[1,256]{1,0:T(1,128)S(1)} collective-permute-done((f32[1,256]{1,0:T(1,128)S(1)}, f32[1,256]{1,0:T(1,128)S(1)}, u32[]{:S(2)}, u32[]{:S(2)}) %collective-permute-start.27) | collective-permute-done | bytes 1056 | tf_op jit(solution)/shard_map/ppermute | solution.py:440
  108.8 6.2 %collective-permute-done.29 = f32[1,256]{1,0:T(1,128)S(1)} collective-permute-done((f32[1,256]{1,0:T(1,128)S(1)}, f32[1,256]{1,0:T(1,128)S(1)}, u32[]{:S(2)}, u32[]{:S(2)}) %collective-permute-start.29) | collective-permute-done | bytes 1056 | tf_op jit(solution)/shard_map/ppermute | solution.py:440
  115.0 4.2 %collective-permute-done.31 = f32[1,256]{1,0:T(1,128)S(1)} collective-permute-done((f32[1,256]{1,0:T(1,128)S(1)}, f32[1,256]{1,0:T(1,128)S(1)}, u32[]{:S(2)}, u32[]{:S(2)}) %collective-permute-start.31) | collective-permute-done | bytes 1056 | tf_op jit(solution)/shard_map/ppermute | solution.py:440
  119.2 2.8 %outputs.7 = (f32[96,13824]{1,0:T(8,128)}, bf16[13824,256]{1,0:T(8,128)(2,1)}, bf16[96,13824]{1,0:T(8,128)(2,1)}) custom-call(f32[96,13824]{1,0:T(8,128)S(1)} %convert_add_fusion.base_ref, bf16[96,256]{1,0:T(8,128)(2,1)S(1)} %get-tuple-element.104.ortho_ref, f32[1,256]{1,0:T(1,128)S(1)} %add_add_fusion.colsq_ref, ...), custom_call_target="tpu_custom_call" | custom-call | flops 352321536 | bytes 7110656 | tf_op jit(solution)/shard_map/outputs/pallas_call | solution.py:325
  122.2 2.4 %collective-permute-start.36 = (bf16[896,256]{1,0:T(8,128)(2,1)S(1)}, bf16[896,256]{1,0:T(8,128)(2,1)S(1)}, u32[]{:S(2)}, u32[]{:S(2)}) collective-permute-start(bf16[896,256]{1,0:T(8,128)(2,1)S(1)} %collective-permute-done.34.refs_0_), channel_id=1, source_target_pairs={{0,2},{2,0},{4,6},{6,4},{8,10},{10,8},{12,14},{14,12},{16,18},{18,... | collective-permute-start | bytes 1376264 | tf_op jit(solution)/shard_map/ppermute | solution.py:498
  126.3 6.7 %collective-permute-done.42.refs_0_ = bf16[896,256]{1,0:T(8,128)(2,1)S(1)} collective-permute-done((bf16[896,256]{1,0:T(8,128)(2,1)S(1)}, bf16[896,256]{1,0:T(8,128)(2,1)S(1)}, u32[]{:S(2)}, u32[]{:S(2)}) %collective-permute-start.42) | collective-permute-done | bytes 458784 | tf_op jit(solution)/shard_map/ppermute | solution.py:497
  132.9 2.4 %collective-permute-start.43 = (bf16[896,256]{1,0:T(8,128)(2,1)S(1)}, bf16[896,256]{1,0:T(8,128)(2,1)S(1)}, u32[]{:S(2)}, u32[]{:S(2)}) collective-permute-start(bf16[896,256]{1,0:T(8,128)(2,1)S(1)} %collective-permute-done.42.refs_0_), channel_id=1, source_target_pairs={{0,2},{2,0},{4,6},{6,4},{8,10},{10,8},{12,14},{14,12},{16,18},{18,... | collective-permute-start | bytes 1376264 | tf_op jit(solution)/shard_map/ppermute | solution.py:498
  137.0 2.5 %collective-permute-start.41 = (bf16[896,256]{1,0:T(8,128)(2,1)S(1)}, bf16[896,256]{1,0:T(8,128)(2,1)S(1)}, u32[]{:S(2)}, u32[]{:S(2)}) collective-permute-start(bf16[896,256]{1,0:T(8,128)(2,1)S(1)} %collective-permute-done.35.refs_0_), channel_id=1, source_target_pairs={{0,2},{2,0},{4,6},{6,4},{8,10},{10,8},{12,14},{14,12},{16,18},{18,... | collective-permute-start | bytes 1376264 | tf_op jit(solution)/shard_map/ppermute | solution.py:498
  141.3 3.2 %collective-permute-done.45.refs_0_ = bf16[896,256]{1,0:T(8,128)(2,1)S(1)} collective-permute-done((bf16[896,256]{1,0:T(8,128)(2,1)S(1)}, bf16[896,256]{1,0:T(8,128)(2,1)S(1)}, u32[]{:S(2)}, u32[]{:S(2)}) %collective-permute-start.45) | collective-permute-done | bytes 458784 | tf_op jit(solution)/shard_map/ppermute | solution.py:497
  144.4 2.6 %collective-permute-start.46 = (bf16[896,256]{1,0:T(8,128)(2,1)S(1)}, bf16[896,256]{1,0:T(8,128)(2,1)S(1)}, u32[]{:S(2)}, u32[]{:S(2)}) collective-permute-start(bf16[896,256]{1,0:T(8,128)(2,1)S(1)} %collective-permute-done.45.refs_0_), channel_id=1, source_target_pairs={{0,2},{2,0},{4,6},{6,4},{8,10},{10,8},{12,14},{14,12},{16,18},{18,... | collective-permute-start | bytes 1376264 | tf_op jit(solution)/shard_map/ppermute | solution.py:498
  (96 shorter events, 41.9 us)
Async XLA Ops:
  13.5 9.7 %collective-permute-start.5 = (bf16[96,1280]{1,0:T(8,128)(2,1)S(1)}, bf16[96,1280]{1,0:T(8,128)(2,1)S(1)}, u32[]{:S(2)}, u32[]{:S(2)}) collective-permute-start(bf16[96,1280]{1,0:T(8,128)(2,1)S(1)} %get-tuple-element.81), channel_id=1, source_target_pairs={{0,4},{2,6},{4,0},{6,2},{8,12},{10,14},{12,8},{14,10},{16,20},{18,... | collective-permute-start | bytes 737288 | tf_op jit(solution)/shard_map/ppermute | solution.py:404
  16.8 17.4 %collective-permute-start.10 = (bf16[96,1280]{1,0:T(8,128)(2,1)S(1)}, bf16[96,1280]{1,0:T(8,128)(2,1)S(1)}, u32[]{:S(2)}, u32[]{:S(2)}) collective-permute-start(bf16[96,1280]{1,0:T(8,128)(2,1)S(1)} %get-tuple-element.89), channel_id=1, source_target_pairs={{0,8},{2,10},{4,12},{6,14},{8,0},{10,2},{12,4},{14,6},{16,24},{18,... | collective-permute-start | bytes 737288 | tf_op jit(solution)/shard_map/ppermute | solution.py:404
  18.1 16.1 %collective-permute-start.9 = (bf16[96,1280]{1,0:T(8,128)(2,1)S(1)}, bf16[96,1280]{1,0:T(8,128)(2,1)S(1)}, u32[]{:S(2)}, u32[]{:S(2)}) collective-permute-start(bf16[96,1280]{1,0:T(8,128)(2,1)S(1)} %get-tuple-element.87), channel_id=1, source_target_pairs={{0,6},{2,4},{4,2},{6,0},{8,14},{10,12},{12,10},{14,8},{16,22},{18,... | collective-permute-start | bytes 737288 | tf_op jit(solution)/shard_map/ppermute | solution.py:404
  23.7 10.0 %collective-permute-start.7 = (f32[96,256]{1,0:T(8,128)S(1)}, f32[96,256]{1,0:T(8,128)S(1)}, u32[]{:S(2)}, u32[]{:S(2)}) collective-permute-start(f32[96,256]{1,0:T(8,128)S(1)} %collective-permute-done.2), channel_id=1, source_target_pairs={{8,0},{16,8},{24,16},{28,24},{20,28},{12,20},{4,12},{0,4},{2,10},{... | collective-permute-start | bytes 294920 | tf_op jit(solution)/shard_map/ppermute | solution.py:418
  30.6 18.3 %collective-permute-start.15 = (bf16[96,1280]{1,0:T(8,128)(2,1)S(1)}, bf16[96,1280]{1,0:T(8,128)(2,1)S(1)}, u32[]{:S(2)}, u32[]{:S(2)}) collective-permute-start(bf16[96,1280]{1,0:T(8,128)(2,1)S(1)} %get-tuple-element.97), channel_id=1, source_target_pairs={{0,12},{2,14},{4,8},{6,10},{8,4},{10,6},{12,0},{14,2},{16,28},{18,... | collective-permute-start | bytes 737288 | tf_op jit(solution)/shard_map/ppermute | solution.py:404
  30.6 18.3 %collective-permute-start.14 = (bf16[96,1280]{1,0:T(8,128)(2,1)S(1)}, bf16[96,1280]{1,0:T(8,128)(2,1)S(1)}, u32[]{:S(2)}, u32[]{:S(2)}) collective-permute-start(bf16[96,1280]{1,0:T(8,128)(2,1)S(1)} %get-tuple-element.95), channel_id=1, source_target_pairs={{0,10},{2,8},{4,14},{6,12},{8,2},{10,0},{12,6},{14,4},{16,26},{18,... | collective-permute-start | bytes 737288 | tf_op jit(solution)/shard_map/ppermute | solution.py:404
  33.7 13.5 %collective-permute-start.13 = (bf16[96,512]{1,0:T(8,128)(2,1)S(1)}, bf16[96,512]{1,0:T(8,128)(2,1)S(1)}, u32[]{:S(2)}, u32[]{:S(2)}) collective-permute-start(bf16[96,512]{1,0:T(8,128)(2,1)S(1)} %get-tuple-element.93), channel_id=1, source_target_pairs={{0,20},{2,22},{4,16},{6,18},{8,28},{10,30},{12,24},{14,26},{16,4},... | collective-permute-start | bytes 294920 | tf_op jit(solution)/shard_map/ppermute | solution.py:404
  34.2 14.7 %collective-permute-start.12 = (f32[96,256]{1,0:T(8,128)S(1)}, f32[96,256]{1,0:T(8,128)S(1)}, u32[]{:S(2)}, u32[]{:S(2)}) collective-permute-start(f32[96,256]{1,0:T(8,128)S(1)} %collective-permute-done.7), channel_id=1, source_target_pairs={{8,0},{16,8},{24,16},{28,24},{20,28},{12,20},{4,12},{0,4},{2,10},{... | collective-permute-start | bytes 294920 | tf_op jit(solution)/shard_map/ppermute | solution.py:418
  42.5 15.0 %collective-permute-start.18 = (bf16[96,1280]{1,0:T(8,128)(2,1)S(1)}, bf16[96,1280]{1,0:T(8,128)(2,1)S(1)}, u32[]{:S(2)}, u32[]{:S(2)}) collective-permute-start(bf16[96,1280]{1,0:T(8,128)(2,1)S(1)} %get-tuple-element.102), channel_id=1, source_target_pairs={{0,14},{2,12},{4,10},{6,8},{8,6},{10,4},{12,2},{14,0},{16,30},{18,... | collective-permute-start | bytes 737288 | tf_op jit(solution)/shard_map/ppermute | solution.py:404
  47.3 10.2 %collective-permute-start.17 = (bf16[96,512]{1,0:T(8,128)(2,1)S(1)}, bf16[96,512]{1,0:T(8,128)(2,1)S(1)}, u32[]{:S(2)}, u32[]{:S(2)}) collective-permute-start(bf16[96,512]{1,0:T(8,128)(2,1)S(1)} %get-tuple-element.100), channel_id=1, source_target_pairs={{0,22},{2,20},{4,18},{6,16},{8,30},{10,28},{12,26},{14,24},{16,6},... | collective-permute-start | bytes 294920 | tf_op jit(solution)/shard_map/ppermute | solution.py:404
  57.7 22.9 %collective-permute-start.20 = (bf16[96,512]{1,0:T(8,128)(2,1)S(1)}, bf16[96,512]{1,0:T(8,128)(2,1)S(1)}, u32[]{:S(2)}, u32[]{:S(2)}) collective-permute-start(bf16[96,512]{1,0:T(8,128)(2,1)S(1)} %get-tuple-element.109), channel_id=1, source_target_pairs={{0,24},{2,26},{4,28},{6,30},{8,16},{10,18},{12,20},{14,22},{16,8},... | collective-permute-start | bytes 294920 | tf_op jit(solution)/shard_map/ppermute | solution.py:404
  59.9 20.8 %collective-permute-start.23 = (bf16[96,512]{1,0:T(8,128)(2,1)S(1)}, bf16[96,512]{1,0:T(8,128)(2,1)S(1)}, u32[]{:S(2)}, u32[]{:S(2)}) collective-permute-start(bf16[96,512]{1,0:T(8,128)(2,1)S(1)} %get-tuple-element.115), channel_id=1, source_target_pairs={{0,30},{2,28},{4,26},{6,24},{8,22},{10,20},{12,18},{14,16},{16,14}... | collective-permute-start | bytes 294920 | tf_op jit(solution)/shard_map/ppermute | solution.py:404
  62.4 18.3 %collective-permute-start.22 = (bf16[96,512]{1,0:T(8,128)(2,1)S(1)}, bf16[96,512]{1,0:T(8,128)(2,1)S(1)}, u32[]{:S(2)}, u32[]{:S(2)}) collective-permute-start(bf16[96,512]{1,0:T(8,128)(2,1)S(1)} %get-tuple-element.113), channel_id=1, source_target_pairs={{0,28},{2,30},{4,24},{6,26},{8,20},{10,22},{12,16},{14,18},{16,12}... | collective-permute-start | bytes 294920 | tf_op jit(solution)/shard_map/ppermute | solution.py:404
  64.6 16.0 %collective-permute-start.21 = (bf16[96,512]{1,0:T(8,128)(2,1)S(1)}, bf16[96,512]{1,0:T(8,128)(2,1)S(1)}, u32[]{:S(2)}, u32[]{:S(2)}) collective-permute-start(bf16[96,512]{1,0:T(8,128)(2,1)S(1)} %get-tuple-element.111), channel_id=1, source_target_pairs={{0,26},{2,24},{4,30},{6,28},{8,18},{10,16},{12,22},{14,20},{16,10}... | collective-permute-start | bytes 294920 | tf_op jit(solution)/shard_map/ppermute | solution.py:404
  80.7 11.8 %collective-permute-start.24 = (bf16[384,256]{1,0:T(8,128)(2,1)S(1)}, bf16[384,256]{1,0:T(8,128)(2,1)S(1)}, u32[]{:S(2)}, u32[]{:S(2)}) collective-permute-start(bf16[384,256]{1,0:T(8,128)(2,1)S(1)} %get-tuple-element.118), channel_id=1, source_target_pairs={{0,16},{2,18},{4,20},{6,22},{8,24},{10,26},{12,28},{14,30},{16,0},... | collective-permute-start | bytes 589832 | tf_op jit(solution)/shard_map/ppermute | solution.py:476
  93.3 13.5 %collective-permute-start.32 = (bf16[896,256]{1,0:T(8,128)(2,1)S(1)}, bf16[896,256]{1,0:T(8,128)(2,1)S(1)}, u32[]{:S(2)}, u32[]{:S(2)}) collective-permute-start(bf16[896,256]{1,0:T(8,128)(2,1)S(1)} %get-tuple-element.120.refs_0_), channel_id=1, source_target_pairs={{0,8},{8,16},{16,24},{24,28},{28,20},{20,12},{12,4},{4,0},{10,2},{... | collective-permute-start | bytes 1376264 | tf_op jit(solution)/shard_map/ppermute | solution.py:497
  94.2 12.6 %collective-permute-start.33 = (bf16[896,256]{1,0:T(8,128)(2,1)S(1)}, bf16[896,256]{1,0:T(8,128)(2,1)S(1)}, u32[]{:S(2)}, u32[]{:S(2)}) collective-permute-start(bf16[896,256]{1,0:T(8,128)(2,1)S(1)} %get-tuple-element.120.refs_0_), channel_id=1, source_target_pairs={{8,0},{16,8},{24,16},{28,24},{20,28},{12,20},{4,12},{0,4},{2,10},{... | collective-permute-start | bytes 1376264 | tf_op jit(solution)/shard_map/ppermute | solution.py:497
  101.1 18.1 %collective-permute-start.37 = (bf16[896,256]{1,0:T(8,128)(2,1)S(1)}, bf16[896,256]{1,0:T(8,128)(2,1)S(1)}, u32[]{:S(2)}, u32[]{:S(2)}) collective-permute-start(bf16[896,256]{1,0:T(8,128)(2,1)S(1)} %get-tuple-element.120.refs_0_), channel_id=1, source_target_pairs={{0,2},{2,0},{4,6},{6,4},{8,10},{10,8},{12,14},{14,12},{16,18},{18,... | collective-permute-start | bytes 1376264 | tf_op jit(solution)/shard_map/ppermute | solution.py:498
  106.8 12.4 %collective-permute-start.38 = (bf16[896,256]{1,0:T(8,128)(2,1)S(1)}, bf16[896,256]{1,0:T(8,128)(2,1)S(1)}, u32[]{:S(2)}, u32[]{:S(2)}) collective-permute-start(bf16[896,256]{1,0:T(8,128)(2,1)S(1)} %collective-permute-done.32.refs_2_), channel_id=1, source_target_pairs={{0,2},{2,0},{4,6},{6,4},{8,10},{10,8},{12,14},{14,12},{16,18},{18,... | collective-permute-start | bytes 1376264 | tf_op jit(solution)/shard_map/ppermute | solution.py:498
  107.3 14.8 %collective-permute-start.34 = (bf16[896,256]{1,0:T(8,128)(2,1)S(1)}, bf16[896,256]{1,0:T(8,128)(2,1)S(1)}, u32[]{:S(2)}, u32[]{:S(2)}) collective-permute-start(bf16[896,256]{1,0:T(8,128)(2,1)S(1)} %collective-permute-done.32.refs_2_), channel_id=1, source_target_pairs={{0,8},{8,16},{16,24},{24,28},{28,20},{20,12},{12,4},{4,0},{10,2},{... | collective-permute-start | bytes 1376264 | tf_op jit(solution)/shard_map/ppermute | solution.py:497
  122.1 10.8 %collective-permute-start.42 = (bf16[896,256]{1,0:T(8,128)(2,1)S(1)}, bf16[896,256]{1,0:T(8,128)(2,1)S(1)}, u32[]{:S(2)}, u32[]{:S(2)}) collective-permute-start(bf16[896,256]{1,0:T(8,128)(2,1)S(1)} %collective-permute-done.33.refs_0_), channel_id=1, source_target_pairs={{8,0},{16,8},{24,16},{28,24},{20,28},{12,20},{4,12},{0,4},{2,10},{... | collective-permute-start | bytes 1376264 | tf_op jit(solution)/shard_map/ppermute | solution.py:497
  122.2 13.1 %collective-permute-start.36 = (bf16[896,256]{1,0:T(8,128)(2,1)S(1)}, bf16[896,256]{1,0:T(8,128)(2,1)S(1)}, u32[]{:S(2)}, u32[]{:S(2)}) collective-permute-start(bf16[896,256]{1,0:T(8,128)(2,1)S(1)} %collective-permute-done.34.refs_0_), channel_id=1, source_target_pairs={{0,2},{2,0},{4,6},{6,4},{8,10},{10,8},{12,14},{14,12},{16,18},{18,... | collective-permute-start | bytes 1376264 | tf_op jit(solution)/shard_map/ppermute | solution.py:498
  124.5 12.5 %collective-permute-start.35 = (bf16[896,256]{1,0:T(8,128)(2,1)S(1)}, bf16[896,256]{1,0:T(8,128)(2,1)S(1)}, u32[]{:S(2)}, u32[]{:S(2)}) collective-permute-start(bf16[896,256]{1,0:T(8,128)(2,1)S(1)} %collective-permute-done.34.refs_0_), channel_id=1, source_target_pairs={{0,8},{8,16},{16,24},{24,28},{28,20},{20,12},{12,4},{4,0},{10,2},{... | collective-permute-start | bytes 1376264 | tf_op jit(solution)/shard_map/ppermute | solution.py:497
  137.0 10.0 %collective-permute-start.41 = (bf16[896,256]{1,0:T(8,128)(2,1)S(1)}, bf16[896,256]{1,0:T(8,128)(2,1)S(1)}, u32[]{:S(2)}, u32[]{:S(2)}) collective-permute-start(bf16[896,256]{1,0:T(8,128)(2,1)S(1)} %collective-permute-done.35.refs_0_), channel_id=1, source_target_pairs={{0,2},{2,0},{4,6},{6,4},{8,10},{10,8},{12,14},{14,12},{16,18},{18,... | collective-permute-start | bytes 1376264 | tf_op jit(solution)/shard_map/ppermute | solution.py:498
  (24 other events, 151.3 us)

commit v14 on v13

--- a/solution.py
+++ b/solution.py
@@ -11,7 +11,7 @@
 LANES = 128
 SUBLANES = 8
 PANEL = 64
-SPLIT = 3 * LANES
+SPLIT = LANES
 MIB = 1024 * 1024
 FULL = lax.Precision.HIGHEST
 F32 = jnp.float32
@@ -484,10 +484,9 @@
 
     turns, swap = ring_steps(count), swap_pairs(count)
     result = None
-    partial = [part]
+    colsq = part
     for axis, distances in sum_rounds(count):
-        partial.append(sum_round(partial[-1], axis, distances))
-    colsq = partial[-1]
+        colsq = sum_round(colsq, axis, distances)
     arrived, blocks, owners, written = {0: back}, [], [], 0
     waiting = ()
     for n in range(chips):
@@ -499,7 +498,7 @@
         hops = (n + 1) // 2 if n % 2 else -(n // 2)
         owners += [functools.partial(ring_owner, count, hops, far) for far in (False, True)]
         if n == 0:
-            waiting = (arrived[2], partial[-2])
+            waiting = (arrived[2], colsq)
             continue
         if n == 2:
             waiting = ()

time: 153 us -> 147 us (0.961)
  waiting for transfers between devices: 60.7 us -> 38.5 us
  starting transfers between devices: 54.8 us -> 71.8 us
    ppermute x15, waiting for transfers between devices: 4.84 us -> 17.9 us  [exchange(): columns[k] = lax.ppermute(tie(outgoing[k], *after), 'fsdp', pairs)]
    ppermute x7, waiting for transfers between devices: 17.3 us -> 5.85 us  [sum_round(): terms.append(lax.ppermute(x, axis, [(n, n ^ d) for n in range(size)]))]
    ppermute x1, waiting for transfers between devices: 11.7 us -> 2.13 us  [local(): lax.ppermute(theirs, 'fsdp', [(n, n ^ chips) for n in range(count)])]
    ppermute x1, starting transfers between devices: 0.07 us -> 8.51 us  [local(): lax.ppermute(theirs, 'fsdp', [(n, n ^ chips) for n in range(count)])]
    ppermute x4, waiting for transfers between devices: 14.1 us -> 6.43 us  [gather_and_exchange(): ahead = lax.ppermute(ahead, 'fsdp', first)]
    ppermute x7, starting transfers between devices: 1.59 us -> 8.11 us  [local(): arrived[later] = lax.ppermute(block, 'fsdp', turns[(later + 1) % 2])]
    ppermute x7, waiting for transfers between devices: 9.84 us -> 6.1 us  [local(): arrived[later] = lax.ppermute(block, 'fsdp', turns[(later + 1) % 2])]
    ppermute x3, starting transfers between devices: 4.82 us -> 1.71 us  [gather_and_exchange(): behind = lax.ppermute(behind, 'fsdp', second)]
  transfers between devices with their start and end apart: 47 -> 47, of which waited for: 12 -> 14; matrix products, arithmetic and copies ran while one was open for 0% -> 0% of each run, Pallas kernels for 18% -> 18%
where the time goes in v14:
time: 147 us
  starting transfers between devices  71.8 us (49%)
  waiting for transfers between devices  38.5 us (26%)
  Pallas kernels  29 us (20%)
  other arithmetic  3.98 us (3%)
    ppermute x15, starting transfers between devices, exchange(): columns[k] = lax.ppermute(tie(outgoing[k], *after), 'fsdp', pairs)  27.2 us
    ppermute x15, waiting for transfers between devices, exchange(): columns[k] = lax.ppermute(tie(outgoing[k], *after), 'fsdp', pairs)  17.9 us
    pallas_call x1, Pallas kernels, factor_call(): pl.pallas_call(functools.partial(factor_kernel, len(stacked), owner), in_...  14.2 us
    pallas_call x7, Pallas kernels, output_call(): pl.pallas_call(functools.partial(output_kernel, owner, factor), in_specs=...  12.7 us
    ppermute x8, starting transfers between devices, local(): blocks += [block, lax.ppermute(block, 'fsdp', swap)]  9.6 us
    ppermute x7, starting transfers between devices, sum_round(): terms.append(lax.ppermute(x, axis, [(n, n ^ d) for n in range(size)]))  9.31 us
    ppermute x1, starting transfers between devices, local(): lax.ppermute(theirs, 'fsdp', [(n, n ^ chips) for n in range(count)])  8.51 us
    ppermute x7, starting transfers between devices, local(): arrived[later] = lax.ppermute(block, 'fsdp', turns[(later + 1) % 2])  8.11 us
  transfers between devices with their start and end apart: 47, of which 14 were waited for; matrix products, arithmetic and copies ran while one was open for 0% of the time, Pallas kernels for 18%

profile of v14, /device:TPU:1, one launch (start us, length us, event | category | flops | bytes accessed | tf_op | source)
XLA Modules:
  0.0 146.9 jit_solution(10610029878391259055)
XLA Ops:
  0.6 4.0 %convert_add_fusion.base_ref = f32[96,13824]{1,0:T(8,128)S(1)} fusion(f32[96,13824]{1,0:T(8,128)} %param.3, bf16[96,13824]{1,0:T(8,128)(2,1)} %param.4), kind=kLoop, calls=%fused_computation | loop fusion | flops 2654208 | bytes 13271040 | tf_op jit(solution)/shard_map/add | solution.py:456
  7.2 2.1 %collective-permute-start = (f32[96,256]{1,0:T(8,128)S(1)}, f32[96,256]{1,0:T(8,128)S(1)}, u32[]{:S(2)}, u32[]{:S(2)}) collective-permute-start(f32[96,256]{1,0:T(8,128)S(1)} %fusion), channel_id=1, source_target_pairs={{0,1},{1,0},{2,3},{3,2},{4,5},{5,4},{6,7},{7,6},{8,9},{9,8},{10,11... | collective-permute-start | bytes 294920 | tf_op jit(solution)/shard_map/ppermute | solution.py:407
  12.4 2.3 %collective-permute-start.3 = (bf16[96,768]{1,0:T(8,128)(2,1)S(1)}, bf16[96,768]{1,0:T(8,128)(2,1)S(1)}, u32[]{:S(2)}, u32[]{:S(2)}) collective-permute-start(bf16[96,768]{1,0:T(8,128)(2,1)S(1)} %get-tuple-element.77), channel_id=1, source_target_pairs={{0,16},{2,18},{4,20},{6,22},{8,24},{10,26},{12,28},{14,30},{16,0},... | collective-permute-start | bytes 442376 | tf_op jit(solution)/shard_map/ppermute | solution.py:404
  16.3 5.7 %collective-permute-done.3.refs_8_ = bf16[96,768]{1,0:T(8,128)(2,1)S(1)} collective-permute-done((bf16[96,768]{1,0:T(8,128)(2,1)S(1)}, bf16[96,768]{1,0:T(8,128)(2,1)S(1)}, u32[]{:S(2)}, u32[]{:S(2)}) %collective-permute-start.3) | collective-permute-done | bytes 147488 | tf_op jit(solution)/shard_map/ppermute | solution.py:404
  23.6 2.9 %collective-permute-start.8 = (bf16[96,768]{1,0:T(8,128)(2,1)S(1)}, bf16[96,768]{1,0:T(8,128)(2,1)S(1)}, u32[]{:S(2)}, u32[]{:S(2)}) collective-permute-start(bf16[96,768]{1,0:T(8,128)(2,1)S(1)} %get-tuple-element.85), channel_id=1, source_target_pairs={{0,18},{2,16},{4,22},{6,20},{8,26},{10,24},{12,30},{14,28},{16,2},... | collective-permute-start | bytes 442376 | tf_op jit(solution)/shard_map/ppermute | solution.py:404
  28.0 5.7 %collective-permute-done.8.refs_9_ = bf16[96,768]{1,0:T(8,128)(2,1)S(1)} collective-permute-done((bf16[96,768]{1,0:T(8,128)(2,1)S(1)}, bf16[96,768]{1,0:T(8,128)(2,1)S(1)}, u32[]{:S(2)}, u32[]{:S(2)}) %collective-permute-start.8) | collective-permute-done | bytes 147488 | tf_op jit(solution)/shard_map/ppermute | solution.py:404
  34.7 2.5 %collective-permute-start.14 = (bf16[96,1024]{1,0:T(8,128)(2,1)S(1)}, bf16[96,1024]{1,0:T(8,128)(2,1)S(1)}, u32[]{:S(2)}, u32[]{:S(2)}) collective-permute-start(bf16[96,1024]{1,0:T(8,128)(2,1)S(1)} %get-tuple-element.95), channel_id=1, source_target_pairs={{0,10},{2,8},{4,14},{6,12},{8,2},{10,0},{12,6},{14,4},{16,26},{18,... | collective-permute-start | bytes 589832 | tf_op jit(solution)/shard_map/ppermute | solution.py:404
  39.5 6.4 %collective-permute-done.13.refs_10_ = bf16[96,768]{1,0:T(8,128)(2,1)S(1)} collective-permute-done((bf16[96,768]{1,0:T(8,128)(2,1)S(1)}, bf16[96,768]{1,0:T(8,128)(2,1)S(1)}, u32[]{:S(2)}, u32[]{:S(2)}) %collective-permute-start.13) | collective-permute-done | bytes 147488 | tf_op jit(solution)/shard_map/ppermute | solution.py:404
  45.9 4.5 %collective-permute-start.18 = (bf16[96,1024]{1,0:T(8,128)(2,1)S(1)}, bf16[96,1024]{1,0:T(8,128)(2,1)S(1)}, u32[]{:S(2)}, u32[]{:S(2)}) collective-permute-start(bf16[96,1024]{1,0:T(8,128)(2,1)S(1)} %get-tuple-element.102), channel_id=1, source_target_pairs={{0,14},{2,12},{4,10},{6,8},{8,6},{10,4},{12,2},{14,0},{16,30},{18,... | collective-permute-start | bytes 589832 | tf_op jit(solution)/shard_map/ppermute | solution.py:404
  52.7 6.4 %collective-permute-done.16 = f32[96,256]{1,0:T(8,128)S(1)} collective-permute-done((f32[96,256]{1,0:T(8,128)S(1)}, f32[96,256]{1,0:T(8,128)S(1)}, u32[]{:S(2)}, u32[]{:S(2)}) %collective-permute-start.16) | collective-permute-done | bytes 98336 | tf_op jit(solution)/shard_map/ppermute | solution.py:414
  60.5 2.4 %collective-permute-start.20 = (bf16[96,768]{1,0:T(8,128)(2,1)S(1)}, bf16[96,768]{1,0:T(8,128)(2,1)S(1)}, u32[]{:S(2)}, u32[]{:S(2)}) collective-permute-start(bf16[96,768]{1,0:T(8,128)(2,1)S(1)} %get-tuple-element.109), channel_id=1, source_target_pairs={{0,24},{2,26},{4,28},{6,30},{8,16},{10,18},{12,20},{14,22},{16,8},... | collective-permute-start | bytes 442376 | tf_op jit(solution)/shard_map/ppermute | solution.py:404
  62.9 3.3 %collective-permute-start.23 = (bf16[96,768]{1,0:T(8,128)(2,1)S(1)}, bf16[96,768]{1,0:T(8,128)(2,1)S(1)}, u32[]{:S(2)}, u32[]{:S(2)}) collective-permute-start(bf16[96,768]{1,0:T(8,128)(2,1)S(1)} %get-tuple-element.115), channel_id=1, source_target_pairs={{0,30},{2,28},{4,26},{6,24},{8,22},{10,20},{12,18},{14,16},{16,14}... | collective-permute-start | bytes 442376 | tf_op jit(solution)/shard_map/ppermute | solution.py:404
  68.5 14.2 %factor.1 = (bf16[256,1536]{1,0:T(8,128)(2,1)S(1)}, bf16[96,256]{1,0:T(8,128)(2,1)S(1)}) custom-call(f32[96,13824]{1,0:T(8,128)S(1)} %convert_add_fusion.base_ref, f32[8,96,256]{2,1,0:T(8,128)S(1)} %bitcast_dynamic-update-slice_fusion.refs_0_, f32[8,96,256]{2,1,0:T(8,128)S(1)} %collective-permute-done.19.refs_1_), custom_call_target="tpu_custom_call" | custom-call | flops 4026531840 | bytes 2359296 | tf_op jit(solution)/shard_map/factor/pallas_call | solution.py:184
  83.2 8.5 %collective-permute-start.24 = (bf16[128,256]{1,0:T(8,128)(2,1)S(1)}, bf16[128,256]{1,0:T(8,128)(2,1)S(1)}, u32[]{:S(2)}, u32[]{:S(2)}) collective-permute-start(bf16[128,256]{1,0:T(8,128)(2,1)S(1)} %get-tuple-element.118), channel_id=1, source_target_pairs={{0,16},{2,18},{4,20},{6,22},{8,24},{10,26},{12,28},{14,30},{16,0},... | collective-permute-start | bytes 196616 | tf_op jit(solution)/shard_map/ppermute | solution.py:476
  91.7 2.1 %collective-permute-done.24.refs_17_ = bf16[128,256]{1,0:T(8,128)(2,1)S(1)} collective-permute-done((bf16[128,256]{1,0:T(8,128)(2,1)S(1)}, bf16[128,256]{1,0:T(8,128)(2,1)S(1)}, u32[]{:S(2)}, u32[]{:S(2)}) %collective-permute-start.24) | collective-permute-done | bytes 65568 | tf_op jit(solution)/shard_map/ppermute | solution.py:476
  96.5 2.3 %collective-permute-done.25 = f32[1,256]{1,0:T(1,128)S(1)} collective-permute-done((f32[1,256]{1,0:T(1,128)S(1)}, f32[1,256]{1,0:T(1,128)S(1)}, u32[]{:S(2)}, u32[]{:S(2)}) %collective-permute-start.25) | collective-permute-done | bytes 1056 | tf_op jit(solution)/shard_map/ppermute | solution.py:440
  98.8 4.0 %collective-permute-start.26 = (f32[1,256]{1,0:T(1,128)S(1)}, f32[1,256]{1,0:T(1,128)S(1)}, u32[]{:S(2)}, u32[]{:S(2)}) collective-permute-start(f32[1,256]{1,0:T(1,128)S(1)} %add.29), channel_id=1, source_target_pairs={{0,2},{2,0},{4,6},{6,4},{8,10},{10,8},{12,14},{14,12},{16,18},{18,... | collective-permute-start | bytes 3080 | tf_op jit(solution)/shard_map/ppermute | solution.py:440
  105.6 2.2 %collective-permute-done.28 = f32[1,256]{1,0:T(1,128)S(1)} collective-permute-done((f32[1,256]{1,0:T(1,128)S(1)}, f32[1,256]{1,0:T(1,128)S(1)}, u32[]{:S(2)}, u32[]{:S(2)}) %collective-permute-start.28) | collective-permute-done | bytes 1056 | tf_op jit(solution)/shard_map/ppermute | solution.py:440
  108.7 2.7 %collective-permute-start.31 = (f32[1,256]{1,0:T(1,128)S(1)}, f32[1,256]{1,0:T(1,128)S(1)}, u32[]{:S(2)}, u32[]{:S(2)}) collective-permute-start(f32[1,256]{1,0:T(1,128)S(1)} %add_add_fusion.1), channel_id=1, source_target_pairs={{0,24},{2,26},{4,28},{6,30},{8,16},{10,18},{12,20},{14,22},{16,8},... | collective-permute-start | bytes 3080 | tf_op jit(solution)/shard_map/ppermute | solution.py:440
  112.9 2.3 %collective-permute-start.38 = (bf16[896,256]{1,0:T(8,128)(2,1)S(1)}, bf16[896,256]{1,0:T(8,128)(2,1)S(1)}, u32[]{:S(2)}, u32[]{:S(2)}) collective-permute-start(bf16[896,256]{1,0:T(8,128)(2,1)S(1)} %collective-permute-done.32.refs_2_), channel_id=1, source_target_pairs={{0,2},{2,0},{4,6},{6,4},{8,10},{10,8},{12,14},{14,12},{16,18},{18,... | collective-permute-start | bytes 1376264 | tf_op jit(solution)/shard_map/ppermute | solution.py:497
  117.1 2.8 %outputs.7 = (f32[96,13824]{1,0:T(8,128)}, bf16[13824,256]{1,0:T(8,128)(2,1)}, bf16[96,13824]{1,0:T(8,128)(2,1)}) custom-call(f32[96,13824]{1,0:T(8,128)S(1)} %convert_add_fusion.base_ref, bf16[96,256]{1,0:T(8,128)(2,1)S(1)} %get-tuple-element.104.ortho_ref, f32[1,256]{1,0:T(1,128)S(1)} %add_add_fusion.colsq_ref, ...), custom_call_target="tpu_custom_call" | custom-call | flops 352321536 | bytes 7110656 | tf_op jit(solution)/shard_map/outputs/pallas_call | solution.py:325
  120.0 2.8 %collective-permute-done.34.refs_0_ = bf16[896,256]{1,0:T(8,128)(2,1)S(1)} collective-permute-done((bf16[896,256]{1,0:T(8,128)(2,1)S(1)}, bf16[896,256]{1,0:T(8,128)(2,1)S(1)}, u32[]{:S(2)}, u32[]{:S(2)}) %collective-permute-start.34) | collective-permute-done | bytes 458784 | tf_op jit(solution)/shard_map/ppermute | solution.py:496
  133.9 2.6 %collective-permute-start.40 = (bf16[896,256]{1,0:T(8,128)(2,1)S(1)}, bf16[896,256]{1,0:T(8,128)(2,1)S(1)}, u32[]{:S(2)}, u32[]{:S(2)}) collective-permute-start(bf16[896,256]{1,0:T(8,128)(2,1)S(1)} %collective-permute-done.35.refs_0_), channel_id=1, source_target_pairs={{0,8},{8,16},{16,24},{24,28},{28,20},{20,12},{12,4},{4,0},{10,2},{... | collective-permute-start | bytes 1376264 | tf_op jit(solution)/shard_map/ppermute | solution.py:496
  138.5 2.2 %collective-permute-start.46 = (bf16[896,256]{1,0:T(8,128)(2,1)S(1)}, bf16[896,256]{1,0:T(8,128)(2,1)S(1)}, u32[]{:S(2)}, u32[]{:S(2)}) collective-permute-start(bf16[896,256]{1,0:T(8,128)(2,1)S(1)} %collective-permute-done.45.refs_0_), channel_id=1, source_target_pairs={{0,2},{2,0},{4,6},{6,4},{8,10},{10,8},{12,14},{14,12},{16,18},{18,... | collective-permute-start | bytes 1376264 | tf_op jit(solution)/shard_map/ppermute | solution.py:497
  (96 shorter events, 48.8 us)
Async XLA Ops:
  9.9 12.8 %collective-permute-start.5 = (bf16[96,1024]{1,0:T(8,128)(2,1)S(1)}, bf16[96,1024]{1,0:T(8,128)(2,1)S(1)}, u32[]{:S(2)}, u32[]{:S(2)}) collective-permute-start(bf16[96,1024]{1,0:T(8,128)(2,1)S(1)} %get-tuple-element.81), channel_id=1, source_target_pairs={{0,4},{2,6},{4,0},{6,2},{8,12},{10,14},{12,8},{14,10},{16,20},{18,... | collective-permute-start | bytes 589832 | tf_op jit(solution)/shard_map/ppermute | solution.py:404
  11.2 12.4 %collective-permute-start.4 = (bf16[96,1024]{1,0:T(8,128)(2,1)S(1)}, bf16[96,1024]{1,0:T(8,128)(2,1)S(1)}, u32[]{:S(2)}, u32[]{:S(2)}) collective-permute-start(bf16[96,1024]{1,0:T(8,128)(2,1)S(1)} %get-tuple-element.79), channel_id=1, source_target_pairs={{0,2},{2,0},{4,6},{6,4},{8,10},{10,8},{12,14},{14,12},{16,18},{18,... | collective-permute-start | bytes 589832 | tf_op jit(solution)/shard_map/ppermute | solution.py:404
  12.4 9.6 %collective-permute-start.3 = (bf16[96,768]{1,0:T(8,128)(2,1)S(1)}, bf16[96,768]{1,0:T(8,128)(2,1)S(1)}, u32[]{:S(2)}, u32[]{:S(2)}) collective-permute-start(bf16[96,768]{1,0:T(8,128)(2,1)S(1)} %get-tuple-element.77), channel_id=1, source_target_pairs={{0,16},{2,18},{4,20},{6,22},{8,24},{10,26},{12,28},{14,30},{16,0},... | collective-permute-start | bytes 442376 | tf_op jit(solution)/shard_map/ppermute | solution.py:404
  14.8 11.8 %collective-permute-start.1 = (f32[96,256]{1,0:T(8,128)S(1)}, f32[96,256]{1,0:T(8,128)S(1)}, u32[]{:S(2)}, u32[]{:S(2)}) collective-permute-start(f32[96,256]{1,0:T(8,128)S(1)} %get-tuple-element.75), channel_id=1, source_target_pairs={{0,8},{8,16},{16,24},{24,28},{28,20},{20,12},{12,4},{4,0},{10,2},{... | collective-permute-start | bytes 294920 | tf_op jit(solution)/shard_map/ppermute | solution.py:414
  15.0 11.5 %collective-permute-start.2 = (f32[96,256]{1,0:T(8,128)S(1)}, f32[96,256]{1,0:T(8,128)S(1)}, u32[]{:S(2)}, u32[]{:S(2)}) collective-permute-start(f32[96,256]{1,0:T(8,128)S(1)} %get-tuple-element.75), channel_id=1, source_target_pairs={{8,0},{16,8},{24,16},{28,24},{20,28},{12,20},{4,12},{0,4},{2,10},{... | collective-permute-start | bytes 294920 | tf_op jit(solution)/shard_map/ppermute | solution.py:418
  22.0 15.6 %collective-permute-start.10 = (bf16[96,1024]{1,0:T(8,128)(2,1)S(1)}, bf16[96,1024]{1,0:T(8,128)(2,1)S(1)}, u32[]{:S(2)}, u32[]{:S(2)}) collective-permute-start(bf16[96,1024]{1,0:T(8,128)(2,1)S(1)} %get-tuple-element.89), channel_id=1, source_target_pairs={{0,8},{2,10},{4,12},{6,14},{8,0},{10,2},{12,4},{14,6},{16,24},{18,... | collective-permute-start | bytes 589832 | tf_op jit(solution)/shard_map/ppermute | solution.py:404
  22.7 14.9 %collective-permute-start.9 = (bf16[96,1024]{1,0:T(8,128)(2,1)S(1)}, bf16[96,1024]{1,0:T(8,128)(2,1)S(1)}, u32[]{:S(2)}, u32[]{:S(2)}) collective-permute-start(bf16[96,1024]{1,0:T(8,128)(2,1)S(1)} %get-tuple-element.87), channel_id=1, source_target_pairs={{0,6},{2,4},{4,2},{6,0},{8,14},{10,12},{12,10},{14,8},{16,22},{18,... | collective-permute-start | bytes 589832 | tf_op jit(solution)/shard_map/ppermute | solution.py:404
  23.6 10.2 %collective-permute-start.8 = (bf16[96,768]{1,0:T(8,128)(2,1)S(1)}, bf16[96,768]{1,0:T(8,128)(2,1)S(1)}, u32[]{:S(2)}, u32[]{:S(2)}) collective-permute-start(bf16[96,768]{1,0:T(8,128)(2,1)S(1)} %get-tuple-element.85), channel_id=1, source_target_pairs={{0,18},{2,16},{4,22},{6,20},{8,26},{10,24},{12,30},{14,28},{16,2},... | collective-permute-start | bytes 442376 | tf_op jit(solution)/shard_map/ppermute | solution.py:404
  27.6 9.7 %collective-permute-start.7 = (f32[96,256]{1,0:T(8,128)S(1)}, f32[96,256]{1,0:T(8,128)S(1)}, u32[]{:S(2)}, u32[]{:S(2)}) collective-permute-start(f32[96,256]{1,0:T(8,128)S(1)} %collective-permute-done.2), channel_id=1, source_target_pairs={{8,0},{16,8},{24,16},{28,24},{20,28},{12,20},{4,12},{0,4},{2,10},{... | collective-permute-start | bytes 294920 | tf_op jit(solution)/shard_map/ppermute | solution.py:418
  33.8 16.6 %collective-permute-start.15 = (bf16[96,1024]{1,0:T(8,128)(2,1)S(1)}, bf16[96,1024]{1,0:T(8,128)(2,1)S(1)}, u32[]{:S(2)}, u32[]{:S(2)}) collective-permute-start(bf16[96,1024]{1,0:T(8,128)(2,1)S(1)} %get-tuple-element.97), channel_id=1, source_target_pairs={{0,12},{2,14},{4,8},{6,10},{8,4},{10,6},{12,0},{14,2},{16,28},{18,... | collective-permute-start | bytes 589832 | tf_op jit(solution)/shard_map/ppermute | solution.py:404
  34.7 17.3 %collective-permute-start.14 = (bf16[96,1024]{1,0:T(8,128)(2,1)S(1)}, bf16[96,1024]{1,0:T(8,128)(2,1)S(1)}, u32[]{:S(2)}, u32[]{:S(2)}) collective-permute-start(bf16[96,1024]{1,0:T(8,128)(2,1)S(1)} %get-tuple-element.95), channel_id=1, source_target_pairs={{0,10},{2,8},{4,14},{6,12},{8,2},{10,0},{12,6},{14,4},{16,26},{18,... | collective-permute-start | bytes 589832 | tf_op jit(solution)/shard_map/ppermute | solution.py:404
  37.6 14.4 %collective-permute-start.11 = (f32[96,256]{1,0:T(8,128)S(1)}, f32[96,256]{1,0:T(8,128)S(1)}, u32[]{:S(2)}, u32[]{:S(2)}) collective-permute-start(f32[96,256]{1,0:T(8,128)S(1)} %collective-permute-done.6), channel_id=1, source_target_pairs={{0,8},{8,16},{16,24},{24,28},{28,20},{20,12},{12,4},{4,0},{10,2},{... | collective-permute-start | bytes 294920 | tf_op jit(solution)/shard_map/ppermute | solution.py:414
  39.5 12.5 %collective-permute-start.12 = (f32[96,256]{1,0:T(8,128)S(1)}, f32[96,256]{1,0:T(8,128)S(1)}, u32[]{:S(2)}, u32[]{:S(2)}) collective-permute-start(f32[96,256]{1,0:T(8,128)S(1)} %collective-permute-done.7), channel_id=1, source_target_pairs={{8,0},{16,8},{24,16},{28,24},{20,28},{12,20},{4,12},{0,4},{2,10},{... | collective-permute-start | bytes 294920 | tf_op jit(solution)/shard_map/ppermute | solution.py:418
  45.9 13.2 %collective-permute-start.18 = (bf16[96,1024]{1,0:T(8,128)(2,1)S(1)}, bf16[96,1024]{1,0:T(8,128)(2,1)S(1)}, u32[]{:S(2)}, u32[]{:S(2)}) collective-permute-start(bf16[96,1024]{1,0:T(8,128)(2,1)S(1)} %get-tuple-element.102), channel_id=1, source_target_pairs={{0,14},{2,12},{4,10},{6,8},{8,6},{10,4},{12,2},{14,0},{16,30},{18,... | collective-permute-start | bytes 589832 | tf_op jit(solution)/shard_map/ppermute | solution.py:404
  59.2 9.3 %collective-permute-start.19 = (f32[8,96,256]{2,1,0:T(8,128)S(1)}, f32[8,96,256]{2,1,0:T(8,128)S(1)}, u32[]{:S(2)}, u32[]{:S(2)}) collective-permute-start(f32[8,96,256]{2,1,0:T(8,128)S(1)} %bitcast_dynamic-update-slice_fusion.refs_0_), channel_id=1, source_target_pairs={{0,2},{2,0},{4,6},{6,4},{8,10},{10,8},{12,14},{14,12},{16,18},{18,... | collective-permute-start | bytes 2359304 | tf_op jit(solution)/shard_map/ppermute | solution.py:423
  60.5 22.6 %collective-permute-start.20 = (bf16[96,768]{1,0:T(8,128)(2,1)S(1)}, bf16[96,768]{1,0:T(8,128)(2,1)S(1)}, u32[]{:S(2)}, u32[]{:S(2)}) collective-permute-start(bf16[96,768]{1,0:T(8,128)(2,1)S(1)} %get-tuple-element.109), channel_id=1, source_target_pairs={{0,24},{2,26},{4,28},{6,30},{8,16},{10,18},{12,20},{14,22},{16,8},... | collective-permute-start | bytes 442376 | tf_op jit(solution)/shard_map/ppermute | solution.py:404
  62.9 20.2 %collective-permute-start.23 = (bf16[96,768]{1,0:T(8,128)(2,1)S(1)}, bf16[96,768]{1,0:T(8,128)(2,1)S(1)}, u32[]{:S(2)}, u32[]{:S(2)}) collective-permute-start(bf16[96,768]{1,0:T(8,128)(2,1)S(1)} %get-tuple-element.115), channel_id=1, source_target_pairs={{0,30},{2,28},{4,26},{6,24},{8,22},{10,20},{12,18},{14,16},{16,14}... | collective-permute-start | bytes 442376 | tf_op jit(solution)/shard_map/ppermute | solution.py:404
  66.1 17.0 %collective-permute-start.22 = (bf16[96,768]{1,0:T(8,128)(2,1)S(1)}, bf16[96,768]{1,0:T(8,128)(2,1)S(1)}, u32[]{:S(2)}, u32[]{:S(2)}) collective-permute-start(bf16[96,768]{1,0:T(8,128)(2,1)S(1)} %get-tuple-element.113), channel_id=1, source_target_pairs={{0,28},{2,30},{4,24},{6,26},{8,20},{10,22},{12,16},{14,18},{16,12}... | collective-permute-start | bytes 442376 | tf_op jit(solution)/shard_map/ppermute | solution.py:404
  67.7 15.4 %collective-permute-start.21 = (bf16[96,768]{1,0:T(8,128)(2,1)S(1)}, bf16[96,768]{1,0:T(8,128)(2,1)S(1)}, u32[]{:S(2)}, u32[]{:S(2)}) collective-permute-start(bf16[96,768]{1,0:T(8,128)(2,1)S(1)} %get-tuple-element.111), channel_id=1, source_target_pairs={{0,26},{2,24},{4,30},{6,28},{8,18},{10,16},{12,22},{14,20},{16,10}... | collective-permute-start | bytes 442376 | tf_op jit(solution)/shard_map/ppermute | solution.py:404
  83.2 10.6 %collective-permute-start.24 = (bf16[128,256]{1,0:T(8,128)(2,1)S(1)}, bf16[128,256]{1,0:T(8,128)(2,1)S(1)}, u32[]{:S(2)}, u32[]{:S(2)}) collective-permute-start(bf16[128,256]{1,0:T(8,128)(2,1)S(1)} %get-tuple-element.118), channel_id=1, source_target_pairs={{0,16},{2,18},{4,20},{6,22},{8,24},{10,26},{12,28},{14,30},{16,0},... | collective-permute-start | bytes 196616 | tf_op jit(solution)/shard_map/ppermute | solution.py:476
  94.9 18.1 %collective-permute-start.32 = (bf16[896,256]{1,0:T(8,128)(2,1)S(1)}, bf16[896,256]{1,0:T(8,128)(2,1)S(1)}, u32[]{:S(2)}, u32[]{:S(2)}) collective-permute-start(bf16[896,256]{1,0:T(8,128)(2,1)S(1)} %get-tuple-element.120.refs_0_), channel_id=1, source_target_pairs={{0,8},{8,16},{16,24},{24,28},{28,20},{20,12},{12,4},{4,0},{10,2},{... | collective-permute-start | bytes 1376264 | tf_op jit(solution)/shard_map/ppermute | solution.py:496
  95.2 17.7 %collective-permute-start.33 = (bf16[896,256]{1,0:T(8,128)(2,1)S(1)}, bf16[896,256]{1,0:T(8,128)(2,1)S(1)}, u32[]{:S(2)}, u32[]{:S(2)}) collective-permute-start(bf16[896,256]{1,0:T(8,128)(2,1)S(1)} %get-tuple-element.120.refs_0_), channel_id=1, source_target_pairs={{8,0},{16,8},{24,16},{28,24},{20,28},{12,20},{4,12},{0,4},{2,10},{... | collective-permute-start | bytes 1376264 | tf_op jit(solution)/shard_map/ppermute | solution.py:496
  124.3 9.1 %collective-permute-start.35 = (bf16[896,256]{1,0:T(8,128)(2,1)S(1)}, bf16[896,256]{1,0:T(8,128)(2,1)S(1)}, u32[]{:S(2)}, u32[]{:S(2)}) collective-permute-start(bf16[896,256]{1,0:T(8,128)(2,1)S(1)} %collective-permute-done.34.refs_0_), channel_id=1, source_target_pairs={{0,8},{8,16},{16,24},{24,28},{28,20},{20,12},{12,4},{4,0},{10,2},{... | collective-permute-start | bytes 1376264 | tf_op jit(solution)/shard_map/ppermute | solution.py:496
  133.9 9.3 %collective-permute-start.40 = (bf16[896,256]{1,0:T(8,128)(2,1)S(1)}, bf16[896,256]{1,0:T(8,128)(2,1)S(1)}, u32[]{:S(2)}, u32[]{:S(2)}) collective-permute-start(bf16[896,256]{1,0:T(8,128)(2,1)S(1)} %collective-permute-done.35.refs_0_), channel_id=1, source_target_pairs={{0,8},{8,16},{16,24},{24,28},{28,20},{20,12},{12,4},{4,0},{10,2},{... | collective-permute-start | bytes 1376264 | tf_op jit(solution)/shard_map/ppermute | solution.py:496
  (24 other events, 144.9 us)

commit v15 on v12

--- a/solution.py
+++ b/solution.py
@@ -333,9 +333,9 @@
 def exchange_windows(count):
     chips, steps = count // 2, count // 4
     far, near = list(range(chips, count)), list(range(1, chips))
-    each = -(-len(near) // (steps + 1))
-    windows = [far[w : w + 1] + near[w * each : (w + 1) * each] for w in range(steps + 1)]
-    return windows + [far[steps + 1 :]]
+    each = -(-len(near) // steps)
+    windows = [far[w + 1 : w + 2] + near[(w - 1) * each : w * each] for w in range(1, steps + 1)]
+    return [far[:2]] + windows + [far[steps + 2 :]]
 
 
 def gather_and_exchange(sketch, outgoing, count):

time: 138 us -> 140 us (1.014)
  waiting for transfers between devices: 40.4 us -> 46.6 us
  starting transfers between devices: 61.3 us -> 56.5 us
    ppermute x7, starting transfers between devices: 12.4 us -> 7.3 us  [local(): arrived[later] = lax.ppermute(block, 'fsdp', turns[(later + 1) % 2])]
    ppermute x15, waiting for transfers between devices: 14.3 us -> 17.3 us  [exchange(): columns[k] = lax.ppermute(tie(outgoing[k], *after), 'fsdp', pairs)]
    ppermute x4, starting transfers between devices: 1.99 us -> 4.59 us  [gather_and_exchange(): ahead = lax.ppermute(ahead, 'fsdp', first)]
    ppermute x4, waiting for transfers between devices: 7.97 us -> 10 us  [gather_and_exchange(): ahead = lax.ppermute(ahead, 'fsdp', first)]
    ppermute x3, starting transfers between devices: 6.55 us -> 4.97 us  [gather_and_exchange(): behind = lax.ppermute(behind, 'fsdp', second)]
  transfers between devices with their start and end apart: 46 -> 46, of which waited for: 17 -> 18; matrix products, arithmetic and copies ran while one was open for 0% -> 0% of each run, Pallas kernels for 19% -> 19%
where the time goes in v15:
time: 140 us
  starting transfers between devices  56.5 us (40%)
  waiting for transfers between devices  46.6 us (33%)
  Pallas kernels  28.8 us (21%)
  other arithmetic  3.98 us (3%)
  local copies, waits for them, and re-layouts  1.43 us (1%)
    ppermute x15, starting transfers between devices, exchange(): columns[k] = lax.ppermute(tie(outgoing[k], *after), 'fsdp', pairs)  22.4 us
    ppermute x15, waiting for transfers between devices, exchange(): columns[k] = lax.ppermute(tie(outgoing[k], *after), 'fsdp', pairs)  17.3 us
    pallas_call x1, Pallas kernels, factor_call(): pl.pallas_call(functools.partial(factor_kernel, len(stacked), owner), in_...  14.2 us
    pallas_call x7, Pallas kernels, output_call(): pl.pallas_call(functools.partial(output_kernel, owner, factor), in_specs=...  12.7 us
    ppermute x7, waiting for transfers between devices, local(): arrived[later] = lax.ppermute(block, 'fsdp', turns[(later + 1) % 2])  10.2 us
    ppermute x4, waiting for transfers between devices, gather_and_exchange(): ahead = lax.ppermute(ahead, 'fsdp', first)  10 us
    ppermute x7, starting transfers between devices, sum_round(): terms.append(lax.ppermute(x, axis, [(n, n ^ d) for n in range(size)]))  8.2 us
    ppermute x7, waiting for transfers between devices, sum_round(): terms.append(lax.ppermute(x, axis, [(n, n ^ d) for n in range(size)]))  7.53 us
  transfers between devices with their start and end apart: 46, of which 18 were waited for; matrix products, arithmetic and copies ran while one was open for 0% of the time, Pallas kernels for 19%

profile of v15, /device:TPU:1, one launch (start us, length us, event | category | flops | bytes accessed | tf_op | source)
XLA Modules:
  0.0 139.6 jit_solution(7399960239826045954)
XLA Ops:
  0.6 4.0 %convert_add_fusion.base_ref = f32[96,13824]{1,0:T(8,128)S(1)} fusion(f32[96,13824]{1,0:T(8,128)} %param.3, bf16[96,13824]{1,0:T(8,128)(2,1)} %param.4), kind=kLoop, calls=%fused_computation | loop fusion | flops 2654208 | bytes 13271040 | tf_op jit(solution)/shard_map/add | solution.py:402
  7.2 2.1 %collective-permute-start = (f32[96,256]{1,0:T(8,128)S(1)}, f32[96,256]{1,0:T(8,128)S(1)}, u32[]{:S(2)}, u32[]{:S(2)}) collective-permute-start(f32[96,256]{1,0:T(8,128)S(1)} %fusion), channel_id=1, source_target_pairs={{0,1},{1,0},{2,3},{3,2},{4,5},{5,4},{6,7},{7,6},{8,9},{9,8},{10,11... | collective-permute-start | bytes 294920 | tf_op jit(solution)/shard_map/ppermute | solution.py:353
  9.8 3.2 %collective-permute-start.4 = (bf16[96,896]{1,0:T(8,128)(2,1)S(1)}, bf16[96,896]{1,0:T(8,128)(2,1)S(1)}, u32[]{:S(2)}, u32[]{:S(2)}) collective-permute-start(bf16[96,896]{1,0:T(8,128)(2,1)S(1)} %get-tuple-element.76), channel_id=1, source_target_pairs={{0,18},{2,16},{4,22},{6,20},{8,26},{10,24},{12,30},{14,28},{16,2},... | collective-permute-start | bytes 516104 | tf_op jit(solution)/shard_map/ppermute | solution.py:350
  15.8 9.5 %collective-permute-done.4.refs_9_ = bf16[96,896]{1,0:T(8,128)(2,1)S(1)} collective-permute-done((bf16[96,896]{1,0:T(8,128)(2,1)S(1)}, bf16[96,896]{1,0:T(8,128)(2,1)S(1)}, u32[]{:S(2)}, u32[]{:S(2)}) %collective-permute-start.4) | collective-permute-done | bytes 172064 | tf_op jit(solution)/shard_map/ppermute | solution.py:350
  25.5 3.3 %collective-permute-done.3.refs_8_ = bf16[96,896]{1,0:T(8,128)(2,1)S(1)} collective-permute-done((bf16[96,896]{1,0:T(8,128)(2,1)S(1)}, bf16[96,896]{1,0:T(8,128)(2,1)S(1)}, u32[]{:S(2)}, u32[]{:S(2)}) %collective-permute-start.3) | collective-permute-done | bytes 172064 | tf_op jit(solution)/shard_map/ppermute | solution.py:350
  30.1 4.7 %collective-permute-start.6 = (f32[96,256]{1,0:T(8,128)S(1)}, f32[96,256]{1,0:T(8,128)S(1)}, u32[]{:S(2)}, u32[]{:S(2)}) collective-permute-start(f32[96,256]{1,0:T(8,128)S(1)} %collective-permute-done.2), channel_id=1, source_target_pairs={{8,0},{16,8},{24,16},{28,24},{20,28},{12,20},{4,12},{0,4},{2,10},{... | collective-permute-start | bytes 294920 | tf_op jit(solution)/shard_map/ppermute | solution.py:364
  34.9 2.4 %collective-permute-start.14 = (bf16[96,896]{1,0:T(8,128)(2,1)S(1)}, bf16[96,896]{1,0:T(8,128)(2,1)S(1)}, u32[]{:S(2)}, u32[]{:S(2)}) collective-permute-start(bf16[96,896]{1,0:T(8,128)(2,1)S(1)} %get-tuple-element.92), channel_id=1, source_target_pairs={{0,8},{2,10},{4,12},{6,14},{8,0},{10,2},{12,4},{14,6},{16,24},{18,... | collective-permute-start | bytes 516104 | tf_op jit(solution)/shard_map/ppermute | solution.py:350
  37.3 2.0 %collective-permute-start.13 = (bf16[96,896]{1,0:T(8,128)(2,1)S(1)}, bf16[96,896]{1,0:T(8,128)(2,1)S(1)}, u32[]{:S(2)}, u32[]{:S(2)}) collective-permute-start(bf16[96,896]{1,0:T(8,128)(2,1)S(1)} %get-tuple-element.90), channel_id=1, source_target_pairs={{0,6},{2,4},{4,2},{6,0},{8,14},{10,12},{12,10},{14,8},{16,22},{18,... | collective-permute-start | bytes 516104 | tf_op jit(solution)/shard_map/ppermute | solution.py:350
  44.4 2.5 %collective-permute-start.18 = (bf16[96,896]{1,0:T(8,128)(2,1)S(1)}, bf16[96,896]{1,0:T(8,128)(2,1)S(1)}, u32[]{:S(2)}, u32[]{:S(2)}) collective-permute-start(bf16[96,896]{1,0:T(8,128)(2,1)S(1)} %get-tuple-element.99), channel_id=1, source_target_pairs={{0,12},{2,14},{4,8},{6,10},{8,4},{10,6},{12,0},{14,2},{16,28},{18,... | collective-permute-start | bytes 516104 | tf_op jit(solution)/shard_map/ppermute | solution.py:350
  48.6 3.0 %collective-permute-done.12.refs_11_ = bf16[96,896]{1,0:T(8,128)(2,1)S(1)} collective-permute-done((bf16[96,896]{1,0:T(8,128)(2,1)S(1)}, bf16[96,896]{1,0:T(8,128)(2,1)S(1)}, u32[]{:S(2)}, u32[]{:S(2)}) %collective-permute-start.12) | collective-permute-done | bytes 172064 | tf_op jit(solution)/shard_map/ppermute | solution.py:350
  51.6 2.2 %collective-permute-start.16 = (bf16[96,896]{1,0:T(8,128)(2,1)S(1)}, bf16[96,896]{1,0:T(8,128)(2,1)S(1)}, u32[]{:S(2)}, u32[]{:S(2)}) collective-permute-start(bf16[96,896]{1,0:T(8,128)(2,1)S(1)} %get-tuple-element.95), channel_id=1, source_target_pairs={{0,24},{2,26},{4,28},{6,30},{8,16},{10,18},{12,20},{14,22},{16,8},... | collective-permute-start | bytes 516104 | tf_op jit(solution)/shard_map/ppermute | solution.py:350
  54.1 10.0 %collective-permute-done.15 = f32[96,256]{1,0:T(8,128)S(1)} collective-permute-done((f32[96,256]{1,0:T(8,128)S(1)}, f32[96,256]{1,0:T(8,128)S(1)}, u32[]{:S(2)}, u32[]{:S(2)}) %collective-permute-start.15) | collective-permute-done | bytes 98336 | tf_op jit(solution)/shard_map/ppermute | solution.py:360
  65.7 2.4 %collective-permute-start.23 = (bf16[96,896]{1,0:T(8,128)(2,1)S(1)}, bf16[96,896]{1,0:T(8,128)(2,1)S(1)}, u32[]{:S(2)}, u32[]{:S(2)}) collective-permute-start(bf16[96,896]{1,0:T(8,128)(2,1)S(1)} %get-tuple-element.112), channel_id=1, source_target_pairs={{0,30},{2,28},{4,26},{6,24},{8,22},{10,20},{12,18},{14,16},{16,14}... | collective-permute-start | bytes 516104 | tf_op jit(solution)/shard_map/ppermute | solution.py:350
  68.1 2.1 %collective-permute-start.22 = (bf16[96,896]{1,0:T(8,128)(2,1)S(1)}, bf16[96,896]{1,0:T(8,128)(2,1)S(1)}, u32[]{:S(2)}, u32[]{:S(2)}) collective-permute-start(bf16[96,896]{1,0:T(8,128)(2,1)S(1)} %get-tuple-element.110), channel_id=1, source_target_pairs={{0,28},{2,30},{4,24},{6,26},{8,20},{10,22},{12,16},{14,18},{16,12}... | collective-permute-start | bytes 516104 | tf_op jit(solution)/shard_map/ppermute | solution.py:350
  70.2 14.2 %factor.1 = (bf16[256,1536]{1,0:T(8,128)(2,1)S(1)}, bf16[96,256]{1,0:T(8,128)(2,1)S(1)}) custom-call(f32[96,13824]{1,0:T(8,128)S(1)} %convert_add_fusion.base_ref, f32[8,96,256]{2,1,0:T(8,128)S(1)} %bitcast_dynamic-update-slice_fusion.refs_0_, f32[8,96,256]{2,1,0:T(8,128)S(1)} %collective-permute-done.19.refs_1_), custom_call_target="tpu_custom_call" | custom-call | flops 4026531840 | bytes 2359296 | tf_op jit(solution)/shard_map/factor/pallas_call | solution.py:166
  85.8 2.2 %collective-permute-start.31 = (bf16[896,256]{1,0:T(8,128)(2,1)S(1)}, bf16[896,256]{1,0:T(8,128)(2,1)S(1)}, u32[]{:S(2)}, u32[]{:S(2)}) collective-permute-start(bf16[896,256]{1,0:T(8,128)(2,1)S(1)} %get-tuple-element.114.refs_0_), channel_id=1, source_target_pairs={{0,8},{8,16},{16,24},{24,28},{28,20},{20,12},{12,4},{4,0},{10,2},{... | collective-permute-start | bytes 1376264 | tf_op jit(solution)/shard_map/ppermute | solution.py:436
  88.0 2.3 %collective-permute-start.32 = (bf16[896,256]{1,0:T(8,128)(2,1)S(1)}, bf16[896,256]{1,0:T(8,128)(2,1)S(1)}, u32[]{:S(2)}, u32[]{:S(2)}) collective-permute-start(bf16[896,256]{1,0:T(8,128)(2,1)S(1)} %get-tuple-element.114.refs_0_), channel_id=1, source_target_pairs={{8,0},{16,8},{24,16},{28,24},{20,28},{12,20},{4,12},{0,4},{2,10},{... | collective-permute-start | bytes 1376264 | tf_op jit(solution)/shard_map/ppermute | solution.py:436
  90.3 2.7 %collective-permute-done.24 = f32[1,256]{1,0:T(1,128)S(1)} collective-permute-done((f32[1,256]{1,0:T(1,128)S(1)}, f32[1,256]{1,0:T(1,128)S(1)}, u32[]{:S(2)}, u32[]{:S(2)}) %collective-permute-start.24) | collective-permute-done | bytes 1056 | tf_op jit(solution)/shard_map/ppermute | solution.py:386
  95.0 2.3 %collective-permute-start.26 = (f32[1,256]{1,0:T(1,128)S(1)}, f32[1,256]{1,0:T(1,128)S(1)}, u32[]{:S(2)}, u32[]{:S(2)}) collective-permute-start(f32[1,256]{1,0:T(1,128)S(1)} %add.29), channel_id=1, source_target_pairs={{0,4},{2,6},{4,0},{6,2},{8,12},{10,14},{12,8},{14,10},{16,20},{18,... | collective-permute-start | bytes 3080 | tf_op jit(solution)/shard_map/ppermute | solution.py:386
  97.4 2.6 %collective-permute-done.26 = f32[1,256]{1,0:T(1,128)S(1)} collective-permute-done((f32[1,256]{1,0:T(1,128)S(1)}, f32[1,256]{1,0:T(1,128)S(1)}, u32[]{:S(2)}, u32[]{:S(2)}) %collective-permute-start.26) | collective-permute-done | bytes 1056 | tf_op jit(solution)/shard_map/ppermute | solution.py:386
  102.4 2.1 %collective-permute-start.30 = (f32[1,256]{1,0:T(1,128)S(1)}, f32[1,256]{1,0:T(1,128)S(1)}, u32[]{:S(2)}, u32[]{:S(2)}) collective-permute-start(f32[1,256]{1,0:T(1,128)S(1)} %add_add_fusion.1), channel_id=1, source_target_pairs={{0,24},{2,26},{4,28},{6,30},{8,16},{10,18},{12,20},{14,22},{16,8},... | collective-permute-start | bytes 3080 | tf_op jit(solution)/shard_map/ppermute | solution.py:386
  109.5 2.8 %outputs.7 = (f32[96,13824]{1,0:T(8,128)}, bf16[13824,256]{1,0:T(8,128)(2,1)}, bf16[96,13824]{1,0:T(8,128)(2,1)}) custom-call(f32[96,13824]{1,0:T(8,128)S(1)} %convert_add_fusion.base_ref, bf16[96,256]{1,0:T(8,128)(2,1)S(1)} %get-tuple-element.101.ortho_ref, f32[1,256]{1,0:T(1,128)S(1)} %add_add_fusion.colsq_ref, ...), custom_call_target="tpu_custom_call" | custom-call | flops 352321536 | bytes 7110656 | tf_op jit(solution)/shard_map/outputs/pallas_call | solution.py:271
  112.7 3.0 %collective-permute-done.33.refs_0_ = bf16[896,256]{1,0:T(8,128)(2,1)S(1)} collective-permute-done((bf16[896,256]{1,0:T(8,128)(2,1)S(1)}, bf16[896,256]{1,0:T(8,128)(2,1)S(1)}, u32[]{:S(2)}, u32[]{:S(2)}) %collective-permute-start.33) | collective-permute-done | bytes 458784 | tf_op jit(solution)/shard_map/ppermute | solution.py:436
  133.4 2.3 %collective-permute-done.39.refs_2_ = bf16[896,256]{1,0:T(8,128)(2,1)S(1)} collective-permute-done((bf16[896,256]{1,0:T(8,128)(2,1)S(1)}, bf16[896,256]{1,0:T(8,128)(2,1)S(1)}, u32[]{:S(2)}, u32[]{:S(2)}) %collective-permute-start.39) | collective-permute-done | bytes 458784 | tf_op jit(solution)/shard_map/ppermute | solution.py:436
  (93 shorter events, 48.6 us)
Async XLA Ops:
  9.8 15.5 %collective-permute-start.4 = (bf16[96,896]{1,0:T(8,128)(2,1)S(1)}, bf16[96,896]{1,0:T(8,128)(2,1)S(1)}, u32[]{:S(2)}, u32[]{:S(2)}) collective-permute-start(bf16[96,896]{1,0:T(8,128)(2,1)S(1)} %get-tuple-element.76), channel_id=1, source_target_pairs={{0,18},{2,16},{4,22},{6,20},{8,26},{10,24},{12,30},{14,28},{16,2},... | collective-permute-start | bytes 516104 | tf_op jit(solution)/shard_map/ppermute | solution.py:350
  13.0 15.8 %collective-permute-start.3 = (bf16[96,896]{1,0:T(8,128)(2,1)S(1)}, bf16[96,896]{1,0:T(8,128)(2,1)S(1)}, u32[]{:S(2)}, u32[]{:S(2)}) collective-permute-start(bf16[96,896]{1,0:T(8,128)(2,1)S(1)} %get-tuple-element.74), channel_id=1, source_target_pairs={{0,16},{2,18},{4,20},{6,22},{8,24},{10,26},{12,28},{14,30},{16,0},... | collective-permute-start | bytes 516104 | tf_op jit(solution)/shard_map/ppermute | solution.py:350
  13.1 15.9 %collective-permute-start.1 = (f32[96,256]{1,0:T(8,128)S(1)}, f32[96,256]{1,0:T(8,128)S(1)}, u32[]{:S(2)}, u32[]{:S(2)}) collective-permute-start(f32[96,256]{1,0:T(8,128)S(1)} %get-tuple-element.72), channel_id=1, source_target_pairs={{0,8},{8,16},{16,24},{24,28},{28,20},{20,12},{12,4},{4,0},{10,2},{... | collective-permute-start | bytes 294920 | tf_op jit(solution)/shard_map/ppermute | solution.py:360
  14.4 14.7 %collective-permute-start.2 = (f32[96,256]{1,0:T(8,128)S(1)}, f32[96,256]{1,0:T(8,128)S(1)}, u32[]{:S(2)}, u32[]{:S(2)}) collective-permute-start(f32[96,256]{1,0:T(8,128)S(1)} %get-tuple-element.72), channel_id=1, source_target_pairs={{8,0},{16,8},{24,16},{28,24},{20,28},{12,20},{4,12},{0,4},{2,10},{... | collective-permute-start | bytes 294920 | tf_op jit(solution)/shard_map/ppermute | solution.py:364
  14.6 20.3 %collective-permute-start.9 = (bf16[96,896]{1,0:T(8,128)(2,1)S(1)}, bf16[96,896]{1,0:T(8,128)(2,1)S(1)}, u32[]{:S(2)}, u32[]{:S(2)}) collective-permute-start(bf16[96,896]{1,0:T(8,128)(2,1)S(1)} %get-tuple-element.84), channel_id=1, source_target_pairs={{0,4},{2,6},{4,0},{6,2},{8,12},{10,14},{12,8},{14,10},{16,20},{18,... | collective-permute-start | bytes 516104 | tf_op jit(solution)/shard_map/ppermute | solution.py:350
  25.3 12.0 %collective-permute-start.8 = (bf16[96,896]{1,0:T(8,128)(2,1)S(1)}, bf16[96,896]{1,0:T(8,128)(2,1)S(1)}, u32[]{:S(2)}, u32[]{:S(2)}) collective-permute-start(bf16[96,896]{1,0:T(8,128)(2,1)S(1)} %get-tuple-element.82), channel_id=1, source_target_pairs={{0,2},{2,0},{4,6},{6,4},{8,10},{10,8},{12,14},{14,12},{16,18},{18,... | collective-permute-start | bytes 516104 | tf_op jit(solution)/shard_map/ppermute | solution.py:350
  28.8 10.9 %collective-permute-start.7 = (bf16[96,896]{1,0:T(8,128)(2,1)S(1)}, bf16[96,896]{1,0:T(8,128)(2,1)S(1)}, u32[]{:S(2)}, u32[]{:S(2)}) collective-permute-start(bf16[96,896]{1,0:T(8,128)(2,1)S(1)} %get-tuple-element.80), channel_id=1, source_target_pairs={{0,20},{2,22},{4,16},{6,18},{8,28},{10,30},{12,24},{14,26},{16,4},... | collective-permute-start | bytes 516104 | tf_op jit(solution)/shard_map/ppermute | solution.py:350
  29.0 11.4 %collective-permute-start.5 = (f32[96,256]{1,0:T(8,128)S(1)}, f32[96,256]{1,0:T(8,128)S(1)}, u32[]{:S(2)}, u32[]{:S(2)}) collective-permute-start(f32[96,256]{1,0:T(8,128)S(1)} %collective-permute-done.1), channel_id=1, source_target_pairs={{0,8},{8,16},{16,24},{24,28},{28,20},{20,12},{12,4},{4,0},{10,2},{... | collective-permute-start | bytes 294920 | tf_op jit(solution)/shard_map/ppermute | solution.py:360
  30.1 11.2 %collective-permute-start.6 = (f32[96,256]{1,0:T(8,128)S(1)}, f32[96,256]{1,0:T(8,128)S(1)}, u32[]{:S(2)}, u32[]{:S(2)}) collective-permute-start(f32[96,256]{1,0:T(8,128)S(1)} %collective-permute-done.2), channel_id=1, source_target_pairs={{8,0},{16,8},{24,16},{28,24},{20,28},{12,20},{4,12},{0,4},{2,10},{... | collective-permute-start | bytes 294920 | tf_op jit(solution)/shard_map/ppermute | solution.py:364
  34.9 9.5 %collective-permute-start.14 = (bf16[96,896]{1,0:T(8,128)(2,1)S(1)}, bf16[96,896]{1,0:T(8,128)(2,1)S(1)}, u32[]{:S(2)}, u32[]{:S(2)}) collective-permute-start(bf16[96,896]{1,0:T(8,128)(2,1)S(1)} %get-tuple-element.92), channel_id=1, source_target_pairs={{0,8},{2,10},{4,12},{6,14},{8,0},{10,2},{12,4},{14,6},{16,24},{18,... | collective-permute-start | bytes 516104 | tf_op jit(solution)/shard_map/ppermute | solution.py:350
  37.3 9.6 %collective-permute-start.13 = (bf16[96,896]{1,0:T(8,128)(2,1)S(1)}, bf16[96,896]{1,0:T(8,128)(2,1)S(1)}, u32[]{:S(2)}, u32[]{:S(2)}) collective-permute-start(bf16[96,896]{1,0:T(8,128)(2,1)S(1)} %get-tuple-element.90), channel_id=1, source_target_pairs={{0,6},{2,4},{4,2},{6,0},{8,14},{10,12},{12,10},{14,8},{16,22},{18,... | collective-permute-start | bytes 516104 | tf_op jit(solution)/shard_map/ppermute | solution.py:350
  39.7 11.9 %collective-permute-start.12 = (bf16[96,896]{1,0:T(8,128)(2,1)S(1)}, bf16[96,896]{1,0:T(8,128)(2,1)S(1)}, u32[]{:S(2)}, u32[]{:S(2)}) collective-permute-start(bf16[96,896]{1,0:T(8,128)(2,1)S(1)} %get-tuple-element.88), channel_id=1, source_target_pairs={{0,22},{2,20},{4,18},{6,16},{8,30},{10,28},{12,26},{14,24},{16,6},... | collective-permute-start | bytes 516104 | tf_op jit(solution)/shard_map/ppermute | solution.py:350
  41.3 12.5 %collective-permute-start.10 = (f32[96,256]{1,0:T(8,128)S(1)}, f32[96,256]{1,0:T(8,128)S(1)}, u32[]{:S(2)}, u32[]{:S(2)}) collective-permute-start(f32[96,256]{1,0:T(8,128)S(1)} %collective-permute-done.5), channel_id=1, source_target_pairs={{0,8},{8,16},{16,24},{24,28},{28,20},{20,12},{12,4},{4,0},{10,2},{... | collective-permute-start | bytes 294920 | tf_op jit(solution)/shard_map/ppermute | solution.py:360
  43.2 10.6 %collective-permute-start.11 = (f32[96,256]{1,0:T(8,128)S(1)}, f32[96,256]{1,0:T(8,128)S(1)}, u32[]{:S(2)}, u32[]{:S(2)}) collective-permute-start(f32[96,256]{1,0:T(8,128)S(1)} %collective-permute-done.6), channel_id=1, source_target_pairs={{8,0},{16,8},{24,16},{28,24},{20,28},{12,20},{4,12},{0,4},{2,10},{... | collective-permute-start | bytes 294920 | tf_op jit(solution)/shard_map/ppermute | solution.py:364
  44.4 19.8 %collective-permute-start.18 = (bf16[96,896]{1,0:T(8,128)(2,1)S(1)}, bf16[96,896]{1,0:T(8,128)(2,1)S(1)}, u32[]{:S(2)}, u32[]{:S(2)}) collective-permute-start(bf16[96,896]{1,0:T(8,128)(2,1)S(1)} %get-tuple-element.99), channel_id=1, source_target_pairs={{0,12},{2,14},{4,8},{6,10},{8,4},{10,6},{12,0},{14,2},{16,28},{18,... | collective-permute-start | bytes 516104 | tf_op jit(solution)/shard_map/ppermute | solution.py:350
  46.9 17.3 %collective-permute-start.17 = (bf16[96,896]{1,0:T(8,128)(2,1)S(1)}, bf16[96,896]{1,0:T(8,128)(2,1)S(1)}, u32[]{:S(2)}, u32[]{:S(2)}) collective-permute-start(bf16[96,896]{1,0:T(8,128)(2,1)S(1)} %get-tuple-element.97), channel_id=1, source_target_pairs={{0,10},{2,8},{4,14},{6,12},{8,2},{10,0},{12,6},{14,4},{16,26},{18,... | collective-permute-start | bytes 516104 | tf_op jit(solution)/shard_map/ppermute | solution.py:350
  51.6 12.6 %collective-permute-start.16 = (bf16[96,896]{1,0:T(8,128)(2,1)S(1)}, bf16[96,896]{1,0:T(8,128)(2,1)S(1)}, u32[]{:S(2)}, u32[]{:S(2)}) collective-permute-start(bf16[96,896]{1,0:T(8,128)(2,1)S(1)} %get-tuple-element.95), channel_id=1, source_target_pairs={{0,24},{2,26},{4,28},{6,30},{8,16},{10,18},{12,20},{14,22},{16,8},... | collective-permute-start | bytes 516104 | tf_op jit(solution)/shard_map/ppermute | solution.py:350
  53.8 10.3 %collective-permute-start.15 = (f32[96,256]{1,0:T(8,128)S(1)}, f32[96,256]{1,0:T(8,128)S(1)}, u32[]{:S(2)}, u32[]{:S(2)}) collective-permute-start(f32[96,256]{1,0:T(8,128)S(1)} %collective-permute-done.10), channel_id=1, source_target_pairs={{0,8},{8,16},{16,24},{24,28},{28,20},{20,12},{12,4},{4,0},{10,2},{... | collective-permute-start | bytes 294920 | tf_op jit(solution)/shard_map/ppermute | solution.py:360
  64.3 20.2 %collective-permute-start.21 = (bf16[96,896]{1,0:T(8,128)(2,1)S(1)}, bf16[96,896]{1,0:T(8,128)(2,1)S(1)}, u32[]{:S(2)}, u32[]{:S(2)}) collective-permute-start(bf16[96,896]{1,0:T(8,128)(2,1)S(1)} %get-tuple-element.108), channel_id=1, source_target_pairs={{0,26},{2,24},{4,30},{6,28},{8,18},{10,16},{12,22},{14,20},{16,10}... | collective-permute-start | bytes 516104 | tf_op jit(solution)/shard_map/ppermute | solution.py:350
  65.7 18.7 %collective-permute-start.20 = (bf16[96,896]{1,0:T(8,128)(2,1)S(1)}, bf16[96,896]{1,0:T(8,128)(2,1)S(1)}, u32[]{:S(2)}, u32[]{:S(2)}) collective-permute-start(bf16[96,896]{1,0:T(8,128)(2,1)S(1)} %get-tuple-element.106), channel_id=1, source_target_pairs={{0,14},{2,12},{4,10},{6,8},{8,6},{10,4},{12,2},{14,0},{16,30},{18,... | collective-permute-start | bytes 516104 | tf_op jit(solution)/shard_map/ppermute | solution.py:350
  65.7 18.8 %collective-permute-start.23 = (bf16[96,896]{1,0:T(8,128)(2,1)S(1)}, bf16[96,896]{1,0:T(8,128)(2,1)S(1)}, u32[]{:S(2)}, u32[]{:S(2)}) collective-permute-start(bf16[96,896]{1,0:T(8,128)(2,1)S(1)} %get-tuple-element.112), channel_id=1, source_target_pairs={{0,30},{2,28},{4,26},{6,24},{8,22},{10,20},{12,18},{14,16},{16,14}... | collective-permute-start | bytes 516104 | tf_op jit(solution)/shard_map/ppermute | solution.py:350
  68.1 16.4 %collective-permute-start.22 = (bf16[96,896]{1,0:T(8,128)(2,1)S(1)}, bf16[96,896]{1,0:T(8,128)(2,1)S(1)}, u32[]{:S(2)}, u32[]{:S(2)}) collective-permute-start(bf16[96,896]{1,0:T(8,128)(2,1)S(1)} %get-tuple-element.110), channel_id=1, source_target_pairs={{0,28},{2,30},{4,24},{6,26},{8,20},{10,22},{12,16},{14,18},{16,12}... | collective-permute-start | bytes 516104 | tf_op jit(solution)/shard_map/ppermute | solution.py:350
  85.8 20.8 %collective-permute-start.31 = (bf16[896,256]{1,0:T(8,128)(2,1)S(1)}, bf16[896,256]{1,0:T(8,128)(2,1)S(1)}, u32[]{:S(2)}, u32[]{:S(2)}) collective-permute-start(bf16[896,256]{1,0:T(8,128)(2,1)S(1)} %get-tuple-element.114.refs_0_), channel_id=1, source_target_pairs={{0,8},{8,16},{16,24},{24,28},{28,20},{20,12},{12,4},{4,0},{10,2},{... | collective-permute-start | bytes 1376264 | tf_op jit(solution)/shard_map/ppermute | solution.py:436
  88.0 18.6 %collective-permute-start.32 = (bf16[896,256]{1,0:T(8,128)(2,1)S(1)}, bf16[896,256]{1,0:T(8,128)(2,1)S(1)}, u32[]{:S(2)}, u32[]{:S(2)}) collective-permute-start(bf16[896,256]{1,0:T(8,128)(2,1)S(1)} %get-tuple-element.114.refs_0_), channel_id=1, source_target_pairs={{8,0},{16,8},{24,16},{28,24},{20,28},{12,20},{4,12},{0,4},{2,10},{... | collective-permute-start | bytes 1376264 | tf_op jit(solution)/shard_map/ppermute | solution.py:436
  (23 other events, 126.2 us)

commit v16 on v12

--- a/solution.py
+++ b/solution.py
@@ -307,12 +307,12 @@
     return first, second
 
 
-def ring_owner(count, hops, other, me):
+def ring_owner(count, hops, other, me, sign=1):
     chips = count // 2
     half = chips // 2
     core, chip = me & 1, me >> 1
     place = jnp.where((chip & 1) == 0, chip >> 1, chips - 1 - (chip >> 1))
-    forward = hops * (2 * core - 1)
+    forward = hops * sign * (2 * core - 1)
     place = lax.rem(place + chips + (-forward if other else forward), chips)
     chip = jnp.where(place < half, 2 * place, 2 * (chips - 1 - place) + 1)
     return 2 * chip + (1 - core if other else core)
@@ -350,21 +350,21 @@
             columns[k] = lax.ppermute(tie(outgoing[k], *after), "fsdp", pairs)
 
     exchange(windows[0], sketch)
-    sketch = sketch + lax.ppermute(sketch, "tp", [(0, 1), (1, 0)])
-    hops, held = [0], [sketch]
-    ahead = behind = sketch
+    across = [(0, 1), (1, 0)]
+    sketch = sketch + lax.ppermute(sketch, "tp", across)
+    turns = [(2 * a + half, 2 * b + half) for half in (0, 1) for a, b in (first, second)[half]]
+    hops, held, block = [0], [sketch], sketch
     for step in range(1, chips // 2 + 1):
         work = [columns[k] for k in windows[step - 2]] if step > 1 else []
-        ahead, behind, *_ = lax.optimization_barrier((ahead, behind, *work))
-        exchange(windows[step], ahead, behind)
-        ahead = lax.ppermute(ahead, "fsdp", first)
-        held.append(ahead)
+        block = tie(block, *work)
+        exchange(windows[step], block)
+        block = lax.ppermute(block, ("fsdp", "tp"), turns)
+        held.append(block)
         hops.append(step)
         if 2 * step < chips:
-            behind = lax.ppermute(behind, "fsdp", second)
-            held.append(behind)
+            held.append(lax.ppermute(block, "tp", across))
             hops.append(-step)
-    exchange(windows[-1], ahead, behind)
+    exchange(windows[-1], block)
     held = tie(jnp.stack(held), *[columns[k] for k in windows[-3]])
     other = lax.ppermute(held, "fsdp", swap_pairs(count))
     ways = [(h, far) for far in (False, True) for h in hops]
@@ -406,7 +406,8 @@
     if ring:
         outgoing = pack_call(base, share, count)
         pieces, ways, columns = gather_and_exchange(sketch, outgoing, count)
-        owner = owner_of([functools.partial(ring_owner, count, *way) for way in ways])
+        ways = [functools.partial(ring_owner, count, *way) for way in ways]
+        owner = lambda me, n: ways[n](me, 1 - 2 * lax.axis_index("tp"))
     else:
         padded = jnp.pad(base_b, ((0, 0), (0, share * count - cols)))
         columns = jnp.swapaxes(padded.reshape(rows, count, share), 0, 1)

time: 138 us -> 139 us (level)
  starting transfers between devices: 61.3 us -> 72.1 us
  waiting for transfers between devices: 40.4 us -> 29.9 us
    ppermute x15, starting transfers between devices: 23 us -> 28.4 us  [exchange(): columns[k] = lax.ppermute(tie(outgoing[k], *after), 'fsdp', pairs)]
    ppermute x15, waiting for transfers between devices: 14.3 us -> 9.98 us  [exchange(): columns[k] = lax.ppermute(tie(outgoing[k], *after), 'fsdp', pairs)]
    ppermute x8, waiting for transfers between devices: 7.98 us -> 4.06 us  [the longest x3 2.27 us: gather_and_exchange(): held.append(lax.ppermute(block, 'tp', across))]
    ppermute x8, starting transfers between devices: 10.6 us -> 13.7 us  [the longest x3 9.4 us: gather_and_exchange(): held.append(lax.ppermute(block, 'tp', across))]
    ppermute x7, starting transfers between devices: 12.4 us -> 14.3 us  [local(): arrived[later] = lax.ppermute(block, 'fsdp', turns[(later + 1) % 2])]
    ppermute x7, waiting for transfers between devices: 7.38 us -> 5.52 us  [sum_round(): terms.append(lax.ppermute(x, axis, [(n, n ^ d) for n in range(size)]))]
    ppermute x7, starting transfers between devices: 7.18 us -> 8.84 us  [sum_round(): terms.append(lax.ppermute(x, axis, [(n, n ^ d) for n in range(size)]))]
  transfers between devices with their start and end apart: 46 -> 46, of which waited for: 17 -> 16; matrix products, arithmetic and copies ran while one was open for 0% -> 0% of each run, Pallas kernels for 19% -> 19%
where the time goes in v16:
time: 139 us; the launch traced here: 138 us
  starting transfers between devices  72.1 us (52%)
  waiting for transfers between devices  29.9 us (22%)
  Pallas kernels  28.8 us (21%)
  other arithmetic  3.98 us (3%)
  local copies, waits for them, and re-layouts  1.43 us (1%)
    ppermute x15, starting transfers between devices, exchange(): columns[k] = lax.ppermute(tie(outgoing[k], *after), 'fsdp', pairs)  28.4 us
    ppermute x7, starting transfers between devices, local(): arrived[later] = lax.ppermute(block, 'fsdp', turns[(later + 1) % 2])  14.3 us
    pallas_call x1, Pallas kernels, factor_call(): pl.pallas_call(functools.partial(factor_kernel, len(stacked), owner), in_...  14.2 us
    pallas_call x7, Pallas kernels, output_call(): pl.pallas_call(functools.partial(output_kernel, owner, factor), in_specs=...  12.7 us
    ppermute x15, waiting for transfers between devices, exchange(): columns[k] = lax.ppermute(tie(outgoing[k], *after), 'fsdp', pairs)  9.98 us
    ppermute x7, waiting for transfers between devices, local(): arrived[later] = lax.ppermute(block, 'fsdp', turns[(later + 1) % 2])  9.88 us
    ppermute x3, starting transfers between devices, gather_and_exchange(): held.append(lax.ppermute(block, 'tp', across))  9.4 us
    ppermute x7, starting transfers between devices, sum_round(): terms.append(lax.ppermute(x, axis, [(n, n ^ d) for n in range(size)]))  8.84 us
  transfers between devices with their start and end apart: 46, of which 16 were waited for; matrix products, arithmetic and copies ran while one was open for 0% of the time, Pallas kernels for 19%

profile of v16, /device:TPU:1, one launch (start us, length us, event | category | flops | bytes accessed | tf_op | source)
XLA Modules:
  0.0 138.4 jit_solution(8545810685920053986)
XLA Ops:
  0.6 4.0 %convert_add_fusion.base_ref = f32[96,13824]{1,0:T(8,128)S(1)} fusion(f32[96,13824]{1,0:T(8,128)} %param.3, bf16[96,13824]{1,0:T(8,128)(2,1)} %param.4), kind=kLoop, calls=%fused_computation | loop fusion | flops 2654208 | bytes 13271040 | tf_op jit(solution)/shard_map/add | solution.py:402
  7.2 2.1 %collective-permute-start = (f32[96,256]{1,0:T(8,128)S(1)}, f32[96,256]{1,0:T(8,128)S(1)}, u32[]{:S(2)}, u32[]{:S(2)}) collective-permute-start(f32[96,256]{1,0:T(8,128)S(1)} %fusion), channel_id=1, source_target_pairs={{0,1},{1,0},{2,3},{3,2},{4,5},{5,4},{6,7},{7,6},{8,9},{9,8},{10,11... | collective-permute-start | bytes 294920 | tf_op jit(solution)/shard_map/ppermute | solution.py:354
  12.3 2.3 %collective-permute-start.3 = (bf16[96,896]{1,0:T(8,128)(2,1)S(1)}, bf16[96,896]{1,0:T(8,128)(2,1)S(1)}, u32[]{:S(2)}, u32[]{:S(2)}) collective-permute-start(bf16[96,896]{1,0:T(8,128)(2,1)S(1)} %get-tuple-element.67), channel_id=1, source_target_pairs={{0,16},{2,18},{4,20},{6,22},{8,24},{10,26},{12,28},{14,30},{16,0},... | collective-permute-start | bytes 516104 | tf_op jit(solution)/shard_map/ppermute | solution.py:350
  18.9 4.1 %collective-permute-done.3.refs_8_ = bf16[96,896]{1,0:T(8,128)(2,1)S(1)} collective-permute-done((bf16[96,896]{1,0:T(8,128)(2,1)S(1)}, bf16[96,896]{1,0:T(8,128)(2,1)S(1)}, u32[]{:S(2)}, u32[]{:S(2)}) %collective-permute-start.3) | collective-permute-done | bytes 172064 | tf_op jit(solution)/shard_map/ppermute | solution.py:350
  23.2 6.6 %collective-permute-start.2 = (f32[96,256]{1,0:T(8,128)S(1)}, f32[96,256]{1,0:T(8,128)S(1)}, u32[]{:S(2)}, u32[]{:S(2)}) collective-permute-start(f32[96,256]{1,0:T(8,128)S(1)} %collective-permute-done.1), channel_id=1, source_target_pairs={{0,1},{1,0},{2,3},{3,2},{4,5},{5,4},{6,7},{7,6},{8,9},{9,8},{10,11... | collective-permute-start | bytes 294920 | tf_op jit(solution)/shard_map/ppermute | solution.py:365
  32.5 2.3 %collective-permute-start.13 = (bf16[96,896]{1,0:T(8,128)(2,1)S(1)}, bf16[96,896]{1,0:T(8,128)(2,1)S(1)}, u32[]{:S(2)}, u32[]{:S(2)}) collective-permute-start(bf16[96,896]{1,0:T(8,128)(2,1)S(1)} %get-tuple-element.81), channel_id=1, source_target_pairs={{0,20},{2,22},{4,16},{6,18},{8,28},{10,30},{12,24},{14,26},{16,4},... | collective-permute-start | bytes 516104 | tf_op jit(solution)/shard_map/ppermute | solution.py:350
  36.4 4.7 %collective-permute-start.18 = (bf16[96,896]{1,0:T(8,128)(2,1)S(1)}, bf16[96,896]{1,0:T(8,128)(2,1)S(1)}, u32[]{:S(2)}, u32[]{:S(2)}) collective-permute-start(bf16[96,896]{1,0:T(8,128)(2,1)S(1)} %get-tuple-element.90), channel_id=1, source_target_pairs={{0,14},{2,12},{4,10},{6,8},{8,6},{10,4},{12,2},{14,0},{16,30},{18,... | collective-permute-start | bytes 516104 | tf_op jit(solution)/shard_map/ppermute | solution.py:350
  41.1 3.4 %collective-permute-done.14.refs_5_ = bf16[96,896]{1,0:T(8,128)(2,1)S(1)} collective-permute-done((bf16[96,896]{1,0:T(8,128)(2,1)S(1)}, bf16[96,896]{1,0:T(8,128)(2,1)S(1)}, u32[]{:S(2)}, u32[]{:S(2)}) %collective-permute-start.14) | collective-permute-done | bytes 172064 | tf_op jit(solution)/shard_map/ppermute | solution.py:350
  46.7 1.8 %collective-permute-start.12 = (f32[96,256]{1,0:T(8,128)S(1)}, f32[96,256]{1,0:T(8,128)S(1)}, u32[]{:S(2)}, u32[]{:S(2)}) collective-permute-start(f32[96,256]{1,0:T(8,128)S(1)} %collective-permute-done.11), channel_id=1, source_target_pairs={{0,1},{1,0},{2,3},{3,2},{4,5},{5,4},{6,7},{7,6},{8,9},{9,8},{10,11... | collective-permute-start | bytes 294920 | tf_op jit(solution)/shard_map/ppermute | solution.py:365
  48.5 2.3 %collective-permute-done.12 = f32[96,256]{1,0:T(8,128)S(1)} collective-permute-done((f32[96,256]{1,0:T(8,128)S(1)}, f32[96,256]{1,0:T(8,128)S(1)}, u32[]{:S(2)}, u32[]{:S(2)}) %collective-permute-start.12) | collective-permute-done | bytes 98336 | tf_op jit(solution)/shard_map/ppermute | solution.py:365
  50.8 1.8 %collective-permute-done.16 = f32[96,256]{1,0:T(8,128)S(1)} collective-permute-done((f32[96,256]{1,0:T(8,128)S(1)}, f32[96,256]{1,0:T(8,128)S(1)}, u32[]{:S(2)}, u32[]{:S(2)}) %collective-permute-start.16) | collective-permute-done | bytes 98336 | tf_op jit(solution)/shard_map/ppermute | solution.py:361
  52.6 2.4 %collective-permute-done.17.refs_11_ = bf16[96,896]{1,0:T(8,128)(2,1)S(1)} collective-permute-done((bf16[96,896]{1,0:T(8,128)(2,1)S(1)}, bf16[96,896]{1,0:T(8,128)(2,1)S(1)}, u32[]{:S(2)}, u32[]{:S(2)}) %collective-permute-start.17) | collective-permute-done | bytes 172064 | tf_op jit(solution)/shard_map/ppermute | solution.py:350
  55.0 4.0 %collective-permute-start.20 = (bf16[96,896]{1,0:T(8,128)(2,1)S(1)}, bf16[96,896]{1,0:T(8,128)(2,1)S(1)}, u32[]{:S(2)}, u32[]{:S(2)}) collective-permute-start(bf16[96,896]{1,0:T(8,128)(2,1)S(1)} %get-tuple-element.96), channel_id=1, source_target_pairs={{0,24},{2,26},{4,28},{6,30},{8,16},{10,18},{12,20},{14,22},{16,8},... | collective-permute-start | bytes 516104 | tf_op jit(solution)/shard_map/ppermute | solution.py:350
  60.7 3.2 %collective-permute-start.22 = (bf16[96,896]{1,0:T(8,128)(2,1)S(1)}, bf16[96,896]{1,0:T(8,128)(2,1)S(1)}, u32[]{:S(2)}, u32[]{:S(2)}) collective-permute-start(bf16[96,896]{1,0:T(8,128)(2,1)S(1)} %get-tuple-element.100), channel_id=1, source_target_pairs={{0,28},{2,30},{4,24},{6,26},{8,20},{10,22},{12,16},{14,18},{16,12}... | collective-permute-start | bytes 516104 | tf_op jit(solution)/shard_map/ppermute | solution.py:350
  63.9 14.2 %factor.1 = (bf16[256,1536]{1,0:T(8,128)(2,1)S(1)}, bf16[96,256]{1,0:T(8,128)(2,1)S(1)}) custom-call(f32[96,13824]{1,0:T(8,128)S(1)} %convert_add_fusion.base_ref, f32[8,96,256]{2,1,0:T(8,128)S(1)} %bitcast_dynamic-update-slice_fusion.refs_0_, f32[8,96,256]{2,1,0:T(8,128)S(1)} %collective-permute-done.19.refs_1_), custom_call_target="tpu_custom_call" | custom-call | flops 4026531840 | bytes 2359296 | tf_op jit(solution)/shard_map/factor/pallas_call | solution.py:166
  80.6 9.8 %collective-permute-start.32 = (bf16[896,256]{1,0:T(8,128)(2,1)S(1)}, bf16[896,256]{1,0:T(8,128)(2,1)S(1)}, u32[]{:S(2)}, u32[]{:S(2)}) collective-permute-start(bf16[896,256]{1,0:T(8,128)(2,1)S(1)} %get-tuple-element.104.refs_0_), channel_id=1, source_target_pairs={{8,0},{16,8},{24,16},{28,24},{20,28},{12,20},{4,12},{0,4},{2,10},{... | collective-permute-start | bytes 1376264 | tf_op jit(solution)/shard_map/ppermute | solution.py:437
  92.9 1.8 %collective-permute-start.25 = (f32[1,256]{1,0:T(1,128)S(1)}, f32[1,256]{1,0:T(1,128)S(1)}, u32[]{:S(2)}, u32[]{:S(2)}) collective-permute-start(f32[1,256]{1,0:T(1,128)S(1)} %add.29), channel_id=1, source_target_pairs={{0,2},{2,0},{4,6},{6,4},{8,10},{10,8},{12,14},{14,12},{16,18},{18,... | collective-permute-start | bytes 3080 | tf_op jit(solution)/shard_map/ppermute | solution.py:386
  103.2 2.1 %collective-permute-done.30 = f32[1,256]{1,0:T(1,128)S(1)} collective-permute-done((f32[1,256]{1,0:T(1,128)S(1)}, f32[1,256]{1,0:T(1,128)S(1)}, u32[]{:S(2)}, u32[]{:S(2)}) %collective-permute-start.30) | collective-permute-done | bytes 1056 | tf_op jit(solution)/shard_map/ppermute | solution.py:386
  108.3 2.8 %outputs.7 = (f32[96,13824]{1,0:T(8,128)}, bf16[13824,256]{1,0:T(8,128)(2,1)}, bf16[96,13824]{1,0:T(8,128)(2,1)}) custom-call(f32[96,13824]{1,0:T(8,128)S(1)} %convert_add_fusion.base_ref, bf16[96,256]{1,0:T(8,128)(2,1)S(1)} %get-tuple-element.92.ortho_ref, f32[1,256]{1,0:T(1,128)S(1)} %add_add_fusion.colsq_ref, ...), custom_call_target="tpu_custom_call" | custom-call | flops 352321536 | bytes 7110656 | tf_op jit(solution)/shard_map/outputs/pallas_call | solution.py:271
  111.5 3.0 %collective-permute-done.33.refs_0_ = bf16[896,256]{1,0:T(8,128)(2,1)S(1)} collective-permute-done((bf16[896,256]{1,0:T(8,128)(2,1)S(1)}, bf16[896,256]{1,0:T(8,128)(2,1)S(1)}, u32[]{:S(2)}, u32[]{:S(2)}) %collective-permute-start.33) | collective-permute-done | bytes 458784 | tf_op jit(solution)/shard_map/ppermute | solution.py:437
  117.2 1.7 %outputs.8 = (f32[96,13824]{1,0:T(8,128)}, bf16[13824,256]{1,0:T(8,128)(2,1)}, bf16[96,13824]{1,0:T(8,128)(2,1)}) custom-call(f32[96,13824]{1,0:T(8,128)S(1)} %convert_add_fusion.base_ref, bf16[96,256]{1,0:T(8,128)(2,1)S(1)} %get-tuple-element.92.ortho_ref, ...), custom_call_target="tpu_custom_call", output_to_operand_aliasing={{0}: (5, {}), {1}: (6, {}), {2}: (7, {})} | custom-call | flops 176160768 | bytes 3555328 | tf_op jit(solution)/shard_map/outputs/pallas_call | solution.py:271
  123.0 2.1 %collective-permute-done.34.refs_0_ = bf16[896,256]{1,0:T(8,128)(2,1)S(1)} collective-permute-done((bf16[896,256]{1,0:T(8,128)(2,1)S(1)}, bf16[896,256]{1,0:T(8,128)(2,1)S(1)}, u32[]{:S(2)}, u32[]{:S(2)}) %collective-permute-start.34) | collective-permute-done | bytes 458784 | tf_op jit(solution)/shard_map/ppermute | solution.py:437
  132.2 2.3 %collective-permute-done.39.refs_2_ = bf16[896,256]{1,0:T(8,128)(2,1)S(1)} collective-permute-done((bf16[896,256]{1,0:T(8,128)(2,1)S(1)}, bf16[896,256]{1,0:T(8,128)(2,1)S(1)}, u32[]{:S(2)}, u32[]{:S(2)}) %collective-permute-start.39) | collective-permute-done | bytes 458784 | tf_op jit(solution)/shard_map/ppermute | solution.py:437
  135.1 1.9 %outputs.12 = (f32[96,13824]{1,0:T(8,128)}, bf16[13824,256]{1,0:T(8,128)(2,1)}, bf16[96,13824]{1,0:T(8,128)(2,1)}) custom-call(f32[96,13824]{1,0:T(8,128)S(1)} %convert_add_fusion.base_ref, bf16[96,256]{1,0:T(8,128)(2,1)S(1)} %get-tuple-element.92.ortho_ref, ...), custom_call_target="tpu_custom_call", output_to_operand_aliasing={{0}: (6, {}), {1}: (7, {}), {2}: (8, {})} | custom-call | flops 264241152 | bytes 5332992 | tf_op jit(solution)/shard_map/outputs/pallas_call | solution.py:271
  (93 shorter events, 50.9 us)
Async XLA Ops:
  12.3 10.6 %collective-permute-start.3 = (bf16[96,896]{1,0:T(8,128)(2,1)S(1)}, bf16[96,896]{1,0:T(8,128)(2,1)S(1)}, u32[]{:S(2)}, u32[]{:S(2)}) collective-permute-start(bf16[96,896]{1,0:T(8,128)(2,1)S(1)} %get-tuple-element.67), channel_id=1, source_target_pairs={{0,16},{2,18},{4,20},{6,22},{8,24},{10,26},{12,28},{14,30},{16,0},... | collective-permute-start | bytes 516104 | tf_op jit(solution)/shard_map/ppermute | solution.py:350
  14.7 8.3 %collective-permute-start.1 = (f32[96,256]{1,0:T(8,128)S(1)}, f32[96,256]{1,0:T(8,128)S(1)}, u32[]{:S(2)}, u32[]{:S(2)}) collective-permute-start(f32[96,256]{1,0:T(8,128)S(1)} %get-tuple-element.130), channel_id=1, source_target_pairs={{0,8},{8,16},{16,24},{24,28},{28,20},{20,12},{12,4},{4,0},{10,2},{... | collective-permute-start | bytes 294920 | tf_op jit(solution)/shard_map/ppermute | solution.py:361
  14.9 14.8 %collective-permute-start.10 = (bf16[96,896]{1,0:T(8,128)(2,1)S(1)}, bf16[96,896]{1,0:T(8,128)(2,1)S(1)}, u32[]{:S(2)}, u32[]{:S(2)}) collective-permute-start(bf16[96,896]{1,0:T(8,128)(2,1)S(1)} %get-tuple-element.78), channel_id=1, source_target_pairs={{0,8},{2,10},{4,12},{6,14},{8,0},{10,2},{12,4},{14,6},{16,24},{18,... | collective-permute-start | bytes 516104 | tf_op jit(solution)/shard_map/ppermute | solution.py:350
  16.2 15.2 %collective-permute-start.9 = (bf16[96,896]{1,0:T(8,128)(2,1)S(1)}, bf16[96,896]{1,0:T(8,128)(2,1)S(1)}, u32[]{:S(2)}, u32[]{:S(2)}) collective-permute-start(bf16[96,896]{1,0:T(8,128)(2,1)S(1)} %get-tuple-element.76), channel_id=1, source_target_pairs={{0,6},{2,4},{4,2},{6,0},{8,14},{10,12},{12,10},{14,8},{16,22},{18,... | collective-permute-start | bytes 516104 | tf_op jit(solution)/shard_map/ppermute | solution.py:350
  17.8 14.8 %collective-permute-start.8 = (bf16[96,896]{1,0:T(8,128)(2,1)S(1)}, bf16[96,896]{1,0:T(8,128)(2,1)S(1)}, u32[]{:S(2)}, u32[]{:S(2)}) collective-permute-start(bf16[96,896]{1,0:T(8,128)(2,1)S(1)} %get-tuple-element.74), channel_id=1, source_target_pairs={{0,18},{2,16},{4,22},{6,20},{8,26},{10,24},{12,30},{14,28},{16,2},... | collective-permute-start | bytes 516104 | tf_op jit(solution)/shard_map/ppermute | solution.py:350
  23.0 11.9 %collective-permute-start.6 = (f32[96,256]{1,0:T(8,128)S(1)}, f32[96,256]{1,0:T(8,128)S(1)}, u32[]{:S(2)}, u32[]{:S(2)}) collective-permute-start(f32[96,256]{1,0:T(8,128)S(1)} %collective-permute-done.1), channel_id=1, source_target_pairs={{0,8},{8,16},{16,24},{24,28},{28,20},{20,12},{12,4},{4,0},{10,2},{... | collective-permute-start | bytes 294920 | tf_op jit(solution)/shard_map/ppermute | solution.py:361
  23.2 12.1 %collective-permute-start.2 = (f32[96,256]{1,0:T(8,128)S(1)}, f32[96,256]{1,0:T(8,128)S(1)}, u32[]{:S(2)}, u32[]{:S(2)}) collective-permute-start(f32[96,256]{1,0:T(8,128)S(1)} %collective-permute-done.1), channel_id=1, source_target_pairs={{0,1},{1,0},{2,3},{3,2},{4,5},{5,4},{6,7},{7,6},{8,9},{9,8},{10,11... | collective-permute-start | bytes 294920 | tf_op jit(solution)/shard_map/ppermute | solution.py:365
  31.4 13.1 %collective-permute-start.14 = (bf16[96,896]{1,0:T(8,128)(2,1)S(1)}, bf16[96,896]{1,0:T(8,128)(2,1)S(1)}, u32[]{:S(2)}, u32[]{:S(2)}) collective-permute-start(bf16[96,896]{1,0:T(8,128)(2,1)S(1)} %get-tuple-element.83), channel_id=1, source_target_pairs={{0,10},{2,8},{4,14},{6,12},{8,2},{10,0},{12,6},{14,4},{16,26},{18,... | collective-permute-start | bytes 516104 | tf_op jit(solution)/shard_map/ppermute | solution.py:350
  32.5 13.0 %collective-permute-start.13 = (bf16[96,896]{1,0:T(8,128)(2,1)S(1)}, bf16[96,896]{1,0:T(8,128)(2,1)S(1)}, u32[]{:S(2)}, u32[]{:S(2)}) collective-permute-start(bf16[96,896]{1,0:T(8,128)(2,1)S(1)} %get-tuple-element.81), channel_id=1, source_target_pairs={{0,20},{2,22},{4,16},{6,18},{8,28},{10,30},{12,24},{14,26},{16,4},... | collective-permute-start | bytes 516104 | tf_op jit(solution)/shard_map/ppermute | solution.py:350
  34.8 10.7 %collective-permute-start.11 = (f32[96,256]{1,0:T(8,128)S(1)}, f32[96,256]{1,0:T(8,128)S(1)}, u32[]{:S(2)}, u32[]{:S(2)}) collective-permute-start(f32[96,256]{1,0:T(8,128)S(1)} %collective-permute-done.6), channel_id=1, source_target_pairs={{0,8},{8,16},{16,24},{24,28},{28,20},{20,12},{12,4},{4,0},{10,2},{... | collective-permute-start | bytes 294920 | tf_op jit(solution)/shard_map/ppermute | solution.py:361
  35.3 13.2 %collective-permute-start.7 = (f32[96,256]{1,0:T(8,128)S(1)}, f32[96,256]{1,0:T(8,128)S(1)}, u32[]{:S(2)}, u32[]{:S(2)}) collective-permute-start(f32[96,256]{1,0:T(8,128)S(1)} %collective-permute-done.6), channel_id=1, source_target_pairs={{0,1},{1,0},{2,3},{3,2},{4,5},{5,4},{6,7},{7,6},{8,9},{9,8},{10,11... | collective-permute-start | bytes 294920 | tf_op jit(solution)/shard_map/ppermute | solution.py:365
  36.4 16.2 %collective-permute-start.18 = (bf16[96,896]{1,0:T(8,128)(2,1)S(1)}, bf16[96,896]{1,0:T(8,128)(2,1)S(1)}, u32[]{:S(2)}, u32[]{:S(2)}) collective-permute-start(bf16[96,896]{1,0:T(8,128)(2,1)S(1)} %get-tuple-element.90), channel_id=1, source_target_pairs={{0,14},{2,12},{4,10},{6,8},{8,6},{10,4},{12,2},{14,0},{16,30},{18,... | collective-permute-start | bytes 516104 | tf_op jit(solution)/shard_map/ppermute | solution.py:350
  44.5 10.5 %collective-permute-start.17 = (bf16[96,896]{1,0:T(8,128)(2,1)S(1)}, bf16[96,896]{1,0:T(8,128)(2,1)S(1)}, u32[]{:S(2)}, u32[]{:S(2)}) collective-permute-start(bf16[96,896]{1,0:T(8,128)(2,1)S(1)} %get-tuple-element.88), channel_id=1, source_target_pairs={{0,22},{2,20},{4,18},{6,16},{8,30},{10,28},{12,26},{14,24},{16,6},... | collective-permute-start | bytes 516104 | tf_op jit(solution)/shard_map/ppermute | solution.py:350
  55.0 8.8 %collective-permute-start.19 = (f32[8,96,256]{2,1,0:T(8,128)S(1)}, f32[8,96,256]{2,1,0:T(8,128)S(1)}, u32[]{:S(2)}, u32[]{:S(2)}) collective-permute-start(f32[8,96,256]{2,1,0:T(8,128)S(1)} %bitcast_dynamic-update-slice_fusion.refs_0_), channel_id=1, source_target_pairs={{0,2},{2,0},{4,6},{6,4},{8,10},{10,8},{12,14},{14,12},{16,18},{18,... | collective-permute-start | bytes 2359304 | tf_op jit(solution)/shard_map/ppermute | solution.py:369
  55.0 23.1 %collective-permute-start.20 = (bf16[96,896]{1,0:T(8,128)(2,1)S(1)}, bf16[96,896]{1,0:T(8,128)(2,1)S(1)}, u32[]{:S(2)}, u32[]{:S(2)}) collective-permute-start(bf16[96,896]{1,0:T(8,128)(2,1)S(1)} %get-tuple-element.96), channel_id=1, source_target_pairs={{0,24},{2,26},{4,28},{6,30},{8,16},{10,18},{12,20},{14,22},{16,8},... | collective-permute-start | bytes 516104 | tf_op jit(solution)/shard_map/ppermute | solution.py:350
  59.0 19.1 %collective-permute-start.23 = (bf16[96,896]{1,0:T(8,128)(2,1)S(1)}, bf16[96,896]{1,0:T(8,128)(2,1)S(1)}, u32[]{:S(2)}, u32[]{:S(2)}) collective-permute-start(bf16[96,896]{1,0:T(8,128)(2,1)S(1)} %get-tuple-element.102), channel_id=1, source_target_pairs={{0,30},{2,28},{4,26},{6,24},{8,22},{10,20},{12,18},{14,16},{16,14}... | collective-permute-start | bytes 516104 | tf_op jit(solution)/shard_map/ppermute | solution.py:350
  60.7 17.5 %collective-permute-start.22 = (bf16[96,896]{1,0:T(8,128)(2,1)S(1)}, bf16[96,896]{1,0:T(8,128)(2,1)S(1)}, u32[]{:S(2)}, u32[]{:S(2)}) collective-permute-start(bf16[96,896]{1,0:T(8,128)(2,1)S(1)} %get-tuple-element.100), channel_id=1, source_target_pairs={{0,28},{2,30},{4,24},{6,26},{8,20},{10,22},{12,16},{14,18},{16,12}... | collective-permute-start | bytes 516104 | tf_op jit(solution)/shard_map/ppermute | solution.py:350
  63.9 14.3 %collective-permute-start.21 = (bf16[96,896]{1,0:T(8,128)(2,1)S(1)}, bf16[96,896]{1,0:T(8,128)(2,1)S(1)}, u32[]{:S(2)}, u32[]{:S(2)}) collective-permute-start(bf16[96,896]{1,0:T(8,128)(2,1)S(1)} %get-tuple-element.98), channel_id=1, source_target_pairs={{0,26},{2,24},{4,30},{6,28},{8,18},{10,16},{12,22},{14,20},{16,10}... | collective-permute-start | bytes 516104 | tf_op jit(solution)/shard_map/ppermute | solution.py:350
  79.5 25.9 %collective-permute-start.31 = (bf16[896,256]{1,0:T(8,128)(2,1)S(1)}, bf16[896,256]{1,0:T(8,128)(2,1)S(1)}, u32[]{:S(2)}, u32[]{:S(2)}) collective-permute-start(bf16[896,256]{1,0:T(8,128)(2,1)S(1)} %get-tuple-element.104.refs_0_), channel_id=1, source_target_pairs={{0,8},{8,16},{16,24},{24,28},{28,20},{20,12},{12,4},{4,0},{10,2},{... | collective-permute-start | bytes 1376264 | tf_op jit(solution)/shard_map/ppermute | solution.py:437
  80.6 24.7 %collective-permute-start.32 = (bf16[896,256]{1,0:T(8,128)(2,1)S(1)}, bf16[896,256]{1,0:T(8,128)(2,1)S(1)}, u32[]{:S(2)}, u32[]{:S(2)}) collective-permute-start(bf16[896,256]{1,0:T(8,128)(2,1)S(1)} %get-tuple-element.104.refs_0_), channel_id=1, source_target_pairs={{8,0},{16,8},{24,16},{28,24},{20,28},{12,20},{4,12},{0,4},{2,10},{... | collective-permute-start | bytes 1376264 | tf_op jit(solution)/shard_map/ppermute | solution.py:437
  111.5 9.0 %collective-permute-start.41 = (bf16[896,256]{1,0:T(8,128)(2,1)S(1)}, bf16[896,256]{1,0:T(8,128)(2,1)S(1)}, u32[]{:S(2)}, u32[]{:S(2)}) collective-permute-start(bf16[896,256]{1,0:T(8,128)(2,1)S(1)} %collective-permute-done.32.refs_0_), channel_id=1, source_target_pairs={{8,0},{16,8},{24,16},{28,24},{20,28},{12,20},{4,12},{0,4},{2,10},{... | collective-permute-start | bytes 1376264 | tf_op jit(solution)/shard_map/ppermute | solution.py:437
  116.1 9.0 %collective-permute-start.34 = (bf16[896,256]{1,0:T(8,128)(2,1)S(1)}, bf16[896,256]{1,0:T(8,128)(2,1)S(1)}, u32[]{:S(2)}, u32[]{:S(2)}) collective-permute-start(bf16[896,256]{1,0:T(8,128)(2,1)S(1)} %collective-permute-done.33.refs_0_), channel_id=1, source_target_pairs={{0,8},{8,16},{16,24},{24,28},{28,20},{20,12},{12,4},{4,0},{10,2},{... | collective-permute-start | bytes 1376264 | tf_op jit(solution)/shard_map/ppermute | solution.py:437
  121.0 9.0 %collective-permute-start.44 = (bf16[896,256]{1,0:T(8,128)(2,1)S(1)}, bf16[896,256]{1,0:T(8,128)(2,1)S(1)}, u32[]{:S(2)}, u32[]{:S(2)}) collective-permute-start(bf16[896,256]{1,0:T(8,128)(2,1)S(1)} %collective-permute-done.41.refs_0_), channel_id=1, source_target_pairs={{8,0},{16,8},{24,16},{28,24},{20,28},{12,20},{4,12},{0,4},{2,10},{... | collective-permute-start | bytes 1376264 | tf_op jit(solution)/shard_map/ppermute | solution.py:437
  126.3 8.2 %collective-permute-start.39 = (bf16[896,256]{1,0:T(8,128)(2,1)S(1)}, bf16[896,256]{1,0:T(8,128)(2,1)S(1)}, u32[]{:S(2)}, u32[]{:S(2)}) collective-permute-start(bf16[896,256]{1,0:T(8,128)(2,1)S(1)} %collective-permute-done.34.refs_0_), channel_id=1, source_target_pairs={{0,8},{8,16},{16,24},{24,28},{28,20},{20,12},{12,4},{4,0},{10,2},{... | collective-permute-start | bytes 1376264 | tf_op jit(solution)/shard_map/ppermute | solution.py:437
  (23 other events, 115.9 us)

commit v17 on v16

--- a/solution.py
+++ b/solution.py
@@ -333,9 +333,9 @@
 def exchange_windows(count):
     chips, steps = count // 2, count // 4
     far, near = list(range(chips, count)), list(range(1, chips))
-    each = -(-len(near) // (steps + 1))
-    windows = [far[w : w + 1] + near[w * each : (w + 1) * each] for w in range(steps + 1)]
-    return windows + [far[steps + 1 :]]
+    each = -(-len(near) // steps)
+    windows = [far[w + 1 : w + 2] + near[(w - 1) * each : w * each] for w in range(1, steps + 1)]
+    return [far[:2]] + windows + [far[steps + 2 :]]
 
 
 def gather_and_exchange(sketch, outgoing, count):

time: 139 us -> 137 us (0.986)
  starting transfers between devices: 72.1 us -> 59.4 us
  waiting for transfers between devices: 29.9 us -> 41.1 us
    ppermute x15, waiting for transfers between devices: 9.98 us -> 19.1 us  [exchange(): columns[k] = lax.ppermute(tie(outgoing[k], *after), 'fsdp', pairs)]
    ppermute x15, starting transfers between devices: 28.4 us -> 21.5 us  [exchange(): columns[k] = lax.ppermute(tie(outgoing[k], *after), 'fsdp', pairs)]
    ppermute x7, starting transfers between devices: 14.3 us -> 9.27 us  [local(): arrived[later] = lax.ppermute(block, 'fsdp', turns[(later + 1) % 2])]
    ppermute x4, waiting for transfers between devices: 1.79 us -> 3.68 us  [gather_and_exchange(): block = lax.ppermute(block, ('fsdp', 'tp'), turns)]
  transfers between devices with their start and end apart: 46 -> 46, of which waited for: 16 -> 14; matrix products, arithmetic and copies ran while one was open for 0% -> 0% of each run, Pallas kernels for 19% -> 19%
where the time goes in v17:
time: 137 us
  starting transfers between devices  59.4 us (43%)
  waiting for transfers between devices  41.1 us (30%)
  Pallas kernels  28.8 us (21%)
  other arithmetic  3.98 us (3%)
  local copies, waits for them, and re-layouts  1.43 us (1%)
    ppermute x15, starting transfers between devices, exchange(): columns[k] = lax.ppermute(tie(outgoing[k], *after), 'fsdp', pairs)  21.5 us
    ppermute x15, waiting for transfers between devices, exchange(): columns[k] = lax.ppermute(tie(outgoing[k], *after), 'fsdp', pairs)  19.1 us
    pallas_call x1, Pallas kernels, factor_call(): pl.pallas_call(functools.partial(factor_kernel, len(stacked), owner), in_...  14.2 us
    pallas_call x7, Pallas kernels, output_call(): pl.pallas_call(functools.partial(output_kernel, owner, factor), in_specs=...  12.7 us
    ppermute x7, starting transfers between devices, local(): arrived[later] = lax.ppermute(block, 'fsdp', turns[(later + 1) % 2])  9.27 us
    ppermute x7, waiting for transfers between devices, local(): arrived[later] = lax.ppermute(block, 'fsdp', turns[(later + 1) % 2])  8.73 us
    ppermute x3, starting transfers between devices, gather_and_exchange(): held.append(lax.ppermute(block, 'tp', across))  8.18 us
    ppermute x7, starting transfers between devices, sum_round(): terms.append(lax.ppermute(x, axis, [(n, n ^ d) for n in range(size)]))  7.9 us
  transfers between devices with their start and end apart: 46, of which 14 were waited for; matrix products, arithmetic and copies ran while one was open for 0% of the time, Pallas kernels for 19%

profile of v17, /device:TPU:1, one launch (start us, length us, event | category | flops | bytes accessed | tf_op | source)
XLA Modules:
  0.0 137.1 jit_solution(15796462540615400780)
XLA Ops:
  0.6 4.0 %convert_add_fusion.base_ref = f32[96,13824]{1,0:T(8,128)S(1)} fusion(f32[96,13824]{1,0:T(8,128)} %param.3, bf16[96,13824]{1,0:T(8,128)(2,1)} %param.4), kind=kLoop, calls=%fused_computation | loop fusion | flops 2654208 | bytes 13271040 | tf_op jit(solution)/shard_map/add | solution.py:402
  7.2 2.1 %collective-permute-start = (f32[96,256]{1,0:T(8,128)S(1)}, f32[96,256]{1,0:T(8,128)S(1)}, u32[]{:S(2)}, u32[]{:S(2)}) collective-permute-start(f32[96,256]{1,0:T(8,128)S(1)} %fusion), channel_id=1, source_target_pairs={{0,1},{1,0},{2,3},{3,2},{4,5},{5,4},{6,7},{7,6},{8,9},{9,8},{10,11... | collective-permute-start | bytes 294920 | tf_op jit(solution)/shard_map/ppermute | solution.py:354
  9.8 3.2 %collective-permute-start.4 = (bf16[96,896]{1,0:T(8,128)(2,1)S(1)}, bf16[96,896]{1,0:T(8,128)(2,1)S(1)}, u32[]{:S(2)}, u32[]{:S(2)}) collective-permute-start(bf16[96,896]{1,0:T(8,128)(2,1)S(1)} %get-tuple-element.69), channel_id=1, source_target_pairs={{0,18},{2,16},{4,22},{6,20},{8,26},{10,24},{12,30},{14,28},{16,2},... | collective-permute-start | bytes 516104 | tf_op jit(solution)/shard_map/ppermute | solution.py:350
  15.7 9.6 %collective-permute-done.4.refs_9_ = bf16[96,896]{1,0:T(8,128)(2,1)S(1)} collective-permute-done((bf16[96,896]{1,0:T(8,128)(2,1)S(1)}, bf16[96,896]{1,0:T(8,128)(2,1)S(1)}, u32[]{:S(2)}, u32[]{:S(2)}) %collective-permute-start.4) | collective-permute-done | bytes 172064 | tf_op jit(solution)/shard_map/ppermute | solution.py:350
  25.3 3.5 %collective-permute-done.3.refs_8_ = bf16[96,896]{1,0:T(8,128)(2,1)S(1)} collective-permute-done((bf16[96,896]{1,0:T(8,128)(2,1)S(1)}, bf16[96,896]{1,0:T(8,128)(2,1)S(1)}, u32[]{:S(2)}, u32[]{:S(2)}) %collective-permute-start.3) | collective-permute-done | bytes 172064 | tf_op jit(solution)/shard_map/ppermute | solution.py:350
  30.0 5.2 %collective-permute-start.2 = (f32[96,256]{1,0:T(8,128)S(1)}, f32[96,256]{1,0:T(8,128)S(1)}, u32[]{:S(2)}, u32[]{:S(2)}) collective-permute-start(f32[96,256]{1,0:T(8,128)S(1)} %collective-permute-done.1), channel_id=1, source_target_pairs={{0,1},{1,0},{2,3},{3,2},{4,5},{5,4},{6,7},{7,6},{8,9},{9,8},{10,11... | collective-permute-start | bytes 294920 | tf_op jit(solution)/shard_map/ppermute | solution.py:365
  35.3 2.0 %collective-permute-start.14 = (bf16[96,896]{1,0:T(8,128)(2,1)S(1)}, bf16[96,896]{1,0:T(8,128)(2,1)S(1)}, u32[]{:S(2)}, u32[]{:S(2)}) collective-permute-start(bf16[96,896]{1,0:T(8,128)(2,1)S(1)} %get-tuple-element.83), channel_id=1, source_target_pairs={{0,8},{2,10},{4,12},{6,14},{8,0},{10,2},{12,4},{14,6},{16,24},{18,... | collective-permute-start | bytes 516104 | tf_op jit(solution)/shard_map/ppermute | solution.py:350
  37.2 2.6 %collective-permute-start.13 = (bf16[96,896]{1,0:T(8,128)(2,1)S(1)}, bf16[96,896]{1,0:T(8,128)(2,1)S(1)}, u32[]{:S(2)}, u32[]{:S(2)}) collective-permute-start(bf16[96,896]{1,0:T(8,128)(2,1)S(1)} %get-tuple-element.81), channel_id=1, source_target_pairs={{0,6},{2,4},{4,2},{6,0},{8,14},{10,12},{12,10},{14,8},{16,22},{18,... | collective-permute-start | bytes 516104 | tf_op jit(solution)/shard_map/ppermute | solution.py:350
  46.1 4.1 %collective-permute-done.12.refs_11_ = bf16[96,896]{1,0:T(8,128)(2,1)S(1)} collective-permute-done((bf16[96,896]{1,0:T(8,128)(2,1)S(1)}, bf16[96,896]{1,0:T(8,128)(2,1)S(1)}, u32[]{:S(2)}, u32[]{:S(2)}) %collective-permute-start.12) | collective-permute-done | bytes 172064 | tf_op jit(solution)/shard_map/ppermute | solution.py:350
  50.3 2.1 %collective-permute-start.16 = (bf16[96,896]{1,0:T(8,128)(2,1)S(1)}, bf16[96,896]{1,0:T(8,128)(2,1)S(1)}, u32[]{:S(2)}, u32[]{:S(2)}) collective-permute-start(bf16[96,896]{1,0:T(8,128)(2,1)S(1)} %get-tuple-element.86), channel_id=1, source_target_pairs={{0,24},{2,26},{4,28},{6,30},{8,16},{10,18},{12,20},{14,22},{16,8},... | collective-permute-start | bytes 516104 | tf_op jit(solution)/shard_map/ppermute | solution.py:350
  54.0 2.7 %collective-permute-done.11 = f32[96,256]{1,0:T(8,128)S(1)} collective-permute-done((f32[96,256]{1,0:T(8,128)S(1)}, f32[96,256]{1,0:T(8,128)S(1)}, u32[]{:S(2)}, u32[]{:S(2)}) %collective-permute-start.11) | collective-permute-done | bytes 98336 | tf_op jit(solution)/shard_map/ppermute | solution.py:365
  56.7 3.7 %collective-permute-done.15 = f32[96,256]{1,0:T(8,128)S(1)} collective-permute-done((f32[96,256]{1,0:T(8,128)S(1)}, f32[96,256]{1,0:T(8,128)S(1)}, u32[]{:S(2)}, u32[]{:S(2)}) %collective-permute-start.15) | collective-permute-done | bytes 98336 | tf_op jit(solution)/shard_map/ppermute | solution.py:361
  60.5 3.2 %collective-permute-start.21 = (bf16[96,896]{1,0:T(8,128)(2,1)S(1)}, bf16[96,896]{1,0:T(8,128)(2,1)S(1)}, u32[]{:S(2)}, u32[]{:S(2)}) collective-permute-start(bf16[96,896]{1,0:T(8,128)(2,1)S(1)} %get-tuple-element.98), channel_id=1, source_target_pairs={{0,26},{2,24},{4,30},{6,28},{8,18},{10,16},{12,22},{14,20},{16,10}... | collective-permute-start | bytes 516104 | tf_op jit(solution)/shard_map/ppermute | solution.py:350
  63.7 1.9 %collective-permute-start.23 = (bf16[96,896]{1,0:T(8,128)(2,1)S(1)}, bf16[96,896]{1,0:T(8,128)(2,1)S(1)}, u32[]{:S(2)}, u32[]{:S(2)}) collective-permute-start(bf16[96,896]{1,0:T(8,128)(2,1)S(1)} %get-tuple-element.102), channel_id=1, source_target_pairs={{0,30},{2,28},{4,26},{6,24},{8,22},{10,20},{12,18},{14,16},{16,14}... | collective-permute-start | bytes 516104 | tf_op jit(solution)/shard_map/ppermute | solution.py:350
  65.6 2.6 %collective-permute-start.22 = (bf16[96,896]{1,0:T(8,128)(2,1)S(1)}, bf16[96,896]{1,0:T(8,128)(2,1)S(1)}, u32[]{:S(2)}, u32[]{:S(2)}) collective-permute-start(bf16[96,896]{1,0:T(8,128)(2,1)S(1)} %get-tuple-element.100), channel_id=1, source_target_pairs={{0,28},{2,30},{4,24},{6,26},{8,20},{10,22},{12,16},{14,18},{16,12}... | collective-permute-start | bytes 516104 | tf_op jit(solution)/shard_map/ppermute | solution.py:350
  68.2 14.2 %factor.1 = (bf16[256,1536]{1,0:T(8,128)(2,1)S(1)}, bf16[96,256]{1,0:T(8,128)(2,1)S(1)}) custom-call(f32[96,13824]{1,0:T(8,128)S(1)} %convert_add_fusion.base_ref, f32[8,96,256]{2,1,0:T(8,128)S(1)} %bitcast_dynamic-update-slice_fusion.refs_0_, f32[8,96,256]{2,1,0:T(8,128)S(1)} %collective-permute-done.19.refs_1_), custom_call_target="tpu_custom_call" | custom-call | flops 4026531840 | bytes 2359296 | tf_op jit(solution)/shard_map/factor/pallas_call | solution.py:166
  83.9 4.2 %collective-permute-start.32 = (bf16[896,256]{1,0:T(8,128)(2,1)S(1)}, bf16[896,256]{1,0:T(8,128)(2,1)S(1)}, u32[]{:S(2)}, u32[]{:S(2)}) collective-permute-start(bf16[896,256]{1,0:T(8,128)(2,1)S(1)} %get-tuple-element.104.refs_0_), channel_id=1, source_target_pairs={{8,0},{16,8},{24,16},{28,24},{20,28},{12,20},{4,12},{0,4},{2,10},{... | collective-permute-start | bytes 1376264 | tf_op jit(solution)/shard_map/ppermute | solution.py:437
  88.9 1.9 %collective-permute-done.24 = f32[1,256]{1,0:T(1,128)S(1)} collective-permute-done((f32[1,256]{1,0:T(1,128)S(1)}, f32[1,256]{1,0:T(1,128)S(1)}, u32[]{:S(2)}, u32[]{:S(2)}) %collective-permute-start.24) | collective-permute-done | bytes 1056 | tf_op jit(solution)/shard_map/ppermute | solution.py:386
  94.3 2.9 %collective-permute-done.26 = f32[1,256]{1,0:T(1,128)S(1)} collective-permute-done((f32[1,256]{1,0:T(1,128)S(1)}, f32[1,256]{1,0:T(1,128)S(1)}, u32[]{:S(2)}, u32[]{:S(2)}) %collective-permute-start.26) | collective-permute-done | bytes 1056 | tf_op jit(solution)/shard_map/ppermute | solution.py:386
  102.1 1.9 %collective-permute-done.30 = f32[1,256]{1,0:T(1,128)S(1)} collective-permute-done((f32[1,256]{1,0:T(1,128)S(1)}, f32[1,256]{1,0:T(1,128)S(1)}, u32[]{:S(2)}, u32[]{:S(2)}) %collective-permute-start.30) | collective-permute-done | bytes 1056 | tf_op jit(solution)/shard_map/ppermute | solution.py:386
  107.0 2.8 %outputs.7 = (f32[96,13824]{1,0:T(8,128)}, bf16[13824,256]{1,0:T(8,128)(2,1)}, bf16[96,13824]{1,0:T(8,128)(2,1)}) custom-call(f32[96,13824]{1,0:T(8,128)S(1)} %convert_add_fusion.base_ref, bf16[96,256]{1,0:T(8,128)(2,1)S(1)} %get-tuple-element.92.ortho_ref, f32[1,256]{1,0:T(1,128)S(1)} %add_add_fusion.colsq_ref, ...), custom_call_target="tpu_custom_call" | custom-call | flops 352321536 | bytes 7110656 | tf_op jit(solution)/shard_map/outputs/pallas_call | solution.py:271
  110.2 3.0 %collective-permute-done.33.refs_0_ = bf16[896,256]{1,0:T(8,128)(2,1)S(1)} collective-permute-done((bf16[896,256]{1,0:T(8,128)(2,1)S(1)}, bf16[896,256]{1,0:T(8,128)(2,1)S(1)}, u32[]{:S(2)}, u32[]{:S(2)}) %collective-permute-start.33) | collective-permute-done | bytes 458784 | tf_op jit(solution)/shard_map/ppermute | solution.py:437
  121.7 2.0 %collective-permute-done.34.refs_0_ = bf16[896,256]{1,0:T(8,128)(2,1)S(1)} collective-permute-done((bf16[896,256]{1,0:T(8,128)(2,1)S(1)}, bf16[896,256]{1,0:T(8,128)(2,1)S(1)}, u32[]{:S(2)}, u32[]{:S(2)}) %collective-permute-start.34) | collective-permute-done | bytes 458784 | tf_op jit(solution)/shard_map/ppermute | solution.py:437
  131.3 1.9 %collective-permute-done.39.refs_2_ = bf16[896,256]{1,0:T(8,128)(2,1)S(1)} collective-permute-done((bf16[896,256]{1,0:T(8,128)(2,1)S(1)}, bf16[896,256]{1,0:T(8,128)(2,1)S(1)}, u32[]{:S(2)}, u32[]{:S(2)}) %collective-permute-start.39) | collective-permute-done | bytes 458784 | tf_op jit(solution)/shard_map/ppermute | solution.py:437
  (93 shorter events, 48.7 us)
Async XLA Ops:
  9.8 15.5 %collective-permute-start.4 = (bf16[96,896]{1,0:T(8,128)(2,1)S(1)}, bf16[96,896]{1,0:T(8,128)(2,1)S(1)}, u32[]{:S(2)}, u32[]{:S(2)}) collective-permute-start(bf16[96,896]{1,0:T(8,128)(2,1)S(1)} %get-tuple-element.69), channel_id=1, source_target_pairs={{0,18},{2,16},{4,22},{6,20},{8,26},{10,24},{12,30},{14,28},{16,2},... | collective-permute-start | bytes 516104 | tf_op jit(solution)/shard_map/ppermute | solution.py:350
  13.0 15.8 %collective-permute-start.3 = (bf16[96,896]{1,0:T(8,128)(2,1)S(1)}, bf16[96,896]{1,0:T(8,128)(2,1)S(1)}, u32[]{:S(2)}, u32[]{:S(2)}) collective-permute-start(bf16[96,896]{1,0:T(8,128)(2,1)S(1)} %get-tuple-element.67), channel_id=1, source_target_pairs={{0,16},{2,18},{4,20},{6,22},{8,24},{10,26},{12,28},{14,30},{16,0},... | collective-permute-start | bytes 516104 | tf_op jit(solution)/shard_map/ppermute | solution.py:350
  13.1 15.7 %collective-permute-start.1 = (f32[96,256]{1,0:T(8,128)S(1)}, f32[96,256]{1,0:T(8,128)S(1)}, u32[]{:S(2)}, u32[]{:S(2)}) collective-permute-start(f32[96,256]{1,0:T(8,128)S(1)} %get-tuple-element.130), channel_id=1, source_target_pairs={{0,8},{8,16},{16,24},{24,28},{28,20},{20,12},{12,4},{4,0},{10,2},{... | collective-permute-start | bytes 294920 | tf_op jit(solution)/shard_map/ppermute | solution.py:361
  14.4 20.9 %collective-permute-start.9 = (bf16[96,896]{1,0:T(8,128)(2,1)S(1)}, bf16[96,896]{1,0:T(8,128)(2,1)S(1)}, u32[]{:S(2)}, u32[]{:S(2)}) collective-permute-start(bf16[96,896]{1,0:T(8,128)(2,1)S(1)} %get-tuple-element.76), channel_id=1, source_target_pairs={{0,4},{2,6},{4,0},{6,2},{8,12},{10,14},{12,8},{14,10},{16,20},{18,... | collective-permute-start | bytes 516104 | tf_op jit(solution)/shard_map/ppermute | solution.py:350
  15.7 21.6 %collective-permute-start.8 = (bf16[96,896]{1,0:T(8,128)(2,1)S(1)}, bf16[96,896]{1,0:T(8,128)(2,1)S(1)}, u32[]{:S(2)}, u32[]{:S(2)}) collective-permute-start(bf16[96,896]{1,0:T(8,128)(2,1)S(1)} %get-tuple-element.74), channel_id=1, source_target_pairs={{0,2},{2,0},{4,6},{6,4},{8,10},{10,8},{12,14},{14,12},{16,18},{18,... | collective-permute-start | bytes 516104 | tf_op jit(solution)/shard_map/ppermute | solution.py:350
  25.3 14.5 %collective-permute-start.7 = (bf16[96,896]{1,0:T(8,128)(2,1)S(1)}, bf16[96,896]{1,0:T(8,128)(2,1)S(1)}, u32[]{:S(2)}, u32[]{:S(2)}) collective-permute-start(bf16[96,896]{1,0:T(8,128)(2,1)S(1)} %get-tuple-element.72), channel_id=1, source_target_pairs={{0,20},{2,22},{4,16},{6,18},{8,28},{10,30},{12,24},{14,26},{16,4},... | collective-permute-start | bytes 516104 | tf_op jit(solution)/shard_map/ppermute | solution.py:350
  28.8 11.1 %collective-permute-start.5 = (f32[96,256]{1,0:T(8,128)S(1)}, f32[96,256]{1,0:T(8,128)S(1)}, u32[]{:S(2)}, u32[]{:S(2)}) collective-permute-start(f32[96,256]{1,0:T(8,128)S(1)} %collective-permute-done.1), channel_id=1, source_target_pairs={{0,8},{8,16},{16,24},{24,28},{28,20},{20,12},{12,4},{4,0},{10,2},{... | collective-permute-start | bytes 294920 | tf_op jit(solution)/shard_map/ppermute | solution.py:361
  30.0 9.9 %collective-permute-start.2 = (f32[96,256]{1,0:T(8,128)S(1)}, f32[96,256]{1,0:T(8,128)S(1)}, u32[]{:S(2)}, u32[]{:S(2)}) collective-permute-start(f32[96,256]{1,0:T(8,128)S(1)} %collective-permute-done.1), channel_id=1, source_target_pairs={{0,1},{1,0},{2,3},{3,2},{4,5},{5,4},{6,7},{7,6},{8,9},{9,8},{10,11... | collective-permute-start | bytes 294920 | tf_op jit(solution)/shard_map/ppermute | solution.py:365
  39.9 10.4 %collective-permute-start.12 = (bf16[96,896]{1,0:T(8,128)(2,1)S(1)}, bf16[96,896]{1,0:T(8,128)(2,1)S(1)}, u32[]{:S(2)}, u32[]{:S(2)}) collective-permute-start(bf16[96,896]{1,0:T(8,128)(2,1)S(1)} %get-tuple-element.79), channel_id=1, source_target_pairs={{0,22},{2,20},{4,18},{6,16},{8,30},{10,28},{12,26},{14,24},{16,6},... | collective-permute-start | bytes 516104 | tf_op jit(solution)/shard_map/ppermute | solution.py:350
  39.9 12.5 %collective-permute-start.10 = (f32[96,256]{1,0:T(8,128)S(1)}, f32[96,256]{1,0:T(8,128)S(1)}, u32[]{:S(2)}, u32[]{:S(2)}) collective-permute-start(f32[96,256]{1,0:T(8,128)S(1)} %collective-permute-done.5), channel_id=1, source_target_pairs={{0,8},{8,16},{16,24},{24,28},{28,20},{20,12},{12,4},{4,0},{10,2},{... | collective-permute-start | bytes 294920 | tf_op jit(solution)/shard_map/ppermute | solution.py:361
  39.9 12.7 %collective-permute-start.6 = (f32[96,256]{1,0:T(8,128)S(1)}, f32[96,256]{1,0:T(8,128)S(1)}, u32[]{:S(2)}, u32[]{:S(2)}) collective-permute-start(f32[96,256]{1,0:T(8,128)S(1)} %collective-permute-done.5), channel_id=1, source_target_pairs={{0,1},{1,0},{2,3},{3,2},{4,5},{5,4},{6,7},{7,6},{8,9},{9,8},{10,11... | collective-permute-start | bytes 294920 | tf_op jit(solution)/shard_map/ppermute | solution.py:365
  41.6 18.8 %collective-permute-start.18 = (bf16[96,896]{1,0:T(8,128)(2,1)S(1)}, bf16[96,896]{1,0:T(8,128)(2,1)S(1)}, u32[]{:S(2)}, u32[]{:S(2)}) collective-permute-start(bf16[96,896]{1,0:T(8,128)(2,1)S(1)} %get-tuple-element.90), channel_id=1, source_target_pairs={{0,12},{2,14},{4,8},{6,10},{8,4},{10,6},{12,0},{14,2},{16,28},{18,... | collective-permute-start | bytes 516104 | tf_op jit(solution)/shard_map/ppermute | solution.py:350
  45.3 15.1 %collective-permute-start.17 = (bf16[96,896]{1,0:T(8,128)(2,1)S(1)}, bf16[96,896]{1,0:T(8,128)(2,1)S(1)}, u32[]{:S(2)}, u32[]{:S(2)}) collective-permute-start(bf16[96,896]{1,0:T(8,128)(2,1)S(1)} %get-tuple-element.88), channel_id=1, source_target_pairs={{0,10},{2,8},{4,14},{6,12},{8,2},{10,0},{12,6},{14,4},{16,26},{18,... | collective-permute-start | bytes 516104 | tf_op jit(solution)/shard_map/ppermute | solution.py:350
  50.3 10.2 %collective-permute-start.16 = (bf16[96,896]{1,0:T(8,128)(2,1)S(1)}, bf16[96,896]{1,0:T(8,128)(2,1)S(1)}, u32[]{:S(2)}, u32[]{:S(2)}) collective-permute-start(bf16[96,896]{1,0:T(8,128)(2,1)S(1)} %get-tuple-element.86), channel_id=1, source_target_pairs={{0,24},{2,26},{4,28},{6,30},{8,16},{10,18},{12,20},{14,22},{16,8},... | collective-permute-start | bytes 516104 | tf_op jit(solution)/shard_map/ppermute | solution.py:350
  60.5 21.9 %collective-permute-start.21 = (bf16[96,896]{1,0:T(8,128)(2,1)S(1)}, bf16[96,896]{1,0:T(8,128)(2,1)S(1)}, u32[]{:S(2)}, u32[]{:S(2)}) collective-permute-start(bf16[96,896]{1,0:T(8,128)(2,1)S(1)} %get-tuple-element.98), channel_id=1, source_target_pairs={{0,26},{2,24},{4,30},{6,28},{8,18},{10,16},{12,22},{14,20},{16,10}... | collective-permute-start | bytes 516104 | tf_op jit(solution)/shard_map/ppermute | solution.py:350
  63.7 18.8 %collective-permute-start.20 = (bf16[96,896]{1,0:T(8,128)(2,1)S(1)}, bf16[96,896]{1,0:T(8,128)(2,1)S(1)}, u32[]{:S(2)}, u32[]{:S(2)}) collective-permute-start(bf16[96,896]{1,0:T(8,128)(2,1)S(1)} %get-tuple-element.96), channel_id=1, source_target_pairs={{0,14},{2,12},{4,10},{6,8},{8,6},{10,4},{12,2},{14,0},{16,30},{18,... | collective-permute-start | bytes 516104 | tf_op jit(solution)/shard_map/ppermute | solution.py:350
  63.7 18.8 %collective-permute-start.23 = (bf16[96,896]{1,0:T(8,128)(2,1)S(1)}, bf16[96,896]{1,0:T(8,128)(2,1)S(1)}, u32[]{:S(2)}, u32[]{:S(2)}) collective-permute-start(bf16[96,896]{1,0:T(8,128)(2,1)S(1)} %get-tuple-element.102), channel_id=1, source_target_pairs={{0,30},{2,28},{4,26},{6,24},{8,22},{10,20},{12,18},{14,16},{16,14}... | collective-permute-start | bytes 516104 | tf_op jit(solution)/shard_map/ppermute | solution.py:350
  65.6 16.8 %collective-permute-start.22 = (bf16[96,896]{1,0:T(8,128)(2,1)S(1)}, bf16[96,896]{1,0:T(8,128)(2,1)S(1)}, u32[]{:S(2)}, u32[]{:S(2)}) collective-permute-start(bf16[96,896]{1,0:T(8,128)(2,1)S(1)} %get-tuple-element.100), channel_id=1, source_target_pairs={{0,28},{2,30},{4,24},{6,26},{8,20},{10,22},{12,16},{14,18},{16,12}... | collective-permute-start | bytes 516104 | tf_op jit(solution)/shard_map/ppermute | solution.py:350
  83.8 20.2 %collective-permute-start.31 = (bf16[896,256]{1,0:T(8,128)(2,1)S(1)}, bf16[896,256]{1,0:T(8,128)(2,1)S(1)}, u32[]{:S(2)}, u32[]{:S(2)}) collective-permute-start(bf16[896,256]{1,0:T(8,128)(2,1)S(1)} %get-tuple-element.104.refs_0_), channel_id=1, source_target_pairs={{0,8},{8,16},{16,24},{24,28},{28,20},{20,12},{12,4},{4,0},{10,2},{... | collective-permute-start | bytes 1376264 | tf_op jit(solution)/shard_map/ppermute | solution.py:437
  83.9 20.1 %collective-permute-start.32 = (bf16[896,256]{1,0:T(8,128)(2,1)S(1)}, bf16[896,256]{1,0:T(8,128)(2,1)S(1)}, u32[]{:S(2)}, u32[]{:S(2)}) collective-permute-start(bf16[896,256]{1,0:T(8,128)(2,1)S(1)} %get-tuple-element.104.refs_0_), channel_id=1, source_target_pairs={{8,0},{16,8},{24,16},{28,24},{20,28},{12,20},{4,12},{0,4},{2,10},{... | collective-permute-start | bytes 1376264 | tf_op jit(solution)/shard_map/ppermute | solution.py:437
  110.2 9.0 %collective-permute-start.41 = (bf16[896,256]{1,0:T(8,128)(2,1)S(1)}, bf16[896,256]{1,0:T(8,128)(2,1)S(1)}, u32[]{:S(2)}, u32[]{:S(2)}) collective-permute-start(bf16[896,256]{1,0:T(8,128)(2,1)S(1)} %collective-permute-done.32.refs_0_), channel_id=1, source_target_pairs={{8,0},{16,8},{24,16},{28,24},{20,28},{12,20},{4,12},{0,4},{2,10},{... | collective-permute-start | bytes 1376264 | tf_op jit(solution)/shard_map/ppermute | solution.py:437
  114.7 9.0 %collective-permute-start.34 = (bf16[896,256]{1,0:T(8,128)(2,1)S(1)}, bf16[896,256]{1,0:T(8,128)(2,1)S(1)}, u32[]{:S(2)}, u32[]{:S(2)}) collective-permute-start(bf16[896,256]{1,0:T(8,128)(2,1)S(1)} %collective-permute-done.33.refs_0_), channel_id=1, source_target_pairs={{0,8},{8,16},{16,24},{24,28},{28,20},{20,12},{12,4},{4,0},{10,2},{... | collective-permute-start | bytes 1376264 | tf_op jit(solution)/shard_map/ppermute | solution.py:437
  119.9 8.9 %collective-permute-start.44 = (bf16[896,256]{1,0:T(8,128)(2,1)S(1)}, bf16[896,256]{1,0:T(8,128)(2,1)S(1)}, u32[]{:S(2)}, u32[]{:S(2)}) collective-permute-start(bf16[896,256]{1,0:T(8,128)(2,1)S(1)} %collective-permute-done.41.refs_0_), channel_id=1, source_target_pairs={{8,0},{16,8},{24,16},{28,24},{20,28},{12,20},{4,12},{0,4},{2,10},{... | collective-permute-start | bytes 1376264 | tf_op jit(solution)/shard_map/ppermute | solution.py:437
  124.7 8.6 %collective-permute-start.39 = (bf16[896,256]{1,0:T(8,128)(2,1)S(1)}, bf16[896,256]{1,0:T(8,128)(2,1)S(1)}, u32[]{:S(2)}, u32[]{:S(2)}) collective-permute-start(bf16[896,256]{1,0:T(8,128)(2,1)S(1)} %collective-permute-done.34.refs_0_), channel_id=1, source_target_pairs={{0,8},{8,16},{16,24},{24,28},{28,20},{20,12},{12,4},{4,0},{10,2},{... | collective-permute-start | bytes 1376264 | tf_op jit(solution)/shard_map/ppermute | solution.py:437
  (23 other events, 122.4 us)

commit v18 on v17

--- a/solution.py
+++ b/solution.py
@@ -372,11 +372,11 @@
 
 
 def sum_rounds(count):
-    rounds, bit = [("tp", [1])], 1
+    rounds, bit = [], 1
     while bit < count:
         rounds.append(("fsdp", [bit, 2 * bit, 3 * bit] if 2 * bit < count else [bit]))
         bit *= 4
-    return rounds
+    return rounds[::-1]
 
 
 def sum_round(x, axis, distances):
@@ -441,11 +441,12 @@
         if n == 0:
             waiting = (arrived[2], colsq)
             continue
+        if n == 1:
+            colsq = sum_round(tie(colsq, blocks[-1]), "tp", [1])
         if n == 2:
             waiting = ()
             continue
-        upto = 2 * n + (2 if n == 1 else 1 if n + 1 == chips else 0)
-        upto = min(upto, written + 4) if n + 1 < chips else upto
+        upto = {1: 4, 3: 6, chips - 1: 2 * n + 1}.get(n, 2 * n)
         result = write(owner_of(owners[written:upto]), blocks[written:upto], colsq, result)
         written, waiting = upto, tuple(result)
     return tuple(write(owner_of(owners[written:]), blocks[written:], colsq, result))

time: 137 us -> 145 us (1.058)
  waiting for transfers between devices: 41.1 us -> 51.9 us
  starting transfers between devices: 59.4 us -> 55.6 us
    ppermute x7, waiting for transfers between devices: 6.78 us -> 12.7 us  [sum_round(): terms.append(lax.ppermute(x, axis, [(n, n ^ d) for n in range(size)]))]
    ppermute x7, waiting for transfers between devices: 8.73 us -> 12.6 us  [local(): arrived[later] = lax.ppermute(block, 'fsdp', turns[(later + 1) % 2])]
    ppermute x7, starting transfers between devices: 9.27 us -> 6.52 us  [local(): arrived[later] = lax.ppermute(block, 'fsdp', turns[(later + 1) % 2])]
  transfers between devices with their start and end apart: 46 -> 46, of which waited for: 14 -> 15; matrix products, arithmetic and copies ran while one was open for 0% -> 0% of each run, Pallas kernels for 19% -> 18%
where the time goes in v18:
time: 145 us; the launch traced here: 144 us
  starting transfers between devices  55.6 us (38%)
  waiting for transfers between devices  51.9 us (36%)
  Pallas kernels  28.8 us (20%)
  other arithmetic  3.98 us (3%)
    ppermute x15, starting transfers between devices, exchange(): columns[k] = lax.ppermute(tie(outgoing[k], *after), 'fsdp', pairs)  21.5 us
    ppermute x15, waiting for transfers between devices, exchange(): columns[k] = lax.ppermute(tie(outgoing[k], *after), 'fsdp', pairs)  19.1 us
    pallas_call x1, Pallas kernels, factor_call(): pl.pallas_call(functools.partial(factor_kernel, len(stacked), owner), in_...  14.2 us
    pallas_call x7, Pallas kernels, output_call(): pl.pallas_call(functools.partial(output_kernel, owner, factor), in_specs=...  12.8 us
    ppermute x7, waiting for transfers between devices, sum_round(): terms.append(lax.ppermute(x, axis, [(n, n ^ d) for n in range(size)]))  12.7 us
    ppermute x7, waiting for transfers between devices, local(): arrived[later] = lax.ppermute(block, 'fsdp', turns[(later + 1) % 2])  12.6 us
    ppermute x3, starting transfers between devices, gather_and_exchange(): held.append(lax.ppermute(block, 'tp', across))  8.18 us
    ppermute x7, starting transfers between devices, sum_round(): terms.append(lax.ppermute(x, axis, [(n, n ^ d) for n in range(size)]))  7.5 us
  transfers between devices with their start and end apart: 46, of which 15 were waited for; matrix products, arithmetic and copies ran while one was open for 0% of the time, Pallas kernels for 18%

profile of v18, /device:TPU:1, one launch (start us, length us, event | category | flops | bytes accessed | tf_op | source)
XLA Modules:
  0.0 144.1 jit_solution(11158016367794103791)
XLA Ops:
  0.6 4.0 %convert_add_fusion.base_ref = f32[96,13824]{1,0:T(8,128)S(1)} fusion(f32[96,13824]{1,0:T(8,128)} %param.3, bf16[96,13824]{1,0:T(8,128)(2,1)} %param.4), kind=kLoop, calls=%fused_computation | loop fusion | flops 2654208 | bytes 13271040 | tf_op jit(solution)/shard_map/add | solution.py:402
  7.2 2.1 %collective-permute-start = (f32[96,256]{1,0:T(8,128)S(1)}, f32[96,256]{1,0:T(8,128)S(1)}, u32[]{:S(2)}, u32[]{:S(2)}) collective-permute-start(f32[96,256]{1,0:T(8,128)S(1)} %fusion), channel_id=1, source_target_pairs={{0,1},{1,0},{2,3},{3,2},{4,5},{5,4},{6,7},{7,6},{8,9},{9,8},{10,11... | collective-permute-start | bytes 294920 | tf_op jit(solution)/shard_map/ppermute | solution.py:354
  9.8 3.2 %collective-permute-start.4 = (bf16[96,896]{1,0:T(8,128)(2,1)S(1)}, bf16[96,896]{1,0:T(8,128)(2,1)S(1)}, u32[]{:S(2)}, u32[]{:S(2)}) collective-permute-start(bf16[96,896]{1,0:T(8,128)(2,1)S(1)} %get-tuple-element.70), channel_id=1, source_target_pairs={{0,18},{2,16},{4,22},{6,20},{8,26},{10,24},{12,30},{14,28},{16,2},... | collective-permute-start | bytes 516104 | tf_op jit(solution)/shard_map/ppermute | solution.py:350
  15.7 9.6 %collective-permute-done.4.refs_9_ = bf16[96,896]{1,0:T(8,128)(2,1)S(1)} collective-permute-done((bf16[96,896]{1,0:T(8,128)(2,1)S(1)}, bf16[96,896]{1,0:T(8,128)(2,1)S(1)}, u32[]{:S(2)}, u32[]{:S(2)}) %collective-permute-start.4) | collective-permute-done | bytes 172064 | tf_op jit(solution)/shard_map/ppermute | solution.py:350
  25.3 3.5 %collective-permute-done.3.refs_8_ = bf16[96,896]{1,0:T(8,128)(2,1)S(1)} collective-permute-done((bf16[96,896]{1,0:T(8,128)(2,1)S(1)}, bf16[96,896]{1,0:T(8,128)(2,1)S(1)}, u32[]{:S(2)}, u32[]{:S(2)}) %collective-permute-start.3) | collective-permute-done | bytes 172064 | tf_op jit(solution)/shard_map/ppermute | solution.py:350
  30.0 5.2 %collective-permute-start.2 = (f32[96,256]{1,0:T(8,128)S(1)}, f32[96,256]{1,0:T(8,128)S(1)}, u32[]{:S(2)}, u32[]{:S(2)}) collective-permute-start(f32[96,256]{1,0:T(8,128)S(1)} %collective-permute-done.1), channel_id=1, source_target_pairs={{0,1},{1,0},{2,3},{3,2},{4,5},{5,4},{6,7},{7,6},{8,9},{9,8},{10,11... | collective-permute-start | bytes 294920 | tf_op jit(solution)/shard_map/ppermute | solution.py:365
  35.3 2.0 %collective-permute-start.14 = (bf16[96,896]{1,0:T(8,128)(2,1)S(1)}, bf16[96,896]{1,0:T(8,128)(2,1)S(1)}, u32[]{:S(2)}, u32[]{:S(2)}) collective-permute-start(bf16[96,896]{1,0:T(8,128)(2,1)S(1)} %get-tuple-element.84), channel_id=1, source_target_pairs={{0,8},{2,10},{4,12},{6,14},{8,0},{10,2},{12,4},{14,6},{16,24},{18,... | collective-permute-start | bytes 516104 | tf_op jit(solution)/shard_map/ppermute | solution.py:350
  37.2 2.6 %collective-permute-start.13 = (bf16[96,896]{1,0:T(8,128)(2,1)S(1)}, bf16[96,896]{1,0:T(8,128)(2,1)S(1)}, u32[]{:S(2)}, u32[]{:S(2)}) collective-permute-start(bf16[96,896]{1,0:T(8,128)(2,1)S(1)} %get-tuple-element.82), channel_id=1, source_target_pairs={{0,6},{2,4},{4,2},{6,0},{8,14},{10,12},{12,10},{14,8},{16,22},{18,... | collective-permute-start | bytes 516104 | tf_op jit(solution)/shard_map/ppermute | solution.py:350
  46.1 4.1 %collective-permute-done.12.refs_11_ = bf16[96,896]{1,0:T(8,128)(2,1)S(1)} collective-permute-done((bf16[96,896]{1,0:T(8,128)(2,1)S(1)}, bf16[96,896]{1,0:T(8,128)(2,1)S(1)}, u32[]{:S(2)}, u32[]{:S(2)}) %collective-permute-start.12) | collective-permute-done | bytes 172064 | tf_op jit(solution)/shard_map/ppermute | solution.py:350
  50.3 2.1 %collective-permute-start.16 = (bf16[96,896]{1,0:T(8,128)(2,1)S(1)}, bf16[96,896]{1,0:T(8,128)(2,1)S(1)}, u32[]{:S(2)}, u32[]{:S(2)}) collective-permute-start(bf16[96,896]{1,0:T(8,128)(2,1)S(1)} %get-tuple-element.87), channel_id=1, source_target_pairs={{0,24},{2,26},{4,28},{6,30},{8,16},{10,18},{12,20},{14,22},{16,8},... | collective-permute-start | bytes 516104 | tf_op jit(solution)/shard_map/ppermute | solution.py:350
  54.0 2.7 %collective-permute-done.11 = f32[96,256]{1,0:T(8,128)S(1)} collective-permute-done((f32[96,256]{1,0:T(8,128)S(1)}, f32[96,256]{1,0:T(8,128)S(1)}, u32[]{:S(2)}, u32[]{:S(2)}) %collective-permute-start.11) | collective-permute-done | bytes 98336 | tf_op jit(solution)/shard_map/ppermute | solution.py:365
  56.7 3.7 %collective-permute-done.15 = f32[96,256]{1,0:T(8,128)S(1)} collective-permute-done((f32[96,256]{1,0:T(8,128)S(1)}, f32[96,256]{1,0:T(8,128)S(1)}, u32[]{:S(2)}, u32[]{:S(2)}) %collective-permute-start.15) | collective-permute-done | bytes 98336 | tf_op jit(solution)/shard_map/ppermute | solution.py:361
  60.5 3.2 %collective-permute-start.21 = (bf16[96,896]{1,0:T(8,128)(2,1)S(1)}, bf16[96,896]{1,0:T(8,128)(2,1)S(1)}, u32[]{:S(2)}, u32[]{:S(2)}) collective-permute-start(bf16[96,896]{1,0:T(8,128)(2,1)S(1)} %get-tuple-element.99), channel_id=1, source_target_pairs={{0,26},{2,24},{4,30},{6,28},{8,18},{10,16},{12,22},{14,20},{16,10}... | collective-permute-start | bytes 516104 | tf_op jit(solution)/shard_map/ppermute | solution.py:350
  65.6 2.6 %collective-permute-start.22 = (bf16[96,896]{1,0:T(8,128)(2,1)S(1)}, bf16[96,896]{1,0:T(8,128)(2,1)S(1)}, u32[]{:S(2)}, u32[]{:S(2)}) collective-permute-start(bf16[96,896]{1,0:T(8,128)(2,1)S(1)} %get-tuple-element.101), channel_id=1, source_target_pairs={{0,28},{2,30},{4,24},{6,26},{8,20},{10,22},{12,16},{14,18},{16,12}... | collective-permute-start | bytes 516104 | tf_op jit(solution)/shard_map/ppermute | solution.py:350
  68.2 14.2 %factor.1 = (bf16[256,1536]{1,0:T(8,128)(2,1)S(1)}, bf16[96,256]{1,0:T(8,128)(2,1)S(1)}) custom-call(f32[96,13824]{1,0:T(8,128)S(1)} %convert_add_fusion.base_ref, f32[8,96,256]{2,1,0:T(8,128)S(1)} %bitcast_dynamic-update-slice_fusion.refs_0_, f32[8,96,256]{2,1,0:T(8,128)S(1)} %collective-permute-done.19.refs_1_), custom_call_target="tpu_custom_call" | custom-call | flops 4026531840 | bytes 2359296 | tf_op jit(solution)/shard_map/factor/pallas_call | solution.py:166
  83.9 4.2 %collective-permute-start.31 = (bf16[896,256]{1,0:T(8,128)(2,1)S(1)}, bf16[896,256]{1,0:T(8,128)(2,1)S(1)}, u32[]{:S(2)}, u32[]{:S(2)}) collective-permute-start(bf16[896,256]{1,0:T(8,128)(2,1)S(1)} %get-tuple-element.105.refs_0_), channel_id=1, source_target_pairs={{8,0},{16,8},{24,16},{28,24},{20,28},{12,20},{4,12},{0,4},{2,10},{... | collective-permute-start | bytes 1376264 | tf_op jit(solution)/shard_map/ppermute | solution.py:437
  91.7 5.6 %collective-permute-done.24 = f32[1,256]{1,0:T(1,128)S(1)} collective-permute-done((f32[1,256]{1,0:T(1,128)S(1)}, f32[1,256]{1,0:T(1,128)S(1)}, u32[]{:S(2)}, u32[]{:S(2)}) %collective-permute-start.24) | collective-permute-done | bytes 1056 | tf_op jit(solution)/shard_map/ppermute | solution.py:386
  99.0 2.2 %collective-permute-start.27 = (f32[1,256]{1,0:T(1,128)S(1)}, f32[1,256]{1,0:T(1,128)S(1)}, u32[]{:S(2)}, u32[]{:S(2)}) collective-permute-start(f32[1,256]{1,0:T(1,128)S(1)} %add_add_fusion.1), channel_id=1, source_target_pairs={{0,2},{2,0},{4,6},{6,4},{8,10},{10,8},{12,14},{14,12},{16,18},{18,... | collective-permute-start | bytes 3080 | tf_op jit(solution)/shard_map/ppermute | solution.py:386
  103.7 2.0 %collective-permute-done.29 = f32[1,256]{1,0:T(1,128)S(1)} collective-permute-done((f32[1,256]{1,0:T(1,128)S(1)}, f32[1,256]{1,0:T(1,128)S(1)}, u32[]{:S(2)}, u32[]{:S(2)}) %collective-permute-start.29) | collective-permute-done | bytes 1056 | tf_op jit(solution)/shard_map/ppermute | solution.py:386
  107.5 2.7 %collective-permute-done.33 = f32[1,256]{1,0:T(1,128)S(1)} collective-permute-done((f32[1,256]{1,0:T(1,128)S(1)}, f32[1,256]{1,0:T(1,128)S(1)}, u32[]{:S(2)}, u32[]{:S(2)}) %collective-permute-start.33) | collective-permute-done | bytes 1056 | tf_op jit(solution)/shard_map/ppermute | solution.py:386
  110.3 2.8 %outputs.7 = (f32[96,13824]{1,0:T(8,128)}, bf16[13824,256]{1,0:T(8,128)(2,1)}, bf16[96,13824]{1,0:T(8,128)(2,1)}) custom-call(f32[96,13824]{1,0:T(8,128)S(1)} %convert_add_fusion.base_ref, bf16[96,256]{1,0:T(8,128)(2,1)S(1)} %get-tuple-element.93.ortho_ref, f32[1,256]{1,0:T(1,128)S(1)} %add.35.colsq_ref, bf16[896,256]{1,0:T(8,128)(2,1)S(1)} %get-tuple-element.105.refs_0_, ...), custom_call_target="tpu_custom_call" | custom-call | flops 352321536 | bytes 7110656 | tf_op jit(solution)/shard_map/outputs/pallas_call | solution.py:271
  117.5 8.0 %collective-permute-done.41.refs_0_ = bf16[896,256]{1,0:T(8,128)(2,1)S(1)} collective-permute-done((bf16[896,256]{1,0:T(8,128)(2,1)S(1)}, bf16[896,256]{1,0:T(8,128)(2,1)S(1)}, u32[]{:S(2)}, u32[]{:S(2)}) %collective-permute-start.41) | collective-permute-done | bytes 458784 | tf_op jit(solution)/shard_map/ppermute | solution.py:437
  125.5 2.0 %collective-permute-start.42 = (bf16[896,256]{1,0:T(8,128)(2,1)S(1)}, bf16[896,256]{1,0:T(8,128)(2,1)S(1)}, u32[]{:S(2)}, u32[]{:S(2)}) collective-permute-start(bf16[896,256]{1,0:T(8,128)(2,1)S(1)} %collective-permute-done.41.refs_0_), channel_id=1, source_target_pairs={{0,2},{2,0},{4,6},{6,4},{8,10},{10,8},{12,14},{14,12},{16,18},{18,... | collective-permute-start | bytes 1376264 | tf_op jit(solution)/shard_map/ppermute | solution.py:438
  132.5 4.6 %collective-permute-done.44.refs_0_ = bf16[896,256]{1,0:T(8,128)(2,1)S(1)} collective-permute-done((bf16[896,256]{1,0:T(8,128)(2,1)S(1)}, bf16[896,256]{1,0:T(8,128)(2,1)S(1)}, u32[]{:S(2)}, u32[]{:S(2)}) %collective-permute-start.44) | collective-permute-done | bytes 458784 | tf_op jit(solution)/shard_map/ppermute | solution.py:437
  (93 shorter events, 44.2 us)
Async XLA Ops:
  9.8 15.5 %collective-permute-start.4 = (bf16[96,896]{1,0:T(8,128)(2,1)S(1)}, bf16[96,896]{1,0:T(8,128)(2,1)S(1)}, u32[]{:S(2)}, u32[]{:S(2)}) collective-permute-start(bf16[96,896]{1,0:T(8,128)(2,1)S(1)} %get-tuple-element.70), channel_id=1, source_target_pairs={{0,18},{2,16},{4,22},{6,20},{8,26},{10,24},{12,30},{14,28},{16,2},... | collective-permute-start | bytes 516104 | tf_op jit(solution)/shard_map/ppermute | solution.py:350
  13.0 15.8 %collective-permute-start.3 = (bf16[96,896]{1,0:T(8,128)(2,1)S(1)}, bf16[96,896]{1,0:T(8,128)(2,1)S(1)}, u32[]{:S(2)}, u32[]{:S(2)}) collective-permute-start(bf16[96,896]{1,0:T(8,128)(2,1)S(1)} %get-tuple-element.68), channel_id=1, source_target_pairs={{0,16},{2,18},{4,20},{6,22},{8,24},{10,26},{12,28},{14,30},{16,0},... | collective-permute-start | bytes 516104 | tf_op jit(solution)/shard_map/ppermute | solution.py:350
  13.1 15.7 %collective-permute-start.1 = (f32[96,256]{1,0:T(8,128)S(1)}, f32[96,256]{1,0:T(8,128)S(1)}, u32[]{:S(2)}, u32[]{:S(2)}) collective-permute-start(f32[96,256]{1,0:T(8,128)S(1)} %get-tuple-element.132), channel_id=1, source_target_pairs={{0,8},{8,16},{16,24},{24,28},{28,20},{20,12},{12,4},{4,0},{10,2},{... | collective-permute-start | bytes 294920 | tf_op jit(solution)/shard_map/ppermute | solution.py:361
  14.4 20.9 %collective-permute-start.9 = (bf16[96,896]{1,0:T(8,128)(2,1)S(1)}, bf16[96,896]{1,0:T(8,128)(2,1)S(1)}, u32[]{:S(2)}, u32[]{:S(2)}) collective-permute-start(bf16[96,896]{1,0:T(8,128)(2,1)S(1)} %get-tuple-element.77), channel_id=1, source_target_pairs={{0,4},{2,6},{4,0},{6,2},{8,12},{10,14},{12,8},{14,10},{16,20},{18,... | collective-permute-start | bytes 516104 | tf_op jit(solution)/shard_map/ppermute | solution.py:350
  15.7 21.6 %collective-permute-start.8 = (bf16[96,896]{1,0:T(8,128)(2,1)S(1)}, bf16[96,896]{1,0:T(8,128)(2,1)S(1)}, u32[]{:S(2)}, u32[]{:S(2)}) collective-permute-start(bf16[96,896]{1,0:T(8,128)(2,1)S(1)} %get-tuple-element.75), channel_id=1, source_target_pairs={{0,2},{2,0},{4,6},{6,4},{8,10},{10,8},{12,14},{14,12},{16,18},{18,... | collective-permute-start | bytes 516104 | tf_op jit(solution)/shard_map/ppermute | solution.py:350
  25.3 14.5 %collective-permute-start.7 = (bf16[96,896]{1,0:T(8,128)(2,1)S(1)}, bf16[96,896]{1,0:T(8,128)(2,1)S(1)}, u32[]{:S(2)}, u32[]{:S(2)}) collective-permute-start(bf16[96,896]{1,0:T(8,128)(2,1)S(1)} %get-tuple-element.73), channel_id=1, source_target_pairs={{0,20},{2,22},{4,16},{6,18},{8,28},{10,30},{12,24},{14,26},{16,4},... | collective-permute-start | bytes 516104 | tf_op jit(solution)/shard_map/ppermute | solution.py:350
  28.8 11.1 %collective-permute-start.5 = (f32[96,256]{1,0:T(8,128)S(1)}, f32[96,256]{1,0:T(8,128)S(1)}, u32[]{:S(2)}, u32[]{:S(2)}) collective-permute-start(f32[96,256]{1,0:T(8,128)S(1)} %collective-permute-done.1), channel_id=1, source_target_pairs={{0,8},{8,16},{16,24},{24,28},{28,20},{20,12},{12,4},{4,0},{10,2},{... | collective-permute-start | bytes 294920 | tf_op jit(solution)/shard_map/ppermute | solution.py:361
  30.0 9.9 %collective-permute-start.2 = (f32[96,256]{1,0:T(8,128)S(1)}, f32[96,256]{1,0:T(8,128)S(1)}, u32[]{:S(2)}, u32[]{:S(2)}) collective-permute-start(f32[96,256]{1,0:T(8,128)S(1)} %collective-permute-done.1), channel_id=1, source_target_pairs={{0,1},{1,0},{2,3},{3,2},{4,5},{5,4},{6,7},{7,6},{8,9},{9,8},{10,11... | collective-permute-start | bytes 294920 | tf_op jit(solution)/shard_map/ppermute | solution.py:365
  39.9 10.4 %collective-permute-start.12 = (bf16[96,896]{1,0:T(8,128)(2,1)S(1)}, bf16[96,896]{1,0:T(8,128)(2,1)S(1)}, u32[]{:S(2)}, u32[]{:S(2)}) collective-permute-start(bf16[96,896]{1,0:T(8,128)(2,1)S(1)} %get-tuple-element.80), channel_id=1, source_target_pairs={{0,22},{2,20},{4,18},{6,16},{8,30},{10,28},{12,26},{14,24},{16,6},... | collective-permute-start | bytes 516104 | tf_op jit(solution)/shard_map/ppermute | solution.py:350
  39.9 12.5 %collective-permute-start.10 = (f32[96,256]{1,0:T(8,128)S(1)}, f32[96,256]{1,0:T(8,128)S(1)}, u32[]{:S(2)}, u32[]{:S(2)}) collective-permute-start(f32[96,256]{1,0:T(8,128)S(1)} %collective-permute-done.5), channel_id=1, source_target_pairs={{0,8},{8,16},{16,24},{24,28},{28,20},{20,12},{12,4},{4,0},{10,2},{... | collective-permute-start | bytes 294920 | tf_op jit(solution)/shard_map/ppermute | solution.py:361
  39.9 12.7 %collective-permute-start.6 = (f32[96,256]{1,0:T(8,128)S(1)}, f32[96,256]{1,0:T(8,128)S(1)}, u32[]{:S(2)}, u32[]{:S(2)}) collective-permute-start(f32[96,256]{1,0:T(8,128)S(1)} %collective-permute-done.5), channel_id=1, source_target_pairs={{0,1},{1,0},{2,3},{3,2},{4,5},{5,4},{6,7},{7,6},{8,9},{9,8},{10,11... | collective-permute-start | bytes 294920 | tf_op jit(solution)/shard_map/ppermute | solution.py:365
  41.6 18.8 %collective-permute-start.18 = (bf16[96,896]{1,0:T(8,128)(2,1)S(1)}, bf16[96,896]{1,0:T(8,128)(2,1)S(1)}, u32[]{:S(2)}, u32[]{:S(2)}) collective-permute-start(bf16[96,896]{1,0:T(8,128)(2,1)S(1)} %get-tuple-element.91), channel_id=1, source_target_pairs={{0,12},{2,14},{4,8},{6,10},{8,4},{10,6},{12,0},{14,2},{16,28},{18,... | collective-permute-start | bytes 516104 | tf_op jit(solution)/shard_map/ppermute | solution.py:350
  45.3 15.1 %collective-permute-start.17 = (bf16[96,896]{1,0:T(8,128)(2,1)S(1)}, bf16[96,896]{1,0:T(8,128)(2,1)S(1)}, u32[]{:S(2)}, u32[]{:S(2)}) collective-permute-start(bf16[96,896]{1,0:T(8,128)(2,1)S(1)} %get-tuple-element.89), channel_id=1, source_target_pairs={{0,10},{2,8},{4,14},{6,12},{8,2},{10,0},{12,6},{14,4},{16,26},{18,... | collective-permute-start | bytes 516104 | tf_op jit(solution)/shard_map/ppermute | solution.py:350
  50.3 10.2 %collective-permute-start.16 = (bf16[96,896]{1,0:T(8,128)(2,1)S(1)}, bf16[96,896]{1,0:T(8,128)(2,1)S(1)}, u32[]{:S(2)}, u32[]{:S(2)}) collective-permute-start(bf16[96,896]{1,0:T(8,128)(2,1)S(1)} %get-tuple-element.87), channel_id=1, source_target_pairs={{0,24},{2,26},{4,28},{6,30},{8,16},{10,18},{12,20},{14,22},{16,8},... | collective-permute-start | bytes 516104 | tf_op jit(solution)/shard_map/ppermute | solution.py:350
  60.5 21.9 %collective-permute-start.21 = (bf16[96,896]{1,0:T(8,128)(2,1)S(1)}, bf16[96,896]{1,0:T(8,128)(2,1)S(1)}, u32[]{:S(2)}, u32[]{:S(2)}) collective-permute-start(bf16[96,896]{1,0:T(8,128)(2,1)S(1)} %get-tuple-element.99), channel_id=1, source_target_pairs={{0,26},{2,24},{4,30},{6,28},{8,18},{10,16},{12,22},{14,20},{16,10}... | collective-permute-start | bytes 516104 | tf_op jit(solution)/shard_map/ppermute | solution.py:350
  63.7 18.8 %collective-permute-start.20 = (bf16[96,896]{1,0:T(8,128)(2,1)S(1)}, bf16[96,896]{1,0:T(8,128)(2,1)S(1)}, u32[]{:S(2)}, u32[]{:S(2)}) collective-permute-start(bf16[96,896]{1,0:T(8,128)(2,1)S(1)} %get-tuple-element.97), channel_id=1, source_target_pairs={{0,14},{2,12},{4,10},{6,8},{8,6},{10,4},{12,2},{14,0},{16,30},{18,... | collective-permute-start | bytes 516104 | tf_op jit(solution)/shard_map/ppermute | solution.py:350
  63.7 18.8 %collective-permute-start.23 = (bf16[96,896]{1,0:T(8,128)(2,1)S(1)}, bf16[96,896]{1,0:T(8,128)(2,1)S(1)}, u32[]{:S(2)}, u32[]{:S(2)}) collective-permute-start(bf16[96,896]{1,0:T(8,128)(2,1)S(1)} %get-tuple-element.103), channel_id=1, source_target_pairs={{0,30},{2,28},{4,26},{6,24},{8,22},{10,20},{12,18},{14,16},{16,14}... | collective-permute-start | bytes 516104 | tf_op jit(solution)/shard_map/ppermute | solution.py:350
  65.6 16.8 %collective-permute-start.22 = (bf16[96,896]{1,0:T(8,128)(2,1)S(1)}, bf16[96,896]{1,0:T(8,128)(2,1)S(1)}, u32[]{:S(2)}, u32[]{:S(2)}) collective-permute-start(bf16[96,896]{1,0:T(8,128)(2,1)S(1)} %get-tuple-element.101), channel_id=1, source_target_pairs={{0,28},{2,30},{4,24},{6,26},{8,20},{10,22},{12,16},{14,18},{16,12}... | collective-permute-start | bytes 516104 | tf_op jit(solution)/shard_map/ppermute | solution.py:350
  83.8 21.8 %collective-permute-start.30 = (bf16[896,256]{1,0:T(8,128)(2,1)S(1)}, bf16[896,256]{1,0:T(8,128)(2,1)S(1)}, u32[]{:S(2)}, u32[]{:S(2)}) collective-permute-start(bf16[896,256]{1,0:T(8,128)(2,1)S(1)} %get-tuple-element.105.refs_0_), channel_id=1, source_target_pairs={{0,8},{8,16},{16,24},{24,28},{28,20},{20,12},{12,4},{4,0},{10,2},{... | collective-permute-start | bytes 1376264 | tf_op jit(solution)/shard_map/ppermute | solution.py:437
  83.9 21.8 %collective-permute-start.31 = (bf16[896,256]{1,0:T(8,128)(2,1)S(1)}, bf16[896,256]{1,0:T(8,128)(2,1)S(1)}, u32[]{:S(2)}, u32[]{:S(2)}) collective-permute-start(bf16[896,256]{1,0:T(8,128)(2,1)S(1)} %get-tuple-element.105.refs_0_), channel_id=1, source_target_pairs={{8,0},{16,8},{24,16},{28,24},{20,28},{12,20},{4,12},{0,4},{2,10},{... | collective-permute-start | bytes 1376264 | tf_op jit(solution)/shard_map/ppermute | solution.py:437
  114.3 11.2 %collective-permute-start.41 = (bf16[896,256]{1,0:T(8,128)(2,1)S(1)}, bf16[896,256]{1,0:T(8,128)(2,1)S(1)}, u32[]{:S(2)}, u32[]{:S(2)}) collective-permute-start(bf16[896,256]{1,0:T(8,128)(2,1)S(1)} %collective-permute-done.31.refs_0_), channel_id=1, source_target_pairs={{8,0},{16,8},{24,16},{28,24},{20,28},{12,20},{4,12},{0,4},{2,10},{... | collective-permute-start | bytes 1376264 | tf_op jit(solution)/shard_map/ppermute | solution.py:437
  114.7 12.9 %collective-permute-start.36 = (bf16[896,256]{1,0:T(8,128)(2,1)S(1)}, bf16[896,256]{1,0:T(8,128)(2,1)S(1)}, u32[]{:S(2)}, u32[]{:S(2)}) collective-permute-start(bf16[896,256]{1,0:T(8,128)(2,1)S(1)} %collective-permute-done.34.refs_0_), channel_id=1, source_target_pairs={{0,2},{2,0},{4,6},{6,4},{8,10},{10,8},{12,14},{14,12},{16,18},{18,... | collective-permute-start | bytes 1376264 | tf_op jit(solution)/shard_map/ppermute | solution.py:438
  115.1 14.1 %collective-permute-start.35 = (bf16[896,256]{1,0:T(8,128)(2,1)S(1)}, bf16[896,256]{1,0:T(8,128)(2,1)S(1)}, u32[]{:S(2)}, u32[]{:S(2)}) collective-permute-start(bf16[896,256]{1,0:T(8,128)(2,1)S(1)} %collective-permute-done.34.refs_0_), channel_id=1, source_target_pairs={{0,8},{8,16},{16,24},{24,28},{28,20},{20,12},{12,4},{4,0},{10,2},{... | collective-permute-start | bytes 1376264 | tf_op jit(solution)/shard_map/ppermute | solution.py:437
  129.9 10.8 %collective-permute-start.39 = (bf16[896,256]{1,0:T(8,128)(2,1)S(1)}, bf16[896,256]{1,0:T(8,128)(2,1)S(1)}, u32[]{:S(2)}, u32[]{:S(2)}) collective-permute-start(bf16[896,256]{1,0:T(8,128)(2,1)S(1)} %collective-permute-done.35.refs_0_), channel_id=1, source_target_pairs={{0,8},{8,16},{16,24},{24,28},{28,20},{20,12},{12,4},{4,0},{10,2},{... | collective-permute-start | bytes 1376264 | tf_op jit(solution)/shard_map/ppermute | solution.py:437
  (23 other events, 131.2 us)

commit v19 on v17

--- a/solution.py
+++ b/solution.py
@@ -333,9 +333,10 @@
 def exchange_windows(count):
     chips, steps = count // 2, count // 4
     far, near = list(range(chips, count)), list(range(1, chips))
-    each = -(-len(near) // steps)
-    windows = [far[w + 1 : w + 2] + near[(w - 1) * each : w * each] for w in range(1, steps + 1)]
-    return [far[:2]] + windows + [far[steps + 2 :]]
+    windows = [far[:2] + near[:1]]
+    windows += [far[w + 1 : w + 2] + near[w : w + 1] for w in range(1, steps)]
+    windows += [far[steps + 1 : steps + 2] + near[steps : steps + 2]]
+    return windows + [far[steps + 2 :] + near[steps + 2 :]]
 
 
 def gather_and_exchange(sketch, outgoing, count):

time: 137 us -> 140 us (1.022)
  waiting for transfers between devices: 41.1 us -> 42.8 us
    ppermute x15, starting transfers between devices: 21.5 us -> 28.1 us  [exchange(): columns[k] = lax.ppermute(tie(outgoing[k], *after), 'fsdp', pairs)]
    ppermute x3, starting transfers between devices: 8.18 us -> 3.27 us  [gather_and_exchange(): held.append(lax.ppermute(block, 'tp', across))]
    ppermute x7, starting transfers between devices: 9.27 us -> 5.81 us  [local(): arrived[later] = lax.ppermute(block, 'fsdp', turns[(later + 1) % 2])]
    ppermute x4, waiting for transfers between devices: 3.68 us -> 1.74 us  [gather_and_exchange(): block = lax.ppermute(block, ('fsdp', 'tp'), turns)]
    ppermute x15, waiting for transfers between devices: 19.1 us -> 20.8 us  [exchange(): columns[k] = lax.ppermute(tie(outgoing[k], *after), 'fsdp', pairs)]
    ppermute x4, starting transfers between devices: 2.88 us -> 4.29 us  [gather_and_exchange(): block = lax.ppermute(block, ('fsdp', 'tp'), turns)]
  transfers between devices with their start and end apart: 46 -> 46, of which waited for: 14 -> 15; matrix products, arithmetic and copies ran while one was open for 0% -> 0% of each run, Pallas kernels for 19% -> 19%
where the time goes in v19:
time: 140 us; the launch traced here: 139 us
  starting transfers between devices  59.9 us (43%)
  waiting for transfers between devices  42.8 us (31%)
  Pallas kernels  28.7 us (20%)
  other arithmetic  3.98 us (3%)
  local copies, waits for them, and re-layouts  1.43 us (1%)
    ppermute x15, starting transfers between devices, exchange(): columns[k] = lax.ppermute(tie(outgoing[k], *after), 'fsdp', pairs)  28.1 us
    ppermute x15, waiting for transfers between devices, exchange(): columns[k] = lax.ppermute(tie(outgoing[k], *after), 'fsdp', pairs)  20.8 us
    pallas_call x1, Pallas kernels, factor_call(): pl.pallas_call(functools.partial(factor_kernel, len(stacked), owner), in_...  14.2 us
    pallas_call x7, Pallas kernels, output_call(): pl.pallas_call(functools.partial(output_kernel, owner, factor), in_specs=...  12.7 us
    ppermute x7, waiting for transfers between devices, local(): arrived[later] = lax.ppermute(block, 'fsdp', turns[(later + 1) % 2])  9.15 us
    ppermute x8, starting transfers between devices, local(): blocks += [block, lax.ppermute(block, 'fsdp', swap)]  8.17 us
    ppermute x7, starting transfers between devices, sum_round(): terms.append(lax.ppermute(x, axis, [(n, n ^ d) for n in range(size)]))  8.06 us
    ppermute x7, waiting for transfers between devices, sum_round(): terms.append(lax.ppermute(x, axis, [(n, n ^ d) for n in range(size)]))  6.79 us
  transfers between devices with their start and end apart: 46, of which 15 were waited for; matrix products, arithmetic and copies ran while one was open for 0% of the time, Pallas kernels for 19%

profile of v19, /device:TPU:1, one launch (start us, length us, event | category | flops | bytes accessed | tf_op | source)
XLA Modules:
  0.0 139.2 jit_solution(6542086762701840500)
XLA Ops:
  0.6 4.0 %convert_add_fusion.base_ref = f32[96,13824]{1,0:T(8,128)S(1)} fusion(f32[96,13824]{1,0:T(8,128)} %param.3, bf16[96,13824]{1,0:T(8,128)(2,1)} %param.4), kind=kLoop, calls=%fused_computation | loop fusion | flops 2654208 | bytes 13271040 | tf_op jit(solution)/shard_map/add | solution.py:403
  7.2 2.1 %collective-permute-start = (f32[96,256]{1,0:T(8,128)S(1)}, f32[96,256]{1,0:T(8,128)S(1)}, u32[]{:S(2)}, u32[]{:S(2)}) collective-permute-start(f32[96,256]{1,0:T(8,128)S(1)} %fusion), channel_id=1, source_target_pairs={{0,1},{1,0},{2,3},{3,2},{4,5},{5,4},{6,7},{7,6},{8,9},{9,8},{10,11... | collective-permute-start | bytes 294920 | tf_op jit(solution)/shard_map/ppermute | solution.py:355
  10.8 2.3 %collective-permute-start.4 = (bf16[96,896]{1,0:T(8,128)(2,1)S(1)}, bf16[96,896]{1,0:T(8,128)(2,1)S(1)}, u32[]{:S(2)}, u32[]{:S(2)}) collective-permute-start(bf16[96,896]{1,0:T(8,128)(2,1)S(1)} %get-tuple-element.69), channel_id=1, source_target_pairs={{0,18},{2,16},{4,22},{6,20},{8,26},{10,24},{12,30},{14,28},{16,2},... | collective-permute-start | bytes 516104 | tf_op jit(solution)/shard_map/ppermute | solution.py:351
  15.8 2.0 %collective-permute-start.8 = (bf16[96,896]{1,0:T(8,128)(2,1)S(1)}, bf16[96,896]{1,0:T(8,128)(2,1)S(1)}, u32[]{:S(2)}, u32[]{:S(2)}) collective-permute-start(bf16[96,896]{1,0:T(8,128)(2,1)S(1)} %get-tuple-element.74), channel_id=1, source_target_pairs={{0,20},{2,22},{4,16},{6,18},{8,28},{10,30},{12,24},{14,26},{16,4},... | collective-permute-start | bytes 516104 | tf_op jit(solution)/shard_map/ppermute | solution.py:351
  17.8 11.6 %collective-permute-done.4.refs_9_ = bf16[96,896]{1,0:T(8,128)(2,1)S(1)} collective-permute-done((bf16[96,896]{1,0:T(8,128)(2,1)S(1)}, bf16[96,896]{1,0:T(8,128)(2,1)S(1)}, u32[]{:S(2)}, u32[]{:S(2)}) %collective-permute-start.4) | collective-permute-done | bytes 172064 | tf_op jit(solution)/shard_map/ppermute | solution.py:351
  29.4 2.8 %collective-permute-done.3.refs_8_ = bf16[96,896]{1,0:T(8,128)(2,1)S(1)} collective-permute-done((bf16[96,896]{1,0:T(8,128)(2,1)S(1)}, bf16[96,896]{1,0:T(8,128)(2,1)S(1)}, u32[]{:S(2)}, u32[]{:S(2)}) %collective-permute-start.3) | collective-permute-done | bytes 172064 | tf_op jit(solution)/shard_map/ppermute | solution.py:351
  33.5 1.9 %collective-permute-start.13 = (bf16[96,896]{1,0:T(8,128)(2,1)S(1)}, bf16[96,896]{1,0:T(8,128)(2,1)S(1)}, u32[]{:S(2)}, u32[]{:S(2)}) collective-permute-start(bf16[96,896]{1,0:T(8,128)(2,1)S(1)} %get-tuple-element.81), channel_id=1, source_target_pairs={{0,6},{2,4},{4,2},{6,0},{8,14},{10,12},{12,10},{14,8},{16,22},{18,... | collective-permute-start | bytes 516104 | tf_op jit(solution)/shard_map/ppermute | solution.py:351
  35.4 2.0 %collective-permute-start.2 = (f32[96,256]{1,0:T(8,128)S(1)}, f32[96,256]{1,0:T(8,128)S(1)}, u32[]{:S(2)}, u32[]{:S(2)}) collective-permute-start(f32[96,256]{1,0:T(8,128)S(1)} %collective-permute-done.1), channel_id=1, source_target_pairs={{0,1},{1,0},{2,3},{3,2},{4,5},{5,4},{6,7},{7,6},{8,9},{9,8},{10,11... | collective-permute-start | bytes 294920 | tf_op jit(solution)/shard_map/ppermute | solution.py:366
  41.9 3.1 %collective-permute-done.13.refs_3_ = bf16[96,896]{1,0:T(8,128)(2,1)S(1)} collective-permute-done((bf16[96,896]{1,0:T(8,128)(2,1)S(1)}, bf16[96,896]{1,0:T(8,128)(2,1)S(1)}, u32[]{:S(2)}, u32[]{:S(2)}) %collective-permute-start.13) | collective-permute-done | bytes 172064 | tf_op jit(solution)/shard_map/ppermute | solution.py:351
  45.0 1.9 %collective-permute-start.15 = (bf16[96,896]{1,0:T(8,128)(2,1)S(1)}, bf16[96,896]{1,0:T(8,128)(2,1)S(1)}, u32[]{:S(2)}, u32[]{:S(2)}) collective-permute-start(bf16[96,896]{1,0:T(8,128)(2,1)S(1)} %get-tuple-element.84), channel_id=1, source_target_pairs={{0,24},{2,26},{4,28},{6,30},{8,16},{10,18},{12,20},{14,22},{16,8},... | collective-permute-start | bytes 516104 | tf_op jit(solution)/shard_map/ppermute | solution.py:351
  49.7 4.1 %collective-permute-done.11 = f32[96,256]{1,0:T(8,128)S(1)} collective-permute-done((f32[96,256]{1,0:T(8,128)S(1)}, f32[96,256]{1,0:T(8,128)S(1)}, u32[]{:S(2)}, u32[]{:S(2)}) %collective-permute-start.11) | collective-permute-done | bytes 98336 | tf_op jit(solution)/shard_map/ppermute | solution.py:366
  55.7 4.0 %collective-permute-start.21 = (bf16[96,896]{1,0:T(8,128)(2,1)S(1)}, bf16[96,896]{1,0:T(8,128)(2,1)S(1)}, u32[]{:S(2)}, u32[]{:S(2)}) collective-permute-start(bf16[96,896]{1,0:T(8,128)(2,1)S(1)} %get-tuple-element.98), channel_id=1, source_target_pairs={{0,26},{2,24},{4,30},{6,28},{8,18},{10,16},{12,22},{14,20},{16,10}... | collective-permute-start | bytes 516104 | tf_op jit(solution)/shard_map/ppermute | solution.py:351
  61.2 1.8 %collective-permute-start.23 = (bf16[96,896]{1,0:T(8,128)(2,1)S(1)}, bf16[96,896]{1,0:T(8,128)(2,1)S(1)}, u32[]{:S(2)}, u32[]{:S(2)}) collective-permute-start(bf16[96,896]{1,0:T(8,128)(2,1)S(1)} %get-tuple-element.102), channel_id=1, source_target_pairs={{0,30},{2,28},{4,26},{6,24},{8,22},{10,20},{12,18},{14,16},{16,14}... | collective-permute-start | bytes 516104 | tf_op jit(solution)/shard_map/ppermute | solution.py:351
  64.6 1.8 %collective-permute-start.22 = (bf16[96,896]{1,0:T(8,128)(2,1)S(1)}, bf16[96,896]{1,0:T(8,128)(2,1)S(1)}, u32[]{:S(2)}, u32[]{:S(2)}) collective-permute-start(bf16[96,896]{1,0:T(8,128)(2,1)S(1)} %get-tuple-element.100), channel_id=1, source_target_pairs={{0,28},{2,30},{4,24},{6,26},{8,20},{10,22},{12,16},{14,18},{16,12}... | collective-permute-start | bytes 516104 | tf_op jit(solution)/shard_map/ppermute | solution.py:351
  66.4 5.9 %collective-permute-start.20 = (bf16[96,896]{1,0:T(8,128)(2,1)S(1)}, bf16[96,896]{1,0:T(8,128)(2,1)S(1)}, u32[]{:S(2)}, u32[]{:S(2)}) collective-permute-start(bf16[96,896]{1,0:T(8,128)(2,1)S(1)} %get-tuple-element.96), channel_id=1, source_target_pairs={{0,14},{2,12},{4,10},{6,8},{8,6},{10,4},{12,2},{14,0},{16,30},{18,... | collective-permute-start | bytes 516104 | tf_op jit(solution)/shard_map/ppermute | solution.py:351
  72.3 14.2 %factor.1 = (bf16[256,1536]{1,0:T(8,128)(2,1)S(1)}, bf16[96,256]{1,0:T(8,128)(2,1)S(1)}) custom-call(f32[96,13824]{1,0:T(8,128)S(1)} %convert_add_fusion.base_ref, f32[8,96,256]{2,1,0:T(8,128)S(1)} %bitcast_dynamic-update-slice_fusion.refs_0_, f32[8,96,256]{2,1,0:T(8,128)S(1)} %collective-permute-done.17.refs_1_), custom_call_target="tpu_custom_call" | custom-call | flops 4026531840 | bytes 2359296 | tf_op jit(solution)/shard_map/factor/pallas_call | solution.py:166
  89.4 1.7 %collective-permute-start.24 = (f32[1,256]{1,0:T(1,128)S(1)}, f32[1,256]{1,0:T(1,128)S(1)}, u32[]{:S(2)}, u32[]{:S(2)}) collective-permute-start(f32[1,256]{1,0:T(1,128)S(1)} %get-tuple-element.103), channel_id=1, source_target_pairs={{0,1},{1,0},{2,3},{3,2},{4,5},{5,4},{6,7},{7,6},{8,9},{9,8},{10,11... | collective-permute-start | bytes 3080 | tf_op jit(solution)/shard_map/ppermute | solution.py:387
  95.1 5.5 %collective-permute-done.26 = f32[1,256]{1,0:T(1,128)S(1)} collective-permute-done((f32[1,256]{1,0:T(1,128)S(1)}, f32[1,256]{1,0:T(1,128)S(1)}, u32[]{:S(2)}, u32[]{:S(2)}) %collective-permute-start.26) | collective-permute-done | bytes 1056 | tf_op jit(solution)/shard_map/ppermute | solution.py:387
  101.1 3.2 %collective-permute-start.30 = (f32[1,256]{1,0:T(1,128)S(1)}, f32[1,256]{1,0:T(1,128)S(1)}, u32[]{:S(2)}, u32[]{:S(2)}) collective-permute-start(f32[1,256]{1,0:T(1,128)S(1)} %add_add_fusion.1), channel_id=1, source_target_pairs={{0,24},{2,26},{4,28},{6,30},{8,16},{10,18},{12,20},{14,22},{16,8},... | collective-permute-start | bytes 3080 | tf_op jit(solution)/shard_map/ppermute | solution.py:387
  105.8 1.9 %collective-permute-start.37 = (bf16[896,256]{1,0:T(8,128)(2,1)S(1)}, bf16[896,256]{1,0:T(8,128)(2,1)S(1)}, u32[]{:S(2)}, u32[]{:S(2)}) collective-permute-start(bf16[896,256]{1,0:T(8,128)(2,1)S(1)} %collective-permute-done.31.refs_2_), channel_id=1, source_target_pairs={{0,2},{2,0},{4,6},{6,4},{8,10},{10,8},{12,14},{14,12},{16,18},{18,... | collective-permute-start | bytes 1376264 | tf_op jit(solution)/shard_map/ppermute | solution.py:439
  109.1 2.8 %outputs.7 = (f32[96,13824]{1,0:T(8,128)}, bf16[13824,256]{1,0:T(8,128)(2,1)}, bf16[96,13824]{1,0:T(8,128)(2,1)}) custom-call(f32[96,13824]{1,0:T(8,128)S(1)} %convert_add_fusion.base_ref, bf16[96,256]{1,0:T(8,128)(2,1)S(1)} %get-tuple-element.88.ortho_ref, f32[1,256]{1,0:T(1,128)S(1)} %add_add_fusion.colsq_ref, ...), custom_call_target="tpu_custom_call" | custom-call | flops 352321536 | bytes 7110656 | tf_op jit(solution)/shard_map/outputs/pallas_call | solution.py:271
  112.3 2.9 %collective-permute-done.33.refs_0_ = bf16[896,256]{1,0:T(8,128)(2,1)S(1)} collective-permute-done((bf16[896,256]{1,0:T(8,128)(2,1)S(1)}, bf16[896,256]{1,0:T(8,128)(2,1)S(1)}, u32[]{:S(2)}, u32[]{:S(2)}) %collective-permute-start.33) | collective-permute-done | bytes 458784 | tf_op jit(solution)/shard_map/ppermute | solution.py:438
  132.9 2.3 %collective-permute-done.39.refs_2_ = bf16[896,256]{1,0:T(8,128)(2,1)S(1)} collective-permute-done((bf16[896,256]{1,0:T(8,128)(2,1)S(1)}, bf16[896,256]{1,0:T(8,128)(2,1)S(1)}, u32[]{:S(2)}, u32[]{:S(2)}) %collective-permute-start.39) | collective-permute-done | bytes 458784 | tf_op jit(solution)/shard_map/ppermute | solution.py:438
  135.8 1.9 %outputs.12 = (f32[96,13824]{1,0:T(8,128)}, bf16[13824,256]{1,0:T(8,128)(2,1)}, bf16[96,13824]{1,0:T(8,128)(2,1)}) custom-call(f32[96,13824]{1,0:T(8,128)S(1)} %convert_add_fusion.base_ref, bf16[96,256]{1,0:T(8,128)(2,1)S(1)} %get-tuple-element.88.ortho_ref, ...), custom_call_target="tpu_custom_call", output_to_operand_aliasing={{0}: (6, {}), {1}: (7, {}), {2}: (8, {})} | custom-call | flops 264241152 | bytes 5332992 | tf_op jit(solution)/shard_map/outputs/pallas_call | solution.py:271
  (93 shorter events, 50.4 us)
Async XLA Ops:
  10.8 18.6 %collective-permute-start.4 = (bf16[96,896]{1,0:T(8,128)(2,1)S(1)}, bf16[96,896]{1,0:T(8,128)(2,1)S(1)}, u32[]{:S(2)}, u32[]{:S(2)}) collective-permute-start(bf16[96,896]{1,0:T(8,128)(2,1)S(1)} %get-tuple-element.69), channel_id=1, source_target_pairs={{0,18},{2,16},{4,22},{6,20},{8,26},{10,24},{12,30},{14,28},{16,2},... | collective-permute-start | bytes 516104 | tf_op jit(solution)/shard_map/ppermute | solution.py:351
  13.1 19.2 %collective-permute-start.3 = (bf16[96,896]{1,0:T(8,128)(2,1)S(1)}, bf16[96,896]{1,0:T(8,128)(2,1)S(1)}, u32[]{:S(2)}, u32[]{:S(2)}) collective-permute-start(bf16[96,896]{1,0:T(8,128)(2,1)S(1)} %get-tuple-element.67), channel_id=1, source_target_pairs={{0,16},{2,18},{4,20},{6,22},{8,24},{10,26},{12,28},{14,30},{16,0},... | collective-permute-start | bytes 516104 | tf_op jit(solution)/shard_map/ppermute | solution.py:351
  13.2 19.1 %collective-permute-start.1 = (f32[96,256]{1,0:T(8,128)S(1)}, f32[96,256]{1,0:T(8,128)S(1)}, u32[]{:S(2)}, u32[]{:S(2)}) collective-permute-start(f32[96,256]{1,0:T(8,128)S(1)} %get-tuple-element.130), channel_id=1, source_target_pairs={{0,8},{8,16},{16,24},{24,28},{28,20},{20,12},{12,4},{4,0},{10,2},{... | collective-permute-start | bytes 294920 | tf_op jit(solution)/shard_map/ppermute | solution.py:362
  14.5 23.0 %collective-permute-start.9 = (bf16[96,896]{1,0:T(8,128)(2,1)S(1)}, bf16[96,896]{1,0:T(8,128)(2,1)S(1)}, u32[]{:S(2)}, u32[]{:S(2)}) collective-permute-start(bf16[96,896]{1,0:T(8,128)(2,1)S(1)} %get-tuple-element.76), channel_id=1, source_target_pairs={{0,4},{2,6},{4,0},{6,2},{8,12},{10,14},{12,8},{14,10},{16,20},{18,... | collective-permute-start | bytes 516104 | tf_op jit(solution)/shard_map/ppermute | solution.py:351
  15.8 23.4 %collective-permute-start.8 = (bf16[96,896]{1,0:T(8,128)(2,1)S(1)}, bf16[96,896]{1,0:T(8,128)(2,1)S(1)}, u32[]{:S(2)}, u32[]{:S(2)}) collective-permute-start(bf16[96,896]{1,0:T(8,128)(2,1)S(1)} %get-tuple-element.74), channel_id=1, source_target_pairs={{0,20},{2,22},{4,16},{6,18},{8,28},{10,30},{12,24},{14,26},{16,4},... | collective-permute-start | bytes 516104 | tf_op jit(solution)/shard_map/ppermute | solution.py:351
  33.5 11.5 %collective-permute-start.13 = (bf16[96,896]{1,0:T(8,128)(2,1)S(1)}, bf16[96,896]{1,0:T(8,128)(2,1)S(1)}, u32[]{:S(2)}, u32[]{:S(2)}) collective-permute-start(bf16[96,896]{1,0:T(8,128)(2,1)S(1)} %get-tuple-element.81), channel_id=1, source_target_pairs={{0,6},{2,4},{4,2},{6,0},{8,14},{10,12},{12,10},{14,8},{16,22},{18,... | collective-permute-start | bytes 516104 | tf_op jit(solution)/shard_map/ppermute | solution.py:351
  37.4 11.1 %collective-permute-start.12 = (bf16[96,896]{1,0:T(8,128)(2,1)S(1)}, bf16[96,896]{1,0:T(8,128)(2,1)S(1)}, u32[]{:S(2)}, u32[]{:S(2)}) collective-permute-start(bf16[96,896]{1,0:T(8,128)(2,1)S(1)} %get-tuple-element.79), channel_id=1, source_target_pairs={{0,22},{2,20},{4,18},{6,16},{8,30},{10,28},{12,26},{14,24},{16,6},... | collective-permute-start | bytes 516104 | tf_op jit(solution)/shard_map/ppermute | solution.py:351
  39.2 9.4 %collective-permute-start.10 = (f32[96,256]{1,0:T(8,128)S(1)}, f32[96,256]{1,0:T(8,128)S(1)}, u32[]{:S(2)}, u32[]{:S(2)}) collective-permute-start(f32[96,256]{1,0:T(8,128)S(1)} %collective-permute-done.6), channel_id=1, source_target_pairs={{0,8},{8,16},{16,24},{24,28},{28,20},{20,12},{12,4},{4,0},{10,2},{... | collective-permute-start | bytes 294920 | tf_op jit(solution)/shard_map/ppermute | solution.py:362
  39.8 15.8 %collective-permute-start.16 = (bf16[96,896]{1,0:T(8,128)(2,1)S(1)}, bf16[96,896]{1,0:T(8,128)(2,1)S(1)}, u32[]{:S(2)}, u32[]{:S(2)}) collective-permute-start(bf16[96,896]{1,0:T(8,128)(2,1)S(1)} %get-tuple-element.86), channel_id=1, source_target_pairs={{0,8},{2,10},{4,12},{6,14},{8,0},{10,2},{12,4},{14,6},{16,24},{18,... | collective-permute-start | bytes 516104 | tf_op jit(solution)/shard_map/ppermute | solution.py:351
  40.6 9.1 %collective-permute-start.7 = (f32[96,256]{1,0:T(8,128)S(1)}, f32[96,256]{1,0:T(8,128)S(1)}, u32[]{:S(2)}, u32[]{:S(2)}) collective-permute-start(f32[96,256]{1,0:T(8,128)S(1)} %collective-permute-done.6), channel_id=1, source_target_pairs={{0,1},{1,0},{2,3},{3,2},{4,5},{5,4},{6,7},{7,6},{8,9},{9,8},{10,11... | collective-permute-start | bytes 294920 | tf_op jit(solution)/shard_map/ppermute | solution.py:366
  45.0 10.6 %collective-permute-start.15 = (bf16[96,896]{1,0:T(8,128)(2,1)S(1)}, bf16[96,896]{1,0:T(8,128)(2,1)S(1)}, u32[]{:S(2)}, u32[]{:S(2)}) collective-permute-start(bf16[96,896]{1,0:T(8,128)(2,1)S(1)} %get-tuple-element.84), channel_id=1, source_target_pairs={{0,24},{2,26},{4,28},{6,30},{8,16},{10,18},{12,20},{14,22},{16,8},... | collective-permute-start | bytes 516104 | tf_op jit(solution)/shard_map/ppermute | solution.py:351
  55.6 10.8 %collective-permute-start.17 = (f32[8,96,256]{2,1,0:T(8,128)S(1)}, f32[8,96,256]{2,1,0:T(8,128)S(1)}, u32[]{:S(2)}, u32[]{:S(2)}) collective-permute-start(f32[8,96,256]{2,1,0:T(8,128)S(1)} %bitcast_dynamic-update-slice_fusion.refs_0_), channel_id=1, source_target_pairs={{0,2},{2,0},{4,6},{6,4},{8,10},{10,8},{12,14},{14,12},{16,18},{18,... | collective-permute-start | bytes 2359304 | tf_op jit(solution)/shard_map/ppermute | solution.py:370
  55.7 8.9 %collective-permute-start.21 = (bf16[96,896]{1,0:T(8,128)(2,1)S(1)}, bf16[96,896]{1,0:T(8,128)(2,1)S(1)}, u32[]{:S(2)}, u32[]{:S(2)}) collective-permute-start(bf16[96,896]{1,0:T(8,128)(2,1)S(1)} %get-tuple-element.98), channel_id=1, source_target_pairs={{0,26},{2,24},{4,30},{6,28},{8,18},{10,16},{12,22},{14,20},{16,10}... | collective-permute-start | bytes 516104 | tf_op jit(solution)/shard_map/ppermute | solution.py:351
  59.6 26.9 %collective-permute-start.19 = (bf16[96,896]{1,0:T(8,128)(2,1)S(1)}, bf16[96,896]{1,0:T(8,128)(2,1)S(1)}, u32[]{:S(2)}, u32[]{:S(2)}) collective-permute-start(bf16[96,896]{1,0:T(8,128)(2,1)S(1)} %get-tuple-element.94), channel_id=1, source_target_pairs={{0,12},{2,14},{4,8},{6,10},{8,4},{10,6},{12,0},{14,2},{16,28},{18,... | collective-permute-start | bytes 516104 | tf_op jit(solution)/shard_map/ppermute | solution.py:351
  60.1 26.5 %collective-permute-start.18 = (bf16[96,896]{1,0:T(8,128)(2,1)S(1)}, bf16[96,896]{1,0:T(8,128)(2,1)S(1)}, u32[]{:S(2)}, u32[]{:S(2)}) collective-permute-start(bf16[96,896]{1,0:T(8,128)(2,1)S(1)} %get-tuple-element.92), channel_id=1, source_target_pairs={{0,10},{2,8},{4,14},{6,12},{8,2},{10,0},{12,6},{14,4},{16,26},{18,... | collective-permute-start | bytes 516104 | tf_op jit(solution)/shard_map/ppermute | solution.py:351
  61.2 25.3 %collective-permute-start.23 = (bf16[96,896]{1,0:T(8,128)(2,1)S(1)}, bf16[96,896]{1,0:T(8,128)(2,1)S(1)}, u32[]{:S(2)}, u32[]{:S(2)}) collective-permute-start(bf16[96,896]{1,0:T(8,128)(2,1)S(1)} %get-tuple-element.102), channel_id=1, source_target_pairs={{0,30},{2,28},{4,26},{6,24},{8,22},{10,20},{12,18},{14,16},{16,14}... | collective-permute-start | bytes 516104 | tf_op jit(solution)/shard_map/ppermute | solution.py:351
  64.6 21.9 %collective-permute-start.22 = (bf16[96,896]{1,0:T(8,128)(2,1)S(1)}, bf16[96,896]{1,0:T(8,128)(2,1)S(1)}, u32[]{:S(2)}, u32[]{:S(2)}) collective-permute-start(bf16[96,896]{1,0:T(8,128)(2,1)S(1)} %get-tuple-element.100), channel_id=1, source_target_pairs={{0,28},{2,30},{4,24},{6,26},{8,20},{10,22},{12,16},{14,18},{16,12}... | collective-permute-start | bytes 516104 | tf_op jit(solution)/shard_map/ppermute | solution.py:351
  66.4 20.2 %collective-permute-start.20 = (bf16[96,896]{1,0:T(8,128)(2,1)S(1)}, bf16[96,896]{1,0:T(8,128)(2,1)S(1)}, u32[]{:S(2)}, u32[]{:S(2)}) collective-permute-start(bf16[96,896]{1,0:T(8,128)(2,1)S(1)} %get-tuple-element.96), channel_id=1, source_target_pairs={{0,14},{2,12},{4,10},{6,8},{8,6},{10,4},{12,2},{14,0},{16,30},{18,... | collective-permute-start | bytes 516104 | tf_op jit(solution)/shard_map/ppermute | solution.py:351
  87.9 17.8 %collective-permute-start.31 = (bf16[896,256]{1,0:T(8,128)(2,1)S(1)}, bf16[896,256]{1,0:T(8,128)(2,1)S(1)}, u32[]{:S(2)}, u32[]{:S(2)}) collective-permute-start(bf16[896,256]{1,0:T(8,128)(2,1)S(1)} %get-tuple-element.104.refs_0_), channel_id=1, source_target_pairs={{0,8},{8,16},{16,24},{24,28},{28,20},{20,12},{12,4},{4,0},{10,2},{... | collective-permute-start | bytes 1376264 | tf_op jit(solution)/shard_map/ppermute | solution.py:438
  88.0 17.8 %collective-permute-start.32 = (bf16[896,256]{1,0:T(8,128)(2,1)S(1)}, bf16[896,256]{1,0:T(8,128)(2,1)S(1)}, u32[]{:S(2)}, u32[]{:S(2)}) collective-permute-start(bf16[896,256]{1,0:T(8,128)(2,1)S(1)} %get-tuple-element.104.refs_0_), channel_id=1, source_target_pairs={{8,0},{16,8},{24,16},{28,24},{20,28},{12,20},{4,12},{0,4},{2,10},{... | collective-permute-start | bytes 1376264 | tf_op jit(solution)/shard_map/ppermute | solution.py:438
  112.3 9.0 %collective-permute-start.41 = (bf16[896,256]{1,0:T(8,128)(2,1)S(1)}, bf16[896,256]{1,0:T(8,128)(2,1)S(1)}, u32[]{:S(2)}, u32[]{:S(2)}) collective-permute-start(bf16[896,256]{1,0:T(8,128)(2,1)S(1)} %collective-permute-done.32.refs_0_), channel_id=1, source_target_pairs={{8,0},{16,8},{24,16},{28,24},{20,28},{12,20},{4,12},{0,4},{2,10},{... | collective-permute-start | bytes 1376264 | tf_op jit(solution)/shard_map/ppermute | solution.py:438
  116.9 9.0 %collective-permute-start.34 = (bf16[896,256]{1,0:T(8,128)(2,1)S(1)}, bf16[896,256]{1,0:T(8,128)(2,1)S(1)}, u32[]{:S(2)}, u32[]{:S(2)}) collective-permute-start(bf16[896,256]{1,0:T(8,128)(2,1)S(1)} %collective-permute-done.33.refs_0_), channel_id=1, source_target_pairs={{0,8},{8,16},{16,24},{24,28},{28,20},{20,12},{12,4},{4,0},{10,2},{... | collective-permute-start | bytes 1376264 | tf_op jit(solution)/shard_map/ppermute | solution.py:438
  121.7 9.0 %collective-permute-start.44 = (bf16[896,256]{1,0:T(8,128)(2,1)S(1)}, bf16[896,256]{1,0:T(8,128)(2,1)S(1)}, u32[]{:S(2)}, u32[]{:S(2)}) collective-permute-start(bf16[896,256]{1,0:T(8,128)(2,1)S(1)} %collective-permute-done.41.refs_0_), channel_id=1, source_target_pairs={{8,0},{16,8},{24,16},{28,24},{20,28},{12,20},{4,12},{0,4},{2,10},{... | collective-permute-start | bytes 1376264 | tf_op jit(solution)/shard_map/ppermute | solution.py:438
  127.1 8.2 %collective-permute-start.39 = (bf16[896,256]{1,0:T(8,128)(2,1)S(1)}, bf16[896,256]{1,0:T(8,128)(2,1)S(1)}, u32[]{:S(2)}, u32[]{:S(2)}) collective-permute-start(bf16[896,256]{1,0:T(8,128)(2,1)S(1)} %collective-permute-done.34.refs_0_), channel_id=1, source_target_pairs={{0,8},{8,16},{16,24},{24,28},{28,20},{20,12},{12,4},{4,0},{10,2},{... | collective-permute-start | bytes 1376264 | tf_op jit(solution)/shard_map/ppermute | solution.py:438
  (23 other events, 121.1 us)

commit v20 on v17

--- a/solution.py
+++ b/solution.py
@@ -333,9 +333,10 @@
 def exchange_windows(count):
     chips, steps = count // 2, count // 4
     far, near = list(range(chips, count)), list(range(1, chips))
-    each = -(-len(near) // steps)
-    windows = [far[w + 1 : w + 2] + near[(w - 1) * each : w * each] for w in range(1, steps + 1)]
-    return [far[:2]] + windows + [far[steps + 2 :]]
+    windows = [far[:2], [far[2]] + near[:2]]
+    windows += [[far[w + 1], near[w]] for w in range(2, steps)]
+    windows[-1].insert(1, far[steps + 1])
+    return windows + [near[steps:], far[steps + 2 :]]
 
 
 def gather_and_exchange(sketch, outgoing, count):

time: 137 us -> 146 us (1.066)
  starting transfers between devices: 59.4 us -> 65.7 us
  waiting for transfers between devices: 41.1 us -> 43.5 us
    ppermute x15, starting transfers between devices: 21.5 us -> 29.3 us  [exchange(): columns[k] = lax.ppermute(tie(outgoing[k], *after), 'fsdp', pairs)]
    ppermute x7, starting transfers between devices: 9.27 us -> 6.67 us  [local(): arrived[later] = lax.ppermute(block, 'fsdp', turns[(later + 1) % 2])]
    ppermute x3, starting transfers between devices: 8.18 us -> 6.02 us  [gather_and_exchange(): held.append(lax.ppermute(block, 'tp', across))]
    ppermute x3, waiting for transfers between devices: 2.74 us -> 4.22 us  [gather_and_exchange(): held.append(lax.ppermute(block, 'tp', across))]
  transfers between devices with their start and end apart: 46 -> 46, of which waited for: 14 -> 15; matrix products, arithmetic and copies ran while one was open for 0% -> 0% of each run, Pallas kernels for 19% -> 18%
where the time goes in v20:
time: 146 us
  starting transfers between devices  65.7 us (45%)
  waiting for transfers between devices  43.5 us (30%)
  Pallas kernels  28.7 us (20%)
  other arithmetic  3.98 us (3%)
    ppermute x15, starting transfers between devices, exchange(): columns[k] = lax.ppermute(tie(outgoing[k], *after), 'fsdp', pairs)  29.3 us
    ppermute x15, waiting for transfers between devices, exchange(): columns[k] = lax.ppermute(tie(outgoing[k], *after), 'fsdp', pairs)  19.3 us
    pallas_call x1, Pallas kernels, factor_call(): pl.pallas_call(functools.partial(factor_kernel, len(stacked), owner), in_...  14.2 us
    pallas_call x7, Pallas kernels, output_call(): pl.pallas_call(functools.partial(output_kernel, owner, factor), in_specs=...  12.7 us
    ppermute x7, starting transfers between devices, sum_round(): terms.append(lax.ppermute(x, axis, [(n, n ^ d) for n in range(size)]))  9.01 us
    ppermute x7, waiting for transfers between devices, local(): arrived[later] = lax.ppermute(block, 'fsdp', turns[(later + 1) % 2])  8.69 us
    ppermute x8, starting transfers between devices, local(): blocks += [block, lax.ppermute(block, 'fsdp', swap)]  8.41 us
    ppermute x7, waiting for transfers between devices, sum_round(): terms.append(lax.ppermute(x, axis, [(n, n ^ d) for n in range(size)]))  7.67 us
  transfers between devices with their start and end apart: 46, of which 15 were waited for; matrix products, arithmetic and copies ran while one was open for 0% of the time, Pallas kernels for 18%

profile of v20, /device:TPU:1, one launch (start us, length us, event | category | flops | bytes accessed | tf_op | source)
XLA Modules:
  0.0 145.7 jit_solution(8308072106140397683)
XLA Ops:
  0.6 4.0 %convert_add_fusion.base_ref = f32[96,13824]{1,0:T(8,128)S(1)} fusion(f32[96,13824]{1,0:T(8,128)} %param.3, bf16[96,13824]{1,0:T(8,128)(2,1)} %param.4), kind=kLoop, calls=%fused_computation | loop fusion | flops 2654208 | bytes 13271040 | tf_op jit(solution)/shard_map/add | solution.py:403
  7.2 2.1 %collective-permute-start = (f32[96,256]{1,0:T(8,128)S(1)}, f32[96,256]{1,0:T(8,128)S(1)}, u32[]{:S(2)}, u32[]{:S(2)}) collective-permute-start(f32[96,256]{1,0:T(8,128)S(1)} %fusion), channel_id=1, source_target_pairs={{0,1},{1,0},{2,3},{3,2},{4,5},{5,4},{6,7},{7,6},{8,9},{9,8},{10,11... | collective-permute-start | bytes 294920 | tf_op jit(solution)/shard_map/ppermute | solution.py:355
  9.8 3.2 %collective-permute-start.4 = (bf16[96,896]{1,0:T(8,128)(2,1)S(1)}, bf16[96,896]{1,0:T(8,128)(2,1)S(1)}, u32[]{:S(2)}, u32[]{:S(2)}) collective-permute-start(bf16[96,896]{1,0:T(8,128)(2,1)S(1)} %get-tuple-element.69), channel_id=1, source_target_pairs={{0,18},{2,16},{4,22},{6,20},{8,26},{10,24},{12,30},{14,28},{16,2},... | collective-permute-start | bytes 516104 | tf_op jit(solution)/shard_map/ppermute | solution.py:351
  15.7 9.6 %collective-permute-done.4.refs_9_ = bf16[96,896]{1,0:T(8,128)(2,1)S(1)} collective-permute-done((bf16[96,896]{1,0:T(8,128)(2,1)S(1)}, bf16[96,896]{1,0:T(8,128)(2,1)S(1)}, u32[]{:S(2)}, u32[]{:S(2)}) %collective-permute-start.4) | collective-permute-done | bytes 172064 | tf_op jit(solution)/shard_map/ppermute | solution.py:351
  25.3 3.5 %collective-permute-done.3.refs_8_ = bf16[96,896]{1,0:T(8,128)(2,1)S(1)} collective-permute-done((bf16[96,896]{1,0:T(8,128)(2,1)S(1)}, bf16[96,896]{1,0:T(8,128)(2,1)S(1)}, u32[]{:S(2)}, u32[]{:S(2)}) %collective-permute-start.3) | collective-permute-done | bytes 172064 | tf_op jit(solution)/shard_map/ppermute | solution.py:351
  30.0 5.2 %collective-permute-start.2 = (f32[96,256]{1,0:T(8,128)S(1)}, f32[96,256]{1,0:T(8,128)S(1)}, u32[]{:S(2)}, u32[]{:S(2)}) collective-permute-start(f32[96,256]{1,0:T(8,128)S(1)} %collective-permute-done.1), channel_id=1, source_target_pairs={{0,1},{1,0},{2,3},{3,2},{4,5},{5,4},{6,7},{7,6},{8,9},{9,8},{10,11... | collective-permute-start | bytes 294920 | tf_op jit(solution)/shard_map/ppermute | solution.py:366
  35.3 2.1 %collective-permute-start.13 = (bf16[96,896]{1,0:T(8,128)(2,1)S(1)}, bf16[96,896]{1,0:T(8,128)(2,1)S(1)}, u32[]{:S(2)}, u32[]{:S(2)}) collective-permute-start(bf16[96,896]{1,0:T(8,128)(2,1)S(1)} %get-tuple-element.81), channel_id=1, source_target_pairs={{0,6},{2,4},{4,2},{6,0},{8,14},{10,12},{12,10},{14,8},{16,22},{18,... | collective-permute-start | bytes 516104 | tf_op jit(solution)/shard_map/ppermute | solution.py:351
  41.1 2.7 %collective-permute-done.13.refs_3_ = bf16[96,896]{1,0:T(8,128)(2,1)S(1)} collective-permute-done((bf16[96,896]{1,0:T(8,128)(2,1)S(1)}, bf16[96,896]{1,0:T(8,128)(2,1)S(1)}, u32[]{:S(2)}, u32[]{:S(2)}) %collective-permute-start.13) | collective-permute-done | bytes 172064 | tf_op jit(solution)/shard_map/ppermute | solution.py:351
  43.9 4.7 %collective-permute-start.16 = (bf16[96,896]{1,0:T(8,128)(2,1)S(1)}, bf16[96,896]{1,0:T(8,128)(2,1)S(1)}, u32[]{:S(2)}, u32[]{:S(2)}) collective-permute-start(bf16[96,896]{1,0:T(8,128)(2,1)S(1)} %get-tuple-element.86), channel_id=1, source_target_pairs={{0,26},{2,24},{4,30},{6,28},{8,18},{10,16},{12,22},{14,20},{16,10}... | collective-permute-start | bytes 516104 | tf_op jit(solution)/shard_map/ppermute | solution.py:351
  48.5 2.0 %collective-permute-start.15 = (bf16[96,896]{1,0:T(8,128)(2,1)S(1)}, bf16[96,896]{1,0:T(8,128)(2,1)S(1)}, u32[]{:S(2)}, u32[]{:S(2)}) collective-permute-start(bf16[96,896]{1,0:T(8,128)(2,1)S(1)} %get-tuple-element.84), channel_id=1, source_target_pairs={{0,24},{2,26},{4,28},{6,30},{8,16},{10,18},{12,20},{14,22},{16,8},... | collective-permute-start | bytes 516104 | tf_op jit(solution)/shard_map/ppermute | solution.py:351
  51.5 4.2 %collective-permute-done.11 = f32[96,256]{1,0:T(8,128)S(1)} collective-permute-done((f32[96,256]{1,0:T(8,128)S(1)}, f32[96,256]{1,0:T(8,128)S(1)}, u32[]{:S(2)}, u32[]{:S(2)}) %collective-permute-start.11) | collective-permute-done | bytes 98336 | tf_op jit(solution)/shard_map/ppermute | solution.py:366
  55.7 3.6 %collective-permute-done.14 = f32[96,256]{1,0:T(8,128)S(1)} collective-permute-done((f32[96,256]{1,0:T(8,128)S(1)}, f32[96,256]{1,0:T(8,128)S(1)}, u32[]{:S(2)}, u32[]{:S(2)}) %collective-permute-start.14) | collective-permute-done | bytes 98336 | tf_op jit(solution)/shard_map/ppermute | solution.py:362
  59.5 7.6 %collective-permute-start.21 = (bf16[96,896]{1,0:T(8,128)(2,1)S(1)}, bf16[96,896]{1,0:T(8,128)(2,1)S(1)}, u32[]{:S(2)}, u32[]{:S(2)}) collective-permute-start(bf16[96,896]{1,0:T(8,128)(2,1)S(1)} %get-tuple-element.98), channel_id=1, source_target_pairs={{0,14},{2,12},{4,10},{6,8},{8,6},{10,4},{12,2},{14,0},{16,30},{18,... | collective-permute-start | bytes 516104 | tf_op jit(solution)/shard_map/ppermute | solution.py:351
  68.9 2.0 %collective-permute-start.23 = (bf16[96,896]{1,0:T(8,128)(2,1)S(1)}, bf16[96,896]{1,0:T(8,128)(2,1)S(1)}, u32[]{:S(2)}, u32[]{:S(2)}) collective-permute-start(bf16[96,896]{1,0:T(8,128)(2,1)S(1)} %get-tuple-element.102), channel_id=1, source_target_pairs={{0,30},{2,28},{4,26},{6,24},{8,22},{10,20},{12,18},{14,16},{16,14}... | collective-permute-start | bytes 516104 | tf_op jit(solution)/shard_map/ppermute | solution.py:351
  70.9 2.2 %collective-permute-start.22 = (bf16[96,896]{1,0:T(8,128)(2,1)S(1)}, bf16[96,896]{1,0:T(8,128)(2,1)S(1)}, u32[]{:S(2)}, u32[]{:S(2)}) collective-permute-start(bf16[96,896]{1,0:T(8,128)(2,1)S(1)} %get-tuple-element.100), channel_id=1, source_target_pairs={{0,28},{2,30},{4,24},{6,26},{8,20},{10,22},{12,16},{14,18},{16,12}... | collective-permute-start | bytes 516104 | tf_op jit(solution)/shard_map/ppermute | solution.py:351
  73.1 14.2 %factor.1 = (bf16[256,1536]{1,0:T(8,128)(2,1)S(1)}, bf16[96,256]{1,0:T(8,128)(2,1)S(1)}) custom-call(f32[96,13824]{1,0:T(8,128)S(1)} %convert_add_fusion.base_ref, f32[8,96,256]{2,1,0:T(8,128)S(1)} %bitcast_dynamic-update-slice_fusion.refs_0_, f32[8,96,256]{2,1,0:T(8,128)S(1)} %collective-permute-done.18.refs_1_), custom_call_target="tpu_custom_call" | custom-call | flops 4026531840 | bytes 2359296 | tf_op jit(solution)/shard_map/factor/pallas_call | solution.py:166
  88.0 2.8 %collective-permute-done.22.refs_14_ = bf16[96,896]{1,0:T(8,128)(2,1)S(1)} collective-permute-done((bf16[96,896]{1,0:T(8,128)(2,1)S(1)}, bf16[96,896]{1,0:T(8,128)(2,1)S(1)}, u32[]{:S(2)}, u32[]{:S(2)}) %collective-permute-start.22) | collective-permute-done | bytes 172064 | tf_op jit(solution)/shard_map/ppermute | solution.py:351
  96.9 1.9 %collective-permute-start.25 = (f32[1,256]{1,0:T(1,128)S(1)}, f32[1,256]{1,0:T(1,128)S(1)}, u32[]{:S(2)}, u32[]{:S(2)}) collective-permute-start(f32[1,256]{1,0:T(1,128)S(1)} %add.29), channel_id=1, source_target_pairs={{0,2},{2,0},{4,6},{6,4},{8,10},{10,8},{12,14},{14,12},{16,18},{18,... | collective-permute-start | bytes 3080 | tf_op jit(solution)/shard_map/ppermute | solution.py:387
  100.5 5.7 %collective-permute-done.26 = f32[1,256]{1,0:T(1,128)S(1)} collective-permute-done((f32[1,256]{1,0:T(1,128)S(1)}, f32[1,256]{1,0:T(1,128)S(1)}, u32[]{:S(2)}, u32[]{:S(2)}) %collective-permute-start.26) | collective-permute-done | bytes 1056 | tf_op jit(solution)/shard_map/ppermute | solution.py:387
  107.6 2.2 %collective-permute-start.30 = (f32[1,256]{1,0:T(1,128)S(1)}, f32[1,256]{1,0:T(1,128)S(1)}, u32[]{:S(2)}, u32[]{:S(2)}) collective-permute-start(f32[1,256]{1,0:T(1,128)S(1)} %add_add_fusion.1), channel_id=1, source_target_pairs={{0,24},{2,26},{4,28},{6,30},{8,16},{10,18},{12,20},{14,22},{16,8},... | collective-permute-start | bytes 3080 | tf_op jit(solution)/shard_map/ppermute | solution.py:387
  111.8 2.3 %collective-permute-start.37 = (bf16[896,256]{1,0:T(8,128)(2,1)S(1)}, bf16[896,256]{1,0:T(8,128)(2,1)S(1)}, u32[]{:S(2)}, u32[]{:S(2)}) collective-permute-start(bf16[896,256]{1,0:T(8,128)(2,1)S(1)} %collective-permute-done.31.refs_2_), channel_id=1, source_target_pairs={{0,2},{2,0},{4,6},{6,4},{8,10},{10,8},{12,14},{14,12},{16,18},{18,... | collective-permute-start | bytes 1376264 | tf_op jit(solution)/shard_map/ppermute | solution.py:439
  115.6 2.8 %outputs.7 = (f32[96,13824]{1,0:T(8,128)}, bf16[13824,256]{1,0:T(8,128)(2,1)}, bf16[96,13824]{1,0:T(8,128)(2,1)}) custom-call(f32[96,13824]{1,0:T(8,128)S(1)} %convert_add_fusion.base_ref, bf16[96,256]{1,0:T(8,128)(2,1)S(1)} %get-tuple-element.90.ortho_ref, f32[1,256]{1,0:T(1,128)S(1)} %add_add_fusion.colsq_ref, ...), custom_call_target="tpu_custom_call" | custom-call | flops 352321536 | bytes 7110656 | tf_op jit(solution)/shard_map/outputs/pallas_call | solution.py:271
  118.8 3.0 %collective-permute-done.33.refs_0_ = bf16[896,256]{1,0:T(8,128)(2,1)S(1)} collective-permute-done((bf16[896,256]{1,0:T(8,128)(2,1)S(1)}, bf16[896,256]{1,0:T(8,128)(2,1)S(1)}, u32[]{:S(2)}, u32[]{:S(2)}) %collective-permute-start.33) | collective-permute-done | bytes 458784 | tf_op jit(solution)/shard_map/ppermute | solution.py:438
  139.6 2.2 %collective-permute-done.39.refs_2_ = bf16[896,256]{1,0:T(8,128)(2,1)S(1)} collective-permute-done((bf16[896,256]{1,0:T(8,128)(2,1)S(1)}, bf16[896,256]{1,0:T(8,128)(2,1)S(1)}, u32[]{:S(2)}, u32[]{:S(2)}) %collective-permute-start.39) | collective-permute-done | bytes 458784 | tf_op jit(solution)/shard_map/ppermute | solution.py:438
  (93 shorter events, 48.8 us)
Async XLA Ops:
  9.8 15.5 %collective-permute-start.4 = (bf16[96,896]{1,0:T(8,128)(2,1)S(1)}, bf16[96,896]{1,0:T(8,128)(2,1)S(1)}, u32[]{:S(2)}, u32[]{:S(2)}) collective-permute-start(bf16[96,896]{1,0:T(8,128)(2,1)S(1)} %get-tuple-element.69), channel_id=1, source_target_pairs={{0,18},{2,16},{4,22},{6,20},{8,26},{10,24},{12,30},{14,28},{16,2},... | collective-permute-start | bytes 516104 | tf_op jit(solution)/shard_map/ppermute | solution.py:351
  13.0 15.8 %collective-permute-start.3 = (bf16[96,896]{1,0:T(8,128)(2,1)S(1)}, bf16[96,896]{1,0:T(8,128)(2,1)S(1)}, u32[]{:S(2)}, u32[]{:S(2)}) collective-permute-start(bf16[96,896]{1,0:T(8,128)(2,1)S(1)} %get-tuple-element.67), channel_id=1, source_target_pairs={{0,16},{2,18},{4,20},{6,22},{8,24},{10,26},{12,28},{14,30},{16,0},... | collective-permute-start | bytes 516104 | tf_op jit(solution)/shard_map/ppermute | solution.py:351
  13.1 15.7 %collective-permute-start.1 = (f32[96,256]{1,0:T(8,128)S(1)}, f32[96,256]{1,0:T(8,128)S(1)}, u32[]{:S(2)}, u32[]{:S(2)}) collective-permute-start(f32[96,256]{1,0:T(8,128)S(1)} %get-tuple-element.130), channel_id=1, source_target_pairs={{0,8},{8,16},{16,24},{24,28},{28,20},{20,12},{12,4},{4,0},{10,2},{... | collective-permute-start | bytes 294920 | tf_op jit(solution)/shard_map/ppermute | solution.py:362
  14.4 20.9 %collective-permute-start.9 = (bf16[96,896]{1,0:T(8,128)(2,1)S(1)}, bf16[96,896]{1,0:T(8,128)(2,1)S(1)}, u32[]{:S(2)}, u32[]{:S(2)}) collective-permute-start(bf16[96,896]{1,0:T(8,128)(2,1)S(1)} %get-tuple-element.76), channel_id=1, source_target_pairs={{0,4},{2,6},{4,0},{6,2},{8,12},{10,14},{12,8},{14,10},{16,20},{18,... | collective-permute-start | bytes 516104 | tf_op jit(solution)/shard_map/ppermute | solution.py:351
  15.7 21.7 %collective-permute-start.8 = (bf16[96,896]{1,0:T(8,128)(2,1)S(1)}, bf16[96,896]{1,0:T(8,128)(2,1)S(1)}, u32[]{:S(2)}, u32[]{:S(2)}) collective-permute-start(bf16[96,896]{1,0:T(8,128)(2,1)S(1)} %get-tuple-element.74), channel_id=1, source_target_pairs={{0,2},{2,0},{4,6},{6,4},{8,10},{10,8},{12,14},{14,12},{16,18},{18,... | collective-permute-start | bytes 516104 | tf_op jit(solution)/shard_map/ppermute | solution.py:351
  25.3 13.5 %collective-permute-start.7 = (bf16[96,896]{1,0:T(8,128)(2,1)S(1)}, bf16[96,896]{1,0:T(8,128)(2,1)S(1)}, u32[]{:S(2)}, u32[]{:S(2)}) collective-permute-start(bf16[96,896]{1,0:T(8,128)(2,1)S(1)} %get-tuple-element.72), channel_id=1, source_target_pairs={{0,20},{2,22},{4,16},{6,18},{8,28},{10,30},{12,24},{14,26},{16,4},... | collective-permute-start | bytes 516104 | tf_op jit(solution)/shard_map/ppermute | solution.py:351
  28.8 10.0 %collective-permute-start.5 = (f32[96,256]{1,0:T(8,128)S(1)}, f32[96,256]{1,0:T(8,128)S(1)}, u32[]{:S(2)}, u32[]{:S(2)}) collective-permute-start(f32[96,256]{1,0:T(8,128)S(1)} %collective-permute-done.1), channel_id=1, source_target_pairs={{0,8},{8,16},{16,24},{24,28},{28,20},{20,12},{12,4},{4,0},{10,2},{... | collective-permute-start | bytes 294920 | tf_op jit(solution)/shard_map/ppermute | solution.py:362
  30.0 10.2 %collective-permute-start.2 = (f32[96,256]{1,0:T(8,128)S(1)}, f32[96,256]{1,0:T(8,128)S(1)}, u32[]{:S(2)}, u32[]{:S(2)}) collective-permute-start(f32[96,256]{1,0:T(8,128)S(1)} %collective-permute-done.1), channel_id=1, source_target_pairs={{0,1},{1,0},{2,3},{3,2},{4,5},{5,4},{6,7},{7,6},{8,9},{9,8},{10,11... | collective-permute-start | bytes 294920 | tf_op jit(solution)/shard_map/ppermute | solution.py:366
  37.4 11.2 %collective-permute-start.12 = (bf16[96,896]{1,0:T(8,128)(2,1)S(1)}, bf16[96,896]{1,0:T(8,128)(2,1)S(1)}, u32[]{:S(2)}, u32[]{:S(2)}) collective-permute-start(bf16[96,896]{1,0:T(8,128)(2,1)S(1)} %get-tuple-element.79), channel_id=1, source_target_pairs={{0,22},{2,20},{4,18},{6,16},{8,30},{10,28},{12,26},{14,24},{16,6},... | collective-permute-start | bytes 516104 | tf_op jit(solution)/shard_map/ppermute | solution.py:351
  38.8 11.7 %collective-permute-start.10 = (f32[96,256]{1,0:T(8,128)S(1)}, f32[96,256]{1,0:T(8,128)S(1)}, u32[]{:S(2)}, u32[]{:S(2)}) collective-permute-start(f32[96,256]{1,0:T(8,128)S(1)} %collective-permute-done.5), channel_id=1, source_target_pairs={{0,8},{8,16},{16,24},{24,28},{28,20},{20,12},{12,4},{4,0},{10,2},{... | collective-permute-start | bytes 294920 | tf_op jit(solution)/shard_map/ppermute | solution.py:362
  39.4 20.0 %collective-permute-start.17 = (bf16[96,896]{1,0:T(8,128)(2,1)S(1)}, bf16[96,896]{1,0:T(8,128)(2,1)S(1)}, u32[]{:S(2)}, u32[]{:S(2)}) collective-permute-start(bf16[96,896]{1,0:T(8,128)(2,1)S(1)} %get-tuple-element.88), channel_id=1, source_target_pairs={{0,8},{2,10},{4,12},{6,14},{8,0},{10,2},{12,4},{14,6},{16,24},{18,... | collective-permute-start | bytes 516104 | tf_op jit(solution)/shard_map/ppermute | solution.py:351
  40.3 11.2 %collective-permute-start.6 = (f32[96,256]{1,0:T(8,128)S(1)}, f32[96,256]{1,0:T(8,128)S(1)}, u32[]{:S(2)}, u32[]{:S(2)}) collective-permute-start(f32[96,256]{1,0:T(8,128)S(1)} %collective-permute-done.5), channel_id=1, source_target_pairs={{0,1},{1,0},{2,3},{3,2},{4,5},{5,4},{6,7},{7,6},{8,9},{9,8},{10,11... | collective-permute-start | bytes 294920 | tf_op jit(solution)/shard_map/ppermute | solution.py:366
  43.9 15.6 %collective-permute-start.16 = (bf16[96,896]{1,0:T(8,128)(2,1)S(1)}, bf16[96,896]{1,0:T(8,128)(2,1)S(1)}, u32[]{:S(2)}, u32[]{:S(2)}) collective-permute-start(bf16[96,896]{1,0:T(8,128)(2,1)S(1)} %get-tuple-element.86), channel_id=1, source_target_pairs={{0,26},{2,24},{4,30},{6,28},{8,18},{10,16},{12,22},{14,20},{16,10}... | collective-permute-start | bytes 516104 | tf_op jit(solution)/shard_map/ppermute | solution.py:351
  48.5 10.9 %collective-permute-start.15 = (bf16[96,896]{1,0:T(8,128)(2,1)S(1)}, bf16[96,896]{1,0:T(8,128)(2,1)S(1)}, u32[]{:S(2)}, u32[]{:S(2)}) collective-permute-start(bf16[96,896]{1,0:T(8,128)(2,1)S(1)} %get-tuple-element.84), channel_id=1, source_target_pairs={{0,24},{2,26},{4,28},{6,30},{8,16},{10,18},{12,20},{14,22},{16,8},... | collective-permute-start | bytes 516104 | tf_op jit(solution)/shard_map/ppermute | solution.py:351
  59.4 11.5 %collective-permute-start.18 = (f32[8,96,256]{2,1,0:T(8,128)S(1)}, f32[8,96,256]{2,1,0:T(8,128)S(1)}, u32[]{:S(2)}, u32[]{:S(2)}) collective-permute-start(f32[8,96,256]{2,1,0:T(8,128)S(1)} %bitcast_dynamic-update-slice_fusion.refs_0_), channel_id=1, source_target_pairs={{0,2},{2,0},{4,6},{6,4},{8,10},{10,8},{12,14},{14,12},{16,18},{18,... | collective-permute-start | bytes 2359304 | tf_op jit(solution)/shard_map/ppermute | solution.py:370
  59.5 27.8 %collective-permute-start.21 = (bf16[96,896]{1,0:T(8,128)(2,1)S(1)}, bf16[96,896]{1,0:T(8,128)(2,1)S(1)}, u32[]{:S(2)}, u32[]{:S(2)}) collective-permute-start(bf16[96,896]{1,0:T(8,128)(2,1)S(1)} %get-tuple-element.98), channel_id=1, source_target_pairs={{0,14},{2,12},{4,10},{6,8},{8,6},{10,4},{12,2},{14,0},{16,30},{18,... | collective-permute-start | bytes 516104 | tf_op jit(solution)/shard_map/ppermute | solution.py:351
  67.2 20.2 %collective-permute-start.20 = (bf16[96,896]{1,0:T(8,128)(2,1)S(1)}, bf16[96,896]{1,0:T(8,128)(2,1)S(1)}, u32[]{:S(2)}, u32[]{:S(2)}) collective-permute-start(bf16[96,896]{1,0:T(8,128)(2,1)S(1)} %get-tuple-element.96), channel_id=1, source_target_pairs={{0,12},{2,14},{4,8},{6,10},{8,4},{10,6},{12,0},{14,2},{16,28},{18,... | collective-permute-start | bytes 516104 | tf_op jit(solution)/shard_map/ppermute | solution.py:351
  67.2 20.1 %collective-permute-start.19 = (bf16[96,896]{1,0:T(8,128)(2,1)S(1)}, bf16[96,896]{1,0:T(8,128)(2,1)S(1)}, u32[]{:S(2)}, u32[]{:S(2)}) collective-permute-start(bf16[96,896]{1,0:T(8,128)(2,1)S(1)} %get-tuple-element.94), channel_id=1, source_target_pairs={{0,10},{2,8},{4,14},{6,12},{8,2},{10,0},{12,6},{14,4},{16,26},{18,... | collective-permute-start | bytes 516104 | tf_op jit(solution)/shard_map/ppermute | solution.py:351
  68.9 19.1 %collective-permute-start.23 = (bf16[96,896]{1,0:T(8,128)(2,1)S(1)}, bf16[96,896]{1,0:T(8,128)(2,1)S(1)}, u32[]{:S(2)}, u32[]{:S(2)}) collective-permute-start(bf16[96,896]{1,0:T(8,128)(2,1)S(1)} %get-tuple-element.102), channel_id=1, source_target_pairs={{0,30},{2,28},{4,26},{6,24},{8,22},{10,20},{12,18},{14,16},{16,14}... | collective-permute-start | bytes 516104 | tf_op jit(solution)/shard_map/ppermute | solution.py:351
  70.9 19.9 %collective-permute-start.22 = (bf16[96,896]{1,0:T(8,128)(2,1)S(1)}, bf16[96,896]{1,0:T(8,128)(2,1)S(1)}, u32[]{:S(2)}, u32[]{:S(2)}) collective-permute-start(bf16[96,896]{1,0:T(8,128)(2,1)S(1)} %get-tuple-element.100), channel_id=1, source_target_pairs={{0,28},{2,30},{4,24},{6,26},{8,20},{10,22},{12,16},{14,18},{16,12}... | collective-permute-start | bytes 516104 | tf_op jit(solution)/shard_map/ppermute | solution.py:351
  92.2 19.7 %collective-permute-start.31 = (bf16[896,256]{1,0:T(8,128)(2,1)S(1)}, bf16[896,256]{1,0:T(8,128)(2,1)S(1)}, u32[]{:S(2)}, u32[]{:S(2)}) collective-permute-start(bf16[896,256]{1,0:T(8,128)(2,1)S(1)} %get-tuple-element.104.refs_0_), channel_id=1, source_target_pairs={{0,8},{8,16},{16,24},{24,28},{28,20},{20,12},{12,4},{4,0},{10,2},{... | collective-permute-start | bytes 1376264 | tf_op jit(solution)/shard_map/ppermute | solution.py:438
  93.8 18.0 %collective-permute-start.32 = (bf16[896,256]{1,0:T(8,128)(2,1)S(1)}, bf16[896,256]{1,0:T(8,128)(2,1)S(1)}, u32[]{:S(2)}, u32[]{:S(2)}) collective-permute-start(bf16[896,256]{1,0:T(8,128)(2,1)S(1)} %get-tuple-element.104.refs_0_), channel_id=1, source_target_pairs={{8,0},{16,8},{24,16},{28,24},{20,28},{12,20},{4,12},{0,4},{2,10},{... | collective-permute-start | bytes 1376264 | tf_op jit(solution)/shard_map/ppermute | solution.py:438
  118.8 9.0 %collective-permute-start.41 = (bf16[896,256]{1,0:T(8,128)(2,1)S(1)}, bf16[896,256]{1,0:T(8,128)(2,1)S(1)}, u32[]{:S(2)}, u32[]{:S(2)}) collective-permute-start(bf16[896,256]{1,0:T(8,128)(2,1)S(1)} %collective-permute-done.32.refs_0_), channel_id=1, source_target_pairs={{8,0},{16,8},{24,16},{28,24},{20,28},{12,20},{4,12},{0,4},{2,10},{... | collective-permute-start | bytes 1376264 | tf_op jit(solution)/shard_map/ppermute | solution.py:438
  128.3 9.0 %collective-permute-start.44 = (bf16[896,256]{1,0:T(8,128)(2,1)S(1)}, bf16[896,256]{1,0:T(8,128)(2,1)S(1)}, u32[]{:S(2)}, u32[]{:S(2)}) collective-permute-start(bf16[896,256]{1,0:T(8,128)(2,1)S(1)} %collective-permute-done.41.refs_0_), channel_id=1, source_target_pairs={{8,0},{16,8},{24,16},{28,24},{20,28},{12,20},{4,12},{0,4},{2,10},{... | collective-permute-start | bytes 1376264 | tf_op jit(solution)/shard_map/ppermute | solution.py:438
  (23 other events, 133.8 us)

commit v21 on v17

--- a/solution.py
+++ b/solution.py
@@ -334,7 +334,8 @@
     chips, steps = count // 2, count // 4
     far, near = list(range(chips, count)), list(range(1, chips))
     each = -(-len(near) // steps)
-    windows = [far[w + 1 : w + 2] + near[(w - 1) * each : w * each] for w in range(1, steps + 1)]
+    cuts = [0] + [w * each - 1 for w in range(1, steps)] + [len(near)]
+    windows = [far[w + 1 : w + 2] + near[cuts[w - 1] : cuts[w]] for w in range(1, steps + 1)]
     return [far[:2]] + windows + [far[steps + 2 :]]
 
 

time: 137 us -> 144 us (1.051)
  waiting for transfers between devices: 41.1 us -> 45.1 us
  starting transfers between devices: 59.4 us -> 61.8 us
    ppermute x15, waiting for transfers between devices: 19.1 us -> 27.4 us  [exchange(): columns[k] = lax.ppermute(tie(outgoing[k], *after), 'fsdp', pairs)]
    ppermute x3, starting transfers between devices: 8.18 us -> 3.2 us  [gather_and_exchange(): held.append(lax.ppermute(block, 'tp', across))]
    ppermute x15, starting transfers between devices: 21.5 us -> 25.6 us  [exchange(): columns[k] = lax.ppermute(tie(outgoing[k], *after), 'fsdp', pairs)]
    ppermute x4, waiting for transfers between devices: 3.68 us -> 0.01 us  [gather_and_exchange(): block = lax.ppermute(block, ('fsdp', 'tp'), turns)]
    ppermute x7, waiting for transfers between devices: 8.73 us -> 5.82 us  [local(): arrived[later] = lax.ppermute(block, 'fsdp', turns[(later + 1) % 2])]
    ppermute x8, starting transfers between devices: 7.49 us -> 9.86 us  [local(): blocks += [block, lax.ppermute(block, 'fsdp', swap)]]
  transfers between devices with their start and end apart: 46 -> 46, of which waited for: 14 -> 15; matrix products, arithmetic and copies ran while one was open for 0% -> 0% of each run, Pallas kernels for 19% -> 18%
where the time goes in v21:
time: 144 us; the launch traced here: 143 us
  starting transfers between devices  61.8 us (43%)
  waiting for transfers between devices  45.1 us (31%)
  Pallas kernels  28.8 us (20%)
  other arithmetic  3.98 us (3%)
    ppermute x15, waiting for transfers between devices, exchange(): columns[k] = lax.ppermute(tie(outgoing[k], *after), 'fsdp', pairs)  27.4 us
    ppermute x15, starting transfers between devices, exchange(): columns[k] = lax.ppermute(tie(outgoing[k], *after), 'fsdp', pairs)  25.6 us
    pallas_call x1, Pallas kernels, factor_call(): pl.pallas_call(functools.partial(factor_kernel, len(stacked), owner), in_...  14.2 us
    pallas_call x7, Pallas kernels, output_call(): pl.pallas_call(functools.partial(output_kernel, owner, factor), in_specs=...  12.7 us
    ppermute x7, starting transfers between devices, local(): arrived[later] = lax.ppermute(block, 'fsdp', turns[(later + 1) % 2])  9.92 us
    ppermute x8, starting transfers between devices, local(): blocks += [block, lax.ppermute(block, 'fsdp', swap)]  9.86 us
    ppermute x7, waiting for transfers between devices, sum_round(): terms.append(lax.ppermute(x, axis, [(n, n ^ d) for n in range(size)]))  8.16 us
    ppermute x7, starting transfers between devices, sum_round(): terms.append(lax.ppermute(x, axis, [(n, n ^ d) for n in range(size)]))  7.27 us
  transfers between devices with their start and end apart: 46, of which 15 were waited for; matrix products, arithmetic and copies ran while one was open for 0% of the time, Pallas kernels for 18%

profile of v21, /device:TPU:1, one launch (start us, length us, event | category | flops | bytes accessed | tf_op | source)
XLA Modules:
  0.0 143.4 jit_solution(16088716305804553985)
XLA Ops:
  0.6 4.0 %convert_add_fusion.base_ref = f32[96,13824]{1,0:T(8,128)S(1)} fusion(f32[96,13824]{1,0:T(8,128)} %param.3, bf16[96,13824]{1,0:T(8,128)(2,1)} %param.4), kind=kLoop, calls=%fused_computation | loop fusion | flops 2654208 | bytes 13271040 | tf_op jit(solution)/shard_map/add | solution.py:403
  9.8 3.2 %collective-permute-start.4 = (bf16[96,896]{1,0:T(8,128)(2,1)S(1)}, bf16[96,896]{1,0:T(8,128)(2,1)S(1)}, u32[]{:S(2)}, u32[]{:S(2)}) collective-permute-start(bf16[96,896]{1,0:T(8,128)(2,1)S(1)} %get-tuple-element.69), channel_id=1, source_target_pairs={{0,18},{2,16},{4,22},{6,20},{8,26},{10,24},{12,30},{14,28},{16,2},... | collective-permute-start | bytes 516104 | tf_op jit(solution)/shard_map/ppermute | solution.py:351
  15.1 2.6 %collective-permute-start.7 = (bf16[96,896]{1,0:T(8,128)(2,1)S(1)}, bf16[96,896]{1,0:T(8,128)(2,1)S(1)}, u32[]{:S(2)}, u32[]{:S(2)}) collective-permute-start(bf16[96,896]{1,0:T(8,128)(2,1)S(1)} %get-tuple-element.72), channel_id=1, source_target_pairs={{0,20},{2,22},{4,16},{6,18},{8,28},{10,30},{12,24},{14,26},{16,4},... | collective-permute-start | bytes 516104 | tf_op jit(solution)/shard_map/ppermute | solution.py:351
  17.7 11.3 %collective-permute-done.4.refs_9_ = bf16[96,896]{1,0:T(8,128)(2,1)S(1)} collective-permute-done((bf16[96,896]{1,0:T(8,128)(2,1)S(1)}, bf16[96,896]{1,0:T(8,128)(2,1)S(1)}, u32[]{:S(2)}, u32[]{:S(2)}) %collective-permute-start.4) | collective-permute-done | bytes 172064 | tf_op jit(solution)/shard_map/ppermute | solution.py:351
  29.0 3.5 %collective-permute-done.3.refs_8_ = bf16[96,896]{1,0:T(8,128)(2,1)S(1)} collective-permute-done((bf16[96,896]{1,0:T(8,128)(2,1)S(1)}, bf16[96,896]{1,0:T(8,128)(2,1)S(1)}, u32[]{:S(2)}, u32[]{:S(2)}) %collective-permute-start.3) | collective-permute-done | bytes 172064 | tf_op jit(solution)/shard_map/ppermute | solution.py:351
  37.1 2.6 %collective-permute-start.11 = (bf16[96,896]{1,0:T(8,128)(2,1)S(1)}, bf16[96,896]{1,0:T(8,128)(2,1)S(1)}, u32[]{:S(2)}, u32[]{:S(2)}) collective-permute-start(bf16[96,896]{1,0:T(8,128)(2,1)S(1)} %get-tuple-element.77), channel_id=1, source_target_pairs={{0,22},{2,20},{4,18},{6,16},{8,30},{10,28},{12,26},{14,24},{16,6},... | collective-permute-start | bytes 516104 | tf_op jit(solution)/shard_map/ppermute | solution.py:351
  41.6 4.4 %collective-permute-done.13.refs_3_ = bf16[96,896]{1,0:T(8,128)(2,1)S(1)} collective-permute-done((bf16[96,896]{1,0:T(8,128)(2,1)S(1)}, bf16[96,896]{1,0:T(8,128)(2,1)S(1)}, u32[]{:S(2)}, u32[]{:S(2)}) %collective-permute-start.13) | collective-permute-done | bytes 172064 | tf_op jit(solution)/shard_map/ppermute | solution.py:351
  49.6 3.7 %collective-permute-start.15 = (bf16[96,896]{1,0:T(8,128)(2,1)S(1)}, bf16[96,896]{1,0:T(8,128)(2,1)S(1)}, u32[]{:S(2)}, u32[]{:S(2)}) collective-permute-start(bf16[96,896]{1,0:T(8,128)(2,1)S(1)} %get-tuple-element.84), channel_id=1, source_target_pairs={{0,24},{2,26},{4,28},{6,30},{8,16},{10,18},{12,20},{14,22},{16,8},... | collective-permute-start | bytes 516104 | tf_op jit(solution)/shard_map/ppermute | solution.py:351
  53.4 3.7 %collective-permute-done.10 = f32[96,256]{1,0:T(8,128)S(1)} collective-permute-done((f32[96,256]{1,0:T(8,128)S(1)}, f32[96,256]{1,0:T(8,128)S(1)}, u32[]{:S(2)}, u32[]{:S(2)}) %collective-permute-start.10) | collective-permute-done | bytes 98336 | tf_op jit(solution)/shard_map/ppermute | solution.py:366
  57.2 4.4 %collective-permute-done.15.refs_12_ = bf16[96,896]{1,0:T(8,128)(2,1)S(1)} collective-permute-done((bf16[96,896]{1,0:T(8,128)(2,1)S(1)}, bf16[96,896]{1,0:T(8,128)(2,1)S(1)}, u32[]{:S(2)}, u32[]{:S(2)}) %collective-permute-start.15) | collective-permute-done | bytes 172064 | tf_op jit(solution)/shard_map/ppermute | solution.py:351
  62.0 2.9 %collective-permute-start.21 = (bf16[96,896]{1,0:T(8,128)(2,1)S(1)}, bf16[96,896]{1,0:T(8,128)(2,1)S(1)}, u32[]{:S(2)}, u32[]{:S(2)}) collective-permute-start(bf16[96,896]{1,0:T(8,128)(2,1)S(1)} %get-tuple-element.98), channel_id=1, source_target_pairs={{0,26},{2,24},{4,30},{6,28},{8,18},{10,16},{12,22},{14,20},{16,10}... | collective-permute-start | bytes 516104 | tf_op jit(solution)/shard_map/ppermute | solution.py:351
  64.9 2.7 %collective-permute-start.19 = (bf16[96,896]{1,0:T(8,128)(2,1)S(1)}, bf16[96,896]{1,0:T(8,128)(2,1)S(1)}, u32[]{:S(2)}, u32[]{:S(2)}) collective-permute-start(bf16[96,896]{1,0:T(8,128)(2,1)S(1)} %get-tuple-element.94), channel_id=1, source_target_pairs={{0,12},{2,14},{4,8},{6,10},{8,4},{10,6},{12,0},{14,2},{16,28},{18,... | collective-permute-start | bytes 516104 | tf_op jit(solution)/shard_map/ppermute | solution.py:351
  68.7 3.3 %collective-permute-start.22 = (bf16[96,896]{1,0:T(8,128)(2,1)S(1)}, bf16[96,896]{1,0:T(8,128)(2,1)S(1)}, u32[]{:S(2)}, u32[]{:S(2)}) collective-permute-start(bf16[96,896]{1,0:T(8,128)(2,1)S(1)} %get-tuple-element.100), channel_id=1, source_target_pairs={{0,28},{2,30},{4,24},{6,26},{8,20},{10,22},{12,16},{14,18},{16,12}... | collective-permute-start | bytes 516104 | tf_op jit(solution)/shard_map/ppermute | solution.py:351
  72.0 14.2 %factor.1 = (bf16[256,1536]{1,0:T(8,128)(2,1)S(1)}, bf16[96,256]{1,0:T(8,128)(2,1)S(1)}) custom-call(f32[96,13824]{1,0:T(8,128)S(1)} %convert_add_fusion.base_ref, f32[8,96,256]{2,1,0:T(8,128)S(1)} %bitcast_dynamic-update-slice_fusion.refs_0_, f32[8,96,256]{2,1,0:T(8,128)S(1)} %collective-permute-done.18.refs_1_), custom_call_target="tpu_custom_call" | custom-call | flops 4026531840 | bytes 2359296 | tf_op jit(solution)/shard_map/factor/pallas_call | solution.py:166
  89.3 2.9 %collective-permute-start.32 = (bf16[896,256]{1,0:T(8,128)(2,1)S(1)}, bf16[896,256]{1,0:T(8,128)(2,1)S(1)}, u32[]{:S(2)}, u32[]{:S(2)}) collective-permute-start(bf16[896,256]{1,0:T(8,128)(2,1)S(1)} %get-tuple-element.104.refs_0_), channel_id=1, source_target_pairs={{8,0},{16,8},{24,16},{28,24},{20,28},{12,20},{4,12},{0,4},{2,10},{... | collective-permute-start | bytes 1376264 | tf_op jit(solution)/shard_map/ppermute | solution.py:438
  92.3 2.7 %collective-permute-done.24 = f32[1,256]{1,0:T(1,128)S(1)} collective-permute-done((f32[1,256]{1,0:T(1,128)S(1)}, f32[1,256]{1,0:T(1,128)S(1)}, u32[]{:S(2)}, u32[]{:S(2)}) %collective-permute-start.24) | collective-permute-done | bytes 1056 | tf_op jit(solution)/shard_map/ppermute | solution.py:387
  98.6 4.6 %collective-permute-done.26 = f32[1,256]{1,0:T(1,128)S(1)} collective-permute-done((f32[1,256]{1,0:T(1,128)S(1)}, f32[1,256]{1,0:T(1,128)S(1)}, u32[]{:S(2)}, u32[]{:S(2)}) %collective-permute-start.26) | collective-permute-done | bytes 1056 | tf_op jit(solution)/shard_map/ppermute | solution.py:387
  104.7 2.2 %collective-permute-start.30 = (f32[1,256]{1,0:T(1,128)S(1)}, f32[1,256]{1,0:T(1,128)S(1)}, u32[]{:S(2)}, u32[]{:S(2)}) collective-permute-start(f32[1,256]{1,0:T(1,128)S(1)} %add_add_fusion.1), channel_id=1, source_target_pairs={{0,24},{2,26},{4,28},{6,30},{8,16},{10,18},{12,20},{14,22},{16,8},... | collective-permute-start | bytes 3080 | tf_op jit(solution)/shard_map/ppermute | solution.py:387
  109.0 2.3 %collective-permute-start.37 = (bf16[896,256]{1,0:T(8,128)(2,1)S(1)}, bf16[896,256]{1,0:T(8,128)(2,1)S(1)}, u32[]{:S(2)}, u32[]{:S(2)}) collective-permute-start(bf16[896,256]{1,0:T(8,128)(2,1)S(1)} %collective-permute-done.31.refs_2_), channel_id=1, source_target_pairs={{0,2},{2,0},{4,6},{6,4},{8,10},{10,8},{12,14},{14,12},{16,18},{18,... | collective-permute-start | bytes 1376264 | tf_op jit(solution)/shard_map/ppermute | solution.py:439
  111.3 2.3 %collective-permute-start.33 = (bf16[896,256]{1,0:T(8,128)(2,1)S(1)}, bf16[896,256]{1,0:T(8,128)(2,1)S(1)}, u32[]{:S(2)}, u32[]{:S(2)}) collective-permute-start(bf16[896,256]{1,0:T(8,128)(2,1)S(1)} %collective-permute-done.31.refs_2_), channel_id=1, source_target_pairs={{0,8},{8,16},{16,24},{24,28},{28,20},{20,12},{12,4},{4,0},{10,2},{... | collective-permute-start | bytes 1376264 | tf_op jit(solution)/shard_map/ppermute | solution.py:438
  113.6 2.8 %outputs.7 = (f32[96,13824]{1,0:T(8,128)}, bf16[13824,256]{1,0:T(8,128)(2,1)}, bf16[96,13824]{1,0:T(8,128)(2,1)}) custom-call(f32[96,13824]{1,0:T(8,128)S(1)} %convert_add_fusion.base_ref, bf16[96,256]{1,0:T(8,128)(2,1)S(1)} %get-tuple-element.90.ortho_ref, f32[1,256]{1,0:T(1,128)S(1)} %add_add_fusion.colsq_ref, ...), custom_call_target="tpu_custom_call" | custom-call | flops 352321536 | bytes 7110656 | tf_op jit(solution)/shard_map/outputs/pallas_call | solution.py:271
  116.5 2.5 %collective-permute-done.33.refs_0_ = bf16[896,256]{1,0:T(8,128)(2,1)S(1)} collective-permute-done((bf16[896,256]{1,0:T(8,128)(2,1)S(1)}, bf16[896,256]{1,0:T(8,128)(2,1)S(1)}, u32[]{:S(2)}, u32[]{:S(2)}) %collective-permute-start.33) | collective-permute-done | bytes 458784 | tf_op jit(solution)/shard_map/ppermute | solution.py:438
  130.4 2.6 %collective-permute-start.39 = (bf16[896,256]{1,0:T(8,128)(2,1)S(1)}, bf16[896,256]{1,0:T(8,128)(2,1)S(1)}, u32[]{:S(2)}, u32[]{:S(2)}) collective-permute-start(bf16[896,256]{1,0:T(8,128)(2,1)S(1)} %collective-permute-done.34.refs_0_), channel_id=1, source_target_pairs={{0,8},{8,16},{16,24},{24,28},{28,20},{20,12},{12,4},{4,0},{10,2},{... | collective-permute-start | bytes 1376264 | tf_op jit(solution)/shard_map/ppermute | solution.py:438
  134.9 2.2 %collective-permute-start.45 = (bf16[896,256]{1,0:T(8,128)(2,1)S(1)}, bf16[896,256]{1,0:T(8,128)(2,1)S(1)}, u32[]{:S(2)}, u32[]{:S(2)}) collective-permute-start(bf16[896,256]{1,0:T(8,128)(2,1)S(1)} %collective-permute-done.44.refs_0_), channel_id=1, source_target_pairs={{0,2},{2,0},{4,6},{6,4},{8,10},{10,8},{12,14},{14,12},{16,18},{18,... | collective-permute-start | bytes 1376264 | tf_op jit(solution)/shard_map/ppermute | solution.py:439
  (93 shorter events, 48.9 us)
Async XLA Ops:
  9.8 19.2 %collective-permute-start.4 = (bf16[96,896]{1,0:T(8,128)(2,1)S(1)}, bf16[96,896]{1,0:T(8,128)(2,1)S(1)}, u32[]{:S(2)}, u32[]{:S(2)}) collective-permute-start(bf16[96,896]{1,0:T(8,128)(2,1)S(1)} %get-tuple-element.69), channel_id=1, source_target_pairs={{0,18},{2,16},{4,22},{6,20},{8,26},{10,24},{12,30},{14,28},{16,2},... | collective-permute-start | bytes 516104 | tf_op jit(solution)/shard_map/ppermute | solution.py:351
  13.0 19.5 %collective-permute-start.3 = (bf16[96,896]{1,0:T(8,128)(2,1)S(1)}, bf16[96,896]{1,0:T(8,128)(2,1)S(1)}, u32[]{:S(2)}, u32[]{:S(2)}) collective-permute-start(bf16[96,896]{1,0:T(8,128)(2,1)S(1)} %get-tuple-element.67), channel_id=1, source_target_pairs={{0,16},{2,18},{4,20},{6,22},{8,24},{10,26},{12,28},{14,30},{16,0},... | collective-permute-start | bytes 516104 | tf_op jit(solution)/shard_map/ppermute | solution.py:351
  13.1 19.4 %collective-permute-start.1 = (f32[96,256]{1,0:T(8,128)S(1)}, f32[96,256]{1,0:T(8,128)S(1)}, u32[]{:S(2)}, u32[]{:S(2)}) collective-permute-start(f32[96,256]{1,0:T(8,128)S(1)} %get-tuple-element.130), channel_id=1, source_target_pairs={{0,8},{8,16},{16,24},{24,28},{28,20},{20,12},{12,4},{4,0},{10,2},{... | collective-permute-start | bytes 294920 | tf_op jit(solution)/shard_map/ppermute | solution.py:362
  14.4 22.6 %collective-permute-start.8 = (bf16[96,896]{1,0:T(8,128)(2,1)S(1)}, bf16[96,896]{1,0:T(8,128)(2,1)S(1)}, u32[]{:S(2)}, u32[]{:S(2)}) collective-permute-start(bf16[96,896]{1,0:T(8,128)(2,1)S(1)} %get-tuple-element.74), channel_id=1, source_target_pairs={{0,2},{2,0},{4,6},{6,4},{8,10},{10,8},{12,14},{14,12},{16,18},{18,... | collective-permute-start | bytes 516104 | tf_op jit(solution)/shard_map/ppermute | solution.py:351
  15.1 22.0 %collective-permute-start.7 = (bf16[96,896]{1,0:T(8,128)(2,1)S(1)}, bf16[96,896]{1,0:T(8,128)(2,1)S(1)}, u32[]{:S(2)}, u32[]{:S(2)}) collective-permute-start(bf16[96,896]{1,0:T(8,128)(2,1)S(1)} %get-tuple-element.72), channel_id=1, source_target_pairs={{0,20},{2,22},{4,16},{6,18},{8,28},{10,30},{12,24},{14,26},{16,4},... | collective-permute-start | bytes 516104 | tf_op jit(solution)/shard_map/ppermute | solution.py:351
  33.7 12.3 %collective-permute-start.13 = (bf16[96,896]{1,0:T(8,128)(2,1)S(1)}, bf16[96,896]{1,0:T(8,128)(2,1)S(1)}, u32[]{:S(2)}, u32[]{:S(2)}) collective-permute-start(bf16[96,896]{1,0:T(8,128)(2,1)S(1)} %get-tuple-element.81), channel_id=1, source_target_pairs={{0,6},{2,4},{4,2},{6,0},{8,14},{10,12},{12,10},{14,8},{16,22},{18,... | collective-permute-start | bytes 516104 | tf_op jit(solution)/shard_map/ppermute | solution.py:351
  37.0 11.1 %collective-permute-start.12 = (bf16[96,896]{1,0:T(8,128)(2,1)S(1)}, bf16[96,896]{1,0:T(8,128)(2,1)S(1)}, u32[]{:S(2)}, u32[]{:S(2)}) collective-permute-start(bf16[96,896]{1,0:T(8,128)(2,1)S(1)} %get-tuple-element.79), channel_id=1, source_target_pairs={{0,4},{2,6},{4,0},{6,2},{8,12},{10,14},{12,8},{14,10},{16,20},{18,... | collective-permute-start | bytes 516104 | tf_op jit(solution)/shard_map/ppermute | solution.py:351
  37.1 12.5 %collective-permute-start.11 = (bf16[96,896]{1,0:T(8,128)(2,1)S(1)}, bf16[96,896]{1,0:T(8,128)(2,1)S(1)}, u32[]{:S(2)}, u32[]{:S(2)}) collective-permute-start(bf16[96,896]{1,0:T(8,128)(2,1)S(1)} %get-tuple-element.77), channel_id=1, source_target_pairs={{0,22},{2,20},{4,18},{6,16},{8,30},{10,28},{12,26},{14,24},{16,6},... | collective-permute-start | bytes 516104 | tf_op jit(solution)/shard_map/ppermute | solution.py:351
  39.7 13.6 %collective-permute-start.9 = (f32[96,256]{1,0:T(8,128)S(1)}, f32[96,256]{1,0:T(8,128)S(1)}, u32[]{:S(2)}, u32[]{:S(2)}) collective-permute-start(f32[96,256]{1,0:T(8,128)S(1)} %collective-permute-done.5), channel_id=1, source_target_pairs={{0,8},{8,16},{16,24},{24,28},{28,20},{20,12},{12,4},{4,0},{10,2},{... | collective-permute-start | bytes 294920 | tf_op jit(solution)/shard_map/ppermute | solution.py:362
  40.5 12.8 %collective-permute-start.6 = (f32[96,256]{1,0:T(8,128)S(1)}, f32[96,256]{1,0:T(8,128)S(1)}, u32[]{:S(2)}, u32[]{:S(2)}) collective-permute-start(f32[96,256]{1,0:T(8,128)S(1)} %collective-permute-done.5), channel_id=1, source_target_pairs={{0,1},{1,0},{2,3},{3,2},{4,5},{5,4},{6,7},{7,6},{8,9},{9,8},{10,11... | collective-permute-start | bytes 294920 | tf_op jit(solution)/shard_map/ppermute | solution.py:366
  46.0 11.1 %collective-permute-start.17 = (bf16[96,896]{1,0:T(8,128)(2,1)S(1)}, bf16[96,896]{1,0:T(8,128)(2,1)S(1)}, u32[]{:S(2)}, u32[]{:S(2)}) collective-permute-start(bf16[96,896]{1,0:T(8,128)(2,1)S(1)} %get-tuple-element.88), channel_id=1, source_target_pairs={{0,10},{2,8},{4,14},{6,12},{8,2},{10,0},{12,6},{14,4},{16,26},{18,... | collective-permute-start | bytes 516104 | tf_op jit(solution)/shard_map/ppermute | solution.py:351
  48.1 9.1 %collective-permute-start.16 = (bf16[96,896]{1,0:T(8,128)(2,1)S(1)}, bf16[96,896]{1,0:T(8,128)(2,1)S(1)}, u32[]{:S(2)}, u32[]{:S(2)}) collective-permute-start(bf16[96,896]{1,0:T(8,128)(2,1)S(1)} %get-tuple-element.86), channel_id=1, source_target_pairs={{0,8},{2,10},{4,12},{6,14},{8,0},{10,2},{12,4},{14,6},{16,24},{18,... | collective-permute-start | bytes 516104 | tf_op jit(solution)/shard_map/ppermute | solution.py:351
  49.6 11.9 %collective-permute-start.15 = (bf16[96,896]{1,0:T(8,128)(2,1)S(1)}, bf16[96,896]{1,0:T(8,128)(2,1)S(1)}, u32[]{:S(2)}, u32[]{:S(2)}) collective-permute-start(bf16[96,896]{1,0:T(8,128)(2,1)S(1)} %get-tuple-element.84), channel_id=1, source_target_pairs={{0,24},{2,26},{4,28},{6,30},{8,16},{10,18},{12,20},{14,22},{16,8},... | collective-permute-start | bytes 516104 | tf_op jit(solution)/shard_map/ppermute | solution.py:351
  62.0 24.2 %collective-permute-start.21 = (bf16[96,896]{1,0:T(8,128)(2,1)S(1)}, bf16[96,896]{1,0:T(8,128)(2,1)S(1)}, u32[]{:S(2)}, u32[]{:S(2)}) collective-permute-start(bf16[96,896]{1,0:T(8,128)(2,1)S(1)} %get-tuple-element.98), channel_id=1, source_target_pairs={{0,26},{2,24},{4,30},{6,28},{8,18},{10,16},{12,22},{14,20},{16,10}... | collective-permute-start | bytes 516104 | tf_op jit(solution)/shard_map/ppermute | solution.py:351
  64.9 21.3 %collective-permute-start.20 = (bf16[96,896]{1,0:T(8,128)(2,1)S(1)}, bf16[96,896]{1,0:T(8,128)(2,1)S(1)}, u32[]{:S(2)}, u32[]{:S(2)}) collective-permute-start(bf16[96,896]{1,0:T(8,128)(2,1)S(1)} %get-tuple-element.96), channel_id=1, source_target_pairs={{0,14},{2,12},{4,10},{6,8},{8,6},{10,4},{12,2},{14,0},{16,30},{18,... | collective-permute-start | bytes 516104 | tf_op jit(solution)/shard_map/ppermute | solution.py:351
  64.9 21.4 %collective-permute-start.19 = (bf16[96,896]{1,0:T(8,128)(2,1)S(1)}, bf16[96,896]{1,0:T(8,128)(2,1)S(1)}, u32[]{:S(2)}, u32[]{:S(2)}) collective-permute-start(bf16[96,896]{1,0:T(8,128)(2,1)S(1)} %get-tuple-element.94), channel_id=1, source_target_pairs={{0,12},{2,14},{4,8},{6,10},{8,4},{10,6},{12,0},{14,2},{16,28},{18,... | collective-permute-start | bytes 516104 | tf_op jit(solution)/shard_map/ppermute | solution.py:351
  67.6 18.7 %collective-permute-start.23 = (bf16[96,896]{1,0:T(8,128)(2,1)S(1)}, bf16[96,896]{1,0:T(8,128)(2,1)S(1)}, u32[]{:S(2)}, u32[]{:S(2)}) collective-permute-start(bf16[96,896]{1,0:T(8,128)(2,1)S(1)} %get-tuple-element.102), channel_id=1, source_target_pairs={{0,30},{2,28},{4,26},{6,24},{8,22},{10,20},{12,18},{14,16},{16,14}... | collective-permute-start | bytes 516104 | tf_op jit(solution)/shard_map/ppermute | solution.py:351
  68.7 19.3 %collective-permute-start.22 = (bf16[96,896]{1,0:T(8,128)(2,1)S(1)}, bf16[96,896]{1,0:T(8,128)(2,1)S(1)}, u32[]{:S(2)}, u32[]{:S(2)}) collective-permute-start(bf16[96,896]{1,0:T(8,128)(2,1)S(1)} %get-tuple-element.100), channel_id=1, source_target_pairs={{0,28},{2,30},{4,24},{6,26},{8,20},{10,22},{12,16},{14,18},{16,12}... | collective-permute-start | bytes 516104 | tf_op jit(solution)/shard_map/ppermute | solution.py:351
  89.3 19.7 %collective-permute-start.31 = (bf16[896,256]{1,0:T(8,128)(2,1)S(1)}, bf16[896,256]{1,0:T(8,128)(2,1)S(1)}, u32[]{:S(2)}, u32[]{:S(2)}) collective-permute-start(bf16[896,256]{1,0:T(8,128)(2,1)S(1)} %get-tuple-element.104.refs_0_), channel_id=1, source_target_pairs={{0,8},{8,16},{16,24},{24,28},{28,20},{20,12},{12,4},{4,0},{10,2},{... | collective-permute-start | bytes 1376264 | tf_op jit(solution)/shard_map/ppermute | solution.py:438
  89.3 19.6 %collective-permute-start.32 = (bf16[896,256]{1,0:T(8,128)(2,1)S(1)}, bf16[896,256]{1,0:T(8,128)(2,1)S(1)}, u32[]{:S(2)}, u32[]{:S(2)}) collective-permute-start(bf16[896,256]{1,0:T(8,128)(2,1)S(1)} %get-tuple-element.104.refs_0_), channel_id=1, source_target_pairs={{8,0},{16,8},{24,16},{28,24},{20,28},{12,20},{4,12},{0,4},{2,10},{... | collective-permute-start | bytes 1376264 | tf_op jit(solution)/shard_map/ppermute | solution.py:438
  116.4 9.0 %collective-permute-start.41 = (bf16[896,256]{1,0:T(8,128)(2,1)S(1)}, bf16[896,256]{1,0:T(8,128)(2,1)S(1)}, u32[]{:S(2)}, u32[]{:S(2)}) collective-permute-start(bf16[896,256]{1,0:T(8,128)(2,1)S(1)} %collective-permute-done.32.refs_0_), channel_id=1, source_target_pairs={{8,0},{16,8},{24,16},{28,24},{20,28},{12,20},{4,12},{0,4},{2,10},{... | collective-permute-start | bytes 1376264 | tf_op jit(solution)/shard_map/ppermute | solution.py:438
  120.8 9.1 %collective-permute-start.34 = (bf16[896,256]{1,0:T(8,128)(2,1)S(1)}, bf16[896,256]{1,0:T(8,128)(2,1)S(1)}, u32[]{:S(2)}, u32[]{:S(2)}) collective-permute-start(bf16[896,256]{1,0:T(8,128)(2,1)S(1)} %collective-permute-done.33.refs_0_), channel_id=1, source_target_pairs={{0,8},{8,16},{16,24},{24,28},{28,20},{20,12},{12,4},{4,0},{10,2},{... | collective-permute-start | bytes 1376264 | tf_op jit(solution)/shard_map/ppermute | solution.py:438
  126.8 8.1 %collective-permute-start.44 = (bf16[896,256]{1,0:T(8,128)(2,1)S(1)}, bf16[896,256]{1,0:T(8,128)(2,1)S(1)}, u32[]{:S(2)}, u32[]{:S(2)}) collective-permute-start(bf16[896,256]{1,0:T(8,128)(2,1)S(1)} %collective-permute-done.41.refs_0_), channel_id=1, source_target_pairs={{8,0},{16,8},{24,16},{28,24},{20,28},{12,20},{4,12},{0,4},{2,10},{... | collective-permute-start | bytes 1376264 | tf_op jit(solution)/shard_map/ppermute | solution.py:438
  130.4 9.3 %collective-permute-start.39 = (bf16[896,256]{1,0:T(8,128)(2,1)S(1)}, bf16[896,256]{1,0:T(8,128)(2,1)S(1)}, u32[]{:S(2)}, u32[]{:S(2)}) collective-permute-start(bf16[896,256]{1,0:T(8,128)(2,1)S(1)} %collective-permute-done.34.refs_0_), channel_id=1, source_target_pairs={{0,8},{8,16},{16,24},{24,28},{28,20},{20,12},{12,4},{4,0},{10,2},{... | collective-permute-start | bytes 1376264 | tf_op jit(solution)/shard_map/ppermute | solution.py:438
  (23 other events, 125.1 us)
